TPU v7x, 32 devices: a whole 2x2x4 slice. The times are simulated.
32 devices in a mesh: groups: 2 (over y), wide: 4 (over z), narrow: 4 (over x, core).
Axes of the slice: x: 2, y: 2, z: 4, core: 2. Of those that a mesh axis runs over, the one named last changes fastest.
Arguments:
- ssm_input: bfloat16 [4096, 2048], P(('groups', 'wide', 'narrow')), parts along dimension 0, may hold values from -6 to 6
- gate_input: bfloat16 [4096, 2048], P(('groups', 'wide', 'narrow')), parts along dimension 0, may hold values from -6 to 6
- b_proj: bfloat16 [4096, 128], P(('groups', 'wide', 'narrow')), parts along dimension 0, may hold values from -0.59765625 to 0.59765625
- c_proj: bfloat16 [4096, 128], P(('groups', 'wide', 'narrow')), parts along dimension 0, may hold values from -0.59765625 to 0.59765625
- dt_raw: float32 [4096, 32], P(('groups', 'wide', 'narrow')), parts along dimension 0, may hold values from -4 to 4
- a_log: float32 [32], replicated, may hold values from -5.3 to -0.7
- dt_bias: float32 [32], replicated, may hold values from -3.5 to -1.5
- d_skip: float32 [32], replicated, may hold values from 0.5 to 1.5
- norm_gain: float32 [2048], replicated, may hold values from 0.25 to 1.75
- state_in: float32 [32, 32, 64, 128], P(('groups', 'wide', 'narrow')), parts along dimension 0, may hold values from -6 to 6
- out_proj: bfloat16 [2048, 2048], P(None, 'narrow'), may hold values from -0.125 to 0.125
- expert_in: bfloat16 [16, 2048, 768], P(('wide', 'narrow')), may hold values from -0.125 to 0.125
- expert_out: bfloat16 [16, 384, 2048], P(('wide', 'narrow')), may hold values from -0.3125 to 0.3125
- route_ids: int32 [4096, 8], P(('groups', 'wide', 'narrow')), parts along dimension 0, may hold values from 0 to 15, all different within a row; in each aligned block of 128 rows (0 to 127, 128 to 255, ...) at most 80 rows name the same one
- route_weights: float32 [4096, 8], P(('groups', 'wide', 'narrow')), parts along dimension 0, may hold values from 0.05 to 0.3
Outputs:
- layer_out: bfloat16 [4096, 2048], P(('groups', 'wide', 'narrow')), parts along dimension 0
- state_out: float32 [32, 32, 64, 128], P(('groups', 'wide', 'narrow')), parts along dimension 0
There are 2 independent parts, one for each index of `groups`. A program takes and returns all parts, laid end to end along the dimension named above; an argument that names none is the same for every part. Nothing has to cross between parts.
Inputs may be any that keep to these rules, and one draw needn't show every extreme that they name: `route_ids`: each row names 8 different experts; among the rows of one clip no expert is named more than 80 times, and that count is reached in some clip of every draw.
All inputs are finite; a program needn't handle non-finite values.
Results may differ from a plain program's by a relative error of at most 0.0063.
Values may be sent and summed in bfloat16 or wider, within the bound.
No kernel may reach another device: no remote copies, remote signals or barrier semaphores. Data moves between devices by JAX's collectives and lax.ppermute only.
A program may use at most 128 MiB of HBM per device.

v0:
```python
import jax
import jax.numpy as jnp
from jax import lax
from jax.sharding import PartitionSpec as P

epsilon = 1e-05


def ssm_mixer(
    ssm_input, gate_input, b_proj, c_proj, dt_raw, a_log, dt_bias, d_skip, norm_gain, state_in
):
    length = ssm_input.shape[0]
    head_count = dt_raw.shape[1]
    head_dim = ssm_input.shape[1] // head_count
    step_size = jax.nn.softplus(dt_raw + dt_bias[None, :])
    decay_log = jnp.cumsum(step_size * (-jnp.exp(a_log))[None, :], axis=0)
    decay_heads = decay_log.T
    causal = jnp.arange(length)[:, None] >= jnp.arange(length)[None, :]
    spread = decay_heads[:, :, None] - decay_heads[:, None, :]
    spread = jnp.where(causal[None], spread, 0.0)
    scores = jnp.dot(c_proj, b_proj.T, preferred_element_type=jnp.float32)
    mixing = jnp.where(causal[None], jnp.exp(spread), 0.0) * scores[None] * step_size.T[:, None, :]
    mixing = mixing.astype(jnp.bfloat16)
    values = ssm_input.reshape(length, head_count, head_dim)
    within = jnp.einsum("hts,shp->thp", mixing, values, preferred_element_type=jnp.float32)
    carried = jnp.einsum(
        "tn,hpn->thp", c_proj.astype(jnp.float32), state_in, precision=lax.Precision.HIGHEST
    )
    mixed_rows = (
        within
        + jnp.exp(decay_log)[:, :, None] * carried
        + d_skip[None, :, None] * values.astype(jnp.float32)
    )
    gated_rows = mixed_rows.reshape(length, -1) * jax.nn.silu(gate_input.astype(jnp.float32))
    normed = (
        gated_rows
        * lax.rsqrt(jnp.mean(gated_rows * gated_rows, axis=1, keepdims=True) + epsilon)
        * norm_gain[None, :]
    )
    normed = normed.astype(jnp.bfloat16)
    tail_weight = jnp.exp(decay_log[-1][None, :] - decay_log) * step_size
    scaled = (values.astype(jnp.float32) * tail_weight[:, :, None]).astype(jnp.bfloat16)
    state_next = jnp.exp(decay_log[-1])[:, None, None] * state_in + jnp.einsum(
        "thp,tn->hpn", scaled, b_proj, preferred_element_type=jnp.float32
    )
    return (normed, state_next)


def slot_positions(route_ids, experts):
    flat_ids = route_ids.reshape(-1)
    onehot = (flat_ids[:, None] == jnp.arange(experts, dtype=jnp.int32)[None, :]).astype(jnp.int32)
    earlier = jnp.cumsum(onehot, axis=0) - onehot
    return (flat_ids, jnp.sum(earlier * onehot, axis=1))


def body(
    ssm_input,
    gate_input,
    b_proj,
    c_proj,
    dt_raw,
    a_log,
    dt_bias,
    d_skip,
    norm_gain,
    state_in,
    out_proj,
    expert_in,
    expert_out,
    route_ids,
    route_weights,
):
    normed, state_next = ssm_mixer(
        ssm_input,
        gate_input,
        b_proj,
        c_proj,
        dt_raw,
        a_log,
        dt_bias,
        d_skip,
        norm_gain,
        state_in[0],
    )
    mixer_rows = jnp.dot(
        normed,
        lax.all_gather(out_proj, "narrow", axis=1, tiled=True),
        preferred_element_type=jnp.float32,
    ).astype(jnp.bfloat16)
    frames_here = mixer_rows.shape[0]
    model_width = mixer_rows.shape[1]
    topk_count = route_ids.shape[1]
    local_experts = expert_in.shape[0]
    devices = lax.axis_size(("wide", "narrow"))
    experts = local_experts * devices
    capacity = max(2, frames_here * topk_count * 5 // (4 * experts))
    flat_ids, positions = slot_positions(route_ids, experts)
    owners = jnp.arange(frames_here * topk_count, dtype=jnp.int32) // topk_count
    slot_table = (
        jnp.full((experts, capacity), frames_here, jnp.int32).at[flat_ids, positions].set(owners)
    )
    padded = jnp.concatenate([mixer_rows, jnp.zeros((1, model_width), jnp.bfloat16)], axis=0)
    outgoing = padded[slot_table]
    hidden_width = expert_out.shape[1]
    projected = jnp.einsum(
        "nlcd,ldf->nlcf",
        lax.all_to_all(
            outgoing.reshape(devices, local_experts, capacity, model_width),
            ("wide", "narrow"),
            split_axis=0,
            concat_axis=0,
            tiled=True,
        ),
        expert_in,
        preferred_element_type=jnp.float32,
    )
    hidden = (jax.nn.silu(projected[..., :hidden_width]) * projected[..., hidden_width:]).astype(
        jnp.bfloat16
    )
    returned = lax.all_to_all(
        jnp.einsum("nlcf,lfd->nlcd", hidden, expert_out, preferred_element_type=jnp.float32).astype(
            jnp.bfloat16
        ),
        ("wide", "narrow"),
        split_axis=0,
        concat_axis=0,
        tiled=True,
    )
    returned = returned.reshape(experts, capacity, model_width)
    picked = returned[flat_ids, positions].reshape(frames_here, topk_count, model_width)
    expert_sum = jnp.einsum("tk,tkd->td", route_weights, picked.astype(jnp.float32))
    layer_out = (mixer_rows.astype(jnp.float32) + expert_sum).astype(jnp.bfloat16)
    return (layer_out, state_next[None])


def solution(mesh):
    placed = (
        P(("groups", "wide", "narrow"), None),
        P(("groups", "wide", "narrow"), None),
        P(("groups", "wide", "narrow"), None),
        P(("groups", "wide", "narrow"), None),
        P(("groups", "wide", "narrow"), None),
        P(),
        P(),
        P(),
        P(),
        P(("groups", "wide", "narrow"), None, None, None),
        P(None, "narrow"),
        P(("wide", "narrow"), None, None),
        P(("wide", "narrow"), None, None),
        P(("groups", "wide", "narrow"), None),
        P(("groups", "wide", "narrow"), None),
    )
    return jax.shard_map(
        body,
        mesh=mesh,
        in_specs=placed,
        out_specs=(
            P(("groups", "wide", "narrow"), None),
            P(("groups", "wide", "narrow"), None, None, None),
        ),
        check_vma=False,
    )
```

profile of v0, /device:TPU:15, one launch (start us, length us, event | category | flops | bytes accessed | tf_op | source)
XLA Modules:
  0.0 374.9 jit_solution(9893308557942044334)
XLA Ops:
  7.2 0.0 copy-start
  7.2 0.0 copy-start.10
  7.2 0.0 all-gather.2.cloned.1.call-start
  7.3 0.7 all-gather.2.cloned.1.call-update
  8.0 0.9 copy.61
  8.9 0.1 eq.29
  9.0 0.1 eq.25
  9.1 0.1 reshape.134
  9.2 0.7 exponential_negate_fusion
  9.8 0.8 broadcast_multiply_fusion
  10.7 0.1 copy.55
  10.8 0.2 reduce_window_sum.26
  10.9 0.1 copy.68
  11.1 4.5 %reduce-window.6 = s32[16,8,128]{2,1,0:T(8,128)S(1)} reduce-window(s32[16,8,128]{2,1,0:T(8,128)S(1)} %fusion.37, s32[]{:T(128)} %constant.44.clone.1), window={size=1x1x128 pad=0_0x0_0x127_0}, to_apply=%region_2.3 | reduce-window | flops 2080768 | bytes 131076 | tf_op jit(solution)/shard_map/reduce-window
  15.6 0.1 slice.25
  15.6 0.1 copy.64
  15.8 0.1 copy.65
  15.9 0.1 broadcast_add_fusion
  16.1 0.1 multiply_reduce_fusion.1
  16.2 0.1 and_reduce_fusion
  16.3 4.3 %scatter_custom_fusion = s32[1280]{0:T(1024)S(1)} fusion(s32[1024]{0:T(1024)S(1)} %get-tuple-element.8, s32[1024]{0:T(1024)S(1)} %get-tuple-element.7, s32[]{:T(128)} %constant.43.clone.1), kind=kCustom, calls=%fused_computation.74 | custom fusion | bytes 5124
  20.6 0.1 reshape.146
  20.7 0.1 reshape.149
  20.7 0.1 copy.56
  20.8 2.1 copy.58
  22.9 0.1 copy.59
  23.1 0.1 exponential_multiply_fusion
  23.2 0.1 fusion.50
  23.3 2.4 convolution_bitcast_fusion
  25.7 0.0 copy-done.12
  25.7 1.7 fusion.13
  27.4 2.7 copy.60
  30.1 1.8 multiply_reduce_fusion
  32.0 36.6 %all-gather.2.cloned.1.call-done = bf16[2048,2048]{1,0:T(8,128)(2,1)} async-done(((bf16[2048,512]{1,0:T(8,128)(2,1)}), bf16[2048,2048]{1,0:T(8,128)(2,1)}) %all-gather.2.cloned.1.call-update) | async-done | bytes 8388624 | tf_op jit(solution)/shard_map/all_gather | solution.py:87
  68.6 5.4 %convolution_convert_fusion = bf16[128,2048]{1,0:T(8,128)(2,1)S(1)} fusion(bf16[2048,2048]{1,0:T(8,128)(2,1)} %all-gather.2.cloned.1.call-done, f32[2048]{0:T(1024)S(1)} %copy-done.14, f32[128]{0:T(128)S(1)} %add_rsqrt_fusion, f32[128,2048]{1,0:T(8,128)} %copy.60, bf16[128,2048]{1,0:T(8,128)(2,1)} %param.16), kind=kOutput, calls=%fused_computation.9 | convolution fusion | flops 1076363264 | bytes 10494464 | tf_op jit(solution)/shard_map/dot_general | solution.py:85
  74.0 0.8 copy-done.3
  74.8 0.9 concatenate.7
  75.6 11.9 %gather_fusion = bf16[1280,2048]{1,0:T(8,128)(2,1)} fusion(bf16[129,2048]{1,0:T(8,128)(2,1)} %concatenate.7, s32[2048]{0:T(1024)S(1)} %pad_clamp_fusion), kind=kCustom, calls=%fused_computation | custom fusion | bytes 10490880 | tf_op jit(solution)/shard_map/gather | solution.py:103
  87.6 120.7 %all_to_all.10 = bf16[16,1,80,2048]{3,2,1,0:T(8,128)(2,1)S(1)} all-to-all(bf16[16,1,80,2048]{3,2,1,0:T(8,128)(2,1)} %bitcast.95), channel_id=1, replica_groups=mesh['groups'=2,'wide'=4,'narrow'=4] {'wide','narrow'}, dimensions={0} | all-to-all | bytes 10485760 | tf_op jit(solution)/shard_map/all_to_all | solution.py:107
  208.3 4.3 %fusion.5 = f32[16,1,80,768]{3,2,0,1:T(8,128)S(1)} fusion(bf16[1,2048,768]{2,1,0:T(8,128)(2,1)S(1)} %copy-done, bf16[16,1,80,2048]{3,2,1,0:T(8,128)(2,1)S(1)} %all_to_all.10), kind=kOutput, calls=%fused_computation.11 | convolution fusion | flops 4026531840 | bytes 12320768 | tf_op jit(solution)/shard_map/nlcd,ldf->nlcf/dot_general | solution.py:105
  212.6 4.7 %convert_bitcast_fusion = bf16[16,1,80,2048]{3,2,1,0:T(8,128)(2,1)} fusion(bf16[1,384,2048]{2,1,0:T(8,128)(2,1)S(1)} %copy-done.13, f32[16,1,80,768]{3,2,0,1:T(8,128)S(1)} %fusion.5), kind=kOutput, calls=%fused_computation.5 | convolution fusion | flops 2018836480 | bytes 10747904 | tf_op jit(solution)/shard_map/nlcf,lfd->nlcd/dot_general | solution.py:121
  217.3 5.5 %all-to-all-start.1 = ((bf16[16,1,80,2048]{3,2,1,0:T(8,128)(2,1)}), bf16[16,1,80,2048]{3,2,1,0:T(8,128)(2,1)}, u32[]{:S(2)}, u32[]{:S(2)}) async-start(bf16[16,1,80,2048]{3,2,1,0:T(8,128)(2,1)} %convert_bitcast_fusion), calls=%async_computation.1 | async-start | bytes 10485760 | tf_op jit(solution)/shard_map/all_to_all | solution.py:120
  222.9 0.1 copy.69
  223.1 2.7 fusion.14
  225.7 112.1 %all-to-all-done.1 = bf16[16,1,80,2048]{3,2,1,0:T(8,128)(2,1)} async-done(((bf16[16,1,80,2048]{3,2,1,0:T(8,128)(2,1)}), bf16[16,1,80,2048]{3,2,1,0:T(8,128)(2,1)}, u32[]{:S(2)}, u32[]{:S(2)}) %all-to-all-start.1) | async-done | bytes 5242912 | tf_op jit(solution)/shard_map/all_to_all | solution.py:120
  337.8 25.6 %gather_fusion.1 = bf16[1024,2048]{1,0:T(8,128)(2,1)} fusion(bf16[16,80,2048]{2,1,0:T(8,128)(2,1)} %bitcast.27, s32[1024]{0:T(1024)S(1)} %bitcast.94), kind=kCustom, calls=%fused_computation.1 | custom fusion | bytes 8396800 | tf_op jit(solution)/shard_map/gather | solution.py:130
  363.4 3.5 fusion.2
  366.9 1.1 fusion.20
  (39 shorter events, 0.3 us)
Async XLA Ops:
  7.2 201.1 %copy-start = (bf16[1,2048,768]{2,1,0:T(8,128)(2,1)S(1)}, bf16[1,2048,768]{2,1,0:T(8,128)(2,1)}, u32[]{:S(2)}) copy-start(bf16[1,2048,768]{2,1,0:T(8,128)(2,1)} %param.26) | copy-start | bytes 9437188
  7.2 8.9 %copy-start.11 = (s32[2]{0:T(128)S(1)}, s32[2]{0:T(128)}, u32[]{:S(2)}) copy-start(s32[2]{0:T(128)} %constant.57) | copy-start | bytes 28
  7.2 9.0 %copy-start.10 = (s32[2]{0:T(128)S(1)}, s32[2]{0:T(128)}, u32[]{:S(2)}) copy-start(s32[2]{0:T(128)} %constant.60) | copy-start | bytes 28
  7.2 15.8 %copy-start.7 = (f32[128,32]{0,1:T(8,128)S(1)}, f32[128,32]{0,1:T(8,128)}, u32[]{:S(2)}) copy-start(f32[128,32]{0,1:T(8,128)} %param.19) | copy-start | bytes 49156
  7.2 15.8 %copy-start.9 = (f32[32]{0:T(128)S(1)}, f32[32]{0:T(128)}, u32[]{:S(2)}) copy-start(f32[32]{0:T(128)} %param.21) | copy-start | bytes 388
  7.2 15.9 %copy-start.6 = (bf16[128,128]{1,0:T(8,128)(2,1)S(1)}, bf16[128,128]{1,0:T(8,128)(2,1)}, u32[]{:S(2)}) copy-start(bf16[128,128]{1,0:T(8,128)(2,1)} %param.17) | copy-start | bytes 98308
  7.2 15.9 %copy-start.5 = (bf16[128,128]{1,0:T(8,128)(2,1)S(1)}, bf16[128,128]{1,0:T(8,128)(2,1)}, u32[]{:S(2)}) copy-start(bf16[128,128]{1,0:T(8,128)(2,1)} %param.18) | copy-start | bytes 98308
  7.2 61.3 %all-gather.2.cloned.1.call-start = ((), (), s32[]{:S(2)}) async-start(), calls=%async_computation.2 | async-start | bytes 10485760 | tf_op jit(solution)/shard_map/all_gather | solution.py:87
  20.8 4.9 %copy-start.12 = (f32[32]{0:T(128)S(1)}, f32[32]{0:T(128)}, u32[]{:S(2)}) copy-start(f32[32]{0:T(128)} %param.22) | copy-start | bytes 388
  23.0 2.7 copy-start.1
  23.0 2.7 copy-start.2
  25.7 42.9 %copy-start.14 = (f32[2048]{0:T(1024)S(1)}, f32[2048]{0:T(1024)}, u32[]{:S(2)}) copy-start(f32[2048]{0:T(1024)} %param.23) | copy-start | bytes 24580
  73.9 0.8 copy-start.3
  208.3 4.3 %copy-start.13 = (bf16[1,384,2048]{2,1,0:T(8,128)(2,1)S(1)}, bf16[1,384,2048]{2,1,0:T(8,128)(2,1)}, u32[]{:S(2)}) copy-start(bf16[1,384,2048]{2,1,0:T(8,128)(2,1)} %param.27) | copy-start | bytes 4718596
  217.3 5.6 %copy-start.8 = (f32[128,8]{0,1:T(8,128)S(1)}, f32[128,8]{0,1:T(8,128)}, u32[]{:S(2)}) copy-start(f32[128,8]{0,1:T(8,128)} %param.29) | copy-start | bytes 12292
  217.3 120.5 %all-to-all-start.1 = ((bf16[16,1,80,2048]{3,2,1,0:T(8,128)(2,1)}), bf16[16,1,80,2048]{3,2,1,0:T(8,128)(2,1)}, u32[]{:S(2)}, u32[]{:S(2)}) async-start(bf16[16,1,80,2048]{3,2,1,0:T(8,128)(2,1)} %convert_bitcast_fusion), calls=%async_computation.1 | async-start | bytes 10485760 | tf_op jit(solution)/shard_map/all_to_all | solution.py:120
  363.4 3.5 copy-start.4
Sparse Core Ops, SparseCore 0:
  9.6 58.8 all-gather.1
where the time goes:
time: 376 us; the launch traced here: 375 us
  waiting for transfers between devices  149 us (40%)
  blocking collectives  121 us (32%)
  local copies, waits for them, and re-layouts  50.5 us (13%)
  matrix products  24.7 us (7%)
  between operations  14.3 us (4%)
  other arithmetic  9.62 us (3%)
  starting transfers between devices  5.58 us (1%)
    all_to_all x1, blocking collectives, body(): lax.all_to_all(outgoing.reshape(devices, local_experts, capacity, model_w...  121 us
    all_to_all x1, waiting for transfers between devices, body(): lax.all_to_all(jnp.einsum('nlcf,lfd->nlcd', hidden, expert_out, preferred...  112 us
    all_gather x1, waiting for transfers between devices, body(): lax.all_gather(out_proj, 'narrow', axis=1, tiled=True)  36.6 us
    gather x1, local copies, waits for them, and re-layouts, body(): returned[flat_ids, positions].reshape(frames_here, topk_count, model_width)  25.6 us
    gather x1, local copies, waits for them, and re-layouts, body(): outgoing = padded[slot_table]  11.9 us
    unnamed x34, local copies, waits for them, and re-layouts  8.42 us
  transfers between devices with their start and end apart: 2, of which 2 were waited for; matrix products, arithmetic and copies ran while one was open for 7% of the time, Pallas kernels for 0%

commit v1 on v0

--- a/solution.py
+++ b/solution.py
@@ -82,6 +82,59 @@
         norm_gain,
         state_in[0],
     )
+    frames_here, topk_count = route_ids.shape
+    local_experts = expert_in.shape[0]
+    experts = local_experts * lax.axis_size(("wide", "narrow"))
+    if experts <= 4 * topk_count:
+        layer_out = dense_experts(normed, out_proj, expert_in, expert_out, route_ids, route_weights)
+    else:
+        layer_out = routed_experts(normed, out_proj, expert_in, expert_out, route_ids, route_weights)
+    return (layer_out, state_next[None])
+
+
+def dense_experts(normed, out_proj, expert_in, expert_out, route_ids, route_weights):
+    frames_here, topk_count = route_ids.shape
+    local_experts = expert_in.shape[0]
+    model_width = expert_in.shape[1]
+    wide, narrow = lax.axis_size("wide"), lax.axis_size("narrow")
+    devices = wide * narrow
+    me = lax.axis_index(("wide", "narrow"))
+    row_norms = lax.all_gather(normed, "narrow", axis=0, tiled=True)
+    columns = jnp.dot(row_norms, out_proj, preferred_element_type=jnp.float32).astype(jnp.bfloat16)
+    width = columns.shape[1]
+    all_rows = lax.all_gather(columns, ("wide", "narrow"), axis=0, tiled=False)
+    all_rows = all_rows.reshape(wide, narrow, narrow * frames_here, width)
+    ids_all = lax.all_gather(route_ids, ("wide", "narrow"), axis=0, tiled=True)
+    weights_all = lax.all_gather(route_weights, ("wide", "narrow"), axis=0, tiled=True)
+    total = None
+    for local in range(local_experts):
+        gate = jnp.sum(
+            jnp.where(ids_all == me * local_experts + local, weights_all, 0.0), axis=1, keepdims=True
+        )
+        projected = None
+        for block in range(narrow):
+            part = jnp.dot(
+                all_rows[:, block].reshape(devices * frames_here, width),
+                expert_in[local, block * width : (block + 1) * width],
+                preferred_element_type=jnp.float32,
+            )
+            projected = part if projected is None else projected + part
+        hidden_width = expert_out.shape[1]
+        hidden = (jax.nn.silu(projected[:, :hidden_width]) * projected[:, hidden_width:]).astype(
+            jnp.bfloat16
+        )
+        result = gate * jnp.dot(hidden, expert_out[local], preferred_element_type=jnp.float32)
+        total = result if total is None else total + result
+    summed = lax.psum_scatter(
+        total.astype(jnp.bfloat16), ("wide", "narrow"), scatter_dimension=0, tiled=True
+    )
+    mine = lax.dynamic_slice_in_dim(all_rows, lax.axis_index("wide"), 1, 0)[0]
+    mine = lax.dynamic_slice_in_dim(mine, lax.axis_index("narrow") * frames_here, frames_here, 1)
+    mine = mine.transpose(1, 0, 2).reshape(frames_here, model_width)
+    return (mine.astype(jnp.float32) + summed.astype(jnp.float32)).astype(jnp.bfloat16)
+
+
+def routed_experts(normed, out_proj, expert_in, expert_out, route_ids, route_weights):
     mixer_rows = jnp.dot(
         normed,
         lax.all_gather(out_proj, "narrow", axis=1, tiled=True),
@@ -130,7 +183,7 @@
     picked = returned[flat_ids, positions].reshape(frames_here, topk_count, model_width)
     expert_sum = jnp.einsum("tk,tkd->td", route_weights, picked.astype(jnp.float32))
     layer_out = (mixer_rows.astype(jnp.float32) + expert_sum).astype(jnp.bfloat16)
-    return (layer_out, state_next[None])
+    return layer_out
 
 
 def solution(mesh):

time: 376 us -> 258 us (0.69)
  the two profiles are of different devices: /device:TPU:15 before, /device:TPU:0 now
where the time goes in v1:
time: 258 us
  waiting for transfers between devices  161 us (62%)
  blocking collectives  39.1 us (15%)
  matrix products  24.9 us (10%)
  between operations  14 us (5%)
  other arithmetic  9.77 us (4%)
  local copies, waits for them, and re-layouts  9.32 us (4%)
    reduce_scatter x1, waiting for transfers between devices, dense_experts(): lax.psum_scatter(total.astype(jnp.bfloat16), ('wide', 'narrow'), scatter_...  99 us
    all_gather x1, waiting for transfers between devices, dense_experts(): all_rows = lax.all_gather(columns, ('wide', 'narrow'), axis=0, tiled=False)  36.2 us
    all_gather x1, waiting for transfers between devices, dense_experts(): row_norms = lax.all_gather(normed, 'narrow', axis=0, tiled=True)  25.4 us
    all_gather x1, blocking collectives, dense_experts(): lax.all_gather(route_weights, ('wide', 'narrow'), axis=0, tiled=True)  21 us
    all_gather x1, blocking collectives, dense_experts(): ids_all = lax.all_gather(route_ids, ('wide', 'narrow'), axis=0, tiled=True)  18.1 us
    dot_general x4, matrix products, dense_experts(): jnp.dot(all_rows[:, block].reshape(devices * frames_here, width), expert_...  8.45 us
    dot_general x1, matrix products, dense_experts(): jnp.dot(hidden, expert_out[local], preferred_element_type=jnp.float32)  8.1 us
  transfers between devices with their start and end apart: 3, of which 3 were waited for; matrix products, arithmetic and copies ran while one was open for 1% of the time, Pallas kernels for 0%

profile of v1, /device:TPU:0, one launch (start us, length us, event | category | flops | bytes accessed | tf_op | source)
XLA Modules:
  0.0 257.8 jit_solution(10509200775549441779)
XLA Ops:
  7.2 0.0 copy-start
  7.2 0.0 all-gather.4.cloned.1.call-start
  7.2 0.8 exponential_negate_fusion
  8.0 0.8 broadcast_multiply_fusion
  8.8 0.1 copy.26
  8.9 0.2 reduce_window_sum.11
  9.1 0.1 copy.33
  9.2 1.3 copy.29
  10.6 0.0 copy-start.2
  10.6 0.1 copy.27
  10.6 0.1 copy.30
  10.7 0.9 exponential_multiply_fusion
  11.6 0.9 fusion.39
  12.5 0.0 copy-start.7
  12.5 0.0 copy-start.12
  12.5 0.9 convolution_bitcast_fusion
  13.4 0.0 copy-done.2
  13.5 0.3 copy-done.4
  13.7 1.6 fusion.5
  15.4 1.6 copy.31
  17.0 1.5 multiply_reduce_fusion
  18.5 2.2 multiply_convert_fusion.3
  20.7 0.0 all-gather.4.cloned.1.call-update
  20.7 0.0 copy-start.10
  20.7 0.0 copy-start.11
  20.8 0.0 all-gather.6.cloned.1.call-start
  20.8 25.4 %all-gather.4.cloned.1.call-done = bf16[512,2048]{1,0:T(8,128)(2,1)} async-done(((bf16[128,2048]{1,0:T(8,128)(2,1)}), bf16[512,2048]{1,0:T(8,128)(2,1)}) %all-gather.4.cloned.1.call-update) | async-done | bytes 2097168 | tf_op jit(solution)/shard_map/all_gather | solution.py:102
  46.2 3.6 %convolution_convert_fusion = bf16[512,512]{1,0:T(8,128)(2,1)} fusion(bf16[512,2048]{1,0:T(8,128)(2,1)} %all-gather.4.cloned.1.call-done, bf16[2048,512]{1,0:T(8,128)(2,1)S(1)} %copy-done), kind=kOutput, calls=%fused_computation.17 | convolution fusion | flops 1074003968 | bytes 4718592 | tf_op jit(solution)/shard_map/dot_general | solution.py:103
  49.8 0.0 all-gather.6.cloned.1.call-update
  49.8 0.0 reduce-scatter.2.cloned.1.call-start
  49.9 21.0 %all_gather.19 = f32[2048,8]{0,1:T(8,128)S(1)} all-gather(f32[128,8]{0,1:T(8,128)S(1)} %copy-done.10), channel_id=1, replica_groups=mesh['groups'=2,'wide'=4,'narrow'=4] {'wide','narrow'}, dimensions={0}, use_global_device_ids=true | all-gather | bytes 69632 | tf_op jit(solution)/shard_map/all_gather | solution.py:108
  70.9 18.1 %all_gather.18 = s32[2048,8]{0,1:T(8,128)S(1)} all-gather(s32[128,8]{0,1:T(8,128)S(1)} %copy-done.11), channel_id=1, replica_groups=mesh['groups'=2,'wide'=4,'narrow'=4] {'wide','narrow'}, dimensions={0}, use_global_device_ids=true | all-gather | bytes 69632 | tf_op jit(solution)/shard_map/all_gather | solution.py:107
  89.0 36.2 %all-gather.6.cloned.1.call-done = bf16[8192,512]{1,0:T(8,128)(2,1)} async-done(((bf16[512,512]{1,0:T(8,128)(2,1)}), bf16[8192,512]{1,0:T(8,128)(2,1)}) %all-gather.6.cloned.1.call-update) | async-done | bytes 8388624 | tf_op jit(solution)/shard_map/all_gather | solution.py:105
  125.2 4.1 %fusion.38 = (bf16[4,1,512,512]{3,2,1,0:T(8,128)(2,1)S(1)}, bf16[4,1,512,512]{3,2,1,0:T(8,128)(2,1)S(1)}, bf16[4,1,512,512]{3,2,1,0:T(8,128)(2,1)S(1)}, bf16[4,1,512,512]{3,2,1,0:T(8,128)(2,1)S(1)}) fusion(bf16[4,4,512,512]{3,2,1,0:T(8,128)(2,1)} %bitcast.64), kind=kLoop, calls=%fused_computation.61 | loop fusion | bytes 16777216 | tf_op jit(solution)/shard_map/slice | solution.py:117
  129.3 0.3 copy-done.6
  129.6 1.8 fusion.20
  131.4 1.8 fusion.24
  133.2 1.8 fusion.22
  135.0 3.1 %add_add_fusion = f32[2048,768]{1,0:T(8,128)S(1)} fusion(f32[2048,768]{1,0:T(8,128)S(1)} %fusion.20, f32[2048,768]{1,0:T(8,128)S(1)} %fusion.24, f32[2048,768]{1,0:T(8,128)S(1)} %fusion.22, bf16[2048,512]{1,0:T(8,128)(2,1)S(1)} %bitcast.66, bf16[1,2048,768]{2,1,0:T(8,128)(2,1)} %param.26), kind=kOutput, calls=%fused_computation.1 | convolution fusion | flops 1615331328 | bytes 28049408 | tf_op jit(solution)/shard_map/dot_general | solution.py:116
  138.0 8.1 %multiply_convert_fusion = bf16[2048,2048]{1,0:T(8,128)(2,1)} fusion(f32[2048]{0:T(1024)S(1)} %select_reduce_fusion, f32[2048,768]{1,0:T(8,128)S(1)} %add_add_fusion, bf16[1,384,2048]{2,1,0:T(8,128)(2,1)} %param.27), kind=kOutput, calls=%fused_computation | convolution fusion | flops 3234332672 | bytes 16261120 | tf_op jit(solution)/shard_map/dot_general | solution.py:126
  146.1 0.0 reduce-scatter.2.cloned.1.call-update
  146.2 1.0 copy-done.3
  147.2 0.3 copy-done.5
  147.5 1.3 fusion.6
  148.8 1.4 convert_bitcast_fusion
  150.2 0.1 copy.34
  150.3 99.0 %reduce-scatter.2.cloned.1.call-done = bf16[128,2048]{1,0:T(8,128)(2,1)} async-done(((bf16[2048,2048]{1,0:T(8,128)(2,1)}), bf16[128,2048]{1,0:T(8,128)(2,1)}) %reduce-scatter.2.cloned.1.call-update) | async-done | bytes 524304 | tf_op jit(solution)/shard_map/reduce_scatter | solution.py:128
  249.3 1.9 add_convert_fusion
  (21 shorter events, 0.1 us)
Async XLA Ops:
  7.2 39.0 %copy-start = (bf16[2048,512]{1,0:T(8,128)(2,1)S(1)}, bf16[2048,512]{1,0:T(8,128)(2,1)}, u32[]{:S(2)}) copy-start(bf16[2048,512]{1,0:T(8,128)(2,1)} %param.25) | copy-start | bytes 6291460
  7.2 39.0 %all-gather.4.cloned.1.call-start = ((), (), s32[]{:S(2)}) async-start(), calls=%async_computation.1 | async-start | bytes 2621440 | tf_op jit(solution)/shard_map/all_gather | solution.py:102
  10.6 2.9 %copy-start.2 = (bf16[128,2048]{0,1:T(8,128)(2,1)}, bf16[128,2048]{0,1:T(8,128)(2,1)S(1)}, u32[]{:S(2)}) copy-start(bf16[128,2048]{0,1:T(8,128)(2,1)S(1)} %copy.29) | copy-start | bytes 1572868
  12.5 1.3 copy-start.4
  12.5 1.3 copy-start.7
  12.5 1.2 copy-start.12
  15.4 3.1 %copy-start.9 = (f32[2048]{0:T(1024)S(1)}, f32[2048]{0:T(1024)}, u32[]{:S(2)}) copy-start(f32[2048]{0:T(1024)} %param.23) | copy-start | bytes 24580
  20.7 29.2 %copy-start.10 = (f32[128,8]{0,1:T(8,128)S(1)}, f32[128,8]{0,1:T(8,128)}, u32[]{:S(2)}) copy-start(f32[128,8]{0,1:T(8,128)} %param.29) | copy-start | bytes 12292
  20.7 50.1 %copy-start.11 = (s32[128,8]{0,1:T(8,128)S(1)}, s32[128,8]{0,1:T(8,128)}, u32[]{:S(2)}) copy-start(s32[128,8]{0,1:T(8,128)} %param.28) | copy-start | bytes 12292
  20.8 104.4 %all-gather.6.cloned.1.call-start = ((), (), s32[]{:S(2)}) async-start(), calls=%async_computation.3 | async-start | bytes 8912896 | tf_op jit(solution)/shard_map/all_gather | solution.py:105
  49.8 199.5 %reduce-scatter.2.cloned.1.call-start = ((), (), s32[]{:S(2)}) async-start(), calls=%async_computation.2 | async-start | bytes 8912896 | tf_op jit(solution)/shard_map/reduce_scatter | solution.py:128
  125.2 4.4 %copy-start.6 = (bf16[1,2048,768]{2,1,0:T(8,128)(2,1)S(1)}, bf16[1,2048,768]{2,1,0:T(8,128)(2,1)}, u32[]{:S(2)}) copy-start(bf16[1,2048,768]{2,1,0:T(8,128)(2,1)} %param.26) | copy-start | bytes 9437188
  146.1 1.0 copy-start.3
  146.1 1.4 copy-start.5
  146.1 1.4 copy-start.8
  148.8 102.5 %copy-start.1 = (bf16[2048,512]{1,0:T(8,128)(2,1)S(1)}, bf16[2048,512]{1,0:T(8,128)(2,1)}, u32[]{:S(2)}) copy-start(bf16[2048,512]{1,0:T(8,128)(2,1)} %param.25) | copy-start | bytes 6291460
Sparse Core Ops, SparseCore 0:
  20.9 25.2 all-gather.3
  50.0 75.1 all-gather.5
  146.3 102.9 reduce-scatter.1

commit v2 on v0

--- a/solution.py
+++ b/solution.py
@@ -82,6 +82,150 @@
         norm_gain,
         state_in[0],
     )
+    frames_here, topk_count = route_ids.shape
+    local_experts = expert_in.shape[0]
+    experts = local_experts * lax.axis_size(("wide", "narrow"))
+    wide, narrow = lax.axis_size("wide"), lax.axis_size("narrow")
+    if experts <= 4 * topk_count and narrow == 4 and wide & (wide - 1) == 0 and local_experts == 1:
+        layer_out = dense_experts(
+            normed, out_proj, expert_in[0], expert_out[0], route_ids, route_weights
+        )
+    else:
+        layer_out = routed_experts(normed, out_proj, expert_in, expert_out, route_ids, route_weights)
+    return (layer_out, state_next[None])
+
+
+def routes(wide, move):
+    pairs = []
+    for z in range(wide):
+        for x in range(2):
+            for core in range(2):
+                to = move(z, x, core)
+                if to is not None:
+                    pairs.append(((z * 2 + x) * 2 + core, (to[0] * 2 + to[1]) * 2 + to[2]))
+    return pairs
+
+
+def pick(index, table, arrays):
+    used = sorted(set(table))
+    out = arrays[used[0]]
+    for name in used[1:]:
+        here = [i for i, entry in enumerate(table) if entry == name]
+        test = index == here[0]
+        for i in here[1:]:
+            test = test | (index == i)
+        out = jnp.where(test, arrays[name], out)
+    return out
+
+
+def dense_experts(normed, out_proj, expert_in, expert_out, route_ids, route_weights):
+    frames = route_ids.shape[0]
+    wide = lax.axis_size("wide")
+    z = lax.axis_index("wide")
+    x, core = lax.axis_index("narrow") // 2, lax.axis_index("narrow") % 2
+    axes = ("wide", "narrow")
+
+    def send(value, move):
+        return lax.ppermute(value, axes, routes(wide, move))
+
+    def to_core(value):
+        return send(value, lambda z, x, c: (z, x, 1 - c))
+
+    def to_x(value):
+        return send(value, lambda z, x, c: (z, 1 - x, c))
+
+    out_other, in_other, down_other = to_core(out_proj), to_core(expert_in), to_core(expert_out)
+
+    experts = wide * 4
+    gates = jnp.sum(
+        jnp.where(route_ids[:, :, None] == jnp.arange(experts), route_weights[:, :, None], 0.0), axis=1
+    )
+    other = to_x(gates)
+    gates = jnp.stack([jnp.where(x == 0, gates, other), jnp.where(x == 0, other, gates)])[None]
+    step = 1
+    while step < wide:
+        gates = jnp.concatenate([gates, send(gates, lambda z, x, c: (z ^ step, x, c))], axis=0)
+        step *= 2
+    mine = (z * 2 + x) * 2 + core
+    pair = jnp.stack([mine, mine + 1 - 2 * core])
+    gates = jnp.sum(
+        jnp.where(pair[:, None] == jnp.arange(experts), gates[..., None, :], 0.0), axis=-1
+    ).reshape(wide, 2 * frames, 2)
+
+    def project(rows):
+        first = jnp.dot(rows, out_proj, preferred_element_type=jnp.float32).astype(jnp.bfloat16)
+        second = jnp.dot(rows, out_other, preferred_element_type=jnp.float32).astype(jnp.bfloat16)
+        return jnp.where(
+            core == 0,
+            jnp.concatenate([first, second], axis=1),
+            jnp.concatenate([second, first], axis=1),
+        )
+
+    own = project(normed)
+    peer = project(to_x(normed))
+    block = jnp.where(x == 0, jnp.concatenate([own, peer]), jnp.concatenate([peer, own]))
+
+    order = [sorted((o for o in range(wide) if o != p), key=lambda o: (abs(o - p), o)) for p in range(wide)]
+    came = {}
+    up = down = block
+    for k in range(1, wide):
+        up = send(up, lambda z, x, c: (z + 1, x, c) if z + 1 < wide and z + 1 >= k else None)
+        down = send(down, lambda z, x, c: (z - 1, x, c) if z >= 1 and z - 1 + k < wide else None)
+        came[-k], came[k] = up, down
+    slots = [block]
+    for s in range(wide - 1):
+        slots.append(pick(z, [order[p][s] - p for p in range(wide)], came))
+    across = [to_x(slot) for slot in slots]
+
+    half = block.shape[1]
+    hidden_width = expert_out.shape[0]
+    partial = []
+    for s in range(wide):
+        rows = jnp.where(
+            x == 0,
+            jnp.concatenate([slots[s], across[s]], axis=1),
+            jnp.concatenate([across[s], slots[s]], axis=1),
+        )
+        if s == 0:
+            mixer_rows = lax.dynamic_slice_in_dim(rows, x * frames, frames, 0)
+            gate = gates[0]
+        else:
+            where_from = jnp.asarray([p ^ order[p][s - 1] for p in range(wide)])[z]
+            gate = lax.dynamic_index_in_dim(gates, where_from, 0, keepdims=False)
+        total = None
+        for e, (w_in, w_down) in enumerate(((expert_in, expert_out), (in_other, down_other))):
+            v = jnp.dot(rows, w_in, preferred_element_type=jnp.float32)
+            hidden = jax.nn.silu(v[:, :hidden_width]) * v[:, hidden_width:] * gate[:, e : e + 1]
+            part = jnp.dot(hidden.astype(jnp.bfloat16), w_down, preferred_element_type=jnp.float32)
+            total = part if total is None else total + part
+        partial.append(total)
+
+    sums = [None] * wide
+    for s in reversed(range(wide)):
+        away = lax.dynamic_slice_in_dim(partial[s], (1 - x) * frames, frames, 0)
+        kept = lax.dynamic_slice_in_dim(partial[s], x * frames, frames, 0)
+        sums[s] = kept + to_x(away.astype(jnp.bfloat16)).astype(jnp.float32)
+    got_down = got_up = None
+    for k in range(wide - 1, 0, -1):
+        for side in (-1, 1):
+            table = [1 + order[p].index(p + side * k) if 0 <= p + side * k < wide else None for p in range(wide)]
+            some = next(t for t in table if t is not None)
+            load = pick(z, [some if t is None else t for t in table], sums)
+            got = got_down if side < 0 else got_up
+            if got is not None:
+                load = load + got.astype(jnp.float32)
+            load = load.astype(jnp.bfloat16)
+            if side < 0:
+                got_down = send(load, lambda z, x, c: (z - 1, x, c) if z >= k else None)
+            else:
+                got_up = send(load, lambda z, x, c: (z + 1, x, c) if z + k < wide else None)
+    total = sums[0]
+    if wide > 1:
+        total = total + got_down.astype(jnp.float32) + got_up.astype(jnp.float32)
+    return (mixer_rows.astype(jnp.float32) + total).astype(jnp.bfloat16)
+
+
+def routed_experts(normed, out_proj, expert_in, expert_out, route_ids, route_weights):
     mixer_rows = jnp.dot(
         normed,
         lax.all_gather(out_proj, "narrow", axis=1, tiled=True),
@@ -130,7 +274,7 @@
     picked = returned[flat_ids, positions].reshape(frames_here, topk_count, model_width)
     expert_sum = jnp.einsum("tk,tkd->td", route_weights, picked.astype(jnp.float32))
     layer_out = (mixer_rows.astype(jnp.float32) + expert_sum).astype(jnp.bfloat16)
-    return (layer_out, state_next[None])
+    return layer_out
 
 
 def solution(mesh):

time: 376 us -> 185 us (0.49)
  the two profiles are of different devices: /device:TPU:15 before, /device:TPU:0 now
where the time goes in v2:
time: 185 us; the launch traced here: 184 us
  waiting for transfers between devices  86.6 us (47%)
  starting transfers between devices  43.5 us (24%)
  matrix products  34.5 us (19%)
  other arithmetic  7.57 us (4%)
  between operations  7.05 us (4%)
  local copies, waits for them, and re-layouts  5.14 us (3%)
    ppermute x27, waiting for transfers between devices, send(): return lax.ppermute(value, axes, routes(wide, move))  86.6 us
    ppermute x27, starting transfers between devices, send(): return lax.ppermute(value, axes, routes(wide, move))  43.5 us
    dot_general x8, matrix products, dense_experts(): v = jnp.dot(rows, w_in, preferred_element_type=jnp.float32)  15.5 us
    dot_general x8, matrix products, dense_experts(): jnp.dot(hidden.astype(jnp.bfloat16), w_down, preferred_element_type=jnp.f...  6.35 us
    dot_general x2, matrix products, project(): jnp.dot(rows, out_proj, preferred_element_type=jnp.float32)  4.44 us
    dot_general x2, matrix products, project(): jnp.dot(rows, out_other, preferred_element_type=jnp.float32)  4.44 us
  transfers between devices with their start and end apart: 27, of which 14 were waited for; matrix products, arithmetic and copies ran while one was open for 24% of the time, Pallas kernels for 0%

profile of v2, /device:TPU:0, one launch (start us, length us, event | category | flops | bytes accessed | tf_op | source)
XLA Modules:
  0.0 184.4 jit_solution(8836024790982776028)
XLA Ops:
  3.0 1.3 copy.62
  9.8 1.2 multiply_convert_fusion.2
  10.9 2.5 %collective-permute-start.1 = (bf16[128,2048]{1,0:T(8,128)(2,1)}, bf16[128,2048]{1,0:T(8,128)(2,1)}, u32[]{:S(2)}, u32[]{:S(2)}) collective-permute-start(bf16[128,2048]{1,0:T(8,128)(2,1)} %multiply_convert_fusion.2), channel_id=1, source_target_pairs={{0,2},{1,3},{2,0},{3,1},{4,6},{5,7},{6,4},{7,5},{8,10},{9,11},{10,... | collective-permute-start | bytes 1572872 | tf_op jit(solution)/shard_map/ppermute | solution.py:129
  14.1 2.2 %convolution_convert_fusion.3 = bf16[128,512]{1,0:T(8,128)(2,1)S(1)} fusion(bf16[128,2048]{1,0:T(8,128)(2,1)} %multiply_convert_fusion.2, bf16[2048,512]{1,0:T(8,128)(2,1)} %param.28), kind=kOutput, calls=%fused_computation.18 | convolution fusion | flops 268500992 | bytes 2752512 | tf_op jit(solution)/shard_map/dot_general | solution.py:156
  16.4 10.0 %collective-permute-done.3 = f32[128,16]{0,1:T(8,128)S(1)} collective-permute-done((f32[128,16]{0,1:T(8,128)S(1)}, f32[128,16]{0,1:T(8,128)S(1)}, u32[]{:S(2)}, u32[]{:S(2)}) %collective-permute-start.3) | collective-permute-done | bytes 8224 | tf_op jit(solution)/shard_map/ppermute | solution.py:129
  26.4 1.8 collective-permute-start.4
  35.9 2.7 %collective-permute-start.5 = (f32[2,2,128,16]{2,3,1,0:T(8,128)S(1)}, f32[2,2,128,16]{2,3,1,0:T(8,128)S(1)}, u32[]{:S(2)}, u32[]{:S(2)}) collective-permute-start(f32[2,2,128,16]{2,3,1,0:T(8,128)S(1)} %pad_maximum_fusion.1), channel_id=1, source_target_pairs={{0,8},{1,9},{2,10},{3,11},{4,12},{5,13},{6,14},{7,15},{8,0},{9,1},... | collective-permute-start | bytes 98312 | tf_op jit(solution)/shard_map/ppermute | solution.py:129
  38.5 2.2 %convolution_convert_fusion.1 = bf16[128,512]{1,0:T(8,128)(2,1)S(1)} fusion(bf16[128,2048]{1,0:T(8,128)(2,1)} %collective-permute-done.1, bf16[2048,512]{1,0:T(8,128)(2,1)} %param.28), kind=kOutput, calls=%fused_computation.16 | convolution fusion | flops 268500992 | bytes 2752512 | tf_op jit(solution)/shard_map/dot_general | solution.py:156
  40.8 2.2 %convolution_convert_fusion = bf16[128,512]{1,0:T(8,128)(2,1)S(1)} fusion(bf16[128,2048]{1,0:T(8,128)(2,1)} %collective-permute-done.1, bf16[2048,512]{1,0:T(8,128)(2,1)} %collective-permute-done), kind=kOutput, calls=%fused_computation.15 | convolution fusion | flops 268500992 | bytes 2752512 | tf_op jit(solution)/shard_map/dot_general | solution.py:157
  43.1 2.2 %convolution_convert_fusion.2 = bf16[128,512]{1,0:T(8,128)(2,1)S(1)} fusion(bf16[128,2048]{1,0:T(8,128)(2,1)} %multiply_convert_fusion.2, bf16[2048,512]{1,0:T(8,128)(2,1)} %collective-permute-done), kind=kOutput, calls=%fused_computation.17 | convolution fusion | flops 268500992 | bytes 2752512 | tf_op jit(solution)/shard_map/dot_general | solution.py:157
  45.5 1.4 collective-permute-start.9
  47.0 4.6 %collective-permute-start.10 = (bf16[256,1024]{1,0:T(8,128)(2,1)S(1)}, bf16[256,1024]{1,0:T(8,128)(2,1)S(1)}, u32[]{:S(2)}, u32[]{:S(2)}) collective-permute-start(bf16[256,1024]{1,0:T(8,128)(2,1)S(1)} %maximum_select_fusion.4), channel_id=1, source_target_pairs={{0,4},{1,5},{2,6},{3,7},{4,8},{5,9},{6,10},{7,11},{8,12},{9,13},{1... | collective-permute-start | bytes 1572872 | tf_op jit(solution)/shard_map/ppermute | solution.py:129
  51.7 1.5 collective-permute-start.2
  53.3 7.4 %collective-permute-done.9 = bf16[256,1024]{1,0:T(8,128)(2,1)S(1)} collective-permute-done((bf16[256,1024]{1,0:T(8,128)(2,1)S(1)}, bf16[256,1024]{1,0:T(8,128)(2,1)S(1)}, u32[]{:S(2)}, u32[]{:S(2)}) %collective-permute-start.9) | collective-permute-done | bytes 524320 | tf_op jit(solution)/shard_map/ppermute | solution.py:129
  60.6 1.3 collective-permute-start.13
  62.7 12.0 %collective-permute-done.13 = bf16[256,1024]{1,0:T(8,128)(2,1)S(1)} collective-permute-done((bf16[256,1024]{1,0:T(8,128)(2,1)S(1)}, bf16[256,1024]{1,0:T(8,128)(2,1)S(1)}, u32[]{:S(2)}, u32[]{:S(2)}) %collective-permute-start.13) | collective-permute-done | bytes 524320 | tf_op jit(solution)/shard_map/ppermute | solution.py:129
  74.7 1.3 collective-permute-start.14
  77.3 1.0 fusion.86
  78.2 9.5 %collective-permute-done.14 = bf16[256,1024]{1,0:T(8,128)(2,1)S(1)} collective-permute-done((bf16[256,1024]{1,0:T(8,128)(2,1)S(1)}, bf16[256,1024]{1,0:T(8,128)(2,1)S(1)}, u32[]{:S(2)}, u32[]{:S(2)}) %collective-permute-start.14) | collective-permute-done | bytes 524320 | tf_op jit(solution)/shard_map/ppermute | solution.py:129
  87.9 1.6 collective-permute-start.17
  90.3 2.9 %fusion.104 = f32[256,768]{1,0:T(8,128)S(1)} fusion(bf16[256,2048]{1,0:T(8,128)(2,1)S(1)} %maximum_select_fusion, bf16[2048,768]{1,0:T(8,128)(2,1)} %collective-permute-done.6), kind=kOutput, calls=%fused_computation.165 | convolution fusion | flops 805306368 | bytes 4980736 | tf_op jit(solution)/shard_map/dot_general | solution.py:197
  93.8 1.5 collective-permute-start.11
  95.3 7.6 %collective-permute-done.17 = bf16[256,1024]{1,0:T(8,128)(2,1)S(1)} collective-permute-done((bf16[256,1024]{1,0:T(8,128)(2,1)S(1)}, bf16[256,1024]{1,0:T(8,128)(2,1)S(1)}, u32[]{:S(2)}, u32[]{:S(2)}) %collective-permute-start.17) | collective-permute-done | bytes 524320 | tf_op jit(solution)/shard_map/ppermute | solution.py:129
  102.9 1.0 fusion.65
  104.7 2.9 %fusion.64 = f32[256,768]{1,0:T(8,128)S(1)} fusion(bf16[2048,768]{1,0:T(8,128)(2,1)} %collective-permute-done.6, bf16[256,1024]{1,0:T(8,128)(2,1)S(1)} %collective-permute-done.17, bf16[256,1024]{1,0:T(8,128)(2,1)S(1)} %get-tuple-element.7, pred[]{:T(512)S(6)} %eq.24), kind=kOutput, calls=%fused_computation.104 | convolution fusion | flops 810024960 | bytes 4980737 | tf_op jit(solution)/shard_map/dot_general | solution.py:197
  108.5 1.6 collective-permute-start.18
  110.0 4.1 %collective-permute-done.19 = bf16[256,1024]{1,0:T(8,128)(2,1)S(1)} collective-permute-done((bf16[256,1024]{1,0:T(8,128)(2,1)S(1)}, bf16[256,1024]{1,0:T(8,128)(2,1)S(1)}, u32[]{:S(2)}, u32[]{:S(2)}) %collective-permute-start.19) | collective-permute-done | bytes 524320 | tf_op jit(solution)/shard_map/ppermute | solution.py:129
  114.1 1.0 fusion.63
  115.9 2.9 %fusion.62 = f32[256,768]{1,0:T(8,128)S(1)} fusion(bf16[2048,768]{1,0:T(8,128)(2,1)} %collective-permute-done.6, bf16[256,1024]{1,0:T(8,128)(2,1)S(1)} %collective-permute-done.19, bf16[256,1024]{1,0:T(8,128)(2,1)S(1)} %get-tuple-element.6, pred[]{:T(512)S(6)} %eq.24), kind=kOutput, calls=%fused_computation.102 | convolution fusion | flops 810024960 | bytes 4980737 | tf_op jit(solution)/shard_map/dot_general | solution.py:197
  119.7 1.6 collective-permute-start.20
  121.2 4.1 %collective-permute-done.11 = bf16[256,1024]{1,0:T(8,128)(2,1)S(1)} collective-permute-done((bf16[256,1024]{1,0:T(8,128)(2,1)S(1)}, bf16[256,1024]{1,0:T(8,128)(2,1)S(1)}, u32[]{:S(2)}, u32[]{:S(2)}) %collective-permute-start.11) | collective-permute-done | bytes 524320 | tf_op jit(solution)/shard_map/ppermute | solution.py:129
  125.3 1.0 fusion.67
  127.1 2.9 %fusion.66 = f32[256,768]{1,0:T(8,128)S(1)} fusion(bf16[2048,768]{1,0:T(8,128)(2,1)} %collective-permute-done.6, bf16[256,1024]{1,0:T(8,128)(2,1)S(1)} %collective-permute-done.11, bf16[256,1024]{1,0:T(8,128)(2,1)S(1)} %get-tuple-element.8, pred[]{:T(512)S(6)} %eq.24), kind=kOutput, calls=%fused_computation.106 | convolution fusion | flops 810024960 | bytes 4980737 | tf_op jit(solution)/shard_map/dot_general | solution.py:197
  130.0 6.6 %collective-permute-done.18 = bf16[128,2048]{1,0:T(8,128)(2,1)S(1)} collective-permute-done((bf16[128,2048]{1,0:T(8,128)(2,1)S(1)}, bf16[128,2048]{1,0:T(8,128)(2,1)S(1)}, u32[]{:S(2)}, u32[]{:S(2)}) %collective-permute-start.18) | collective-permute-done | bytes 524320 | tf_op jit(solution)/shard_map/ppermute | solution.py:129
  137.4 1.7 collective-permute-start.24
  140.0 1.6 collective-permute-start.12
  141.6 6.2 %collective-permute-done.20 = bf16[128,2048]{1,0:T(8,128)(2,1)S(1)} collective-permute-done((bf16[128,2048]{1,0:T(8,128)(2,1)S(1)}, bf16[128,2048]{1,0:T(8,128)(2,1)S(1)}, u32[]{:S(2)}, u32[]{:S(2)}) %collective-permute-start.20) | collective-permute-done | bytes 524320 | tf_op jit(solution)/shard_map/ppermute | solution.py:129
  147.8 1.0 collective-permute-done.24
  150.0 5.0 %collective-permute-start.25 = (bf16[128,2048]{1,0:T(8,128)(2,1)S(1)}, bf16[128,2048]{1,0:T(8,128)(2,1)S(1)}, u32[]{:S(2)}, u32[]{:S(2)}) collective-permute-start(bf16[128,2048]{1,0:T(8,128)(2,1)S(1)} %get-tuple-element.3), channel_id=1, source_target_pairs={{0,4},{1,5},{2,6},{3,7},{4,8},{5,9},{6,10},{7,11},{16,20},{17,21},... | collective-permute-start | bytes 1572872 | tf_op jit(solution)/shard_map/ppermute | solution.py:129
  156.0 1.6 collective-permute-start.8
  157.5 1.5 collective-permute-done.12
  159.1 8.1 %collective-permute-done.25 = bf16[128,2048]{1,0:T(8,128)(2,1)S(1)} collective-permute-done((bf16[128,2048]{1,0:T(8,128)(2,1)S(1)}, bf16[128,2048]{1,0:T(8,128)(2,1)S(1)}, u32[]{:S(2)}, u32[]{:S(2)}) %collective-permute-start.25) | collective-permute-done | bytes 524320 | tf_op jit(solution)/shard_map/ppermute | solution.py:129
  167.7 4.4 %collective-permute-start.26 = (bf16[128,2048]{1,0:T(8,128)(2,1)S(1)}, bf16[128,2048]{1,0:T(8,128)(2,1)S(1)}, u32[]{:S(2)}, u32[]{:S(2)}) collective-permute-start(bf16[128,2048]{1,0:T(8,128)(2,1)S(1)} %get-tuple-element.5), channel_id=1, source_target_pairs={{0,4},{1,5},{2,6},{3,7},{4,8},{5,9},{6,10},{7,11},{8,12},{9,13},{1... | collective-permute-start | bytes 1572872 | tf_op jit(solution)/shard_map/ppermute | solution.py:129
  172.1 1.3 collective-permute-start.23
  173.4 1.3 fusion.2
  174.7 4.0 %collective-permute-done.26 = bf16[128,2048]{1,0:T(8,128)(2,1)S(1)} collective-permute-done((bf16[128,2048]{1,0:T(8,128)(2,1)S(1)}, bf16[128,2048]{1,0:T(8,128)(2,1)S(1)}, u32[]{:S(2)}, u32[]{:S(2)}) %collective-permute-start.26) | collective-permute-done | bytes 524320 | tf_op jit(solution)/shard_map/ppermute | solution.py:129
  178.7 4.4 %collective-permute-done.23 = bf16[128,2048]{1,0:T(8,128)(2,1)S(1)} collective-permute-done((bf16[128,2048]{1,0:T(8,128)(2,1)S(1)}, bf16[128,2048]{1,0:T(8,128)(2,1)S(1)}, u32[]{:S(2)}, u32[]{:S(2)}) %collective-permute-start.23) | collective-permute-done | bytes 524320 | tf_op jit(solution)/shard_map/ppermute | solution.py:129
  183.2 1.2 add_convert_fusion
  (108 shorter events, 22.6 us)
Async XLA Ops:
  0.6 4.7 %copy-start = (bf16[128,128]{1,0:T(8,128)(2,1)S(1)}, bf16[128,128]{1,0:T(8,128)(2,1)}, u32[]{:S(2)}) copy-start(bf16[128,128]{1,0:T(8,128)(2,1)} %param.21) | copy-start | bytes 98308
  0.6 40.1 %collective-permute-start = (bf16[2048,512]{1,0:T(8,128)(2,1)}, bf16[2048,512]{1,0:T(8,128)(2,1)}, u32[]{:S(2)}, u32[]{:S(2)}) collective-permute-start(bf16[2048,512]{1,0:T(8,128)(2,1)} %param.28), channel_id=1, source_target_pairs={{0,1},{1,0},{2,3},{3,2},{4,5},{5,4},{6,7},{7,6},{8,9},{9,8},{10,11... | collective-permute-start | bytes 6291464 | tf_op jit(solution)/shard_map/ppermute | solution.py:129
  4.4 2.9 %copy-start.2 = (bf16[128,2048]{0,1:T(8,128)(2,1)}, bf16[128,2048]{0,1:T(8,128)(2,1)S(1)}, u32[]{:S(2)}) copy-start(bf16[128,2048]{0,1:T(8,128)(2,1)S(1)} %copy.62) | copy-start | bytes 1572868
  6.3 1.3 copy-start.4
  6.3 1.3 copy-start.11
  8.2 1.0 copy-start.6
  8.2 1.5 copy-start.8
  9.2 4.2 %copy-start.9 = (f32[128,8]{0,1:T(8,128)S(1)}, f32[128,8]{0,1:T(8,128)}, u32[]{:S(2)}) copy-start(f32[128,8]{0,1:T(8,128)} %param.32) | copy-start | bytes 12292
  9.3 4.2 %copy-start.10 = (s32[128,8]{0,1:T(8,128)S(1)}, s32[128,8]{0,1:T(8,128)}, u32[]{:S(2)}) copy-start(s32[128,8]{0,1:T(8,128)} %param.31) | copy-start | bytes 12292
  9.3 4.3 %copy-start.1 = (bf16[1,384,2048]{2,1,0:T(8,128)(2,1)S(1)}, bf16[1,384,2048]{2,1,0:T(8,128)(2,1)}, u32[]{:S(2)}) copy-start(bf16[1,384,2048]{2,1,0:T(8,128)(2,1)} %param.30) | copy-start | bytes 4718596
  9.7 18.6 %copy-start.15 = (s32[4]{0:T(128)S(1)}, s32[4]{0:T(128)}, u32[]{:S(2)}) copy-start(s32[4]{0:T(128)} %constant.77.clone) | copy-start | bytes 52
  9.7 20.4 %copy-start.14 = (s32[4]{0:T(128)S(1)}, s32[4]{0:T(128)}, u32[]{:S(2)}) copy-start(s32[4]{0:T(128)} %constant.78.clone) | copy-start | bytes 52
  9.7 22.3 %copy-start.13 = (s32[4]{0:T(128)S(1)}, s32[4]{0:T(128)}, u32[]{:S(2)}) copy-start(s32[4]{0:T(128)} %constant.79.clone) | copy-start | bytes 52
  10.9 27.6 %collective-permute-start.1 = (bf16[128,2048]{1,0:T(8,128)(2,1)}, bf16[128,2048]{1,0:T(8,128)(2,1)}, u32[]{:S(2)}, u32[]{:S(2)}) collective-permute-start(bf16[128,2048]{1,0:T(8,128)(2,1)} %multiply_convert_fusion.2), channel_id=1, source_target_pairs={{0,2},{1,3},{2,0},{3,1},{4,6},{5,7},{6,4},{7,5},{8,10},{9,11},{10,... | collective-permute-start | bytes 1572872 | tf_op jit(solution)/shard_map/ppermute | solution.py:129
  13.4 13.0 %collective-permute-start.3 = (f32[128,16]{0,1:T(8,128)S(1)}, f32[128,16]{0,1:T(8,128)S(1)}, u32[]{:S(2)}, u32[]{:S(2)}) collective-permute-start(f32[128,16]{0,1:T(8,128)S(1)} %select_reduce_fusion.1), channel_id=1, source_target_pairs={{0,2},{1,3},{2,0},{3,1},{4,6},{5,7},{6,4},{7,5},{8,10},{9,11},{10,... | collective-permute-start | bytes 24584 | tf_op jit(solution)/shard_map/ppermute | solution.py:129
  13.5 94.0 %collective-permute-start.7 = (bf16[384,2048]{1,0:T(8,128)(2,1)S(1)}, bf16[384,2048]{1,0:T(8,128)(2,1)S(1)}, u32[]{:S(2)}, u32[]{:S(2)}) collective-permute-start(bf16[384,2048]{1,0:T(8,128)(2,1)S(1)} %bitcast.92), channel_id=1, source_target_pairs={{0,1},{1,0},{2,3},{3,2},{4,5},{5,4},{6,7},{7,6},{8,9},{9,8},{10,11... | collective-permute-start | bytes 4718600 | tf_op jit(solution)/shard_map/ppermute | solution.py:129
  13.8 76.4 %collective-permute-start.6 = (bf16[2048,768]{1,0:T(8,128)(2,1)}, bf16[2048,768]{1,0:T(8,128)(2,1)}, u32[]{:S(2)}, u32[]{:S(2)}) collective-permute-start(bf16[2048,768]{1,0:T(8,128)(2,1)} %bitcast.107), channel_id=1, source_target_pairs={{0,1},{1,0},{2,3},{3,2},{4,5},{5,4},{6,7},{7,6},{8,9},{9,8},{10,11... | collective-permute-start | bytes 9437192 | tf_op jit(solution)/shard_map/ppermute | solution.py:129
  26.4 9.4 %collective-permute-start.4 = (f32[1,2,128,16]{2,3,1,0:T(8,128)S(1)}, f32[1,2,128,16]{2,3,1,0:T(8,128)S(1)}, u32[]{:S(2)}, u32[]{:S(2)}) collective-permute-start(f32[1,2,128,16]{2,3,1,0:T(8,128)S(1)} %maximum_bitcast_fusion), channel_id=1, source_target_pairs={{0,4},{1,5},{2,6},{3,7},{4,0},{5,1},{6,2},{7,3},{8,12},{9,13},{10,... | collective-permute-start | bytes 49160 | tf_op jit(solution)/shard_map/ppermute | solution.py:129
  35.9 15.7 %collective-permute-start.5 = (f32[2,2,128,16]{2,3,1,0:T(8,128)S(1)}, f32[2,2,128,16]{2,3,1,0:T(8,128)S(1)}, u32[]{:S(2)}, u32[]{:S(2)}) collective-permute-start(f32[2,2,128,16]{2,3,1,0:T(8,128)S(1)} %pad_maximum_fusion.1), channel_id=1, source_target_pairs={{0,8},{1,9},{2,10},{3,11},{4,12},{5,13},{6,14},{7,15},{8,0},{9,1},... | collective-permute-start | bytes 98312 | tf_op jit(solution)/shard_map/ppermute | solution.py:129
  45.3 32.0 %copy-start.12 = (bf16[1,2048,768]{2,1,0:T(8,128)(2,1)S(1)}, bf16[1,2048,768]{2,1,0:T(8,128)(2,1)}, u32[]{:S(2)}) copy-start(bf16[1,2048,768]{2,1,0:T(8,128)(2,1)} %param.29) | copy-start | bytes 9437188
  45.5 15.1 %collective-permute-start.9 = (bf16[256,1024]{1,0:T(8,128)(2,1)S(1)}, bf16[256,1024]{1,0:T(8,128)(2,1)S(1)}, u32[]{:S(2)}, u32[]{:S(2)}) collective-permute-start(bf16[256,1024]{1,0:T(8,128)(2,1)S(1)} %maximum_select_fusion.4), channel_id=1, source_target_pairs={{4,0},{5,1},{6,2},{7,3},{8,4},{9,5},{10,6},{11,7},{12,8},{13,9},{1... | collective-permute-start | bytes 1572872 | tf_op jit(solution)/shard_map/ppermute | solution.py:129
  47.0 15.0 %collective-permute-start.10 = (bf16[256,1024]{1,0:T(8,128)(2,1)S(1)}, bf16[256,1024]{1,0:T(8,128)(2,1)S(1)}, u32[]{:S(2)}, u32[]{:S(2)}) collective-permute-start(bf16[256,1024]{1,0:T(8,128)(2,1)S(1)} %maximum_select_fusion.4), channel_id=1, source_target_pairs={{0,4},{1,5},{2,6},{3,7},{4,8},{5,9},{6,10},{7,11},{8,12},{9,13},{1... | collective-permute-start | bytes 1572872 | tf_op jit(solution)/shard_map/ppermute | solution.py:129
  51.7 25.1 %collective-permute-start.2 = (bf16[256,1024]{1,0:T(8,128)(2,1)S(1)}, bf16[256,1024]{1,0:T(8,128)(2,1)S(1)}, u32[]{:S(2)}, u32[]{:S(2)}) collective-permute-start(bf16[256,1024]{1,0:T(8,128)(2,1)S(1)} %maximum_select_fusion.4), channel_id=1, source_target_pairs={{0,2},{1,3},{2,0},{3,1},{4,6},{5,7},{6,4},{7,5},{8,10},{9,11},{10,... | collective-permute-start | bytes 1572872 | tf_op jit(solution)/shard_map/ppermute | solution.py:129
  60.6 14.0 %collective-permute-start.13 = (bf16[256,1024]{1,0:T(8,128)(2,1)S(1)}, bf16[256,1024]{1,0:T(8,128)(2,1)S(1)}, u32[]{:S(2)}, u32[]{:S(2)}) collective-permute-start(bf16[256,1024]{1,0:T(8,128)(2,1)S(1)} %collective-permute-done.9), channel_id=1, source_target_pairs={{4,0},{5,1},{6,2},{7,3},{8,4},{9,5},{10,6},{11,7},{20,16},{21,17},... | collective-permute-start | bytes 1572872 | tf_op jit(solution)/shard_map/ppermute | solution.py:129
  61.9 14.0 %collective-permute-start.15 = (bf16[256,1024]{1,0:T(8,128)(2,1)S(1)}, bf16[256,1024]{1,0:T(8,128)(2,1)S(1)}, u32[]{:S(2)}, u32[]{:S(2)}) collective-permute-start(bf16[256,1024]{1,0:T(8,128)(2,1)S(1)} %collective-permute-done.10), channel_id=1, source_target_pairs={{4,8},{5,9},{6,10},{7,11},{8,12},{9,13},{10,14},{11,15},{20,24},{2... | collective-permute-start | bytes 1572872 | tf_op jit(solution)/shard_map/ppermute | solution.py:129
  74.7 13.1 %collective-permute-start.14 = (bf16[256,1024]{1,0:T(8,128)(2,1)S(1)}, bf16[256,1024]{1,0:T(8,128)(2,1)S(1)}, u32[]{:S(2)}, u32[]{:S(2)}) collective-permute-start(bf16[256,1024]{1,0:T(8,128)(2,1)S(1)} %collective-permute-done.13), channel_id=1, source_target_pairs={{4,0},{5,1},{6,2},{7,3},{20,16},{21,17},{22,18},{23,19}} | collective-permute-start | bytes 1572872 | tf_op jit(solution)/shard_map/ppermute | solution.py:129
  76.0 11.8 %collective-permute-start.16 = (bf16[256,1024]{1,0:T(8,128)(2,1)S(1)}, bf16[256,1024]{1,0:T(8,128)(2,1)S(1)}, u32[]{:S(2)}, u32[]{:S(2)}) collective-permute-start(bf16[256,1024]{1,0:T(8,128)(2,1)S(1)} %collective-permute-done.15), channel_id=1, source_target_pairs={{8,12},{9,13},{10,14},{11,15},{24,28},{25,29},{26,30},{27,31}} | collective-permute-start | bytes 1572872 | tf_op jit(solution)/shard_map/ppermute | solution.py:129
  87.9 14.9 %collective-permute-start.17 = (bf16[256,1024]{1,0:T(8,128)(2,1)S(1)}, bf16[256,1024]{1,0:T(8,128)(2,1)S(1)}, u32[]{:S(2)}, u32[]{:S(2)}) collective-permute-start(bf16[256,1024]{1,0:T(8,128)(2,1)S(1)} %get-tuple-element.7), channel_id=1, source_target_pairs={{0,2},{1,3},{2,0},{3,1},{4,6},{5,7},{6,4},{7,5},{8,10},{9,11},{10,... | collective-permute-start | bytes 1572872 | tf_op jit(solution)/shard_map/ppermute | solution.py:129
  93.2 20.9 %collective-permute-start.19 = (bf16[256,1024]{1,0:T(8,128)(2,1)S(1)}, bf16[256,1024]{1,0:T(8,128)(2,1)S(1)}, u32[]{:S(2)}, u32[]{:S(2)}) collective-permute-start(bf16[256,1024]{1,0:T(8,128)(2,1)S(1)} %get-tuple-element.6), channel_id=1, source_target_pairs={{0,2},{1,3},{2,0},{3,1},{4,6},{5,7},{6,4},{7,5},{8,10},{9,11},{10,... | collective-permute-start | bytes 1572872 | tf_op jit(solution)/shard_map/ppermute | solution.py:129
  93.8 31.5 %collective-permute-start.11 = (bf16[256,1024]{1,0:T(8,128)(2,1)S(1)}, bf16[256,1024]{1,0:T(8,128)(2,1)S(1)}, u32[]{:S(2)}, u32[]{:S(2)}) collective-permute-start(bf16[256,1024]{1,0:T(8,128)(2,1)S(1)} %get-tuple-element.8), channel_id=1, source_target_pairs={{0,2},{1,3},{2,0},{3,1},{4,6},{5,7},{6,4},{7,5},{8,10},{9,11},{10,... | collective-permute-start | bytes 1572872 | tf_op jit(solution)/shard_map/ppermute | solution.py:129
  108.5 28.1 %collective-permute-start.18 = (bf16[128,2048]{1,0:T(8,128)(2,1)S(1)}, bf16[128,2048]{1,0:T(8,128)(2,1)S(1)}, u32[]{:S(2)}, u32[]{:S(2)}) collective-permute-start(bf16[128,2048]{1,0:T(8,128)(2,1)S(1)} %dynamic-slice_convert_fusion.1), channel_id=1, source_target_pairs={{0,2},{1,3},{2,0},{3,1},{4,6},{5,7},{6,4},{7,5},{8,10},{9,11},{10,... | collective-permute-start | bytes 1572872 | tf_op jit(solution)/shard_map/ppermute | solution.py:129
  119.7 28.1 %collective-permute-start.20 = (bf16[128,2048]{1,0:T(8,128)(2,1)S(1)}, bf16[128,2048]{1,0:T(8,128)(2,1)S(1)}, u32[]{:S(2)}, u32[]{:S(2)}) collective-permute-start(bf16[128,2048]{1,0:T(8,128)(2,1)S(1)} %dynamic-slice_convert_fusion), channel_id=1, source_target_pairs={{0,2},{1,3},{2,0},{3,1},{4,6},{5,7},{6,4},{7,5},{8,10},{9,11},{10,... | collective-permute-start | bytes 1572872 | tf_op jit(solution)/shard_map/ppermute | solution.py:129
  136.7 11.1 %collective-permute-start.21 = (bf16[128,2048]{1,0:T(8,128)(2,1)S(1)}, bf16[128,2048]{1,0:T(8,128)(2,1)S(1)}, u32[]{:S(2)}, u32[]{:S(2)}) collective-permute-start(bf16[128,2048]{1,0:T(8,128)(2,1)S(1)} %fusion.33), channel_id=1, source_target_pairs={{12,8},{13,9},{14,10},{15,11},{28,24},{29,25},{30,26},{31,27}} | collective-permute-start | bytes 1572872 | tf_op jit(solution)/shard_map/ppermute | solution.py:129
  137.4 11.4 %collective-permute-start.24 = (bf16[128,2048]{1,0:T(8,128)(2,1)S(1)}, bf16[128,2048]{1,0:T(8,128)(2,1)S(1)}, u32[]{:S(2)}, u32[]{:S(2)}) collective-permute-start(bf16[128,2048]{1,0:T(8,128)(2,1)S(1)} %fusion.33), channel_id=1, source_target_pairs={{0,4},{1,5},{2,6},{3,7},{16,20},{17,21},{18,22},{19,23}} | collective-permute-start | bytes 1572872 | tf_op jit(solution)/shard_map/ppermute | solution.py:129
  140.0 19.0 %collective-permute-start.12 = (bf16[128,2048]{1,0:T(8,128)(2,1)S(1)}, bf16[128,2048]{1,0:T(8,128)(2,1)S(1)}, u32[]{:S(2)}, u32[]{:S(2)}) collective-permute-start(bf16[128,2048]{1,0:T(8,128)(2,1)S(1)} %dynamic-slice_convert_fusion.2), channel_id=1, source_target_pairs={{0,2},{1,3},{2,0},{3,1},{4,6},{5,7},{6,4},{7,5},{8,10},{9,11},{10,... | collective-permute-start | bytes 1572872 | tf_op jit(solution)/shard_map/ppermute | solution.py:129
  149.3 9.7 %collective-permute-start.22 = (bf16[128,2048]{1,0:T(8,128)(2,1)S(1)}, bf16[128,2048]{1,0:T(8,128)(2,1)S(1)}, u32[]{:S(2)}, u32[]{:S(2)}) collective-permute-start(bf16[128,2048]{1,0:T(8,128)(2,1)S(1)} %get-tuple-element.2), channel_id=1, source_target_pairs={{8,4},{9,5},{10,6},{11,7},{12,8},{13,9},{14,10},{15,11},{24,20},{2... | collective-permute-start | bytes 1572872 | tf_op jit(solution)/shard_map/ppermute | solution.py:129
  150.0 17.1 %collective-permute-start.25 = (bf16[128,2048]{1,0:T(8,128)(2,1)S(1)}, bf16[128,2048]{1,0:T(8,128)(2,1)S(1)}, u32[]{:S(2)}, u32[]{:S(2)}) collective-permute-start(bf16[128,2048]{1,0:T(8,128)(2,1)S(1)} %get-tuple-element.3), channel_id=1, source_target_pairs={{0,4},{1,5},{2,6},{3,7},{4,8},{5,9},{6,10},{7,11},{16,20},{17,21},... | collective-permute-start | bytes 1572872 | tf_op jit(solution)/shard_map/ppermute | solution.py:129
  155.9 17.5 %copy-start.3 = (bf16[128,2048]{0,1:T(8,128)(2,1)S(1)}, bf16[128,2048]{0,1:T(8,128)(2,1)}, u32[]{:S(2)}) copy-start(bf16[128,2048]{0,1:T(8,128)(2,1)} %copy-done.2) | copy-start | bytes 1572868
  156.0 17.4 %copy-start.5 = (f32[1,32,64,128]{3,2,1,0:T(8,128)S(1)}, f32[1,32,64,128]{3,2,1,0:T(8,128)}, u32[]{:S(2)}) copy-start(f32[1,32,64,128]{3,2,1,0:T(8,128)} %param.27) | copy-start | bytes 3145732
  156.0 17.4 %copy-start.7 = (bf16[128,128]{1,0:T(8,128)(2,1)S(1)}, bf16[128,128]{1,0:T(8,128)(2,1)}, u32[]{:S(2)}) copy-start(bf16[128,128]{1,0:T(8,128)(2,1)} %param.20) | copy-start | bytes 98308
  156.0 18.7 %collective-permute-start.8 = (bf16[128,2048]{1,0:T(8,128)(2,1)S(1)}, bf16[128,2048]{1,0:T(8,128)(2,1)S(1)}, u32[]{:S(2)}, u32[]{:S(2)}) collective-permute-start(bf16[128,2048]{1,0:T(8,128)(2,1)S(1)} %dynamic-slice_convert_fusion.3), channel_id=1, source_target_pairs={{0,2},{1,3},{2,0},{3,1},{4,6},{5,7},{6,4},{7,5},{8,10},{9,11},{10,... | collective-permute-start | bytes 1572872 | tf_op jit(solution)/shard_map/ppermute | solution.py:129
  167.7 11.1 %collective-permute-start.26 = (bf16[128,2048]{1,0:T(8,128)(2,1)S(1)}, bf16[128,2048]{1,0:T(8,128)(2,1)S(1)}, u32[]{:S(2)}, u32[]{:S(2)}) collective-permute-start(bf16[128,2048]{1,0:T(8,128)(2,1)S(1)} %get-tuple-element.5), channel_id=1, source_target_pairs={{0,4},{1,5},{2,6},{3,7},{4,8},{5,9},{6,10},{7,11},{8,12},{9,13},{1... | collective-permute-start | bytes 1572872 | tf_op jit(solution)/shard_map/ppermute | solution.py:129
  172.1 11.1 %collective-permute-start.23 = (bf16[128,2048]{1,0:T(8,128)(2,1)S(1)}, bf16[128,2048]{1,0:T(8,128)(2,1)S(1)}, u32[]{:S(2)}, u32[]{:S(2)}) collective-permute-start(bf16[128,2048]{1,0:T(8,128)(2,1)S(1)} %get-tuple-element.4), channel_id=1, source_target_pairs={{4,0},{5,1},{6,2},{7,3},{8,4},{9,5},{10,6},{11,7},{12,8},{13,9},{1... | collective-permute-start | bytes 1572872 | tf_op jit(solution)/shard_map/ppermute | solution.py:129

commit v3 on v0

--- a/solution.py
+++ b/solution.py
@@ -82,6 +82,157 @@
         norm_gain,
         state_in[0],
     )
+    frames_here, topk_count = route_ids.shape
+    local_experts = expert_in.shape[0]
+    experts = local_experts * lax.axis_size(("wide", "narrow"))
+    wide, narrow = lax.axis_size("wide"), lax.axis_size("narrow")
+    if experts <= 4 * topk_count and narrow == 4 and wide & (wide - 1) == 0 and local_experts == 1:
+        layer_out = dense_experts(
+            normed, out_proj, expert_in[0], expert_out[0], route_ids, route_weights
+        )
+    else:
+        layer_out = routed_experts(normed, out_proj, expert_in, expert_out, route_ids, route_weights)
+    return (layer_out, state_next[None])
+
+
+def routes(wide, move):
+    pairs = []
+    for z in range(wide):
+        for x in range(2):
+            for core in range(2):
+                to = move(z, x, core)
+                pairs.append(((z * 2 + x) * 2 + core, (to[0] * 2 + to[1]) * 2 + to[2]))
+    return pairs
+
+
+def dense_experts(normed, out_proj, expert_in, expert_out, route_ids, route_weights):
+    frames = route_ids.shape[0]
+    wide = lax.axis_size("wide")
+    ring = 2 * wide
+    z = lax.axis_index("wide")
+    x, core = lax.axis_index("narrow") // 2, lax.axis_index("narrow") % 2
+    place = jnp.where(x == 0, z, ring - 1 - z)
+    axes = ("wide", "narrow")
+
+    def send(value, move):
+        return lax.ppermute(value, axes, routes(wide, move))
+
+    def to_core(value):
+        return send(value, lambda z, x, c: (z, x, 1 - c))
+
+    def to_x(value):
+        return send(value, lambda z, x, c: (z, 1 - x, c))
+
+    def along(value, step):
+        def move(z, x, c):
+            p = ((z if x == 0 else ring - 1 - z) + step) % ring
+            return (p, 0, c) if p < wide else (ring - 1 - p, 1, c)
+
+        return send(value, move)
+
+    out_other, in_other, down_other = to_core(out_proj), to_core(expert_in), to_core(expert_out)
+
+    experts = wide * 4
+    gates = jnp.sum(
+        jnp.where(route_ids[:, :, None] == jnp.arange(experts), route_weights[:, :, None], 0.0), axis=1
+    )
+    other = to_x(gates)
+    gates = jnp.where(x == 0, jnp.stack([gates, other]), jnp.stack([other, gates]))[:, None]
+    step = 1
+    while step < wide:
+        other = send(gates, lambda z, x, c: (z ^ step, x, c))
+        low = z & step == 0
+        gates = jnp.where(
+            low, jnp.concatenate([gates, other], axis=1), jnp.concatenate([other, gates], axis=1)
+        )
+        step *= 2
+    normed, gates = lax.optimization_barrier((normed, gates))
+    mine = (z * 2 + x) * 2 + core
+    pair = jnp.stack([mine, mine + 1 - 2 * core])
+    gates = jnp.sum(
+        jnp.where(pair[:, None] == jnp.arange(experts), gates[..., None, :], 0.0), axis=-1
+    )
+    gates = jnp.concatenate([gates[0], gates[1, ::-1]])
+    gates = lax.dynamic_slice_in_dim(jnp.concatenate([gates, gates]), place, ring, 0)
+
+    def project(rows):
+        first = jnp.dot(rows, out_proj, preferred_element_type=jnp.float32).astype(jnp.bfloat16)
+        second = jnp.dot(rows, out_other, preferred_element_type=jnp.float32).astype(jnp.bfloat16)
+        return jnp.where(
+            core == 0,
+            jnp.concatenate([first, second], axis=1),
+            jnp.concatenate([second, first], axis=1),
+        )
+
+    halves = range(2)
+    size = frames // 2
+    sent = [to_x(normed[h * size : (h + 1) * size]) for h in halves]
+    own = project(normed)
+    rows = []
+    for h in halves:
+        back = to_x(project(sent[h]))
+        here = own[h * size : (h + 1) * size]
+        rows.append(
+            jnp.where(
+                x == 0,
+                jnp.concatenate([here, back], axis=1),
+                jnp.concatenate([back, here], axis=1),
+            )
+        )
+
+    *rows, in_other, down_other = lax.optimization_barrier((*rows, in_other, down_other))
+    hidden_width = expert_out.shape[0]
+
+    def run_experts(rows, gate):
+        total = None
+        for e, (w_in, w_down) in enumerate(((expert_in, expert_out), (in_other, down_other))):
+            v = jnp.dot(rows, w_in, preferred_element_type=jnp.float32)
+            hidden = jax.nn.silu(v[:, :hidden_width]) * v[:, hidden_width:] * gate[:, e : e + 1]
+            part = jnp.dot(hidden.astype(jnp.bfloat16), w_down, preferred_element_type=jnp.float32)
+            total = part if total is None else total + part
+        return total
+
+    fore, back = list(rows), list(rows)
+    total = run_experts(jnp.concatenate(rows), gates[0])
+    mixer_rows = rows
+    ahead, behind = {}, {}
+    for h in halves:
+        ahead[0, h] = total[h * size : (h + 1) * size]
+    far = ring // 2
+    for k in range(1, far):
+        for h in halves:
+            fore[h] = along(fore[h], 1)
+            back[h] = along(back[h], -1)
+        total = run_experts(
+            jnp.concatenate([back[0], back[1], fore[0], fore[1]]),
+            jnp.concatenate([gates[k], gates[ring - k]]),
+        )
+        for h in halves:
+            ahead[k, h] = total[h * size : (h + 1) * size]
+            behind[k, h] = total[frames + h * size : frames + (h + 1) * size]
+    last = [along(fore[0], 1), along(back[1], -1)]
+    total = run_experts(jnp.concatenate(last), gates[far])
+
+    fore = [along(total[:size].astype(jnp.bfloat16), 1), None]
+    back = [None, along(total[size:].astype(jnp.bfloat16), -1)]
+    for k in range(far - 1, 0, -1):
+        for h in halves:
+            load = ahead[k, h]
+            if fore[h] is not None:
+                load = load + fore[h].astype(jnp.float32)
+            fore[h] = along(load.astype(jnp.bfloat16), 1)
+            load = behind[k, h]
+            if back[h] is not None:
+                load = load + back[h].astype(jnp.float32)
+            back[h] = along(load.astype(jnp.bfloat16), -1)
+    out = []
+    for h in halves:
+        total = ahead[0, h] + fore[h].astype(jnp.float32) + back[h].astype(jnp.float32)
+        out.append((mixer_rows[h].astype(jnp.float32) + total).astype(jnp.bfloat16))
+    return jnp.concatenate(out)
+
+
+def routed_experts(normed, out_proj, expert_in, expert_out, route_ids, route_weights):
     mixer_rows = jnp.dot(
         normed,
         lax.all_gather(out_proj, "narrow", axis=1, tiled=True),
@@ -130,7 +281,7 @@
     picked = returned[flat_ids, positions].reshape(frames_here, topk_count, model_width)
     expert_sum = jnp.einsum("tk,tkd->td", route_weights, picked.astype(jnp.float32))
     layer_out = (mixer_rows.astype(jnp.float32) + expert_sum).astype(jnp.bfloat16)
-    return (layer_out, state_next[None])
+    return layer_out
 
 
 def solution(mesh):

time: 376 us -> 158 us (0.42)
  the two profiles are of different devices: /device:TPU:15 before, /device:TPU:0 now
where the time goes in v3:
time: 158 us; the launch traced here: 157 us
  waiting for transfers between devices  63.3 us (40%)
  starting transfers between devices  40.9 us (26%)
  matrix products  39.7 us (25%)
  other arithmetic  7.6 us (5%)
  local copies, waits for them, and re-layouts  4.05 us (3%)
    ppermute x38, waiting for transfers between devices, send(): return lax.ppermute(value, axes, routes(wide, move))  63.3 us
    ppermute x38, starting transfers between devices, send(): return lax.ppermute(value, axes, routes(wide, move))  40.9 us
    dot_general x10, matrix products, run_experts(): v = jnp.dot(rows, w_in, preferred_element_type=jnp.float32)  17.8 us
    dot_general x10, matrix products, run_experts(): jnp.dot(hidden.astype(jnp.bfloat16), w_down, preferred_element_type=jnp.f...  6.7 us
    dot_general x3, matrix products, project(): jnp.dot(rows, out_other, preferred_element_type=jnp.float32)  6.16 us
  transfers between devices with their start and end apart: 38, of which 25 were waited for; matrix products, arithmetic and copies ran while one was open for 20% of the time, Pallas kernels for 0%

profile of v3, /device:TPU:0, one launch (start us, length us, event | category | flops | bytes accessed | tf_op | source)
XLA Modules:
  0.0 157.0 jit_solution(14400898324742620497)
XLA Ops:
  1.4 3.0 %collective-permute-start = (f32[128,16]{0,1:T(8,128)S(1)}, f32[128,16]{0,1:T(8,128)S(1)}, u32[]{:S(2)}, u32[]{:S(2)}) collective-permute-start(f32[128,16]{0,1:T(8,128)S(1)} %select_reduce_fusion.1), channel_id=1, source_target_pairs={{0,2},{1,3},{2,0},{3,1},{4,6},{5,7},{6,4},{7,5},{8,10},{9,11},{10,... | collective-permute-start | bytes 24584 | tf_op jit(solution)/shard_map/ppermute | solution.py:118
  6.8 1.3 copy.49
  11.3 1.7 %fusion.2 = f32[128,32,64]{0,2,1:T(8,128)} fusion(f32[128,32,64]{0,2,1:T(8,128)S(1)} %convolution_bitcast_fusion, bf16[128,32,64]{0,2,1:T(8,128)(2,1)S(1)} %bitcast.123, f32[1,32,64,128]{3,2,1,0:T(8,128)S(1)} %copy-done.5, f32[32]{0:T(128)S(1)} %copy-done.9, f32[128,32]{0,1:T(8,128)S(1)} %copy.50, bf16[128,128]{1,0:T(8,128)(2,1)S(1)} %copy-done), kind=kOutput, calls=%fused_computation.9 | convolution fusion | flops 403963904 | bytes 3719296 | tf_op jit(solution)/shard_map/tn,hpn->thp/dot_general | solution.py:26
  12.9 1.6 %copy.51 = f32[128,2048]{1,0:T(8,128)S(1)} copy(f32[128,2048]{0,1:T(8,128)} %bitcast.125) | data formatting | bytes 2097152 | tf_op jit(solution)/shard_map/reshape | solution.py:34
  15.0 1.4 multiply_convert_fusion.2
  16.6 1.6 %collective-permute-start.1 = (f32[2,1,128,16]{2,3,1,0:T(8,128)S(1)}, f32[2,1,128,16]{2,3,1,0:T(8,128)S(1)}, u32[]{:S(2)}, u32[]{:S(2)}) collective-permute-start(f32[2,1,128,16]{2,3,1,0:T(8,128)S(1)} %maximum_select_fusion.7), channel_id=1, source_target_pairs={{0,4},{1,5},{2,6},{3,7},{4,0},{5,1},{6,2},{7,3},{8,12},{9,13},{10,... | collective-permute-start | bytes 49160 | tf_op jit(solution)/shard_map/ppermute | solution.py:118
  18.3 2.1 %collective-permute-done.1 = f32[2,1,128,16]{2,3,1,0:T(8,128)S(1)} collective-permute-done((f32[2,1,128,16]{2,3,1,0:T(8,128)S(1)}, f32[2,1,128,16]{2,3,1,0:T(8,128)S(1)}, u32[]{:S(2)}, u32[]{:S(2)}) %collective-permute-start.1) | collective-permute-done | bytes 16416 | tf_op jit(solution)/shard_map/ppermute | solution.py:118
  20.4 2.6 %collective-permute-start.2 = (f32[2,2,128,16]{2,3,1,0:T(8,128)S(1)}, f32[2,2,128,16]{2,3,1,0:T(8,128)S(1)}, u32[]{:S(2)}, u32[]{:S(2)}) collective-permute-start(f32[2,2,128,16]{2,3,1,0:T(8,128)S(1)} %maximum_select_fusion.6), channel_id=1, source_target_pairs={{0,8},{1,9},{2,10},{3,11},{4,12},{5,13},{6,14},{7,15},{8,0},{9,1},... | collective-permute-start | bytes 98312 | tf_op jit(solution)/shard_map/ppermute | solution.py:118
  22.9 2.7 %fusion.3 = f32[1,32,64,128]{3,2,1,0:T(8,128)} fusion(f32[1,32,64,128]{3,2,1,0:T(8,128)} %param.24, bf16[128,32,64]{0,2,1:T(8,128)(2,1)} %bitcast.124, f32[128,32]{0,1:T(8,128)S(1)} %get-tuple-element.34, f32[32]{0:T(128)S(1)} %fusion.123, bf16[128,128]{1,0:T(8,128)(2,1)S(1)} %copy-done.7), kind=kOutput, calls=%fused_computation.11 | convolution fusion | flops 68419584 | bytes 2670720 | tf_op jit(solution)/shard_map/thp,tn->hpn/dot_general | solution.py:43
  26.3 1.5 collective-permute-start.4
  28.0 2.0 %convolution_convert_fusion.1 = bf16[128,512]{1,0:T(8,128)(2,1)S(1)} fusion(bf16[128,2048]{1,0:T(8,128)(2,1)S(1)} %multiply_convert_fusion.2, bf16[2048,512]{1,0:T(8,128)(2,1)} %param.25), kind=kOutput, calls=%fused_computation.18 | convolution fusion | flops 268500992 | bytes 2752512 | tf_op jit(solution)/shard_map/dot_general | solution.py:159
  30.1 4.9 %collective-permute-done.6 = bf16[64,2048]{1,0:T(8,128)(2,1)S(1)} collective-permute-done((bf16[64,2048]{1,0:T(8,128)(2,1)S(1)}, bf16[64,2048]{1,0:T(8,128)(2,1)S(1)}, u32[]{:S(2)}, u32[]{:S(2)}) %collective-permute-start.6) | collective-permute-done | bytes 262176 | tf_op jit(solution)/shard_map/ppermute | solution.py:118
  35.5 3.2 %collective-permute-done.4 = bf16[64,2048]{1,0:T(8,128)(2,1)S(1)} collective-permute-done((bf16[64,2048]{1,0:T(8,128)(2,1)S(1)}, bf16[64,2048]{1,0:T(8,128)(2,1)S(1)}, u32[]{:S(2)}, u32[]{:S(2)}) %collective-permute-start.4) | collective-permute-done | bytes 262176 | tf_op jit(solution)/shard_map/ppermute | solution.py:118
  39.1 2.1 %convolution_convert_fusion.2 = bf16[64,512]{1,0:T(8,128)(2,1)S(1)} fusion(bf16[64,2048]{1,0:T(8,128)(2,1)S(1)} %collective-permute-done.6, bf16[2048,512]{1,0:T(8,128)(2,1)} %collective-permute-done.3), kind=kOutput, calls=%fused_computation.19 | convolution fusion | flops 134250496 | bytes 2424832 | tf_op jit(solution)/shard_map/dot_general | solution.py:160
  41.8 2.1 %convolution_convert_fusion.4 = bf16[64,512]{1,0:T(8,128)(2,1)S(1)} fusion(bf16[64,2048]{1,0:T(8,128)(2,1)S(1)} %collective-permute-done.4, bf16[2048,512]{1,0:T(8,128)(2,1)} %collective-permute-done.3), kind=kOutput, calls=%fused_computation.21 | convolution fusion | flops 134250496 | bytes 2424832 | tf_op jit(solution)/shard_map/dot_general | solution.py:160
  43.9 1.6 collective-permute-start.5
  45.5 2.0 %convolution_convert_fusion = bf16[128,512]{1,0:T(8,128)(2,1)S(1)} fusion(bf16[128,2048]{1,0:T(8,128)(2,1)S(1)} %multiply_convert_fusion.2, bf16[2048,512]{1,0:T(8,128)(2,1)} %collective-permute-done.3), kind=kOutput, calls=%fused_computation.17 | convolution fusion | flops 268500992 | bytes 2752512 | tf_op jit(solution)/shard_map/dot_general | solution.py:160
  47.8 1.2 collective-permute-done.5
  49.1 1.6 %collective-permute-start.12 = (bf16[64,2048]{1,0:T(8,128)(2,1)S(1)}, bf16[64,2048]{1,0:T(8,128)(2,1)S(1)}, u32[]{:S(2)}, u32[]{:S(2)}) collective-permute-start(bf16[64,2048]{1,0:T(8,128)(2,1)S(1)} %maximum_select_fusion.1), channel_id=1, source_target_pairs={{0,4},{1,5},{2,0},{3,1},{4,8},{5,9},{6,2},{7,3},{8,12},{9,13},{10,... | collective-permute-start | bytes 786440 | tf_op jit(solution)/shard_map/ppermute | solution.py:118
  51.2 1.5 collective-permute-start.11
  53.9 2.6 %fusion.132 = f32[128,768]{1,0:T(8,128)S(1)} fusion(bf16[128,2048]{1,0:T(8,128)(2,1)S(1)} %constant_dynamic-update-slice_fusion, bf16[2048,768]{1,0:T(8,128)(2,1)} %collective-permute-done.8), kind=kOutput, calls=%fused_computation.229 | convolution fusion | flops 402653184 | bytes 4063232 | tf_op jit(solution)/shard_map/dot_general | solution.py:189
  57.0 2.6 %collective-permute-done.10 = bf16[64,2048]{1,0:T(8,128)(2,1)S(1)} collective-permute-done((bf16[64,2048]{1,0:T(8,128)(2,1)S(1)}, bf16[64,2048]{1,0:T(8,128)(2,1)S(1)}, u32[]{:S(2)}, u32[]{:S(2)}) %collective-permute-start.10) | collective-permute-done | bytes 262176 | tf_op jit(solution)/shard_map/ppermute | solution.py:118
  59.6 2.8 %collective-permute-done.11 = bf16[64,2048]{1,0:T(8,128)(2,1)S(1)} collective-permute-done((bf16[64,2048]{1,0:T(8,128)(2,1)S(1)}, bf16[64,2048]{1,0:T(8,128)(2,1)S(1)}, u32[]{:S(2)}, u32[]{:S(2)}) %collective-permute-start.11) | collective-permute-done | bytes 262176 | tf_op jit(solution)/shard_map/ppermute | solution.py:118
  62.5 2.9 %fusion.133 = f32[256,768]{1,0:T(8,128)S(1)} fusion(bf16[256,2048]{1,0:T(8,128)(2,1)S(1)} %constant_dynamic-update-slice_fusion.2, bf16[2048,768]{1,0:T(8,128)(2,1)} %collective-permute-done.8), kind=kOutput, calls=%fused_computation.230 | convolution fusion | flops 805306368 | bytes 4980736 | tf_op jit(solution)/shard_map/dot_general | solution.py:189
  68.5 1.1 collective-permute-start.16
  69.7 1.6 collective-permute-start.17
  71.3 5.9 %collective-permute-done.14 = bf16[64,2048]{1,0:T(8,128)(2,1)S(1)} collective-permute-done((bf16[64,2048]{1,0:T(8,128)(2,1)S(1)}, bf16[64,2048]{1,0:T(8,128)(2,1)S(1)}, u32[]{:S(2)}, u32[]{:S(2)}) %collective-permute-start.14) | collective-permute-done | bytes 262176 | tf_op jit(solution)/shard_map/ppermute | solution.py:118
  78.3 2.9 %fusion.134 = f32[256,768]{1,0:T(8,128)S(1)} fusion(bf16[256,2048]{1,0:T(8,128)(2,1)S(1)} %constant_dynamic-update-slice_fusion.6, bf16[2048,768]{1,0:T(8,128)(2,1)} %collective-permute-done.8), kind=kOutput, calls=%fused_computation.231 | convolution fusion | flops 805306368 | bytes 4980736 | tf_op jit(solution)/shard_map/dot_general | solution.py:189
  82.1 1.6 %collective-permute-start.19 = (bf16[64,2048]{1,0:T(8,128)(2,1)S(1)}, bf16[64,2048]{1,0:T(8,128)(2,1)S(1)}, u32[]{:S(2)}, u32[]{:S(2)}) collective-permute-start(bf16[64,2048]{1,0:T(8,128)(2,1)S(1)} %collective-permute-done.15), channel_id=1, source_target_pairs={{0,2},{1,3},{2,6},{3,7},{4,0},{5,1},{6,10},{7,11},{8,4},{9,5},{10,... | collective-permute-start | bytes 786440 | tf_op jit(solution)/shard_map/ppermute | solution.py:118
  84.9 1.7 %collective-permute-start.20 = (bf16[64,2048]{1,0:T(8,128)(2,1)S(1)}, bf16[64,2048]{1,0:T(8,128)(2,1)S(1)}, u32[]{:S(2)}, u32[]{:S(2)}) collective-permute-start(bf16[64,2048]{1,0:T(8,128)(2,1)S(1)} %collective-permute-done.16), channel_id=1, source_target_pairs={{0,4},{1,5},{2,0},{3,1},{4,8},{5,9},{6,2},{7,3},{8,12},{9,13},{10,... | collective-permute-start | bytes 786440 | tf_op jit(solution)/shard_map/ppermute | solution.py:118
  87.1 4.3 %collective-permute-done.18 = bf16[64,2048]{1,0:T(8,128)(2,1)S(1)} collective-permute-done((bf16[64,2048]{1,0:T(8,128)(2,1)S(1)}, bf16[64,2048]{1,0:T(8,128)(2,1)S(1)}, u32[]{:S(2)}, u32[]{:S(2)}) %collective-permute-start.18) | collective-permute-done | bytes 262176 | tf_op jit(solution)/shard_map/ppermute | solution.py:118
  91.5 2.6 %collective-permute-done.21 = bf16[64,2048]{1,0:T(8,128)(2,1)S(1)} collective-permute-done((bf16[64,2048]{1,0:T(8,128)(2,1)S(1)}, bf16[64,2048]{1,0:T(8,128)(2,1)S(1)}, u32[]{:S(2)}, u32[]{:S(2)}) %collective-permute-start.21) | collective-permute-done | bytes 262176 | tf_op jit(solution)/shard_map/ppermute | solution.py:118
  94.1 2.9 %fusion.135 = f32[256,768]{1,0:T(8,128)S(1)} fusion(bf16[256,2048]{1,0:T(8,128)(2,1)S(1)} %constant_dynamic-update-slice_fusion.10, bf16[2048,768]{1,0:T(8,128)(2,1)} %collective-permute-done.8), kind=kOutput, calls=%fused_computation.232 | convolution fusion | flops 805306368 | bytes 4980736 | tf_op jit(solution)/shard_map/dot_general | solution.py:189
  98.8 1.7 %collective-permute-start.22 = (bf16[64,2048]{1,0:T(8,128)(2,1)S(1)}, bf16[64,2048]{1,0:T(8,128)(2,1)S(1)}, u32[]{:S(2)}, u32[]{:S(2)}) collective-permute-start(bf16[64,2048]{1,0:T(8,128)(2,1)S(1)} %collective-permute-done.20), channel_id=1, source_target_pairs={{0,4},{1,5},{2,0},{3,1},{4,8},{5,9},{6,2},{7,3},{8,12},{9,13},{10,... | collective-permute-start | bytes 786440 | tf_op jit(solution)/shard_map/ppermute | solution.py:118
  101.7 3.5 %collective-permute-done.22 = bf16[64,2048]{1,0:T(8,128)(2,1)S(1)} collective-permute-done((bf16[64,2048]{1,0:T(8,128)(2,1)S(1)}, bf16[64,2048]{1,0:T(8,128)(2,1)S(1)}, u32[]{:S(2)}, u32[]{:S(2)}) %collective-permute-start.22) | collective-permute-done | bytes 262176 | tf_op jit(solution)/shard_map/ppermute | solution.py:118
  105.2 2.1 %collective-permute-done.23 = bf16[64,2048]{1,0:T(8,128)(2,1)S(1)} collective-permute-done((bf16[64,2048]{1,0:T(8,128)(2,1)S(1)}, bf16[64,2048]{1,0:T(8,128)(2,1)S(1)}, u32[]{:S(2)}, u32[]{:S(2)}) %collective-permute-start.23) | collective-permute-done | bytes 262176 | tf_op jit(solution)/shard_map/ppermute | solution.py:118
  107.3 2.5 %fusion.136 = f32[128,768]{1,0:T(8,128)S(1)} fusion(bf16[128,2048]{1,0:T(8,128)(2,1)S(1)} %constant_dynamic-update-slice_fusion.14, bf16[2048,768]{1,0:T(8,128)(2,1)} %collective-permute-done.8), kind=kOutput, calls=%fused_computation.233 | convolution fusion | flops 402653184 | bytes 4063232 | tf_op jit(solution)/shard_map/dot_general | solution.py:189
  111.5 1.9 %collective-permute-start.34 = (bf16[64,2048]{1,0:T(8,128)(2,1)S(1)}, bf16[64,2048]{1,0:T(8,128)(2,1)S(1)}, u32[]{:S(2)}, u32[]{:S(2)}) collective-permute-start(bf16[64,2048]{1,0:T(8,128)(2,1)S(1)} %get-tuple-element.29), channel_id=1, source_target_pairs={{0,2},{1,3},{2,6},{3,7},{4,0},{5,1},{6,10},{7,11},{8,4},{9,5},{10,... | collective-permute-start | bytes 786440 | tf_op jit(solution)/shard_map/ppermute | solution.py:118
  113.6 2.0 %collective-permute-start.31 = (bf16[64,2048]{1,0:T(8,128)(2,1)S(1)}, bf16[64,2048]{1,0:T(8,128)(2,1)S(1)}, u32[]{:S(2)}, u32[]{:S(2)}) collective-permute-start(bf16[64,2048]{1,0:T(8,128)(2,1)S(1)} %get-tuple-element.27), channel_id=1, source_target_pairs={{0,4},{1,5},{2,0},{3,1},{4,8},{5,9},{6,2},{7,3},{8,12},{9,13},{10,... | collective-permute-start | bytes 786440 | tf_op jit(solution)/shard_map/ppermute | solution.py:118
  115.6 2.3 %collective-permute-done.24 = bf16[64,2048]{1,0:T(8,128)(2,1)S(1)} collective-permute-done((bf16[64,2048]{1,0:T(8,128)(2,1)S(1)}, bf16[64,2048]{1,0:T(8,128)(2,1)S(1)}, u32[]{:S(2)}, u32[]{:S(2)}) %collective-permute-start.24) | collective-permute-done | bytes 262176 | tf_op jit(solution)/shard_map/ppermute | solution.py:118
  118.9 1.6 %collective-permute-start.25 = (bf16[64,2048]{1,0:T(8,128)(2,1)S(1)}, bf16[64,2048]{1,0:T(8,128)(2,1)S(1)}, u32[]{:S(2)}, u32[]{:S(2)}) collective-permute-start(bf16[64,2048]{1,0:T(8,128)(2,1)S(1)} %get-tuple-element.22), channel_id=1, source_target_pairs={{0,4},{1,5},{2,0},{3,1},{4,8},{5,9},{6,2},{7,3},{8,12},{9,13},{10,... | collective-permute-start | bytes 786440 | tf_op jit(solution)/shard_map/ppermute | solution.py:118
  122.1 6.1 %collective-permute-done.25 = bf16[64,2048]{1,0:T(8,128)(2,1)S(1)} collective-permute-done((bf16[64,2048]{1,0:T(8,128)(2,1)S(1)}, bf16[64,2048]{1,0:T(8,128)(2,1)S(1)}, u32[]{:S(2)}, u32[]{:S(2)}) %collective-permute-start.25) | collective-permute-done | bytes 262176 | tf_op jit(solution)/shard_map/ppermute | solution.py:118
  128.2 1.5 collective-permute-done.35
  135.0 4.3 %collective-permute-done.26 = bf16[64,2048]{1,0:T(8,128)(2,1)S(1)} collective-permute-done((bf16[64,2048]{1,0:T(8,128)(2,1)S(1)}, bf16[64,2048]{1,0:T(8,128)(2,1)S(1)}, u32[]{:S(2)}, u32[]{:S(2)}) %collective-permute-start.26) | collective-permute-done | bytes 262176 | tf_op jit(solution)/shard_map/ppermute | solution.py:118
  140.2 3.9 %collective-permute-done.32 = bf16[64,2048]{1,0:T(8,128)(2,1)S(1)} collective-permute-done((bf16[64,2048]{1,0:T(8,128)(2,1)S(1)}, bf16[64,2048]{1,0:T(8,128)(2,1)S(1)}, u32[]{:S(2)}, u32[]{:S(2)}) %collective-permute-start.32) | collective-permute-done | bytes 262176 | tf_op jit(solution)/shard_map/ppermute | solution.py:118
  144.1 1.3 collective-permute-done.36
  150.2 1.8 %collective-permute-done.27 = bf16[64,2048]{1,0:T(8,128)(2,1)S(1)} collective-permute-done((bf16[64,2048]{1,0:T(8,128)(2,1)S(1)}, bf16[64,2048]{1,0:T(8,128)(2,1)S(1)}, u32[]{:S(2)}, u32[]{:S(2)}) %collective-permute-start.27) | collective-permute-done | bytes 262176 | tf_op jit(solution)/shard_map/ppermute | solution.py:118
  153.0 1.9 %collective-permute-done.33 = bf16[64,2048]{1,0:T(8,128)(2,1)S(1)} collective-permute-done((bf16[64,2048]{1,0:T(8,128)(2,1)S(1)}, bf16[64,2048]{1,0:T(8,128)(2,1)S(1)}, u32[]{:S(2)}, u32[]{:S(2)}) %collective-permute-start.33) | collective-permute-done | bytes 262176 | tf_op jit(solution)/shard_map/ppermute | solution.py:118
  (140 shorter events, 40.2 us)
Async XLA Ops:
  0.6 8.5 %copy-start = (bf16[128,128]{1,0:T(8,128)(2,1)S(1)}, bf16[128,128]{1,0:T(8,128)(2,1)}, u32[]{:S(2)}) copy-start(bf16[128,128]{1,0:T(8,128)(2,1)} %param.18) | copy-start | bytes 98308
  1.4 15.2 %collective-permute-start = (f32[128,16]{0,1:T(8,128)S(1)}, f32[128,16]{0,1:T(8,128)S(1)}, u32[]{:S(2)}, u32[]{:S(2)}) collective-permute-start(f32[128,16]{0,1:T(8,128)S(1)} %select_reduce_fusion.1), channel_id=1, source_target_pairs={{0,2},{1,3},{2,0},{3,1},{4,6},{5,7},{6,4},{7,5},{8,10},{9,11},{10,... | collective-permute-start | bytes 24584 | tf_op jit(solution)/shard_map/ppermute | solution.py:118
  4.4 34.7 %collective-permute-start.3 = (bf16[2048,512]{1,0:T(8,128)(2,1)}, bf16[2048,512]{1,0:T(8,128)(2,1)}, u32[]{:S(2)}, u32[]{:S(2)}) collective-permute-start(bf16[2048,512]{1,0:T(8,128)(2,1)} %param.25), channel_id=1, source_target_pairs={{0,1},{1,0},{2,3},{3,2},{4,5},{5,4},{6,7},{7,6},{8,9},{9,8},{10,11... | collective-permute-start | bytes 6291464 | tf_op jit(solution)/shard_map/ppermute | solution.py:118
  4.4 44.7 %collective-permute-start.8 = (bf16[2048,768]{1,0:T(8,128)(2,1)}, bf16[2048,768]{1,0:T(8,128)(2,1)}, u32[]{:S(2)}, u32[]{:S(2)}) collective-permute-start(bf16[2048,768]{1,0:T(8,128)(2,1)} %bitcast.121), channel_id=1, source_target_pairs={{0,1},{1,0},{2,3},{3,2},{4,5},{5,4},{6,7},{7,6},{8,9},{9,8},{10,11... | collective-permute-start | bytes 9437192 | tf_op jit(solution)/shard_map/ppermute | solution.py:118
  4.9 44.2 %collective-permute-start.9 = (bf16[384,2048]{1,0:T(8,128)(2,1)}, bf16[384,2048]{1,0:T(8,128)(2,1)S(1)}, u32[]{:S(2)}, u32[]{:S(2)}) collective-permute-start(bf16[384,2048]{1,0:T(8,128)(2,1)} %bitcast.120), channel_id=1, source_target_pairs={{0,1},{1,0},{2,3},{3,2},{4,5},{5,4},{6,7},{7,6},{8,9},{9,8},{10,11... | collective-permute-start | bytes 4718600 | tf_op jit(solution)/shard_map/ppermute | solution.py:118
  8.2 2.8 %copy-start.4 = (bf16[128,2048]{0,1:T(8,128)(2,1)}, bf16[128,2048]{0,1:T(8,128)(2,1)S(1)}, u32[]{:S(2)}) copy-start(bf16[128,2048]{0,1:T(8,128)(2,1)S(1)} %copy.49) | copy-start | bytes 1572868
  10.0 1.3 copy-start.5
  10.0 1.3 copy-start.9
  12.9 1.6 %copy-start.6 = (bf16[128,2048]{1,0:T(8,128)(2,1)S(1)}, bf16[128,2048]{1,0:T(8,128)(2,1)}, u32[]{:S(2)}) copy-start(bf16[128,2048]{1,0:T(8,128)(2,1)} %param.16) | copy-start | bytes 1572868
  12.9 2.1 %copy-start.8 = (f32[2048]{0:T(1024)S(1)}, f32[2048]{0:T(1024)}, u32[]{:S(2)}) copy-start(f32[2048]{0:T(1024)} %param.23) | copy-start | bytes 24580
  14.6 8.4 %copy-start.7 = (bf16[128,128]{1,0:T(8,128)(2,1)S(1)}, bf16[128,128]{1,0:T(8,128)(2,1)}, u32[]{:S(2)}) copy-start(bf16[128,128]{1,0:T(8,128)(2,1)} %param.17) | copy-start | bytes 98308
  16.6 3.8 %collective-permute-start.1 = (f32[2,1,128,16]{2,3,1,0:T(8,128)S(1)}, f32[2,1,128,16]{2,3,1,0:T(8,128)S(1)}, u32[]{:S(2)}, u32[]{:S(2)}) collective-permute-start(f32[2,1,128,16]{2,3,1,0:T(8,128)S(1)} %maximum_select_fusion.7), channel_id=1, source_target_pairs={{0,4},{1,5},{2,6},{3,7},{4,0},{5,1},{6,2},{7,3},{8,12},{9,13},{10,... | collective-permute-start | bytes 49160 | tf_op jit(solution)/shard_map/ppermute | solution.py:118
  20.4 5.3 %collective-permute-start.2 = (f32[2,2,128,16]{2,3,1,0:T(8,128)S(1)}, f32[2,2,128,16]{2,3,1,0:T(8,128)S(1)}, u32[]{:S(2)}, u32[]{:S(2)}) collective-permute-start(f32[2,2,128,16]{2,3,1,0:T(8,128)S(1)} %maximum_select_fusion.6), channel_id=1, source_target_pairs={{0,8},{1,9},{2,10},{3,11},{4,12},{5,13},{6,14},{7,15},{8,0},{9,1},... | collective-permute-start | bytes 98312 | tf_op jit(solution)/shard_map/ppermute | solution.py:118
  25.6 9.4 %copy-start.2 = (bf16[2048,512]{1,0:T(8,128)(2,1)S(1)}, bf16[2048,512]{1,0:T(8,128)(2,1)}, u32[]{:S(2)}) copy-start(bf16[2048,512]{1,0:T(8,128)(2,1)} %param.25) | copy-start | bytes 6291460
  25.7 9.3 %collective-permute-start.6 = (bf16[64,2048]{1,0:T(8,128)(2,1)S(1)}, bf16[64,2048]{1,0:T(8,128)(2,1)S(1)}, u32[]{:S(2)}, u32[]{:S(2)}) collective-permute-start(bf16[64,2048]{1,0:T(8,128)(2,1)S(1)} %get-tuple-element.30), channel_id=1, source_target_pairs={{0,2},{1,3},{2,0},{3,1},{4,6},{5,7},{6,4},{7,5},{8,10},{9,11},{10,... | collective-permute-start | bytes 786440 | tf_op jit(solution)/shard_map/ppermute | solution.py:118
  26.3 12.4 %collective-permute-start.4 = (bf16[64,2048]{1,0:T(8,128)(2,1)S(1)}, bf16[64,2048]{1,0:T(8,128)(2,1)S(1)}, u32[]{:S(2)}, u32[]{:S(2)}) collective-permute-start(bf16[64,2048]{1,0:T(8,128)(2,1)S(1)} %get-tuple-element.31), channel_id=1, source_target_pairs={{0,2},{1,3},{2,0},{3,1},{4,6},{5,7},{6,4},{7,5},{8,10},{9,11},{10,... | collective-permute-start | bytes 786440 | tf_op jit(solution)/shard_map/ppermute | solution.py:118
  41.2 6.4 %collective-permute-start.7 = (bf16[64,1024]{1,0:T(8,128)(2,1)S(1)}, bf16[64,1024]{1,0:T(8,128)(2,1)S(1)}, u32[]{:S(2)}, u32[]{:S(2)}) collective-permute-start(bf16[64,1024]{1,0:T(8,128)(2,1)S(1)} %maximum_select_fusion.4), channel_id=1, source_target_pairs={{0,2},{1,3},{2,0},{3,1},{4,6},{5,7},{6,4},{7,5},{8,10},{9,11},{10,... | collective-permute-start | bytes 393224 | tf_op jit(solution)/shard_map/ppermute | solution.py:118
  43.9 5.0 %collective-permute-start.5 = (bf16[64,1024]{1,0:T(8,128)(2,1)S(1)}, bf16[64,1024]{1,0:T(8,128)(2,1)S(1)}, u32[]{:S(2)}, u32[]{:S(2)}) collective-permute-start(bf16[64,1024]{1,0:T(8,128)(2,1)S(1)} %maximum_select_fusion.3), channel_id=1, source_target_pairs={{0,2},{1,3},{2,0},{3,1},{4,6},{5,7},{6,4},{7,5},{8,10},{9,11},{10,... | collective-permute-start | bytes 393224 | tf_op jit(solution)/shard_map/ppermute | solution.py:118
  47.5 5.7 %copy-start.3 = (bf16[1,2048,768]{2,1,0:T(8,128)(2,1)S(1)}, bf16[1,2048,768]{2,1,0:T(8,128)(2,1)}, u32[]{:S(2)}) copy-start(bf16[1,2048,768]{2,1,0:T(8,128)(2,1)} %param.26) | copy-start | bytes 9437188
  49.1 13.3 %collective-permute-start.12 = (bf16[64,2048]{1,0:T(8,128)(2,1)S(1)}, bf16[64,2048]{1,0:T(8,128)(2,1)S(1)}, u32[]{:S(2)}, u32[]{:S(2)}) collective-permute-start(bf16[64,2048]{1,0:T(8,128)(2,1)S(1)} %maximum_select_fusion.1), channel_id=1, source_target_pairs={{0,4},{1,5},{2,0},{3,1},{4,8},{5,9},{6,2},{7,3},{8,12},{9,13},{10,... | collective-permute-start | bytes 786440 | tf_op jit(solution)/shard_map/ppermute | solution.py:118
  50.7 8.9 %collective-permute-start.10 = (bf16[64,2048]{1,0:T(8,128)(2,1)S(1)}, bf16[64,2048]{1,0:T(8,128)(2,1)S(1)}, u32[]{:S(2)}, u32[]{:S(2)}) collective-permute-start(bf16[64,2048]{1,0:T(8,128)(2,1)S(1)} %maximum_select_fusion.1), channel_id=1, source_target_pairs={{0,2},{1,3},{2,6},{3,7},{4,0},{5,1},{6,10},{7,11},{8,4},{9,5},{10,... | collective-permute-start | bytes 786440 | tf_op jit(solution)/shard_map/ppermute | solution.py:118
  51.2 11.2 %collective-permute-start.11 = (bf16[64,2048]{1,0:T(8,128)(2,1)S(1)}, bf16[64,2048]{1,0:T(8,128)(2,1)S(1)}, u32[]{:S(2)}, u32[]{:S(2)}) collective-permute-start(bf16[64,2048]{1,0:T(8,128)(2,1)S(1)} %maximum_select_fusion.2), channel_id=1, source_target_pairs={{0,2},{1,3},{2,6},{3,7},{4,0},{5,1},{6,10},{7,11},{8,4},{9,5},{10,... | collective-permute-start | bytes 786440 | tf_op jit(solution)/shard_map/ppermute | solution.py:118
  52.7 9.8 %collective-permute-start.13 = (bf16[64,2048]{1,0:T(8,128)(2,1)S(1)}, bf16[64,2048]{1,0:T(8,128)(2,1)S(1)}, u32[]{:S(2)}, u32[]{:S(2)}) collective-permute-start(bf16[64,2048]{1,0:T(8,128)(2,1)S(1)} %maximum_select_fusion.2), channel_id=1, source_target_pairs={{0,4},{1,5},{2,0},{3,1},{4,8},{5,9},{6,2},{7,3},{8,12},{9,13},{10,... | collective-permute-start | bytes 786440 | tf_op jit(solution)/shard_map/ppermute | solution.py:118
  53.8 2.6 %copy-start.1 = (bf16[1,384,2048]{2,1,0:T(8,128)(2,1)S(1)}, bf16[1,384,2048]{2,1,0:T(8,128)(2,1)}, u32[]{:S(2)}) copy-start(bf16[1,384,2048]{2,1,0:T(8,128)(2,1)} %param.27) | copy-start | bytes 4718596
  66.3 10.8 %collective-permute-start.15 = (bf16[64,2048]{1,0:T(8,128)(2,1)S(1)}, bf16[64,2048]{1,0:T(8,128)(2,1)S(1)}, u32[]{:S(2)}, u32[]{:S(2)}) collective-permute-start(bf16[64,2048]{1,0:T(8,128)(2,1)S(1)} %collective-permute-done.11), channel_id=1, source_target_pairs={{0,2},{1,3},{2,6},{3,7},{4,0},{5,1},{6,10},{7,11},{8,4},{9,5},{10,... | collective-permute-start | bytes 786440 | tf_op jit(solution)/shard_map/ppermute | solution.py:118
  66.8 10.3 %collective-permute-start.14 = (bf16[64,2048]{1,0:T(8,128)(2,1)S(1)}, bf16[64,2048]{1,0:T(8,128)(2,1)S(1)}, u32[]{:S(2)}, u32[]{:S(2)}) collective-permute-start(bf16[64,2048]{1,0:T(8,128)(2,1)S(1)} %collective-permute-done.10), channel_id=1, source_target_pairs={{0,2},{1,3},{2,6},{3,7},{4,0},{5,1},{6,10},{7,11},{8,4},{9,5},{10,... | collective-permute-start | bytes 786440 | tf_op jit(solution)/shard_map/ppermute | solution.py:118
  68.5 8.6 %collective-permute-start.16 = (bf16[64,2048]{1,0:T(8,128)(2,1)S(1)}, bf16[64,2048]{1,0:T(8,128)(2,1)S(1)}, u32[]{:S(2)}, u32[]{:S(2)}) collective-permute-start(bf16[64,2048]{1,0:T(8,128)(2,1)S(1)} %collective-permute-done.12), channel_id=1, source_target_pairs={{0,4},{1,5},{2,0},{3,1},{4,8},{5,9},{6,2},{7,3},{8,12},{9,13},{10,... | collective-permute-start | bytes 786440 | tf_op jit(solution)/shard_map/ppermute | solution.py:118
  69.7 8.6 %collective-permute-start.17 = (bf16[64,2048]{1,0:T(8,128)(2,1)S(1)}, bf16[64,2048]{1,0:T(8,128)(2,1)S(1)}, u32[]{:S(2)}, u32[]{:S(2)}) collective-permute-start(bf16[64,2048]{1,0:T(8,128)(2,1)S(1)} %collective-permute-done.13), channel_id=1, source_target_pairs={{0,4},{1,5},{2,0},{3,1},{4,8},{5,9},{6,2},{7,3},{8,12},{9,13},{10,... | collective-permute-start | bytes 786440 | tf_op jit(solution)/shard_map/ppermute | solution.py:118
  82.1 9.3 %collective-permute-start.19 = (bf16[64,2048]{1,0:T(8,128)(2,1)S(1)}, bf16[64,2048]{1,0:T(8,128)(2,1)S(1)}, u32[]{:S(2)}, u32[]{:S(2)}) collective-permute-start(bf16[64,2048]{1,0:T(8,128)(2,1)S(1)} %collective-permute-done.15), channel_id=1, source_target_pairs={{0,2},{1,3},{2,6},{3,7},{4,0},{5,1},{6,10},{7,11},{8,4},{9,5},{10,... | collective-permute-start | bytes 786440 | tf_op jit(solution)/shard_map/ppermute | solution.py:118
  83.7 7.6 %collective-permute-start.18 = (bf16[64,2048]{1,0:T(8,128)(2,1)S(1)}, bf16[64,2048]{1,0:T(8,128)(2,1)S(1)}, u32[]{:S(2)}, u32[]{:S(2)}) collective-permute-start(bf16[64,2048]{1,0:T(8,128)(2,1)S(1)} %collective-permute-done.14), channel_id=1, source_target_pairs={{0,2},{1,3},{2,6},{3,7},{4,0},{5,1},{6,10},{7,11},{8,4},{9,5},{10,... | collective-permute-start | bytes 786440 | tf_op jit(solution)/shard_map/ppermute | solution.py:118
  84.9 6.6 %collective-permute-start.20 = (bf16[64,2048]{1,0:T(8,128)(2,1)S(1)}, bf16[64,2048]{1,0:T(8,128)(2,1)S(1)}, u32[]{:S(2)}, u32[]{:S(2)}) collective-permute-start(bf16[64,2048]{1,0:T(8,128)(2,1)S(1)} %collective-permute-done.16), channel_id=1, source_target_pairs={{0,4},{1,5},{2,0},{3,1},{4,8},{5,9},{6,2},{7,3},{8,12},{9,13},{10,... | collective-permute-start | bytes 786440 | tf_op jit(solution)/shard_map/ppermute | solution.py:118
  86.6 7.5 %collective-permute-start.21 = (bf16[64,2048]{1,0:T(8,128)(2,1)S(1)}, bf16[64,2048]{1,0:T(8,128)(2,1)S(1)}, u32[]{:S(2)}, u32[]{:S(2)}) collective-permute-start(bf16[64,2048]{1,0:T(8,128)(2,1)S(1)} %collective-permute-done.17), channel_id=1, source_target_pairs={{0,4},{1,5},{2,0},{3,1},{4,8},{5,9},{6,2},{7,3},{8,12},{9,13},{10,... | collective-permute-start | bytes 786440 | tf_op jit(solution)/shard_map/ppermute | solution.py:118
  98.8 6.4 %collective-permute-start.22 = (bf16[64,2048]{1,0:T(8,128)(2,1)S(1)}, bf16[64,2048]{1,0:T(8,128)(2,1)S(1)}, u32[]{:S(2)}, u32[]{:S(2)}) collective-permute-start(bf16[64,2048]{1,0:T(8,128)(2,1)S(1)} %collective-permute-done.20), channel_id=1, source_target_pairs={{0,4},{1,5},{2,0},{3,1},{4,8},{5,9},{6,2},{7,3},{8,12},{9,13},{10,... | collective-permute-start | bytes 786440 | tf_op jit(solution)/shard_map/ppermute | solution.py:118
  100.5 6.8 %collective-permute-start.23 = (bf16[64,2048]{1,0:T(8,128)(2,1)S(1)}, bf16[64,2048]{1,0:T(8,128)(2,1)S(1)}, u32[]{:S(2)}, u32[]{:S(2)}) collective-permute-start(bf16[64,2048]{1,0:T(8,128)(2,1)S(1)} %collective-permute-done.19), channel_id=1, source_target_pairs={{0,2},{1,3},{2,6},{3,7},{4,0},{5,1},{6,10},{7,11},{8,4},{9,5},{10,... | collective-permute-start | bytes 786440 | tf_op jit(solution)/shard_map/ppermute | solution.py:118
  111.4 6.5 %collective-permute-start.24 = (bf16[64,2048]{1,0:T(8,128)(2,1)S(1)}, bf16[64,2048]{1,0:T(8,128)(2,1)S(1)}, u32[]{:S(2)}, u32[]{:S(2)}) collective-permute-start(bf16[64,2048]{1,0:T(8,128)(2,1)S(1)} %get-tuple-element.28), channel_id=1, source_target_pairs={{0,4},{1,5},{2,0},{3,1},{4,8},{5,9},{6,2},{7,3},{8,12},{9,13},{10,... | collective-permute-start | bytes 786440 | tf_op jit(solution)/shard_map/ppermute | solution.py:118
  111.5 7.3 %collective-permute-start.34 = (bf16[64,2048]{1,0:T(8,128)(2,1)S(1)}, bf16[64,2048]{1,0:T(8,128)(2,1)S(1)}, u32[]{:S(2)}, u32[]{:S(2)}) collective-permute-start(bf16[64,2048]{1,0:T(8,128)(2,1)S(1)} %get-tuple-element.29), channel_id=1, source_target_pairs={{0,2},{1,3},{2,6},{3,7},{4,0},{5,1},{6,10},{7,11},{8,4},{9,5},{10,... | collective-permute-start | bytes 786440 | tf_op jit(solution)/shard_map/ppermute | solution.py:118
  113.5 8.6 %collective-permute-start.28 = (bf16[64,2048]{1,0:T(8,128)(2,1)S(1)}, bf16[64,2048]{1,0:T(8,128)(2,1)S(1)}, u32[]{:S(2)}, u32[]{:S(2)}) collective-permute-start(bf16[64,2048]{1,0:T(8,128)(2,1)S(1)} %get-tuple-element.26), channel_id=1, source_target_pairs={{0,2},{1,3},{2,6},{3,7},{4,0},{5,1},{6,10},{7,11},{8,4},{9,5},{10,... | collective-permute-start | bytes 786440 | tf_op jit(solution)/shard_map/ppermute | solution.py:118
  113.6 8.5 %collective-permute-start.31 = (bf16[64,2048]{1,0:T(8,128)(2,1)S(1)}, bf16[64,2048]{1,0:T(8,128)(2,1)S(1)}, u32[]{:S(2)}, u32[]{:S(2)}) collective-permute-start(bf16[64,2048]{1,0:T(8,128)(2,1)S(1)} %get-tuple-element.27), channel_id=1, source_target_pairs={{0,4},{1,5},{2,0},{3,1},{4,8},{5,9},{6,2},{7,3},{8,12},{9,13},{10,... | collective-permute-start | bytes 786440 | tf_op jit(solution)/shard_map/ppermute | solution.py:118
  118.9 9.3 %collective-permute-start.25 = (bf16[64,2048]{1,0:T(8,128)(2,1)S(1)}, bf16[64,2048]{1,0:T(8,128)(2,1)S(1)}, u32[]{:S(2)}, u32[]{:S(2)}) collective-permute-start(bf16[64,2048]{1,0:T(8,128)(2,1)S(1)} %get-tuple-element.22), channel_id=1, source_target_pairs={{0,4},{1,5},{2,0},{3,1},{4,8},{5,9},{6,2},{7,3},{8,12},{9,13},{10,... | collective-permute-start | bytes 786440 | tf_op jit(solution)/shard_map/ppermute | solution.py:118
  120.5 9.2 %collective-permute-start.35 = (bf16[64,2048]{1,0:T(8,128)(2,1)S(1)}, bf16[64,2048]{1,0:T(8,128)(2,1)S(1)}, u32[]{:S(2)}, u32[]{:S(2)}) collective-permute-start(bf16[64,2048]{1,0:T(8,128)(2,1)S(1)} %get-tuple-element.23), channel_id=1, source_target_pairs={{0,2},{1,3},{2,6},{3,7},{4,0},{5,1},{6,10},{7,11},{8,4},{9,5},{10,... | collective-permute-start | bytes 786440 | tf_op jit(solution)/shard_map/ppermute | solution.py:118
  130.1 9.2 %collective-permute-start.26 = (bf16[64,2048]{1,0:T(8,128)(2,1)S(1)}, bf16[64,2048]{1,0:T(8,128)(2,1)S(1)}, u32[]{:S(2)}, u32[]{:S(2)}) collective-permute-start(bf16[64,2048]{1,0:T(8,128)(2,1)S(1)} %get-tuple-element.18), channel_id=1, source_target_pairs={{0,4},{1,5},{2,0},{3,1},{4,8},{5,9},{6,2},{7,3},{8,12},{9,13},{10,... | collective-permute-start | bytes 786440 | tf_op jit(solution)/shard_map/ppermute | solution.py:118
  131.1 9.1 %collective-permute-start.29 = (bf16[64,2048]{1,0:T(8,128)(2,1)S(1)}, bf16[64,2048]{1,0:T(8,128)(2,1)S(1)}, u32[]{:S(2)}, u32[]{:S(2)}) collective-permute-start(bf16[64,2048]{1,0:T(8,128)(2,1)S(1)} %get-tuple-element.21), channel_id=1, source_target_pairs={{0,2},{1,3},{2,6},{3,7},{4,0},{5,1},{6,10},{7,11},{8,4},{9,5},{10,... | collective-permute-start | bytes 786440 | tf_op jit(solution)/shard_map/ppermute | solution.py:118
  132.2 11.9 %collective-permute-start.32 = (bf16[64,2048]{1,0:T(8,128)(2,1)S(1)}, bf16[64,2048]{1,0:T(8,128)(2,1)S(1)}, u32[]{:S(2)}, u32[]{:S(2)}) collective-permute-start(bf16[64,2048]{1,0:T(8,128)(2,1)S(1)} %get-tuple-element.20), channel_id=1, source_target_pairs={{0,4},{1,5},{2,0},{3,1},{4,8},{5,9},{6,2},{7,3},{8,12},{9,13},{10,... | collective-permute-start | bytes 786440 | tf_op jit(solution)/shard_map/ppermute | solution.py:118
  133.1 12.2 %collective-permute-start.36 = (bf16[64,2048]{1,0:T(8,128)(2,1)S(1)}, bf16[64,2048]{1,0:T(8,128)(2,1)S(1)}, u32[]{:S(2)}, u32[]{:S(2)}) collective-permute-start(bf16[64,2048]{1,0:T(8,128)(2,1)S(1)} %get-tuple-element.19), channel_id=1, source_target_pairs={{0,2},{1,3},{2,6},{3,7},{4,0},{5,1},{6,10},{7,11},{8,4},{9,5},{10,... | collective-permute-start | bytes 786440 | tf_op jit(solution)/shard_map/ppermute | solution.py:118
  145.6 6.4 %collective-permute-start.27 = (bf16[64,2048]{1,0:T(8,128)(2,1)S(1)}, bf16[64,2048]{1,0:T(8,128)(2,1)S(1)}, u32[]{:S(2)}, u32[]{:S(2)}) collective-permute-start(bf16[64,2048]{1,0:T(8,128)(2,1)S(1)} %get-tuple-element.14), channel_id=1, source_target_pairs={{0,4},{1,5},{2,0},{3,1},{4,8},{5,9},{6,2},{7,3},{8,12},{9,13},{10,... | collective-permute-start | bytes 786440 | tf_op jit(solution)/shard_map/ppermute | solution.py:118
  146.6 6.4 %collective-permute-start.30 = (bf16[64,2048]{1,0:T(8,128)(2,1)S(1)}, bf16[64,2048]{1,0:T(8,128)(2,1)S(1)}, u32[]{:S(2)}, u32[]{:S(2)}) collective-permute-start(bf16[64,2048]{1,0:T(8,128)(2,1)S(1)} %get-tuple-element.17), channel_id=1, source_target_pairs={{0,2},{1,3},{2,6},{3,7},{4,0},{5,1},{6,10},{7,11},{8,4},{9,5},{10,... | collective-permute-start | bytes 786440 | tf_op jit(solution)/shard_map/ppermute | solution.py:118
  147.7 7.2 %collective-permute-start.33 = (bf16[64,2048]{1,0:T(8,128)(2,1)S(1)}, bf16[64,2048]{1,0:T(8,128)(2,1)S(1)}, u32[]{:S(2)}, u32[]{:S(2)}) collective-permute-start(bf16[64,2048]{1,0:T(8,128)(2,1)S(1)} %get-tuple-element.16), channel_id=1, source_target_pairs={{0,4},{1,5},{2,0},{3,1},{4,8},{5,9},{6,2},{7,3},{8,12},{9,13},{10,... | collective-permute-start | bytes 786440 | tf_op jit(solution)/shard_map/ppermute | solution.py:118
  148.7 7.2 %collective-permute-start.37 = (bf16[64,2048]{1,0:T(8,128)(2,1)S(1)}, bf16[64,2048]{1,0:T(8,128)(2,1)S(1)}, u32[]{:S(2)}, u32[]{:S(2)}) collective-permute-start(bf16[64,2048]{1,0:T(8,128)(2,1)S(1)} %get-tuple-element.15), channel_id=1, source_target_pairs={{0,2},{1,3},{2,6},{3,7},{4,0},{5,1},{6,10},{7,11},{8,4},{9,5},{10,... | collective-permute-start | bytes 786440 | tf_op jit(solution)/shard_map/ppermute | solution.py:118

commit v4 on v3

--- a/solution.py
+++ b/solution.py
@@ -1,49 +1,305 @@
+import functools
+
 import jax
 import jax.numpy as jnp
 from jax import lax
+from jax.experimental import pallas as pl
+from jax.experimental.pallas import tpu as pltpu
 from jax.sharding import PartitionSpec as P
 
 epsilon = 1e-05
+
+
+CHUNK = 8
+NT = (((1,), (1,)), ((), ()))
+TN = (((0,), (0,)), ((), ()))
+
+
+def decays(dt_ref, bias_ref, a_ref):
+    frames = dt_ref.shape[1]
+    step_size = jax.nn.softplus(dt_ref[...] + bias_ref[...])
+    rise = step_size * -jnp.exp(a_ref[...])
+    s = lax.broadcasted_iota(jnp.int32, (frames, frames), 0)
+    t = lax.broadcasted_iota(jnp.int32, (frames, frames), 1)
+    upto = jnp.where(s <= t, 1.0, 0.0)
+    decay = jnp.dot(rise, upto, precision=lax.Precision.HIGHEST, preferred_element_type=jnp.float32)
+    return step_size, decay
+
+
+def mixer_kernel(
+    x_ref, z_ref, b_ref, c_ref, dt_ref, bias_ref, a_ref, skip_ref, gain_ref, state_ref, out_ref, g_ref, ss_ref
+):
+    i = pl.program_id(0)
+    frames, width = x_ref.shape
+    head = width // CHUNK
+    step_size, decay = decays(dt_ref, bias_ref, a_ref)
+    decay_col = decay.T
+    carry_col = jnp.exp(decay_col)
+    t = lax.broadcasted_iota(jnp.int32, (frames, frames), 0)
+    s = lax.broadcasted_iota(jnp.int32, (frames, frames), 1)
+    c = c_ref[...]
+    scores = lax.dot_general(c, b_ref[...], NT, preferred_element_type=jnp.float32)
+    scores = jnp.where(s <= t, scores, 0.0)
+    cc = jnp.concatenate([c, c], axis=1)
+    left = lax.broadcasted_iota(jnp.int32, (frames, 2 * head), 1) < head
+    squares = None
+    for pair in range(CHUNK // 2):
+        mixes = []
+        for h in (2 * pair, 2 * pair + 1):
+            spread = jnp.exp(jnp.minimum(decay_col[:, h : h + 1] - decay[h : h + 1, :], 0.0))
+            mixes.append((spread * (scores * step_size[h : h + 1, :])).astype(jnp.bfloat16))
+        at = slice(2 * head * pair, 2 * head * (pair + 1))
+        x = x_ref[:, at]
+        zero = jnp.zeros_like(x)
+        y = jnp.dot(
+            jnp.concatenate(mixes, axis=1),
+            jnp.concatenate([jnp.where(left, x, zero), jnp.where(left, zero, x)], axis=0),
+            preferred_element_type=jnp.float32,
+        )
+        state = state_ref[at, :]
+        high = state.astype(jnp.bfloat16)
+        low = (state - high.astype(jnp.float32)).astype(jnp.bfloat16)
+        carried = lax.dot_general(
+            cc, jnp.concatenate([high, low], axis=1), NT, preferred_element_type=jnp.float32
+        )
+        factor = jnp.where(
+            left, carry_col[:, 2 * pair : 2 * pair + 1], carry_col[:, 2 * pair + 1 : 2 * pair + 2]
+        )
+        mixed = y + factor * carried + skip_ref[:, at] * x.astype(jnp.float32)
+        z = z_ref[:, at].astype(jnp.float32)
+        g = mixed * jax.nn.silu(z)
+        g_ref[i, :, at] = g
+        squares = g * g if squares is None else squares + g * g
+
+    @pl.when(i == 0)
+    def _():
+        ss_ref[...] = squares
+
+    @pl.when(i > 0)
+    def _():
+        ss_ref[...] += squares
+
+    steps = g_ref.shape[0]
+
+    @pl.when(i == steps - 1)
+    def _():
+        mean = jnp.sum(ss_ref[...], axis=1, keepdims=True) / (steps * width)
+        scale = lax.rsqrt(mean + epsilon)
+        for j in range(steps):
+            at = slice(j * width, (j + 1) * width)
+            out_ref[:, at] = (g_ref[j] * scale * gain_ref[:, at]).astype(jnp.bfloat16)
+
+
+def state_kernel(x_ref, b_ref, dt_ref, bias_ref, a_ref, state_ref, out_ref):
+    frames, width = x_ref.shape
+    head = width // CHUNK
+    step_size, decay = decays(dt_ref, bias_ref, a_ref)
+    end = decay[:, frames - 1 : frames]
+    tail = (jnp.exp(end - decay) * step_size).T
+    kept = jnp.exp(end)
+    left = lax.broadcasted_iota(jnp.int32, (frames, 2 * head), 1) < head
+    upper = lax.broadcasted_iota(jnp.int32, (2 * head, b_ref.shape[1]), 0) < head
+    for pair in range(CHUNK // 2):
+        at = slice(2 * head * pair, 2 * head * (pair + 1))
+        factor = jnp.where(left, tail[:, 2 * pair : 2 * pair + 1], tail[:, 2 * pair + 1 : 2 * pair + 2])
+        scaled = (x_ref[:, at].astype(jnp.float32) * factor).astype(jnp.bfloat16)
+        added = lax.dot_general(scaled, b_ref[...], TN, preferred_element_type=jnp.float32)
+        keep = jnp.where(upper, kept[2 * pair : 2 * pair + 1, :], kept[2 * pair + 1 : 2 * pair + 2, :])
+        out_ref[at, :] = keep * state_ref[at, :] + added
 
 
 def ssm_mixer(
     ssm_input, gate_input, b_proj, c_proj, dt_raw, a_log, dt_bias, d_skip, norm_gain, state_in
 ):
-    length = ssm_input.shape[0]
-    head_count = dt_raw.shape[1]
-    head_dim = ssm_input.shape[1] // head_count
-    step_size = jax.nn.softplus(dt_raw + dt_bias[None, :])
-    decay_log = jnp.cumsum(step_size * (-jnp.exp(a_log))[None, :], axis=0)
-    decay_heads = decay_log.T
-    causal = jnp.arange(length)[:, None] >= jnp.arange(length)[None, :]
-    spread = decay_heads[:, :, None] - decay_heads[:, None, :]
-    spread = jnp.where(causal[None], spread, 0.0)
-    scores = jnp.dot(c_proj, b_proj.T, preferred_element_type=jnp.float32)
-    mixing = jnp.where(causal[None], jnp.exp(spread), 0.0) * scores[None] * step_size.T[:, None, :]
-    mixing = mixing.astype(jnp.bfloat16)
-    values = ssm_input.reshape(length, head_count, head_dim)
-    within = jnp.einsum("hts,shp->thp", mixing, values, preferred_element_type=jnp.float32)
-    carried = jnp.einsum(
-        "tn,hpn->thp", c_proj.astype(jnp.float32), state_in, precision=lax.Precision.HIGHEST
-    )
-    mixed_rows = (
-        within
-        + jnp.exp(decay_log)[:, :, None] * carried
-        + d_skip[None, :, None] * values.astype(jnp.float32)
-    )
-    gated_rows = mixed_rows.reshape(length, -1) * jax.nn.silu(gate_input.astype(jnp.float32))
-    normed = (
-        gated_rows
-        * lax.rsqrt(jnp.mean(gated_rows * gated_rows, axis=1, keepdims=True) + epsilon)
-        * norm_gain[None, :]
-    )
-    normed = normed.astype(jnp.bfloat16)
-    tail_weight = jnp.exp(decay_log[-1][None, :] - decay_log) * step_size
-    scaled = (values.astype(jnp.float32) * tail_weight[:, :, None]).astype(jnp.bfloat16)
-    state_next = jnp.exp(decay_log[-1])[:, None, None] * state_in + jnp.einsum(
-        "thp,tn->hpn", scaled, b_proj, preferred_element_type=jnp.float32
-    )
+    frames, width = ssm_input.shape
+    heads, head, inner = state_in.shape
+    steps = heads // CHUNK
+    part = width // steps
+    dt = dt_raw.T
+    state = state_in.reshape(width, inner)
+    column = pl.BlockSpec((frames, part), lambda i: (0, i))
+    whole = pl.BlockSpec((frames, inner), lambda i: (0, 0))
+    per_head = pl.BlockSpec((CHUNK, frames), lambda i: (i, 0))
+    scalar = pl.BlockSpec((CHUNK, 1), lambda i: (i, 0))
+    rows = pl.BlockSpec((part, inner), lambda i: (i, 0))
+    full_row = pl.BlockSpec((1, width), lambda i: (0, 0))
+    normed = pl.pallas_call(
+        mixer_kernel,
+        grid=(steps,),
+        in_specs=[
+            column,
+            column,
+            whole,
+            whole,
+            per_head,
+            scalar,
+            scalar,
+            pl.BlockSpec((1, part), lambda i: (0, i)),
+            full_row,
+            rows,
+        ],
+        out_specs=pl.BlockSpec((frames, width), lambda i: (0, 0)),
+        out_shape=jax.ShapeDtypeStruct((frames, width), jnp.bfloat16),
+        scratch_shapes=[
+            pltpu.VMEM((steps, frames, part), jnp.float32),
+            pltpu.VMEM((frames, 2 * head), jnp.float32),
+        ],
+        compiler_params=pltpu.CompilerParams(vmem_limit_bytes=24 << 20),
+        cost_estimate=pl.CostEstimate(flops=400_000_000, bytes_accessed=6_000_000, transcendentals=2_000_000),
+        name="mixer",
+    )(
+        ssm_input,
+        gate_input,
+        b_proj,
+        c_proj,
+        dt,
+        dt_bias[:, None],
+        a_log[:, None],
+        jnp.repeat(d_skip, head)[None, :],
+        norm_gain[None, :],
+        state,
+    )
+
+    def state_next(ssm_input):
+        out = pl.pallas_call(
+            state_kernel,
+            grid=(steps,),
+            in_specs=[column, whole, per_head, scalar, scalar, rows],
+            out_specs=rows,
+            out_shape=jax.ShapeDtypeStruct((width, inner), jnp.float32),
+            compiler_params=pltpu.CompilerParams(vmem_limit_bytes=16 << 20),
+            cost_estimate=pl.CostEstimate(flops=70_000_000, bytes_accessed=3_000_000, transcendentals=20_000),
+            name="state",
+        )(ssm_input, b_proj, dt, dt_bias[:, None], a_log[:, None], state)
+        return out.reshape(heads, head, inner)
+
     return (normed, state_next)
+
+
+def project_kernel(core_ref, rows_ref, mine_ref, other_ref, out_ref):
+    i = pl.program_id(0)
+    steps = pl.num_programs(0) // 2
+
+    @pl.when(i < steps)
+    def _():
+        out_ref[...] = jnp.dot(
+            rows_ref[...], mine_ref[...], preferred_element_type=jnp.float32
+        ).astype(jnp.bfloat16)
+
+    @pl.when(i >= steps)
+    def _():
+        out_ref[...] = jnp.dot(
+            rows_ref[...], other_ref[...], preferred_element_type=jnp.float32
+        ).astype(jnp.bfloat16)
+
+
+def project(core, rows, mine, other):
+    count, depth = rows.shape
+    width = mine.shape[1]
+    wide = min(width, 256)
+    steps = width // wide
+    return pl.pallas_call(
+        project_kernel,
+        grid_spec=pltpu.PrefetchScalarGridSpec(
+            num_scalar_prefetch=1,
+            grid=(2 * steps,),
+            in_specs=[
+                pl.BlockSpec((count, depth), lambda i, c: (0, 0)),
+                pl.BlockSpec((depth, wide), lambda i, c: (0, jnp.minimum(i, steps - 1))),
+                pl.BlockSpec((depth, wide), lambda i, c: (0, jnp.maximum(i - steps, 0))),
+            ],
+            out_specs=pl.BlockSpec(
+                (count, wide),
+                lambda i, c: (0, jnp.where(i < steps, c[0], 1 - c[0]) * steps + i % steps),
+            ),
+        ),
+        out_shape=jax.ShapeDtypeStruct((count, 2 * width), jnp.bfloat16),
+        compiler_params=pltpu.CompilerParams(vmem_limit_bytes=16 << 20),
+        cost_estimate=pl.CostEstimate(
+            flops=4 * count * depth * width, bytes_accessed=4 * depth * width, transcendentals=0
+        ),
+        name="project",
+    )(core[None], rows, mine, other)
+
+
+def experts_kernel(parts, gate_ref, *refs):
+    row_refs, refs = refs[:parts], refs[parts:]
+    weights, refs = (refs[0:3], refs[3:6]), refs[6:]
+    outs, (rows, total) = refs[:-2], refs[-2:]
+    i = pl.program_id(0)
+    steps = pl.num_programs(0) // 2
+    size = row_refs[0].shape[0]
+
+    @pl.when(i == 0)
+    def _():
+        for p in range(parts):
+            rows[p * size : (p + 1) * size, :] = row_refs[p][...]
+        total[...] = jnp.zeros_like(total)
+
+    def add(e):
+        gate_in, up_in, down = weights[e]
+        r = rows[...]
+        gated = jnp.dot(r, gate_in[...], preferred_element_type=jnp.float32)
+        up = jnp.dot(r, up_in[...], preferred_element_type=jnp.float32)
+        hidden = (jax.nn.silu(gated) * up * gate_ref[:, e : e + 1]).astype(jnp.bfloat16)
+        total[...] += jnp.dot(hidden, down[...], preferred_element_type=jnp.float32)
+
+    pl.when(i < steps)(functools.partial(add, 0))
+    pl.when(i >= steps)(functools.partial(add, 1))
+
+    @pl.when(i == 2 * steps - 1)
+    def _():
+        for p in range(parts):
+            outs[p][...] = total[p * size : (p + 1) * size, :].astype(outs[p].dtype)
+
+
+def run_experts(parts, gate, mine, other, out_type):
+    size, depth = parts[0].shape
+    hidden, width = mine[1].shape
+    count = len(parts) * size
+    cut = 128 if hidden % 128 == 0 else hidden
+    steps = hidden // cut
+    first = lambda i: jnp.minimum(i, steps - 1)
+    second = lambda i: jnp.maximum(i - steps, 0)
+    in_specs = [pl.BlockSpec((count, 2), lambda i: (0, 0))]
+    in_specs += [pl.BlockSpec((size, depth), lambda i: (0, 0)) for _ in parts]
+    operands = [gate, *parts]
+    for pick, (w_in, w_down) in ((first, mine), (second, other)):
+        in_specs += [
+            pl.BlockSpec((depth, cut), lambda i, pick=pick: (0, pick(i))),
+            pl.BlockSpec((depth, cut), lambda i, pick=pick: (0, steps + pick(i))),
+            pl.BlockSpec((cut, width), lambda i, pick=pick: (pick(i), 0)),
+        ]
+        operands += [w_in, w_in, w_down]
+    return pl.pallas_call(
+        functools.partial(experts_kernel, len(parts)),
+        grid=(2 * steps,),
+        in_specs=in_specs,
+        out_specs=[pl.BlockSpec((size, width), lambda i: (0, 0)) for _ in parts],
+        out_shape=[jax.ShapeDtypeStruct((size, width), out_type) for _ in parts],
+        scratch_shapes=[
+            pltpu.VMEM((count, depth), jnp.bfloat16),
+            pltpu.VMEM((count, width), jnp.float32),
+        ],
+        compiler_params=pltpu.CompilerParams(vmem_limit_bytes=32 << 20),
+        cost_estimate=pl.CostEstimate(
+            flops=12 * count * depth * hidden, bytes_accessed=12 * depth * hidden, transcendentals=2 * count * hidden
+        ),
+        name="experts",
+    )(*operands)
+
+
+def add_kernel(total_ref, got_ref, out_ref):
+    out_ref[...] = (total_ref[...] + got_ref[...].astype(jnp.float32)).astype(jnp.bfloat16)
+
+
+def add_on(total, got):
+    return pl.pallas_call(
+        add_kernel,
+        out_shape=jax.ShapeDtypeStruct(got.shape, jnp.bfloat16),
+        cost_estimate=pl.CostEstimate(flops=got.size, bytes_accessed=8 * got.size, transcendentals=0),
+        name="add_on",
+    )(total, got)
 
 
 def slot_positions(route_ids, experts):
@@ -87,12 +343,13 @@
     experts = local_experts * lax.axis_size(("wide", "narrow"))
     wide, narrow = lax.axis_size("wide"), lax.axis_size("narrow")
     if experts <= 4 * topk_count and narrow == 4 and wide & (wide - 1) == 0 and local_experts == 1:
-        layer_out = dense_experts(
-            normed, out_proj, expert_in[0], expert_out[0], route_ids, route_weights
+        layer_out, ssm_input = dense_experts(
+            normed, out_proj, expert_in[0], expert_out[0], route_ids, route_weights, ssm_input
         )
     else:
         layer_out = routed_experts(normed, out_proj, expert_in, expert_out, route_ids, route_weights)
-    return (layer_out, state_next[None])
+    state = state_next(ssm_input)
+    return (layer_out, state[None])
 
 
 def routes(wide, move):
@@ -105,7 +362,7 @@
     return pairs
 
 
-def dense_experts(normed, out_proj, expert_in, expert_out, route_ids, route_weights):
+def dense_experts(normed, out_proj, expert_in, expert_out, route_ids, route_weights, held):
     frames = route_ids.shape[0]
     wide = lax.axis_size("wide")
     ring = 2 * wide
@@ -146,7 +403,6 @@
             low, jnp.concatenate([gates, other], axis=1), jnp.concatenate([other, gates], axis=1)
         )
         step *= 2
-    normed, gates = lax.optimization_barrier((normed, gates))
     mine = (z * 2 + x) * 2 + core
     pair = jnp.stack([mine, mine + 1 - 2 * core])
     gates = jnp.sum(
@@ -155,22 +411,13 @@
     gates = jnp.concatenate([gates[0], gates[1, ::-1]])
     gates = lax.dynamic_slice_in_dim(jnp.concatenate([gates, gates]), place, ring, 0)
 
-    def project(rows):
-        first = jnp.dot(rows, out_proj, preferred_element_type=jnp.float32).astype(jnp.bfloat16)
-        second = jnp.dot(rows, out_other, preferred_element_type=jnp.float32).astype(jnp.bfloat16)
-        return jnp.where(
-            core == 0,
-            jnp.concatenate([first, second], axis=1),
-            jnp.concatenate([second, first], axis=1),
-        )
-
     halves = range(2)
     size = frames // 2
     sent = [to_x(normed[h * size : (h + 1) * size]) for h in halves]
-    own = project(normed)
+    own = project(core, normed, out_proj, out_other)
     rows = []
     for h in halves:
-        back = to_x(project(sent[h]))
+        back = to_x(project(core, sent[h], out_proj, out_other))
         here = own[h * size : (h + 1) * size]
         rows.append(
             jnp.where(
@@ -179,57 +426,43 @@
                 jnp.concatenate([back, here], axis=1),
             )
         )
-
-    *rows, in_other, down_other = lax.optimization_barrier((*rows, in_other, down_other))
-    hidden_width = expert_out.shape[0]
-
-    def run_experts(rows, gate):
-        total = None
-        for e, (w_in, w_down) in enumerate(((expert_in, expert_out), (in_other, down_other))):
-            v = jnp.dot(rows, w_in, preferred_element_type=jnp.float32)
-            hidden = jax.nn.silu(v[:, :hidden_width]) * v[:, hidden_width:] * gate[:, e : e + 1]
-            part = jnp.dot(hidden.astype(jnp.bfloat16), w_down, preferred_element_type=jnp.float32)
-            total = part if total is None else total + part
-        return total
+    *rows, in_other, down_other, gates, held = lax.optimization_barrier(
+        (*rows, in_other, down_other, gates, held)
+    )
+    first, second = (expert_in, expert_out), (in_other, down_other)
 
     fore, back = list(rows), list(rows)
-    total = run_experts(jnp.concatenate(rows), gates[0])
-    mixer_rows = rows
     ahead, behind = {}, {}
-    for h in halves:
-        ahead[0, h] = total[h * size : (h + 1) * size]
+    ahead[0, 0], ahead[0, 1] = run_experts(rows, gates[0], first, second, jnp.float32)
     far = ring // 2
     for k in range(1, far):
         for h in halves:
             fore[h] = along(fore[h], 1)
             back[h] = along(back[h], -1)
-        total = run_experts(
-            jnp.concatenate([back[0], back[1], fore[0], fore[1]]),
+        ahead[k, 0], ahead[k, 1], behind[k, 0], behind[k, 1] = run_experts(
+            [back[0], back[1], fore[0], fore[1]],
             jnp.concatenate([gates[k], gates[ring - k]]),
-        )
-        for h in halves:
-            ahead[k, h] = total[h * size : (h + 1) * size]
-            behind[k, h] = total[frames + h * size : frames + (h + 1) * size]
+            first,
+            second,
+            jnp.float32,
+        )
     last = [along(fore[0], 1), along(back[1], -1)]
-    total = run_experts(jnp.concatenate(last), gates[far])
-
-    fore = [along(total[:size].astype(jnp.bfloat16), 1), None]
-    back = [None, along(total[size:].astype(jnp.bfloat16), -1)]
+    last = run_experts(last, gates[far], first, second, jnp.bfloat16)
+
+    fore, back = [along(last[0], 1), None], [None, along(last[1], -1)]
     for k in range(far - 1, 0, -1):
         for h in halves:
-            load = ahead[k, h]
-            if fore[h] is not None:
-                load = load + fore[h].astype(jnp.float32)
-            fore[h] = along(load.astype(jnp.bfloat16), 1)
-            load = behind[k, h]
-            if back[h] is not None:
-                load = load + back[h].astype(jnp.float32)
-            back[h] = along(load.astype(jnp.bfloat16), -1)
+            for way, step, totals in ((fore, 1, ahead), (back, -1, behind)):
+                if way[h] is None:
+                    load = totals[k, h].astype(jnp.bfloat16)
+                else:
+                    load = add_on(totals[k, h], way[h])
+                way[h] = along(load, step)
     out = []
     for h in halves:
         total = ahead[0, h] + fore[h].astype(jnp.float32) + back[h].astype(jnp.float32)
-        out.append((mixer_rows[h].astype(jnp.float32) + total).astype(jnp.bfloat16))
-    return jnp.concatenate(out)
+        out.append((rows[h].astype(jnp.float32) + total).astype(jnp.bfloat16))
+    return jnp.concatenate(out), held
 
 
 def routed_experts(normed, out_proj, expert_in, expert_out, route_ids, route_weights):

time: 158 us -> 197 us (1.25)
  Pallas kernels: 0 us -> 81.4 us
  matrix products: 39.7 us -> 0 us
  waiting for transfers between devices: 63.3 us -> 27.7 us
  local copies, waits for them, and re-layouts: 4.05 us -> 35.7 us
    pallas_call x0 -> x20, Pallas kernels: none -> 81.4 us  [the longest x5 43.7 us: run_experts(): pl.pallas_call(functools.partial(experts_kernel, len(parts)), grid=(2 * s...]
    dot_general x30 -> x0, matrix products: 39.7 us -> none  [the longest x10 17.8 us: run_experts(): v = jnp.dot(rows, w_in, preferred_element_type=jnp.float32)]
    ppermute x38, waiting for transfers between devices: 63.3 us -> 27.7 us  [send(): return lax.ppermute(value, axes, routes(wide, move))]
    unnamed x32 -> x105, local copies, waits for them, and re-layouts: 1.91 us -> 31.8 us
    broadcast_in_dim x0 -> x3, local copies, waits for them, and re-layouts: none -> 2.19 us  [the longest x1 0.74 us: ssm_mixer(): a_log[:, None]]
  transfers between devices with their start and end apart: 38 -> 38, of which waited for: 25 -> 11; matrix products, arithmetic and copies ran while one was open for 20% -> 5% of each run, Pallas kernels for 0% -> 42%
where the time goes in v4:
time: 197 us; the launch traced here: 195 us
  Pallas kernels  81.4 us (41%)
  starting transfers between devices  42.4 us (22%)
  local copies, waits for them, and re-layouts  35.7 us (18%)
  waiting for transfers between devices  27.7 us (14%)
  other arithmetic  6.84 us (3%)
    pallas_call x5, Pallas kernels, run_experts(): pl.pallas_call(functools.partial(experts_kernel, len(parts)), grid=(2 * s...  43.7 us
    ppermute x38, starting transfers between devices, send(): return lax.ppermute(value, axes, routes(wide, move))  42.4 us
    unnamed x105, local copies, waits for them, and re-layouts  31.8 us
    ppermute x38, waiting for transfers between devices, send(): return lax.ppermute(value, axes, routes(wide, move))  27.7 us
    pallas_call x10, Pallas kernels, add_on(): pl.pallas_call(add_kernel, out_shape=jax.ShapeDtypeStruct(got.shape, jnp....  18.7 us
    pallas_call x3, Pallas kernels, project(): pl.pallas_call(project_kernel, grid_spec=pltpu.PrefetchScalarGridSpec(num...  10.9 us
    pallas_call x1, Pallas kernels, state_next(): pl.pallas_call(state_kernel, grid=(steps,), in_specs=[column, whole, per_...  4.28 us
  transfers between devices with their start and end apart: 38, of which 11 were waited for; matrix products, arithmetic and copies ran while one was open for 5% of the time, Pallas kernels for 42%

profile of v4, /device:TPU:0, one launch (start us, length us, event | category | flops | bytes accessed | tf_op | source)
XLA Modules:
  0.0 195.0 jit_solution(8518834228292366783)
XLA Ops:
  1.9 3.0 %collective-permute-start.7 = (f32[128,16]{0,1:T(8,128)S(1)}, f32[128,16]{0,1:T(8,128)S(1)}, u32[]{:S(2)}, u32[]{:S(2)}) collective-permute-start(f32[128,16]{0,1:T(8,128)S(1)} %select_reduce_fusion.1), channel_id=1, source_target_pairs={{0,2},{1,3},{2,0},{3,1},{4,6},{5,7},{6,4},{7,5},{8,10},{9,11},{10,... | collective-permute-start | bytes 24584 | tf_op jit(solution)/shard_map/ppermute | solution.py:375
  7.2 1.2 copy-done.8
  13.4 3.7 %mixer.1.rows_ref = bf16[128,2048]{1,0:T(8,128)(2,1)S(1)} custom-call(bf16[128,2048]{1,0:T(8,128)(2,1)S(1)} %copy-done.26, bf16[128,2048]{1,0:T(8,128)(2,1)S(1)} %copy-done.48, bf16[128,128]{1,0:T(8,128)(2,1)S(1)} %copy-done.44, bf16[128,128]{1,0:T(8,128)(2,1)S(1)} %copy-done.49, f32[32,128]{1,0:T(8,128)S(1)} %bitcast.45, f32[32,1]{1,0:T(8,128)S(1)} %copy.49.bias_ref, ...), custom_call_target="tpu_custom_call" | custom-call | flops 400000000 | bytes 6000000 | tf_op jit(solution)/shard_map/mixer/pallas_call | solution.py:126
  18.7 2.2 %collective-permute-start.8 = (f32[2,1,128,16]{2,3,1,0:T(8,128)S(1)}, f32[2,1,128,16]{2,3,1,0:T(8,128)S(1)}, u32[]{:S(2)}, u32[]{:S(2)}) collective-permute-start(f32[2,1,128,16]{2,3,1,0:T(8,128)S(1)} %maximum_select_fusion.4), channel_id=1, source_target_pairs={{0,4},{1,5},{2,6},{3,7},{4,0},{5,1},{6,2},{7,3},{8,12},{9,13},{10,... | collective-permute-start | bytes 49160 | tf_op jit(solution)/shard_map/ppermute | solution.py:375
  20.9 1.6 collective-permute-done.8
  22.6 3.0 %collective-permute-start.9 = (f32[2,2,128,16]{2,3,1,0:T(8,128)S(1)}, f32[2,2,128,16]{2,3,1,0:T(8,128)S(1)}, u32[]{:S(2)}, u32[]{:S(2)}) collective-permute-start(f32[2,2,128,16]{2,3,1,0:T(8,128)S(1)} %maximum_select_fusion.3), channel_id=1, source_target_pairs={{0,8},{1,9},{2,10},{3,11},{4,12},{5,13},{6,14},{7,15},{8,0},{9,1},... | collective-permute-start | bytes 98312 | tf_op jit(solution)/shard_map/ppermute | solution.py:375
  25.7 2.1 %collective-permute-done.9 = f32[2,2,128,16]{2,3,1,0:T(8,128)S(1)} collective-permute-done((f32[2,2,128,16]{2,3,1,0:T(8,128)S(1)}, f32[2,2,128,16]{2,3,1,0:T(8,128)S(1)}, u32[]{:S(2)}, u32[]{:S(2)}) %collective-permute-start.9) | collective-permute-done | bytes 32800 | tf_op jit(solution)/shard_map/ppermute | solution.py:375
  27.8 1.5 collective-permute-start.1
  30.1 3.6 %project.5 = bf16[64,1024]{1,0:T(8,128)(2,1)S(1)} custom-call(s32[1]{0:T(128)} %bitcast.core_ref, bf16[64,2048]{1,0:T(8,128)(2,1)S(1)} %collective-permute-done.3.rows_ref, bf16[2048,512]{1,0:T(8,128)(2,1)S(1)} %copy-done.1, bf16[2048,512]{1,0:T(8,128)(2,1)} %collective-permute-done.other_ref), custom_call_target="tpu_custom_call" | custom-call | flops 268435456 | bytes 4194304 | tf_op jit(solution)/shard_map/project/pallas_call | solution.py:201
  34.4 3.6 %project.4 = bf16[64,1024]{1,0:T(8,128)(2,1)S(1)} custom-call(s32[1]{0:T(128)} %bitcast.core_ref, bf16[64,2048]{1,0:T(8,128)(2,1)S(1)} %collective-permute-done.1.rows_ref, bf16[2048,512]{1,0:T(8,128)(2,1)S(1)} %copy-done.1, bf16[2048,512]{1,0:T(8,128)(2,1)} %collective-permute-done.other_ref), custom_call_target="tpu_custom_call" | custom-call | flops 268435456 | bytes 4194304 | tf_op jit(solution)/shard_map/project/pallas_call | solution.py:201
  38.0 2.5 %collective-permute-start.2 = (bf16[64,1024]{1,0:T(8,128)(2,1)S(1)}, bf16[64,1024]{1,0:T(8,128)(2,1)S(1)}, u32[]{:S(2)}, u32[]{:S(2)}) collective-permute-start(bf16[64,1024]{1,0:T(8,128)(2,1)S(1)} %project.4), channel_id=1, source_target_pairs={{0,2},{1,3},{2,0},{3,1},{4,6},{5,7},{6,4},{7,5},{8,10},{9,11},{10,... | collective-permute-start | bytes 393224 | tf_op jit(solution)/shard_map/ppermute | solution.py:375
  40.5 3.8 %project.3 = bf16[128,1024]{1,0:T(8,128)(2,1)S(1)} custom-call(s32[1]{0:T(128)} %bitcast.core_ref, bf16[128,2048]{1,0:T(8,128)(2,1)S(1)} %copy-done.7, bf16[2048,512]{1,0:T(8,128)(2,1)S(1)} %copy-done.2, bf16[2048,512]{1,0:T(8,128)(2,1)} %collective-permute-done.other_ref), custom_call_target="tpu_custom_call" | custom-call | flops 536870912 | bytes 4194304 | tf_op jit(solution)/shard_map/project/pallas_call | solution.py:201
  44.6 1.5 collective-permute-start.12
  46.6 6.5 %collective-permute-done.12.refs_2_ = bf16[64,2048]{1,0:T(8,128)(2,1)S(1)} collective-permute-done((bf16[64,2048]{1,0:T(8,128)(2,1)S(1)}, bf16[64,2048]{1,0:T(8,128)(2,1)S(1)}, u32[]{:S(2)}, u32[]{:S(2)}) %collective-permute-start.12) | collective-permute-done | bytes 262176 | tf_op jit(solution)/shard_map/ppermute | solution.py:375
  53.1 1.4 collective-permute-start.16
  56.6 1.4 collective-permute-start.10
  59.3 3.0 %collective-permute-done.16.refs_2_ = bf16[64,2048]{1,0:T(8,128)(2,1)S(1)} collective-permute-done((bf16[64,2048]{1,0:T(8,128)(2,1)S(1)}, bf16[64,2048]{1,0:T(8,128)(2,1)S(1)}, u32[]{:S(2)}, u32[]{:S(2)}) %collective-permute-start.16) | collective-permute-done | bytes 262176 | tf_op jit(solution)/shard_map/ppermute | solution.py:375
  62.3 1.4 collective-permute-start.20
  65.8 4.1 %collective-permute-done.10.refs_0_ = bf16[64,2048]{1,0:T(8,128)(2,1)S(1)} collective-permute-done((bf16[64,2048]{1,0:T(8,128)(2,1)S(1)}, bf16[64,2048]{1,0:T(8,128)(2,1)S(1)}, u32[]{:S(2)}, u32[]{:S(2)}) %collective-permute-start.10) | collective-permute-done | bytes 262176 | tf_op jit(solution)/shard_map/ppermute | solution.py:375
  71.3 1.4 collective-permute-start.17
  73.6 1.9 collective-permute-start.22
  76.2 4.7 %collective-permute-done.14.refs_0_ = bf16[64,2048]{1,0:T(8,128)(2,1)S(1)} collective-permute-done((bf16[64,2048]{1,0:T(8,128)(2,1)S(1)}, bf16[64,2048]{1,0:T(8,128)(2,1)S(1)}, u32[]{:S(2)}, u32[]{:S(2)}) %collective-permute-start.14) | collective-permute-done | bytes 262176 | tf_op jit(solution)/shard_map/ppermute | solution.py:375
  81.4 1.5 collective-permute-start.21
  83.7 8.2 %experts.9 = (bf16[64,2048]{1,0:T(8,128)(2,1)S(1)}, bf16[64,2048]{1,0:T(8,128)(2,1)}) custom-call(f32[128,2]{1,0:T(8,128)S(1)} %get-tuple-element.47.gate_ref, bf16[64,2048]{1,0:T(8,128)(2,1)S(1)} %collective-permute-done.22.refs_0_, bf16[64,2048]{1,0:T(8,128)(2,1)S(1)} %collective-permute-done.23.refs_1_, bf16[2048,768]{1,0:T(8,128)(2,1)S(1)} %bitcast.33, ...), custom_call_target="tpu_custom_call" | custom-call | flops 1207959552 | bytes 9437184 | tf_op jit(solution)/shard_map/experts/pallas_call | solution.py:274
  91.9 1.7 collective-permute-start.24
  93.7 9.4 %experts.8 = (f32[64,2048]{1,0:T(8,128)S(1)}, f32[64,2048]{1,0:T(8,128)S(1)}, f32[64,2048]{1,0:T(8,128)S(1)}, f32[64,2048]{1,0:T(8,128)S(1)}) custom-call(f32[256,2]{1,0:T(8,128)S(1)} %pad_maximum_fusion.3.gate_ref, bf16[64,2048]{1,0:T(8,128)(2,1)S(1)} %collective-permute-done.18.refs_0_, bf16[64,2048]{1,0:T(8,128)(2,1)S(1)} %collective-permute-done.19.refs_1_, ...), custom_call_target="tpu_custom_call" | custom-call | flops 2415919104 | bytes 9437184 | tf_op jit(solution)/shard_map/experts/pallas_call | solution.py:274
  107.1 1.9 add_on.10
  109.0 1.5 collective-permute-start.25
  115.2 9.3 %experts.7 = (f32[64,2048]{1,0:T(8,128)S(1)}, f32[64,2048]{1,0:T(8,128)S(1)}, f32[64,2048]{1,0:T(8,128)S(1)}, f32[64,2048]{1,0:T(8,128)S(1)}) custom-call(f32[256,2]{1,0:T(8,128)S(1)} %pad_maximum_fusion.2.gate_ref, bf16[64,2048]{1,0:T(8,128)(2,1)S(1)} %copy-done.41, bf16[64,2048]{1,0:T(8,128)(2,1)S(1)} %copy-done.39, bf16[64,2048]{1,0:T(8,128)(2,1)S(1)} %copy-done.37, ...), custom_call_target="tpu_custom_call" | custom-call | flops 2415919104 | bytes 9437184 | tf_op jit(solution)/shard_map/experts/pallas_call | solution.py:274
  127.8 1.7 collective-permute-start.31
  129.5 1.9 add_on.13
  131.7 1.9 add_on.17
  134.1 1.9 add_on.11
  136.0 1.5 collective-permute-start.26
  142.2 9.3 %experts.6 = (f32[64,2048]{1,0:T(8,128)S(1)}, f32[64,2048]{1,0:T(8,128)S(1)}, f32[64,2048]{1,0:T(8,128)S(1)}, f32[64,2048]{1,0:T(8,128)S(1)}) custom-call(f32[256,2]{1,0:T(8,128)S(1)} %pad_maximum_fusion.1.gate_ref, bf16[64,2048]{1,0:T(8,128)(2,1)S(1)} %copy-done.33, bf16[64,2048]{1,0:T(8,128)(2,1)S(1)} %copy-done.31, bf16[64,2048]{1,0:T(8,128)(2,1)S(1)} %copy-done.29, ...), custom_call_target="tpu_custom_call" | custom-call | flops 2415919104 | bytes 9437184 | tf_op jit(solution)/shard_map/experts/pallas_call | solution.py:274
  154.7 1.9 add_on.15
  156.6 1.7 collective-permute-start.32
  158.3 1.9 add_on.14
  160.1 1.9 add_on.18
  162.9 1.9 add_on.12
  164.7 1.5 collective-permute-start.27
  168.5 4.3 %state.1 = f32[2048,128]{1,0:T(8,128)} custom-call(bf16[128,2048]{1,0:T(8,128)(2,1)S(1)} %copy-done.27, bf16[128,128]{1,0:T(8,128)(2,1)S(1)} %copy-done.45, f32[32,128]{1,0:T(8,128)S(1)} %bitcast.46, f32[32,1]{1,0:T(8,128)S(1)} %copy.49.bias_ref, f32[32,1]{1,0:T(8,128)S(1)} %copy.50.a_ref, f32[2048,128]{1,0:T(8,128)S(1)} %bitcast.44), custom_call_target="tpu_custom_call" | custom-call | flops 70000000 | bytes 3000000 | tf_op jit(solution)/shard_map/state/pallas_call | solution.py:164
  172.8 7.6 %experts.5 = (f32[64,2048]{1,0:T(8,128)S(1)}, f32[64,2048]{1,0:T(8,128)S(1)}) custom-call(f32[128,2]{1,0:T(8,128)S(1)} %get-tuple-element.46.gate_ref, bf16[64,2048]{1,0:T(8,128)(2,1)S(1)} %copy-done.4, bf16[64,2048]{1,0:T(8,128)(2,1)S(1)} %maximum_select_fusion.1.refs_1_, bf16[2048,768]{1,0:T(8,128)(2,1)S(1)} %bitcast.41, bf16[2048,768]{1,0:T(8,128)(2,1)S(1)} %bitcast.42, ...), custom_call_target="tpu_custom_call" | custom-call | flops 1207959552 | bytes 9437184 | tf_op jit(solution)/shard_map/experts/pallas_call | solution.py:274
  181.9 2.0 %add_on.16 = bf16[64,2048]{1,0:T(8,128)(2,1)} custom-call(f32[64,2048]{1,0:T(8,128)} %copy-done.18, bf16[64,2048]{1,0:T(8,128)(2,1)} %collective-permute-done.32.got_ref), custom_call_target="tpu_custom_call" | custom-call | flops 131072 | bytes 1048576 | tf_op jit(solution)/shard_map/add_on/pallas_call | solution.py:297
  183.9 1.7 collective-permute-start.33
  185.6 1.9 add_on.19
  189.0 1.5 collective-permute-done.33
  190.5 3.6 %collective-permute-done.37 = bf16[64,2048]{1,0:T(8,128)(2,1)S(1)} collective-permute-done((bf16[64,2048]{1,0:T(8,128)(2,1)}, bf16[64,2048]{1,0:T(8,128)(2,1)S(1)}, u32[]{:S(2)}, u32[]{:S(2)}) %collective-permute-start.37) | collective-permute-done | bytes 262176 | tf_op jit(solution)/shard_map/ppermute | solution.py:375
  (181 shorter events, 50.2 us)
Async XLA Ops:
  0.6 43.9 %collective-permute-start.5 = (bf16[2048,768]{1,0:T(8,128)(2,1)}, bf16[2048,768]{1,0:T(8,128)(2,1)}, u32[]{:S(2)}, u32[]{:S(2)}) collective-permute-start(bf16[2048,768]{1,0:T(8,128)(2,1)} %bitcast.32), channel_id=1, source_target_pairs={{0,1},{1,0},{2,3},{3,2},{4,5},{5,4},{6,7},{7,6},{8,9},{9,8},{10,11... | collective-permute-start | bytes 9437192 | tf_op jit(solution)/shard_map/ppermute | solution.py:375
  1.1 28.9 %collective-permute-start = (bf16[2048,512]{1,0:T(8,128)(2,1)}, bf16[2048,512]{1,0:T(8,128)(2,1)}, u32[]{:S(2)}, u32[]{:S(2)}) collective-permute-start(bf16[2048,512]{1,0:T(8,128)(2,1)} %mine_ref.5), channel_id=1, source_target_pairs={{0,1},{1,0},{2,3},{3,2},{4,5},{5,4},{6,7},{7,6},{8,9},{9,8},{10,11... | collective-permute-start | bytes 6291464 | tf_op jit(solution)/shard_map/ppermute | solution.py:375
  1.9 16.8 %collective-permute-start.7 = (f32[128,16]{0,1:T(8,128)S(1)}, f32[128,16]{0,1:T(8,128)S(1)}, u32[]{:S(2)}, u32[]{:S(2)}) collective-permute-start(f32[128,16]{0,1:T(8,128)S(1)} %select_reduce_fusion.1), channel_id=1, source_target_pairs={{0,2},{1,3},{2,0},{3,1},{4,6},{5,7},{6,4},{7,5},{8,10},{9,11},{10,... | collective-permute-start | bytes 24584 | tf_op jit(solution)/shard_map/ppermute | solution.py:375
  17.1 13.0 %copy-start.1 = (bf16[2048,512]{1,0:T(8,128)(2,1)S(1)}, bf16[2048,512]{1,0:T(8,128)(2,1)}, u32[]{:S(2)}) copy-start(bf16[2048,512]{1,0:T(8,128)(2,1)} %mine_ref.5) | copy-start | bytes 6291460
  18.7 11.4 %collective-permute-start.3 = (bf16[64,2048]{1,0:T(8,128)(2,1)}, bf16[64,2048]{1,0:T(8,128)(2,1)S(1)}, u32[]{:S(2)}, u32[]{:S(2)}) collective-permute-start(bf16[64,2048]{1,0:T(8,128)(2,1)} %get-tuple-element.54), channel_id=1, source_target_pairs={{0,2},{1,3},{2,0},{3,1},{4,6},{5,7},{6,4},{7,5},{8,10},{9,11},{10,... | collective-permute-start | bytes 786440 | tf_op jit(solution)/shard_map/ppermute | solution.py:375
  18.7 25.8 %collective-permute-start.6 = (bf16[384,2048]{1,0:T(8,128)(2,1)}, bf16[384,2048]{1,0:T(8,128)(2,1)}, u32[]{:S(2)}, u32[]{:S(2)}) collective-permute-start(bf16[384,2048]{1,0:T(8,128)(2,1)} %bitcast.7.refs_4_.refs_6_), channel_id=1, source_target_pairs={{0,1},{1,0},{2,3},{3,2},{4,5},{5,4},{6,7},{7,6},{8,9},{9,8},{10,11... | collective-permute-start | bytes 4718600 | tf_op jit(solution)/shard_map/ppermute | solution.py:375
  18.7 3.9 %collective-permute-start.8 = (f32[2,1,128,16]{2,3,1,0:T(8,128)S(1)}, f32[2,1,128,16]{2,3,1,0:T(8,128)S(1)}, u32[]{:S(2)}, u32[]{:S(2)}) collective-permute-start(f32[2,1,128,16]{2,3,1,0:T(8,128)S(1)} %maximum_select_fusion.4), channel_id=1, source_target_pairs={{0,4},{1,5},{2,6},{3,7},{4,0},{5,1},{6,2},{7,3},{8,12},{9,13},{10,... | collective-permute-start | bytes 49160 | tf_op jit(solution)/shard_map/ppermute | solution.py:375
  22.6 5.2 %collective-permute-start.9 = (f32[2,2,128,16]{2,3,1,0:T(8,128)S(1)}, f32[2,2,128,16]{2,3,1,0:T(8,128)S(1)}, u32[]{:S(2)}, u32[]{:S(2)}) collective-permute-start(f32[2,2,128,16]{2,3,1,0:T(8,128)S(1)} %maximum_select_fusion.3), channel_id=1, source_target_pairs={{0,8},{1,9},{2,10},{3,11},{4,12},{5,13},{6,14},{7,15},{8,0},{9,1},... | collective-permute-start | bytes 98312 | tf_op jit(solution)/shard_map/ppermute | solution.py:375
  27.8 6.6 %collective-permute-start.1 = (bf16[64,2048]{1,0:T(8,128)(2,1)S(1)}, bf16[64,2048]{1,0:T(8,128)(2,1)S(1)}, u32[]{:S(2)}, u32[]{:S(2)}) collective-permute-start(bf16[64,2048]{1,0:T(8,128)(2,1)S(1)} %get-tuple-element.55), channel_id=1, source_target_pairs={{0,2},{1,3},{2,0},{3,1},{4,6},{5,7},{6,4},{7,5},{8,10},{9,11},{10,... | collective-permute-start | bytes 786440 | tf_op jit(solution)/shard_map/ppermute | solution.py:375
  33.7 6.9 %copy-start.2 = (bf16[2048,512]{1,0:T(8,128)(2,1)S(1)}, bf16[2048,512]{1,0:T(8,128)(2,1)}, u32[]{:S(2)}) copy-start(bf16[2048,512]{1,0:T(8,128)(2,1)} %mine_ref.5) | copy-start | bytes 6291460
  33.7 10.7 %collective-permute-start.4 = (bf16[64,1024]{1,0:T(8,128)(2,1)S(1)}, bf16[64,1024]{1,0:T(8,128)(2,1)S(1)}, u32[]{:S(2)}, u32[]{:S(2)}) collective-permute-start(bf16[64,1024]{1,0:T(8,128)(2,1)S(1)} %project.5), channel_id=1, source_target_pairs={{0,2},{1,3},{2,0},{3,1},{4,6},{5,7},{6,4},{7,5},{8,10},{9,11},{10,... | collective-permute-start | bytes 393224 | tf_op jit(solution)/shard_map/ppermute | solution.py:375
  38.0 6.4 %collective-permute-start.2 = (bf16[64,1024]{1,0:T(8,128)(2,1)S(1)}, bf16[64,1024]{1,0:T(8,128)(2,1)S(1)}, u32[]{:S(2)}, u32[]{:S(2)}) collective-permute-start(bf16[64,1024]{1,0:T(8,128)(2,1)S(1)} %project.4), channel_id=1, source_target_pairs={{0,2},{1,3},{2,0},{3,1},{4,6},{5,7},{6,4},{7,5},{8,10},{9,11},{10,... | collective-permute-start | bytes 393224 | tf_op jit(solution)/shard_map/ppermute | solution.py:375
  40.5 43.2 %copy-start = (bf16[1,2048,768]{2,1,0:T(8,128)(2,1)S(1)}, bf16[1,2048,768]{2,1,0:T(8,128)(2,1)}, u32[]{:S(2)}) copy-start(bf16[1,2048,768]{2,1,0:T(8,128)(2,1)} %param.26) | copy-start | bytes 9437188
  44.6 8.5 %collective-permute-start.12 = (bf16[64,2048]{1,0:T(8,128)(2,1)S(1)}, bf16[64,2048]{1,0:T(8,128)(2,1)S(1)}, u32[]{:S(2)}, u32[]{:S(2)}) collective-permute-start(bf16[64,2048]{1,0:T(8,128)(2,1)S(1)} %maximum_select_fusion.refs_0_), channel_id=1, source_target_pairs={{0,4},{1,5},{2,0},{3,1},{4,8},{5,9},{6,2},{7,3},{8,12},{9,13},{10,... | collective-permute-start | bytes 786440 | tf_op jit(solution)/shard_map/ppermute | solution.py:375
  46.1 9.1 %collective-permute-start.11 = (bf16[64,2048]{1,0:T(8,128)(2,1)S(1)}, bf16[64,2048]{1,0:T(8,128)(2,1)S(1)}, u32[]{:S(2)}, u32[]{:S(2)}) collective-permute-start(bf16[64,2048]{1,0:T(8,128)(2,1)S(1)} %maximum_select_fusion.1.refs_1_), channel_id=1, source_target_pairs={{0,2},{1,3},{2,6},{3,7},{4,0},{5,1},{6,10},{7,11},{8,4},{9,5},{10,... | collective-permute-start | bytes 786440 | tf_op jit(solution)/shard_map/ppermute | solution.py:375
  53.1 9.2 %collective-permute-start.16 = (bf16[64,2048]{1,0:T(8,128)(2,1)S(1)}, bf16[64,2048]{1,0:T(8,128)(2,1)S(1)}, u32[]{:S(2)}, u32[]{:S(2)}) collective-permute-start(bf16[64,2048]{1,0:T(8,128)(2,1)S(1)} %collective-permute-done.12.refs_2_), channel_id=1, source_target_pairs={{0,4},{1,5},{2,0},{3,1},{4,8},{5,9},{6,2},{7,3},{8,12},{9,13},{10,... | collective-permute-start | bytes 786440 | tf_op jit(solution)/shard_map/ppermute | solution.py:375
  55.2 9.2 %collective-permute-start.15 = (bf16[64,2048]{1,0:T(8,128)(2,1)S(1)}, bf16[64,2048]{1,0:T(8,128)(2,1)S(1)}, u32[]{:S(2)}, u32[]{:S(2)}) collective-permute-start(bf16[64,2048]{1,0:T(8,128)(2,1)S(1)} %collective-permute-done.11.refs_1_), channel_id=1, source_target_pairs={{0,2},{1,3},{2,6},{3,7},{4,0},{5,1},{6,10},{7,11},{8,4},{9,5},{10,... | collective-permute-start | bytes 786440 | tf_op jit(solution)/shard_map/ppermute | solution.py:375
  56.6 13.3 %collective-permute-start.10 = (bf16[64,2048]{1,0:T(8,128)(2,1)S(1)}, bf16[64,2048]{1,0:T(8,128)(2,1)S(1)}, u32[]{:S(2)}, u32[]{:S(2)}) collective-permute-start(bf16[64,2048]{1,0:T(8,128)(2,1)S(1)} %maximum_select_fusion.refs_0_), channel_id=1, source_target_pairs={{0,2},{1,3},{2,6},{3,7},{4,0},{5,1},{6,10},{7,11},{8,4},{9,5},{10,... | collective-permute-start | bytes 786440 | tf_op jit(solution)/shard_map/ppermute | solution.py:375
  58.7 12.6 %collective-permute-start.13 = (bf16[64,2048]{1,0:T(8,128)(2,1)S(1)}, bf16[64,2048]{1,0:T(8,128)(2,1)S(1)}, u32[]{:S(2)}, u32[]{:S(2)}) collective-permute-start(bf16[64,2048]{1,0:T(8,128)(2,1)S(1)} %maximum_select_fusion.1.refs_1_), channel_id=1, source_target_pairs={{0,4},{1,5},{2,0},{3,1},{4,8},{5,9},{6,2},{7,3},{8,12},{9,13},{10,... | collective-permute-start | bytes 786440 | tf_op jit(solution)/shard_map/ppermute | solution.py:375
  62.3 11.2 %collective-permute-start.20 = (bf16[64,2048]{1,0:T(8,128)(2,1)S(1)}, bf16[64,2048]{1,0:T(8,128)(2,1)S(1)}, u32[]{:S(2)}, u32[]{:S(2)}) collective-permute-start(bf16[64,2048]{1,0:T(8,128)(2,1)S(1)} %collective-permute-done.16.refs_2_), channel_id=1, source_target_pairs={{0,4},{1,5},{2,0},{3,1},{4,8},{5,9},{6,2},{7,3},{8,12},{9,13},{10,... | collective-permute-start | bytes 786440 | tf_op jit(solution)/shard_map/ppermute | solution.py:375
  64.4 11.1 %collective-permute-start.19 = (bf16[64,2048]{1,0:T(8,128)(2,1)S(1)}, bf16[64,2048]{1,0:T(8,128)(2,1)S(1)}, u32[]{:S(2)}, u32[]{:S(2)}) collective-permute-start(bf16[64,2048]{1,0:T(8,128)(2,1)S(1)} %collective-permute-done.15.refs_1_), channel_id=1, source_target_pairs={{0,2},{1,3},{2,6},{3,7},{4,0},{5,1},{6,10},{7,11},{8,4},{9,5},{10,... | collective-permute-start | bytes 786440 | tf_op jit(solution)/shard_map/ppermute | solution.py:375
  69.9 11.0 %collective-permute-start.14 = (bf16[64,2048]{1,0:T(8,128)(2,1)S(1)}, bf16[64,2048]{1,0:T(8,128)(2,1)S(1)}, u32[]{:S(2)}, u32[]{:S(2)}) collective-permute-start(bf16[64,2048]{1,0:T(8,128)(2,1)S(1)} %collective-permute-done.10.refs_0_), channel_id=1, source_target_pairs={{0,2},{1,3},{2,6},{3,7},{4,0},{5,1},{6,10},{7,11},{8,4},{9,5},{10,... | collective-permute-start | bytes 786440 | tf_op jit(solution)/shard_map/ppermute | solution.py:375
  71.3 10.1 %collective-permute-start.17 = (bf16[64,2048]{1,0:T(8,128)(2,1)S(1)}, bf16[64,2048]{1,0:T(8,128)(2,1)S(1)}, u32[]{:S(2)}, u32[]{:S(2)}) collective-permute-start(bf16[64,2048]{1,0:T(8,128)(2,1)S(1)} %collective-permute-done.13.refs_3_), channel_id=1, source_target_pairs={{0,4},{1,5},{2,0},{3,1},{4,8},{5,9},{6,2},{7,3},{8,12},{9,13},{10,... | collective-permute-start | bytes 786440 | tf_op jit(solution)/shard_map/ppermute | solution.py:375
  73.6 10.1 %collective-permute-start.22 = (bf16[64,2048]{1,0:T(8,128)(2,1)S(1)}, bf16[64,2048]{1,0:T(8,128)(2,1)S(1)}, u32[]{:S(2)}, u32[]{:S(2)}) collective-permute-start(bf16[64,2048]{1,0:T(8,128)(2,1)S(1)} %collective-permute-done.20.refs_2_), channel_id=1, source_target_pairs={{0,4},{1,5},{2,0},{3,1},{4,8},{5,9},{6,2},{7,3},{8,12},{9,13},{10,... | collective-permute-start | bytes 786440 | tf_op jit(solution)/shard_map/ppermute | solution.py:375
  75.5 8.2 %collective-permute-start.23 = (bf16[64,2048]{1,0:T(8,128)(2,1)S(1)}, bf16[64,2048]{1,0:T(8,128)(2,1)S(1)}, u32[]{:S(2)}, u32[]{:S(2)}) collective-permute-start(bf16[64,2048]{1,0:T(8,128)(2,1)S(1)} %collective-permute-done.19.refs_1_), channel_id=1, source_target_pairs={{0,2},{1,3},{2,6},{3,7},{4,0},{5,1},{6,10},{7,11},{8,4},{9,5},{10,... | collective-permute-start | bytes 786440 | tf_op jit(solution)/shard_map/ppermute | solution.py:375
  80.9 11.0 %copy-start.40 = (bf16[64,2048]{1,0:T(8,128)(2,1)}, bf16[64,2048]{1,0:T(8,128)(2,1)S(1)}, u32[]{:S(2)}) copy-start(bf16[64,2048]{1,0:T(8,128)(2,1)S(1)} %collective-permute-done.14.refs_0_) | copy-start | bytes 786436
  80.9 12.8 %collective-permute-start.18 = (bf16[64,2048]{1,0:T(8,128)(2,1)S(1)}, bf16[64,2048]{1,0:T(8,128)(2,1)S(1)}, u32[]{:S(2)}, u32[]{:S(2)}) collective-permute-start(bf16[64,2048]{1,0:T(8,128)(2,1)S(1)} %collective-permute-done.14.refs_0_), channel_id=1, source_target_pairs={{0,2},{1,3},{2,6},{3,7},{4,0},{5,1},{6,10},{7,11},{8,4},{9,5},{10,... | collective-permute-start | bytes 786440 | tf_op jit(solution)/shard_map/ppermute | solution.py:375
  81.4 10.5 %copy-start.42 = (bf16[64,2048]{1,0:T(8,128)(2,1)}, bf16[64,2048]{1,0:T(8,128)(2,1)S(1)}, u32[]{:S(2)}) copy-start(bf16[64,2048]{1,0:T(8,128)(2,1)S(1)} %collective-permute-done.17.refs_3_) | copy-start | bytes 786436
  81.4 12.3 %collective-permute-start.21 = (bf16[64,2048]{1,0:T(8,128)(2,1)S(1)}, bf16[64,2048]{1,0:T(8,128)(2,1)S(1)}, u32[]{:S(2)}, u32[]{:S(2)}) collective-permute-start(bf16[64,2048]{1,0:T(8,128)(2,1)S(1)} %collective-permute-done.17.refs_3_), channel_id=1, source_target_pairs={{0,4},{1,5},{2,0},{3,1},{4,8},{5,9},{6,2},{7,3},{8,12},{9,13},{10,... | collective-permute-start | bytes 786440 | tf_op jit(solution)/shard_map/ppermute | solution.py:375
  91.9 14.5 %collective-permute-start.24 = (bf16[64,2048]{1,0:T(8,128)(2,1)S(1)}, bf16[64,2048]{1,0:T(8,128)(2,1)S(1)}, u32[]{:S(2)}, u32[]{:S(2)}) collective-permute-start(bf16[64,2048]{1,0:T(8,128)(2,1)S(1)} %get-tuple-element.33), channel_id=1, source_target_pairs={{0,4},{1,5},{2,0},{3,1},{4,8},{5,9},{6,2},{7,3},{8,12},{9,13},{10,... | collective-permute-start | bytes 786440 | tf_op jit(solution)/shard_map/ppermute | solution.py:375
  105.5 24.0 %collective-permute-start.28 = (bf16[64,2048]{1,0:T(8,128)(2,1)}, bf16[64,2048]{1,0:T(8,128)(2,1)}, u32[]{:S(2)}, u32[]{:S(2)}) collective-permute-start(bf16[64,2048]{1,0:T(8,128)(2,1)} %convert_element_type.32), channel_id=1, source_target_pairs={{0,2},{1,3},{2,6},{3,7},{4,0},{5,1},{6,10},{7,11},{8,4},{9,5},{10,... | collective-permute-start | bytes 786440 | tf_op jit(solution)/shard_map/ppermute | solution.py:375
  105.9 25.8 %collective-permute-start.34 = (bf16[64,2048]{1,0:T(8,128)(2,1)}, bf16[64,2048]{1,0:T(8,128)(2,1)}, u32[]{:S(2)}, u32[]{:S(2)}) collective-permute-start(bf16[64,2048]{1,0:T(8,128)(2,1)} %get-tuple-element.44), channel_id=1, source_target_pairs={{0,2},{1,3},{2,6},{3,7},{4,0},{5,1},{6,10},{7,11},{8,4},{9,5},{10,... | collective-permute-start | bytes 786440 | tf_op jit(solution)/shard_map/ppermute | solution.py:375
  109.0 25.1 %collective-permute-start.25 = (bf16[64,2048]{1,0:T(8,128)(2,1)}, bf16[64,2048]{1,0:T(8,128)(2,1)}, u32[]{:S(2)}, u32[]{:S(2)}) collective-permute-start(bf16[64,2048]{1,0:T(8,128)(2,1)} %add_on.10), channel_id=1, source_target_pairs={{0,4},{1,5},{2,0},{3,1},{4,8},{5,9},{6,2},{7,3},{8,12},{9,13},{10,... | collective-permute-start | bytes 786440 | tf_op jit(solution)/shard_map/ppermute | solution.py:375
  115.2 11.7 %copy-start.15 = (f32[64,2048]{1,0:T(8,128)S(1)}, f32[64,2048]{1,0:T(8,128)}, u32[]{:S(2)}) copy-start(f32[64,2048]{1,0:T(8,128)} %copy-done.14) | copy-start | bytes 1572868
  127.8 26.9 %collective-permute-start.31 = (bf16[64,2048]{1,0:T(8,128)(2,1)}, bf16[64,2048]{1,0:T(8,128)(2,1)}, u32[]{:S(2)}, u32[]{:S(2)}) collective-permute-start(bf16[64,2048]{1,0:T(8,128)(2,1)} %convert_element_type.36), channel_id=1, source_target_pairs={{0,4},{1,5},{2,0},{3,1},{4,8},{5,9},{6,2},{7,3},{8,12},{9,13},{10,... | collective-permute-start | bytes 786440 | tf_op jit(solution)/shard_map/ppermute | solution.py:375
  131.4 26.9 %collective-permute-start.29 = (bf16[64,2048]{1,0:T(8,128)(2,1)}, bf16[64,2048]{1,0:T(8,128)(2,1)}, u32[]{:S(2)}, u32[]{:S(2)}) collective-permute-start(bf16[64,2048]{1,0:T(8,128)(2,1)} %add_on.13), channel_id=1, source_target_pairs={{0,2},{1,3},{2,6},{3,7},{4,0},{5,1},{6,10},{7,11},{8,4},{9,5},{10,... | collective-permute-start | bytes 786440 | tf_op jit(solution)/shard_map/ppermute | solution.py:375
  133.6 26.6 %collective-permute-start.35 = (bf16[64,2048]{1,0:T(8,128)(2,1)}, bf16[64,2048]{1,0:T(8,128)(2,1)}, u32[]{:S(2)}, u32[]{:S(2)}) collective-permute-start(bf16[64,2048]{1,0:T(8,128)(2,1)} %add_on.17), channel_id=1, source_target_pairs={{0,2},{1,3},{2,6},{3,7},{4,0},{5,1},{6,10},{7,11},{8,4},{9,5},{10,... | collective-permute-start | bytes 786440 | tf_op jit(solution)/shard_map/ppermute | solution.py:375
  136.0 26.9 %collective-permute-start.26 = (bf16[64,2048]{1,0:T(8,128)(2,1)}, bf16[64,2048]{1,0:T(8,128)(2,1)}, u32[]{:S(2)}, u32[]{:S(2)}) collective-permute-start(bf16[64,2048]{1,0:T(8,128)(2,1)} %add_on.11), channel_id=1, source_target_pairs={{0,4},{1,5},{2,0},{3,1},{4,8},{5,9},{6,2},{7,3},{8,12},{9,13},{10,... | collective-permute-start | bytes 786440 | tf_op jit(solution)/shard_map/ppermute | solution.py:375
  154.7 11.5 %copy-start.45 = (bf16[128,128]{1,0:T(8,128)(2,1)S(1)}, bf16[128,128]{1,0:T(8,128)(2,1)}, u32[]{:S(2)}) copy-start(bf16[128,128]{1,0:T(8,128)(2,1)} %b_ref.3) | copy-start | bytes 98308
  154.7 11.5 %copy-start.47 = (f32[128,32]{0,1:T(8,128)S(1)}, f32[128,32]{0,1:T(8,128)}, u32[]{:S(2)}) copy-start(f32[128,32]{0,1:T(8,128)} %param.19) | copy-start | bytes 49156
  156.6 25.4 %collective-permute-start.32 = (bf16[64,2048]{1,0:T(8,128)(2,1)}, bf16[64,2048]{1,0:T(8,128)(2,1)}, u32[]{:S(2)}, u32[]{:S(2)}) collective-permute-start(bf16[64,2048]{1,0:T(8,128)(2,1)} %add_on.15), channel_id=1, source_target_pairs={{0,4},{1,5},{2,0},{3,1},{4,8},{5,9},{6,2},{7,3},{8,12},{9,13},{10,... | collective-permute-start | bytes 786440 | tf_op jit(solution)/shard_map/ppermute | solution.py:375
  162.0 23.6 %collective-permute-start.36 = (bf16[64,2048]{1,0:T(8,128)(2,1)}, bf16[64,2048]{1,0:T(8,128)(2,1)}, u32[]{:S(2)}, u32[]{:S(2)}) collective-permute-start(bf16[64,2048]{1,0:T(8,128)(2,1)} %add_on.18), channel_id=1, source_target_pairs={{0,2},{1,3},{2,6},{3,7},{4,0},{5,1},{6,10},{7,11},{8,4},{9,5},{10,... | collective-permute-start | bytes 786440 | tf_op jit(solution)/shard_map/ppermute | solution.py:375
  162.3 25.5 %collective-permute-start.30 = (bf16[64,2048]{1,0:T(8,128)(2,1)}, bf16[64,2048]{1,0:T(8,128)(2,1)}, u32[]{:S(2)}, u32[]{:S(2)}) collective-permute-start(bf16[64,2048]{1,0:T(8,128)(2,1)} %add_on.14), channel_id=1, source_target_pairs={{0,2},{1,3},{2,6},{3,7},{4,0},{5,1},{6,10},{7,11},{8,4},{9,5},{10,... | collective-permute-start | bytes 786440 | tf_op jit(solution)/shard_map/ppermute | solution.py:375
  164.7 8.0 %copy-start.4 = (bf16[64,2048]{1,0:T(8,128)(2,1)S(1)}, bf16[64,2048]{1,0:T(8,128)(2,1)}, u32[]{:S(2)}) copy-start(bf16[64,2048]{1,0:T(8,128)(2,1)} %copy-done.3) | copy-start | bytes 786436
  164.7 23.1 %collective-permute-start.27 = (bf16[64,2048]{1,0:T(8,128)(2,1)}, bf16[64,2048]{1,0:T(8,128)(2,1)}, u32[]{:S(2)}, u32[]{:S(2)}) collective-permute-start(bf16[64,2048]{1,0:T(8,128)(2,1)} %add_on.12), channel_id=1, source_target_pairs={{0,4},{1,5},{2,0},{3,1},{4,8},{5,9},{6,2},{7,3},{8,12},{9,13},{10,... | collective-permute-start | bytes 786440 | tf_op jit(solution)/shard_map/ppermute | solution.py:375
  181.9 12.1 %copy-start.11 = (f32[64,2048]{1,0:T(8,128)S(1)}, f32[64,2048]{1,0:T(8,128)}, u32[]{:S(2)}) copy-start(f32[64,2048]{1,0:T(8,128)} %copy-done.10) | copy-start | bytes 1572868
  183.9 6.6 %collective-permute-start.33 = (bf16[64,2048]{1,0:T(8,128)(2,1)}, bf16[64,2048]{1,0:T(8,128)(2,1)S(1)}, u32[]{:S(2)}, u32[]{:S(2)}) collective-permute-start(bf16[64,2048]{1,0:T(8,128)(2,1)} %add_on.16), channel_id=1, source_target_pairs={{0,4},{1,5},{2,0},{3,1},{4,8},{5,9},{6,2},{7,3},{8,12},{9,13},{10,... | collective-permute-start | bytes 786440 | tf_op jit(solution)/shard_map/ppermute | solution.py:375
  187.5 6.6 %collective-permute-start.37 = (bf16[64,2048]{1,0:T(8,128)(2,1)}, bf16[64,2048]{1,0:T(8,128)(2,1)S(1)}, u32[]{:S(2)}, u32[]{:S(2)}) collective-permute-start(bf16[64,2048]{1,0:T(8,128)(2,1)} %add_on.19), channel_id=1, source_target_pairs={{0,2},{1,3},{2,6},{3,7},{4,0},{5,1},{6,10},{7,11},{8,4},{9,5},{10,... | collective-permute-start | bytes 786440 | tf_op jit(solution)/shard_map/ppermute | solution.py:375
  (42 other events, 51.9 us)

commit v5 on v4

v5 whole, which is shorter than its diff:
```python
import functools

import jax
import jax.numpy as jnp
from jax import lax
from jax.experimental import pallas as pl
from jax.experimental.pallas import tpu as pltpu
from jax.sharding import PartitionSpec as P

epsilon = 1e-05


CHUNK = 8
NT = (((1,), (1,)), ((), ()))
TN = (((0,), (0,)), ((), ()))


def decays(dt_ref, bias_ref, a_ref, step_ref, decay_ref):
    frames, heads = dt_ref.shape
    step_size = jax.nn.softplus(dt_ref[...] + bias_ref[...])
    rise = step_size * -jnp.exp(a_ref[...])
    s = lax.broadcasted_iota(jnp.int32, (frames, frames), 0)
    t = lax.broadcasted_iota(jnp.int32, (frames, frames), 1)
    upto = jnp.where(s <= t, 1.0, 0.0)
    step_ref[...] = step_size.T
    decay_ref[...] = jnp.dot(
        rise.T, upto, precision=lax.Precision.HIGHEST, preferred_element_type=jnp.float32
    )


def mixer_kernel(
    skip_ref,
    x_ref,
    z_ref,
    b_ref,
    c_ref,
    dt_ref,
    bias_ref,
    a_ref,
    gain_ref,
    state_ref,
    out_ref,
    g_ref,
    ss_ref,
    step_ref,
    decay_ref,
):
    i = pl.program_id(0)
    frames, width = x_ref.shape
    head = width // CHUNK
    pl.when(i == 0)(lambda: decays(dt_ref, bias_ref, a_ref, step_ref, decay_ref))
    chunk = pl.ds(pl.multiple_of(i * CHUNK, CHUNK), CHUNK)
    step_size, decay = step_ref[chunk, :], decay_ref[chunk, :]
    decay_col = decay.T
    carry_col = jnp.exp(decay_col)
    t = lax.broadcasted_iota(jnp.int32, (frames, frames), 0)
    s = lax.broadcasted_iota(jnp.int32, (frames, frames), 1)
    c = c_ref[...]
    scores = lax.dot_general(c, b_ref[...], NT, preferred_element_type=jnp.float32)
    scores = jnp.where(s <= t, scores, 0.0)
    cc = jnp.concatenate([c, c], axis=1)
    left = lax.broadcasted_iota(jnp.int32, (frames, 2 * head), 1) < head
    squares = None
    for pair in range(CHUNK // 2):
        mixes = []
        for h in (2 * pair, 2 * pair + 1):
            spread = jnp.exp(jnp.minimum(decay_col[:, h : h + 1] - decay[h : h + 1, :], 0.0))
            mixes.append((spread * (scores * step_size[h : h + 1, :])).astype(jnp.bfloat16))
        at = slice(2 * head * pair, 2 * head * (pair + 1))
        x = x_ref[:, at]
        zero = jnp.zeros_like(x)
        y = jnp.dot(
            jnp.concatenate(mixes, axis=1),
            jnp.concatenate([jnp.where(left, x, zero), jnp.where(left, zero, x)], axis=0),
            preferred_element_type=jnp.float32,
        )
        state = state_ref[at, :]
        high = state.astype(jnp.bfloat16)
        low = (state - high.astype(jnp.float32)).astype(jnp.bfloat16)
        carried = lax.dot_general(
            cc, jnp.concatenate([high, low], axis=1), NT, preferred_element_type=jnp.float32
        )
        factor = jnp.where(
            left, carry_col[:, 2 * pair : 2 * pair + 1], carry_col[:, 2 * pair + 1 : 2 * pair + 2]
        )
        skip = jnp.where(left[:1], skip_ref[i * CHUNK + 2 * pair], skip_ref[i * CHUNK + 2 * pair + 1])
        mixed = y + factor * carried + skip * x.astype(jnp.float32)
        z = z_ref[:, at].astype(jnp.float32)
        g = mixed * jax.nn.silu(z)
        g_ref[i, :, at] = g
        squares = g * g if squares is None else squares + g * g

    @pl.when(i == 0)
    def _():
        ss_ref[...] = squares

    @pl.when(i > 0)
    def _():
        ss_ref[...] += squares

    steps = g_ref.shape[0]

    @pl.when(i == steps - 1)
    def _():
        mean = jnp.sum(ss_ref[...], axis=1, keepdims=True) / (steps * width)
        scale = lax.rsqrt(mean + epsilon)
        for j in range(steps):
            at = slice(j * width, (j + 1) * width)
            out_ref[:, at] = (g_ref[j] * scale * gain_ref[:, at]).astype(jnp.bfloat16)


def state_kernel(x_ref, b_ref, dt_ref, bias_ref, a_ref, state_ref, out_ref, step_ref, decay_ref):
    i = pl.program_id(0)
    frames, width = x_ref.shape
    head = width // CHUNK
    pl.when(i == 0)(lambda: decays(dt_ref, bias_ref, a_ref, step_ref, decay_ref))
    chunk = pl.ds(pl.multiple_of(i * CHUNK, CHUNK), CHUNK)
    step_size, decay = step_ref[chunk, :], decay_ref[chunk, :]
    end = decay[:, frames - 1 : frames]
    tail = (jnp.exp(end - decay) * step_size).T
    kept = jnp.exp(end)
    left = lax.broadcasted_iota(jnp.int32, (frames, 2 * head), 1) < head
    upper = lax.broadcasted_iota(jnp.int32, (2 * head, b_ref.shape[1]), 0) < head
    for pair in range(CHUNK // 2):
        at = slice(2 * head * pair, 2 * head * (pair + 1))
        factor = jnp.where(left, tail[:, 2 * pair : 2 * pair + 1], tail[:, 2 * pair + 1 : 2 * pair + 2])
        scaled = (x_ref[:, at].astype(jnp.float32) * factor).astype(jnp.bfloat16)
        added = lax.dot_general(scaled, b_ref[...], TN, preferred_element_type=jnp.float32)
        keep = jnp.where(upper, kept[2 * pair : 2 * pair + 1, :], kept[2 * pair + 1 : 2 * pair + 2, :])
        out_ref[at, :] = keep * state_ref[at, :] + added


def ssm_mixer(
    ssm_input, gate_input, b_proj, c_proj, dt_raw, a_log, dt_bias, d_skip, norm_gain, state_in
):
    frames, width = ssm_input.shape
    heads, head, inner = state_in.shape
    steps = heads // CHUNK
    part = width // steps
    state = state_in.reshape(width, inner)
    column = pl.BlockSpec((frames, part), lambda i: (0, i))
    whole = pl.BlockSpec((frames, inner), lambda i: (0, 0))
    per_head = pl.BlockSpec((frames, heads), lambda i: (0, 0))
    scalar = pl.BlockSpec((1, heads), lambda i: (0, 0))
    rows = pl.BlockSpec((part, inner), lambda i: (i, 0))
    full_row = pl.BlockSpec((1, width), lambda i: (0, 0))
    tables = [pltpu.VMEM((heads, frames), jnp.float32)] * 2
    normed = pl.pallas_call(
        mixer_kernel,
        grid=(steps,),
        in_specs=[
            pl.BlockSpec(memory_space=pltpu.SMEM),
            column,
            column,
            whole,
            whole,
            per_head,
            scalar,
            scalar,
            full_row,
            rows,
        ],
        out_specs=pl.BlockSpec((frames, width), lambda i: (0, 0)),
        out_shape=jax.ShapeDtypeStruct((frames, width), jnp.bfloat16),
        scratch_shapes=[
            pltpu.VMEM((steps, frames, part), jnp.float32),
            pltpu.VMEM((frames, 2 * head), jnp.float32),
            *tables,
        ],
        compiler_params=pltpu.CompilerParams(vmem_limit_bytes=56 << 20),
        cost_estimate=pl.CostEstimate(flops=400_000_000, bytes_accessed=6_000_000, transcendentals=2_000_000),
        name="mixer",
    )(
        d_skip,
        ssm_input,
        gate_input,
        b_proj,
        c_proj,
        dt_raw,
        dt_bias[None, :],
        a_log[None, :],
        norm_gain[None, :],
        state,
    )

    def state_next(ssm_input):
        out = pl.pallas_call(
            state_kernel,
            grid=(steps,),
            in_specs=[column, whole, per_head, scalar, scalar, rows],
            out_specs=rows,
            out_shape=jax.ShapeDtypeStruct((width, inner), jnp.float32),
            scratch_shapes=tables,
            compiler_params=pltpu.CompilerParams(vmem_limit_bytes=16 << 20),
            cost_estimate=pl.CostEstimate(flops=70_000_000, bytes_accessed=3_000_000, transcendentals=20_000),
            name="state",
        )(ssm_input, b_proj, dt_raw, dt_bias[None, :], a_log[None, :], state)
        return out.reshape(heads, head, inner)

    return (normed, state_next)


def slot_positions(route_ids, experts):
    flat_ids = route_ids.reshape(-1)
    onehot = (flat_ids[:, None] == jnp.arange(experts, dtype=jnp.int32)[None, :]).astype(jnp.int32)
    earlier = jnp.cumsum(onehot, axis=0) - onehot
    return (flat_ids, jnp.sum(earlier * onehot, axis=1))


def body(
    ssm_input,
    gate_input,
    b_proj,
    c_proj,
    dt_raw,
    a_log,
    dt_bias,
    d_skip,
    norm_gain,
    state_in,
    out_proj,
    expert_in,
    expert_out,
    route_ids,
    route_weights,
):
    normed, state_next = ssm_mixer(
        ssm_input,
        gate_input,
        b_proj,
        c_proj,
        dt_raw,
        a_log,
        dt_bias,
        d_skip,
        norm_gain,
        state_in[0],
    )
    frames_here, topk_count = route_ids.shape
    local_experts = expert_in.shape[0]
    experts = local_experts * lax.axis_size(("wide", "narrow"))
    wide, narrow = lax.axis_size("wide"), lax.axis_size("narrow")
    if experts <= 4 * topk_count and narrow == 4 and wide & (wide - 1) == 0 and local_experts == 1:
        layer_out, state = dense_experts(
            normed,
            out_proj,
            expert_in[0],
            expert_out[0],
            route_ids,
            route_weights,
            functools.partial(state_next, ssm_input),
        )
    else:
        layer_out = routed_experts(normed, out_proj, expert_in, expert_out, route_ids, route_weights)
        state = state_next(ssm_input)
    return (layer_out, state[None])


def routes(wide, move):
    pairs = []
    for z in range(wide):
        for x in range(2):
            for core in range(2):
                to = move(z, x, core)
                pairs.append(((z * 2 + x) * 2 + core, (to[0] * 2 + to[1]) * 2 + to[2]))
    return pairs


def dense_experts(normed, out_proj, expert_in, expert_out, route_ids, route_weights, state_next):
    frames = route_ids.shape[0]
    wide = lax.axis_size("wide")
    ring = 2 * wide
    z = lax.axis_index("wide")
    x, core = lax.axis_index("narrow") // 2, lax.axis_index("narrow") % 2
    place = jnp.where(x == 0, z, ring - 1 - z)
    axes = ("wide", "narrow")

    def send(value, move):
        return lax.ppermute(value, axes, routes(wide, move))

    def to_core(value):
        return send(value, lambda z, x, c: (z, x, 1 - c))

    def to_x(value):
        return send(value, lambda z, x, c: (z, 1 - x, c))

    def along(value, step):
        def move(z, x, c):
            p = ((z if x == 0 else ring - 1 - z) + step) % ring
            return (p, 0, c) if p < wide else (ring - 1 - p, 1, c)

        return send(value, move)

    out_other, in_other, down_other = to_core(out_proj), to_core(expert_in), to_core(expert_out)

    halves = range(2)
    size = frames // 2
    sent = [to_x(normed[h * size : (h + 1) * size]) for h in halves]

    columns = lax.optimization_barrier(
        jnp.where(
            core == 0,
            jnp.concatenate([out_proj, out_other], axis=1),
            jnp.concatenate([out_other, out_proj], axis=1),
        )
    )

    def project(rows):
        return jnp.dot(rows, columns, preferred_element_type=jnp.float32).astype(jnp.bfloat16)

    own = project(normed)
    rows, backs = [], []
    for h in halves:
        backs.append(to_x(project(sent[h])))
        here = own[h * size : (h + 1) * size]
        rows.append(
            jnp.where(
                x == 0,
                jnp.concatenate([here, backs[h]], axis=1),
                jnp.concatenate([backs[h], here], axis=1),
            )
        )

    experts = wide * 4
    gates = jnp.sum(
        jnp.where(route_ids[:, :, None] == jnp.arange(experts), route_weights[:, :, None], 0.0), axis=1
    )
    gates, _ = lax.optimization_barrier((gates, normed))
    other = to_x(gates)
    gates = jnp.where(x == 0, jnp.stack([gates, other]), jnp.stack([other, gates]))[:, None]
    step = 1
    while step < wide:
        gates, _ = lax.optimization_barrier((gates, sent[1] if step == 1 else rows[0]))
        other = send(gates, lambda z, x, c: (z ^ step, x, c))
        low = z & step == 0
        gates = jnp.where(
            low, jnp.concatenate([gates, other], axis=1), jnp.concatenate([other, gates], axis=1)
        )
        step *= 2
    mine = (z * 2 + x) * 2 + core
    pair = jnp.stack([mine, mine + 1 - 2 * core])
    gates = jnp.sum(
        jnp.where(pair[:, None] == jnp.arange(experts), gates[..., None, :], 0.0), axis=-1
    )
    gates = jnp.concatenate([gates[0], gates[1, ::-1]])
    gates = lax.dynamic_slice_in_dim(jnp.concatenate([gates, gates]), place, ring, 0)

    far = ring // 2
    fore, back = list(rows), list(rows)
    fore_at, back_at = {0: fore}, {0: back}
    for k in range(1, far):
        fore_at[k] = [along(fore_at[k - 1][h], 1) for h in halves]
        back_at[k] = [along(back_at[k - 1][h], -1) for h in halves]
    last = [along(fore_at[far - 1][0], 1), along(back_at[far - 1][1], -1)]

    hidden_width = expert_out.shape[0]
    early, in_other, down_other, expert_in, expert_out = lax.optimization_barrier(
        (rows[1], in_other, down_other, expert_in, expert_out)
    )
    joined_in = jnp.concatenate(
        [
            expert_in[:, :hidden_width],
            in_other[:, :hidden_width],
            expert_in[:, hidden_width:],
            in_other[:, hidden_width:],
        ],
        axis=1,
    )
    joined_down = jnp.concatenate([expert_out, down_other], axis=0)
    joined_in, joined_down = lax.optimization_barrier((joined_in, joined_down))
    is_first = jnp.arange(2 * hidden_width)[None, :] < hidden_width

    def run_experts(parts, gate):
        v = jnp.dot(jnp.concatenate(parts), joined_in, preferred_element_type=jnp.float32)
        hidden = jax.nn.silu(v[:, : 2 * hidden_width]) * v[:, 2 * hidden_width :]
        hidden = (hidden * jnp.where(is_first, gate[:, :1], gate[:, 1:])).astype(jnp.bfloat16)
        return jnp.dot(hidden, joined_down, preferred_element_type=jnp.float32)

    def cut(total, at):
        return [total[at + h * size : at + (h + 1) * size] for h in halves]

    ahead, behind = {}, {}
    ahead[0] = cut(run_experts([early if h == 1 else rows[h] for h in halves], gates[0]), 0)
    for k in range(1, far):
        total = run_experts(
            [*back_at[k], *fore_at[k]], jnp.concatenate([gates[k], gates[ring - k]])
        )
        ahead[k], behind[k] = cut(total, 0), cut(total, frames)
    state = state_next()
    last[0], last[1], state, *near = lax.optimization_barrier(
        (last[0], last[1], state, *ahead[far - 1], *behind[far - 1])
    )
    ahead[far - 1], behind[far - 1] = near[:2], near[2:]
    total = run_experts(last, gates[far]).astype(jnp.bfloat16)

    fore, back = [along(total[:size], 1), None], [None, along(total[size:], -1)]
    for k in range(far - 1, 0, -1):
        before = None
        for h in halves if k < far - 1 else (None,):
            todo = ((fore, 1, ahead, h), (back, -1, behind, h))
            if h is None:
                todo = (
                    (fore, 1, ahead, 1),
                    (back, -1, behind, 0),
                    (fore, 1, ahead, 0),
                    (back, -1, behind, 1),
                )
            loads = []
            for way, step, totals, at in todo:
                load = totals[k][at]
                if way[at] is not None:
                    got = way[at]
                    if before is not None:
                        got = lax.optimization_barrier((got, *before))[0]
                    load = load + got.astype(jnp.float32)
                loads.append(load.astype(jnp.bfloat16))
            before = loads
            for (way, step, totals, at), load in zip(todo, loads):
                way[at] = along(load, step)
    out = []
    for h in halves:
        total = ahead[0][h] + fore[h].astype(jnp.float32) + back[h].astype(jnp.float32)
        out.append((rows[h].astype(jnp.float32) + total).astype(jnp.bfloat16))
    return jnp.concatenate(out), state


def routed_experts(normed, out_proj, expert_in, expert_out, route_ids, route_weights):
    mixer_rows = jnp.dot(
        normed,
        lax.all_gather(out_proj, "narrow", axis=1, tiled=True),
        preferred_element_type=jnp.float32,
    ).astype(jnp.bfloat16)
    frames_here = mixer_rows.shape[0]
    model_width = mixer_rows.shape[1]
    topk_count = route_ids.shape[1]
    local_experts = expert_in.shape[0]
    devices = lax.axis_size(("wide", "narrow"))
    experts = local_experts * devices
    capacity = max(2, frames_here * topk_count * 5 // (4 * experts))
    flat_ids, positions = slot_positions(route_ids, experts)
    owners = jnp.arange(frames_here * topk_count, dtype=jnp.int32) // topk_count
    slot_table = (
        jnp.full((experts, capacity), frames_here, jnp.int32).at[flat_ids, positions].set(owners)
    )
    padded = jnp.concatenate([mixer_rows, jnp.zeros((1, model_width), jnp.bfloat16)], axis=0)
    outgoing = padded[slot_table]
    hidden_width = expert_out.shape[1]
    projected = jnp.einsum(
        "nlcd,ldf->nlcf",
        lax.all_to_all(
            outgoing.reshape(devices, local_experts, capacity, model_width),
            ("wide", "narrow"),
            split_axis=0,
            concat_axis=0,
            tiled=True,
        ),
        expert_in,
        preferred_element_type=jnp.float32,
    )
    hidden = (jax.nn.silu(projected[..., :hidden_width]) * projected[..., hidden_width:]).astype(
        jnp.bfloat16
    )
    returned = lax.all_to_all(
        jnp.einsum("nlcf,lfd->nlcd", hidden, expert_out, preferred_element_type=jnp.float32).astype(
            jnp.bfloat16
        ),
        ("wide", "narrow"),
        split_axis=0,
        concat_axis=0,
        tiled=True,
    )
    returned = returned.reshape(experts, capacity, model_width)
    picked = returned[flat_ids, positions].reshape(frames_here, topk_count, model_width)
    expert_sum = jnp.einsum("tk,tkd->td", route_weights, picked.astype(jnp.float32))
    layer_out = (mixer_rows.astype(jnp.float32) + expert_sum).astype(jnp.bfloat16)
    return layer_out


def solution(mesh):
    placed = (
        P(("groups", "wide", "narrow"), None),
        P(("groups", "wide", "narrow"), None),
        P(("groups", "wide", "narrow"), None),
        P(("groups", "wide", "narrow"), None),
        P(("groups", "wide", "narrow"), None),
        P(),
        P(),
        P(),
        P(),
        P(("groups", "wide", "narrow"), None, None, None),
        P(None, "narrow"),
        P(("wide", "narrow"), None, None),
        P(("wide", "narrow"), None, None),
        P(("groups", "wide", "narrow"), None),
        P(("groups", "wide", "narrow"), None),
    )
    return jax.shard_map(
        body,
        mesh=mesh,
        in_specs=placed,
        out_specs=(
            P(("groups", "wide", "narrow"), None),
            P(("groups", "wide", "narrow"), None, None, None),
        ),
        check_vma=False,
    )
```

time: 197 us -> 140 us (0.71)
  Pallas kernels: 81.4 us -> 9.01 us
  local copies, waits for them, and re-layouts: 35.7 us -> 7.4 us
  waiting for transfers between devices: 27.7 us -> 52.9 us
  matrix products: 0 us -> 15.9 us
  starting transfers between devices: 42.4 us -> 44.9 us
    pallas_call x19 -> x1, Pallas kernels: 77.1 us -> 5.45 us  [ssm_mixer(): pl.pallas_call(mixer_kernel, grid=(steps,), in_specs=[pl.BlockSpec(memory...]
    unnamed x105 -> x23, local copies, waits for them, and re-layouts: 31.8 us -> 1.87 us
    ppermute x38, waiting for transfers between devices: 27.7 us -> 52.9 us  [send(): return lax.ppermute(value, axes, routes(wide, move))]
    dot_general x0 -> x13, matrix products: none -> 15.9 us  [the longest x5 7.49 us: run_experts(): jnp.dot(jnp.concatenate(parts), joined_in, preferred_element_type=jnp.flo...]
    slice x0 -> x4, local copies, waits for them, and re-layouts: none -> 3.63 us  [the longest x1 3.46 us: dense_experts(): expert_in[:, :hidden_width]]
    select_n x2 -> x3, other arithmetic: 0.16 us -> 3.73 us  [the longest x1 3.58 us: dense_experts(): jnp.where(core == 0, jnp.concatenate([out_proj, out_other], axis=1), jnp....]
    concatenate x1 -> x3, other arithmetic: 0.84 us -> 3.35 us  [the longest x1 1.78 us: dense_experts(): joined_down = jnp.concatenate([expert_out, down_other], axis=0)]
    ppermute x38, starting transfers between devices: 42.4 us -> 44.9 us  [send(): return lax.ppermute(value, axes, routes(wide, move))]
  transfers between devices with their start and end apart: 38 -> 38, of which waited for: 11 -> 19; matrix products, arithmetic and copies ran while one was open for 5% -> 21% of each run, Pallas kernels for 42% -> 6%
where the time goes in v5:
time: 140 us
  waiting for transfers between devices  52.9 us (38%)
  starting transfers between devices  44.9 us (32%)
  matrix products  15.9 us (11%)
  Pallas kernels  9.01 us (6%)
  other arithmetic  8.34 us (6%)
  local copies, waits for them, and re-layouts  7.4 us (5%)
    ppermute x38, waiting for transfers between devices, send(): return lax.ppermute(value, axes, routes(wide, move))  52.9 us
    ppermute x38, starting transfers between devices, send(): return lax.ppermute(value, axes, routes(wide, move))  44.9 us
    dot_general x5, matrix products, run_experts(): jnp.dot(jnp.concatenate(parts), joined_in, preferred_element_type=jnp.flo...  7.49 us
    pallas_call x1, Pallas kernels, ssm_mixer(): pl.pallas_call(mixer_kernel, grid=(steps,), in_specs=[pl.BlockSpec(memory...  5.45 us
    dot_general x5, matrix products, run_experts(): return jnp.dot(hidden, joined_down, preferred_element_type=jnp.float32)  5.05 us
    select_n x1, other arithmetic, dense_experts(): jnp.where(core == 0, jnp.concatenate([out_proj, out_other], axis=1), jnp....  3.58 us
    pallas_call x1, Pallas kernels, state_next(): pl.pallas_call(state_kernel, grid=(steps,), in_specs=[column, whole, per_...  3.56 us
    slice x1, local copies, waits for them, and re-layouts, dense_experts(): expert_in[:, :hidden_width]  3.46 us
  transfers between devices with their start and end apart: 38, of which 19 were waited for; matrix products, arithmetic and copies ran while one was open for 21% of the time, Pallas kernels for 6%

profile of v5, /device:TPU:0, one launch (start us, length us, event | category | flops | bytes accessed | tf_op | source)
XLA Modules:
  0.0 139.6 jit_solution(4536271200773242191)
XLA Ops:
  1.2 1.8 %copy.26.dt_ref = f32[128,32]{1,0:T(8,128)} copy(f32[128,32]{0,1:T(8,128)} %param.19) | data formatting | bytes 32768 | tf_op args[4]
  3.1 5.5 %mixer.1 = bf16[128,2048]{1,0:T(8,128)(2,1)} custom-call(f32[32]{0:T(128)} %skip_ref.1, bf16[128,2048]{1,0:T(8,128)(2,1)} %x_ref.3, bf16[128,2048]{1,0:T(8,128)(2,1)} %z_ref.1, bf16[128,128]{1,0:T(8,128)(2,1)} %b_ref.3, bf16[128,128]{1,0:T(8,128)(2,1)} %c_ref.1, f32[128,32]{1,0:T(8,128)} %copy.26.dt_ref, f32[1,32]{1,0:T(1,128)} %bitcast.64, ...), custom_call_target="tpu_custom_call" | custom-call | flops 400000000 | bytes 6000000 | tf_op jit(solution)/shard_map/mixer/pallas_call | solution.py:148
  8.5 1.9 %fusion.106 = (bf16[64,2048]{1,0:T(8,128)(2,1)}, bf16[64,2048]{1,0:T(8,128)(2,1)}) fusion(bf16[128,2048]{1,0:T(8,128)(2,1)} %mixer.1), kind=kLoop, calls=%fused_computation.164 | loop fusion | bytes 1048576 | tf_op jit(solution)/shard_map/slice | solution.py:298
  10.4 2.3 %collective-permute-start.3 = (bf16[64,2048]{1,0:T(8,128)(2,1)}, bf16[64,2048]{1,0:T(8,128)(2,1)S(1)}, u32[]{:S(2)}, u32[]{:S(2)}) collective-permute-start(bf16[64,2048]{1,0:T(8,128)(2,1)} %get-tuple-element.65), channel_id=1, source_target_pairs={{0,2},{1,3},{2,0},{3,1},{4,6},{5,7},{6,4},{7,5},{8,10},{9,11},{10,... | collective-permute-start | bytes 786440 | tf_op jit(solution)/shard_map/ppermute | solution.py:279
  13.5 6.5 %collective-permute-done.7 = f32[128,16]{0,1:T(8,128)S(1)} collective-permute-done((f32[128,16]{0,1:T(8,128)S(1)}, f32[128,16]{0,1:T(8,128)S(1)}, u32[]{:S(2)}, u32[]{:S(2)}) %collective-permute-start.7) | collective-permute-done | bytes 8224 | tf_op jit(solution)/shard_map/ppermute | solution.py:279
  20.1 1.7 %collective-permute-start.1 = (bf16[64,2048]{1,0:T(8,128)(2,1)}, bf16[64,2048]{1,0:T(8,128)(2,1)}, u32[]{:S(2)}, u32[]{:S(2)}) collective-permute-start(bf16[64,2048]{1,0:T(8,128)(2,1)} %get-tuple-element.64), channel_id=1, source_target_pairs={{0,2},{1,3},{2,0},{3,1},{4,6},{5,7},{6,4},{7,5},{8,10},{9,11},{10,... | collective-permute-start | bytes 786440 | tf_op jit(solution)/shard_map/ppermute | solution.py:279
  21.8 1.6 %collective-permute-start.8 = (f32[2,1,128,16]{2,3,1,0:T(8,128)S(1)}, f32[2,1,128,16]{2,3,1,0:T(8,128)S(1)}, u32[]{:S(2)}, u32[]{:S(2)}) collective-permute-start(f32[2,1,128,16]{2,3,1,0:T(8,128)S(1)} %maximum_select_fusion.5), channel_id=1, source_target_pairs={{0,4},{1,5},{2,6},{3,7},{4,0},{5,1},{6,2},{7,3},{8,12},{9,13},{10,... | collective-permute-start | bytes 49160 | tf_op jit(solution)/shard_map/ppermute | solution.py:279
  23.4 3.6 %state.1 = f32[2048,128]{1,0:T(8,128)} custom-call(bf16[128,2048]{1,0:T(8,128)(2,1)S(1)} %copy-done.1, bf16[128,128]{1,0:T(8,128)(2,1)S(1)} %copy-done.3, f32[128,32]{1,0:T(8,128)S(1)} %copy-done.2, f32[1,32]{1,0:T(1,128)S(1)} %bitcast.65, f32[1,32]{1,0:T(1,128)S(1)} %bitcast.67, f32[2048,128]{1,0:T(8,128)S(1)} %bitcast.63), custom_call_target="tpu_custom_call" | custom-call | flops 70000000 | bytes 3000000 | tf_op jit(solution)/shard_map/state/pallas_call | solution.py:187
  27.0 3.6 %maximum_select_fusion = bf16[2048,1024]{1,0:T(8,128)(2,1)S(1)} fusion(bf16[2048,512]{1,0:T(8,128)(2,1)} %collective-permute-done, bf16[2048,512]{1,0:T(8,128)(2,1)S(1)} %copy-done.7, pred[]{:T(512)S(6)} %eq.44), kind=kLoop, calls=%fused_computation.1 | loop fusion | flops 18874368 | bytes 8388609 | tf_op jit(solution)/shard_map/jit(_where)/select_n | solution.py:301
  32.1 1.8 %convolution_convert_fusion.3 = bf16[64,1024]{1,0:T(8,128)(2,1)S(1)} fusion(bf16[64,2048]{1,0:T(8,128)(2,1)} %collective-permute-done.1, bf16[2048,1024]{1,0:T(8,128)(2,1)S(1)} %maximum_select_fusion), kind=kOutput, calls=%fused_computation.6 | convolution fusion | flops 268500992 | bytes 4587520 | tf_op jit(solution)/shard_map/dot_general | solution.py:309
  33.9 1.6 %collective-permute-start.2 = (bf16[64,1024]{1,0:T(8,128)(2,1)S(1)}, bf16[64,1024]{1,0:T(8,128)(2,1)S(1)}, u32[]{:S(2)}, u32[]{:S(2)}) collective-permute-start(bf16[64,1024]{1,0:T(8,128)(2,1)S(1)} %convolution_convert_fusion.3), channel_id=1, source_target_pairs={{0,2},{1,3},{2,0},{3,1},{4,6},{5,7},{6,4},{7,5},{8,10},{9,11},{10,... | collective-permute-start | bytes 393224 | tf_op jit(solution)/shard_map/ppermute | solution.py:279
  36.3 3.1 %collective-permute-done.2 = bf16[64,1024]{1,0:T(8,128)(2,1)S(1)} collective-permute-done((bf16[64,1024]{1,0:T(8,128)(2,1)S(1)}, bf16[64,1024]{1,0:T(8,128)(2,1)S(1)}, u32[]{:S(2)}, u32[]{:S(2)}) %collective-permute-start.2) | collective-permute-done | bytes 131104 | tf_op jit(solution)/shard_map/ppermute | solution.py:279
  39.9 2.6 %collective-permute-start.9 = (f32[2,2,128,16]{2,3,1,0:T(8,128)S(1)}, f32[2,2,128,16]{2,3,1,0:T(8,128)S(1)}, u32[]{:S(2)}, u32[]{:S(2)}) collective-permute-start(f32[2,2,128,16]{2,3,1,0:T(8,128)S(1)} %maximum_select_fusion.4), channel_id=1, source_target_pairs={{0,8},{1,9},{2,10},{3,11},{4,12},{5,13},{6,14},{7,15},{8,0},{9,1},... | collective-permute-start | bytes 98312 | tf_op jit(solution)/shard_map/ppermute | solution.py:279
  42.6 1.2 collective-permute-start.13
  43.8 3.6 %collective-permute-done.9 = f32[2,2,128,16]{2,3,1,0:T(8,128)S(1)} collective-permute-done((f32[2,2,128,16]{2,3,1,0:T(8,128)S(1)}, f32[2,2,128,16]{2,3,1,0:T(8,128)S(1)}, u32[]{:S(2)}, u32[]{:S(2)}) %collective-permute-start.9) | collective-permute-done | bytes 32800 | tf_op jit(solution)/shard_map/ppermute | solution.py:279
  47.4 4.1 %collective-permute-start.11 = (bf16[64,2048]{1,0:T(8,128)(2,1)S(1)}, bf16[64,2048]{1,0:T(8,128)(2,1)S(1)}, u32[]{:S(2)}, u32[]{:S(2)}) collective-permute-start(bf16[64,2048]{1,0:T(8,128)(2,1)S(1)} %maximum_select_fusion.2), channel_id=1, source_target_pairs={{0,2},{1,3},{2,6},{3,7},{4,0},{5,1},{6,10},{7,11},{8,4},{9,5},{10,... | collective-permute-start | bytes 786440 | tf_op jit(solution)/shard_map/ppermute | solution.py:279
  51.7 1.4 %collective-permute-start.10 = (bf16[64,2048]{1,0:T(8,128)(2,1)S(1)}, bf16[64,2048]{1,0:T(8,128)(2,1)S(1)}, u32[]{:S(2)}, u32[]{:S(2)}) collective-permute-start(bf16[64,2048]{1,0:T(8,128)(2,1)S(1)} %maximum_select_fusion.1), channel_id=1, source_target_pairs={{0,2},{1,3},{2,6},{3,7},{4,0},{5,1},{6,10},{7,11},{8,4},{9,5},{10,... | collective-permute-start | bytes 786440 | tf_op jit(solution)/shard_map/ppermute | solution.py:279
  53.8 4.5 %collective-permute-done.11 = bf16[64,2048]{1,0:T(8,128)(2,1)S(1)} collective-permute-done((bf16[64,2048]{1,0:T(8,128)(2,1)S(1)}, bf16[64,2048]{1,0:T(8,128)(2,1)S(1)}, u32[]{:S(2)}, u32[]{:S(2)}) %collective-permute-start.11) | collective-permute-done | bytes 262176 | tf_op jit(solution)/shard_map/ppermute | solution.py:279
  58.2 2.5 %collective-permute-start.15 = (bf16[64,2048]{1,0:T(8,128)(2,1)S(1)}, bf16[64,2048]{1,0:T(8,128)(2,1)S(1)}, u32[]{:S(2)}, u32[]{:S(2)}) collective-permute-start(bf16[64,2048]{1,0:T(8,128)(2,1)S(1)} %collective-permute-done.11), channel_id=1, source_target_pairs={{0,2},{1,3},{2,6},{3,7},{4,0},{5,1},{6,10},{7,11},{8,4},{9,5},{10,... | collective-permute-start | bytes 786440 | tf_op jit(solution)/shard_map/ppermute | solution.py:279
  60.8 3.0 %collective-permute-done.10 = bf16[64,2048]{1,0:T(8,128)(2,1)S(1)} collective-permute-done((bf16[64,2048]{1,0:T(8,128)(2,1)S(1)}, bf16[64,2048]{1,0:T(8,128)(2,1)S(1)}, u32[]{:S(2)}, u32[]{:S(2)}) %collective-permute-start.10) | collective-permute-done | bytes 262176 | tf_op jit(solution)/shard_map/ppermute | solution.py:279
  63.8 2.5 %collective-permute-start.14 = (bf16[64,2048]{1,0:T(8,128)(2,1)S(1)}, bf16[64,2048]{1,0:T(8,128)(2,1)S(1)}, u32[]{:S(2)}, u32[]{:S(2)}) collective-permute-start(bf16[64,2048]{1,0:T(8,128)(2,1)S(1)} %collective-permute-done.10), channel_id=1, source_target_pairs={{0,2},{1,3},{2,6},{3,7},{4,0},{5,1},{6,10},{7,11},{8,4},{9,5},{10,... | collective-permute-start | bytes 786440 | tf_op jit(solution)/shard_map/ppermute | solution.py:279
  66.3 3.1 %collective-permute-done.15 = bf16[64,2048]{1,0:T(8,128)(2,1)S(1)} collective-permute-done((bf16[64,2048]{1,0:T(8,128)(2,1)S(1)}, bf16[64,2048]{1,0:T(8,128)(2,1)S(1)}, u32[]{:S(2)}, u32[]{:S(2)}) %collective-permute-start.15) | collective-permute-done | bytes 262176 | tf_op jit(solution)/shard_map/ppermute | solution.py:279
  69.5 2.5 %collective-permute-start.20 = (bf16[64,2048]{1,0:T(8,128)(2,1)S(1)}, bf16[64,2048]{1,0:T(8,128)(2,1)S(1)}, u32[]{:S(2)}, u32[]{:S(2)}) collective-permute-start(bf16[64,2048]{1,0:T(8,128)(2,1)S(1)} %collective-permute-done.15), channel_id=1, source_target_pairs={{0,2},{1,3},{2,6},{3,7},{4,0},{5,1},{6,10},{7,11},{8,4},{9,5},{10,... | collective-permute-start | bytes 786440 | tf_op jit(solution)/shard_map/ppermute | solution.py:279
  72.0 3.0 %collective-permute-done.14 = bf16[64,2048]{1,0:T(8,128)(2,1)S(1)} collective-permute-done((bf16[64,2048]{1,0:T(8,128)(2,1)S(1)}, bf16[64,2048]{1,0:T(8,128)(2,1)S(1)}, u32[]{:S(2)}, u32[]{:S(2)}) %collective-permute-start.14) | collective-permute-done | bytes 262176 | tf_op jit(solution)/shard_map/ppermute | solution.py:279
  75.1 2.5 %collective-permute-start.22 = (bf16[64,2048]{1,0:T(8,128)(2,1)S(1)}, bf16[64,2048]{1,0:T(8,128)(2,1)S(1)}, u32[]{:S(2)}, u32[]{:S(2)}) collective-permute-start(bf16[64,2048]{1,0:T(8,128)(2,1)S(1)} %collective-permute-done.14), channel_id=1, source_target_pairs={{0,2},{1,3},{2,6},{3,7},{4,0},{5,1},{6,10},{7,11},{8,4},{9,5},{10,... | collective-permute-start | bytes 786440 | tf_op jit(solution)/shard_map/ppermute | solution.py:279
  77.6 2.9 %collective-permute-done.20 = bf16[64,2048]{1,0:T(8,128)(2,1)S(1)} collective-permute-done((bf16[64,2048]{1,0:T(8,128)(2,1)S(1)}, bf16[64,2048]{1,0:T(8,128)(2,1)S(1)}, u32[]{:S(2)}, u32[]{:S(2)}) %collective-permute-start.20) | collective-permute-done | bytes 262176 | tf_op jit(solution)/shard_map/ppermute | solution.py:279
  81.4 3.5 %fusion.101 = (bf16[2048,384]{1,0:T(8,128)(2,1)S(1)}, bf16[2048,384]{1,0:T(8,128)(2,1)S(1)}, bf16[2048,384]{1,0:T(8,128)(2,1)S(1)}, bf16[2048,384]{1,0:T(8,128)(2,1)S(1)}) fusion(bf16[2048,768]{1,0:T(8,128)(2,1)} %bitcast.4, bf16[2048,768]{1,0:T(8,128)(2,1)} %collective-permute-done.5), kind=kLoop, calls=%fused_computation.159 | loop fusion | bytes 12582912 | tf_op jit(solution)/shard_map/slice | solution.py:362
  85.6 1.8 %pad_maximum_fusion.1 = bf16[768,2048]{1,0:T(8,128)(2,1)S(1)} fusion(bf16[384,2048]{1,0:T(8,128)(2,1)} %collective-permute-done.6, bf16[384,2048]{1,0:T(8,128)(2,1)S(1)} %bitcast.69), kind=kLoop, calls=%fused_computation.2 | loop fusion | flops 6291456 | bytes 6291456 | tf_op jit(solution)/shard_map/concatenate | solution.py:369
  87.4 1.8 %fusion.16 = f32[256,1536]{1,0:T(8,128)S(1)} fusion(bf16[2048,1536]{1,0:T(8,128)(2,1)S(1)} %pad_maximum_fusion, bf16[64,2048]{1,0:T(8,128)(2,1)S(1)} %collective-permute-done.23, bf16[64,2048]{1,0:T(8,128)(2,1)S(1)} %collective-permute-done.18, bf16[64,2048]{1,0:T(8,128)(2,1)S(1)} %collective-permute-done.20, bf16[64,2048]{1,0:T(8,128)(2,1)S(1)} %collective-permute-done.22), kind=kOutput, calls=%fused_computation.23 | convolution fusion | flops 1614807040 | bytes 8912896 | tf_op jit(solution)/shard_map/dot_general | solution.py:374
  89.2 1.2 fusion.56
  90.6 1.0 fusion.44
  91.6 1.8 %fusion = f32[256,1536]{1,0:T(8,128)S(1)} fusion(bf16[2048,1536]{1,0:T(8,128)(2,1)S(1)} %pad_maximum_fusion, bf16[64,2048]{1,0:T(8,128)(2,1)S(1)} %collective-permute-done.13, bf16[64,2048]{1,0:T(8,128)(2,1)S(1)} %collective-permute-done.12, bf16[64,2048]{1,0:T(8,128)(2,1)S(1)} %collective-permute-done.11, bf16[64,2048]{1,0:T(8,128)(2,1)S(1)} %collective-permute-done.10), kind=kOutput, calls=%fused_computation.7 | convolution fusion | flops 1614807040 | bytes 8912896 | tf_op jit(solution)/shard_map/dot_general | solution.py:374
  93.4 1.8 %fusion.8 = f32[256,1536]{1,0:T(8,128)S(1)} fusion(bf16[2048,1536]{1,0:T(8,128)(2,1)S(1)} %pad_maximum_fusion, bf16[64,2048]{1,0:T(8,128)(2,1)S(1)} %collective-permute-done.17, bf16[64,2048]{1,0:T(8,128)(2,1)S(1)} %collective-permute-done.16, bf16[64,2048]{1,0:T(8,128)(2,1)S(1)} %collective-permute-done.15, bf16[64,2048]{1,0:T(8,128)(2,1)S(1)} %collective-permute-done.14), kind=kOutput, calls=%fused_computation.15 | convolution fusion | flops 1614807040 | bytes 8912896 | tf_op jit(solution)/shard_map/dot_general | solution.py:374
  95.2 1.2 fusion.52
  98.3 1.2 collective-permute-start.24
  99.5 1.2 fusion.54
  101.6 1.2 collective-permute-start.31
  103.7 3.7 %collective-permute-done.24 = bf16[64,2048]{1,0:T(8,128)(2,1)S(1)} collective-permute-done((bf16[64,2048]{1,0:T(8,128)(2,1)S(1)}, bf16[64,2048]{1,0:T(8,128)(2,1)S(1)}, u32[]{:S(2)}, u32[]{:S(2)}) %collective-permute-start.24) | collective-permute-done | bytes 262176 | tf_op jit(solution)/shard_map/ppermute | solution.py:279
  107.4 1.3 collective-permute-start.25
  108.8 6.8 %collective-permute-done.34 = bf16[64,2048]{1,0:T(8,128)(2,1)S(1)} collective-permute-done((bf16[64,2048]{1,0:T(8,128)(2,1)S(1)}, bf16[64,2048]{1,0:T(8,128)(2,1)S(1)}, u32[]{:S(2)}, u32[]{:S(2)}) %collective-permute-start.34) | collective-permute-done | bytes 262176 | tf_op jit(solution)/shard_map/ppermute | solution.py:279
  116.5 2.1 %collective-permute-done.25 = bf16[64,2048]{1,0:T(8,128)(2,1)S(1)} collective-permute-done((bf16[64,2048]{1,0:T(8,128)(2,1)S(1)}, bf16[64,2048]{1,0:T(8,128)(2,1)S(1)}, u32[]{:S(2)}, u32[]{:S(2)}) %collective-permute-start.25) | collective-permute-done | bytes 262176 | tf_op jit(solution)/shard_map/ppermute | solution.py:279
  118.7 1.5 %collective-permute-start.29 = (bf16[64,2048]{1,0:T(8,128)(2,1)S(1)}, bf16[64,2048]{1,0:T(8,128)(2,1)S(1)}, u32[]{:S(2)}, u32[]{:S(2)}) collective-permute-start(bf16[64,2048]{1,0:T(8,128)(2,1)S(1)} %get-tuple-element.54), channel_id=1, source_target_pairs={{0,2},{1,3},{2,6},{3,7},{4,0},{5,1},{6,10},{7,11},{8,4},{9,5},{10,... | collective-permute-start | bytes 786440 | tf_op jit(solution)/shard_map/ppermute | solution.py:279
  120.8 2.5 %collective-permute-done.35 = bf16[64,2048]{1,0:T(8,128)(2,1)S(1)} collective-permute-done((bf16[64,2048]{1,0:T(8,128)(2,1)S(1)}, bf16[64,2048]{1,0:T(8,128)(2,1)S(1)}, u32[]{:S(2)}, u32[]{:S(2)}) %collective-permute-start.35) | collective-permute-done | bytes 262176 | tf_op jit(solution)/shard_map/ppermute | solution.py:279
  123.4 1.7 %collective-permute-start.32 = (bf16[64,2048]{1,0:T(8,128)(2,1)S(1)}, bf16[64,2048]{1,0:T(8,128)(2,1)S(1)}, u32[]{:S(2)}, u32[]{:S(2)}) collective-permute-start(bf16[64,2048]{1,0:T(8,128)(2,1)S(1)} %get-tuple-element.50), channel_id=1, source_target_pairs={{0,4},{1,5},{2,0},{3,1},{4,8},{5,9},{6,2},{7,3},{8,12},{9,13},{10,... | collective-permute-start | bytes 786440 | tf_op jit(solution)/shard_map/ppermute | solution.py:279
  126.7 1.5 %collective-permute-start.30 = (bf16[64,2048]{1,0:T(8,128)(2,1)S(1)}, bf16[64,2048]{1,0:T(8,128)(2,1)S(1)}, u32[]{:S(2)}, u32[]{:S(2)}) collective-permute-start(bf16[64,2048]{1,0:T(8,128)(2,1)S(1)} %get-tuple-element.52), channel_id=1, source_target_pairs={{0,2},{1,3},{2,6},{3,7},{4,0},{5,1},{6,10},{7,11},{8,4},{9,5},{10,... | collective-permute-start | bytes 786440 | tf_op jit(solution)/shard_map/ppermute | solution.py:279
  129.8 1.6 %collective-permute-done.36 = bf16[64,2048]{1,0:T(8,128)(2,1)S(1)} collective-permute-done((bf16[64,2048]{1,0:T(8,128)(2,1)S(1)}, bf16[64,2048]{1,0:T(8,128)(2,1)S(1)}, u32[]{:S(2)}, u32[]{:S(2)}) %collective-permute-start.36) | collective-permute-done | bytes 262176 | tf_op jit(solution)/shard_map/ppermute | solution.py:279
  132.0 1.6 %collective-permute-start.33 = (bf16[64,2048]{1,0:T(8,128)(2,1)S(1)}, bf16[64,2048]{1,0:T(8,128)(2,1)S(1)}, u32[]{:S(2)}, u32[]{:S(2)}) collective-permute-start(bf16[64,2048]{1,0:T(8,128)(2,1)S(1)} %get-tuple-element.48), channel_id=1, source_target_pairs={{0,4},{1,5},{2,0},{3,1},{4,8},{5,9},{6,2},{7,3},{8,12},{9,13},{10,... | collective-permute-start | bytes 786440 | tf_op jit(solution)/shard_map/ppermute | solution.py:279
  134.8 3.2 %collective-permute-done.37 = bf16[64,2048]{1,0:T(8,128)(2,1)S(1)} collective-permute-done((bf16[64,2048]{1,0:T(8,128)(2,1)S(1)}, bf16[64,2048]{1,0:T(8,128)(2,1)S(1)}, u32[]{:S(2)}, u32[]{:S(2)}) %collective-permute-start.37) | collective-permute-done | bytes 262176 | tf_op jit(solution)/shard_map/ppermute | solution.py:279
  (100 shorter events, 19.0 us)
Async XLA Ops:
  0.6 22.8 %copy-start.1 = (bf16[128,2048]{1,0:T(8,128)(2,1)S(1)}, bf16[128,2048]{1,0:T(8,128)(2,1)}, u32[]{:S(2)}) copy-start(bf16[128,2048]{1,0:T(8,128)(2,1)} %x_ref.3) | copy-start | bytes 1572868
  0.6 22.8 %copy-start.3 = (bf16[128,128]{1,0:T(8,128)(2,1)S(1)}, bf16[128,128]{1,0:T(8,128)(2,1)}, u32[]{:S(2)}) copy-start(bf16[128,128]{1,0:T(8,128)(2,1)} %b_ref.3) | copy-start | bytes 98308
  0.7 22.7 %copy-start.4 = (f32[32]{0:T(128)S(1)}, f32[32]{0:T(128)}, u32[]{:S(2)}) copy-start(f32[32]{0:T(128)} %param.21) | copy-start | bytes 388
  0.7 22.7 %copy-start.5 = (f32[32]{0:T(128)S(1)}, f32[32]{0:T(128)}, u32[]{:S(2)}) copy-start(f32[32]{0:T(128)} %param.20) | copy-start | bytes 388
  0.7 22.7 %copy-start = (f32[1,32,64,128]{3,2,1,0:T(8,128)S(1)}, f32[1,32,64,128]{3,2,1,0:T(8,128)}, u32[]{:S(2)}) copy-start(f32[1,32,64,128]{3,2,1,0:T(8,128)} %param.24) | copy-start | bytes 3145732
  0.7 12.2 %copy-start.8 = (bf16[1,384,2048]{2,1,0:T(8,128)(2,1)S(1)}, bf16[1,384,2048]{2,1,0:T(8,128)(2,1)}, u32[]{:S(2)}) copy-start(bf16[1,384,2048]{2,1,0:T(8,128)(2,1)} %param.27) | copy-start | bytes 4718596
  0.7 12.5 %copy-start.9 = (f32[128,8]{0,1:T(8,128)S(1)}, f32[128,8]{0,1:T(8,128)}, u32[]{:S(2)}) copy-start(f32[128,8]{0,1:T(8,128)} %param.29) | copy-start | bytes 12292
  0.7 12.5 %copy-start.10 = (s32[128,8]{0,1:T(8,128)S(1)}, s32[128,8]{0,1:T(8,128)}, u32[]{:S(2)}) copy-start(s32[128,8]{0,1:T(8,128)} %param.28) | copy-start | bytes 12292
  0.7 26.3 %collective-permute-start = (bf16[2048,512]{1,0:T(8,128)(2,1)}, bf16[2048,512]{1,0:T(8,128)(2,1)}, u32[]{:S(2)}, u32[]{:S(2)}) collective-permute-start(bf16[2048,512]{1,0:T(8,128)(2,1)} %param.25), channel_id=1, source_target_pairs={{0,1},{1,0},{2,3},{3,2},{4,5},{5,4},{6,7},{7,6},{8,9},{9,8},{10,11... | collective-permute-start | bytes 6291464 | tf_op jit(solution)/shard_map/ppermute | solution.py:279
  3.0 20.4 %copy-start.2 = (f32[128,32]{1,0:T(8,128)S(1)}, f32[128,32]{1,0:T(8,128)}, u32[]{:S(2)}) copy-start(f32[128,32]{1,0:T(8,128)} %copy.26.dt_ref) | copy-start | bytes 49156
  10.4 11.4 %collective-permute-start.3 = (bf16[64,2048]{1,0:T(8,128)(2,1)}, bf16[64,2048]{1,0:T(8,128)(2,1)S(1)}, u32[]{:S(2)}, u32[]{:S(2)}) collective-permute-start(bf16[64,2048]{1,0:T(8,128)(2,1)} %get-tuple-element.65), channel_id=1, source_target_pairs={{0,2},{1,3},{2,0},{3,1},{4,6},{5,7},{6,4},{7,5},{8,10},{9,11},{10,... | collective-permute-start | bytes 786440 | tf_op jit(solution)/shard_map/ppermute | solution.py:279
  12.7 68.8 %collective-permute-start.5 = (bf16[2048,768]{1,0:T(8,128)(2,1)}, bf16[2048,768]{1,0:T(8,128)(2,1)}, u32[]{:S(2)}, u32[]{:S(2)}) collective-permute-start(bf16[2048,768]{1,0:T(8,128)(2,1)} %bitcast.4), channel_id=1, source_target_pairs={{0,1},{1,0},{2,3},{3,2},{4,5},{5,4},{6,7},{7,6},{8,9},{9,8},{10,11... | collective-permute-start | bytes 9437192 | tf_op jit(solution)/shard_map/ppermute | solution.py:279
  12.9 38.7 %collective-permute-start.6 = (bf16[384,2048]{1,0:T(8,128)(2,1)S(1)}, bf16[384,2048]{1,0:T(8,128)(2,1)}, u32[]{:S(2)}, u32[]{:S(2)}) collective-permute-start(bf16[384,2048]{1,0:T(8,128)(2,1)S(1)} %bitcast.68), channel_id=1, source_target_pairs={{0,1},{1,0},{2,3},{3,2},{4,5},{5,4},{6,7},{7,6},{8,9},{9,8},{10,11... | collective-permute-start | bytes 4718600 | tf_op jit(solution)/shard_map/ppermute | solution.py:279
  13.2 6.9 %collective-permute-start.7 = (f32[128,16]{0,1:T(8,128)S(1)}, f32[128,16]{0,1:T(8,128)S(1)}, u32[]{:S(2)}, u32[]{:S(2)}) collective-permute-start(f32[128,16]{0,1:T(8,128)S(1)} %select_reduce_fusion.1), channel_id=1, source_target_pairs={{0,2},{1,3},{2,0},{3,1},{4,6},{5,7},{6,4},{7,5},{8,10},{9,11},{10,... | collective-permute-start | bytes 24584 | tf_op jit(solution)/shard_map/ppermute | solution.py:279
  20.1 12.1 %collective-permute-start.1 = (bf16[64,2048]{1,0:T(8,128)(2,1)}, bf16[64,2048]{1,0:T(8,128)(2,1)}, u32[]{:S(2)}, u32[]{:S(2)}) collective-permute-start(bf16[64,2048]{1,0:T(8,128)(2,1)} %get-tuple-element.64), channel_id=1, source_target_pairs={{0,2},{1,3},{2,0},{3,1},{4,6},{5,7},{6,4},{7,5},{8,10},{9,11},{10,... | collective-permute-start | bytes 786440 | tf_op jit(solution)/shard_map/ppermute | solution.py:279
  21.8 5.2 %collective-permute-start.8 = (f32[2,1,128,16]{2,3,1,0:T(8,128)S(1)}, f32[2,1,128,16]{2,3,1,0:T(8,128)S(1)}, u32[]{:S(2)}, u32[]{:S(2)}) collective-permute-start(f32[2,1,128,16]{2,3,1,0:T(8,128)S(1)} %maximum_select_fusion.5), channel_id=1, source_target_pairs={{0,4},{1,5},{2,6},{3,7},{4,0},{5,1},{6,2},{7,3},{8,12},{9,13},{10,... | collective-permute-start | bytes 49160 | tf_op jit(solution)/shard_map/ppermute | solution.py:279
  31.5 4.0 %copy-start.6 = (bf16[128,2048]{1,0:T(8,128)(2,1)S(1)}, bf16[128,2048]{1,0:T(8,128)(2,1)}, u32[]{:S(2)}) copy-start(bf16[128,2048]{1,0:T(8,128)(2,1)} %mixer.1) | copy-start | bytes 1572868
  31.5 11.0 %collective-permute-start.4 = (bf16[64,1024]{1,0:T(8,128)(2,1)S(1)}, bf16[64,1024]{1,0:T(8,128)(2,1)S(1)}, u32[]{:S(2)}, u32[]{:S(2)}) collective-permute-start(bf16[64,1024]{1,0:T(8,128)(2,1)S(1)} %convolution_convert_fusion.2), channel_id=1, source_target_pairs={{0,2},{1,3},{2,0},{3,1},{4,6},{5,7},{6,4},{7,5},{8,10},{9,11},{10,... | collective-permute-start | bytes 393224 | tf_op jit(solution)/shard_map/ppermute | solution.py:279
  33.9 5.4 %collective-permute-start.2 = (bf16[64,1024]{1,0:T(8,128)(2,1)S(1)}, bf16[64,1024]{1,0:T(8,128)(2,1)S(1)}, u32[]{:S(2)}, u32[]{:S(2)}) collective-permute-start(bf16[64,1024]{1,0:T(8,128)(2,1)S(1)} %convolution_convert_fusion.3), channel_id=1, source_target_pairs={{0,2},{1,3},{2,0},{3,1},{4,6},{5,7},{6,4},{7,5},{8,10},{9,11},{10,... | collective-permute-start | bytes 393224 | tf_op jit(solution)/shard_map/ppermute | solution.py:279
  39.4 13.7 %collective-permute-start.12 = (bf16[64,2048]{1,0:T(8,128)(2,1)S(1)}, bf16[64,2048]{1,0:T(8,128)(2,1)S(1)}, u32[]{:S(2)}, u32[]{:S(2)}) collective-permute-start(bf16[64,2048]{1,0:T(8,128)(2,1)S(1)} %maximum_select_fusion.1), channel_id=1, source_target_pairs={{0,4},{1,5},{2,0},{3,1},{4,8},{5,9},{6,2},{7,3},{8,12},{9,13},{10,... | collective-permute-start | bytes 786440 | tf_op jit(solution)/shard_map/ppermute | solution.py:279
  39.9 7.5 %collective-permute-start.9 = (f32[2,2,128,16]{2,3,1,0:T(8,128)S(1)}, f32[2,2,128,16]{2,3,1,0:T(8,128)S(1)}, u32[]{:S(2)}, u32[]{:S(2)}) collective-permute-start(f32[2,2,128,16]{2,3,1,0:T(8,128)S(1)} %maximum_select_fusion.4), channel_id=1, source_target_pairs={{0,8},{1,9},{2,10},{3,11},{4,12},{5,13},{6,14},{7,15},{8,0},{9,1},... | collective-permute-start | bytes 98312 | tf_op jit(solution)/shard_map/ppermute | solution.py:279
  42.6 18.1 %collective-permute-start.13 = (bf16[64,2048]{1,0:T(8,128)(2,1)S(1)}, bf16[64,2048]{1,0:T(8,128)(2,1)S(1)}, u32[]{:S(2)}, u32[]{:S(2)}) collective-permute-start(bf16[64,2048]{1,0:T(8,128)(2,1)S(1)} %maximum_select_fusion.2), channel_id=1, source_target_pairs={{0,4},{1,5},{2,0},{3,1},{4,8},{5,9},{6,2},{7,3},{8,12},{9,13},{10,... | collective-permute-start | bytes 786440 | tf_op jit(solution)/shard_map/ppermute | solution.py:279
  47.4 10.8 %collective-permute-start.11 = (bf16[64,2048]{1,0:T(8,128)(2,1)S(1)}, bf16[64,2048]{1,0:T(8,128)(2,1)S(1)}, u32[]{:S(2)}, u32[]{:S(2)}) collective-permute-start(bf16[64,2048]{1,0:T(8,128)(2,1)S(1)} %maximum_select_fusion.2), channel_id=1, source_target_pairs={{0,2},{1,3},{2,6},{3,7},{4,0},{5,1},{6,10},{7,11},{8,4},{9,5},{10,... | collective-permute-start | bytes 786440 | tf_op jit(solution)/shard_map/ppermute | solution.py:279
  51.7 12.2 %collective-permute-start.10 = (bf16[64,2048]{1,0:T(8,128)(2,1)S(1)}, bf16[64,2048]{1,0:T(8,128)(2,1)S(1)}, u32[]{:S(2)}, u32[]{:S(2)}) collective-permute-start(bf16[64,2048]{1,0:T(8,128)(2,1)S(1)} %maximum_select_fusion.1), channel_id=1, source_target_pairs={{0,2},{1,3},{2,6},{3,7},{4,0},{5,1},{6,10},{7,11},{8,4},{9,5},{10,... | collective-permute-start | bytes 786440 | tf_op jit(solution)/shard_map/ppermute | solution.py:279
  53.1 13.2 %collective-permute-start.16 = (bf16[64,2048]{1,0:T(8,128)(2,1)S(1)}, bf16[64,2048]{1,0:T(8,128)(2,1)S(1)}, u32[]{:S(2)}, u32[]{:S(2)}) collective-permute-start(bf16[64,2048]{1,0:T(8,128)(2,1)S(1)} %collective-permute-done.12), channel_id=1, source_target_pairs={{0,4},{1,5},{2,0},{3,1},{4,8},{5,9},{6,2},{7,3},{8,12},{9,13},{10,... | collective-permute-start | bytes 786440 | tf_op jit(solution)/shard_map/ppermute | solution.py:279
  58.2 11.2 %collective-permute-start.15 = (bf16[64,2048]{1,0:T(8,128)(2,1)S(1)}, bf16[64,2048]{1,0:T(8,128)(2,1)S(1)}, u32[]{:S(2)}, u32[]{:S(2)}) collective-permute-start(bf16[64,2048]{1,0:T(8,128)(2,1)S(1)} %collective-permute-done.11), channel_id=1, source_target_pairs={{0,2},{1,3},{2,6},{3,7},{4,0},{5,1},{6,10},{7,11},{8,4},{9,5},{10,... | collective-permute-start | bytes 786440 | tf_op jit(solution)/shard_map/ppermute | solution.py:279
  60.7 11.2 %collective-permute-start.17 = (bf16[64,2048]{1,0:T(8,128)(2,1)S(1)}, bf16[64,2048]{1,0:T(8,128)(2,1)S(1)}, u32[]{:S(2)}, u32[]{:S(2)}) collective-permute-start(bf16[64,2048]{1,0:T(8,128)(2,1)S(1)} %collective-permute-done.13), channel_id=1, source_target_pairs={{0,4},{1,5},{2,0},{3,1},{4,8},{5,9},{6,2},{7,3},{8,12},{9,13},{10,... | collective-permute-start | bytes 786440 | tf_op jit(solution)/shard_map/ppermute | solution.py:279
  63.8 11.2 %collective-permute-start.14 = (bf16[64,2048]{1,0:T(8,128)(2,1)S(1)}, bf16[64,2048]{1,0:T(8,128)(2,1)S(1)}, u32[]{:S(2)}, u32[]{:S(2)}) collective-permute-start(bf16[64,2048]{1,0:T(8,128)(2,1)S(1)} %collective-permute-done.10), channel_id=1, source_target_pairs={{0,2},{1,3},{2,6},{3,7},{4,0},{5,1},{6,10},{7,11},{8,4},{9,5},{10,... | collective-permute-start | bytes 786440 | tf_op jit(solution)/shard_map/ppermute | solution.py:279
  66.3 11.2 %collective-permute-start.18 = (bf16[64,2048]{1,0:T(8,128)(2,1)S(1)}, bf16[64,2048]{1,0:T(8,128)(2,1)S(1)}, u32[]{:S(2)}, u32[]{:S(2)}) collective-permute-start(bf16[64,2048]{1,0:T(8,128)(2,1)S(1)} %collective-permute-done.16), channel_id=1, source_target_pairs={{0,4},{1,5},{2,0},{3,1},{4,8},{5,9},{6,2},{7,3},{8,12},{9,13},{10,... | collective-permute-start | bytes 786440 | tf_op jit(solution)/shard_map/ppermute | solution.py:279
  69.5 11.0 %collective-permute-start.20 = (bf16[64,2048]{1,0:T(8,128)(2,1)S(1)}, bf16[64,2048]{1,0:T(8,128)(2,1)S(1)}, u32[]{:S(2)}, u32[]{:S(2)}) collective-permute-start(bf16[64,2048]{1,0:T(8,128)(2,1)S(1)} %collective-permute-done.15), channel_id=1, source_target_pairs={{0,2},{1,3},{2,6},{3,7},{4,0},{5,1},{6,10},{7,11},{8,4},{9,5},{10,... | collective-permute-start | bytes 786440 | tf_op jit(solution)/shard_map/ppermute | solution.py:279
  72.0 15.4 %collective-permute-start.23 = (bf16[64,2048]{1,0:T(8,128)(2,1)S(1)}, bf16[64,2048]{1,0:T(8,128)(2,1)S(1)}, u32[]{:S(2)}, u32[]{:S(2)}) collective-permute-start(bf16[64,2048]{1,0:T(8,128)(2,1)S(1)} %collective-permute-done.17), channel_id=1, source_target_pairs={{0,4},{1,5},{2,0},{3,1},{4,8},{5,9},{6,2},{7,3},{8,12},{9,13},{10,... | collective-permute-start | bytes 786440 | tf_op jit(solution)/shard_map/ppermute | solution.py:279
  75.1 12.3 %collective-permute-start.22 = (bf16[64,2048]{1,0:T(8,128)(2,1)S(1)}, bf16[64,2048]{1,0:T(8,128)(2,1)S(1)}, u32[]{:S(2)}, u32[]{:S(2)}) collective-permute-start(bf16[64,2048]{1,0:T(8,128)(2,1)S(1)} %collective-permute-done.14), channel_id=1, source_target_pairs={{0,2},{1,3},{2,6},{3,7},{4,0},{5,1},{6,10},{7,11},{8,4},{9,5},{10,... | collective-permute-start | bytes 786440 | tf_op jit(solution)/shard_map/ppermute | solution.py:279
  77.6 18.9 %collective-permute-start.19 = (bf16[64,2048]{1,0:T(8,128)(2,1)S(1)}, bf16[64,2048]{1,0:T(8,128)(2,1)S(1)}, u32[]{:S(2)}, u32[]{:S(2)}) collective-permute-start(bf16[64,2048]{1,0:T(8,128)(2,1)S(1)} %collective-permute-done.18), channel_id=1, source_target_pairs={{0,4},{1,5},{2,0},{3,1},{4,8},{5,9},{6,2},{7,3},{8,12},{9,13},{10,... | collective-permute-start | bytes 786440 | tf_op jit(solution)/shard_map/ppermute | solution.py:279
  80.5 16.0 %collective-permute-start.21 = (bf16[64,2048]{1,0:T(8,128)(2,1)S(1)}, bf16[64,2048]{1,0:T(8,128)(2,1)S(1)}, u32[]{:S(2)}, u32[]{:S(2)}) collective-permute-start(bf16[64,2048]{1,0:T(8,128)(2,1)S(1)} %collective-permute-done.20), channel_id=1, source_target_pairs={{0,2},{1,3},{2,6},{3,7},{4,0},{5,1},{6,10},{7,11},{8,4},{9,5},{10,... | collective-permute-start | bytes 786440 | tf_op jit(solution)/shard_map/ppermute | solution.py:279
  98.3 9.1 %collective-permute-start.24 = (bf16[64,2048]{1,0:T(8,128)(2,1)S(1)}, bf16[64,2048]{1,0:T(8,128)(2,1)S(1)}, u32[]{:S(2)}, u32[]{:S(2)}) collective-permute-start(bf16[64,2048]{1,0:T(8,128)(2,1)S(1)} %get-tuple-element.62), channel_id=1, source_target_pairs={{0,4},{1,5},{2,0},{3,1},{4,8},{5,9},{6,2},{7,3},{8,12},{9,13},{10,... | collective-permute-start | bytes 786440 | tf_op jit(solution)/shard_map/ppermute | solution.py:279
  100.7 15.8 %collective-permute-start.28 = (bf16[64,2048]{1,0:T(8,128)(2,1)S(1)}, bf16[64,2048]{1,0:T(8,128)(2,1)S(1)}, u32[]{:S(2)}, u32[]{:S(2)}) collective-permute-start(bf16[64,2048]{1,0:T(8,128)(2,1)S(1)} %get-tuple-element.36), channel_id=1, source_target_pairs={{0,2},{1,3},{2,6},{3,7},{4,0},{5,1},{6,10},{7,11},{8,4},{9,5},{10,... | collective-permute-start | bytes 786440 | tf_op jit(solution)/shard_map/ppermute | solution.py:279
  101.6 19.2 %collective-permute-start.31 = (bf16[64,2048]{1,0:T(8,128)(2,1)S(1)}, bf16[64,2048]{1,0:T(8,128)(2,1)S(1)}, u32[]{:S(2)}, u32[]{:S(2)}) collective-permute-start(bf16[64,2048]{1,0:T(8,128)(2,1)S(1)} %get-tuple-element.37), channel_id=1, source_target_pairs={{0,4},{1,5},{2,0},{3,1},{4,8},{5,9},{6,2},{7,3},{8,12},{9,13},{10,... | collective-permute-start | bytes 786440 | tf_op jit(solution)/shard_map/ppermute | solution.py:279
  102.8 12.8 %collective-permute-start.34 = (bf16[64,2048]{1,0:T(8,128)(2,1)S(1)}, bf16[64,2048]{1,0:T(8,128)(2,1)S(1)}, u32[]{:S(2)}, u32[]{:S(2)}) collective-permute-start(bf16[64,2048]{1,0:T(8,128)(2,1)S(1)} %get-tuple-element.63), channel_id=1, source_target_pairs={{0,2},{1,3},{2,6},{3,7},{4,0},{5,1},{6,10},{7,11},{8,4},{9,5},{10,... | collective-permute-start | bytes 786440 | tf_op jit(solution)/shard_map/ppermute | solution.py:279
  107.4 11.2 %collective-permute-start.25 = (bf16[64,2048]{1,0:T(8,128)(2,1)S(1)}, bf16[64,2048]{1,0:T(8,128)(2,1)S(1)}, u32[]{:S(2)}, u32[]{:S(2)}) collective-permute-start(bf16[64,2048]{1,0:T(8,128)(2,1)S(1)} %add_convert_fusion.1), channel_id=1, source_target_pairs={{0,4},{1,5},{2,0},{3,1},{4,8},{5,9},{6,2},{7,3},{8,12},{9,13},{10,... | collective-permute-start | bytes 786440 | tf_op jit(solution)/shard_map/ppermute | solution.py:279
  115.7 7.6 %collective-permute-start.35 = (bf16[64,2048]{1,0:T(8,128)(2,1)S(1)}, bf16[64,2048]{1,0:T(8,128)(2,1)S(1)}, u32[]{:S(2)}, u32[]{:S(2)}) collective-permute-start(bf16[64,2048]{1,0:T(8,128)(2,1)S(1)} %add_convert_fusion), channel_id=1, source_target_pairs={{0,2},{1,3},{2,6},{3,7},{4,0},{5,1},{6,10},{7,11},{8,4},{9,5},{10,... | collective-permute-start | bytes 786440 | tf_op jit(solution)/shard_map/ppermute | solution.py:279
  118.7 7.3 %collective-permute-start.29 = (bf16[64,2048]{1,0:T(8,128)(2,1)S(1)}, bf16[64,2048]{1,0:T(8,128)(2,1)S(1)}, u32[]{:S(2)}, u32[]{:S(2)}) collective-permute-start(bf16[64,2048]{1,0:T(8,128)(2,1)S(1)} %get-tuple-element.54), channel_id=1, source_target_pairs={{0,2},{1,3},{2,6},{3,7},{4,0},{5,1},{6,10},{7,11},{8,4},{9,5},{10,... | collective-permute-start | bytes 786440 | tf_op jit(solution)/shard_map/ppermute | solution.py:279
  120.2 6.4 %collective-permute-start.26 = (bf16[64,2048]{1,0:T(8,128)(2,1)S(1)}, bf16[64,2048]{1,0:T(8,128)(2,1)S(1)}, u32[]{:S(2)}, u32[]{:S(2)}) collective-permute-start(bf16[64,2048]{1,0:T(8,128)(2,1)S(1)} %get-tuple-element.55), channel_id=1, source_target_pairs={{0,4},{1,5},{2,0},{3,1},{4,8},{5,9},{6,2},{7,3},{8,12},{9,13},{10,... | collective-permute-start | bytes 786440 | tf_op jit(solution)/shard_map/ppermute | solution.py:279
  123.4 6.4 %collective-permute-start.32 = (bf16[64,2048]{1,0:T(8,128)(2,1)S(1)}, bf16[64,2048]{1,0:T(8,128)(2,1)S(1)}, u32[]{:S(2)}, u32[]{:S(2)}) collective-permute-start(bf16[64,2048]{1,0:T(8,128)(2,1)S(1)} %get-tuple-element.50), channel_id=1, source_target_pairs={{0,4},{1,5},{2,0},{3,1},{4,8},{5,9},{6,2},{7,3},{8,12},{9,13},{10,... | collective-permute-start | bytes 786440 | tf_op jit(solution)/shard_map/ppermute | solution.py:279
  125.1 6.4 %collective-permute-start.36 = (bf16[64,2048]{1,0:T(8,128)(2,1)S(1)}, bf16[64,2048]{1,0:T(8,128)(2,1)S(1)}, u32[]{:S(2)}, u32[]{:S(2)}) collective-permute-start(bf16[64,2048]{1,0:T(8,128)(2,1)S(1)} %get-tuple-element.51), channel_id=1, source_target_pairs={{0,2},{1,3},{2,6},{3,7},{4,0},{5,1},{6,10},{7,11},{8,4},{9,5},{10,... | collective-permute-start | bytes 786440 | tf_op jit(solution)/shard_map/ppermute | solution.py:279
  126.7 7.7 %collective-permute-start.30 = (bf16[64,2048]{1,0:T(8,128)(2,1)S(1)}, bf16[64,2048]{1,0:T(8,128)(2,1)S(1)}, u32[]{:S(2)}, u32[]{:S(2)}) collective-permute-start(bf16[64,2048]{1,0:T(8,128)(2,1)S(1)} %get-tuple-element.52), channel_id=1, source_target_pairs={{0,2},{1,3},{2,6},{3,7},{4,0},{5,1},{6,10},{7,11},{8,4},{9,5},{10,... | collective-permute-start | bytes 786440 | tf_op jit(solution)/shard_map/ppermute | solution.py:279
  128.2 6.6 %collective-permute-start.27 = (bf16[64,2048]{1,0:T(8,128)(2,1)S(1)}, bf16[64,2048]{1,0:T(8,128)(2,1)S(1)}, u32[]{:S(2)}, u32[]{:S(2)}) collective-permute-start(bf16[64,2048]{1,0:T(8,128)(2,1)S(1)} %get-tuple-element.53), channel_id=1, source_target_pairs={{0,4},{1,5},{2,0},{3,1},{4,8},{5,9},{6,2},{7,3},{8,12},{9,13},{10,... | collective-permute-start | bytes 786440 | tf_op jit(solution)/shard_map/ppermute | solution.py:279
  131.6 6.4 %collective-permute-start.37 = (bf16[64,2048]{1,0:T(8,128)(2,1)S(1)}, bf16[64,2048]{1,0:T(8,128)(2,1)S(1)}, u32[]{:S(2)}, u32[]{:S(2)}) collective-permute-start(bf16[64,2048]{1,0:T(8,128)(2,1)S(1)} %get-tuple-element.49), channel_id=1, source_target_pairs={{0,2},{1,3},{2,6},{3,7},{4,0},{5,1},{6,10},{7,11},{8,4},{9,5},{10,... | collective-permute-start | bytes 786440 | tf_op jit(solution)/shard_map/ppermute | solution.py:279
  132.0 6.4 %collective-permute-start.33 = (bf16[64,2048]{1,0:T(8,128)(2,1)S(1)}, bf16[64,2048]{1,0:T(8,128)(2,1)S(1)}, u32[]{:S(2)}, u32[]{:S(2)}) collective-permute-start(bf16[64,2048]{1,0:T(8,128)(2,1)S(1)} %get-tuple-element.48), channel_id=1, source_target_pairs={{0,4},{1,5},{2,0},{3,1},{4,8},{5,9},{6,2},{7,3},{8,12},{9,13},{10,... | collective-permute-start | bytes 786440 | tf_op jit(solution)/shard_map/ppermute | solution.py:279
  (1 other events, 3.6 us)

commit v6 on v5

--- a/solution.py
+++ b/solution.py
@@ -15,16 +15,23 @@
 TN = (((0,), (0,)), ((), ()))
 
 
+def column_of(row_ref):
+    count = row_ref.shape[1]
+    i = lax.broadcasted_iota(jnp.int32, (count, count), 0)
+    j = lax.broadcasted_iota(jnp.int32, (count, count), 1)
+    return jnp.sum(jnp.where(i == j, row_ref[...], 0.0), axis=1, keepdims=True)
+
+
 def decays(dt_ref, bias_ref, a_ref, step_ref, decay_ref):
-    frames, heads = dt_ref.shape
-    step_size = jax.nn.softplus(dt_ref[...] + bias_ref[...])
-    rise = step_size * -jnp.exp(a_ref[...])
+    frames = dt_ref.shape[1]
+    step_size = jax.nn.softplus(dt_ref[...] + column_of(bias_ref))
+    rise = step_size * -jnp.exp(column_of(a_ref))
     s = lax.broadcasted_iota(jnp.int32, (frames, frames), 0)
     t = lax.broadcasted_iota(jnp.int32, (frames, frames), 1)
     upto = jnp.where(s <= t, 1.0, 0.0)
-    step_ref[...] = step_size.T
+    step_ref[...] = step_size
     decay_ref[...] = jnp.dot(
-        rise.T, upto, precision=lax.Precision.HIGHEST, preferred_element_type=jnp.float32
+        rise, upto, precision=lax.Precision.HIGHEST, preferred_element_type=jnp.float32
     )
 
 
@@ -39,7 +46,8 @@
     a_ref,
     gain_ref,
     state_ref,
-    out_ref,
+    top_ref,
+    bottom_ref,
     g_ref,
     ss_ref,
     step_ref,
@@ -106,7 +114,9 @@
         scale = lax.rsqrt(mean + epsilon)
         for j in range(steps):
             at = slice(j * width, (j + 1) * width)
-            out_ref[:, at] = (g_ref[j] * scale * gain_ref[:, at]).astype(jnp.bfloat16)
+            normed = (g_ref[j] * scale * gain_ref[:, at]).astype(jnp.bfloat16)
+            top_ref[:, at] = normed[: frames // 2]
+            bottom_ref[:, at] = normed[frames // 2 :]
 
 
 def state_kernel(x_ref, b_ref, dt_ref, bias_ref, a_ref, state_ref, out_ref, step_ref, decay_ref):
@@ -138,9 +148,10 @@
     steps = heads // CHUNK
     part = width // steps
     state = state_in.reshape(width, inner)
+    dt = dt_raw.T
     column = pl.BlockSpec((frames, part), lambda i: (0, i))
     whole = pl.BlockSpec((frames, inner), lambda i: (0, 0))
-    per_head = pl.BlockSpec((frames, heads), lambda i: (0, 0))
+    per_head = pl.BlockSpec((heads, frames), lambda i: (0, 0))
     scalar = pl.BlockSpec((1, heads), lambda i: (0, 0))
     rows = pl.BlockSpec((part, inner), lambda i: (i, 0))
     full_row = pl.BlockSpec((1, width), lambda i: (0, 0))
@@ -160,8 +171,8 @@
             full_row,
             rows,
         ],
-        out_specs=pl.BlockSpec((frames, width), lambda i: (0, 0)),
-        out_shape=jax.ShapeDtypeStruct((frames, width), jnp.bfloat16),
+        out_specs=[pl.BlockSpec((frames // 2, width), lambda i: (0, 0))] * 2,
+        out_shape=[jax.ShapeDtypeStruct((frames // 2, width), jnp.bfloat16)] * 2,
         scratch_shapes=[
             pltpu.VMEM((steps, frames, part), jnp.float32),
             pltpu.VMEM((frames, 2 * head), jnp.float32),
@@ -176,7 +187,7 @@
         gate_input,
         b_proj,
         c_proj,
-        dt_raw,
+        dt,
         dt_bias[None, :],
         a_log[None, :],
         norm_gain[None, :],
@@ -194,7 +205,7 @@
             compiler_params=pltpu.CompilerParams(vmem_limit_bytes=16 << 20),
             cost_estimate=pl.CostEstimate(flops=70_000_000, bytes_accessed=3_000_000, transcendentals=20_000),
             name="state",
-        )(ssm_input, b_proj, dt_raw, dt_bias[None, :], a_log[None, :], state)
+        )(ssm_input, b_proj, dt, dt_bias[None, :], a_log[None, :], state)
         return out.reshape(heads, head, inner)
 
     return (normed, state_next)
@@ -248,9 +259,10 @@
             expert_out[0],
             route_ids,
             route_weights,
-            functools.partial(state_next, ssm_input),
+            lambda after: state_next(lax.optimization_barrier((ssm_input, after))[0]),
         )
     else:
+        normed = jnp.concatenate(normed)
         layer_out = routed_experts(normed, out_proj, expert_in, expert_out, route_ids, route_weights)
         state = state_next(ssm_input)
     return (layer_out, state[None])
@@ -295,7 +307,7 @@
 
     halves = range(2)
     size = frames // 2
-    sent = [to_x(normed[h * size : (h + 1) * size]) for h in halves]
+    sent = [to_x(normed[h]) for h in halves]
 
     columns = lax.optimization_barrier(
         jnp.where(
@@ -308,11 +320,11 @@
     def project(rows):
         return jnp.dot(rows, columns, preferred_element_type=jnp.float32).astype(jnp.bfloat16)
 
-    own = project(normed)
+    own = [project(normed[h]) for h in halves]
     rows, backs = [], []
     for h in halves:
         backs.append(to_x(project(sent[h])))
-        here = own[h * size : (h + 1) * size]
+        here = own[h]
         rows.append(
             jnp.where(
                 x == 0,
@@ -321,53 +333,8 @@
             )
         )
 
-    experts = wide * 4
-    gates = jnp.sum(
-        jnp.where(route_ids[:, :, None] == jnp.arange(experts), route_weights[:, :, None], 0.0), axis=1
-    )
-    gates, _ = lax.optimization_barrier((gates, normed))
-    other = to_x(gates)
-    gates = jnp.where(x == 0, jnp.stack([gates, other]), jnp.stack([other, gates]))[:, None]
-    step = 1
-    while step < wide:
-        gates, _ = lax.optimization_barrier((gates, sent[1] if step == 1 else rows[0]))
-        other = send(gates, lambda z, x, c: (z ^ step, x, c))
-        low = z & step == 0
-        gates = jnp.where(
-            low, jnp.concatenate([gates, other], axis=1), jnp.concatenate([other, gates], axis=1)
-        )
-        step *= 2
-    mine = (z * 2 + x) * 2 + core
-    pair = jnp.stack([mine, mine + 1 - 2 * core])
-    gates = jnp.sum(
-        jnp.where(pair[:, None] == jnp.arange(experts), gates[..., None, :], 0.0), axis=-1
-    )
-    gates = jnp.concatenate([gates[0], gates[1, ::-1]])
-    gates = lax.dynamic_slice_in_dim(jnp.concatenate([gates, gates]), place, ring, 0)
-
     far = ring // 2
-    fore, back = list(rows), list(rows)
-    fore_at, back_at = {0: fore}, {0: back}
-    for k in range(1, far):
-        fore_at[k] = [along(fore_at[k - 1][h], 1) for h in halves]
-        back_at[k] = [along(back_at[k - 1][h], -1) for h in halves]
-    last = [along(fore_at[far - 1][0], 1), along(back_at[far - 1][1], -1)]
-
     hidden_width = expert_out.shape[0]
-    early, in_other, down_other, expert_in, expert_out = lax.optimization_barrier(
-        (rows[1], in_other, down_other, expert_in, expert_out)
-    )
-    joined_in = jnp.concatenate(
-        [
-            expert_in[:, :hidden_width],
-            in_other[:, :hidden_width],
-            expert_in[:, hidden_width:],
-            in_other[:, hidden_width:],
-        ],
-        axis=1,
-    )
-    joined_down = jnp.concatenate([expert_out, down_other], axis=0)
-    joined_in, joined_down = lax.optimization_barrier((joined_in, joined_down))
     is_first = jnp.arange(2 * hidden_width)[None, :] < hidden_width
 
     def run_experts(parts, gate):
@@ -376,17 +343,69 @@
         hidden = (hidden * jnp.where(is_first, gate[:, :1], gate[:, 1:])).astype(jnp.bfloat16)
         return jnp.dot(hidden, joined_down, preferred_element_type=jnp.float32)
 
+    experts = wide * 4
+    gates = jnp.sum(
+        jnp.where(route_ids[:, :, None] == jnp.arange(experts), route_weights[:, :, None], 0.0), axis=1
+    )
+    gates, _ = lax.optimization_barrier((gates, sent[1]))
+    other = to_x(gates)
+    step = 1
+    fore_at, back_at = {0: rows}, {0: rows}
+    for k in range(1, far):
+        fore_at[k] = [along(fore_at[k - 1][h], 1) for h in halves]
+        back_at[k] = [along(back_at[k - 1][h], -1) for h in halves]
+        if k == 1:
+            joined_in = jnp.concatenate(
+                [
+                    expert_in[:, :hidden_width],
+                    in_other[:, :hidden_width],
+                    expert_in[:, hidden_width:],
+                    in_other[:, hidden_width:],
+                ],
+                axis=1,
+            )
+            joined_down = jnp.concatenate([expert_out, down_other], axis=0)
+            back_at[1][1], joined_in, joined_down, other = lax.optimization_barrier(
+                (back_at[1][1], joined_in, joined_down, other)
+            )
+            state = state_next(fore_at[1][0])
+            gates = jnp.where(x == 0, jnp.stack([gates, other]), jnp.stack([other, gates]))[:, None]
+        elif step < wide:
+            other, back_at[k][1] = lax.optimization_barrier((other, back_at[k][1]))
+            low = z & step == 0
+            gates = jnp.where(
+                low, jnp.concatenate([gates, other], axis=1), jnp.concatenate([other, gates], axis=1)
+            )
+            step *= 2
+        if step < wide:
+            other = send(gates, lambda z, x, c: (z ^ step, x, c))
+    while step < wide:
+        low = z & step == 0
+        gates = jnp.where(
+            low, jnp.concatenate([gates, other], axis=1), jnp.concatenate([other, gates], axis=1)
+        )
+        step *= 2
+        if step < wide:
+            other = send(gates, lambda z, x, c: (z ^ step, x, c))
+    mine = (z * 2 + x) * 2 + core
+    pair = jnp.stack([mine, mine + 1 - 2 * core])
+    gates = jnp.sum(
+        jnp.where(pair[:, None] == jnp.arange(experts), gates[..., None, :], 0.0), axis=-1
+    )
+    gates = jnp.concatenate([gates[0], gates[1, ::-1]])
+    gates = lax.dynamic_slice_in_dim(jnp.concatenate([gates, gates]), place, ring, 0)
+    last = [along(fore_at[far - 1][0], 1), along(back_at[far - 1][1], -1)]
+
     def cut(total, at):
         return [total[at + h * size : at + (h + 1) * size] for h in halves]
 
     ahead, behind = {}, {}
-    ahead[0] = cut(run_experts([early if h == 1 else rows[h] for h in halves], gates[0]), 0)
+    ahead[0] = cut(run_experts(rows, gates[0]), 0)
     for k in range(1, far):
         total = run_experts(
             [*back_at[k], *fore_at[k]], jnp.concatenate([gates[k], gates[ring - k]])
         )
         ahead[k], behind[k] = cut(total, 0), cut(total, frames)
-    state = state_next()
     last[0], last[1], state, *near = lax.optimization_barrier(
         (last[0], last[1], state, *ahead[far - 1], *behind[far - 1])
     )

time: 140 us -> 137 us (0.979)
  starting transfers between devices: 44.9 us -> 37.5 us
  matrix products: 15.9 us -> 19.9 us
  other arithmetic: 8.34 us -> 12.1 us
  local copies, waits for them, and re-layouts: 7.4 us -> 4.63 us
    ppermute x38, starting transfers between devices: 44.9 us -> 37.5 us  [send(): return lax.ppermute(value, axes, routes(wide, move))]
    dot_general x5, matrix products: 7.49 us -> 10.5 us  [run_experts(): jnp.dot(jnp.concatenate(parts), joined_in, preferred_element_type=jnp.flo...]
    unnamed x23 -> x20, local copies, waits for them, and re-layouts: 1.87 us -> 0.05 us
    select_n x1, other arithmetic: 3.58 us -> 5.23 us  [dense_experts(): jnp.where(core == 0, jnp.concatenate([out_proj, out_other], axis=1), jnp....]
    dot_general x3 -> x4, matrix products: 3.41 us -> 4.36 us  [project(): jnp.dot(rows, columns, preferred_element_type=jnp.float32)]
  transfers between devices with their start and end apart: 38 -> 38, of which waited for: 19 -> 18; matrix products, arithmetic and copies ran while one was open for 21% -> 24% of each run, Pallas kernels for 6% -> 7%
where the time goes in v6:
time: 137 us
  waiting for transfers between devices  52.5 us (38%)
  starting transfers between devices  37.5 us (27%)
  matrix products  19.9 us (15%)
  other arithmetic  12.1 us (9%)
  Pallas kernels  8.93 us (7%)
  local copies, waits for them, and re-layouts  4.63 us (3%)
    ppermute x38, waiting for transfers between devices, send(): return lax.ppermute(value, axes, routes(wide, move))  52.5 us
    ppermute x38, starting transfers between devices, send(): return lax.ppermute(value, axes, routes(wide, move))  37.5 us
    dot_general x5, matrix products, run_experts(): jnp.dot(jnp.concatenate(parts), joined_in, preferred_element_type=jnp.flo...  10.5 us
    pallas_call x1, Pallas kernels, ssm_mixer(): pl.pallas_call(mixer_kernel, grid=(steps,), in_specs=[pl.BlockSpec(memory...  5.36 us
    select_n x1, other arithmetic, dense_experts(): jnp.where(core == 0, jnp.concatenate([out_proj, out_other], axis=1), jnp....  5.23 us
    dot_general x5, matrix products, run_experts(): return jnp.dot(hidden, joined_down, preferred_element_type=jnp.float32)  5.01 us
    dot_general x4, matrix products, project(): jnp.dot(rows, columns, preferred_element_type=jnp.float32)  4.36 us
    pallas_call x1, Pallas kernels, state_next(): pl.pallas_call(state_kernel, grid=(steps,), in_specs=[column, whole, per_...  3.58 us
  transfers between devices with their start and end apart: 38, of which 18 were waited for; matrix products, arithmetic and copies ran while one was open for 24% of the time, Pallas kernels for 7%

profile of v6, /device:TPU:0, one launch (start us, length us, event | category | flops | bytes accessed | tf_op | source)
XLA Modules:
  0.0 136.7 jit_solution(4730727901514878889)
XLA Ops:
  1.1 5.4 %mixer.1 = (bf16[64,2048]{1,0:T(8,128)(2,1)}, bf16[64,2048]{1,0:T(8,128)(2,1)}) custom-call(f32[32]{0:T(128)} %skip_ref.1, bf16[128,2048]{1,0:T(8,128)(2,1)} %x_ref.2, bf16[128,2048]{1,0:T(8,128)(2,1)} %z_ref.1, bf16[128,128]{1,0:T(8,128)(2,1)} %b_ref.3, bf16[128,128]{1,0:T(8,128)(2,1)} %c_ref.1, f32[32,128]{1,0:T(8,128)} %bitcast.67, f32[1,32]{1,0:T(1,128)} %bitcast.69, ...), custom_call_target="tpu_custom_call" | custom-call | flops 400000000 | bytes 6000000 | tf_op jit(solution)/shard_map/mixer/pallas_call | solution.py:159
  6.5 2.5 %collective-permute-start.3 = (bf16[64,2048]{1,0:T(8,128)(2,1)}, bf16[64,2048]{1,0:T(8,128)(2,1)S(1)}, u32[]{:S(2)}, u32[]{:S(2)}) collective-permute-start(bf16[64,2048]{1,0:T(8,128)(2,1)} %get-tuple-element.26), channel_id=1, source_target_pairs={{0,2},{1,3},{2,0},{3,1},{4,6},{5,7},{6,4},{7,5},{8,10},{9,11},{10,... | collective-permute-start | bytes 786440 | tf_op jit(solution)/shard_map/ppermute | solution.py:291
  9.7 2.2 %fusion.101 = (bf16[2048,384]{1,0:T(8,128)(2,1)S(1)}, bf16[2048,384]{1,0:T(8,128)(2,1)S(1)}) fusion(bf16[2048,768]{1,0:T(8,128)(2,1)} %bitcast.5), kind=kLoop, calls=%fused_computation.160 | loop fusion | bytes 6291456 | tf_op jit(solution)/shard_map/slice | solution.py:360
  12.0 5.2 %maximum_select_fusion = bf16[2048,1024]{1,0:T(8,128)(2,1)S(1)} fusion(bf16[2048,512]{1,0:T(8,128)(2,1)} %collective-permute-done, bf16[2048,512]{1,0:T(8,128)(2,1)} %param.25, pred[]{:T(512)S(6)} %eq.44), kind=kLoop, calls=%fused_computation.1 | loop fusion | flops 18874368 | bytes 8388609 | tf_op jit(solution)/shard_map/jit(_where)/select_n | solution.py:313
  18.1 3.8 %collective-permute-done.1 = bf16[64,2048]{1,0:T(8,128)(2,1)} collective-permute-done((bf16[64,2048]{1,0:T(8,128)(2,1)}, bf16[64,2048]{1,0:T(8,128)(2,1)}, u32[]{:S(2)}, u32[]{:S(2)}) %collective-permute-start.1) | collective-permute-done | bytes 262176 | tf_op jit(solution)/shard_map/ppermute | solution.py:291
  21.9 1.8 %convolution_convert_fusion.3 = bf16[64,1024]{1,0:T(8,128)(2,1)S(1)} fusion(bf16[64,2048]{1,0:T(8,128)(2,1)} %collective-permute-done.1, bf16[2048,1024]{1,0:T(8,128)(2,1)S(1)} %maximum_select_fusion), kind=kOutput, calls=%fused_computation.6 | convolution fusion | flops 268500992 | bytes 4587520 | tf_op jit(solution)/shard_map/dot_general | solution.py:321
  23.7 1.8 %collective-permute-start.2 = (bf16[64,1024]{1,0:T(8,128)(2,1)S(1)}, bf16[64,1024]{1,0:T(8,128)(2,1)S(1)}, u32[]{:S(2)}, u32[]{:S(2)}) collective-permute-start(bf16[64,1024]{1,0:T(8,128)(2,1)S(1)} %convolution_convert_fusion.3), channel_id=1, source_target_pairs={{0,2},{1,3},{2,0},{3,1},{4,6},{5,7},{6,4},{7,5},{8,10},{9,11},{10,... | collective-permute-start | bytes 393224 | tf_op jit(solution)/shard_map/ppermute | solution.py:291
  26.8 2.9 %collective-permute-done.2 = bf16[64,1024]{1,0:T(8,128)(2,1)S(1)} collective-permute-done((bf16[64,1024]{1,0:T(8,128)(2,1)S(1)}, bf16[64,1024]{1,0:T(8,128)(2,1)S(1)}, u32[]{:S(2)}, u32[]{:S(2)}) %collective-permute-start.2) | collective-permute-done | bytes 131104 | tf_op jit(solution)/shard_map/ppermute | solution.py:291
  29.8 1.7 %collective-permute-start.14 = (bf16[64,2048]{1,0:T(8,128)(2,1)S(1)}, bf16[64,2048]{1,0:T(8,128)(2,1)}, u32[]{:S(2)}, u32[]{:S(2)}) collective-permute-start(bf16[64,2048]{1,0:T(8,128)(2,1)S(1)} %maximum_select_fusion.1), channel_id=1, source_target_pairs={{0,4},{1,5},{2,0},{3,1},{4,8},{5,9},{6,2},{7,3},{8,12},{9,13},{10,... | collective-permute-start | bytes 786440 | tf_op jit(solution)/shard_map/ppermute | solution.py:291
  33.8 1.5 %collective-permute-start.15 = (bf16[64,2048]{1,0:T(8,128)(2,1)}, bf16[64,2048]{1,0:T(8,128)(2,1)}, u32[]{:S(2)}, u32[]{:S(2)}) collective-permute-start(bf16[64,2048]{1,0:T(8,128)(2,1)} %maximum_select_fusion.2), channel_id=1, source_target_pairs={{0,4},{1,5},{2,0},{3,1},{4,8},{5,9},{6,2},{7,3},{8,12},{9,13},{10,... | collective-permute-start | bytes 786440 | tf_op jit(solution)/shard_map/ppermute | solution.py:291
  35.3 4.2 %collective-permute-done.14 = bf16[64,2048]{1,0:T(8,128)(2,1)} collective-permute-done((bf16[64,2048]{1,0:T(8,128)(2,1)S(1)}, bf16[64,2048]{1,0:T(8,128)(2,1)}, u32[]{:S(2)}, u32[]{:S(2)}) %collective-permute-start.14) | collective-permute-done | bytes 262176 | tf_op jit(solution)/shard_map/ppermute | solution.py:291
  39.8 1.9 %collective-permute-start.8 = (f32[128,16]{0,1:T(8,128)S(1)}, f32[128,16]{0,1:T(8,128)S(1)}, u32[]{:S(2)}, u32[]{:S(2)}) collective-permute-start(f32[128,16]{0,1:T(8,128)S(1)} %select_reduce_fusion.1), channel_id=1, source_target_pairs={{0,2},{1,3},{2,0},{3,1},{4,6},{5,7},{6,4},{7,5},{8,10},{9,11},{10,... | collective-permute-start | bytes 24584 | tf_op jit(solution)/shard_map/ppermute | solution.py:291
  41.9 3.1 %collective-permute-done.15 = bf16[64,2048]{1,0:T(8,128)(2,1)} collective-permute-done((bf16[64,2048]{1,0:T(8,128)(2,1)}, bf16[64,2048]{1,0:T(8,128)(2,1)}, u32[]{:S(2)}, u32[]{:S(2)}) %collective-permute-start.15) | collective-permute-done | bytes 262176 | tf_op jit(solution)/shard_map/ppermute | solution.py:291
  45.3 5.4 %collective-permute-done.17 = bf16[64,2048]{1,0:T(8,128)(2,1)} collective-permute-done((bf16[64,2048]{1,0:T(8,128)(2,1)}, bf16[64,2048]{1,0:T(8,128)(2,1)}, u32[]{:S(2)}, u32[]{:S(2)}) %collective-permute-start.17) | collective-permute-done | bytes 262176 | tf_op jit(solution)/shard_map/ppermute | solution.py:291
  50.9 2.2 %pad_maximum_fusion.1 = bf16[768,2048]{1,0:T(8,128)(2,1)S(1)} fusion(bf16[384,2048]{1,0:T(8,128)(2,1)} %collective-permute-done.7, bf16[384,2048]{1,0:T(8,128)(2,1)} %bitcast.6), kind=kLoop, calls=%fused_computation.2 | loop fusion | flops 6291456 | bytes 6291456 | tf_op jit(solution)/shard_map/concatenate | solution.py:367
  53.2 3.6 %state.1 = f32[2048,128]{1,0:T(8,128)} custom-call(bf16[128,2048]{1,0:T(8,128)(2,1)S(1)} %copy-done.1, bf16[128,128]{1,0:T(8,128)(2,1)S(1)} %copy-done.2, f32[32,128]{1,0:T(8,128)S(1)} %bitcast.68, f32[1,32]{1,0:T(1,128)S(1)} %bitcast.70, f32[1,32]{1,0:T(1,128)S(1)} %bitcast.72, f32[2048,128]{1,0:T(8,128)S(1)} %bitcast.66), custom_call_target="tpu_custom_call" | custom-call | flops 70000000 | bytes 3000000 | tf_op jit(solution)/shard_map/state/pallas_call | solution.py:198
  56.8 1.8 %collective-permute-start.5 = (bf16[64,2048]{1,0:T(8,128)(2,1)}, bf16[64,2048]{1,0:T(8,128)(2,1)S(1)}, u32[]{:S(2)}, u32[]{:S(2)}) collective-permute-start(bf16[64,2048]{1,0:T(8,128)(2,1)} %maximum_select_fusion.2), channel_id=1, source_target_pairs={{0,2},{1,3},{2,6},{3,7},{4,0},{5,1},{6,10},{7,11},{8,4},{9,5},{10,... | collective-permute-start | bytes 786440 | tf_op jit(solution)/shard_map/ppermute | solution.py:291
  58.6 1.8 %collective-permute-start.22 = (bf16[64,2048]{1,0:T(8,128)(2,1)S(1)}, bf16[64,2048]{1,0:T(8,128)(2,1)S(1)}, u32[]{:S(2)}, u32[]{:S(2)}) collective-permute-start(bf16[64,2048]{1,0:T(8,128)(2,1)S(1)} %collective-permute-done.16), channel_id=1, source_target_pairs={{0,2},{1,3},{2,6},{3,7},{4,0},{5,1},{6,10},{7,11},{8,4},{9,5},{10,... | collective-permute-start | bytes 786440 | tf_op jit(solution)/shard_map/ppermute | solution.py:291
  60.6 1.3 collective-permute-start.20
  61.9 2.2 %fusion.102 = (bf16[2048,384]{1,0:T(8,128)(2,1)S(1)}, bf16[2048,384]{1,0:T(8,128)(2,1)S(1)}) fusion(bf16[2048,768]{1,0:T(8,128)(2,1)} %collective-permute-done.6), kind=kLoop, calls=%fused_computation.161 | loop fusion | bytes 6291456 | tf_op jit(solution)/shard_map/slice | solution.py:361
  64.9 2.2 %collective-permute-start.9 = (f32[2,1,128,16]{2,3,1,0:T(8,128)S(1)}, f32[2,1,128,16]{2,3,1,0:T(8,128)S(1)}, u32[]{:S(2)}, u32[]{:S(2)}) collective-permute-start(f32[2,1,128,16]{2,3,1,0:T(8,128)S(1)} %maximum_select_fusion.5), channel_id=1, source_target_pairs={{0,4},{1,5},{2,6},{3,7},{4,0},{5,1},{6,2},{7,3},{8,12},{9,13},{10,... | collective-permute-start | bytes 49160 | tf_op jit(solution)/shard_map/ppermute | solution.py:291
  67.5 2.9 %fusion = f32[256,1536]{1,0:T(8,128)S(1)} fusion(bf16[2048,1536]{1,0:T(8,128)(2,1)S(1)} %pad_maximum_fusion, bf16[64,2048]{1,0:T(8,128)(2,1)} %collective-permute-done.15, bf16[64,2048]{1,0:T(8,128)(2,1)} %collective-permute-done.14, bf16[64,2048]{1,0:T(8,128)(2,1)S(1)} %collective-permute-done.5, bf16[64,2048]{1,0:T(8,128)(2,1)} %collective-permute-done.13), kind=kOutput, calls=%fused_computation.8 | convolution fusion | flops 1614807040 | bytes 8912896 | tf_op jit(solution)/shard_map/dot_general | solution.py:341
  70.4 2.0 %fusion.44 = f32[128,1536]{1,0:T(8,128)S(1)} fusion(bf16[2048,1536]{1,0:T(8,128)(2,1)S(1)} %pad_maximum_fusion, bf16[64,2048]{1,0:T(8,128)(2,1)} %maximum_select_fusion.2, bf16[64,2048]{1,0:T(8,128)(2,1)S(1)} %maximum_select_fusion.1), kind=kOutput, calls=%fused_computation.65 | convolution fusion | flops 806354944 | bytes 7602176 | tf_op jit(solution)/shard_map/dot_general | solution.py:341
  72.4 1.2 collective-permute-done.10
  74.5 1.9 %collective-permute-start.11 = (f32[2,2,128,16]{2,3,1,0:T(8,128)S(1)}, f32[2,2,128,16]{2,3,1,0:T(8,128)S(1)}, u32[]{:S(2)}, u32[]{:S(2)}) collective-permute-start(f32[2,2,128,16]{2,3,1,0:T(8,128)S(1)} %maximum_select_fusion.4), channel_id=1, source_target_pairs={{0,8},{1,9},{2,10},{3,11},{4,12},{5,13},{6,14},{7,15},{8,0},{9,1},... | collective-permute-start | bytes 98312 | tf_op jit(solution)/shard_map/ppermute | solution.py:291
  76.4 2.8 %fusion.8 = f32[256,1536]{1,0:T(8,128)S(1)} fusion(bf16[2048,1536]{1,0:T(8,128)(2,1)S(1)} %pad_maximum_fusion, bf16[64,2048]{1,0:T(8,128)(2,1)S(1)} %collective-permute-done.18, bf16[64,2048]{1,0:T(8,128)(2,1)} %collective-permute-done.17, bf16[64,2048]{1,0:T(8,128)(2,1)S(1)} %collective-permute-done.10, bf16[64,2048]{1,0:T(8,128)(2,1)S(1)} %collective-permute-done.16), kind=kOutput, calls=%fused_computation.16 | convolution fusion | flops 1614807040 | bytes 8912896 | tf_op jit(solution)/shard_map/dot_general | solution.py:341
  79.1 2.2 %collective-permute-done.11 = f32[2,2,128,16]{2,3,1,0:T(8,128)S(1)} collective-permute-done((f32[2,2,128,16]{2,3,1,0:T(8,128)S(1)}, f32[2,2,128,16]{2,3,1,0:T(8,128)S(1)}, u32[]{:S(2)}, u32[]{:S(2)}) %collective-permute-start.11) | collective-permute-done | bytes 32800 | tf_op jit(solution)/shard_map/ppermute | solution.py:291
  81.6 1.8 %fusion.16 = f32[256,1536]{1,0:T(8,128)S(1)} fusion(bf16[2048,1536]{1,0:T(8,128)(2,1)S(1)} %pad_maximum_fusion, bf16[64,2048]{1,0:T(8,128)(2,1)S(1)} %collective-permute-done.23, bf16[64,2048]{1,0:T(8,128)(2,1)S(1)} %collective-permute-done.19, bf16[64,2048]{1,0:T(8,128)(2,1)S(1)} %collective-permute-done.12, bf16[64,2048]{1,0:T(8,128)(2,1)S(1)} %collective-permute-done.22), kind=kOutput, calls=%fused_computation.24 | convolution fusion | flops 1614807040 | bytes 8912896 | tf_op jit(solution)/shard_map/dot_general | solution.py:341
  83.4 1.2 fusion.56
  84.8 1.2 fusion.54
  86.0 5.1 %collective-permute-done.21 = bf16[64,2048]{1,0:T(8,128)(2,1)S(1)} collective-permute-done((bf16[64,2048]{1,0:T(8,128)(2,1)S(1)}, bf16[64,2048]{1,0:T(8,128)(2,1)S(1)}, u32[]{:S(2)}, u32[]{:S(2)}) %collective-permute-start.21) | collective-permute-done | bytes 262176 | tf_op jit(solution)/shard_map/ppermute | solution.py:291
  91.2 1.0 fusion.48
  93.0 1.7 %collective-permute-start.24 = (bf16[64,2048]{1,0:T(8,128)(2,1)S(1)}, bf16[64,2048]{1,0:T(8,128)(2,1)S(1)}, u32[]{:S(2)}, u32[]{:S(2)}) collective-permute-start(bf16[64,2048]{1,0:T(8,128)(2,1)S(1)} %get-tuple-element.66), channel_id=1, source_target_pairs={{0,4},{1,5},{2,0},{3,1},{4,8},{5,9},{6,2},{7,3},{8,12},{9,13},{10,... | collective-permute-start | bytes 786440 | tf_op jit(solution)/shard_map/ppermute | solution.py:291
  94.7 1.2 fusion.52
  96.4 2.0 %collective-permute-start.31 = (bf16[64,2048]{1,0:T(8,128)(2,1)S(1)}, bf16[64,2048]{1,0:T(8,128)(2,1)S(1)}, u32[]{:S(2)}, u32[]{:S(2)}) collective-permute-start(bf16[64,2048]{1,0:T(8,128)(2,1)S(1)} %get-tuple-element.41), channel_id=1, source_target_pairs={{0,4},{1,5},{2,0},{3,1},{4,8},{5,9},{6,2},{7,3},{8,12},{9,13},{10,... | collective-permute-start | bytes 786440 | tf_op jit(solution)/shard_map/ppermute | solution.py:291
  98.4 3.7 %collective-permute-done.24 = bf16[64,2048]{1,0:T(8,128)(2,1)S(1)} collective-permute-done((bf16[64,2048]{1,0:T(8,128)(2,1)S(1)}, bf16[64,2048]{1,0:T(8,128)(2,1)S(1)}, u32[]{:S(2)}, u32[]{:S(2)}) %collective-permute-start.24) | collective-permute-done | bytes 262176 | tf_op jit(solution)/shard_map/ppermute | solution.py:291
  102.1 1.8 %collective-permute-start.25 = (bf16[64,2048]{1,0:T(8,128)(2,1)S(1)}, bf16[64,2048]{1,0:T(8,128)(2,1)S(1)}, u32[]{:S(2)}, u32[]{:S(2)}) collective-permute-start(bf16[64,2048]{1,0:T(8,128)(2,1)S(1)} %add_convert_fusion.1), channel_id=1, source_target_pairs={{0,4},{1,5},{2,0},{3,1},{4,8},{5,9},{6,2},{7,3},{8,12},{9,13},{10,... | collective-permute-start | bytes 786440 | tf_op jit(solution)/shard_map/ppermute | solution.py:291
  105.2 2.4 %collective-permute-done.28 = bf16[64,2048]{1,0:T(8,128)(2,1)S(1)} collective-permute-done((bf16[64,2048]{1,0:T(8,128)(2,1)S(1)}, bf16[64,2048]{1,0:T(8,128)(2,1)S(1)}, u32[]{:S(2)}, u32[]{:S(2)}) %collective-permute-start.28) | collective-permute-done | bytes 262176 | tf_op jit(solution)/shard_map/ppermute | solution.py:291
  107.6 3.4 %collective-permute-done.25 = bf16[64,2048]{1,0:T(8,128)(2,1)S(1)} collective-permute-done((bf16[64,2048]{1,0:T(8,128)(2,1)S(1)}, bf16[64,2048]{1,0:T(8,128)(2,1)S(1)}, u32[]{:S(2)}, u32[]{:S(2)}) %collective-permute-start.25) | collective-permute-done | bytes 262176 | tf_op jit(solution)/shard_map/ppermute | solution.py:291
  111.1 2.1 %collective-permute-start.26 = (bf16[64,2048]{1,0:T(8,128)(2,1)S(1)}, bf16[64,2048]{1,0:T(8,128)(2,1)S(1)}, u32[]{:S(2)}, u32[]{:S(2)}) collective-permute-start(bf16[64,2048]{1,0:T(8,128)(2,1)S(1)} %get-tuple-element.59), channel_id=1, source_target_pairs={{0,4},{1,5},{2,0},{3,1},{4,8},{5,9},{6,2},{7,3},{8,12},{9,13},{10,... | collective-permute-start | bytes 786440 | tf_op jit(solution)/shard_map/ppermute | solution.py:291
  114.5 1.8 %collective-permute-start.32 = (bf16[64,2048]{1,0:T(8,128)(2,1)S(1)}, bf16[64,2048]{1,0:T(8,128)(2,1)S(1)}, u32[]{:S(2)}, u32[]{:S(2)}) collective-permute-start(bf16[64,2048]{1,0:T(8,128)(2,1)S(1)} %get-tuple-element.54), channel_id=1, source_target_pairs={{0,4},{1,5},{2,0},{3,1},{4,8},{5,9},{6,2},{7,3},{8,12},{9,13},{10,... | collective-permute-start | bytes 786440 | tf_op jit(solution)/shard_map/ppermute | solution.py:291
  116.2 3.7 %collective-permute-done.26 = bf16[64,2048]{1,0:T(8,128)(2,1)S(1)} collective-permute-done((bf16[64,2048]{1,0:T(8,128)(2,1)S(1)}, bf16[64,2048]{1,0:T(8,128)(2,1)S(1)}, u32[]{:S(2)}, u32[]{:S(2)}) %collective-permute-start.26) | collective-permute-done | bytes 262176 | tf_op jit(solution)/shard_map/ppermute | solution.py:291
  119.9 2.4 %collective-permute-done.29 = bf16[64,2048]{1,0:T(8,128)(2,1)S(1)} collective-permute-done((bf16[64,2048]{1,0:T(8,128)(2,1)S(1)}, bf16[64,2048]{1,0:T(8,128)(2,1)S(1)}, u32[]{:S(2)}, u32[]{:S(2)}) %collective-permute-start.29) | collective-permute-done | bytes 262176 | tf_op jit(solution)/shard_map/ppermute | solution.py:291
  122.6 1.9 %collective-permute-start.30 = (bf16[64,2048]{1,0:T(8,128)(2,1)S(1)}, bf16[64,2048]{1,0:T(8,128)(2,1)S(1)}, u32[]{:S(2)}, u32[]{:S(2)}) collective-permute-start(bf16[64,2048]{1,0:T(8,128)(2,1)S(1)} %get-tuple-element.56), channel_id=1, source_target_pairs={{0,2},{1,3},{2,6},{3,7},{4,0},{5,1},{6,10},{7,11},{8,4},{9,5},{10,... | collective-permute-start | bytes 786440 | tf_op jit(solution)/shard_map/ppermute | solution.py:291
  124.5 3.4 %collective-permute-done.36 = bf16[64,2048]{1,0:T(8,128)(2,1)S(1)} collective-permute-done((bf16[64,2048]{1,0:T(8,128)(2,1)S(1)}, bf16[64,2048]{1,0:T(8,128)(2,1)S(1)}, u32[]{:S(2)}, u32[]{:S(2)}) %collective-permute-start.36) | collective-permute-done | bytes 262176 | tf_op jit(solution)/shard_map/ppermute | solution.py:291
  128.3 1.8 %collective-permute-start.37 = (bf16[64,2048]{1,0:T(8,128)(2,1)S(1)}, bf16[64,2048]{1,0:T(8,128)(2,1)S(1)}, u32[]{:S(2)}, u32[]{:S(2)}) collective-permute-start(bf16[64,2048]{1,0:T(8,128)(2,1)S(1)} %get-tuple-element.53), channel_id=1, source_target_pairs={{0,2},{1,3},{2,6},{3,7},{4,0},{5,1},{6,10},{7,11},{8,4},{9,5},{10,... | collective-permute-start | bytes 786440 | tf_op jit(solution)/shard_map/ppermute | solution.py:291
  130.8 3.6 %collective-permute-done.33 = bf16[64,2048]{1,0:T(8,128)(2,1)S(1)} collective-permute-done((bf16[64,2048]{1,0:T(8,128)(2,1)S(1)}, bf16[64,2048]{1,0:T(8,128)(2,1)S(1)}, u32[]{:S(2)}, u32[]{:S(2)}) %collective-permute-start.33) | collective-permute-done | bytes 262176 | tf_op jit(solution)/shard_map/ppermute | solution.py:291
  134.6 1.3 fusion.43
  (98 shorter events, 15.7 us)
Async XLA Ops:
  0.6 11.3 %collective-permute-start = (bf16[2048,512]{1,0:T(8,128)(2,1)}, bf16[2048,512]{1,0:T(8,128)(2,1)}, u32[]{:S(2)}, u32[]{:S(2)}) collective-permute-start(bf16[2048,512]{1,0:T(8,128)(2,1)} %param.25), channel_id=1, source_target_pairs={{0,1},{1,0},{2,3},{3,2},{4,5},{5,4},{6,7},{7,6},{8,9},{9,8},{10,11... | collective-permute-start | bytes 6291464 | tf_op jit(solution)/shard_map/ppermute | solution.py:291
  6.5 19.0 %collective-permute-start.3 = (bf16[64,2048]{1,0:T(8,128)(2,1)}, bf16[64,2048]{1,0:T(8,128)(2,1)S(1)}, u32[]{:S(2)}, u32[]{:S(2)}) collective-permute-start(bf16[64,2048]{1,0:T(8,128)(2,1)} %get-tuple-element.26), channel_id=1, source_target_pairs={{0,2},{1,3},{2,0},{3,1},{4,6},{5,7},{6,4},{7,5},{8,10},{9,11},{10,... | collective-permute-start | bytes 786440 | tf_op jit(solution)/shard_map/ppermute | solution.py:291
  9.0 51.6 %collective-permute-start.6 = (bf16[2048,768]{1,0:T(8,128)(2,1)}, bf16[2048,768]{1,0:T(8,128)(2,1)}, u32[]{:S(2)}, u32[]{:S(2)}) collective-permute-start(bf16[2048,768]{1,0:T(8,128)(2,1)} %bitcast.5), channel_id=1, source_target_pairs={{0,1},{1,0},{2,3},{3,2},{4,5},{5,4},{6,7},{7,6},{8,9},{9,8},{10,11... | collective-permute-start | bytes 9437192 | tf_op jit(solution)/shard_map/ppermute | solution.py:291
  9.2 30.6 %collective-permute-start.7 = (bf16[384,2048]{1,0:T(8,128)(2,1)}, bf16[384,2048]{1,0:T(8,128)(2,1)}, u32[]{:S(2)}, u32[]{:S(2)}) collective-permute-start(bf16[384,2048]{1,0:T(8,128)(2,1)} %bitcast.6), channel_id=1, source_target_pairs={{0,1},{1,0},{2,3},{3,2},{4,5},{5,4},{6,7},{7,6},{8,9},{9,8},{10,11... | collective-permute-start | bytes 4718600 | tf_op jit(solution)/shard_map/ppermute | solution.py:291
  9.5 2.4 %copy-start.8 = (f32[128,8]{0,1:T(8,128)S(1)}, f32[128,8]{0,1:T(8,128)}, u32[]{:S(2)}) copy-start(f32[128,8]{0,1:T(8,128)} %param.29) | copy-start | bytes 12292
  9.5 2.4 %copy-start.9 = (s32[128,8]{0,1:T(8,128)S(1)}, s32[128,8]{0,1:T(8,128)}, u32[]{:S(2)}) copy-start(s32[128,8]{0,1:T(8,128)} %param.28) | copy-start | bytes 12292
  9.5 12.4 %collective-permute-start.1 = (bf16[64,2048]{1,0:T(8,128)(2,1)}, bf16[64,2048]{1,0:T(8,128)(2,1)}, u32[]{:S(2)}, u32[]{:S(2)}) collective-permute-start(bf16[64,2048]{1,0:T(8,128)(2,1)} %get-tuple-element.25), channel_id=1, source_target_pairs={{0,2},{1,3},{2,0},{3,1},{4,6},{5,7},{6,4},{7,5},{8,10},{9,11},{10,... | collective-permute-start | bytes 786440 | tf_op jit(solution)/shard_map/ppermute | solution.py:291
  11.9 5.3 %copy-start.7 = (bf16[64,2048]{1,0:T(8,128)(2,1)S(1)}, bf16[64,2048]{1,0:T(8,128)(2,1)}, u32[]{:S(2)}) copy-start(bf16[64,2048]{1,0:T(8,128)(2,1)} %get-tuple-element.25) | copy-start | bytes 786436
  23.7 7.8 %copy-start.6 = (bf16[64,2048]{1,0:T(8,128)(2,1)S(1)}, bf16[64,2048]{1,0:T(8,128)(2,1)}, u32[]{:S(2)}) copy-start(bf16[64,2048]{1,0:T(8,128)(2,1)} %get-tuple-element.26) | copy-start | bytes 786436
  23.7 6.0 %collective-permute-start.2 = (bf16[64,1024]{1,0:T(8,128)(2,1)S(1)}, bf16[64,1024]{1,0:T(8,128)(2,1)S(1)}, u32[]{:S(2)}, u32[]{:S(2)}) collective-permute-start(bf16[64,1024]{1,0:T(8,128)(2,1)S(1)} %convolution_convert_fusion.3), channel_id=1, source_target_pairs={{0,2},{1,3},{2,0},{3,1},{4,6},{5,7},{6,4},{7,5},{8,10},{9,11},{10,... | collective-permute-start | bytes 393224 | tf_op jit(solution)/shard_map/ppermute | solution.py:291
  26.4 6.6 %collective-permute-start.4 = (bf16[64,1024]{1,0:T(8,128)(2,1)S(1)}, bf16[64,1024]{1,0:T(8,128)(2,1)S(1)}, u32[]{:S(2)}, u32[]{:S(2)}) collective-permute-start(bf16[64,1024]{1,0:T(8,128)(2,1)S(1)} %convolution_convert_fusion.1), channel_id=1, source_target_pairs={{0,2},{1,3},{2,0},{3,1},{4,6},{5,7},{6,4},{7,5},{8,10},{9,11},{10,... | collective-permute-start | bytes 393224 | tf_op jit(solution)/shard_map/ppermute | solution.py:291
  29.8 9.6 %collective-permute-start.14 = (bf16[64,2048]{1,0:T(8,128)(2,1)S(1)}, bf16[64,2048]{1,0:T(8,128)(2,1)}, u32[]{:S(2)}, u32[]{:S(2)}) collective-permute-start(bf16[64,2048]{1,0:T(8,128)(2,1)S(1)} %maximum_select_fusion.1), channel_id=1, source_target_pairs={{0,4},{1,5},{2,0},{3,1},{4,8},{5,9},{6,2},{7,3},{8,12},{9,13},{10,... | collective-permute-start | bytes 786440 | tf_op jit(solution)/shard_map/ppermute | solution.py:291
  32.4 9.3 %collective-permute-start.13 = (bf16[64,2048]{1,0:T(8,128)(2,1)S(1)}, bf16[64,2048]{1,0:T(8,128)(2,1)}, u32[]{:S(2)}, u32[]{:S(2)}) collective-permute-start(bf16[64,2048]{1,0:T(8,128)(2,1)S(1)} %maximum_select_fusion.1), channel_id=1, source_target_pairs={{0,2},{1,3},{2,6},{3,7},{4,0},{5,1},{6,10},{7,11},{8,4},{9,5},{10,... | collective-permute-start | bytes 786440 | tf_op jit(solution)/shard_map/ppermute | solution.py:291
  33.8 11.2 %collective-permute-start.15 = (bf16[64,2048]{1,0:T(8,128)(2,1)}, bf16[64,2048]{1,0:T(8,128)(2,1)}, u32[]{:S(2)}, u32[]{:S(2)}) collective-permute-start(bf16[64,2048]{1,0:T(8,128)(2,1)} %maximum_select_fusion.2), channel_id=1, source_target_pairs={{0,4},{1,5},{2,0},{3,1},{4,8},{5,9},{6,2},{7,3},{8,12},{9,13},{10,... | collective-permute-start | bytes 786440 | tf_op jit(solution)/shard_map/ppermute | solution.py:291
  39.4 11.2 %collective-permute-start.17 = (bf16[64,2048]{1,0:T(8,128)(2,1)}, bf16[64,2048]{1,0:T(8,128)(2,1)}, u32[]{:S(2)}, u32[]{:S(2)}) collective-permute-start(bf16[64,2048]{1,0:T(8,128)(2,1)} %collective-permute-done.14), channel_id=1, source_target_pairs={{0,4},{1,5},{2,0},{3,1},{4,8},{5,9},{6,2},{7,3},{8,12},{9,13},{10,... | collective-permute-start | bytes 786440 | tf_op jit(solution)/shard_map/ppermute | solution.py:291
  39.8 13.3 %copy-start = (f32[1,32,64,128]{3,2,1,0:T(8,128)S(1)}, f32[1,32,64,128]{3,2,1,0:T(8,128)}, u32[]{:S(2)}) copy-start(f32[1,32,64,128]{3,2,1,0:T(8,128)} %param.24) | copy-start | bytes 3145732
  39.8 13.4 %copy-start.1 = (bf16[128,2048]{1,0:T(8,128)(2,1)S(1)}, bf16[128,2048]{1,0:T(8,128)(2,1)}, u32[]{:S(2)}) copy-start(bf16[128,2048]{1,0:T(8,128)(2,1)} %x_ref.2) | copy-start | bytes 1572868
  39.8 13.4 %copy-start.2 = (bf16[128,128]{1,0:T(8,128)(2,1)S(1)}, bf16[128,128]{1,0:T(8,128)(2,1)}, u32[]{:S(2)}) copy-start(bf16[128,128]{1,0:T(8,128)(2,1)} %b_ref.3) | copy-start | bytes 98308
  39.8 13.4 %copy-start.3 = (f32[128,32]{0,1:T(8,128)S(1)}, f32[128,32]{0,1:T(8,128)}, u32[]{:S(2)}) copy-start(f32[128,32]{0,1:T(8,128)} %param.19) | copy-start | bytes 49156
  39.8 13.4 %copy-start.4 = (f32[32]{0:T(128)S(1)}, f32[32]{0:T(128)}, u32[]{:S(2)}) copy-start(f32[32]{0:T(128)} %param.21) | copy-start | bytes 388
  39.8 13.4 %copy-start.5 = (f32[32]{0:T(128)S(1)}, f32[32]{0:T(128)}, u32[]{:S(2)}) copy-start(f32[32]{0:T(128)} %param.20) | copy-start | bytes 388
  39.8 25.0 %collective-permute-start.8 = (f32[128,16]{0,1:T(8,128)S(1)}, f32[128,16]{0,1:T(8,128)S(1)}, u32[]{:S(2)}, u32[]{:S(2)}) collective-permute-start(f32[128,16]{0,1:T(8,128)S(1)} %select_reduce_fusion.1), channel_id=1, source_target_pairs={{0,2},{1,3},{2,0},{3,1},{4,6},{5,7},{6,4},{7,5},{8,10},{9,11},{10,... | collective-permute-start | bytes 24584 | tf_op jit(solution)/shard_map/ppermute | solution.py:291
  41.7 15.1 %collective-permute-start.16 = (bf16[64,2048]{1,0:T(8,128)(2,1)}, bf16[64,2048]{1,0:T(8,128)(2,1)S(1)}, u32[]{:S(2)}, u32[]{:S(2)}) collective-permute-start(bf16[64,2048]{1,0:T(8,128)(2,1)} %collective-permute-done.13), channel_id=1, source_target_pairs={{0,2},{1,3},{2,6},{3,7},{4,0},{5,1},{6,10},{7,11},{8,4},{9,5},{10,... | collective-permute-start | bytes 786440 | tf_op jit(solution)/shard_map/ppermute | solution.py:291
  45.0 13.5 %collective-permute-start.18 = (bf16[64,2048]{1,0:T(8,128)(2,1)}, bf16[64,2048]{1,0:T(8,128)(2,1)S(1)}, u32[]{:S(2)}, u32[]{:S(2)}) collective-permute-start(bf16[64,2048]{1,0:T(8,128)(2,1)} %collective-permute-done.15), channel_id=1, source_target_pairs={{0,4},{1,5},{2,0},{3,1},{4,8},{5,9},{6,2},{7,3},{8,12},{9,13},{10,... | collective-permute-start | bytes 786440 | tf_op jit(solution)/shard_map/ppermute | solution.py:291
  50.6 9.7 %collective-permute-start.19 = (bf16[64,2048]{1,0:T(8,128)(2,1)}, bf16[64,2048]{1,0:T(8,128)(2,1)S(1)}, u32[]{:S(2)}, u32[]{:S(2)}) collective-permute-start(bf16[64,2048]{1,0:T(8,128)(2,1)} %collective-permute-done.17), channel_id=1, source_target_pairs={{0,4},{1,5},{2,0},{3,1},{4,8},{5,9},{6,2},{7,3},{8,12},{9,13},{10,... | collective-permute-start | bytes 786440 | tf_op jit(solution)/shard_map/ppermute | solution.py:291
  56.8 8.1 %collective-permute-start.5 = (bf16[64,2048]{1,0:T(8,128)(2,1)}, bf16[64,2048]{1,0:T(8,128)(2,1)S(1)}, u32[]{:S(2)}, u32[]{:S(2)}) collective-permute-start(bf16[64,2048]{1,0:T(8,128)(2,1)} %maximum_select_fusion.2), channel_id=1, source_target_pairs={{0,2},{1,3},{2,6},{3,7},{4,0},{5,1},{6,10},{7,11},{8,4},{9,5},{10,... | collective-permute-start | bytes 786440 | tf_op jit(solution)/shard_map/ppermute | solution.py:291
  58.6 23.0 %collective-permute-start.22 = (bf16[64,2048]{1,0:T(8,128)(2,1)S(1)}, bf16[64,2048]{1,0:T(8,128)(2,1)S(1)}, u32[]{:S(2)}, u32[]{:S(2)}) collective-permute-start(bf16[64,2048]{1,0:T(8,128)(2,1)S(1)} %collective-permute-done.16), channel_id=1, source_target_pairs={{0,2},{1,3},{2,6},{3,7},{4,0},{5,1},{6,10},{7,11},{8,4},{9,5},{10,... | collective-permute-start | bytes 786440 | tf_op jit(solution)/shard_map/ppermute | solution.py:291
  60.4 21.2 %collective-permute-start.23 = (bf16[64,2048]{1,0:T(8,128)(2,1)S(1)}, bf16[64,2048]{1,0:T(8,128)(2,1)S(1)}, u32[]{:S(2)}, u32[]{:S(2)}) collective-permute-start(bf16[64,2048]{1,0:T(8,128)(2,1)S(1)} %collective-permute-done.18), channel_id=1, source_target_pairs={{0,4},{1,5},{2,0},{3,1},{4,8},{5,9},{6,2},{7,3},{8,12},{9,13},{10,... | collective-permute-start | bytes 786440 | tf_op jit(solution)/shard_map/ppermute | solution.py:291
  60.6 25.4 %collective-permute-start.20 = (bf16[64,2048]{1,0:T(8,128)(2,1)S(1)}, bf16[64,2048]{1,0:T(8,128)(2,1)S(1)}, u32[]{:S(2)}, u32[]{:S(2)}) collective-permute-start(bf16[64,2048]{1,0:T(8,128)(2,1)S(1)} %collective-permute-done.19), channel_id=1, source_target_pairs={{0,4},{1,5},{2,0},{3,1},{4,8},{5,9},{6,2},{7,3},{8,12},{9,13},{10,... | collective-permute-start | bytes 786440 | tf_op jit(solution)/shard_map/ppermute | solution.py:291
  64.9 7.5 %collective-permute-start.9 = (f32[2,1,128,16]{2,3,1,0:T(8,128)S(1)}, f32[2,1,128,16]{2,3,1,0:T(8,128)S(1)}, u32[]{:S(2)}, u32[]{:S(2)}) collective-permute-start(f32[2,1,128,16]{2,3,1,0:T(8,128)S(1)} %maximum_select_fusion.5), channel_id=1, source_target_pairs={{0,4},{1,5},{2,6},{3,7},{4,0},{5,1},{6,2},{7,3},{8,12},{9,13},{10,... | collective-permute-start | bytes 49160 | tf_op jit(solution)/shard_map/ppermute | solution.py:291
  67.1 6.5 %collective-permute-start.10 = (bf16[64,2048]{1,0:T(8,128)(2,1)S(1)}, bf16[64,2048]{1,0:T(8,128)(2,1)S(1)}, u32[]{:S(2)}, u32[]{:S(2)}) collective-permute-start(bf16[64,2048]{1,0:T(8,128)(2,1)S(1)} %collective-permute-done.5), channel_id=1, source_target_pairs={{0,2},{1,3},{2,6},{3,7},{4,0},{5,1},{6,10},{7,11},{8,4},{9,5},{10,... | collective-permute-start | bytes 786440 | tf_op jit(solution)/shard_map/ppermute | solution.py:291
  73.6 7.7 %collective-permute-start.12 = (bf16[64,2048]{1,0:T(8,128)(2,1)S(1)}, bf16[64,2048]{1,0:T(8,128)(2,1)S(1)}, u32[]{:S(2)}, u32[]{:S(2)}) collective-permute-start(bf16[64,2048]{1,0:T(8,128)(2,1)S(1)} %collective-permute-done.10), channel_id=1, source_target_pairs={{0,2},{1,3},{2,6},{3,7},{4,0},{5,1},{6,10},{7,11},{8,4},{9,5},{10,... | collective-permute-start | bytes 786440 | tf_op jit(solution)/shard_map/ppermute | solution.py:291
  74.5 6.8 %collective-permute-start.11 = (f32[2,2,128,16]{2,3,1,0:T(8,128)S(1)}, f32[2,2,128,16]{2,3,1,0:T(8,128)S(1)}, u32[]{:S(2)}, u32[]{:S(2)}) collective-permute-start(f32[2,2,128,16]{2,3,1,0:T(8,128)S(1)} %maximum_select_fusion.4), channel_id=1, source_target_pairs={{0,8},{1,9},{2,10},{3,11},{4,12},{5,13},{6,14},{7,15},{8,0},{9,1},... | collective-permute-start | bytes 98312 | tf_op jit(solution)/shard_map/ppermute | solution.py:291
  84.8 6.4 %collective-permute-start.21 = (bf16[64,2048]{1,0:T(8,128)(2,1)S(1)}, bf16[64,2048]{1,0:T(8,128)(2,1)S(1)}, u32[]{:S(2)}, u32[]{:S(2)}) collective-permute-start(bf16[64,2048]{1,0:T(8,128)(2,1)S(1)} %collective-permute-done.12), channel_id=1, source_target_pairs={{0,2},{1,3},{2,6},{3,7},{4,0},{5,1},{6,10},{7,11},{8,4},{9,5},{10,... | collective-permute-start | bytes 786440 | tf_op jit(solution)/shard_map/ppermute | solution.py:291
  93.0 9.1 %collective-permute-start.24 = (bf16[64,2048]{1,0:T(8,128)(2,1)S(1)}, bf16[64,2048]{1,0:T(8,128)(2,1)S(1)}, u32[]{:S(2)}, u32[]{:S(2)}) collective-permute-start(bf16[64,2048]{1,0:T(8,128)(2,1)S(1)} %get-tuple-element.66), channel_id=1, source_target_pairs={{0,4},{1,5},{2,0},{3,1},{4,8},{5,9},{6,2},{7,3},{8,12},{9,13},{10,... | collective-permute-start | bytes 786440 | tf_op jit(solution)/shard_map/ppermute | solution.py:291
  95.9 8.8 %collective-permute-start.34 = (bf16[64,2048]{1,0:T(8,128)(2,1)S(1)}, bf16[64,2048]{1,0:T(8,128)(2,1)S(1)}, u32[]{:S(2)}, u32[]{:S(2)}) collective-permute-start(bf16[64,2048]{1,0:T(8,128)(2,1)S(1)} %get-tuple-element.67), channel_id=1, source_target_pairs={{0,2},{1,3},{2,6},{3,7},{4,0},{5,1},{6,10},{7,11},{8,4},{9,5},{10,... | collective-permute-start | bytes 786440 | tf_op jit(solution)/shard_map/ppermute | solution.py:291
  96.3 11.2 %collective-permute-start.28 = (bf16[64,2048]{1,0:T(8,128)(2,1)S(1)}, bf16[64,2048]{1,0:T(8,128)(2,1)S(1)}, u32[]{:S(2)}, u32[]{:S(2)}) collective-permute-start(bf16[64,2048]{1,0:T(8,128)(2,1)S(1)} %get-tuple-element.40), channel_id=1, source_target_pairs={{0,2},{1,3},{2,6},{3,7},{4,0},{5,1},{6,10},{7,11},{8,4},{9,5},{10,... | collective-permute-start | bytes 786440 | tf_op jit(solution)/shard_map/ppermute | solution.py:291
  96.4 17.6 %collective-permute-start.31 = (bf16[64,2048]{1,0:T(8,128)(2,1)S(1)}, bf16[64,2048]{1,0:T(8,128)(2,1)S(1)}, u32[]{:S(2)}, u32[]{:S(2)}) collective-permute-start(bf16[64,2048]{1,0:T(8,128)(2,1)S(1)} %get-tuple-element.41), channel_id=1, source_target_pairs={{0,4},{1,5},{2,0},{3,1},{4,8},{5,9},{6,2},{7,3},{8,12},{9,13},{10,... | collective-permute-start | bytes 786440 | tf_op jit(solution)/shard_map/ppermute | solution.py:291
  102.1 8.8 %collective-permute-start.25 = (bf16[64,2048]{1,0:T(8,128)(2,1)S(1)}, bf16[64,2048]{1,0:T(8,128)(2,1)S(1)}, u32[]{:S(2)}, u32[]{:S(2)}) collective-permute-start(bf16[64,2048]{1,0:T(8,128)(2,1)S(1)} %add_convert_fusion.1), channel_id=1, source_target_pairs={{0,4},{1,5},{2,0},{3,1},{4,8},{5,9},{6,2},{7,3},{8,12},{9,13},{10,... | collective-permute-start | bytes 786440 | tf_op jit(solution)/shard_map/ppermute | solution.py:291
  104.8 9.2 %collective-permute-start.35 = (bf16[64,2048]{1,0:T(8,128)(2,1)S(1)}, bf16[64,2048]{1,0:T(8,128)(2,1)S(1)}, u32[]{:S(2)}, u32[]{:S(2)}) collective-permute-start(bf16[64,2048]{1,0:T(8,128)(2,1)S(1)} %add_convert_fusion), channel_id=1, source_target_pairs={{0,2},{1,3},{2,6},{3,7},{4,0},{5,1},{6,10},{7,11},{8,4},{9,5},{10,... | collective-permute-start | bytes 786440 | tf_op jit(solution)/shard_map/ppermute | solution.py:291
  111.1 8.8 %collective-permute-start.26 = (bf16[64,2048]{1,0:T(8,128)(2,1)S(1)}, bf16[64,2048]{1,0:T(8,128)(2,1)S(1)}, u32[]{:S(2)}, u32[]{:S(2)}) collective-permute-start(bf16[64,2048]{1,0:T(8,128)(2,1)S(1)} %get-tuple-element.59), channel_id=1, source_target_pairs={{0,4},{1,5},{2,0},{3,1},{4,8},{5,9},{6,2},{7,3},{8,12},{9,13},{10,... | collective-permute-start | bytes 786440 | tf_op jit(solution)/shard_map/ppermute | solution.py:291
  113.2 9.2 %collective-permute-start.29 = (bf16[64,2048]{1,0:T(8,128)(2,1)S(1)}, bf16[64,2048]{1,0:T(8,128)(2,1)S(1)}, u32[]{:S(2)}, u32[]{:S(2)}) collective-permute-start(bf16[64,2048]{1,0:T(8,128)(2,1)S(1)} %get-tuple-element.58), channel_id=1, source_target_pairs={{0,2},{1,3},{2,6},{3,7},{4,0},{5,1},{6,10},{7,11},{8,4},{9,5},{10,... | collective-permute-start | bytes 786440 | tf_op jit(solution)/shard_map/ppermute | solution.py:291
  114.2 13.7 %collective-permute-start.36 = (bf16[64,2048]{1,0:T(8,128)(2,1)S(1)}, bf16[64,2048]{1,0:T(8,128)(2,1)S(1)}, u32[]{:S(2)}, u32[]{:S(2)}) collective-permute-start(bf16[64,2048]{1,0:T(8,128)(2,1)S(1)} %get-tuple-element.55), channel_id=1, source_target_pairs={{0,2},{1,3},{2,6},{3,7},{4,0},{5,1},{6,10},{7,11},{8,4},{9,5},{10,... | collective-permute-start | bytes 786440 | tf_op jit(solution)/shard_map/ppermute | solution.py:291
  114.5 13.4 %collective-permute-start.32 = (bf16[64,2048]{1,0:T(8,128)(2,1)S(1)}, bf16[64,2048]{1,0:T(8,128)(2,1)S(1)}, u32[]{:S(2)}, u32[]{:S(2)}) collective-permute-start(bf16[64,2048]{1,0:T(8,128)(2,1)S(1)} %get-tuple-element.54), channel_id=1, source_target_pairs={{0,4},{1,5},{2,0},{3,1},{4,8},{5,9},{6,2},{7,3},{8,12},{9,13},{10,... | collective-permute-start | bytes 786440 | tf_op jit(solution)/shard_map/ppermute | solution.py:291
  122.5 12.2 %collective-permute-start.27 = (bf16[64,2048]{1,0:T(8,128)(2,1)S(1)}, bf16[64,2048]{1,0:T(8,128)(2,1)S(1)}, u32[]{:S(2)}, u32[]{:S(2)}) collective-permute-start(bf16[64,2048]{1,0:T(8,128)(2,1)S(1)} %get-tuple-element.57), channel_id=1, source_target_pairs={{0,4},{1,5},{2,0},{3,1},{4,8},{5,9},{6,2},{7,3},{8,12},{9,13},{10,... | collective-permute-start | bytes 786440 | tf_op jit(solution)/shard_map/ppermute | solution.py:291
  122.6 12.0 %collective-permute-start.30 = (bf16[64,2048]{1,0:T(8,128)(2,1)S(1)}, bf16[64,2048]{1,0:T(8,128)(2,1)S(1)}, u32[]{:S(2)}, u32[]{:S(2)}) collective-permute-start(bf16[64,2048]{1,0:T(8,128)(2,1)S(1)} %get-tuple-element.56), channel_id=1, source_target_pairs={{0,2},{1,3},{2,6},{3,7},{4,0},{5,1},{6,10},{7,11},{8,4},{9,5},{10,... | collective-permute-start | bytes 786440 | tf_op jit(solution)/shard_map/ppermute | solution.py:291
  128.0 6.4 %collective-permute-start.33 = (bf16[64,2048]{1,0:T(8,128)(2,1)S(1)}, bf16[64,2048]{1,0:T(8,128)(2,1)S(1)}, u32[]{:S(2)}, u32[]{:S(2)}) collective-permute-start(bf16[64,2048]{1,0:T(8,128)(2,1)S(1)} %get-tuple-element.52), channel_id=1, source_target_pairs={{0,4},{1,5},{2,0},{3,1},{4,8},{5,9},{6,2},{7,3},{8,12},{9,13},{10,... | collective-permute-start | bytes 786440 | tf_op jit(solution)/shard_map/ppermute | solution.py:291
  128.3 6.4 %collective-permute-start.37 = (bf16[64,2048]{1,0:T(8,128)(2,1)S(1)}, bf16[64,2048]{1,0:T(8,128)(2,1)S(1)}, u32[]{:S(2)}, u32[]{:S(2)}) collective-permute-start(bf16[64,2048]{1,0:T(8,128)(2,1)S(1)} %get-tuple-element.53), channel_id=1, source_target_pairs={{0,2},{1,3},{2,6},{3,7},{4,0},{5,1},{6,10},{7,11},{8,4},{9,5},{10,... | collective-permute-start | bytes 786440 | tf_op jit(solution)/shard_map/ppermute | solution.py:291

commit v7 on v6

--- a/solution.py
+++ b/solution.py
@@ -259,7 +259,7 @@
             expert_out[0],
             route_ids,
             route_weights,
-            lambda after: state_next(lax.optimization_barrier((ssm_input, after))[0]),
+            lambda tie: state_next(after(ssm_input, tie)),
         )
     else:
         normed = jnp.concatenate(normed)
@@ -278,6 +278,10 @@
     return pairs
 
 
+def after(value, *others):
+    return lax.optimization_barrier((value, *others))[0]
+
+
 def dense_experts(normed, out_proj, expert_in, expert_out, route_ids, route_weights, state_next):
     frames = route_ids.shape[0]
     wide = lax.axis_size("wide")
@@ -321,21 +325,36 @@
         return jnp.dot(rows, columns, preferred_element_type=jnp.float32).astype(jnp.bfloat16)
 
     own = [project(normed[h]) for h in halves]
-    rows, backs = [], []
+    rows, peer = [], None
     for h in halves:
-        backs.append(to_x(project(sent[h])))
-        here = own[h]
+        arrived = sent[h]
+        if peer is not None:
+            arrived = after(arrived, peer)
+        peer = project(arrived)
+        back = to_x(peer)
         rows.append(
             jnp.where(
                 x == 0,
-                jnp.concatenate([here, backs[h]], axis=1),
-                jnp.concatenate([backs[h], here], axis=1),
+                jnp.concatenate([own[h], back], axis=1),
+                jnp.concatenate([back, own[h]], axis=1),
             )
         )
 
     far = ring // 2
     hidden_width = expert_out.shape[0]
     is_first = jnp.arange(2 * hidden_width)[None, :] < hidden_width
+
+    def join(in_other, down_other):
+        joined_in = jnp.concatenate(
+            [
+                expert_in[:, :hidden_width],
+                in_other[:, :hidden_width],
+                expert_in[:, hidden_width:],
+                in_other[:, hidden_width:],
+            ],
+            axis=1,
+        )
+        return joined_in, jnp.concatenate([expert_out, down_other], axis=0)
 
     def run_experts(parts, gate):
         v = jnp.dot(jnp.concatenate(parts), joined_in, preferred_element_type=jnp.float32)
@@ -343,48 +362,41 @@
         hidden = (hidden * jnp.where(is_first, gate[:, :1], gate[:, 1:])).astype(jnp.bfloat16)
         return jnp.dot(hidden, joined_down, preferred_element_type=jnp.float32)
 
+    def merge(gates, other, low):
+        return jnp.where(
+            low, jnp.concatenate([gates, other], axis=1), jnp.concatenate([other, gates], axis=1)
+        )
+
     experts = wide * 4
     gates = jnp.sum(
         jnp.where(route_ids[:, :, None] == jnp.arange(experts), route_weights[:, :, None], 0.0), axis=1
     )
-    gates, _ = lax.optimization_barrier((gates, sent[1]))
-    other = to_x(gates)
-    step = 1
+    other = to_x(after(gates, sent[1]))
+    step = 0
     fore_at, back_at = {0: rows}, {0: rows}
     for k in range(1, far):
         fore_at[k] = [along(fore_at[k - 1][h], 1) for h in halves]
         back_at[k] = [along(back_at[k - 1][h], -1) for h in halves]
         if k == 1:
-            joined_in = jnp.concatenate(
-                [
-                    expert_in[:, :hidden_width],
-                    in_other[:, :hidden_width],
-                    expert_in[:, hidden_width:],
-                    in_other[:, hidden_width:],
-                ],
-                axis=1,
+            fore_at[k][0], back_at[k][0], in_other, down_other = lax.optimization_barrier(
+                (fore_at[k][0], back_at[k][0], in_other, down_other)
             )
-            joined_down = jnp.concatenate([expert_out, down_other], axis=0)
-            back_at[1][1], joined_in, joined_down, other = lax.optimization_barrier(
-                (back_at[1][1], joined_in, joined_down, other)
-            )
-            state = state_next(fore_at[1][0])
-            gates = jnp.where(x == 0, jnp.stack([gates, other]), jnp.stack([other, gates]))[:, None]
-        elif step < wide:
+            for way in (fore_at[k], back_at[k]):
+                way[1] = after(way[1], way[0])
+        if step < wide:
             other, back_at[k][1] = lax.optimization_barrier((other, back_at[k][1]))
-            low = z & step == 0
-            gates = jnp.where(
-                low, jnp.concatenate([gates, other], axis=1), jnp.concatenate([other, gates], axis=1)
-            )
-            step *= 2
-        if step < wide:
-            other = send(gates, lambda z, x, c: (z ^ step, x, c))
+            if step == 0:
+                gates = jnp.where(x == 0, jnp.stack([gates, other]), jnp.stack([other, gates]))
+                gates, step = gates[:, None], 1
+            else:
+                gates, step = merge(gates, other, z & step == 0), 2 * step
+            if step < wide:
+                other = send(gates, lambda z, x, c: (z ^ step, x, c))
+        if k == far - 1:
+            joined = join(in_other, down_other)
+            back_at[k][1], joined_in, joined_down = lax.optimization_barrier((back_at[k][1], *joined))
     while step < wide:
-        low = z & step == 0
-        gates = jnp.where(
-            low, jnp.concatenate([gates, other], axis=1), jnp.concatenate([other, gates], axis=1)
-        )
-        step *= 2
+        gates, step = merge(gates, other, z & step == 0), 2 * step
         if step < wide:
             other = send(gates, lambda z, x, c: (z ^ step, x, c))
     mine = (z * 2 + x) * 2 + core
@@ -396,49 +408,44 @@
     gates = lax.dynamic_slice_in_dim(jnp.concatenate([gates, gates]), place, ring, 0)
     last = [along(fore_at[far - 1][0], 1), along(back_at[far - 1][1], -1)]
 
-    def cut(total, at):
-        return [total[at + h * size : at + (h + 1) * size] for h in halves]
-
-    ahead, behind = {}, {}
-    ahead[0] = cut(run_experts(rows, gates[0]), 0)
-    for k in range(1, far):
-        total = run_experts(
-            [*back_at[k], *fore_at[k]], jnp.concatenate([gates[k], gates[ring - k]])
-        )
-        ahead[k], behind[k] = cut(total, 0), cut(total, frames)
-    last[0], last[1], state, *near = lax.optimization_barrier(
-        (last[0], last[1], state, *ahead[far - 1], *behind[far - 1])
-    )
-    ahead[far - 1], behind[far - 1] = near[:2], near[2:]
+    def hop_experts(k, tie):
+        parts = rows if k == 0 else [*back_at[k], *fore_at[k]]
+        gate = gates[0] if k == 0 else jnp.concatenate([gates[k], gates[ring - k]])
+        if tie is not None:
+            parts = [after(part, tie) for part in parts]
+        total = run_experts(parts, gate)
+        cut = [total[i * size : (i + 1) * size] for i in range(len(parts))]
+        return cut[:2], cut[2:]
+
+    ahead, behind = hop_experts(far - 1, None)
+    last[0], last[1], *near = lax.optimization_barrier((*last, *ahead, *behind))
+    ahead, behind = near[:2], near[2:]
     total = run_experts(last, gates[far]).astype(jnp.bfloat16)
-
     fore, back = [along(total[:size], 1), None], [None, along(total[size:], -1)]
+    tie = total
     for k in range(far - 1, 0, -1):
-        before = None
-        for h in halves if k < far - 1 else (None,):
-            todo = ((fore, 1, ahead, h), (back, -1, behind, h))
-            if h is None:
-                todo = (
-                    (fore, 1, ahead, 1),
-                    (back, -1, behind, 0),
-                    (fore, 1, ahead, 0),
-                    (back, -1, behind, 1),
-                )
+        coming = hop_experts(k - 1, tie)
+        if k == 1:
+            state = state_next(tie)
+        before = ()
+        groups = [((fore, 1, ahead, h), (back, -1, behind, h)) for h in halves]
+        if k == far - 1:
+            groups = [((fore, 1, ahead, 1), (back, -1, behind, 0)), ((fore, 1, ahead, 0), (back, -1, behind, 1))]
+        for group in groups:
             loads = []
-            for way, step, totals, at in todo:
-                load = totals[k][at]
-                if way[at] is not None:
-                    got = way[at]
-                    if before is not None:
-                        got = lax.optimization_barrier((got, *before))[0]
-                    load = load + got.astype(jnp.float32)
+            for way, step, totals, h in group:
+                load = totals[h]
+                if way[h] is not None:
+                    load = load + after(way[h], *before).astype(jnp.float32)
                 loads.append(load.astype(jnp.bfloat16))
             before = loads
-            for (way, step, totals, at), load in zip(todo, loads):
-                way[at] = along(load, step)
+            for (way, step, totals, h), load in zip(group, loads):
+                way[h] = along(load, step)
+        tie = loads[0]
+        ahead, behind = coming
     out = []
     for h in halves:
-        total = ahead[0][h] + fore[h].astype(jnp.float32) + back[h].astype(jnp.float32)
+        total = ahead[h] + fore[h].astype(jnp.float32) + back[h].astype(jnp.float32)
         out.append((rows[h].astype(jnp.float32) + total).astype(jnp.bfloat16))
     return jnp.concatenate(out), state
 

time: 137 us -> 131 us (0.956)
  waiting for transfers between devices: 52.5 us -> 45.8 us
  starting transfers between devices: 37.5 us -> 40.4 us
  other arithmetic: 12.1 us -> 10.3 us
    ppermute x38, waiting for transfers between devices: 52.5 us -> 45.8 us  [send(): return lax.ppermute(value, axes, routes(wide, move))]
    ppermute x38, starting transfers between devices: 37.5 us -> 40.4 us  [send(): return lax.ppermute(value, axes, routes(wide, move))]
    select_n x1, other arithmetic: 5.23 us -> 3.57 us  [dense_experts(): jnp.where(core == 0, jnp.concatenate([out_proj, out_other], axis=1), jnp....]
  transfers between devices with their start and end apart: 38 -> 38, of which waited for: 18 -> 19; matrix products, arithmetic and copies ran while one was open for 24% -> 23% of each run, Pallas kernels for 7% -> 7%
where the time goes in v7:
time: 131 us
  waiting for transfers between devices  45.8 us (35%)
  starting transfers between devices  40.4 us (31%)
  matrix products  18.9 us (14%)
  other arithmetic  10.3 us (8%)
  Pallas kernels  8.93 us (7%)
  local copies, waits for them, and re-layouts  4.98 us (4%)
    ppermute x38, waiting for transfers between devices, send(): return lax.ppermute(value, axes, routes(wide, move))  45.8 us
    ppermute x38, starting transfers between devices, send(): return lax.ppermute(value, axes, routes(wide, move))  40.4 us
    dot_general x5, matrix products, run_experts(): jnp.dot(jnp.concatenate(parts), joined_in, preferred_element_type=jnp.flo...  9.55 us
    pallas_call x1, Pallas kernels, ssm_mixer(): pl.pallas_call(mixer_kernel, grid=(steps,), in_specs=[pl.BlockSpec(memory...  5.36 us
    dot_general x5, matrix products, run_experts(): return jnp.dot(hidden, joined_down, preferred_element_type=jnp.float32)  5.03 us
    dot_general x4, matrix products, project(): jnp.dot(rows, columns, preferred_element_type=jnp.float32)  4.37 us
    pallas_call x1, Pallas kernels, state_next(): pl.pallas_call(state_kernel, grid=(steps,), in_specs=[column, whole, per_...  3.57 us
    select_n x1, other arithmetic, dense_experts(): jnp.where(core == 0, jnp.concatenate([out_proj, out_other], axis=1), jnp....  3.57 us
  transfers between devices with their start and end apart: 38, of which 19 were waited for; matrix products, arithmetic and copies ran while one was open for 23% of the time, Pallas kernels for 7%

profile of v7, /device:TPU:0, one launch (start us, length us, event | category | flops | bytes accessed | tf_op | source)
XLA Modules:
  0.0 130.5 jit_solution(15396467403050562939)
XLA Ops:
  1.1 5.4 %mixer.1 = (bf16[64,2048]{1,0:T(8,128)(2,1)}, bf16[64,2048]{1,0:T(8,128)(2,1)}) custom-call(f32[32]{0:T(128)} %skip_ref.1, bf16[128,2048]{1,0:T(8,128)(2,1)} %x_ref.2, bf16[128,2048]{1,0:T(8,128)(2,1)} %z_ref.1, bf16[128,128]{1,0:T(8,128)(2,1)} %b_ref.3, bf16[128,128]{1,0:T(8,128)(2,1)} %c_ref.1, f32[32,128]{1,0:T(8,128)} %bitcast.66, f32[1,32]{1,0:T(1,128)} %bitcast.68, ...), custom_call_target="tpu_custom_call" | custom-call | flops 400000000 | bytes 6000000 | tf_op jit(solution)/shard_map/mixer/pallas_call | solution.py:159
  6.5 2.5 %collective-permute-start.11 = (bf16[64,2048]{1,0:T(8,128)(2,1)}, bf16[64,2048]{1,0:T(8,128)(2,1)S(1)}, u32[]{:S(2)}, u32[]{:S(2)}) collective-permute-start(bf16[64,2048]{1,0:T(8,128)(2,1)} %get-tuple-element.47), channel_id=1, source_target_pairs={{0,2},{1,3},{2,0},{3,1},{4,6},{5,7},{6,4},{7,5},{8,10},{9,11},{10,... | collective-permute-start | bytes 786440 | tf_op jit(solution)/shard_map/ppermute | solution.py:295
  9.7 2.3 %fusion.101 = (bf16[2048,384]{1,0:T(8,128)(2,1)S(1)}, bf16[2048,384]{1,0:T(8,128)(2,1)S(1)}) fusion(bf16[2048,768]{1,0:T(8,128)(2,1)} %bitcast.5), kind=kLoop, calls=%fused_computation.160 | loop fusion | bytes 6291456 | tf_op jit(solution)/shard_map/slice | solution.py:350
  12.2 3.6 %maximum_select_fusion = bf16[2048,1024]{1,0:T(8,128)(2,1)S(1)} fusion(bf16[2048,512]{1,0:T(8,128)(2,1)} %collective-permute-done, bf16[2048,512]{1,0:T(8,128)(2,1)S(1)} %copy-done.6, pred[]{:T(512)S(6)} %eq.44), kind=kLoop, calls=%fused_computation.1 | loop fusion | flops 18874368 | bytes 8388609 | tf_op jit(solution)/shard_map/jit(_where)/select_n | solution.py:317
  16.7 5.2 %collective-permute-done.1 = bf16[64,2048]{1,0:T(8,128)(2,1)} collective-permute-done((bf16[64,2048]{1,0:T(8,128)(2,1)}, bf16[64,2048]{1,0:T(8,128)(2,1)}, u32[]{:S(2)}, u32[]{:S(2)}) %collective-permute-start.1) | collective-permute-done | bytes 262176 | tf_op jit(solution)/shard_map/ppermute | solution.py:295
  21.9 1.8 %convolution_convert_fusion.3 = bf16[64,1024]{1,0:T(8,128)(2,1)S(1)} fusion(bf16[64,2048]{1,0:T(8,128)(2,1)} %collective-permute-done.1, bf16[2048,1024]{1,0:T(8,128)(2,1)S(1)} %maximum_select_fusion), kind=kOutput, calls=%fused_computation.6 | convolution fusion | flops 268500992 | bytes 4587520 | tf_op jit(solution)/shard_map/dot_general | solution.py:325
  23.7 1.8 %collective-permute-start.2 = (bf16[64,1024]{1,0:T(8,128)(2,1)S(1)}, bf16[64,1024]{1,0:T(8,128)(2,1)S(1)}, u32[]{:S(2)}, u32[]{:S(2)}) collective-permute-start(bf16[64,1024]{1,0:T(8,128)(2,1)S(1)} %convolution_convert_fusion.3), channel_id=1, source_target_pairs={{0,2},{1,3},{2,0},{3,1},{4,6},{5,7},{6,4},{7,5},{8,10},{9,11},{10,... | collective-permute-start | bytes 393224 | tf_op jit(solution)/shard_map/ppermute | solution.py:295
  27.6 1.4 %collective-permute-done.2 = bf16[64,1024]{1,0:T(8,128)(2,1)S(1)} collective-permute-done((bf16[64,1024]{1,0:T(8,128)(2,1)S(1)}, bf16[64,1024]{1,0:T(8,128)(2,1)S(1)}, u32[]{:S(2)}, u32[]{:S(2)}) %collective-permute-start.2) | collective-permute-done | bytes 131104 | tf_op jit(solution)/shard_map/ppermute | solution.py:295
  29.2 1.7 %collective-permute-start.3 = (bf16[64,2048]{1,0:T(8,128)(2,1)S(1)}, bf16[64,2048]{1,0:T(8,128)(2,1)}, u32[]{:S(2)}, u32[]{:S(2)}) collective-permute-start(bf16[64,2048]{1,0:T(8,128)(2,1)S(1)} %maximum_select_fusion.1), channel_id=1, source_target_pairs={{0,4},{1,5},{2,0},{3,1},{4,8},{5,9},{6,2},{7,3},{8,12},{9,13},{10,... | collective-permute-start | bytes 786440 | tf_op jit(solution)/shard_map/ppermute | solution.py:295
  31.8 2.0 %collective-permute-done.13 = bf16[64,1024]{1,0:T(8,128)(2,1)S(1)} collective-permute-done((bf16[64,1024]{1,0:T(8,128)(2,1)S(1)}, bf16[64,1024]{1,0:T(8,128)(2,1)S(1)}, u32[]{:S(2)}, u32[]{:S(2)}) %collective-permute-start.13) | collective-permute-done | bytes 131104 | tf_op jit(solution)/shard_map/ppermute | solution.py:295
  36.1 2.0 %collective-permute-done.3 = bf16[64,2048]{1,0:T(8,128)(2,1)} collective-permute-done((bf16[64,2048]{1,0:T(8,128)(2,1)S(1)}, bf16[64,2048]{1,0:T(8,128)(2,1)}, u32[]{:S(2)}, u32[]{:S(2)}) %collective-permute-start.3) | collective-permute-done | bytes 262176 | tf_op jit(solution)/shard_map/ppermute | solution.py:295
  38.0 2.1 %collective-permute-done.4 = bf16[64,2048]{1,0:T(8,128)(2,1)} collective-permute-done((bf16[64,2048]{1,0:T(8,128)(2,1)S(1)}, bf16[64,2048]{1,0:T(8,128)(2,1)}, u32[]{:S(2)}, u32[]{:S(2)}) %collective-permute-start.4) | collective-permute-done | bytes 262176 | tf_op jit(solution)/shard_map/ppermute | solution.py:295
  41.1 4.7 %collective-permute-done.14 = bf16[64,2048]{1,0:T(8,128)(2,1)} collective-permute-done((bf16[64,2048]{1,0:T(8,128)(2,1)}, bf16[64,2048]{1,0:T(8,128)(2,1)}, u32[]{:S(2)}, u32[]{:S(2)}) %collective-permute-start.14) | collective-permute-done | bytes 262176 | tf_op jit(solution)/shard_map/ppermute | solution.py:295
  45.8 1.6 %collective-permute-start.15 = (f32[2,1,128,16]{2,3,1,0:T(8,128)S(1)}, f32[2,1,128,16]{2,3,1,0:T(8,128)S(1)}, u32[]{:S(2)}, u32[]{:S(2)}) collective-permute-start(f32[2,1,128,16]{2,3,1,0:T(8,128)S(1)} %maximum_select_fusion.5), channel_id=1, source_target_pairs={{0,4},{1,5},{2,6},{3,7},{4,0},{5,1},{6,2},{7,3},{8,12},{9,13},{10,... | collective-permute-start | bytes 49160 | tf_op jit(solution)/shard_map/ppermute | solution.py:295
  48.3 2.2 %fusion.102 = (bf16[2048,384]{1,0:T(8,128)(2,1)S(1)}, bf16[2048,384]{1,0:T(8,128)(2,1)S(1)}) fusion(bf16[2048,768]{1,0:T(8,128)(2,1)} %collective-permute-done.5), kind=kLoop, calls=%fused_computation.161 | loop fusion | bytes 6291456 | tf_op jit(solution)/shard_map/slice | solution.py:351
  50.5 1.2 collective-permute-start.8
  51.7 1.8 %collective-permute-start.22 = (bf16[64,2048]{1,0:T(8,128)(2,1)S(1)}, bf16[64,2048]{1,0:T(8,128)(2,1)S(1)}, u32[]{:S(2)}, u32[]{:S(2)}) collective-permute-start(bf16[64,2048]{1,0:T(8,128)(2,1)S(1)} %collective-permute-done.21), channel_id=1, source_target_pairs={{0,4},{1,5},{2,0},{3,1},{4,8},{5,9},{6,2},{7,3},{8,12},{9,13},{10,... | collective-permute-start | bytes 786440 | tf_op jit(solution)/shard_map/ppermute | solution.py:295
  54.8 2.6 %collective-permute-start.17 = (f32[2,2,128,16]{2,3,1,0:T(8,128)S(1)}, f32[2,2,128,16]{2,3,1,0:T(8,128)S(1)}, u32[]{:S(2)}, u32[]{:S(2)}) collective-permute-start(f32[2,2,128,16]{2,3,1,0:T(8,128)S(1)} %maximum_select_fusion.4), channel_id=1, source_target_pairs={{0,8},{1,9},{2,10},{3,11},{4,12},{5,13},{6,14},{7,15},{8,0},{9,1},... | collective-permute-start | bytes 98312 | tf_op jit(solution)/shard_map/ppermute | solution.py:295
  57.8 2.2 %pad_maximum_fusion.1 = bf16[768,2048]{1,0:T(8,128)(2,1)S(1)} fusion(bf16[384,2048]{1,0:T(8,128)(2,1)} %collective-permute-done.6, bf16[384,2048]{1,0:T(8,128)(2,1)} %bitcast.6), kind=kLoop, calls=%fused_computation.2 | loop fusion | flops 6291456 | bytes 6291456 | tf_op jit(solution)/shard_map/concatenate | solution.py:357
  60.0 1.6 %collective-permute-start.9 = (bf16[64,2048]{1,0:T(8,128)(2,1)S(1)}, bf16[64,2048]{1,0:T(8,128)(2,1)S(1)}, u32[]{:S(2)}, u32[]{:S(2)}) collective-permute-start(bf16[64,2048]{1,0:T(8,128)(2,1)S(1)} %collective-permute-done.8), channel_id=1, source_target_pairs={{0,4},{1,5},{2,0},{3,1},{4,8},{5,9},{6,2},{7,3},{8,12},{9,13},{10,... | collective-permute-start | bytes 786440 | tf_op jit(solution)/shard_map/ppermute | solution.py:295
  61.7 1.8 %collective-permute-start.23 = (bf16[64,2048]{1,0:T(8,128)(2,1)S(1)}, bf16[64,2048]{1,0:T(8,128)(2,1)S(1)}, u32[]{:S(2)}, u32[]{:S(2)}) collective-permute-start(bf16[64,2048]{1,0:T(8,128)(2,1)S(1)} %collective-permute-done.22), channel_id=1, source_target_pairs={{0,4},{1,5},{2,0},{3,1},{4,8},{5,9},{6,2},{7,3},{8,12},{9,13},{10,... | collective-permute-start | bytes 786440 | tf_op jit(solution)/shard_map/ppermute | solution.py:295
  63.7 1.4 %collective-permute-done.18 = bf16[64,2048]{1,0:T(8,128)(2,1)S(1)} collective-permute-done((bf16[64,2048]{1,0:T(8,128)(2,1)S(1)}, bf16[64,2048]{1,0:T(8,128)(2,1)S(1)}, u32[]{:S(2)}, u32[]{:S(2)}) %collective-permute-start.18) | collective-permute-done | bytes 262176 | tf_op jit(solution)/shard_map/ppermute | solution.py:295
  66.1 2.6 %collective-permute-done.9 = bf16[64,2048]{1,0:T(8,128)(2,1)S(1)} collective-permute-done((bf16[64,2048]{1,0:T(8,128)(2,1)S(1)}, bf16[64,2048]{1,0:T(8,128)(2,1)S(1)}, u32[]{:S(2)}, u32[]{:S(2)}) %collective-permute-start.9) | collective-permute-done | bytes 262176 | tf_op jit(solution)/shard_map/ppermute | solution.py:295
  68.7 2.8 %collective-permute-done.23 = bf16[64,2048]{1,0:T(8,128)(2,1)S(1)} collective-permute-done((bf16[64,2048]{1,0:T(8,128)(2,1)S(1)}, bf16[64,2048]{1,0:T(8,128)(2,1)S(1)}, u32[]{:S(2)}, u32[]{:S(2)}) %collective-permute-start.23) | collective-permute-done | bytes 262176 | tf_op jit(solution)/shard_map/ppermute | solution.py:295
  72.1 1.8 %fusion = f32[256,1536]{1,0:T(8,128)S(1)} fusion(bf16[2048,1536]{1,0:T(8,128)(2,1)S(1)} %pad_maximum_fusion, bf16[64,2048]{1,0:T(8,128)(2,1)S(1)} %collective-permute-done.23, bf16[64,2048]{1,0:T(8,128)(2,1)S(1)} %collective-permute-done.9, bf16[64,2048]{1,0:T(8,128)(2,1)S(1)} %collective-permute-done.18, bf16[64,2048]{1,0:T(8,128)(2,1)S(1)} %collective-permute-done.20), kind=kOutput, calls=%fused_computation.8 | convolution fusion | flops 1614807040 | bytes 8912896 | tf_op jit(solution)/shard_map/dot_general | solution.py:360
  73.9 1.2 fusion.52
  75.3 1.8 %collective-permute-start.10 = (bf16[64,2048]{1,0:T(8,128)(2,1)S(1)}, bf16[64,2048]{1,0:T(8,128)(2,1)S(1)}, u32[]{:S(2)}, u32[]{:S(2)}) collective-permute-start(bf16[64,2048]{1,0:T(8,128)(2,1)S(1)} %collective-permute-done.9), channel_id=1, source_target_pairs={{0,4},{1,5},{2,0},{3,1},{4,8},{5,9},{6,2},{7,3},{8,12},{9,13},{10,... | collective-permute-start | bytes 786440 | tf_op jit(solution)/shard_map/ppermute | solution.py:295
  77.1 4.6 %collective-permute-done.10 = bf16[64,2048]{1,0:T(8,128)(2,1)S(1)} collective-permute-done((bf16[64,2048]{1,0:T(8,128)(2,1)S(1)}, bf16[64,2048]{1,0:T(8,128)(2,1)S(1)}, u32[]{:S(2)}, u32[]{:S(2)}) %collective-permute-start.10) | collective-permute-done | bytes 262176 | tf_op jit(solution)/shard_map/ppermute | solution.py:295
  83.6 1.8 %collective-permute-start.34 = (bf16[64,2048]{1,0:T(8,128)(2,1)S(1)}, bf16[64,2048]{1,0:T(8,128)(2,1)S(1)}, u32[]{:S(2)}, u32[]{:S(2)}) collective-permute-start(bf16[64,2048]{1,0:T(8,128)(2,1)S(1)} %get-tuple-element.104), channel_id=1, source_target_pairs={{0,2},{1,3},{2,6},{3,7},{4,0},{5,1},{6,10},{7,11},{8,4},{9,5},{10,... | collective-permute-start | bytes 786440 | tf_op jit(solution)/shard_map/ppermute | solution.py:295
  85.4 1.7 %collective-permute-start.27 = (bf16[64,2048]{1,0:T(8,128)(2,1)S(1)}, bf16[64,2048]{1,0:T(8,128)(2,1)S(1)}, u32[]{:S(2)}, u32[]{:S(2)}) collective-permute-start(bf16[64,2048]{1,0:T(8,128)(2,1)S(1)} %get-tuple-element.71), channel_id=1, source_target_pairs={{0,2},{1,3},{2,6},{3,7},{4,0},{5,1},{6,10},{7,11},{8,4},{9,5},{10,... | collective-permute-start | bytes 786440 | tf_op jit(solution)/shard_map/ppermute | solution.py:295
  87.7 1.8 %fusion.8 = f32[256,1536]{1,0:T(8,128)S(1)} fusion(bf16[2048,1536]{1,0:T(8,128)(2,1)S(1)} %pad_maximum_fusion, bf16[64,2048]{1,0:T(8,128)(2,1)S(1)} %collective-permute-done.22, bf16[64,2048]{1,0:T(8,128)(2,1)S(1)} %collective-permute-done.8, bf16[64,2048]{1,0:T(8,128)(2,1)S(1)} %collective-permute-done.16, bf16[64,2048]{1,0:T(8,128)(2,1)S(1)} %collective-permute-done.7), kind=kOutput, calls=%fused_computation.16 | convolution fusion | flops 1614807040 | bytes 8912896 | tf_op jit(solution)/shard_map/dot_general | solution.py:360
  89.5 1.2 fusion.54
  90.7 5.7 %collective-permute-done.25 = bf16[64,2048]{1,0:T(8,128)(2,1)S(1)} collective-permute-done((bf16[64,2048]{1,0:T(8,128)(2,1)S(1)}, bf16[64,2048]{1,0:T(8,128)(2,1)S(1)}, u32[]{:S(2)}, u32[]{:S(2)}) %collective-permute-start.25) | collective-permute-done | bytes 262176 | tf_op jit(solution)/shard_map/ppermute | solution.py:295
  96.8 1.8 %collective-permute-start.35 = (bf16[64,2048]{1,0:T(8,128)(2,1)S(1)}, bf16[64,2048]{1,0:T(8,128)(2,1)S(1)}, u32[]{:S(2)}, u32[]{:S(2)}) collective-permute-start(bf16[64,2048]{1,0:T(8,128)(2,1)S(1)} %add_convert_fusion), channel_id=1, source_target_pairs={{0,2},{1,3},{2,6},{3,7},{4,0},{5,1},{6,10},{7,11},{8,4},{9,5},{10,... | collective-permute-start | bytes 786440 | tf_op jit(solution)/shard_map/ppermute | solution.py:295
  98.6 2.9 %fusion.16 = f32[256,1536]{1,0:T(8,128)S(1)} fusion(bf16[2048,1536]{1,0:T(8,128)(2,1)S(1)} %pad_maximum_fusion, bf16[64,2048]{1,0:T(8,128)(2,1)S(1)} %collective-permute-done.21, bf16[64,2048]{1,0:T(8,128)(2,1)} %collective-permute-done.3, bf16[64,2048]{1,0:T(8,128)(2,1)} %collective-permute-done.14, bf16[64,2048]{1,0:T(8,128)(2,1)} %collective-permute-done.4), kind=kOutput, calls=%fused_computation.24 | convolution fusion | flops 1614807040 | bytes 8912896 | tf_op jit(solution)/shard_map/dot_general | solution.py:360
  101.5 1.2 fusion.56
  102.8 1.4 %collective-permute-done.26 = bf16[64,2048]{1,0:T(8,128)(2,1)S(1)} collective-permute-done((bf16[64,2048]{1,0:T(8,128)(2,1)S(1)}, bf16[64,2048]{1,0:T(8,128)(2,1)S(1)}, u32[]{:S(2)}, u32[]{:S(2)}) %collective-permute-start.26) | collective-permute-done | bytes 262176 | tf_op jit(solution)/shard_map/ppermute | solution.py:295
  104.4 2.5 %collective-permute-start.30 = (bf16[64,2048]{1,0:T(8,128)(2,1)S(1)}, bf16[64,2048]{1,0:T(8,128)(2,1)S(1)}, u32[]{:S(2)}, u32[]{:S(2)}) collective-permute-start(bf16[64,2048]{1,0:T(8,128)(2,1)S(1)} %get-tuple-element.96), channel_id=1, source_target_pairs={{0,2},{1,3},{2,6},{3,7},{4,0},{5,1},{6,10},{7,11},{8,4},{9,5},{10,... | collective-permute-start | bytes 786440 | tf_op jit(solution)/shard_map/ppermute | solution.py:295
  107.7 1.3 collective-permute-start.36
  109.0 3.6 %state.1 = f32[2048,128]{1,0:T(8,128)} custom-call(bf16[128,2048]{1,0:T(8,128)(2,1)S(1)} %copy-done.1, bf16[128,128]{1,0:T(8,128)(2,1)S(1)} %copy-done.2, f32[32,128]{1,0:T(8,128)S(1)} %bitcast.67, f32[1,32]{1,0:T(1,128)S(1)} %bitcast.69, f32[1,32]{1,0:T(1,128)S(1)} %bitcast.71, f32[2048,128]{1,0:T(8,128)S(1)} %bitcast.65), custom_call_target="tpu_custom_call" | custom-call | flops 70000000 | bytes 3000000 | tf_op jit(solution)/shard_map/state/pallas_call | solution.py:198
  112.6 2.0 %fusion.48 = f32[128,1536]{1,0:T(8,128)S(1)} fusion(bf16[2048,1536]{1,0:T(8,128)(2,1)S(1)} %pad_maximum_fusion, bf16[64,2048]{1,0:T(8,128)(2,1)} %maximum_select_fusion.2, bf16[64,2048]{1,0:T(8,128)(2,1)S(1)} %maximum_select_fusion.1), kind=kOutput, calls=%fused_computation.69 | convolution fusion | flops 806354944 | bytes 7602176 | tf_op jit(solution)/shard_map/dot_general | solution.py:360
  114.9 1.8 %collective-permute-start.31 = (bf16[64,2048]{1,0:T(8,128)(2,1)S(1)}, bf16[64,2048]{1,0:T(8,128)(2,1)S(1)}, u32[]{:S(2)}, u32[]{:S(2)}) collective-permute-start(bf16[64,2048]{1,0:T(8,128)(2,1)S(1)} %get-tuple-element.92), channel_id=1, source_target_pairs={{0,2},{1,3},{2,6},{3,7},{4,0},{5,1},{6,10},{7,11},{8,4},{9,5},{10,... | collective-permute-start | bytes 786440 | tf_op jit(solution)/shard_map/ppermute | solution.py:295
  117.0 3.4 %collective-permute-done.32 = bf16[64,2048]{1,0:T(8,128)(2,1)S(1)} collective-permute-done((bf16[64,2048]{1,0:T(8,128)(2,1)S(1)}, bf16[64,2048]{1,0:T(8,128)(2,1)S(1)}, u32[]{:S(2)}, u32[]{:S(2)}) %collective-permute-start.32) | collective-permute-done | bytes 262176 | tf_op jit(solution)/shard_map/ppermute | solution.py:295
  120.6 2.0 %collective-permute-start.33 = (bf16[64,2048]{1,0:T(8,128)(2,1)S(1)}, bf16[64,2048]{1,0:T(8,128)(2,1)S(1)}, u32[]{:S(2)}, u32[]{:S(2)}) collective-permute-start(bf16[64,2048]{1,0:T(8,128)(2,1)S(1)} %get-tuple-element.90), channel_id=1, source_target_pairs={{0,4},{1,5},{2,0},{3,1},{4,8},{5,9},{6,2},{7,3},{8,12},{9,13},{10,... | collective-permute-start | bytes 786440 | tf_op jit(solution)/shard_map/ppermute | solution.py:295
  123.3 1.1 collective-permute-done.29
  124.5 2.5 %collective-permute-done.37 = bf16[64,2048]{1,0:T(8,128)(2,1)S(1)} collective-permute-done((bf16[64,2048]{1,0:T(8,128)(2,1)S(1)}, bf16[64,2048]{1,0:T(8,128)(2,1)S(1)}, u32[]{:S(2)}, u32[]{:S(2)}) %collective-permute-start.37) | collective-permute-done | bytes 262176 | tf_op jit(solution)/shard_map/ppermute | solution.py:295
  127.0 1.5 %collective-permute-done.33 = bf16[64,2048]{1,0:T(8,128)(2,1)S(1)} collective-permute-done((bf16[64,2048]{1,0:T(8,128)(2,1)S(1)}, bf16[64,2048]{1,0:T(8,128)(2,1)S(1)}, u32[]{:S(2)}, u32[]{:S(2)}) %collective-permute-start.33) | collective-permute-done | bytes 262176 | tf_op jit(solution)/shard_map/ppermute | solution.py:295
  128.5 1.2 fusion.40
  (99 shorter events, 19.1 us)
Async XLA Ops:
  0.6 11.4 %collective-permute-start = (bf16[2048,512]{1,0:T(8,128)(2,1)}, bf16[2048,512]{1,0:T(8,128)(2,1)}, u32[]{:S(2)}, u32[]{:S(2)}) collective-permute-start(bf16[2048,512]{1,0:T(8,128)(2,1)} %param.25), channel_id=1, source_target_pairs={{0,1},{1,0},{2,3},{3,2},{4,5},{5,4},{6,7},{7,6},{8,9},{9,8},{10,11... | collective-permute-start | bytes 6291464 | tf_op jit(solution)/shard_map/ppermute | solution.py:295
  6.5 19.1 %collective-permute-start.11 = (bf16[64,2048]{1,0:T(8,128)(2,1)}, bf16[64,2048]{1,0:T(8,128)(2,1)S(1)}, u32[]{:S(2)}, u32[]{:S(2)}) collective-permute-start(bf16[64,2048]{1,0:T(8,128)(2,1)} %get-tuple-element.47), channel_id=1, source_target_pairs={{0,2},{1,3},{2,0},{3,1},{4,6},{5,7},{6,4},{7,5},{8,10},{9,11},{10,... | collective-permute-start | bytes 786440 | tf_op jit(solution)/shard_map/ppermute | solution.py:295
  9.0 12.9 %collective-permute-start.1 = (bf16[64,2048]{1,0:T(8,128)(2,1)}, bf16[64,2048]{1,0:T(8,128)(2,1)}, u32[]{:S(2)}, u32[]{:S(2)}) collective-permute-start(bf16[64,2048]{1,0:T(8,128)(2,1)} %get-tuple-element.44), channel_id=1, source_target_pairs={{0,2},{1,3},{2,0},{3,1},{4,6},{5,7},{6,4},{7,5},{8,10},{9,11},{10,... | collective-permute-start | bytes 786440 | tf_op jit(solution)/shard_map/ppermute | solution.py:295
  9.1 31.1 %collective-permute-start.5 = (bf16[2048,768]{1,0:T(8,128)(2,1)}, bf16[2048,768]{1,0:T(8,128)(2,1)}, u32[]{:S(2)}, u32[]{:S(2)}) collective-permute-start(bf16[2048,768]{1,0:T(8,128)(2,1)} %bitcast.5), channel_id=1, source_target_pairs={{0,1},{1,0},{2,3},{3,2},{4,5},{5,4},{6,7},{7,6},{8,9},{9,8},{10,11... | collective-permute-start | bytes 9437192 | tf_op jit(solution)/shard_map/ppermute | solution.py:295
  9.3 26.0 %collective-permute-start.6 = (bf16[384,2048]{1,0:T(8,128)(2,1)}, bf16[384,2048]{1,0:T(8,128)(2,1)}, u32[]{:S(2)}, u32[]{:S(2)}) collective-permute-start(bf16[384,2048]{1,0:T(8,128)(2,1)} %bitcast.6), channel_id=1, source_target_pairs={{0,1},{1,0},{2,3},{3,2},{4,5},{5,4},{6,7},{7,6},{8,9},{9,8},{10,11... | collective-permute-start | bytes 4718600 | tf_op jit(solution)/shard_map/ppermute | solution.py:295
  12.0 3.8 %copy-start.8 = (bf16[64,2048]{1,0:T(8,128)(2,1)S(1)}, bf16[64,2048]{1,0:T(8,128)(2,1)}, u32[]{:S(2)}) copy-start(bf16[64,2048]{1,0:T(8,128)(2,1)} %get-tuple-element.47) | copy-start | bytes 786436
  16.7 8.9 %copy-start.7 = (bf16[64,2048]{1,0:T(8,128)(2,1)S(1)}, bf16[64,2048]{1,0:T(8,128)(2,1)}, u32[]{:S(2)}) copy-start(bf16[64,2048]{1,0:T(8,128)(2,1)} %get-tuple-element.44) | copy-start | bytes 786436
  23.7 5.4 %collective-permute-start.2 = (bf16[64,1024]{1,0:T(8,128)(2,1)S(1)}, bf16[64,1024]{1,0:T(8,128)(2,1)S(1)}, u32[]{:S(2)}, u32[]{:S(2)}) collective-permute-start(bf16[64,1024]{1,0:T(8,128)(2,1)S(1)} %convolution_convert_fusion.3), channel_id=1, source_target_pairs={{0,2},{1,3},{2,0},{3,1},{4,6},{5,7},{6,4},{7,5},{8,10},{9,11},{10,... | collective-permute-start | bytes 393224 | tf_op jit(solution)/shard_map/ppermute | solution.py:295
  26.4 8.8 %copy-start.9 = (f32[128,8]{0,1:T(8,128)S(1)}, f32[128,8]{0,1:T(8,128)}, u32[]{:S(2)}) copy-start(f32[128,8]{0,1:T(8,128)} %param.29) | copy-start | bytes 12292
  26.4 8.8 %copy-start.10 = (s32[128,8]{0,1:T(8,128)S(1)}, s32[128,8]{0,1:T(8,128)}, u32[]{:S(2)}) copy-start(s32[128,8]{0,1:T(8,128)} %param.28) | copy-start | bytes 12292
  27.3 6.4 %collective-permute-start.13 = (bf16[64,1024]{1,0:T(8,128)(2,1)S(1)}, bf16[64,1024]{1,0:T(8,128)(2,1)S(1)}, u32[]{:S(2)}, u32[]{:S(2)}) collective-permute-start(bf16[64,1024]{1,0:T(8,128)(2,1)S(1)} %convolution_convert_fusion.1), channel_id=1, source_target_pairs={{0,2},{1,3},{2,0},{3,1},{4,6},{5,7},{6,4},{7,5},{8,10},{9,11},{10,... | collective-permute-start | bytes 393224 | tf_op jit(solution)/shard_map/ppermute | solution.py:295
  29.2 8.9 %collective-permute-start.3 = (bf16[64,2048]{1,0:T(8,128)(2,1)S(1)}, bf16[64,2048]{1,0:T(8,128)(2,1)}, u32[]{:S(2)}, u32[]{:S(2)}) collective-permute-start(bf16[64,2048]{1,0:T(8,128)(2,1)S(1)} %maximum_select_fusion.1), channel_id=1, source_target_pairs={{0,4},{1,5},{2,0},{3,1},{4,8},{5,9},{6,2},{7,3},{8,12},{9,13},{10,... | collective-permute-start | bytes 786440 | tf_op jit(solution)/shard_map/ppermute | solution.py:295
  30.8 9.3 %collective-permute-start.4 = (bf16[64,2048]{1,0:T(8,128)(2,1)S(1)}, bf16[64,2048]{1,0:T(8,128)(2,1)}, u32[]{:S(2)}, u32[]{:S(2)}) collective-permute-start(bf16[64,2048]{1,0:T(8,128)(2,1)S(1)} %maximum_select_fusion.1), channel_id=1, source_target_pairs={{0,2},{1,3},{2,6},{3,7},{4,0},{5,1},{6,10},{7,11},{8,4},{9,5},{10,... | collective-permute-start | bytes 786440 | tf_op jit(solution)/shard_map/ppermute | solution.py:295
  34.5 11.3 %collective-permute-start.14 = (bf16[64,2048]{1,0:T(8,128)(2,1)}, bf16[64,2048]{1,0:T(8,128)(2,1)}, u32[]{:S(2)}, u32[]{:S(2)}) collective-permute-start(bf16[64,2048]{1,0:T(8,128)(2,1)} %maximum_select_fusion.2), channel_id=1, source_target_pairs={{0,2},{1,3},{2,6},{3,7},{4,0},{5,1},{6,10},{7,11},{8,4},{9,5},{10,... | collective-permute-start | bytes 786440 | tf_op jit(solution)/shard_map/ppermute | solution.py:295
  35.3 10.5 %collective-permute-start.12 = (f32[128,16]{0,1:T(8,128)S(1)}, f32[128,16]{0,1:T(8,128)S(1)}, u32[]{:S(2)}, u32[]{:S(2)}) collective-permute-start(f32[128,16]{0,1:T(8,128)S(1)} %select_reduce_fusion.1), channel_id=1, source_target_pairs={{0,2},{1,3},{2,0},{3,1},{4,6},{5,7},{6,4},{7,5},{8,10},{9,11},{10,... | collective-permute-start | bytes 24584 | tf_op jit(solution)/shard_map/ppermute | solution.py:295
  38.0 13.7 %collective-permute-start.21 = (bf16[64,2048]{1,0:T(8,128)(2,1)}, bf16[64,2048]{1,0:T(8,128)(2,1)S(1)}, u32[]{:S(2)}, u32[]{:S(2)}) collective-permute-start(bf16[64,2048]{1,0:T(8,128)(2,1)} %maximum_select_fusion.2), channel_id=1, source_target_pairs={{0,4},{1,5},{2,0},{3,1},{4,8},{5,9},{6,2},{7,3},{8,12},{9,13},{10,... | collective-permute-start | bytes 786440 | tf_op jit(solution)/shard_map/ppermute | solution.py:295
  40.2 23.3 %collective-permute-start.7 = (bf16[64,2048]{1,0:T(8,128)(2,1)}, bf16[64,2048]{1,0:T(8,128)(2,1)S(1)}, u32[]{:S(2)}, u32[]{:S(2)}) collective-permute-start(bf16[64,2048]{1,0:T(8,128)(2,1)} %collective-permute-done.4), channel_id=1, source_target_pairs={{0,2},{1,3},{2,6},{3,7},{4,0},{5,1},{6,10},{7,11},{8,4},{9,5},{10,... | collective-permute-start | bytes 786440 | tf_op jit(solution)/shard_map/ppermute | solution.py:295
  45.8 8.4 %collective-permute-start.15 = (f32[2,1,128,16]{2,3,1,0:T(8,128)S(1)}, f32[2,1,128,16]{2,3,1,0:T(8,128)S(1)}, u32[]{:S(2)}, u32[]{:S(2)}) collective-permute-start(f32[2,1,128,16]{2,3,1,0:T(8,128)S(1)} %maximum_select_fusion.5), channel_id=1, source_target_pairs={{0,4},{1,5},{2,6},{3,7},{4,0},{5,1},{6,2},{7,3},{8,12},{9,13},{10,... | collective-permute-start | bytes 49160 | tf_op jit(solution)/shard_map/ppermute | solution.py:295
  47.4 7.3 %collective-permute-start.16 = (bf16[64,2048]{1,0:T(8,128)(2,1)}, bf16[64,2048]{1,0:T(8,128)(2,1)S(1)}, u32[]{:S(2)}, u32[]{:S(2)}) collective-permute-start(bf16[64,2048]{1,0:T(8,128)(2,1)} %collective-permute-done.14), channel_id=1, source_target_pairs={{0,2},{1,3},{2,6},{3,7},{4,0},{5,1},{6,10},{7,11},{8,4},{9,5},{10,... | collective-permute-start | bytes 786440 | tf_op jit(solution)/shard_map/ppermute | solution.py:295
  50.5 9.6 %collective-permute-start.8 = (bf16[64,2048]{1,0:T(8,128)(2,1)}, bf16[64,2048]{1,0:T(8,128)(2,1)S(1)}, u32[]{:S(2)}, u32[]{:S(2)}) collective-permute-start(bf16[64,2048]{1,0:T(8,128)(2,1)} %collective-permute-done.3), channel_id=1, source_target_pairs={{0,4},{1,5},{2,0},{3,1},{4,8},{5,9},{6,2},{7,3},{8,12},{9,13},{10,... | collective-permute-start | bytes 786440 | tf_op jit(solution)/shard_map/ppermute | solution.py:295
  51.7 10.0 %collective-permute-start.22 = (bf16[64,2048]{1,0:T(8,128)(2,1)S(1)}, bf16[64,2048]{1,0:T(8,128)(2,1)S(1)}, u32[]{:S(2)}, u32[]{:S(2)}) collective-permute-start(bf16[64,2048]{1,0:T(8,128)(2,1)S(1)} %collective-permute-done.21), channel_id=1, source_target_pairs={{0,4},{1,5},{2,0},{3,1},{4,8},{5,9},{6,2},{7,3},{8,12},{9,13},{10,... | collective-permute-start | bytes 786440 | tf_op jit(solution)/shard_map/ppermute | solution.py:295
  54.8 9.0 %collective-permute-start.17 = (f32[2,2,128,16]{2,3,1,0:T(8,128)S(1)}, f32[2,2,128,16]{2,3,1,0:T(8,128)S(1)}, u32[]{:S(2)}, u32[]{:S(2)}) collective-permute-start(f32[2,2,128,16]{2,3,1,0:T(8,128)S(1)} %maximum_select_fusion.4), channel_id=1, source_target_pairs={{0,8},{1,9},{2,10},{3,11},{4,12},{5,13},{6,14},{7,15},{8,0},{9,1},... | collective-permute-start | bytes 98312 | tf_op jit(solution)/shard_map/ppermute | solution.py:295
  57.3 7.8 %collective-permute-start.18 = (bf16[64,2048]{1,0:T(8,128)(2,1)S(1)}, bf16[64,2048]{1,0:T(8,128)(2,1)S(1)}, u32[]{:S(2)}, u32[]{:S(2)}) collective-permute-start(bf16[64,2048]{1,0:T(8,128)(2,1)S(1)} %collective-permute-done.16), channel_id=1, source_target_pairs={{0,2},{1,3},{2,6},{3,7},{4,0},{5,1},{6,10},{7,11},{8,4},{9,5},{10,... | collective-permute-start | bytes 786440 | tf_op jit(solution)/shard_map/ppermute | solution.py:295
  60.0 8.7 %collective-permute-start.9 = (bf16[64,2048]{1,0:T(8,128)(2,1)S(1)}, bf16[64,2048]{1,0:T(8,128)(2,1)S(1)}, u32[]{:S(2)}, u32[]{:S(2)}) collective-permute-start(bf16[64,2048]{1,0:T(8,128)(2,1)S(1)} %collective-permute-done.8), channel_id=1, source_target_pairs={{0,4},{1,5},{2,0},{3,1},{4,8},{5,9},{6,2},{7,3},{8,12},{9,13},{10,... | collective-permute-start | bytes 786440 | tf_op jit(solution)/shard_map/ppermute | solution.py:295
  61.7 9.8 %collective-permute-start.23 = (bf16[64,2048]{1,0:T(8,128)(2,1)S(1)}, bf16[64,2048]{1,0:T(8,128)(2,1)S(1)}, u32[]{:S(2)}, u32[]{:S(2)}) collective-permute-start(bf16[64,2048]{1,0:T(8,128)(2,1)S(1)} %collective-permute-done.22), channel_id=1, source_target_pairs={{0,4},{1,5},{2,0},{3,1},{4,8},{5,9},{6,2},{7,3},{8,12},{9,13},{10,... | collective-permute-start | bytes 786440 | tf_op jit(solution)/shard_map/ppermute | solution.py:295
  63.5 8.6 %collective-permute-start.20 = (bf16[64,2048]{1,0:T(8,128)(2,1)S(1)}, bf16[64,2048]{1,0:T(8,128)(2,1)S(1)}, u32[]{:S(2)}, u32[]{:S(2)}) collective-permute-start(bf16[64,2048]{1,0:T(8,128)(2,1)S(1)} %collective-permute-done.7), channel_id=1, source_target_pairs={{0,2},{1,3},{2,6},{3,7},{4,0},{5,1},{6,10},{7,11},{8,4},{9,5},{10,... | collective-permute-start | bytes 786440 | tf_op jit(solution)/shard_map/ppermute | solution.py:295
  65.1 16.6 %collective-permute-start.19 = (bf16[64,2048]{1,0:T(8,128)(2,1)S(1)}, bf16[64,2048]{1,0:T(8,128)(2,1)S(1)}, u32[]{:S(2)}, u32[]{:S(2)}) collective-permute-start(bf16[64,2048]{1,0:T(8,128)(2,1)S(1)} %collective-permute-done.18), channel_id=1, source_target_pairs={{0,2},{1,3},{2,6},{3,7},{4,0},{5,1},{6,10},{7,11},{8,4},{9,5},{10,... | collective-permute-start | bytes 786440 | tf_op jit(solution)/shard_map/ppermute | solution.py:295
  75.3 6.4 %collective-permute-start.10 = (bf16[64,2048]{1,0:T(8,128)(2,1)S(1)}, bf16[64,2048]{1,0:T(8,128)(2,1)S(1)}, u32[]{:S(2)}, u32[]{:S(2)}) collective-permute-start(bf16[64,2048]{1,0:T(8,128)(2,1)S(1)} %collective-permute-done.9), channel_id=1, source_target_pairs={{0,4},{1,5},{2,0},{3,1},{4,8},{5,9},{6,2},{7,3},{8,12},{9,13},{10,... | collective-permute-start | bytes 786440 | tf_op jit(solution)/shard_map/ppermute | solution.py:295
  83.6 13.2 %collective-permute-start.34 = (bf16[64,2048]{1,0:T(8,128)(2,1)S(1)}, bf16[64,2048]{1,0:T(8,128)(2,1)S(1)}, u32[]{:S(2)}, u32[]{:S(2)}) collective-permute-start(bf16[64,2048]{1,0:T(8,128)(2,1)S(1)} %get-tuple-element.104), channel_id=1, source_target_pairs={{0,2},{1,3},{2,6},{3,7},{4,0},{5,1},{6,10},{7,11},{8,4},{9,5},{10,... | collective-permute-start | bytes 786440 | tf_op jit(solution)/shard_map/ppermute | solution.py:295
  85.4 16.1 %collective-permute-start.27 = (bf16[64,2048]{1,0:T(8,128)(2,1)S(1)}, bf16[64,2048]{1,0:T(8,128)(2,1)S(1)}, u32[]{:S(2)}, u32[]{:S(2)}) collective-permute-start(bf16[64,2048]{1,0:T(8,128)(2,1)S(1)} %get-tuple-element.71), channel_id=1, source_target_pairs={{0,2},{1,3},{2,6},{3,7},{4,0},{5,1},{6,10},{7,11},{8,4},{9,5},{10,... | collective-permute-start | bytes 786440 | tf_op jit(solution)/shard_map/ppermute | solution.py:295
  87.1 9.2 %collective-permute-start.25 = (bf16[64,2048]{1,0:T(8,128)(2,1)S(1)}, bf16[64,2048]{1,0:T(8,128)(2,1)S(1)}, u32[]{:S(2)}, u32[]{:S(2)}) collective-permute-start(bf16[64,2048]{1,0:T(8,128)(2,1)S(1)} %get-tuple-element.105), channel_id=1, source_target_pairs={{0,4},{1,5},{2,0},{3,1},{4,8},{5,9},{6,2},{7,3},{8,12},{9,13},{10,... | collective-permute-start | bytes 786440 | tf_op jit(solution)/shard_map/ppermute | solution.py:295
  87.4 16.9 %collective-permute-start.24 = (bf16[64,2048]{1,0:T(8,128)(2,1)S(1)}, bf16[64,2048]{1,0:T(8,128)(2,1)S(1)}, u32[]{:S(2)}, u32[]{:S(2)}) collective-permute-start(bf16[64,2048]{1,0:T(8,128)(2,1)S(1)} %get-tuple-element.69), channel_id=1, source_target_pairs={{0,4},{1,5},{2,0},{3,1},{4,8},{5,9},{6,2},{7,3},{8,12},{9,13},{10,... | collective-permute-start | bytes 786440 | tf_op jit(solution)/shard_map/ppermute | solution.py:295
  96.4 7.8 %collective-permute-start.26 = (bf16[64,2048]{1,0:T(8,128)(2,1)S(1)}, bf16[64,2048]{1,0:T(8,128)(2,1)S(1)}, u32[]{:S(2)}, u32[]{:S(2)}) collective-permute-start(bf16[64,2048]{1,0:T(8,128)(2,1)S(1)} %add_convert_fusion.1), channel_id=1, source_target_pairs={{0,4},{1,5},{2,0},{3,1},{4,8},{5,9},{6,2},{7,3},{8,12},{9,13},{10,... | collective-permute-start | bytes 786440 | tf_op jit(solution)/shard_map/ppermute | solution.py:295
  96.8 7.5 %collective-permute-start.35 = (bf16[64,2048]{1,0:T(8,128)(2,1)S(1)}, bf16[64,2048]{1,0:T(8,128)(2,1)S(1)}, u32[]{:S(2)}, u32[]{:S(2)}) collective-permute-start(bf16[64,2048]{1,0:T(8,128)(2,1)S(1)} %add_convert_fusion), channel_id=1, source_target_pairs={{0,2},{1,3},{2,6},{3,7},{4,0},{5,1},{6,10},{7,11},{8,4},{9,5},{10,... | collective-permute-start | bytes 786440 | tf_op jit(solution)/shard_map/ppermute | solution.py:295
  102.7 6.2 %copy-start = (f32[1,32,64,128]{3,2,1,0:T(8,128)S(1)}, f32[1,32,64,128]{3,2,1,0:T(8,128)}, u32[]{:S(2)}) copy-start(f32[1,32,64,128]{3,2,1,0:T(8,128)} %param.24) | copy-start | bytes 3145732
  102.8 6.2 %copy-start.1 = (bf16[128,2048]{1,0:T(8,128)(2,1)S(1)}, bf16[128,2048]{1,0:T(8,128)(2,1)}, u32[]{:S(2)}) copy-start(bf16[128,2048]{1,0:T(8,128)(2,1)} %x_ref.2) | copy-start | bytes 1572868
  102.8 6.2 %copy-start.2 = (bf16[128,128]{1,0:T(8,128)(2,1)S(1)}, bf16[128,128]{1,0:T(8,128)(2,1)}, u32[]{:S(2)}) copy-start(bf16[128,128]{1,0:T(8,128)(2,1)} %b_ref.3) | copy-start | bytes 98308
  102.8 6.2 %copy-start.3 = (f32[128,32]{0,1:T(8,128)S(1)}, f32[128,32]{0,1:T(8,128)}, u32[]{:S(2)}) copy-start(f32[128,32]{0,1:T(8,128)} %param.19) | copy-start | bytes 49156
  102.8 6.2 %copy-start.4 = (f32[32]{0:T(128)S(1)}, f32[32]{0:T(128)}, u32[]{:S(2)}) copy-start(f32[32]{0:T(128)} %param.21) | copy-start | bytes 388
  102.8 6.2 %copy-start.5 = (f32[32]{0:T(128)S(1)}, f32[32]{0:T(128)}, u32[]{:S(2)}) copy-start(f32[32]{0:T(128)} %param.20) | copy-start | bytes 388
  104.4 10.1 %collective-permute-start.30 = (bf16[64,2048]{1,0:T(8,128)(2,1)S(1)}, bf16[64,2048]{1,0:T(8,128)(2,1)S(1)}, u32[]{:S(2)}, u32[]{:S(2)}) collective-permute-start(bf16[64,2048]{1,0:T(8,128)(2,1)S(1)} %get-tuple-element.96), channel_id=1, source_target_pairs={{0,2},{1,3},{2,6},{3,7},{4,0},{5,1},{6,10},{7,11},{8,4},{9,5},{10,... | collective-permute-start | bytes 786440 | tf_op jit(solution)/shard_map/ppermute | solution.py:295
  106.9 7.9 %collective-permute-start.28 = (bf16[64,2048]{1,0:T(8,128)(2,1)S(1)}, bf16[64,2048]{1,0:T(8,128)(2,1)S(1)}, u32[]{:S(2)}, u32[]{:S(2)}) collective-permute-start(bf16[64,2048]{1,0:T(8,128)(2,1)S(1)} %get-tuple-element.97), channel_id=1, source_target_pairs={{0,4},{1,5},{2,0},{3,1},{4,8},{5,9},{6,2},{7,3},{8,12},{9,13},{10,... | collective-permute-start | bytes 786440 | tf_op jit(solution)/shard_map/ppermute | solution.py:295
  106.9 13.5 %collective-permute-start.32 = (bf16[64,2048]{1,0:T(8,128)(2,1)S(1)}, bf16[64,2048]{1,0:T(8,128)(2,1)S(1)}, u32[]{:S(2)}, u32[]{:S(2)}) collective-permute-start(bf16[64,2048]{1,0:T(8,128)(2,1)S(1)} %get-tuple-element.95), channel_id=1, source_target_pairs={{0,4},{1,5},{2,0},{3,1},{4,8},{5,9},{6,2},{7,3},{8,12},{9,13},{10,... | collective-permute-start | bytes 786440 | tf_op jit(solution)/shard_map/ppermute | solution.py:295
  107.7 12.7 %collective-permute-start.36 = (bf16[64,2048]{1,0:T(8,128)(2,1)S(1)}, bf16[64,2048]{1,0:T(8,128)(2,1)S(1)}, u32[]{:S(2)}, u32[]{:S(2)}) collective-permute-start(bf16[64,2048]{1,0:T(8,128)(2,1)S(1)} %get-tuple-element.94), channel_id=1, source_target_pairs={{0,2},{1,3},{2,6},{3,7},{4,0},{5,1},{6,10},{7,11},{8,4},{9,5},{10,... | collective-permute-start | bytes 786440 | tf_op jit(solution)/shard_map/ppermute | solution.py:295
  114.9 8.4 %collective-permute-start.31 = (bf16[64,2048]{1,0:T(8,128)(2,1)S(1)}, bf16[64,2048]{1,0:T(8,128)(2,1)S(1)}, u32[]{:S(2)}, u32[]{:S(2)}) collective-permute-start(bf16[64,2048]{1,0:T(8,128)(2,1)S(1)} %get-tuple-element.92), channel_id=1, source_target_pairs={{0,2},{1,3},{2,6},{3,7},{4,0},{5,1},{6,10},{7,11},{8,4},{9,5},{10,... | collective-permute-start | bytes 786440 | tf_op jit(solution)/shard_map/ppermute | solution.py:295
  116.8 7.7 %collective-permute-start.29 = (bf16[64,2048]{1,0:T(8,128)(2,1)S(1)}, bf16[64,2048]{1,0:T(8,128)(2,1)S(1)}, u32[]{:S(2)}, u32[]{:S(2)}) collective-permute-start(bf16[64,2048]{1,0:T(8,128)(2,1)S(1)} %get-tuple-element.93), channel_id=1, source_target_pairs={{0,4},{1,5},{2,0},{3,1},{4,8},{5,9},{6,2},{7,3},{8,12},{9,13},{10,... | collective-permute-start | bytes 786440 | tf_op jit(solution)/shard_map/ppermute | solution.py:295
  120.5 6.4 %collective-permute-start.37 = (bf16[64,2048]{1,0:T(8,128)(2,1)S(1)}, bf16[64,2048]{1,0:T(8,128)(2,1)S(1)}, u32[]{:S(2)}, u32[]{:S(2)}) collective-permute-start(bf16[64,2048]{1,0:T(8,128)(2,1)S(1)} %get-tuple-element.91), channel_id=1, source_target_pairs={{0,2},{1,3},{2,6},{3,7},{4,0},{5,1},{6,10},{7,11},{8,4},{9,5},{10,... | collective-permute-start | bytes 786440 | tf_op jit(solution)/shard_map/ppermute | solution.py:295
  120.6 7.9 %collective-permute-start.33 = (bf16[64,2048]{1,0:T(8,128)(2,1)S(1)}, bf16[64,2048]{1,0:T(8,128)(2,1)S(1)}, u32[]{:S(2)}, u32[]{:S(2)}) collective-permute-start(bf16[64,2048]{1,0:T(8,128)(2,1)S(1)} %get-tuple-element.90), channel_id=1, source_target_pairs={{0,4},{1,5},{2,0},{3,1},{4,8},{5,9},{6,2},{7,3},{8,12},{9,13},{10,... | collective-permute-start | bytes 786440 | tf_op jit(solution)/shard_map/ppermute | solution.py:295
  (1 other events, 2.5 us)

commit v8 on v7

--- a/solution.py
+++ b/solution.py
@@ -309,9 +309,37 @@
 
     out_other, in_other, down_other = to_core(out_proj), to_core(expert_in), to_core(expert_out)
 
+    experts = wide * 4
+    gates = jnp.sum(
+        jnp.where(route_ids[:, :, None] == jnp.arange(experts), route_weights[:, :, None], 0.0), axis=1
+    )
+    normed_top, normed_bottom, other = lax.optimization_barrier((*normed, to_x(gates)))
+    gates = jnp.where(x == 0, jnp.stack([gates, other]), jnp.stack([other, gates]))[:, None]
+
     halves = range(2)
     size = frames // 2
-    sent = [to_x(normed[h]) for h in halves]
+    hidden_width = expert_out.shape[0]
+    expert_in = after(expert_in, normed_top)
+    gate_in, up_in = lax.optimization_barrier((expert_in[:, :hidden_width], expert_in[:, hidden_width:]))
+    sent = [to_x(normed_top), to_x(after(normed_bottom, gate_in))]
+
+    step = 1
+    while step < wide:
+        other = send(gates, lambda z, x, c: (z ^ step, x, c))
+        gates = jnp.where(
+            z & step == 0,
+            jnp.concatenate([gates, other], axis=1),
+            jnp.concatenate([other, gates], axis=1),
+        )
+        step *= 2
+    sent[1], gates = lax.optimization_barrier((sent[1], gates))
+    mine = (z * 2 + x) * 2 + core
+    pair = jnp.stack([mine, mine + 1 - 2 * core])
+    gates = jnp.sum(
+        jnp.where(pair[:, None] == jnp.arange(experts), gates[..., None, :], 0.0), axis=-1
+    )
+    gates = jnp.concatenate([gates[0], gates[1, ::-1]])
+    gates = lax.dynamic_slice_in_dim(jnp.concatenate([gates, gates]), place, ring, 0)
 
     columns = lax.optimization_barrier(
         jnp.where(
@@ -324,7 +352,7 @@
     def project(rows):
         return jnp.dot(rows, columns, preferred_element_type=jnp.float32).astype(jnp.bfloat16)
 
-    own = [project(normed[h]) for h in halves]
+    own = [project(normed_top), project(normed_bottom)]
     rows, peer = [], None
     for h in halves:
         arrived = sent[h]
@@ -341,20 +369,18 @@
         )
 
     far = ring // 2
-    hidden_width = expert_out.shape[0]
+    fore_at, back_at = {0: rows}, {0: rows}
+    for k in range(1, far):
+        fore_at[k] = [along(fore_at[k - 1][h], 1) for h in halves]
+        back_at[k] = [along(back_at[k - 1][h], -1) for h in halves]
+    last = [along(fore_at[far - 1][0], 1), along(back_at[far - 1][1], -1)]
+
+    joined_in = jnp.concatenate(
+        [gate_in, in_other[:, :hidden_width], up_in, in_other[:, hidden_width:]], axis=1
+    )
+    joined_down = jnp.concatenate([expert_out, down_other], axis=0)
+    joined_in, joined_down = lax.optimization_barrier((joined_in, joined_down))
     is_first = jnp.arange(2 * hidden_width)[None, :] < hidden_width
-
-    def join(in_other, down_other):
-        joined_in = jnp.concatenate(
-            [
-                expert_in[:, :hidden_width],
-                in_other[:, :hidden_width],
-                expert_in[:, hidden_width:],
-                in_other[:, hidden_width:],
-            ],
-            axis=1,
-        )
-        return joined_in, jnp.concatenate([expert_out, down_other], axis=0)
 
     def run_experts(parts, gate):
         v = jnp.dot(jnp.concatenate(parts), joined_in, preferred_element_type=jnp.float32)
@@ -362,71 +388,21 @@
         hidden = (hidden * jnp.where(is_first, gate[:, :1], gate[:, 1:])).astype(jnp.bfloat16)
         return jnp.dot(hidden, joined_down, preferred_element_type=jnp.float32)
 
-    def merge(gates, other, low):
-        return jnp.where(
-            low, jnp.concatenate([gates, other], axis=1), jnp.concatenate([other, gates], axis=1)
-        )
-
-    experts = wide * 4
-    gates = jnp.sum(
-        jnp.where(route_ids[:, :, None] == jnp.arange(experts), route_weights[:, :, None], 0.0), axis=1
-    )
-    other = to_x(after(gates, sent[1]))
-    step = 0
-    fore_at, back_at = {0: rows}, {0: rows}
-    for k in range(1, far):
-        fore_at[k] = [along(fore_at[k - 1][h], 1) for h in halves]
-        back_at[k] = [along(back_at[k - 1][h], -1) for h in halves]
-        if k == 1:
-            fore_at[k][0], back_at[k][0], in_other, down_other = lax.optimization_barrier(
-                (fore_at[k][0], back_at[k][0], in_other, down_other)
-            )
-            for way in (fore_at[k], back_at[k]):
-                way[1] = after(way[1], way[0])
-        if step < wide:
-            other, back_at[k][1] = lax.optimization_barrier((other, back_at[k][1]))
-            if step == 0:
-                gates = jnp.where(x == 0, jnp.stack([gates, other]), jnp.stack([other, gates]))
-                gates, step = gates[:, None], 1
-            else:
-                gates, step = merge(gates, other, z & step == 0), 2 * step
-            if step < wide:
-                other = send(gates, lambda z, x, c: (z ^ step, x, c))
-        if k == far - 1:
-            joined = join(in_other, down_other)
-            back_at[k][1], joined_in, joined_down = lax.optimization_barrier((back_at[k][1], *joined))
-    while step < wide:
-        gates, step = merge(gates, other, z & step == 0), 2 * step
-        if step < wide:
-            other = send(gates, lambda z, x, c: (z ^ step, x, c))
-    mine = (z * 2 + x) * 2 + core
-    pair = jnp.stack([mine, mine + 1 - 2 * core])
-    gates = jnp.sum(
-        jnp.where(pair[:, None] == jnp.arange(experts), gates[..., None, :], 0.0), axis=-1
-    )
-    gates = jnp.concatenate([gates[0], gates[1, ::-1]])
-    gates = lax.dynamic_slice_in_dim(jnp.concatenate([gates, gates]), place, ring, 0)
-    last = [along(fore_at[far - 1][0], 1), along(back_at[far - 1][1], -1)]
-
     def hop_experts(k, tie):
         parts = rows if k == 0 else [*back_at[k], *fore_at[k]]
         gate = gates[0] if k == 0 else jnp.concatenate([gates[k], gates[ring - k]])
-        if tie is not None:
-            parts = [after(part, tie) for part in parts]
+        parts = [after(part, tie) for part in parts]
         total = run_experts(parts, gate)
         cut = [total[i * size : (i + 1) * size] for i in range(len(parts))]
         return cut[:2], cut[2:]
 
-    ahead, behind = hop_experts(far - 1, None)
-    last[0], last[1], *near = lax.optimization_barrier((*last, *ahead, *behind))
-    ahead, behind = near[:2], near[2:]
     total = run_experts(last, gates[far]).astype(jnp.bfloat16)
     fore, back = [along(total[:size], 1), None], [None, along(total[size:], -1)]
+    ahead, behind = hop_experts(far - 1, total)
     tie = total
     for k in range(far - 1, 0, -1):
-        coming = hop_experts(k - 1, tie)
-        if k == 1:
-            state = state_next(tie)
+        if k > 1:
+            coming = hop_experts(k - 1, tie)
         before = ()
         groups = [((fore, 1, ahead, h), (back, -1, behind, h)) for h in halves]
         if k == far - 1:
@@ -442,6 +418,9 @@
             for (way, step, totals, h), load in zip(group, loads):
                 way[h] = along(load, step)
         tie = loads[0]
+        if k == 1:
+            coming = hop_experts(0, tie)
+            state = state_next(tie)
         ahead, behind = coming
     out = []
     for h in halves:

time: 131 us -> 128 us (0.977)
  waiting for transfers between devices: 45.8 us -> 42.3 us
  starting transfers between devices: 40.4 us -> 42.1 us
    ppermute x38, waiting for transfers between devices: 45.8 us -> 42.3 us  [send(): return lax.ppermute(value, axes, routes(wide, move))]
    dot_general x5, matrix products: 9.55 us -> 7.31 us  [run_experts(): jnp.dot(jnp.concatenate(parts), joined_in, preferred_element_type=jnp.flo...]
    select_n x1, other arithmetic: 3.57 us -> 5.23 us  [dense_experts(): jnp.where(core == 0, jnp.concatenate([out_proj, out_other], axis=1), jnp....]
    ppermute x38, starting transfers between devices: 40.4 us -> 42.1 us  [send(): return lax.ppermute(value, axes, routes(wide, move))]
  transfers between devices with their start and end apart: 38 -> 38, of which waited for: 19 -> 18; matrix products, arithmetic and copies ran while one was open for 23% -> 25% of each run, Pallas kernels for 7% -> 7%
where the time goes in v8:
time: 128 us; the launch traced here: 127 us
  waiting for transfers between devices  42.3 us (33%)
  starting transfers between devices  42.1 us (33%)
  matrix products  17.6 us (14%)
  other arithmetic  10.8 us (8%)
  Pallas kernels  8.93 us (7%)
  local copies, waits for them, and re-layouts  4.53 us (4%)
    ppermute x38, waiting for transfers between devices, send(): return lax.ppermute(value, axes, routes(wide, move))  42.3 us
    ppermute x38, starting transfers between devices, send(): return lax.ppermute(value, axes, routes(wide, move))  42.1 us
    dot_general x5, matrix products, run_experts(): jnp.dot(jnp.concatenate(parts), joined_in, preferred_element_type=jnp.flo...  7.31 us
    pallas_call x1, Pallas kernels, ssm_mixer(): pl.pallas_call(mixer_kernel, grid=(steps,), in_specs=[pl.BlockSpec(memory...  5.36 us
    dot_general x4, matrix products, project(): jnp.dot(rows, columns, preferred_element_type=jnp.float32)  5.31 us
    select_n x1, other arithmetic, dense_experts(): jnp.where(core == 0, jnp.concatenate([out_proj, out_other], axis=1), jnp....  5.23 us
    dot_general x5, matrix products, run_experts(): return jnp.dot(hidden, joined_down, preferred_element_type=jnp.float32)  4.93 us
    pallas_call x1, Pallas kernels, state_next(): pl.pallas_call(state_kernel, grid=(steps,), in_specs=[column, whole, per_...  3.58 us
  transfers between devices with their start and end apart: 38, of which 18 were waited for; matrix products, arithmetic and copies ran while one was open for 25% of the time, Pallas kernels for 7%

profile of v8, /device:TPU:0, one launch (start us, length us, event | category | flops | bytes accessed | tf_op | source)
XLA Modules:
  0.0 127.3 jit_solution(15666763894156269714)
XLA Ops:
  1.9 2.6 %collective-permute-start = (f32[128,16]{0,1:T(8,128)S(1)}, f32[128,16]{0,1:T(8,128)S(1)}, u32[]{:S(2)}, u32[]{:S(2)}) collective-permute-start(f32[128,16]{0,1:T(8,128)S(1)} %select_reduce_fusion.1), channel_id=1, source_target_pairs={{0,2},{1,3},{2,0},{3,1},{4,6},{5,7},{6,4},{7,5},{8,10},{9,11},{10,... | collective-permute-start | bytes 24584 | tf_op jit(solution)/shard_map/ppermute | solution.py:295
  5.1 5.4 %mixer.1 = (bf16[64,2048]{1,0:T(8,128)(2,1)}, bf16[64,2048]{1,0:T(8,128)(2,1)}) custom-call(f32[32]{0:T(128)} %skip_ref.1, bf16[128,2048]{1,0:T(8,128)(2,1)} %x_ref.2, bf16[128,2048]{1,0:T(8,128)(2,1)} %z_ref.1, bf16[128,128]{1,0:T(8,128)(2,1)} %b_ref.3, bf16[128,128]{1,0:T(8,128)(2,1)} %c_ref.1, f32[32,128]{1,0:T(8,128)} %bitcast.66, f32[1,32]{1,0:T(1,128)} %bitcast.68, ...), custom_call_target="tpu_custom_call" | custom-call | flops 400000000 | bytes 6000000 | tf_op jit(solution)/shard_map/mixer/pallas_call | solution.py:159
  10.5 1.6 %collective-permute-start.12 = (f32[2,1,128,16]{2,3,1,0:T(8,128)S(1)}, f32[2,1,128,16]{2,3,1,0:T(8,128)S(1)}, u32[]{:S(2)}, u32[]{:S(2)}) collective-permute-start(f32[2,1,128,16]{2,3,1,0:T(8,128)S(1)} %maximum_select_fusion.5), channel_id=1, source_target_pairs={{0,4},{1,5},{2,6},{3,7},{4,0},{5,1},{6,2},{7,3},{8,12},{9,13},{10,... | collective-permute-start | bytes 49160 | tf_op jit(solution)/shard_map/ppermute | solution.py:295
  12.1 2.2 %fusion.104 = (bf16[2048,384]{1,0:T(8,128)(2,1)S(1)}, bf16[2048,384]{1,0:T(8,128)(2,1)S(1)}) fusion(bf16[2048,768]{1,0:T(8,128)(2,1)} %bitcast.73), kind=kLoop, calls=%fused_computation.163 | loop fusion | bytes 6291456 | tf_op jit(solution)/shard_map/slice | solution.py:323
  14.9 2.7 %collective-permute-start.13 = (f32[2,2,128,16]{2,3,1,0:T(8,128)S(1)}, f32[2,2,128,16]{2,3,1,0:T(8,128)S(1)}, u32[]{:S(2)}, u32[]{:S(2)}) collective-permute-start(f32[2,2,128,16]{2,3,1,0:T(8,128)S(1)} %maximum_select_fusion.4), channel_id=1, source_target_pairs={{0,8},{1,9},{2,10},{3,11},{4,12},{5,13},{6,14},{7,15},{8,0},{9,1},... | collective-permute-start | bytes 98312 | tf_op jit(solution)/shard_map/ppermute | solution.py:295
  17.6 2.2 %collective-permute-done.13 = f32[2,2,128,16]{2,3,1,0:T(8,128)S(1)} collective-permute-done((f32[2,2,128,16]{2,3,1,0:T(8,128)S(1)}, f32[2,2,128,16]{2,3,1,0:T(8,128)S(1)}, u32[]{:S(2)}, u32[]{:S(2)}) %collective-permute-start.13) | collective-permute-done | bytes 32800 | tf_op jit(solution)/shard_map/ppermute | solution.py:295
  19.8 1.7 %collective-permute-start.2 = (bf16[64,2048]{1,0:T(8,128)(2,1)S(1)}, bf16[64,2048]{1,0:T(8,128)(2,1)S(1)}, u32[]{:S(2)}, u32[]{:S(2)}) collective-permute-start(bf16[64,2048]{1,0:T(8,128)(2,1)S(1)} %copy-done.7), channel_id=1, source_target_pairs={{0,2},{1,3},{2,0},{3,1},{4,6},{5,7},{6,4},{7,5},{8,10},{9,11},{10,... | collective-permute-start | bytes 786440 | tf_op jit(solution)/shard_map/ppermute | solution.py:295
  21.6 2.3 %collective-permute-done.11 = bf16[64,2048]{1,0:T(8,128)(2,1)} collective-permute-done((bf16[64,2048]{1,0:T(8,128)(2,1)}, bf16[64,2048]{1,0:T(8,128)(2,1)}, u32[]{:S(2)}, u32[]{:S(2)}) %collective-permute-start.11) | collective-permute-done | bytes 262176 | tf_op jit(solution)/shard_map/ppermute | solution.py:295
  24.1 5.2 %maximum_select_fusion = bf16[2048,1024]{1,0:T(8,128)(2,1)S(1)} fusion(bf16[2048,512]{1,0:T(8,128)(2,1)} %collective-permute-done.1, bf16[2048,512]{1,0:T(8,128)(2,1)} %param.25, pred[]{:T(512)S(6)} %eq.47), kind=kLoop, calls=%fused_computation.1 | loop fusion | flops 18874368 | bytes 8388609 | tf_op jit(solution)/shard_map/jit(_where)/select_n | solution.py:345
  30.3 1.8 %convolution_convert_fusion.1 = bf16[64,1024]{1,0:T(8,128)(2,1)S(1)} fusion(bf16[64,2048]{1,0:T(8,128)(2,1)} %collective-permute-done.11, bf16[2048,1024]{1,0:T(8,128)(2,1)S(1)} %maximum_select_fusion), kind=kOutput, calls=%fused_computation.4 | convolution fusion | flops 268500992 | bytes 4587520 | tf_op jit(solution)/shard_map/dot_general | solution.py:353
  32.2 2.0 %collective-permute-start.14 = (bf16[64,1024]{1,0:T(8,128)(2,1)S(1)}, bf16[64,1024]{1,0:T(8,128)(2,1)S(1)}, u32[]{:S(2)}, u32[]{:S(2)}) collective-permute-start(bf16[64,1024]{1,0:T(8,128)(2,1)S(1)} %convolution_convert_fusion.1), channel_id=1, source_target_pairs={{0,2},{1,3},{2,0},{3,1},{4,6},{5,7},{6,4},{7,5},{8,10},{9,11},{10,... | collective-permute-start | bytes 393224 | tf_op jit(solution)/shard_map/ppermute | solution.py:295
  34.2 1.8 %convolution_convert_fusion.2 = bf16[64,1024]{1,0:T(8,128)(2,1)S(1)} fusion(bf16[64,2048]{1,0:T(8,128)(2,1)} %get-tuple-element.43, bf16[2048,1024]{1,0:T(8,128)(2,1)S(1)} %maximum_select_fusion), kind=kOutput, calls=%fused_computation.5 | convolution fusion | flops 268500992 | bytes 4587520 | tf_op jit(solution)/shard_map/dot_general | solution.py:353
  37.3 1.9 %collective-permute-start.15 = (bf16[64,2048]{1,0:T(8,128)(2,1)S(1)}, bf16[64,2048]{1,0:T(8,128)(2,1)S(1)}, u32[]{:S(2)}, u32[]{:S(2)}) collective-permute-start(bf16[64,2048]{1,0:T(8,128)(2,1)S(1)} %maximum_select_fusion.2), channel_id=1, source_target_pairs={{0,2},{1,3},{2,6},{3,7},{4,0},{5,1},{6,10},{7,11},{8,4},{9,5},{10,... | collective-permute-start | bytes 786440 | tf_op jit(solution)/shard_map/ppermute | solution.py:295
  39.6 1.4 %collective-permute-start.21 = (bf16[64,2048]{1,0:T(8,128)(2,1)S(1)}, bf16[64,2048]{1,0:T(8,128)(2,1)S(1)}, u32[]{:S(2)}, u32[]{:S(2)}) collective-permute-start(bf16[64,2048]{1,0:T(8,128)(2,1)S(1)} %maximum_select_fusion.2), channel_id=1, source_target_pairs={{0,4},{1,5},{2,0},{3,1},{4,8},{5,9},{6,2},{7,3},{8,12},{9,13},{10,... | collective-permute-start | bytes 786440 | tf_op jit(solution)/shard_map/ppermute | solution.py:295
  41.7 5.0 %collective-permute-done.15 = bf16[64,2048]{1,0:T(8,128)(2,1)S(1)} collective-permute-done((bf16[64,2048]{1,0:T(8,128)(2,1)S(1)}, bf16[64,2048]{1,0:T(8,128)(2,1)S(1)}, u32[]{:S(2)}, u32[]{:S(2)}) %collective-permute-start.15) | collective-permute-done | bytes 262176 | tf_op jit(solution)/shard_map/ppermute | solution.py:295
  46.6 1.9 %collective-permute-start.16 = (bf16[64,2048]{1,0:T(8,128)(2,1)S(1)}, bf16[64,2048]{1,0:T(8,128)(2,1)S(1)}, u32[]{:S(2)}, u32[]{:S(2)}) collective-permute-start(bf16[64,2048]{1,0:T(8,128)(2,1)S(1)} %collective-permute-done.15), channel_id=1, source_target_pairs={{0,2},{1,3},{2,6},{3,7},{4,0},{5,1},{6,10},{7,11},{8,4},{9,5},{10,... | collective-permute-start | bytes 786440 | tf_op jit(solution)/shard_map/ppermute | solution.py:295
  48.8 5.5 %collective-permute-done.21 = bf16[64,2048]{1,0:T(8,128)(2,1)S(1)} collective-permute-done((bf16[64,2048]{1,0:T(8,128)(2,1)S(1)}, bf16[64,2048]{1,0:T(8,128)(2,1)S(1)}, u32[]{:S(2)}, u32[]{:S(2)}) %collective-permute-start.21) | collective-permute-done | bytes 262176 | tf_op jit(solution)/shard_map/ppermute | solution.py:295
  54.4 1.9 %collective-permute-start.5 = (bf16[64,2048]{1,0:T(8,128)(2,1)S(1)}, bf16[64,2048]{1,0:T(8,128)(2,1)S(1)}, u32[]{:S(2)}, u32[]{:S(2)}) collective-permute-start(bf16[64,2048]{1,0:T(8,128)(2,1)S(1)} %collective-permute-done.4), channel_id=1, source_target_pairs={{0,2},{1,3},{2,6},{3,7},{4,0},{5,1},{6,10},{7,11},{8,4},{9,5},{10,... | collective-permute-start | bytes 786440 | tf_op jit(solution)/shard_map/ppermute | solution.py:295
  56.3 1.6 %collective-permute-done.16 = bf16[64,2048]{1,0:T(8,128)(2,1)S(1)} collective-permute-done((bf16[64,2048]{1,0:T(8,128)(2,1)S(1)}, bf16[64,2048]{1,0:T(8,128)(2,1)S(1)}, u32[]{:S(2)}, u32[]{:S(2)}) %collective-permute-start.16) | collective-permute-done | bytes 262176 | tf_op jit(solution)/shard_map/ppermute | solution.py:295
  57.9 1.9 %collective-permute-start.17 = (bf16[64,2048]{1,0:T(8,128)(2,1)S(1)}, bf16[64,2048]{1,0:T(8,128)(2,1)S(1)}, u32[]{:S(2)}, u32[]{:S(2)}) collective-permute-start(bf16[64,2048]{1,0:T(8,128)(2,1)S(1)} %collective-permute-done.16), channel_id=1, source_target_pairs={{0,2},{1,3},{2,6},{3,7},{4,0},{5,1},{6,10},{7,11},{8,4},{9,5},{10,... | collective-permute-start | bytes 786440 | tf_op jit(solution)/shard_map/ppermute | solution.py:295
  60.0 1.9 %pad_maximum_fusion.1 = bf16[768,2048]{1,0:T(8,128)(2,1)S(1)} fusion(bf16[384,2048]{1,0:T(8,128)(2,1)} %collective-permute-done.20, bf16[384,2048]{1,0:T(8,128)(2,1)S(1)} %bitcast.75), kind=kLoop, calls=%fused_computation.2 | loop fusion | flops 6291456 | bytes 6291456 | tf_op jit(solution)/shard_map/concatenate | solution.py:381
  62.0 3.6 %collective-permute-done.22 = bf16[64,2048]{1,0:T(8,128)(2,1)S(1)} collective-permute-done((bf16[64,2048]{1,0:T(8,128)(2,1)S(1)}, bf16[64,2048]{1,0:T(8,128)(2,1)S(1)}, u32[]{:S(2)}, u32[]{:S(2)}) %collective-permute-start.22) | collective-permute-done | bytes 262176 | tf_op jit(solution)/shard_map/ppermute | solution.py:295
  65.7 1.9 %collective-permute-start.6 = (bf16[64,2048]{1,0:T(8,128)(2,1)S(1)}, bf16[64,2048]{1,0:T(8,128)(2,1)S(1)}, u32[]{:S(2)}, u32[]{:S(2)}) collective-permute-start(bf16[64,2048]{1,0:T(8,128)(2,1)S(1)} %collective-permute-done.5), channel_id=1, source_target_pairs={{0,2},{1,3},{2,6},{3,7},{4,0},{5,1},{6,10},{7,11},{8,4},{9,5},{10,... | collective-permute-start | bytes 786440 | tf_op jit(solution)/shard_map/ppermute | solution.py:295
  67.6 1.7 %collective-permute-done.17 = bf16[64,2048]{1,0:T(8,128)(2,1)S(1)} collective-permute-done((bf16[64,2048]{1,0:T(8,128)(2,1)S(1)}, bf16[64,2048]{1,0:T(8,128)(2,1)S(1)}, u32[]{:S(2)}, u32[]{:S(2)}) %collective-permute-start.17) | collective-permute-done | bytes 262176 | tf_op jit(solution)/shard_map/ppermute | solution.py:295
  69.3 1.9 %collective-permute-start.18 = (bf16[64,2048]{1,0:T(8,128)(2,1)S(1)}, bf16[64,2048]{1,0:T(8,128)(2,1)S(1)}, u32[]{:S(2)}, u32[]{:S(2)}) collective-permute-start(bf16[64,2048]{1,0:T(8,128)(2,1)S(1)} %collective-permute-done.17), channel_id=1, source_target_pairs={{0,2},{1,3},{2,6},{3,7},{4,0},{5,1},{6,10},{7,11},{8,4},{9,5},{10,... | collective-permute-start | bytes 786440 | tf_op jit(solution)/shard_map/ppermute | solution.py:295
  71.3 2.2 %fusion.103 = (bf16[2048,384]{1,0:T(8,128)(2,1)S(1)}, bf16[2048,384]{1,0:T(8,128)(2,1)S(1)}) fusion(bf16[2048,768]{1,0:T(8,128)(2,1)} %collective-permute-done.19), kind=kLoop, calls=%fused_computation.162 | loop fusion | bytes 6291456 | tf_op jit(solution)/shard_map/slice | solution.py:379
  74.2 3.0 %collective-permute-done.18 = bf16[64,2048]{1,0:T(8,128)(2,1)S(1)} collective-permute-done((bf16[64,2048]{1,0:T(8,128)(2,1)S(1)}, bf16[64,2048]{1,0:T(8,128)(2,1)S(1)}, u32[]{:S(2)}, u32[]{:S(2)}) %collective-permute-start.18) | collective-permute-done | bytes 262176 | tf_op jit(solution)/shard_map/ppermute | solution.py:295
  77.3 1.2 collective-permute-done.10
  80.2 1.7 %collective-permute-start.34 = (bf16[64,2048]{1,0:T(8,128)(2,1)S(1)}, bf16[64,2048]{1,0:T(8,128)(2,1)S(1)}, u32[]{:S(2)}, u32[]{:S(2)}) collective-permute-start(bf16[64,2048]{1,0:T(8,128)(2,1)S(1)} %get-tuple-element.90), channel_id=1, source_target_pairs={{0,2},{1,3},{2,6},{3,7},{4,0},{5,1},{6,10},{7,11},{8,4},{9,5},{10,... | collective-permute-start | bytes 786440 | tf_op jit(solution)/shard_map/ppermute | solution.py:295
  81.9 1.8 %fusion = f32[256,1536]{1,0:T(8,128)S(1)} fusion(bf16[2048,1536]{1,0:T(8,128)(2,1)S(1)} %pad_maximum_fusion, bf16[64,2048]{1,0:T(8,128)(2,1)S(1)} %collective-permute-done.23, bf16[64,2048]{1,0:T(8,128)(2,1)S(1)} %collective-permute-done.9, bf16[64,2048]{1,0:T(8,128)(2,1)S(1)} %collective-permute-done.17, bf16[64,2048]{1,0:T(8,128)(2,1)S(1)} %collective-permute-done.6), kind=kOutput, calls=%fused_computation.8 | convolution fusion | flops 1614807040 | bytes 8912896 | tf_op jit(solution)/shard_map/dot_general | solution.py:386
  83.7 1.2 fusion.108
  85.4 1.7 %collective-permute-start.27 = (bf16[64,2048]{1,0:T(8,128)(2,1)S(1)}, bf16[64,2048]{1,0:T(8,128)(2,1)S(1)}, u32[]{:S(2)}, u32[]{:S(2)}) collective-permute-start(bf16[64,2048]{1,0:T(8,128)(2,1)S(1)} %get-tuple-element.88), channel_id=1, source_target_pairs={{0,2},{1,3},{2,6},{3,7},{4,0},{5,1},{6,10},{7,11},{8,4},{9,5},{10,... | collective-permute-start | bytes 786440 | tf_op jit(solution)/shard_map/ppermute | solution.py:295
  87.4 1.8 %fusion.16 = f32[256,1536]{1,0:T(8,128)S(1)} fusion(bf16[2048,1536]{1,0:T(8,128)(2,1)S(1)} %pad_maximum_fusion, bf16[64,2048]{1,0:T(8,128)(2,1)S(1)} %collective-permute-done.22, bf16[64,2048]{1,0:T(8,128)(2,1)S(1)} %collective-permute-done.8, bf16[64,2048]{1,0:T(8,128)(2,1)S(1)} %collective-permute-done.16, bf16[64,2048]{1,0:T(8,128)(2,1)S(1)} %collective-permute-done.5), kind=kOutput, calls=%fused_computation.24 | convolution fusion | flops 1614807040 | bytes 8912896 | tf_op jit(solution)/shard_map/dot_general | solution.py:386
  89.2 1.2 fusion.58
  90.4 3.9 %collective-permute-done.24 = bf16[64,2048]{1,0:T(8,128)(2,1)S(1)} collective-permute-done((bf16[64,2048]{1,0:T(8,128)(2,1)S(1)}, bf16[64,2048]{1,0:T(8,128)(2,1)S(1)}, u32[]{:S(2)}, u32[]{:S(2)}) %collective-permute-start.24) | collective-permute-done | bytes 262176 | tf_op jit(solution)/shard_map/ppermute | solution.py:295
  94.8 1.7 %collective-permute-start.35 = (bf16[64,2048]{1,0:T(8,128)(2,1)S(1)}, bf16[64,2048]{1,0:T(8,128)(2,1)S(1)}, u32[]{:S(2)}, u32[]{:S(2)}) collective-permute-start(bf16[64,2048]{1,0:T(8,128)(2,1)S(1)} %get-tuple-element.80), channel_id=1, source_target_pairs={{0,2},{1,3},{2,6},{3,7},{4,0},{5,1},{6,10},{7,11},{8,4},{9,5},{10,... | collective-permute-start | bytes 786440 | tf_op jit(solution)/shard_map/ppermute | solution.py:295
  96.4 1.8 %fusion.8 = f32[256,1536]{1,0:T(8,128)S(1)} fusion(bf16[2048,1536]{1,0:T(8,128)(2,1)S(1)} %pad_maximum_fusion, bf16[64,2048]{1,0:T(8,128)(2,1)S(1)} %collective-permute-done.21, bf16[64,2048]{1,0:T(8,128)(2,1)S(1)} %collective-permute-done.7, bf16[64,2048]{1,0:T(8,128)(2,1)S(1)} %collective-permute-done.15, bf16[64,2048]{1,0:T(8,128)(2,1)S(1)} %collective-permute-done.4), kind=kOutput, calls=%fused_computation.16 | convolution fusion | flops 1614807040 | bytes 8912896 | tf_op jit(solution)/shard_map/dot_general | solution.py:386
  98.2 1.2 fusion.56
  99.4 2.2 %collective-permute-done.26 = bf16[64,2048]{1,0:T(8,128)(2,1)S(1)} collective-permute-done((bf16[64,2048]{1,0:T(8,128)(2,1)S(1)}, bf16[64,2048]{1,0:T(8,128)(2,1)S(1)}, u32[]{:S(2)}, u32[]{:S(2)}) %collective-permute-start.26) | collective-permute-done | bytes 262176 | tf_op jit(solution)/shard_map/ppermute | solution.py:295
  101.7 2.9 %collective-permute-start.30 = (bf16[64,2048]{1,0:T(8,128)(2,1)S(1)}, bf16[64,2048]{1,0:T(8,128)(2,1)S(1)}, u32[]{:S(2)}, u32[]{:S(2)}) collective-permute-start(bf16[64,2048]{1,0:T(8,128)(2,1)S(1)} %get-tuple-element.84), channel_id=1, source_target_pairs={{0,2},{1,3},{2,6},{3,7},{4,0},{5,1},{6,10},{7,11},{8,4},{9,5},{10,... | collective-permute-start | bytes 786440 | tf_op jit(solution)/shard_map/ppermute | solution.py:295
  104.8 2.0 %collective-permute-start.36 = (bf16[64,2048]{1,0:T(8,128)(2,1)S(1)}, bf16[64,2048]{1,0:T(8,128)(2,1)S(1)}, u32[]{:S(2)}, u32[]{:S(2)}) collective-permute-start(bf16[64,2048]{1,0:T(8,128)(2,1)S(1)} %get-tuple-element.78), channel_id=1, source_target_pairs={{0,2},{1,3},{2,6},{3,7},{4,0},{5,1},{6,10},{7,11},{8,4},{9,5},{10,... | collective-permute-start | bytes 786440 | tf_op jit(solution)/shard_map/ppermute | solution.py:295
  106.9 2.6 %collective-permute-done.30 = bf16[64,2048]{1,0:T(8,128)(2,1)S(1)} collective-permute-done((bf16[64,2048]{1,0:T(8,128)(2,1)S(1)}, bf16[64,2048]{1,0:T(8,128)(2,1)S(1)}, u32[]{:S(2)}, u32[]{:S(2)}) %collective-permute-start.30) | collective-permute-done | bytes 262176 | tf_op jit(solution)/shard_map/ppermute | solution.py:295
  109.6 1.5 %collective-permute-done.29 = bf16[64,2048]{1,0:T(8,128)(2,1)S(1)} collective-permute-done((bf16[64,2048]{1,0:T(8,128)(2,1)S(1)}, bf16[64,2048]{1,0:T(8,128)(2,1)S(1)}, u32[]{:S(2)}, u32[]{:S(2)}) %collective-permute-start.29) | collective-permute-done | bytes 262176 | tf_op jit(solution)/shard_map/ppermute | solution.py:295
  111.2 2.8 %collective-permute-done.36 = bf16[64,2048]{1,0:T(8,128)(2,1)S(1)} collective-permute-done((bf16[64,2048]{1,0:T(8,128)(2,1)S(1)}, bf16[64,2048]{1,0:T(8,128)(2,1)S(1)}, u32[]{:S(2)}, u32[]{:S(2)}) %collective-permute-start.36) | collective-permute-done | bytes 262176 | tf_op jit(solution)/shard_map/ppermute | solution.py:295
  114.0 2.5 %collective-permute-done.28 = bf16[64,2048]{1,0:T(8,128)(2,1)S(1)} collective-permute-done((bf16[64,2048]{1,0:T(8,128)(2,1)S(1)}, bf16[64,2048]{1,0:T(8,128)(2,1)S(1)}, u32[]{:S(2)}, u32[]{:S(2)}) %collective-permute-start.28) | collective-permute-done | bytes 262176 | tf_op jit(solution)/shard_map/ppermute | solution.py:295
  116.7 2.0 %collective-permute-start.31 = (bf16[64,2048]{1,0:T(8,128)(2,1)S(1)}, bf16[64,2048]{1,0:T(8,128)(2,1)S(1)}, u32[]{:S(2)}, u32[]{:S(2)}) collective-permute-start(bf16[64,2048]{1,0:T(8,128)(2,1)S(1)} %get-tuple-element.83), channel_id=1, source_target_pairs={{0,4},{1,5},{2,0},{3,1},{4,8},{5,9},{6,2},{7,3},{8,12},{9,13},{10,... | collective-permute-start | bytes 786440 | tf_op jit(solution)/shard_map/ppermute | solution.py:295
  118.8 2.0 %collective-permute-start.37 = (bf16[64,2048]{1,0:T(8,128)(2,1)S(1)}, bf16[64,2048]{1,0:T(8,128)(2,1)S(1)}, u32[]{:S(2)}, u32[]{:S(2)}) collective-permute-start(bf16[64,2048]{1,0:T(8,128)(2,1)S(1)} %get-tuple-element.76), channel_id=1, source_target_pairs={{0,2},{1,3},{2,6},{3,7},{4,0},{5,1},{6,10},{7,11},{8,4},{9,5},{10,... | collective-permute-start | bytes 786440 | tf_op jit(solution)/shard_map/ppermute | solution.py:295
  120.8 3.6 %state.1 = f32[2048,128]{1,0:T(8,128)} custom-call(bf16[128,2048]{1,0:T(8,128)(2,1)S(1)} %copy-done.1, bf16[128,128]{1,0:T(8,128)(2,1)S(1)} %copy-done.2, f32[32,128]{1,0:T(8,128)S(1)} %bitcast.67, f32[1,32]{1,0:T(1,128)S(1)} %bitcast.69, f32[1,32]{1,0:T(1,128)S(1)} %bitcast.71, f32[2048,128]{1,0:T(8,128)S(1)} %bitcast.65), custom_call_target="tpu_custom_call" | custom-call | flops 70000000 | bytes 3000000 | tf_op jit(solution)/shard_map/state/pallas_call | solution.py:198
  (92 shorter events, 14.3 us)
Async XLA Ops:
  0.6 70.7 %collective-permute-start.19 = (bf16[2048,768]{1,0:T(8,128)(2,1)}, bf16[2048,768]{1,0:T(8,128)(2,1)}, u32[]{:S(2)}, u32[]{:S(2)}) collective-permute-start(bf16[2048,768]{1,0:T(8,128)(2,1)} %bitcast.72), channel_id=1, source_target_pairs={{0,1},{1,0},{2,3},{3,2},{4,5},{5,4},{6,7},{7,6},{8,9},{9,8},{10,11... | collective-permute-start | bytes 9437192 | tf_op jit(solution)/shard_map/ppermute | solution.py:295
  1.9 8.6 %collective-permute-start = (f32[128,16]{0,1:T(8,128)S(1)}, f32[128,16]{0,1:T(8,128)S(1)}, u32[]{:S(2)}, u32[]{:S(2)}) collective-permute-start(f32[128,16]{0,1:T(8,128)S(1)} %select_reduce_fusion.1), channel_id=1, source_target_pairs={{0,2},{1,3},{2,0},{3,1},{4,6},{5,7},{6,4},{7,5},{8,10},{9,11},{10,... | collective-permute-start | bytes 24584 | tf_op jit(solution)/shard_map/ppermute | solution.py:295
  4.4 36.5 %collective-permute-start.20 = (bf16[384,2048]{1,0:T(8,128)(2,1)}, bf16[384,2048]{1,0:T(8,128)(2,1)}, u32[]{:S(2)}, u32[]{:S(2)}) collective-permute-start(bf16[384,2048]{1,0:T(8,128)(2,1)} %bitcast.74), channel_id=1, source_target_pairs={{0,1},{1,0},{2,3},{3,2},{4,5},{5,4},{6,7},{7,6},{8,9},{9,8},{10,11... | collective-permute-start | bytes 4718600 | tf_op jit(solution)/shard_map/ppermute | solution.py:295
  4.6 19.5 %collective-permute-start.1 = (bf16[2048,512]{1,0:T(8,128)(2,1)}, bf16[2048,512]{1,0:T(8,128)(2,1)}, u32[]{:S(2)}, u32[]{:S(2)}) collective-permute-start(bf16[2048,512]{1,0:T(8,128)(2,1)} %param.25), channel_id=1, source_target_pairs={{0,1},{1,0},{2,3},{3,2},{4,5},{5,4},{6,7},{7,6},{8,9},{9,8},{10,11... | collective-permute-start | bytes 6291464 | tf_op jit(solution)/shard_map/ppermute | solution.py:295
  10.5 9.4 %copy-start.7 = (bf16[64,2048]{1,0:T(8,128)(2,1)S(1)}, bf16[64,2048]{1,0:T(8,128)(2,1)}, u32[]{:S(2)}) copy-start(bf16[64,2048]{1,0:T(8,128)(2,1)} %get-tuple-element.39) | copy-start | bytes 786436
  10.5 4.4 %collective-permute-start.12 = (f32[2,1,128,16]{2,3,1,0:T(8,128)S(1)}, f32[2,1,128,16]{2,3,1,0:T(8,128)S(1)}, u32[]{:S(2)}, u32[]{:S(2)}) collective-permute-start(f32[2,1,128,16]{2,3,1,0:T(8,128)S(1)} %maximum_select_fusion.5), channel_id=1, source_target_pairs={{0,4},{1,5},{2,6},{3,7},{4,0},{5,1},{6,2},{7,3},{8,12},{9,13},{10,... | collective-permute-start | bytes 49160 | tf_op jit(solution)/shard_map/ppermute | solution.py:295
  14.3 9.6 %collective-permute-start.11 = (bf16[64,2048]{1,0:T(8,128)(2,1)}, bf16[64,2048]{1,0:T(8,128)(2,1)}, u32[]{:S(2)}, u32[]{:S(2)}) collective-permute-start(bf16[64,2048]{1,0:T(8,128)(2,1)} %get-tuple-element.43), channel_id=1, source_target_pairs={{0,2},{1,3},{2,0},{3,1},{4,6},{5,7},{6,4},{7,5},{8,10},{9,11},{10,... | collective-permute-start | bytes 786440 | tf_op jit(solution)/shard_map/ppermute | solution.py:295
  14.9 4.9 %collective-permute-start.13 = (f32[2,2,128,16]{2,3,1,0:T(8,128)S(1)}, f32[2,2,128,16]{2,3,1,0:T(8,128)S(1)}, u32[]{:S(2)}, u32[]{:S(2)}) collective-permute-start(f32[2,2,128,16]{2,3,1,0:T(8,128)S(1)} %maximum_select_fusion.4), channel_id=1, source_target_pairs={{0,8},{1,9},{2,10},{3,11},{4,12},{5,13},{6,14},{7,15},{8,0},{9,1},... | collective-permute-start | bytes 98312 | tf_op jit(solution)/shard_map/ppermute | solution.py:295
  19.8 9.5 %collective-permute-start.2 = (bf16[64,2048]{1,0:T(8,128)(2,1)S(1)}, bf16[64,2048]{1,0:T(8,128)(2,1)S(1)}, u32[]{:S(2)}, u32[]{:S(2)}) collective-permute-start(bf16[64,2048]{1,0:T(8,128)(2,1)S(1)} %copy-done.7), channel_id=1, source_target_pairs={{0,2},{1,3},{2,0},{3,1},{4,6},{5,7},{6,4},{7,5},{8,10},{9,11},{10,... | collective-permute-start | bytes 786440 | tf_op jit(solution)/shard_map/ppermute | solution.py:295
  30.2 9.1 %collective-permute-start.3 = (bf16[64,1024]{1,0:T(8,128)(2,1)S(1)}, bf16[64,1024]{1,0:T(8,128)(2,1)S(1)}, u32[]{:S(2)}, u32[]{:S(2)}) collective-permute-start(bf16[64,1024]{1,0:T(8,128)(2,1)S(1)} %convolution_convert_fusion.3), channel_id=1, source_target_pairs={{0,2},{1,3},{2,0},{3,1},{4,6},{5,7},{6,4},{7,5},{8,10},{9,11},{10,... | collective-permute-start | bytes 393224 | tf_op jit(solution)/shard_map/ppermute | solution.py:295
  32.2 5.1 %collective-permute-start.14 = (bf16[64,1024]{1,0:T(8,128)(2,1)S(1)}, bf16[64,1024]{1,0:T(8,128)(2,1)S(1)}, u32[]{:S(2)}, u32[]{:S(2)}) collective-permute-start(bf16[64,1024]{1,0:T(8,128)(2,1)S(1)} %convolution_convert_fusion.1), channel_id=1, source_target_pairs={{0,2},{1,3},{2,0},{3,1},{4,6},{5,7},{6,4},{7,5},{8,10},{9,11},{10,... | collective-permute-start | bytes 393224 | tf_op jit(solution)/shard_map/ppermute | solution.py:295
  36.0 24.0 %copy-start.6 = (bf16[1,384,2048]{2,1,0:T(8,128)(2,1)S(1)}, bf16[1,384,2048]{2,1,0:T(8,128)(2,1)}, u32[]{:S(2)}) copy-start(bf16[1,384,2048]{2,1,0:T(8,128)(2,1)} %param.27) | copy-start | bytes 4718596
  37.3 9.3 %collective-permute-start.15 = (bf16[64,2048]{1,0:T(8,128)(2,1)S(1)}, bf16[64,2048]{1,0:T(8,128)(2,1)S(1)}, u32[]{:S(2)}, u32[]{:S(2)}) collective-permute-start(bf16[64,2048]{1,0:T(8,128)(2,1)S(1)} %maximum_select_fusion.2), channel_id=1, source_target_pairs={{0,2},{1,3},{2,6},{3,7},{4,0},{5,1},{6,10},{7,11},{8,4},{9,5},{10,... | collective-permute-start | bytes 786440 | tf_op jit(solution)/shard_map/ppermute | solution.py:295
  39.4 9.3 %collective-permute-start.7 = (bf16[64,2048]{1,0:T(8,128)(2,1)S(1)}, bf16[64,2048]{1,0:T(8,128)(2,1)S(1)}, u32[]{:S(2)}, u32[]{:S(2)}) collective-permute-start(bf16[64,2048]{1,0:T(8,128)(2,1)S(1)} %maximum_select_fusion.1), channel_id=1, source_target_pairs={{0,4},{1,5},{2,0},{3,1},{4,8},{5,9},{6,2},{7,3},{8,12},{9,13},{10,... | collective-permute-start | bytes 786440 | tf_op jit(solution)/shard_map/ppermute | solution.py:295
  39.6 14.7 %collective-permute-start.21 = (bf16[64,2048]{1,0:T(8,128)(2,1)S(1)}, bf16[64,2048]{1,0:T(8,128)(2,1)S(1)}, u32[]{:S(2)}, u32[]{:S(2)}) collective-permute-start(bf16[64,2048]{1,0:T(8,128)(2,1)S(1)} %maximum_select_fusion.2), channel_id=1, source_target_pairs={{0,4},{1,5},{2,0},{3,1},{4,8},{5,9},{6,2},{7,3},{8,12},{9,13},{10,... | collective-permute-start | bytes 786440 | tf_op jit(solution)/shard_map/ppermute | solution.py:295
  40.9 13.5 %collective-permute-start.4 = (bf16[64,2048]{1,0:T(8,128)(2,1)S(1)}, bf16[64,2048]{1,0:T(8,128)(2,1)S(1)}, u32[]{:S(2)}, u32[]{:S(2)}) collective-permute-start(bf16[64,2048]{1,0:T(8,128)(2,1)S(1)} %maximum_select_fusion.1), channel_id=1, source_target_pairs={{0,2},{1,3},{2,6},{3,7},{4,0},{5,1},{6,10},{7,11},{8,4},{9,5},{10,... | collective-permute-start | bytes 786440 | tf_op jit(solution)/shard_map/ppermute | solution.py:295
  46.6 11.2 %collective-permute-start.16 = (bf16[64,2048]{1,0:T(8,128)(2,1)S(1)}, bf16[64,2048]{1,0:T(8,128)(2,1)S(1)}, u32[]{:S(2)}, u32[]{:S(2)}) collective-permute-start(bf16[64,2048]{1,0:T(8,128)(2,1)S(1)} %collective-permute-done.15), channel_id=1, source_target_pairs={{0,2},{1,3},{2,6},{3,7},{4,0},{5,1},{6,10},{7,11},{8,4},{9,5},{10,... | collective-permute-start | bytes 786440 | tf_op jit(solution)/shard_map/ppermute | solution.py:295
  48.7 11.2 %collective-permute-start.8 = (bf16[64,2048]{1,0:T(8,128)(2,1)S(1)}, bf16[64,2048]{1,0:T(8,128)(2,1)S(1)}, u32[]{:S(2)}, u32[]{:S(2)}) collective-permute-start(bf16[64,2048]{1,0:T(8,128)(2,1)S(1)} %collective-permute-done.7), channel_id=1, source_target_pairs={{0,4},{1,5},{2,0},{3,1},{4,8},{5,9},{6,2},{7,3},{8,12},{9,13},{10,... | collective-permute-start | bytes 786440 | tf_op jit(solution)/shard_map/ppermute | solution.py:295
  54.3 11.2 %collective-permute-start.22 = (bf16[64,2048]{1,0:T(8,128)(2,1)S(1)}, bf16[64,2048]{1,0:T(8,128)(2,1)S(1)}, u32[]{:S(2)}, u32[]{:S(2)}) collective-permute-start(bf16[64,2048]{1,0:T(8,128)(2,1)S(1)} %collective-permute-done.21), channel_id=1, source_target_pairs={{0,4},{1,5},{2,0},{3,1},{4,8},{5,9},{6,2},{7,3},{8,12},{9,13},{10,... | collective-permute-start | bytes 786440 | tf_op jit(solution)/shard_map/ppermute | solution.py:295
  54.4 11.2 %collective-permute-start.5 = (bf16[64,2048]{1,0:T(8,128)(2,1)S(1)}, bf16[64,2048]{1,0:T(8,128)(2,1)S(1)}, u32[]{:S(2)}, u32[]{:S(2)}) collective-permute-start(bf16[64,2048]{1,0:T(8,128)(2,1)S(1)} %collective-permute-done.4), channel_id=1, source_target_pairs={{0,2},{1,3},{2,6},{3,7},{4,0},{5,1},{6,10},{7,11},{8,4},{9,5},{10,... | collective-permute-start | bytes 786440 | tf_op jit(solution)/shard_map/ppermute | solution.py:295
  57.9 11.4 %collective-permute-start.17 = (bf16[64,2048]{1,0:T(8,128)(2,1)S(1)}, bf16[64,2048]{1,0:T(8,128)(2,1)S(1)}, u32[]{:S(2)}, u32[]{:S(2)}) collective-permute-start(bf16[64,2048]{1,0:T(8,128)(2,1)S(1)} %collective-permute-done.16), channel_id=1, source_target_pairs={{0,2},{1,3},{2,6},{3,7},{4,0},{5,1},{6,10},{7,11},{8,4},{9,5},{10,... | collective-permute-start | bytes 786440 | tf_op jit(solution)/shard_map/ppermute | solution.py:295
  59.9 11.3 %collective-permute-start.9 = (bf16[64,2048]{1,0:T(8,128)(2,1)S(1)}, bf16[64,2048]{1,0:T(8,128)(2,1)S(1)}, u32[]{:S(2)}, u32[]{:S(2)}) collective-permute-start(bf16[64,2048]{1,0:T(8,128)(2,1)S(1)} %collective-permute-done.8), channel_id=1, source_target_pairs={{0,4},{1,5},{2,0},{3,1},{4,8},{5,9},{6,2},{7,3},{8,12},{9,13},{10,... | collective-permute-start | bytes 786440 | tf_op jit(solution)/shard_map/ppermute | solution.py:295
  65.5 14.6 %collective-permute-start.23 = (bf16[64,2048]{1,0:T(8,128)(2,1)S(1)}, bf16[64,2048]{1,0:T(8,128)(2,1)S(1)}, u32[]{:S(2)}, u32[]{:S(2)}) collective-permute-start(bf16[64,2048]{1,0:T(8,128)(2,1)S(1)} %collective-permute-done.22), channel_id=1, source_target_pairs={{0,4},{1,5},{2,0},{3,1},{4,8},{5,9},{6,2},{7,3},{8,12},{9,13},{10,... | collective-permute-start | bytes 786440 | tf_op jit(solution)/shard_map/ppermute | solution.py:295
  65.7 14.6 %collective-permute-start.6 = (bf16[64,2048]{1,0:T(8,128)(2,1)S(1)}, bf16[64,2048]{1,0:T(8,128)(2,1)S(1)}, u32[]{:S(2)}, u32[]{:S(2)}) collective-permute-start(bf16[64,2048]{1,0:T(8,128)(2,1)S(1)} %collective-permute-done.5), channel_id=1, source_target_pairs={{0,2},{1,3},{2,6},{3,7},{4,0},{5,1},{6,10},{7,11},{8,4},{9,5},{10,... | collective-permute-start | bytes 786440 | tf_op jit(solution)/shard_map/ppermute | solution.py:295
  69.3 8.0 %collective-permute-start.18 = (bf16[64,2048]{1,0:T(8,128)(2,1)S(1)}, bf16[64,2048]{1,0:T(8,128)(2,1)S(1)}, u32[]{:S(2)}, u32[]{:S(2)}) collective-permute-start(bf16[64,2048]{1,0:T(8,128)(2,1)S(1)} %collective-permute-done.17), channel_id=1, source_target_pairs={{0,2},{1,3},{2,6},{3,7},{4,0},{5,1},{6,10},{7,11},{8,4},{9,5},{10,... | collective-permute-start | bytes 786440 | tf_op jit(solution)/shard_map/ppermute | solution.py:295
  71.2 7.3 %collective-permute-start.10 = (bf16[64,2048]{1,0:T(8,128)(2,1)S(1)}, bf16[64,2048]{1,0:T(8,128)(2,1)S(1)}, u32[]{:S(2)}, u32[]{:S(2)}) collective-permute-start(bf16[64,2048]{1,0:T(8,128)(2,1)S(1)} %collective-permute-done.9), channel_id=1, source_target_pairs={{0,4},{1,5},{2,0},{3,1},{4,8},{5,9},{6,2},{7,3},{8,12},{9,13},{10,... | collective-permute-start | bytes 786440 | tf_op jit(solution)/shard_map/ppermute | solution.py:295
  80.2 10.1 %collective-permute-start.34 = (bf16[64,2048]{1,0:T(8,128)(2,1)S(1)}, bf16[64,2048]{1,0:T(8,128)(2,1)S(1)}, u32[]{:S(2)}, u32[]{:S(2)}) collective-permute-start(bf16[64,2048]{1,0:T(8,128)(2,1)S(1)} %get-tuple-element.90), channel_id=1, source_target_pairs={{0,2},{1,3},{2,6},{3,7},{4,0},{5,1},{6,10},{7,11},{8,4},{9,5},{10,... | collective-permute-start | bytes 786440 | tf_op jit(solution)/shard_map/ppermute | solution.py:295
  84.9 9.3 %collective-permute-start.24 = (bf16[64,2048]{1,0:T(8,128)(2,1)S(1)}, bf16[64,2048]{1,0:T(8,128)(2,1)S(1)}, u32[]{:S(2)}, u32[]{:S(2)}) collective-permute-start(bf16[64,2048]{1,0:T(8,128)(2,1)S(1)} %get-tuple-element.91), channel_id=1, source_target_pairs={{0,4},{1,5},{2,0},{3,1},{4,8},{5,9},{6,2},{7,3},{8,12},{9,13},{10,... | collective-permute-start | bytes 786440 | tf_op jit(solution)/shard_map/ppermute | solution.py:295
  85.4 12.8 %collective-permute-start.27 = (bf16[64,2048]{1,0:T(8,128)(2,1)S(1)}, bf16[64,2048]{1,0:T(8,128)(2,1)S(1)}, u32[]{:S(2)}, u32[]{:S(2)}) collective-permute-start(bf16[64,2048]{1,0:T(8,128)(2,1)S(1)} %get-tuple-element.88), channel_id=1, source_target_pairs={{0,2},{1,3},{2,6},{3,7},{4,0},{5,1},{6,10},{7,11},{8,4},{9,5},{10,... | collective-permute-start | bytes 786440 | tf_op jit(solution)/shard_map/ppermute | solution.py:295
  87.0 17.7 %collective-permute-start.25 = (bf16[64,2048]{1,0:T(8,128)(2,1)S(1)}, bf16[64,2048]{1,0:T(8,128)(2,1)S(1)}, u32[]{:S(2)}, u32[]{:S(2)}) collective-permute-start(bf16[64,2048]{1,0:T(8,128)(2,1)S(1)} %get-tuple-element.89), channel_id=1, source_target_pairs={{0,4},{1,5},{2,0},{3,1},{4,8},{5,9},{6,2},{7,3},{8,12},{9,13},{10,... | collective-permute-start | bytes 786440 | tf_op jit(solution)/shard_map/ppermute | solution.py:295
  94.3 7.2 %collective-permute-start.26 = (bf16[64,2048]{1,0:T(8,128)(2,1)S(1)}, bf16[64,2048]{1,0:T(8,128)(2,1)S(1)}, u32[]{:S(2)}, u32[]{:S(2)}) collective-permute-start(bf16[64,2048]{1,0:T(8,128)(2,1)S(1)} %get-tuple-element.81), channel_id=1, source_target_pairs={{0,4},{1,5},{2,0},{3,1},{4,8},{5,9},{6,2},{7,3},{8,12},{9,13},{10,... | collective-permute-start | bytes 786440 | tf_op jit(solution)/shard_map/ppermute | solution.py:295
  94.8 10.0 %collective-permute-start.35 = (bf16[64,2048]{1,0:T(8,128)(2,1)S(1)}, bf16[64,2048]{1,0:T(8,128)(2,1)S(1)}, u32[]{:S(2)}, u32[]{:S(2)}) collective-permute-start(bf16[64,2048]{1,0:T(8,128)(2,1)S(1)} %get-tuple-element.80), channel_id=1, source_target_pairs={{0,2},{1,3},{2,6},{3,7},{4,0},{5,1},{6,10},{7,11},{8,4},{9,5},{10,... | collective-permute-start | bytes 786440 | tf_op jit(solution)/shard_map/ppermute | solution.py:295
  101.7 7.9 %collective-permute-start.30 = (bf16[64,2048]{1,0:T(8,128)(2,1)S(1)}, bf16[64,2048]{1,0:T(8,128)(2,1)S(1)}, u32[]{:S(2)}, u32[]{:S(2)}) collective-permute-start(bf16[64,2048]{1,0:T(8,128)(2,1)S(1)} %get-tuple-element.84), channel_id=1, source_target_pairs={{0,2},{1,3},{2,6},{3,7},{4,0},{5,1},{6,10},{7,11},{8,4},{9,5},{10,... | collective-permute-start | bytes 786440 | tf_op jit(solution)/shard_map/ppermute | solution.py:295
  104.6 16.1 %copy-start = (f32[1,32,64,128]{3,2,1,0:T(8,128)S(1)}, f32[1,32,64,128]{3,2,1,0:T(8,128)}, u32[]{:S(2)}) copy-start(f32[1,32,64,128]{3,2,1,0:T(8,128)} %param.24) | copy-start | bytes 3145732
  104.6 16.1 %copy-start.1 = (bf16[128,2048]{1,0:T(8,128)(2,1)S(1)}, bf16[128,2048]{1,0:T(8,128)(2,1)}, u32[]{:S(2)}) copy-start(bf16[128,2048]{1,0:T(8,128)(2,1)} %x_ref.2) | copy-start | bytes 1572868
  104.6 16.1 %copy-start.2 = (bf16[128,128]{1,0:T(8,128)(2,1)S(1)}, bf16[128,128]{1,0:T(8,128)(2,1)}, u32[]{:S(2)}) copy-start(bf16[128,128]{1,0:T(8,128)(2,1)} %b_ref.3) | copy-start | bytes 98308
  104.6 16.1 %copy-start.3 = (f32[128,32]{0,1:T(8,128)S(1)}, f32[128,32]{0,1:T(8,128)}, u32[]{:S(2)}) copy-start(f32[128,32]{0,1:T(8,128)} %param.19) | copy-start | bytes 49156
  104.6 16.1 %copy-start.4 = (f32[32]{0:T(128)S(1)}, f32[32]{0:T(128)}, u32[]{:S(2)}) copy-start(f32[32]{0:T(128)} %param.21) | copy-start | bytes 388
  104.6 16.1 %copy-start.5 = (f32[32]{0:T(128)S(1)}, f32[32]{0:T(128)}, u32[]{:S(2)}) copy-start(f32[32]{0:T(128)} %param.20) | copy-start | bytes 388
  104.6 6.4 %collective-permute-start.29 = (bf16[64,2048]{1,0:T(8,128)(2,1)S(1)}, bf16[64,2048]{1,0:T(8,128)(2,1)S(1)}, u32[]{:S(2)}, u32[]{:S(2)}) collective-permute-start(bf16[64,2048]{1,0:T(8,128)(2,1)S(1)} %get-tuple-element.85), channel_id=1, source_target_pairs={{0,4},{1,5},{2,0},{3,1},{4,8},{5,9},{6,2},{7,3},{8,12},{9,13},{10,... | collective-permute-start | bytes 786440 | tf_op jit(solution)/shard_map/ppermute | solution.py:295
  104.8 9.2 %collective-permute-start.36 = (bf16[64,2048]{1,0:T(8,128)(2,1)S(1)}, bf16[64,2048]{1,0:T(8,128)(2,1)S(1)}, u32[]{:S(2)}, u32[]{:S(2)}) collective-permute-start(bf16[64,2048]{1,0:T(8,128)(2,1)S(1)} %get-tuple-element.78), channel_id=1, source_target_pairs={{0,2},{1,3},{2,6},{3,7},{4,0},{5,1},{6,10},{7,11},{8,4},{9,5},{10,... | collective-permute-start | bytes 786440 | tf_op jit(solution)/shard_map/ppermute | solution.py:295
  106.9 9.6 %collective-permute-start.28 = (bf16[64,2048]{1,0:T(8,128)(2,1)S(1)}, bf16[64,2048]{1,0:T(8,128)(2,1)S(1)}, u32[]{:S(2)}, u32[]{:S(2)}) collective-permute-start(bf16[64,2048]{1,0:T(8,128)(2,1)S(1)} %get-tuple-element.79), channel_id=1, source_target_pairs={{0,4},{1,5},{2,0},{3,1},{4,8},{5,9},{6,2},{7,3},{8,12},{9,13},{10,... | collective-permute-start | bytes 786440 | tf_op jit(solution)/shard_map/ppermute | solution.py:295
  116.6 9.4 %collective-permute-start.32 = (bf16[64,2048]{1,0:T(8,128)(2,1)S(1)}, bf16[64,2048]{1,0:T(8,128)(2,1)S(1)}, u32[]{:S(2)}, u32[]{:S(2)}) collective-permute-start(bf16[64,2048]{1,0:T(8,128)(2,1)S(1)} %get-tuple-element.82), channel_id=1, source_target_pairs={{0,2},{1,3},{2,6},{3,7},{4,0},{5,1},{6,10},{7,11},{8,4},{9,5},{10,... | collective-permute-start | bytes 786440 | tf_op jit(solution)/shard_map/ppermute | solution.py:295
  116.7 9.4 %collective-permute-start.31 = (bf16[64,2048]{1,0:T(8,128)(2,1)S(1)}, bf16[64,2048]{1,0:T(8,128)(2,1)S(1)}, u32[]{:S(2)}, u32[]{:S(2)}) collective-permute-start(bf16[64,2048]{1,0:T(8,128)(2,1)S(1)} %get-tuple-element.83), channel_id=1, source_target_pairs={{0,4},{1,5},{2,0},{3,1},{4,8},{5,9},{6,2},{7,3},{8,12},{9,13},{10,... | collective-permute-start | bytes 786440 | tf_op jit(solution)/shard_map/ppermute | solution.py:295
  118.7 7.4 %collective-permute-start.33 = (bf16[64,2048]{1,0:T(8,128)(2,1)S(1)}, bf16[64,2048]{1,0:T(8,128)(2,1)S(1)}, u32[]{:S(2)}, u32[]{:S(2)}) collective-permute-start(bf16[64,2048]{1,0:T(8,128)(2,1)S(1)} %get-tuple-element.77), channel_id=1, source_target_pairs={{0,4},{1,5},{2,0},{3,1},{4,8},{5,9},{6,2},{7,3},{8,12},{9,13},{10,... | collective-permute-start | bytes 786440 | tf_op jit(solution)/shard_map/ppermute | solution.py:295
  118.8 7.3 %collective-permute-start.37 = (bf16[64,2048]{1,0:T(8,128)(2,1)S(1)}, bf16[64,2048]{1,0:T(8,128)(2,1)S(1)}, u32[]{:S(2)}, u32[]{:S(2)}) collective-permute-start(bf16[64,2048]{1,0:T(8,128)(2,1)S(1)} %get-tuple-element.76), channel_id=1, source_target_pairs={{0,2},{1,3},{2,6},{3,7},{4,0},{5,1},{6,10},{7,11},{8,4},{9,5},{10,... | collective-permute-start | bytes 786440 | tf_op jit(solution)/shard_map/ppermute | solution.py:295

commit v9 on v8

--- a/solution.py
+++ b/solution.py
@@ -319,28 +319,6 @@
     halves = range(2)
     size = frames // 2
     hidden_width = expert_out.shape[0]
-    expert_in = after(expert_in, normed_top)
-    gate_in, up_in = lax.optimization_barrier((expert_in[:, :hidden_width], expert_in[:, hidden_width:]))
-    sent = [to_x(normed_top), to_x(after(normed_bottom, gate_in))]
-
-    step = 1
-    while step < wide:
-        other = send(gates, lambda z, x, c: (z ^ step, x, c))
-        gates = jnp.where(
-            z & step == 0,
-            jnp.concatenate([gates, other], axis=1),
-            jnp.concatenate([other, gates], axis=1),
-        )
-        step *= 2
-    sent[1], gates = lax.optimization_barrier((sent[1], gates))
-    mine = (z * 2 + x) * 2 + core
-    pair = jnp.stack([mine, mine + 1 - 2 * core])
-    gates = jnp.sum(
-        jnp.where(pair[:, None] == jnp.arange(experts), gates[..., None, :], 0.0), axis=-1
-    )
-    gates = jnp.concatenate([gates[0], gates[1, ::-1]])
-    gates = lax.dynamic_slice_in_dim(jnp.concatenate([gates, gates]), place, ring, 0)
-
     columns = lax.optimization_barrier(
         jnp.where(
             core == 0,
@@ -348,11 +326,18 @@
             jnp.concatenate([out_other, out_proj], axis=1),
         )
     )
+    sent = [to_x(normed_top), to_x(after(normed_bottom, columns))]
 
     def project(rows):
         return jnp.dot(rows, columns, preferred_element_type=jnp.float32).astype(jnp.bfloat16)
 
     own = [project(normed_top), project(normed_bottom)]
+
+    def merge(gates, other, low):
+        return jnp.where(
+            low, jnp.concatenate([gates, other], axis=1), jnp.concatenate([other, gates], axis=1)
+        )
+
     rows, peer = [], None
     for h in halves:
         arrived = sent[h]
@@ -370,13 +355,35 @@
 
     far = ring // 2
     fore_at, back_at = {0: rows}, {0: rows}
+    gates, step = after(gates, sent[1]), 1
     for k in range(1, far):
+        if step < wide:
+            other = send(gates, lambda z, x, c: (z ^ step, x, c))
         fore_at[k] = [along(fore_at[k - 1][h], 1) for h in halves]
         back_at[k] = [along(back_at[k - 1][h], -1) for h in halves]
+        if step < wide:
+            other, back_at[k][1] = lax.optimization_barrier((other, back_at[k][1]))
+            gates, step = merge(gates, other, z & step == 0), 2 * step
+    while step < wide:
+        other = send(gates, lambda z, x, c: (z ^ step, x, c))
+        gates, step = merge(gates, other, z & step == 0), 2 * step
+    mine = (z * 2 + x) * 2 + core
+    pair = jnp.stack([mine, mine + 1 - 2 * core])
+    gates = jnp.sum(
+        jnp.where(pair[:, None] == jnp.arange(experts), gates[..., None, :], 0.0), axis=-1
+    )
+    gates = jnp.concatenate([gates[0], gates[1, ::-1]])
+    gates = lax.dynamic_slice_in_dim(jnp.concatenate([gates, gates]), place, ring, 0)
     last = [along(fore_at[far - 1][0], 1), along(back_at[far - 1][1], -1)]
 
     joined_in = jnp.concatenate(
-        [gate_in, in_other[:, :hidden_width], up_in, in_other[:, hidden_width:]], axis=1
+        [
+            expert_in[:, :hidden_width],
+            in_other[:, :hidden_width],
+            expert_in[:, hidden_width:],
+            in_other[:, hidden_width:],
+        ],
+        axis=1,
     )
     joined_down = jnp.concatenate([expert_out, down_other], axis=0)
     joined_in, joined_down = lax.optimization_barrier((joined_in, joined_down))
@@ -399,28 +406,24 @@
     total = run_experts(last, gates[far]).astype(jnp.bfloat16)
     fore, back = [along(total[:size], 1), None], [None, along(total[size:], -1)]
     ahead, behind = hop_experts(far - 1, total)
-    tie = total
+    groups = [((fore, 1, 1), (back, -1, 0)), ((fore, 1, 0), (back, -1, 1))]
     for k in range(far - 1, 0, -1):
-        if k > 1:
-            coming = hop_experts(k - 1, tie)
         before = ()
-        groups = [((fore, 1, ahead, h), (back, -1, behind, h)) for h in halves]
-        if k == far - 1:
-            groups = [((fore, 1, ahead, 1), (back, -1, behind, 0)), ((fore, 1, ahead, 0), (back, -1, behind, 1))]
         for group in groups:
             loads = []
-            for way, step, totals, h in group:
-                load = totals[h]
+            for way, step, h in group:
+                load = (ahead if step > 0 else behind)[h]
                 if way[h] is not None:
                     load = load + after(way[h], *before).astype(jnp.float32)
                 loads.append(load.astype(jnp.bfloat16))
-            before = loads
-            for (way, step, totals, h), load in zip(group, loads):
+            for (way, step, h), load in zip(group, loads):
                 way[h] = along(load, step)
-        tie = loads[0]
-        if k == 1:
-            coming = hop_experts(0, tie)
-            state = state_next(tie)
+            if not before:
+                coming = hop_experts(k - 1, loads[0])
+                before = (*loads, *coming[0], *coming[1])
+                if k == 1:
+                    state = state_next(loads[0])
+                    before += (state,)
         ahead, behind = coming
     out = []
     for h in halves:

time: 128 us -> 130 us (1.016)
  waiting for transfers between devices: 42.3 us -> 46.7 us
  starting transfers between devices: 42.1 us -> 39.8 us
  local copies, waits for them, and re-layouts: 4.53 us -> 2.68 us
  matrix products: 17.6 us -> 19.1 us
    ppermute x38, waiting for transfers between devices: 42.3 us -> 46.7 us  [send(): return lax.ppermute(value, axes, routes(wide, move))]
    dot_general x5, matrix products: 7.31 us -> 10.7 us  [run_experts(): jnp.dot(jnp.concatenate(parts), joined_in, preferred_element_type=jnp.flo...]
    ppermute x38, starting transfers between devices: 42.1 us -> 39.8 us  [send(): return lax.ppermute(value, axes, routes(wide, move))]
    dot_general x4, matrix products: 5.31 us -> 3.39 us  [project(): jnp.dot(rows, columns, preferred_element_type=jnp.float32)]
    slice x2, local copies, waits for them, and re-layouts: 2.24 us -> 0.36 us  [the longest x1 0.32 us: dense_experts(): expert_in[:, :hidden_width]]
    select_n x1, other arithmetic: 5.23 us -> 3.54 us  [dense_experts(): jnp.where(core == 0, jnp.concatenate([out_proj, out_other], axis=1), jnp....]
  transfers between devices with their start and end apart: 38 -> 38, of which waited for: 18 -> 19; matrix products, arithmetic and copies ran while one was open for 25% -> 21% of each run, Pallas kernels for 7% -> 7%
where the time goes in v9:
time: 130 us
  waiting for transfers between devices  46.7 us (36%)
  starting transfers between devices  39.8 us (31%)
  matrix products  19.1 us (15%)
  other arithmetic  11.2 us (9%)
  Pallas kernels  8.93 us (7%)
  local copies, waits for them, and re-layouts  2.68 us (2%)
    ppermute x38, waiting for transfers between devices, send(): return lax.ppermute(value, axes, routes(wide, move))  46.7 us
    ppermute x38, starting transfers between devices, send(): return lax.ppermute(value, axes, routes(wide, move))  39.8 us
    dot_general x5, matrix products, run_experts(): jnp.dot(jnp.concatenate(parts), joined_in, preferred_element_type=jnp.flo...  10.7 us
    pallas_call x1, Pallas kernels, ssm_mixer(): pl.pallas_call(mixer_kernel, grid=(steps,), in_specs=[pl.BlockSpec(memory...  5.36 us
    dot_general x5, matrix products, run_experts(): return jnp.dot(hidden, joined_down, preferred_element_type=jnp.float32)  5.05 us
    pallas_call x1, Pallas kernels, state_next(): pl.pallas_call(state_kernel, grid=(steps,), in_specs=[column, whole, per_...  3.58 us
    select_n x1, other arithmetic, dense_experts(): jnp.where(core == 0, jnp.concatenate([out_proj, out_other], axis=1), jnp....  3.54 us
    dot_general x4, matrix products, project(): jnp.dot(rows, columns, preferred_element_type=jnp.float32)  3.39 us
  transfers between devices with their start and end apart: 38, of which 19 were waited for; matrix products, arithmetic and copies ran while one was open for 21% of the time, Pallas kernels for 7%

profile of v9, /device:TPU:0, one launch (start us, length us, event | category | flops | bytes accessed | tf_op | source)
XLA Modules:
  0.0 129.5 jit_solution(8529431454687103185)
XLA Ops:
  2.0 2.6 %collective-permute-start = (f32[128,16]{0,1:T(8,128)S(1)}, f32[128,16]{0,1:T(8,128)S(1)}, u32[]{:S(2)}, u32[]{:S(2)}) collective-permute-start(f32[128,16]{0,1:T(8,128)S(1)} %select_reduce_fusion.1), channel_id=1, source_target_pairs={{0,2},{1,3},{2,0},{3,1},{4,6},{5,7},{6,4},{7,5},{8,10},{9,11},{10,... | collective-permute-start | bytes 24584 | tf_op jit(solution)/shard_map/ppermute | solution.py:295
  5.1 5.4 %mixer.1 = (bf16[64,2048]{1,0:T(8,128)(2,1)}, bf16[64,2048]{1,0:T(8,128)(2,1)}) custom-call(f32[32]{0:T(128)} %skip_ref.1, bf16[128,2048]{1,0:T(8,128)(2,1)} %x_ref.2, bf16[128,2048]{1,0:T(8,128)(2,1)} %z_ref.1, bf16[128,128]{1,0:T(8,128)(2,1)} %b_ref.3, bf16[128,128]{1,0:T(8,128)(2,1)} %c_ref.1, f32[32,128]{1,0:T(8,128)} %bitcast.67, f32[1,32]{1,0:T(1,128)} %bitcast.69, ...), custom_call_target="tpu_custom_call" | custom-call | flops 400000000 | bytes 6000000 | tf_op jit(solution)/shard_map/mixer/pallas_call | solution.py:159
  10.6 3.5 %maximum_select_fusion = bf16[2048,1024]{1,0:T(8,128)(2,1)S(1)} fusion(bf16[2048,512]{1,0:T(8,128)(2,1)} %collective-permute-done.1, bf16[2048,512]{1,0:T(8,128)(2,1)S(1)} %copy-done.7, pred[]{:T(512)S(6)} %eq.47), kind=kLoop, calls=%fused_computation.1 | loop fusion | flops 18874368 | bytes 8388609 | tf_op jit(solution)/shard_map/jit(_where)/select_n | solution.py:323
  14.2 2.0 %collective-permute-start.11 = (bf16[64,2048]{1,0:T(8,128)(2,1)S(1)}, bf16[64,2048]{1,0:T(8,128)(2,1)S(1)}, u32[]{:S(2)}, u32[]{:S(2)}) collective-permute-start(bf16[64,2048]{1,0:T(8,128)(2,1)S(1)} %copy-done.9), channel_id=1, source_target_pairs={{0,2},{1,3},{2,0},{3,1},{4,6},{5,7},{6,4},{7,5},{8,10},{9,11},{10,... | collective-permute-start | bytes 786440 | tf_op jit(solution)/shard_map/ppermute | solution.py:295
  17.1 2.8 %collective-permute-done.2 = bf16[64,2048]{1,0:T(8,128)(2,1)S(1)} collective-permute-done((bf16[64,2048]{1,0:T(8,128)(2,1)}, bf16[64,2048]{1,0:T(8,128)(2,1)S(1)}, u32[]{:S(2)}, u32[]{:S(2)}) %collective-permute-start.2) | collective-permute-done | bytes 262176 | tf_op jit(solution)/shard_map/ppermute | solution.py:295
  21.7 3.8 %collective-permute-done.11 = bf16[64,2048]{1,0:T(8,128)(2,1)S(1)} collective-permute-done((bf16[64,2048]{1,0:T(8,128)(2,1)S(1)}, bf16[64,2048]{1,0:T(8,128)(2,1)S(1)}, u32[]{:S(2)}, u32[]{:S(2)}) %collective-permute-start.11) | collective-permute-done | bytes 262176 | tf_op jit(solution)/shard_map/ppermute | solution.py:295
  27.5 1.6 %collective-permute-start.7 = (bf16[64,2048]{1,0:T(8,128)(2,1)S(1)}, bf16[64,2048]{1,0:T(8,128)(2,1)}, u32[]{:S(2)}, u32[]{:S(2)}) collective-permute-start(bf16[64,2048]{1,0:T(8,128)(2,1)S(1)} %maximum_select_fusion.1), channel_id=1, source_target_pairs={{0,4},{1,5},{2,0},{3,1},{4,8},{5,9},{6,2},{7,3},{8,12},{9,13},{10,... | collective-permute-start | bytes 786440 | tf_op jit(solution)/shard_map/ppermute | solution.py:295
  29.6 3.2 %collective-permute-done.13 = bf16[64,1024]{1,0:T(8,128)(2,1)S(1)} collective-permute-done((bf16[64,1024]{1,0:T(8,128)(2,1)S(1)}, bf16[64,1024]{1,0:T(8,128)(2,1)S(1)}, u32[]{:S(2)}, u32[]{:S(2)}) %collective-permute-start.13) | collective-permute-done | bytes 131104 | tf_op jit(solution)/shard_map/ppermute | solution.py:295
  33.8 2.9 %collective-permute-done.12 = f32[2,1,128,16]{2,3,1,0:T(8,128)S(1)} collective-permute-done((f32[2,1,128,16]{2,3,1,0:T(8,128)S(1)}, f32[2,1,128,16]{2,3,1,0:T(8,128)S(1)}, u32[]{:S(2)}, u32[]{:S(2)}) %collective-permute-start.12) | collective-permute-done | bytes 16416 | tf_op jit(solution)/shard_map/ppermute | solution.py:295
  37.1 2.0 %collective-permute-start.21 = (bf16[64,2048]{1,0:T(8,128)(2,1)}, bf16[64,2048]{1,0:T(8,128)(2,1)}, u32[]{:S(2)}, u32[]{:S(2)}) collective-permute-start(bf16[64,2048]{1,0:T(8,128)(2,1)} %maximum_select_fusion.2), channel_id=1, source_target_pairs={{0,4},{1,5},{2,0},{3,1},{4,8},{5,9},{6,2},{7,3},{8,12},{9,13},{10,... | collective-permute-start | bytes 786440 | tf_op jit(solution)/shard_map/ppermute | solution.py:295
  39.1 1.1 collective-permute-start.8
  40.2 3.1 %collective-permute-done.14 = bf16[64,2048]{1,0:T(8,128)(2,1)} collective-permute-done((bf16[64,2048]{1,0:T(8,128)(2,1)}, bf16[64,2048]{1,0:T(8,128)(2,1)}, u32[]{:S(2)}, u32[]{:S(2)}) %collective-permute-start.14) | collective-permute-done | bytes 262176 | tf_op jit(solution)/shard_map/ppermute | solution.py:295
  43.7 1.4 %collective-permute-start.16 = (bf16[64,2048]{1,0:T(8,128)(2,1)}, bf16[64,2048]{1,0:T(8,128)(2,1)S(1)}, u32[]{:S(2)}, u32[]{:S(2)}) collective-permute-start(bf16[64,2048]{1,0:T(8,128)(2,1)} %collective-permute-done.14), channel_id=1, source_target_pairs={{0,2},{1,3},{2,6},{3,7},{4,0},{5,1},{6,10},{7,11},{8,4},{9,5},{10,... | collective-permute-start | bytes 786440 | tf_op jit(solution)/shard_map/ppermute | solution.py:295
  45.1 4.3 %collective-permute-done.8 = bf16[64,2048]{1,0:T(8,128)(2,1)} collective-permute-done((bf16[64,2048]{1,0:T(8,128)(2,1)}, bf16[64,2048]{1,0:T(8,128)(2,1)}, u32[]{:S(2)}, u32[]{:S(2)}) %collective-permute-start.8) | collective-permute-done | bytes 262176 | tf_op jit(solution)/shard_map/ppermute | solution.py:295
  49.4 2.6 %collective-permute-start.15 = (f32[2,2,128,16]{2,3,1,0:T(8,128)S(1)}, f32[2,2,128,16]{2,3,1,0:T(8,128)S(1)}, u32[]{:S(2)}, u32[]{:S(2)}) collective-permute-start(f32[2,2,128,16]{2,3,1,0:T(8,128)S(1)} %maximum_select_fusion.4), channel_id=1, source_target_pairs={{0,8},{1,9},{2,10},{3,11},{4,12},{5,13},{6,14},{7,15},{8,0},{9,1},... | collective-permute-start | bytes 98312 | tf_op jit(solution)/shard_map/ppermute | solution.py:295
  52.0 2.3 %collective-permute-start.9 = (bf16[64,2048]{1,0:T(8,128)(2,1)}, bf16[64,2048]{1,0:T(8,128)(2,1)S(1)}, u32[]{:S(2)}, u32[]{:S(2)}) collective-permute-start(bf16[64,2048]{1,0:T(8,128)(2,1)} %collective-permute-done.8), channel_id=1, source_target_pairs={{0,4},{1,5},{2,0},{3,1},{4,8},{5,9},{6,2},{7,3},{8,12},{9,13},{10,... | collective-permute-start | bytes 786440 | tf_op jit(solution)/shard_map/ppermute | solution.py:295
  54.3 1.0 collective-permute-start.22
  55.3 2.2 %pad_maximum_fusion.1 = bf16[768,2048]{1,0:T(8,128)(2,1)S(1)} fusion(bf16[384,2048]{1,0:T(8,128)(2,1)} %collective-permute-done.20, bf16[384,2048]{1,0:T(8,128)(2,1)} %bitcast.76), kind=kLoop, calls=%fused_computation.2 | loop fusion | flops 6291456 | bytes 6291456 | tf_op jit(solution)/shard_map/concatenate | solution.py:388
  58.7 2.7 %collective-permute-done.9 = bf16[64,2048]{1,0:T(8,128)(2,1)S(1)} collective-permute-done((bf16[64,2048]{1,0:T(8,128)(2,1)}, bf16[64,2048]{1,0:T(8,128)(2,1)S(1)}, u32[]{:S(2)}, u32[]{:S(2)}) %collective-permute-start.9) | collective-permute-done | bytes 262176 | tf_op jit(solution)/shard_map/ppermute | solution.py:295
  61.4 2.3 %collective-permute-start.10 = (bf16[64,2048]{1,0:T(8,128)(2,1)S(1)}, bf16[64,2048]{1,0:T(8,128)(2,1)S(1)}, u32[]{:S(2)}, u32[]{:S(2)}) collective-permute-start(bf16[64,2048]{1,0:T(8,128)(2,1)S(1)} %collective-permute-done.9), channel_id=1, source_target_pairs={{0,4},{1,5},{2,0},{3,1},{4,8},{5,9},{6,2},{7,3},{8,12},{9,13},{10,... | collective-permute-start | bytes 786440 | tf_op jit(solution)/shard_map/ppermute | solution.py:295
  63.7 3.3 %collective-permute-done.22 = bf16[64,2048]{1,0:T(8,128)(2,1)S(1)} collective-permute-done((bf16[64,2048]{1,0:T(8,128)(2,1)}, bf16[64,2048]{1,0:T(8,128)(2,1)S(1)}, u32[]{:S(2)}, u32[]{:S(2)}) %collective-permute-start.22) | collective-permute-done | bytes 262176 | tf_op jit(solution)/shard_map/ppermute | solution.py:295
  67.0 2.3 %collective-permute-start.23 = (bf16[64,2048]{1,0:T(8,128)(2,1)S(1)}, bf16[64,2048]{1,0:T(8,128)(2,1)S(1)}, u32[]{:S(2)}, u32[]{:S(2)}) collective-permute-start(bf16[64,2048]{1,0:T(8,128)(2,1)S(1)} %collective-permute-done.22), channel_id=1, source_target_pairs={{0,4},{1,5},{2,0},{3,1},{4,8},{5,9},{6,2},{7,3},{8,12},{9,13},{10,... | collective-permute-start | bytes 786440 | tf_op jit(solution)/shard_map/ppermute | solution.py:295
  69.6 2.2 %fusion.90 = (bf16[2048,384]{1,0:T(8,128)(2,1)S(1)}, bf16[2048,384]{1,0:T(8,128)(2,1)S(1)}) fusion(bf16[2048,768]{1,0:T(8,128)(2,1)} %collective-permute-done.19), kind=kLoop, calls=%fused_computation.149 | loop fusion | bytes 6291456 | tf_op jit(solution)/shard_map/slice | solution.py:382
  72.6 5.6 %collective-permute-done.18 = bf16[64,2048]{1,0:T(8,128)(2,1)S(1)} collective-permute-done((bf16[64,2048]{1,0:T(8,128)(2,1)S(1)}, bf16[64,2048]{1,0:T(8,128)(2,1)S(1)}, u32[]{:S(2)}, u32[]{:S(2)}) %collective-permute-start.18) | collective-permute-done | bytes 262176 | tf_op jit(solution)/shard_map/ppermute | solution.py:295
  78.3 1.0 fusion.32
  80.1 1.8 %fusion = f32[256,1536]{1,0:T(8,128)S(1)} fusion(bf16[2048,1536]{1,0:T(8,128)(2,1)S(1)} %pad_maximum_fusion, bf16[64,2048]{1,0:T(8,128)(2,1)S(1)} %collective-permute-done.23, bf16[64,2048]{1,0:T(8,128)(2,1)S(1)} %collective-permute-done.9, bf16[64,2048]{1,0:T(8,128)(2,1)S(1)} %collective-permute-done.17, bf16[64,2048]{1,0:T(8,128)(2,1)S(1)} %collective-permute-done.6), kind=kOutput, calls=%fused_computation.8 | convolution fusion | flops 1614807040 | bytes 8912896 | tf_op jit(solution)/shard_map/dot_general | solution.py:393
  81.9 1.2 fusion.97
  83.1 1.1 collective-permute-start.24
  84.3 1.1 collective-permute-start.28
  85.4 2.0 %collective-permute-start.26 = (bf16[64,2048]{1,0:T(8,128)(2,1)S(1)}, bf16[64,2048]{1,0:T(8,128)(2,1)S(1)}, u32[]{:S(2)}, u32[]{:S(2)}) collective-permute-start(bf16[64,2048]{1,0:T(8,128)(2,1)S(1)} %get-tuple-element.100), channel_id=1, source_target_pairs={{0,4},{1,5},{2,0},{3,1},{4,8},{5,9},{6,2},{7,3},{8,12},{9,13},{10,... | collective-permute-start | bytes 786440 | tf_op jit(solution)/shard_map/ppermute | solution.py:295
  87.3 2.8 %fusion.8 = f32[256,1536]{1,0:T(8,128)S(1)} fusion(bf16[2048,1536]{1,0:T(8,128)(2,1)S(1)} %pad_maximum_fusion, bf16[64,2048]{1,0:T(8,128)(2,1)S(1)} %collective-permute-done.22, bf16[64,2048]{1,0:T(8,128)(2,1)} %collective-permute-done.8, bf16[64,2048]{1,0:T(8,128)(2,1)S(1)} %collective-permute-done.16, bf16[64,2048]{1,0:T(8,128)(2,1)} %collective-permute-done.5), kind=kOutput, calls=%fused_computation.16 | convolution fusion | flops 1614807040 | bytes 8912896 | tf_op jit(solution)/shard_map/dot_general | solution.py:393
  90.2 1.2 fusion.42
  91.4 1.0 collective-permute-done.24
  92.4 1.1 collective-permute-done.28
  93.6 1.1 collective-permute-start.25
  95.7 2.0 %collective-permute-done.34 = bf16[64,2048]{1,0:T(8,128)(2,1)S(1)} collective-permute-done((bf16[64,2048]{1,0:T(8,128)(2,1)S(1)}, bf16[64,2048]{1,0:T(8,128)(2,1)S(1)}, u32[]{:S(2)}, u32[]{:S(2)}) %collective-permute-start.34) | collective-permute-done | bytes 262176 | tf_op jit(solution)/shard_map/ppermute | solution.py:295
  98.3 2.0 %collective-permute-start.27 = (bf16[64,2048]{1,0:T(8,128)(2,1)S(1)}, bf16[64,2048]{1,0:T(8,128)(2,1)S(1)}, u32[]{:S(2)}, u32[]{:S(2)}) collective-permute-start(bf16[64,2048]{1,0:T(8,128)(2,1)S(1)} %get-tuple-element.80), channel_id=1, source_target_pairs={{0,4},{1,5},{2,0},{3,1},{4,8},{5,9},{6,2},{7,3},{8,12},{9,13},{10,... | collective-permute-start | bytes 786440 | tf_op jit(solution)/shard_map/ppermute | solution.py:295
  100.2 3.0 %fusion.16 = f32[256,1536]{1,0:T(8,128)S(1)} fusion(bf16[2048,1536]{1,0:T(8,128)(2,1)S(1)} %pad_maximum_fusion, bf16[64,2048]{1,0:T(8,128)(2,1)} %collective-permute-done.21, bf16[64,2048]{1,0:T(8,128)(2,1)} %collective-permute-done.7, bf16[64,2048]{1,0:T(8,128)(2,1)} %collective-permute-done.14, bf16[64,2048]{1,0:T(8,128)(2,1)} %collective-permute-done.4), kind=kOutput, calls=%fused_computation.24 | convolution fusion | flops 1614807040 | bytes 8912896 | tf_op jit(solution)/shard_map/dot_general | solution.py:393
  103.2 1.2 fusion.44
  105.7 3.0 %collective-permute-done.35 = bf16[64,2048]{1,0:T(8,128)(2,1)S(1)} collective-permute-done((bf16[64,2048]{1,0:T(8,128)(2,1)S(1)}, bf16[64,2048]{1,0:T(8,128)(2,1)S(1)}, u32[]{:S(2)}, u32[]{:S(2)}) %collective-permute-start.35) | collective-permute-done | bytes 262176 | tf_op jit(solution)/shard_map/ppermute | solution.py:295
  108.8 1.7 %collective-permute-start.36 = (bf16[64,2048]{1,0:T(8,128)(2,1)S(1)}, bf16[64,2048]{1,0:T(8,128)(2,1)S(1)}, u32[]{:S(2)}, u32[]{:S(2)}) collective-permute-start(bf16[64,2048]{1,0:T(8,128)(2,1)S(1)} %get-tuple-element.79), channel_id=1, source_target_pairs={{0,2},{1,3},{2,6},{3,7},{4,0},{5,1},{6,10},{7,11},{8,4},{9,5},{10,... | collective-permute-start | bytes 786440 | tf_op jit(solution)/shard_map/ppermute | solution.py:295
  110.5 3.6 %state.1 = f32[2048,128]{1,0:T(8,128)} custom-call(bf16[128,2048]{1,0:T(8,128)(2,1)S(1)} %copy-done.1, bf16[128,128]{1,0:T(8,128)(2,1)S(1)} %copy-done.2, f32[32,128]{1,0:T(8,128)S(1)} %bitcast.68, f32[1,32]{1,0:T(1,128)S(1)} %bitcast.70, f32[1,32]{1,0:T(1,128)S(1)} %bitcast.72, f32[2048,128]{1,0:T(8,128)S(1)} %bitcast.66), custom_call_target="tpu_custom_call" | custom-call | flops 70000000 | bytes 3000000 | tf_op jit(solution)/shard_map/state/pallas_call | solution.py:198
  114.5 1.7 %collective-permute-start.32 = (bf16[64,2048]{1,0:T(8,128)(2,1)S(1)}, bf16[64,2048]{1,0:T(8,128)(2,1)S(1)}, u32[]{:S(2)}, u32[]{:S(2)}) collective-permute-start(bf16[64,2048]{1,0:T(8,128)(2,1)S(1)} %get-tuple-element.82), channel_id=1, source_target_pairs={{0,2},{1,3},{2,6},{3,7},{4,0},{5,1},{6,10},{7,11},{8,4},{9,5},{10,... | collective-permute-start | bytes 786440 | tf_op jit(solution)/shard_map/ppermute | solution.py:295
  116.1 2.0 %fusion.36 = f32[128,1536]{1,0:T(8,128)S(1)} fusion(bf16[2048,1536]{1,0:T(8,128)(2,1)S(1)} %pad_maximum_fusion, bf16[64,2048]{1,0:T(8,128)(2,1)} %maximum_select_fusion.2, bf16[64,2048]{1,0:T(8,128)(2,1)S(1)} %maximum_select_fusion.1), kind=kOutput, calls=%fused_computation.49 | convolution fusion | flops 806354944 | bytes 7602176 | tf_op jit(solution)/shard_map/dot_general | solution.py:393
  118.9 1.6 %collective-permute-done.29 = bf16[64,2048]{1,0:T(8,128)(2,1)S(1)} collective-permute-done((bf16[64,2048]{1,0:T(8,128)(2,1)S(1)}, bf16[64,2048]{1,0:T(8,128)(2,1)S(1)}, u32[]{:S(2)}, u32[]{:S(2)}) %collective-permute-start.29) | collective-permute-done | bytes 262176 | tf_op jit(solution)/shard_map/ppermute | solution.py:295
  121.0 1.7 %collective-permute-start.37 = (bf16[64,2048]{1,0:T(8,128)(2,1)S(1)}, bf16[64,2048]{1,0:T(8,128)(2,1)S(1)}, u32[]{:S(2)}, u32[]{:S(2)}) collective-permute-start(bf16[64,2048]{1,0:T(8,128)(2,1)S(1)} %get-tuple-element.77), channel_id=1, source_target_pairs={{0,2},{1,3},{2,6},{3,7},{4,0},{5,1},{6,10},{7,11},{8,4},{9,5},{10,... | collective-permute-start | bytes 786440 | tf_op jit(solution)/shard_map/ppermute | solution.py:295
  122.7 4.3 %collective-permute-done.31 = bf16[64,2048]{1,0:T(8,128)(2,1)S(1)} collective-permute-done((bf16[64,2048]{1,0:T(8,128)(2,1)S(1)}, bf16[64,2048]{1,0:T(8,128)(2,1)S(1)}, u32[]{:S(2)}, u32[]{:S(2)}) %collective-permute-start.31) | collective-permute-done | bytes 262176 | tf_op jit(solution)/shard_map/ppermute | solution.py:295
  127.4 1.3 add_convert_fusion.3
  (96 shorter events, 17.6 us)
Async XLA Ops:
  0.6 10.0 %copy-start.7 = (bf16[2048,512]{1,0:T(8,128)(2,1)S(1)}, bf16[2048,512]{1,0:T(8,128)(2,1)}, u32[]{:S(2)}) copy-start(bf16[2048,512]{1,0:T(8,128)(2,1)} %param.25) | copy-start | bytes 6291460
  0.6 10.0 %collective-permute-start.1 = (bf16[2048,512]{1,0:T(8,128)(2,1)}, bf16[2048,512]{1,0:T(8,128)(2,1)}, u32[]{:S(2)}, u32[]{:S(2)}) collective-permute-start(bf16[2048,512]{1,0:T(8,128)(2,1)} %param.25), channel_id=1, source_target_pairs={{0,1},{1,0},{2,3},{3,2},{4,5},{5,4},{6,7},{7,6},{8,9},{9,8},{10,11... | collective-permute-start | bytes 6291464 | tf_op jit(solution)/shard_map/ppermute | solution.py:295
  2.0 8.5 %collective-permute-start = (f32[128,16]{0,1:T(8,128)S(1)}, f32[128,16]{0,1:T(8,128)S(1)}, u32[]{:S(2)}, u32[]{:S(2)}) collective-permute-start(f32[128,16]{0,1:T(8,128)S(1)} %select_reduce_fusion.1), channel_id=1, source_target_pairs={{0,2},{1,3},{2,0},{3,1},{4,6},{5,7},{6,4},{7,5},{8,10},{9,11},{10,... | collective-permute-start | bytes 24584 | tf_op jit(solution)/shard_map/ppermute | solution.py:295
  4.6 65.0 %collective-permute-start.19 = (bf16[2048,768]{1,0:T(8,128)(2,1)}, bf16[2048,768]{1,0:T(8,128)(2,1)}, u32[]{:S(2)}, u32[]{:S(2)}) collective-permute-start(bf16[2048,768]{1,0:T(8,128)(2,1)} %bitcast.73), channel_id=1, source_target_pairs={{0,1},{1,0},{2,3},{3,2},{4,5},{5,4},{6,7},{7,6},{8,9},{9,8},{10,11... | collective-permute-start | bytes 9437192 | tf_op jit(solution)/shard_map/ppermute | solution.py:295
  4.7 39.0 %collective-permute-start.20 = (bf16[384,2048]{1,0:T(8,128)(2,1)}, bf16[384,2048]{1,0:T(8,128)(2,1)}, u32[]{:S(2)}, u32[]{:S(2)}) collective-permute-start(bf16[384,2048]{1,0:T(8,128)(2,1)} %bitcast.75), channel_id=1, source_target_pairs={{0,1},{1,0},{2,3},{3,2},{4,5},{5,4},{6,7},{7,6},{8,9},{9,8},{10,11... | collective-permute-start | bytes 4718600 | tf_op jit(solution)/shard_map/ppermute | solution.py:295
  10.5 9.4 %collective-permute-start.2 = (bf16[64,2048]{1,0:T(8,128)(2,1)}, bf16[64,2048]{1,0:T(8,128)(2,1)S(1)}, u32[]{:S(2)}, u32[]{:S(2)}) collective-permute-start(bf16[64,2048]{1,0:T(8,128)(2,1)} %get-tuple-element.39), channel_id=1, source_target_pairs={{0,2},{1,3},{2,0},{3,1},{4,6},{5,7},{6,4},{7,5},{8,10},{9,11},{10,... | collective-permute-start | bytes 786440 | tf_op jit(solution)/shard_map/ppermute | solution.py:295
  10.6 3.6 %copy-start.9 = (bf16[64,2048]{1,0:T(8,128)(2,1)S(1)}, bf16[64,2048]{1,0:T(8,128)(2,1)}, u32[]{:S(2)}) copy-start(bf16[64,2048]{1,0:T(8,128)(2,1)} %get-tuple-element.42) | copy-start | bytes 786436
  14.2 11.3 %collective-permute-start.11 = (bf16[64,2048]{1,0:T(8,128)(2,1)S(1)}, bf16[64,2048]{1,0:T(8,128)(2,1)S(1)}, u32[]{:S(2)}, u32[]{:S(2)}) collective-permute-start(bf16[64,2048]{1,0:T(8,128)(2,1)S(1)} %copy-done.9), channel_id=1, source_target_pairs={{0,2},{1,3},{2,0},{3,1},{4,6},{5,7},{6,4},{7,5},{8,10},{9,11},{10,... | collective-permute-start | bytes 786440 | tf_op jit(solution)/shard_map/ppermute | solution.py:295
  17.0 3.8 %copy-start.8 = (bf16[64,2048]{1,0:T(8,128)(2,1)S(1)}, bf16[64,2048]{1,0:T(8,128)(2,1)}, u32[]{:S(2)}) copy-start(bf16[64,2048]{1,0:T(8,128)(2,1)} %get-tuple-element.39) | copy-start | bytes 786436
  20.8 6.7 %collective-permute-start.3 = (bf16[64,1024]{1,0:T(8,128)(2,1)S(1)}, bf16[64,1024]{1,0:T(8,128)(2,1)S(1)}, u32[]{:S(2)}, u32[]{:S(2)}) collective-permute-start(bf16[64,1024]{1,0:T(8,128)(2,1)S(1)} %convolution_convert_fusion.3), channel_id=1, source_target_pairs={{0,2},{1,3},{2,0},{3,1},{4,6},{5,7},{6,4},{7,5},{8,10},{9,11},{10,... | collective-permute-start | bytes 393224 | tf_op jit(solution)/shard_map/ppermute | solution.py:295
  21.7 14.9 %copy-start.6 = (bf16[1,2048,768]{2,1,0:T(8,128)(2,1)S(1)}, bf16[1,2048,768]{2,1,0:T(8,128)(2,1)}, u32[]{:S(2)}) copy-start(bf16[1,2048,768]{2,1,0:T(8,128)(2,1)} %param.26) | copy-start | bytes 9437188
  26.4 6.4 %collective-permute-start.13 = (bf16[64,1024]{1,0:T(8,128)(2,1)S(1)}, bf16[64,1024]{1,0:T(8,128)(2,1)S(1)}, u32[]{:S(2)}, u32[]{:S(2)}) collective-permute-start(bf16[64,1024]{1,0:T(8,128)(2,1)S(1)} %convolution_convert_fusion.1), channel_id=1, source_target_pairs={{0,2},{1,3},{2,0},{3,1},{4,6},{5,7},{6,4},{7,5},{8,10},{9,11},{10,... | collective-permute-start | bytes 393224 | tf_op jit(solution)/shard_map/ppermute | solution.py:295
  27.5 9.6 %collective-permute-start.7 = (bf16[64,2048]{1,0:T(8,128)(2,1)S(1)}, bf16[64,2048]{1,0:T(8,128)(2,1)}, u32[]{:S(2)}, u32[]{:S(2)}) collective-permute-start(bf16[64,2048]{1,0:T(8,128)(2,1)S(1)} %maximum_select_fusion.1), channel_id=1, source_target_pairs={{0,4},{1,5},{2,0},{3,1},{4,8},{5,9},{6,2},{7,3},{8,12},{9,13},{10,... | collective-permute-start | bytes 786440 | tf_op jit(solution)/shard_map/ppermute | solution.py:295
  29.2 10.0 %collective-permute-start.4 = (bf16[64,2048]{1,0:T(8,128)(2,1)S(1)}, bf16[64,2048]{1,0:T(8,128)(2,1)}, u32[]{:S(2)}, u32[]{:S(2)}) collective-permute-start(bf16[64,2048]{1,0:T(8,128)(2,1)S(1)} %maximum_select_fusion.1), channel_id=1, source_target_pairs={{0,2},{1,3},{2,6},{3,7},{4,0},{5,1},{6,10},{7,11},{8,4},{9,5},{10,... | collective-permute-start | bytes 786440 | tf_op jit(solution)/shard_map/ppermute | solution.py:295
  32.8 3.9 %collective-permute-start.12 = (f32[2,1,128,16]{2,3,1,0:T(8,128)S(1)}, f32[2,1,128,16]{2,3,1,0:T(8,128)S(1)}, u32[]{:S(2)}, u32[]{:S(2)}) collective-permute-start(f32[2,1,128,16]{2,3,1,0:T(8,128)S(1)} %maximum_select_fusion.5), channel_id=1, source_target_pairs={{0,4},{1,5},{2,6},{3,7},{4,0},{5,1},{6,2},{7,3},{8,12},{9,13},{10,... | collective-permute-start | bytes 49160 | tf_op jit(solution)/shard_map/ppermute | solution.py:295
  36.7 6.7 %collective-permute-start.14 = (bf16[64,2048]{1,0:T(8,128)(2,1)}, bf16[64,2048]{1,0:T(8,128)(2,1)}, u32[]{:S(2)}, u32[]{:S(2)}) collective-permute-start(bf16[64,2048]{1,0:T(8,128)(2,1)} %maximum_select_fusion.2), channel_id=1, source_target_pairs={{0,2},{1,3},{2,6},{3,7},{4,0},{5,1},{6,10},{7,11},{8,4},{9,5},{10,... | collective-permute-start | bytes 786440 | tf_op jit(solution)/shard_map/ppermute | solution.py:295
  37.1 17.2 %collective-permute-start.21 = (bf16[64,2048]{1,0:T(8,128)(2,1)}, bf16[64,2048]{1,0:T(8,128)(2,1)}, u32[]{:S(2)}, u32[]{:S(2)}) collective-permute-start(bf16[64,2048]{1,0:T(8,128)(2,1)} %maximum_select_fusion.2), channel_id=1, source_target_pairs={{0,4},{1,5},{2,0},{3,1},{4,8},{5,9},{6,2},{7,3},{8,12},{9,13},{10,... | collective-permute-start | bytes 786440 | tf_op jit(solution)/shard_map/ppermute | solution.py:295
  39.1 10.2 %collective-permute-start.8 = (bf16[64,2048]{1,0:T(8,128)(2,1)}, bf16[64,2048]{1,0:T(8,128)(2,1)}, u32[]{:S(2)}, u32[]{:S(2)}) collective-permute-start(bf16[64,2048]{1,0:T(8,128)(2,1)} %collective-permute-done.7), channel_id=1, source_target_pairs={{0,4},{1,5},{2,0},{3,1},{4,8},{5,9},{6,2},{7,3},{8,12},{9,13},{10,... | collective-permute-start | bytes 786440 | tf_op jit(solution)/shard_map/ppermute | solution.py:295
  43.4 8.6 %collective-permute-start.5 = (bf16[64,2048]{1,0:T(8,128)(2,1)}, bf16[64,2048]{1,0:T(8,128)(2,1)}, u32[]{:S(2)}, u32[]{:S(2)}) collective-permute-start(bf16[64,2048]{1,0:T(8,128)(2,1)} %collective-permute-done.4), channel_id=1, source_target_pairs={{0,2},{1,3},{2,6},{3,7},{4,0},{5,1},{6,10},{7,11},{8,4},{9,5},{10,... | collective-permute-start | bytes 786440 | tf_op jit(solution)/shard_map/ppermute | solution.py:295
  43.7 14.9 %collective-permute-start.16 = (bf16[64,2048]{1,0:T(8,128)(2,1)}, bf16[64,2048]{1,0:T(8,128)(2,1)S(1)}, u32[]{:S(2)}, u32[]{:S(2)}) collective-permute-start(bf16[64,2048]{1,0:T(8,128)(2,1)} %collective-permute-done.14), channel_id=1, source_target_pairs={{0,2},{1,3},{2,6},{3,7},{4,0},{5,1},{6,10},{7,11},{8,4},{9,5},{10,... | collective-permute-start | bytes 786440 | tf_op jit(solution)/shard_map/ppermute | solution.py:295
  49.4 8.3 %collective-permute-start.15 = (f32[2,2,128,16]{2,3,1,0:T(8,128)S(1)}, f32[2,2,128,16]{2,3,1,0:T(8,128)S(1)}, u32[]{:S(2)}, u32[]{:S(2)}) collective-permute-start(f32[2,2,128,16]{2,3,1,0:T(8,128)S(1)} %maximum_select_fusion.4), channel_id=1, source_target_pairs={{0,8},{1,9},{2,10},{3,11},{4,12},{5,13},{6,14},{7,15},{8,0},{9,1},... | collective-permute-start | bytes 98312 | tf_op jit(solution)/shard_map/ppermute | solution.py:295
  52.0 9.5 %collective-permute-start.9 = (bf16[64,2048]{1,0:T(8,128)(2,1)}, bf16[64,2048]{1,0:T(8,128)(2,1)S(1)}, u32[]{:S(2)}, u32[]{:S(2)}) collective-permute-start(bf16[64,2048]{1,0:T(8,128)(2,1)} %collective-permute-done.8), channel_id=1, source_target_pairs={{0,4},{1,5},{2,0},{3,1},{4,8},{5,9},{6,2},{7,3},{8,12},{9,13},{10,... | collective-permute-start | bytes 786440 | tf_op jit(solution)/shard_map/ppermute | solution.py:295
  54.3 12.8 %collective-permute-start.22 = (bf16[64,2048]{1,0:T(8,128)(2,1)}, bf16[64,2048]{1,0:T(8,128)(2,1)S(1)}, u32[]{:S(2)}, u32[]{:S(2)}) collective-permute-start(bf16[64,2048]{1,0:T(8,128)(2,1)} %collective-permute-done.21), channel_id=1, source_target_pairs={{0,4},{1,5},{2,0},{3,1},{4,8},{5,9},{6,2},{7,3},{8,12},{9,13},{10,... | collective-permute-start | bytes 786440 | tf_op jit(solution)/shard_map/ppermute | solution.py:295
  57.6 22.4 %collective-permute-start.6 = (bf16[64,2048]{1,0:T(8,128)(2,1)}, bf16[64,2048]{1,0:T(8,128)(2,1)S(1)}, u32[]{:S(2)}, u32[]{:S(2)}) collective-permute-start(bf16[64,2048]{1,0:T(8,128)(2,1)} %collective-permute-done.5), channel_id=1, source_target_pairs={{0,2},{1,3},{2,6},{3,7},{4,0},{5,1},{6,10},{7,11},{8,4},{9,5},{10,... | collective-permute-start | bytes 786440 | tf_op jit(solution)/shard_map/ppermute | solution.py:295
  58.6 13.2 %collective-permute-start.17 = (bf16[64,2048]{1,0:T(8,128)(2,1)S(1)}, bf16[64,2048]{1,0:T(8,128)(2,1)S(1)}, u32[]{:S(2)}, u32[]{:S(2)}) collective-permute-start(bf16[64,2048]{1,0:T(8,128)(2,1)S(1)} %collective-permute-done.16), channel_id=1, source_target_pairs={{0,2},{1,3},{2,6},{3,7},{4,0},{5,1},{6,10},{7,11},{8,4},{9,5},{10,... | collective-permute-start | bytes 786440 | tf_op jit(solution)/shard_map/ppermute | solution.py:295
  61.4 11.2 %collective-permute-start.10 = (bf16[64,2048]{1,0:T(8,128)(2,1)S(1)}, bf16[64,2048]{1,0:T(8,128)(2,1)S(1)}, u32[]{:S(2)}, u32[]{:S(2)}) collective-permute-start(bf16[64,2048]{1,0:T(8,128)(2,1)S(1)} %collective-permute-done.9), channel_id=1, source_target_pairs={{0,4},{1,5},{2,0},{3,1},{4,8},{5,9},{6,2},{7,3},{8,12},{9,13},{10,... | collective-permute-start | bytes 786440 | tf_op jit(solution)/shard_map/ppermute | solution.py:295
  67.0 13.0 %collective-permute-start.23 = (bf16[64,2048]{1,0:T(8,128)(2,1)S(1)}, bf16[64,2048]{1,0:T(8,128)(2,1)S(1)}, u32[]{:S(2)}, u32[]{:S(2)}) collective-permute-start(bf16[64,2048]{1,0:T(8,128)(2,1)S(1)} %collective-permute-done.22), channel_id=1, source_target_pairs={{0,4},{1,5},{2,0},{3,1},{4,8},{5,9},{6,2},{7,3},{8,12},{9,13},{10,... | collective-permute-start | bytes 786440 | tf_op jit(solution)/shard_map/ppermute | solution.py:295
  71.8 6.4 %collective-permute-start.18 = (bf16[64,2048]{1,0:T(8,128)(2,1)S(1)}, bf16[64,2048]{1,0:T(8,128)(2,1)S(1)}, u32[]{:S(2)}, u32[]{:S(2)}) collective-permute-start(bf16[64,2048]{1,0:T(8,128)(2,1)S(1)} %collective-permute-done.17), channel_id=1, source_target_pairs={{0,2},{1,3},{2,6},{3,7},{4,0},{5,1},{6,10},{7,11},{8,4},{9,5},{10,... | collective-permute-start | bytes 786440 | tf_op jit(solution)/shard_map/ppermute | solution.py:295
  83.1 9.3 %collective-permute-start.24 = (bf16[64,2048]{1,0:T(8,128)(2,1)S(1)}, bf16[64,2048]{1,0:T(8,128)(2,1)S(1)}, u32[]{:S(2)}, u32[]{:S(2)}) collective-permute-start(bf16[64,2048]{1,0:T(8,128)(2,1)S(1)} %get-tuple-element.99), channel_id=1, source_target_pairs={{0,4},{1,5},{2,0},{3,1},{4,8},{5,9},{6,2},{7,3},{8,12},{9,13},{10,... | collective-permute-start | bytes 786440 | tf_op jit(solution)/shard_map/ppermute | solution.py:295
  84.3 9.3 %collective-permute-start.28 = (bf16[64,2048]{1,0:T(8,128)(2,1)S(1)}, bf16[64,2048]{1,0:T(8,128)(2,1)S(1)}, u32[]{:S(2)}, u32[]{:S(2)}) collective-permute-start(bf16[64,2048]{1,0:T(8,128)(2,1)S(1)} %get-tuple-element.98), channel_id=1, source_target_pairs={{0,2},{1,3},{2,6},{3,7},{4,0},{5,1},{6,10},{7,11},{8,4},{9,5},{10,... | collective-permute-start | bytes 786440 | tf_op jit(solution)/shard_map/ppermute | solution.py:295
  85.3 12.4 %collective-permute-start.34 = (bf16[64,2048]{1,0:T(8,128)(2,1)S(1)}, bf16[64,2048]{1,0:T(8,128)(2,1)S(1)}, u32[]{:S(2)}, u32[]{:S(2)}) collective-permute-start(bf16[64,2048]{1,0:T(8,128)(2,1)S(1)} %get-tuple-element.101), channel_id=1, source_target_pairs={{0,2},{1,3},{2,6},{3,7},{4,0},{5,1},{6,10},{7,11},{8,4},{9,5},{10,... | collective-permute-start | bytes 786440 | tf_op jit(solution)/shard_map/ppermute | solution.py:295
  85.4 12.7 %collective-permute-start.26 = (bf16[64,2048]{1,0:T(8,128)(2,1)S(1)}, bf16[64,2048]{1,0:T(8,128)(2,1)S(1)}, u32[]{:S(2)}, u32[]{:S(2)}) collective-permute-start(bf16[64,2048]{1,0:T(8,128)(2,1)S(1)} %get-tuple-element.100), channel_id=1, source_target_pairs={{0,4},{1,5},{2,0},{3,1},{4,8},{5,9},{6,2},{7,3},{8,12},{9,13},{10,... | collective-permute-start | bytes 786440 | tf_op jit(solution)/shard_map/ppermute | solution.py:295
  93.6 10.9 %collective-permute-start.25 = (bf16[64,2048]{1,0:T(8,128)(2,1)S(1)}, bf16[64,2048]{1,0:T(8,128)(2,1)S(1)}, u32[]{:S(2)}, u32[]{:S(2)}) collective-permute-start(bf16[64,2048]{1,0:T(8,128)(2,1)S(1)} %get-tuple-element.89), channel_id=1, source_target_pairs={{0,4},{1,5},{2,0},{3,1},{4,8},{5,9},{6,2},{7,3},{8,12},{9,13},{10,... | collective-permute-start | bytes 786440 | tf_op jit(solution)/shard_map/ppermute | solution.py:295
  94.7 9.8 %collective-permute-start.30 = (bf16[64,2048]{1,0:T(8,128)(2,1)S(1)}, bf16[64,2048]{1,0:T(8,128)(2,1)S(1)}, u32[]{:S(2)}, u32[]{:S(2)}) collective-permute-start(bf16[64,2048]{1,0:T(8,128)(2,1)S(1)} %get-tuple-element.88), channel_id=1, source_target_pairs={{0,2},{1,3},{2,6},{3,7},{4,0},{5,1},{6,10},{7,11},{8,4},{9,5},{10,... | collective-permute-start | bytes 786440 | tf_op jit(solution)/shard_map/ppermute | solution.py:295
  98.2 10.5 %collective-permute-start.35 = (bf16[64,2048]{1,0:T(8,128)(2,1)S(1)}, bf16[64,2048]{1,0:T(8,128)(2,1)S(1)}, u32[]{:S(2)}, u32[]{:S(2)}) collective-permute-start(bf16[64,2048]{1,0:T(8,128)(2,1)S(1)} %get-tuple-element.81), channel_id=1, source_target_pairs={{0,2},{1,3},{2,6},{3,7},{4,0},{5,1},{6,10},{7,11},{8,4},{9,5},{10,... | collective-permute-start | bytes 786440 | tf_op jit(solution)/shard_map/ppermute | solution.py:295
  98.3 10.4 %collective-permute-start.27 = (bf16[64,2048]{1,0:T(8,128)(2,1)S(1)}, bf16[64,2048]{1,0:T(8,128)(2,1)S(1)}, u32[]{:S(2)}, u32[]{:S(2)}) collective-permute-start(bf16[64,2048]{1,0:T(8,128)(2,1)S(1)} %get-tuple-element.80), channel_id=1, source_target_pairs={{0,4},{1,5},{2,0},{3,1},{4,8},{5,9},{6,2},{7,3},{8,12},{9,13},{10,... | collective-permute-start | bytes 786440 | tf_op jit(solution)/shard_map/ppermute | solution.py:295
  104.4 6.1 %copy-start = (f32[1,32,64,128]{3,2,1,0:T(8,128)S(1)}, f32[1,32,64,128]{3,2,1,0:T(8,128)}, u32[]{:S(2)}) copy-start(f32[1,32,64,128]{3,2,1,0:T(8,128)} %param.24) | copy-start | bytes 3145732
  104.4 6.1 %copy-start.1 = (bf16[128,2048]{1,0:T(8,128)(2,1)S(1)}, bf16[128,2048]{1,0:T(8,128)(2,1)}, u32[]{:S(2)}) copy-start(bf16[128,2048]{1,0:T(8,128)(2,1)} %x_ref.2) | copy-start | bytes 1572868
  104.5 6.1 %copy-start.2 = (bf16[128,128]{1,0:T(8,128)(2,1)S(1)}, bf16[128,128]{1,0:T(8,128)(2,1)}, u32[]{:S(2)}) copy-start(bf16[128,128]{1,0:T(8,128)(2,1)} %b_ref.3) | copy-start | bytes 98308
  104.5 6.0 %copy-start.3 = (f32[128,32]{0,1:T(8,128)S(1)}, f32[128,32]{0,1:T(8,128)}, u32[]{:S(2)}) copy-start(f32[128,32]{0,1:T(8,128)} %param.19) | copy-start | bytes 49156
  104.5 6.0 %copy-start.4 = (f32[32]{0:T(128)S(1)}, f32[32]{0:T(128)}, u32[]{:S(2)}) copy-start(f32[32]{0:T(128)} %param.21) | copy-start | bytes 388
  104.5 6.0 %copy-start.5 = (f32[32]{0:T(128)S(1)}, f32[32]{0:T(128)}, u32[]{:S(2)}) copy-start(f32[32]{0:T(128)} %param.20) | copy-start | bytes 388
  104.7 18.0 %collective-permute-start.33 = (bf16[64,2048]{1,0:T(8,128)(2,1)S(1)}, bf16[64,2048]{1,0:T(8,128)(2,1)S(1)}, u32[]{:S(2)}, u32[]{:S(2)}) collective-permute-start(bf16[64,2048]{1,0:T(8,128)(2,1)S(1)} %get-tuple-element.83), channel_id=1, source_target_pairs={{0,4},{1,5},{2,0},{3,1},{4,8},{5,9},{6,2},{7,3},{8,12},{9,13},{10,... | collective-permute-start | bytes 786440 | tf_op jit(solution)/shard_map/ppermute | solution.py:295
  108.8 10.1 %collective-permute-start.36 = (bf16[64,2048]{1,0:T(8,128)(2,1)S(1)}, bf16[64,2048]{1,0:T(8,128)(2,1)S(1)}, u32[]{:S(2)}, u32[]{:S(2)}) collective-permute-start(bf16[64,2048]{1,0:T(8,128)(2,1)S(1)} %get-tuple-element.79), channel_id=1, source_target_pairs={{0,2},{1,3},{2,6},{3,7},{4,0},{5,1},{6,10},{7,11},{8,4},{9,5},{10,... | collective-permute-start | bytes 786440 | tf_op jit(solution)/shard_map/ppermute | solution.py:295
  114.1 6.4 %collective-permute-start.29 = (bf16[64,2048]{1,0:T(8,128)(2,1)S(1)}, bf16[64,2048]{1,0:T(8,128)(2,1)S(1)}, u32[]{:S(2)}, u32[]{:S(2)}) collective-permute-start(bf16[64,2048]{1,0:T(8,128)(2,1)S(1)} %get-tuple-element.78), channel_id=1, source_target_pairs={{0,4},{1,5},{2,0},{3,1},{4,8},{5,9},{6,2},{7,3},{8,12},{9,13},{10,... | collective-permute-start | bytes 786440 | tf_op jit(solution)/shard_map/ppermute | solution.py:295
  114.5 8.2 %collective-permute-start.32 = (bf16[64,2048]{1,0:T(8,128)(2,1)S(1)}, bf16[64,2048]{1,0:T(8,128)(2,1)S(1)}, u32[]{:S(2)}, u32[]{:S(2)}) collective-permute-start(bf16[64,2048]{1,0:T(8,128)(2,1)S(1)} %get-tuple-element.82), channel_id=1, source_target_pairs={{0,2},{1,3},{2,6},{3,7},{4,0},{5,1},{6,10},{7,11},{8,4},{9,5},{10,... | collective-permute-start | bytes 786440 | tf_op jit(solution)/shard_map/ppermute | solution.py:295
  120.6 6.4 %collective-permute-start.31 = (bf16[64,2048]{1,0:T(8,128)(2,1)S(1)}, bf16[64,2048]{1,0:T(8,128)(2,1)S(1)}, u32[]{:S(2)}, u32[]{:S(2)}) collective-permute-start(bf16[64,2048]{1,0:T(8,128)(2,1)S(1)} %get-tuple-element.76), channel_id=1, source_target_pairs={{0,4},{1,5},{2,0},{3,1},{4,8},{5,9},{6,2},{7,3},{8,12},{9,13},{10,... | collective-permute-start | bytes 786440 | tf_op jit(solution)/shard_map/ppermute | solution.py:295
  121.0 6.4 %collective-permute-start.37 = (bf16[64,2048]{1,0:T(8,128)(2,1)S(1)}, bf16[64,2048]{1,0:T(8,128)(2,1)S(1)}, u32[]{:S(2)}, u32[]{:S(2)}) collective-permute-start(bf16[64,2048]{1,0:T(8,128)(2,1)S(1)} %get-tuple-element.77), channel_id=1, source_target_pairs={{0,2},{1,3},{2,6},{3,7},{4,0},{5,1},{6,10},{7,11},{8,4},{9,5},{10,... | collective-permute-start | bytes 786440 | tf_op jit(solution)/shard_map/ppermute | solution.py:295

commit v10 on v9

--- a/solution.py
+++ b/solution.py
@@ -259,7 +259,7 @@
             expert_out[0],
             route_ids,
             route_weights,
-            lambda tie: state_next(after(ssm_input, tie)),
+            functools.partial(state_next, ssm_input),
         )
     else:
         normed = jnp.concatenate(normed)
@@ -313,8 +313,12 @@
     gates = jnp.sum(
         jnp.where(route_ids[:, :, None] == jnp.arange(experts), route_weights[:, :, None], 0.0), axis=1
     )
-    normed_top, normed_bottom, other = lax.optimization_barrier((*normed, to_x(gates)))
-    gates = jnp.where(x == 0, jnp.stack([gates, other]), jnp.stack([other, gates]))[:, None]
+    high = gates.astype(jnp.bfloat16)
+    low = (gates - high.astype(jnp.float32)).astype(jnp.bfloat16)
+    lanes = -(-2 * experts // 128) * 128
+    spare = jnp.zeros((frames, lanes - 2 * experts), jnp.bfloat16)
+    gates = jnp.concatenate([high, low, spare], axis=1)
+    normed_top, normed_bottom = normed
 
     halves = range(2)
     size = frames // 2
@@ -332,48 +336,27 @@
         return jnp.dot(rows, columns, preferred_element_type=jnp.float32).astype(jnp.bfloat16)
 
     own = [project(normed_top), project(normed_bottom)]
-
-    def merge(gates, other, low):
-        return jnp.where(
-            low, jnp.concatenate([gates, other], axis=1), jnp.concatenate([other, gates], axis=1)
-        )
-
     rows, peer = [], None
     for h in halves:
         arrived = sent[h]
         if peer is not None:
-            arrived = after(arrived, peer)
+            arrived, state = lax.optimization_barrier((arrived, state_next()))
         peer = project(arrived)
         back = to_x(peer)
+        gate = gates[h * size : (h + 1) * size]
         rows.append(
             jnp.where(
                 x == 0,
-                jnp.concatenate([own[h], back], axis=1),
-                jnp.concatenate([back, own[h]], axis=1),
+                jnp.concatenate([own[h], back, gate], axis=1),
+                jnp.concatenate([back, own[h], gate], axis=1),
             )
         )
 
     far = ring // 2
     fore_at, back_at = {0: rows}, {0: rows}
-    gates, step = after(gates, sent[1]), 1
     for k in range(1, far):
-        if step < wide:
-            other = send(gates, lambda z, x, c: (z ^ step, x, c))
         fore_at[k] = [along(fore_at[k - 1][h], 1) for h in halves]
         back_at[k] = [along(back_at[k - 1][h], -1) for h in halves]
-        if step < wide:
-            other, back_at[k][1] = lax.optimization_barrier((other, back_at[k][1]))
-            gates, step = merge(gates, other, z & step == 0), 2 * step
-    while step < wide:
-        other = send(gates, lambda z, x, c: (z ^ step, x, c))
-        gates, step = merge(gates, other, z & step == 0), 2 * step
-    mine = (z * 2 + x) * 2 + core
-    pair = jnp.stack([mine, mine + 1 - 2 * core])
-    gates = jnp.sum(
-        jnp.where(pair[:, None] == jnp.arange(experts), gates[..., None, :], 0.0), axis=-1
-    )
-    gates = jnp.concatenate([gates[0], gates[1, ::-1]])
-    gates = lax.dynamic_slice_in_dim(jnp.concatenate([gates, gates]), place, ring, 0)
     last = [along(fore_at[far - 1][0], 1), along(back_at[far - 1][1], -1)]
 
     joined_in = jnp.concatenate(
@@ -385,25 +368,34 @@
         ],
         axis=1,
     )
+    depth = expert_in.shape[0]
+    joined_in = jnp.pad(joined_in, ((0, lanes), (0, 0)))
     joined_down = jnp.concatenate([expert_out, down_other], axis=0)
     joined_in, joined_down = lax.optimization_barrier((joined_in, joined_down))
     is_first = jnp.arange(2 * hidden_width)[None, :] < hidden_width
 
-    def run_experts(parts, gate):
-        v = jnp.dot(jnp.concatenate(parts), joined_in, preferred_element_type=jnp.float32)
+    mine = (z * 2 + x) * 2 + core
+    lane = jnp.arange(2 * experts)[None, :] % experts
+    choose = [lane == mine, lane == mine + 1 - 2 * core]
+
+    def run_experts(parts):
+        parts = jnp.concatenate(parts)
+        v = jnp.dot(parts, joined_in, preferred_element_type=jnp.float32)
+        gate = parts[:, depth : depth + 2 * experts].astype(jnp.float32)
+        gate = [jnp.sum(jnp.where(test, gate, 0.0), axis=1, keepdims=True) for test in choose]
         hidden = jax.nn.silu(v[:, : 2 * hidden_width]) * v[:, 2 * hidden_width :]
-        hidden = (hidden * jnp.where(is_first, gate[:, :1], gate[:, 1:])).astype(jnp.bfloat16)
+        hidden = (hidden * jnp.where(is_first, gate[0], gate[1])).astype(jnp.bfloat16)
         return jnp.dot(hidden, joined_down, preferred_element_type=jnp.float32)
 
     def hop_experts(k, tie):
         parts = rows if k == 0 else [*back_at[k], *fore_at[k]]
-        gate = gates[0] if k == 0 else jnp.concatenate([gates[k], gates[ring - k]])
-        parts = [after(part, tie) for part in parts]
-        total = run_experts(parts, gate)
+        total = run_experts([after(part, tie) for part in parts])
+        if k == 0:
+            return total, ()
         cut = [total[i * size : (i + 1) * size] for i in range(len(parts))]
         return cut[:2], cut[2:]
 
-    total = run_experts(last, gates[far]).astype(jnp.bfloat16)
+    total = run_experts(last).astype(jnp.bfloat16)
     fore, back = [along(total[:size], 1), None], [None, along(total[size:], -1)]
     ahead, behind = hop_experts(far - 1, total)
     groups = [((fore, 1, 1), (back, -1, 0)), ((fore, 1, 0), (back, -1, 1))]
@@ -419,17 +411,16 @@
             for (way, step, h), load in zip(group, loads):
                 way[h] = along(load, step)
             if not before:
+                before = tuple(loads)
+                if k < far - 1:
+                    coming = hop_experts(k - 1, loads[0])
+                    before += (*coming[0], *coming[1]) if k > 1 else (coming[0],)
+            elif k == far - 1:
                 coming = hop_experts(k - 1, loads[0])
-                before = (*loads, *coming[0], *coming[1])
-                if k == 1:
-                    state = state_next(loads[0])
-                    before += (state,)
         ahead, behind = coming
-    out = []
-    for h in halves:
-        total = ahead[h] + fore[h].astype(jnp.float32) + back[h].astype(jnp.float32)
-        out.append((rows[h].astype(jnp.float32) + total).astype(jnp.bfloat16))
-    return jnp.concatenate(out), state
+    total = ahead + jnp.concatenate(fore).astype(jnp.float32) + jnp.concatenate(back).astype(jnp.float32)
+    mixer_rows = jnp.concatenate([row[:, :depth] for row in rows]).astype(jnp.float32)
+    return (mixer_rows + total).astype(jnp.bfloat16), state
 
 
 def routed_experts(normed, out_proj, expert_in, expert_out, route_ids, route_weights):

time: 130 us -> 138 us (1.062)
  local copies, waits for them, and re-layouts: 2.68 us -> 10.1 us
  starting transfers between devices: 39.8 us -> 35 us
  other arithmetic: 11.2 us -> 15.2 us
  waiting for transfers between devices: 46.7 us -> 50.3 us
  matrix products: 19.1 us -> 16.6 us
    concatenate x1, other arithmetic: 0.72 us -> 6.15 us  [dense_experts(): jnp.concatenate([expert_in[:, :hidden_width], in_other[:, :hidden_width],...]
    ppermute x38 -> x35, starting transfers between devices: 39.8 us -> 35 us  [send(): return lax.ppermute(value, axes, routes(wide, move))]
    unnamed x20 -> x35, local copies, waits for them, and re-layouts: 0.06 us -> 4.15 us
    ppermute x38 -> x35, waiting for transfers between devices: 46.7 us -> 50.3 us  [send(): return lax.ppermute(value, axes, routes(wide, move))]
    dot_general x5, matrix products: 10.7 us -> 8.21 us  [run_experts(): v = jnp.dot(parts, joined_in, preferred_element_type=jnp.float32)]
    concatenate x0 -> x6, local copies, waits for them, and re-layouts: none -> 2.13 us  [the longest x5 2.05 us: run_experts(): parts = jnp.concatenate(parts)]
  transfers between devices with their start and end apart: 38 -> 35, of which waited for: 19 -> 17; matrix products, arithmetic and copies ran while one was open for 21% -> 24% of each run, Pallas kernels for 7% -> 6%
where the time goes in v10:
time: 138 us; the launch traced here: 137 us
  waiting for transfers between devices  50.3 us (36%)
  starting transfers between devices  35 us (25%)
  matrix products  16.6 us (12%)
  other arithmetic  15.2 us (11%)
  local copies, waits for them, and re-layouts  10.1 us (7%)
  Pallas kernels  8.92 us (6%)
    ppermute x35, waiting for transfers between devices, send(): return lax.ppermute(value, axes, routes(wide, move))  50.3 us
    ppermute x35, starting transfers between devices, send(): return lax.ppermute(value, axes, routes(wide, move))  35 us
    dot_general x5, matrix products, run_experts(): v = jnp.dot(parts, joined_in, preferred_element_type=jnp.float32)  8.21 us
    concatenate x1, other arithmetic, dense_experts(): jnp.concatenate([expert_in[:, :hidden_width], in_other[:, :hidden_width],...  6.15 us
    pallas_call x1, Pallas kernels, ssm_mixer(): pl.pallas_call(mixer_kernel, grid=(steps,), in_specs=[pl.BlockSpec(memory...  5.35 us
    dot_general x5, matrix products, run_experts(): return jnp.dot(hidden, joined_down, preferred_element_type=jnp.float32)  5.03 us
    unnamed x35, local copies, waits for them, and re-layouts  4.15 us
    select_n x1, other arithmetic, dense_experts(): jnp.where(core == 0, jnp.concatenate([out_proj, out_other], axis=1), jnp....  3.59 us
  transfers between devices with their start and end apart: 35, of which 17 were waited for; matrix products, arithmetic and copies ran while one was open for 24% of the time, Pallas kernels for 6%

profile of v10, /device:TPU:0, one launch (start us, length us, event | category | flops | bytes accessed | tf_op | source)
XLA Modules:
  0.0 137.4 jit_solution(693045604348280494)
XLA Ops:
  1.2 5.3 %mixer.1 = (bf16[64,2048]{1,0:T(8,128)(2,1)}, bf16[64,2048]{1,0:T(8,128)(2,1)}) custom-call(f32[32]{0:T(128)} %skip_ref.1, bf16[128,2048]{1,0:T(8,128)(2,1)} %x_ref.3, bf16[128,2048]{1,0:T(8,128)(2,1)} %z_ref.1, bf16[128,128]{1,0:T(8,128)(2,1)} %b_ref.3, bf16[128,128]{1,0:T(8,128)(2,1)} %c_ref.1, f32[32,128]{1,0:T(8,128)} %bitcast.34, f32[1,32]{1,0:T(1,128)} %bitcast.36, ...), custom_call_target="tpu_custom_call" | custom-call | flops 400000000 | bytes 6000000 | tf_op jit(solution)/shard_map/mixer/pallas_call | solution.py:159
  6.6 2.7 %collective-permute-start.1 = (bf16[64,2048]{1,0:T(8,128)(2,1)}, bf16[64,2048]{1,0:T(8,128)(2,1)S(1)}, u32[]{:S(2)}, u32[]{:S(2)}) collective-permute-start(bf16[64,2048]{1,0:T(8,128)(2,1)} %get-tuple-element.29), channel_id=1, source_target_pairs={{0,2},{1,3},{2,0},{3,1},{4,6},{5,7},{6,4},{7,5},{8,10},{9,11},{10,... | collective-permute-start | bytes 786440 | tf_op jit(solution)/shard_map/ppermute | solution.py:295
  10.2 3.6 %state.1 = f32[2048,128]{1,0:T(8,128)} custom-call(bf16[128,2048]{1,0:T(8,128)(2,1)S(1)} %copy-done.1, bf16[128,128]{1,0:T(8,128)(2,1)S(1)} %copy-done.2, f32[32,128]{1,0:T(8,128)S(1)} %bitcast.35, f32[1,32]{1,0:T(1,128)S(1)} %bitcast.37, f32[1,32]{1,0:T(1,128)S(1)} %bitcast.39, f32[2048,128]{1,0:T(8,128)S(1)} %bitcast.33), custom_call_target="tpu_custom_call" | custom-call | flops 70000000 | bytes 3000000 | tf_op jit(solution)/shard_map/state/pallas_call | solution.py:198
  13.9 3.6 %maximum_select_fusion = bf16[2048,1024]{1,0:T(8,128)(2,1)S(1)} fusion(bf16[2048,512]{1,0:T(8,128)(2,1)} %collective-permute-done, bf16[2048,512]{1,0:T(8,128)(2,1)S(1)} %copy-done.7, pred[]{:T(512)S(6)} %eq.47), kind=kLoop, calls=%fused_computation.8 | loop fusion | flops 18874368 | bytes 8388609 | tf_op jit(solution)/shard_map/jit(_where)/select_n | solution.py:327
  18.5 2.0 %collective-permute-start.2 = (bf16[64,1024]{1,0:T(8,128)(2,1)S(1)}, bf16[64,1024]{1,0:T(8,128)(2,1)S(1)}, u32[]{:S(2)}, u32[]{:S(2)}) collective-permute-start(bf16[64,1024]{1,0:T(8,128)(2,1)S(1)} %convolution_convert_fusion.3), channel_id=1, source_target_pairs={{0,2},{1,3},{2,0},{3,1},{4,6},{5,7},{6,4},{7,5},{8,10},{9,11},{10,... | collective-permute-start | bytes 393224 | tf_op jit(solution)/shard_map/ppermute | solution.py:295
  22.2 4.5 %collective-permute-done.3 = bf16[64,2048]{1,0:T(8,128)(2,1)S(1)} collective-permute-done((bf16[64,2048]{1,0:T(8,128)(2,1)S(1)}, bf16[64,2048]{1,0:T(8,128)(2,1)S(1)}, u32[]{:S(2)}, u32[]{:S(2)}) %collective-permute-start.3) | collective-permute-done | bytes 262176 | tf_op jit(solution)/shard_map/ppermute | solution.py:295
  28.7 1.6 %collective-permute-start.8 = (bf16[64,2176]{1,0:T(8,128)(2,1)S(1)}, bf16[64,2176]{1,0:T(8,128)(2,1)}, u32[]{:S(2)}, u32[]{:S(2)}) collective-permute-start(bf16[64,2176]{1,0:T(8,128)(2,1)S(1)} %fusion.42), channel_id=1, source_target_pairs={{0,4},{1,5},{2,0},{3,1},{4,8},{5,9},{6,2},{7,3},{8,12},{9,13},{10,... | collective-permute-start | bytes 835592 | tf_op jit(solution)/shard_map/ppermute | solution.py:295
  30.8 3.2 %collective-permute-done.4 = bf16[64,1024]{1,0:T(8,128)(2,1)S(1)} collective-permute-done((bf16[64,1024]{1,0:T(8,128)(2,1)S(1)}, bf16[64,1024]{1,0:T(8,128)(2,1)S(1)}, u32[]{:S(2)}, u32[]{:S(2)}) %collective-permute-start.4) | collective-permute-done | bytes 131104 | tf_op jit(solution)/shard_map/ppermute | solution.py:295
  34.7 2.0 %collective-permute-start.18 = (bf16[64,2176]{1,0:T(8,128)(2,1)}, bf16[64,2176]{1,0:T(8,128)(2,1)}, u32[]{:S(2)}, u32[]{:S(2)}) collective-permute-start(bf16[64,2176]{1,0:T(8,128)(2,1)} %fusion.41), channel_id=1, source_target_pairs={{0,4},{1,5},{2,0},{3,1},{4,8},{5,9},{6,2},{7,3},{8,12},{9,13},{10,... | collective-permute-start | bytes 835592 | tf_op jit(solution)/shard_map/ppermute | solution.py:295
  36.8 3.3 %collective-permute-done.8 = bf16[64,2176]{1,0:T(8,128)(2,1)} collective-permute-done((bf16[64,2176]{1,0:T(8,128)(2,1)S(1)}, bf16[64,2176]{1,0:T(8,128)(2,1)}, u32[]{:S(2)}, u32[]{:S(2)}) %collective-permute-start.8) | collective-permute-done | bytes 278560 | tf_op jit(solution)/shard_map/ppermute | solution.py:295
  40.4 2.1 %collective-permute-start.6 = (bf16[64,2176]{1,0:T(8,128)(2,1)}, bf16[64,2176]{1,0:T(8,128)(2,1)S(1)}, u32[]{:S(2)}, u32[]{:S(2)}) collective-permute-start(bf16[64,2176]{1,0:T(8,128)(2,1)} %collective-permute-done.5), channel_id=1, source_target_pairs={{0,2},{1,3},{2,6},{3,7},{4,0},{5,1},{6,10},{7,11},{8,4},{9,5},{10,... | collective-permute-start | bytes 835592 | tf_op jit(solution)/shard_map/ppermute | solution.py:295
  42.5 3.5 %collective-permute-done.12 = bf16[64,2176]{1,0:T(8,128)(2,1)} collective-permute-done((bf16[64,2176]{1,0:T(8,128)(2,1)}, bf16[64,2176]{1,0:T(8,128)(2,1)}, u32[]{:S(2)}, u32[]{:S(2)}) %collective-permute-start.12) | collective-permute-done | bytes 278560 | tf_op jit(solution)/shard_map/ppermute | solution.py:295
  46.5 1.6 %collective-permute-start.19 = (bf16[64,2176]{1,0:T(8,128)(2,1)}, bf16[64,2176]{1,0:T(8,128)(2,1)S(1)}, u32[]{:S(2)}, u32[]{:S(2)}) collective-permute-start(bf16[64,2176]{1,0:T(8,128)(2,1)} %collective-permute-done.18), channel_id=1, source_target_pairs={{0,4},{1,5},{2,0},{3,1},{4,8},{5,9},{6,2},{7,3},{8,12},{9,13},{10,... | collective-permute-start | bytes 835592 | tf_op jit(solution)/shard_map/ppermute | solution.py:295
  48.0 3.9 %collective-permute-done.9 = bf16[64,2176]{1,0:T(8,128)(2,1)} collective-permute-done((bf16[64,2176]{1,0:T(8,128)(2,1)}, bf16[64,2176]{1,0:T(8,128)(2,1)}, u32[]{:S(2)}, u32[]{:S(2)}) %collective-permute-start.9) | collective-permute-done | bytes 278560 | tf_op jit(solution)/shard_map/ppermute | solution.py:295
  52.6 2.3 %pad_maximum_fusion = bf16[768,2048]{1,0:T(8,128)(2,1)S(1)} fusion(bf16[384,2048]{1,0:T(8,128)(2,1)} %collective-permute-done.17, bf16[384,2048]{1,0:T(8,128)(2,1)} %bitcast.7), kind=kLoop, calls=%fused_computation.9 | loop fusion | flops 6291456 | bytes 6291456 | tf_op jit(solution)/shard_map/concatenate | solution.py:373
  54.9 1.4 %collective-permute-start.7 = (bf16[64,2176]{1,0:T(8,128)(2,1)S(1)}, bf16[64,2176]{1,0:T(8,128)(2,1)S(1)}, u32[]{:S(2)}, u32[]{:S(2)}) collective-permute-start(bf16[64,2176]{1,0:T(8,128)(2,1)S(1)} %collective-permute-done.6), channel_id=1, source_target_pairs={{0,2},{1,3},{2,6},{3,7},{4,0},{5,1},{6,10},{7,11},{8,4},{9,5},{10,... | collective-permute-start | bytes 835592 | tf_op jit(solution)/shard_map/ppermute | solution.py:295
  56.3 1.5 %collective-permute-done.13 = bf16[64,2176]{1,0:T(8,128)(2,1)S(1)} collective-permute-done((bf16[64,2176]{1,0:T(8,128)(2,1)}, bf16[64,2176]{1,0:T(8,128)(2,1)S(1)}, u32[]{:S(2)}, u32[]{:S(2)}) %collective-permute-start.13) | collective-permute-done | bytes 278560 | tf_op jit(solution)/shard_map/ppermute | solution.py:295
  58.1 1.7 %collective-permute-start.20 = (bf16[64,2176]{1,0:T(8,128)(2,1)S(1)}, bf16[64,2176]{1,0:T(8,128)(2,1)S(1)}, u32[]{:S(2)}, u32[]{:S(2)}) collective-permute-start(bf16[64,2176]{1,0:T(8,128)(2,1)S(1)} %collective-permute-done.19), channel_id=1, source_target_pairs={{0,4},{1,5},{2,0},{3,1},{4,8},{5,9},{6,2},{7,3},{8,12},{9,13},{10,... | collective-permute-start | bytes 835592 | tf_op jit(solution)/shard_map/ppermute | solution.py:295
  59.9 3.9 %collective-permute-done.10 = bf16[64,2176]{1,0:T(8,128)(2,1)S(1)} collective-permute-done((bf16[64,2176]{1,0:T(8,128)(2,1)}, bf16[64,2176]{1,0:T(8,128)(2,1)S(1)}, u32[]{:S(2)}, u32[]{:S(2)}) %collective-permute-start.10) | collective-permute-done | bytes 278560 | tf_op jit(solution)/shard_map/ppermute | solution.py:295
  64.5 2.2 %fusion.70 = (bf16[2048,384]{1,0:T(8,128)(2,1)S(1)}, bf16[2048,384]{1,0:T(8,128)(2,1)S(1)}) fusion(bf16[2048,768]{1,0:T(8,128)(2,1)} %collective-permute-done.16), kind=kLoop, calls=%fused_computation.127 | loop fusion | bytes 6291456 | tf_op jit(solution)/shard_map/slice | solution.py:365
  66.7 6.2 %fusion.6 = bf16[2176,1536]{1,0:T(8,128)(2,1)S(1)} fusion(bf16[2048,384]{1,0:T(8,128)(2,1)S(1)} %get-tuple-element.71, bf16[2048,384]{1,0:T(8,128)(2,1)S(1)} %get-tuple-element.69, bf16[2048,384]{1,0:T(8,128)(2,1)S(1)} %get-tuple-element.70, bf16[2048,384]{1,0:T(8,128)(2,1)S(1)} %get-tuple-element.68), kind=kLoop, calls=%fused_computation.7 | loop fusion | flops 43450368 | bytes 12976128 | tf_op jit(solution)/shard_map/concatenate | solution.py:362
  72.8 1.6 %collective-permute-start.15 = (bf16[64,2176]{1,0:T(8,128)(2,1)S(1)}, bf16[64,2176]{1,0:T(8,128)(2,1)S(1)}, u32[]{:S(2)}, u32[]{:S(2)}) collective-permute-start(bf16[64,2176]{1,0:T(8,128)(2,1)S(1)} %collective-permute-done.14), channel_id=1, source_target_pairs={{0,2},{1,3},{2,6},{3,7},{4,0},{5,1},{6,10},{7,11},{8,4},{9,5},{10,... | collective-permute-start | bytes 835592 | tf_op jit(solution)/shard_map/ppermute | solution.py:295
  74.5 5.2 %collective-permute-done.15 = bf16[64,2176]{1,0:T(8,128)(2,1)S(1)} collective-permute-done((bf16[64,2176]{1,0:T(8,128)(2,1)S(1)}, bf16[64,2176]{1,0:T(8,128)(2,1)S(1)}, u32[]{:S(2)}, u32[]{:S(2)}) %collective-permute-start.15) | collective-permute-done | bytes 278560 | tf_op jit(solution)/shard_map/ppermute | solution.py:295
  79.7 1.1 fusion.76
  81.8 2.0 %fusion.77 = f32[256,1536]{1,0:T(8,128)S(1)} fusion(bf16[256,2176]{1,0:T(8,128)(2,1)S(1)} %constant_dynamic-update-slice_fusion.2, bf16[2176,1536]{1,0:T(8,128)(2,1)S(1)} %fusion.6), kind=kOutput, calls=%fused_computation.134 | convolution fusion | flops 1711276032 | bytes 9371648 | tf_op jit(solution)/shard_map/dot_general | solution.py:383
  84.9 1.1 collective-permute-start.31
  86.0 1.2 fusion.75
  88.2 1.1 collective-permute-start.25
  89.3 1.0 collective-permute-done.21
  91.4 1.0 constant_dynamic-update-slice_fusion.7
  92.5 2.0 %fusion.78 = f32[256,1536]{1,0:T(8,128)S(1)} fusion(bf16[256,2176]{1,0:T(8,128)(2,1)S(1)} %constant_dynamic-update-slice_fusion.6, bf16[2176,1536]{1,0:T(8,128)(2,1)S(1)} %fusion.6), kind=kOutput, calls=%fused_computation.135 | convolution fusion | flops 1711276032 | bytes 9371648 | tf_op jit(solution)/shard_map/dot_general | solution.py:383
  94.6 1.2 fusion.21
  96.9 1.0 constant_dynamic-update-slice_fusion.12
  97.9 1.0 constant_dynamic-update-slice_fusion.11
  99.9 2.0 %fusion.79 = f32[256,1536]{1,0:T(8,128)S(1)} fusion(bf16[256,2176]{1,0:T(8,128)(2,1)S(1)} %constant_dynamic-update-slice_fusion.10, bf16[2176,1536]{1,0:T(8,128)(2,1)S(1)} %fusion.6), kind=kOutput, calls=%fused_computation.136 | convolution fusion | flops 1711276032 | bytes 9371648 | tf_op jit(solution)/shard_map/dot_general | solution.py:383
  102.0 1.9 %collective-permute-start.24 = (bf16[64,2048]{1,0:T(8,128)(2,1)S(1)}, bf16[64,2048]{1,0:T(8,128)(2,1)S(1)}, u32[]{:S(2)}, u32[]{:S(2)}) collective-permute-start(bf16[64,2048]{1,0:T(8,128)(2,1)S(1)} %get-tuple-element.77), channel_id=1, source_target_pairs={{0,4},{1,5},{2,0},{3,1},{4,8},{5,9},{6,2},{7,3},{8,12},{9,13},{10,... | collective-permute-start | bytes 786440 | tf_op jit(solution)/shard_map/ppermute | solution.py:295
  103.9 2.0 %collective-permute-start.23 = (bf16[64,2048]{1,0:T(8,128)(2,1)S(1)}, bf16[64,2048]{1,0:T(8,128)(2,1)S(1)}, u32[]{:S(2)}, u32[]{:S(2)}) collective-permute-start(bf16[64,2048]{1,0:T(8,128)(2,1)S(1)} %get-tuple-element.85), channel_id=1, source_target_pairs={{0,4},{1,5},{2,0},{3,1},{4,8},{5,9},{6,2},{7,3},{8,12},{9,13},{10,... | collective-permute-start | bytes 786440 | tf_op jit(solution)/shard_map/ppermute | solution.py:295
  106.1 1.2 fusion.23
  107.3 6.6 %collective-permute-done.23 = bf16[64,2048]{1,0:T(8,128)(2,1)S(1)} collective-permute-done((bf16[64,2048]{1,0:T(8,128)(2,1)S(1)}, bf16[64,2048]{1,0:T(8,128)(2,1)S(1)}, u32[]{:S(2)}, u32[]{:S(2)}) %collective-permute-start.23) | collective-permute-done | bytes 262176 | tf_op jit(solution)/shard_map/ppermute | solution.py:295
  113.9 4.3 %collective-permute-done.27 = bf16[64,2048]{1,0:T(8,128)(2,1)S(1)} collective-permute-done((bf16[64,2048]{1,0:T(8,128)(2,1)S(1)}, bf16[64,2048]{1,0:T(8,128)(2,1)S(1)}, u32[]{:S(2)}, u32[]{:S(2)}) %collective-permute-start.27) | collective-permute-done | bytes 262176 | tf_op jit(solution)/shard_map/ppermute | solution.py:295
  118.4 1.0 constant_dynamic-update-slice_fusion.14
  119.4 1.1 fusion.80
  120.8 2.2 %collective-permute-start.26 = (bf16[64,2048]{1,0:T(8,128)(2,1)S(1)}, bf16[64,2048]{1,0:T(8,128)(2,1)S(1)}, u32[]{:S(2)}, u32[]{:S(2)}) collective-permute-start(bf16[64,2048]{1,0:T(8,128)(2,1)S(1)} %get-tuple-element.75), channel_id=1, source_target_pairs={{0,4},{1,5},{2,0},{3,1},{4,8},{5,9},{6,2},{7,3},{8,12},{9,13},{10,... | collective-permute-start | bytes 786440 | tf_op jit(solution)/shard_map/ppermute | solution.py:295
  123.0 1.9 %collective-permute-start.30 = (bf16[64,2048]{1,0:T(8,128)(2,1)S(1)}, bf16[64,2048]{1,0:T(8,128)(2,1)S(1)}, u32[]{:S(2)}, u32[]{:S(2)}) collective-permute-start(bf16[64,2048]{1,0:T(8,128)(2,1)S(1)} %get-tuple-element.78), channel_id=1, source_target_pairs={{0,2},{1,3},{2,6},{3,7},{4,0},{5,1},{6,10},{7,11},{8,4},{9,5},{10,... | collective-permute-start | bytes 786440 | tf_op jit(solution)/shard_map/ppermute | solution.py:295
  125.6 3.3 %collective-permute-done.26 = bf16[64,2048]{1,0:T(8,128)(2,1)S(1)} collective-permute-done((bf16[64,2048]{1,0:T(8,128)(2,1)S(1)}, bf16[64,2048]{1,0:T(8,128)(2,1)S(1)}, u32[]{:S(2)}, u32[]{:S(2)}) %collective-permute-start.26) | collective-permute-done | bytes 262176 | tf_op jit(solution)/shard_map/ppermute | solution.py:295
  129.9 1.6 %collective-permute-start.34 = (bf16[64,2048]{1,0:T(8,128)(2,1)S(1)}, bf16[64,2048]{1,0:T(8,128)(2,1)S(1)}, u32[]{:S(2)}, u32[]{:S(2)}) collective-permute-start(bf16[64,2048]{1,0:T(8,128)(2,1)S(1)} %get-tuple-element.72), channel_id=1, source_target_pairs={{0,2},{1,3},{2,6},{3,7},{4,0},{5,1},{6,10},{7,11},{8,4},{9,5},{10,... | collective-permute-start | bytes 786440 | tf_op jit(solution)/shard_map/ppermute | solution.py:295
  132.6 3.3 %collective-permute-done.28 = bf16[64,2048]{1,0:T(8,128)(2,1)S(1)} collective-permute-done((bf16[64,2048]{1,0:T(8,128)(2,1)S(1)}, bf16[64,2048]{1,0:T(8,128)(2,1)S(1)}, u32[]{:S(2)}, u32[]{:S(2)}) %collective-permute-start.28) | collective-permute-done | bytes 262176 | tf_op jit(solution)/shard_map/ppermute | solution.py:295
  136.3 1.1 add_convert_fusion
  (110 shorter events, 20.1 us)
Async XLA Ops:
  0.6 9.5 %copy-start.3 = (f32[128,32]{0,1:T(8,128)S(1)}, f32[128,32]{0,1:T(8,128)}, u32[]{:S(2)}) copy-start(f32[128,32]{0,1:T(8,128)} %param.19) | copy-start | bytes 49156
  0.6 9.5 %copy-start.4 = (f32[32]{0:T(128)S(1)}, f32[32]{0:T(128)}, u32[]{:S(2)}) copy-start(f32[32]{0:T(128)} %param.21) | copy-start | bytes 388
  0.7 9.5 %copy-start.5 = (f32[32]{0:T(128)S(1)}, f32[32]{0:T(128)}, u32[]{:S(2)}) copy-start(f32[32]{0:T(128)} %param.20) | copy-start | bytes 388
  0.7 9.5 %copy-start = (f32[1,32,64,128]{3,2,1,0:T(8,128)S(1)}, f32[1,32,64,128]{3,2,1,0:T(8,128)}, u32[]{:S(2)}) copy-start(f32[1,32,64,128]{3,2,1,0:T(8,128)} %param.24) | copy-start | bytes 3145732
  0.7 9.5 %copy-start.1 = (bf16[128,2048]{1,0:T(8,128)(2,1)S(1)}, bf16[128,2048]{1,0:T(8,128)(2,1)}, u32[]{:S(2)}) copy-start(bf16[128,2048]{1,0:T(8,128)(2,1)} %x_ref.3) | copy-start | bytes 1572868
  0.7 9.5 %copy-start.2 = (bf16[128,128]{1,0:T(8,128)(2,1)S(1)}, bf16[128,128]{1,0:T(8,128)(2,1)}, u32[]{:S(2)}) copy-start(bf16[128,128]{1,0:T(8,128)(2,1)} %b_ref.3) | copy-start | bytes 98308
  0.7 9.1 %copy-start.11 = (s32[128,8]{0,1:T(8,128)S(1)}, s32[128,8]{0,1:T(8,128)}, u32[]{:S(2)}) copy-start(s32[128,8]{0,1:T(8,128)} %param.28) | copy-start | bytes 12292
  0.7 9.0 %copy-start.10 = (f32[128,8]{0,1:T(8,128)S(1)}, f32[128,8]{0,1:T(8,128)}, u32[]{:S(2)}) copy-start(f32[128,8]{0,1:T(8,128)} %param.29) | copy-start | bytes 12292
  0.7 13.1 %collective-permute-start = (bf16[2048,512]{1,0:T(8,128)(2,1)}, bf16[2048,512]{1,0:T(8,128)(2,1)}, u32[]{:S(2)}, u32[]{:S(2)}) collective-permute-start(bf16[2048,512]{1,0:T(8,128)(2,1)} %param.25), channel_id=1, source_target_pairs={{0,1},{1,0},{2,3},{3,2},{4,5},{5,4},{6,7},{7,6},{8,9},{9,8},{10,11... | collective-permute-start | bytes 6291464 | tf_op jit(solution)/shard_map/ppermute | solution.py:295
  6.6 11.0 %collective-permute-start.1 = (bf16[64,2048]{1,0:T(8,128)(2,1)}, bf16[64,2048]{1,0:T(8,128)(2,1)S(1)}, u32[]{:S(2)}, u32[]{:S(2)}) collective-permute-start(bf16[64,2048]{1,0:T(8,128)(2,1)} %get-tuple-element.29), channel_id=1, source_target_pairs={{0,2},{1,3},{2,0},{3,1},{4,6},{5,7},{6,4},{7,5},{8,10},{9,11},{10,... | collective-permute-start | bytes 786440 | tf_op jit(solution)/shard_map/ppermute | solution.py:295
  9.2 55.2 %collective-permute-start.16 = (bf16[2048,768]{1,0:T(8,128)(2,1)}, bf16[2048,768]{1,0:T(8,128)(2,1)}, u32[]{:S(2)}, u32[]{:S(2)}) collective-permute-start(bf16[2048,768]{1,0:T(8,128)(2,1)} %bitcast.40), channel_id=1, source_target_pairs={{0,1},{1,0},{2,3},{3,2},{4,5},{5,4},{6,7},{7,6},{8,9},{9,8},{10,11... | collective-permute-start | bytes 9437192 | tf_op jit(solution)/shard_map/ppermute | solution.py:295
  9.3 25.4 %collective-permute-start.17 = (bf16[384,2048]{1,0:T(8,128)(2,1)}, bf16[384,2048]{1,0:T(8,128)(2,1)}, u32[]{:S(2)}, u32[]{:S(2)}) collective-permute-start(bf16[384,2048]{1,0:T(8,128)(2,1)} %bitcast.7), channel_id=1, source_target_pairs={{0,1},{1,0},{2,3},{3,2},{4,5},{5,4},{6,7},{7,6},{8,9},{9,8},{10,11... | collective-permute-start | bytes 4718600 | tf_op jit(solution)/shard_map/ppermute | solution.py:295
  10.0 3.8 %copy-start.7 = (bf16[2048,512]{1,0:T(8,128)(2,1)S(1)}, bf16[2048,512]{1,0:T(8,128)(2,1)}, u32[]{:S(2)}) copy-start(bf16[2048,512]{1,0:T(8,128)(2,1)} %param.25) | copy-start | bytes 6291460
  13.8 3.6 %copy-start.9 = (bf16[64,2048]{1,0:T(8,128)(2,1)S(1)}, bf16[64,2048]{1,0:T(8,128)(2,1)}, u32[]{:S(2)}) copy-start(bf16[64,2048]{1,0:T(8,128)(2,1)} %get-tuple-element.31) | copy-start | bytes 786436
  17.5 9.2 %collective-permute-start.3 = (bf16[64,2048]{1,0:T(8,128)(2,1)S(1)}, bf16[64,2048]{1,0:T(8,128)(2,1)S(1)}, u32[]{:S(2)}, u32[]{:S(2)}) collective-permute-start(bf16[64,2048]{1,0:T(8,128)(2,1)S(1)} %copy-done.9), channel_id=1, source_target_pairs={{0,2},{1,3},{2,0},{3,1},{4,6},{5,7},{6,4},{7,5},{8,10},{9,11},{10,... | collective-permute-start | bytes 786440 | tf_op jit(solution)/shard_map/ppermute | solution.py:295
  18.5 2.9 %copy-start.8 = (bf16[64,2048]{1,0:T(8,128)(2,1)S(1)}, bf16[64,2048]{1,0:T(8,128)(2,1)}, u32[]{:S(2)}) copy-start(bf16[64,2048]{1,0:T(8,128)(2,1)} %get-tuple-element.29) | copy-start | bytes 786436
  18.5 10.1 %collective-permute-start.2 = (bf16[64,1024]{1,0:T(8,128)(2,1)S(1)}, bf16[64,1024]{1,0:T(8,128)(2,1)S(1)}, u32[]{:S(2)}, u32[]{:S(2)}) collective-permute-start(bf16[64,1024]{1,0:T(8,128)(2,1)S(1)} %convolution_convert_fusion.3), channel_id=1, source_target_pairs={{0,2},{1,3},{2,0},{3,1},{4,6},{5,7},{6,4},{7,5},{8,10},{9,11},{10,... | collective-permute-start | bytes 393224 | tf_op jit(solution)/shard_map/ppermute | solution.py:295
  26.7 13.3 %copy-start.6 = (bf16[1,2048,768]{2,1,0:T(8,128)(2,1)S(1)}, bf16[1,2048,768]{2,1,0:T(8,128)(2,1)}, u32[]{:S(2)}) copy-start(bf16[1,2048,768]{2,1,0:T(8,128)(2,1)} %param.26) | copy-start | bytes 9437188
  27.5 6.4 %collective-permute-start.4 = (bf16[64,1024]{1,0:T(8,128)(2,1)S(1)}, bf16[64,1024]{1,0:T(8,128)(2,1)S(1)}, u32[]{:S(2)}, u32[]{:S(2)}) collective-permute-start(bf16[64,1024]{1,0:T(8,128)(2,1)S(1)} %convolution_convert_fusion.1), channel_id=1, source_target_pairs={{0,2},{1,3},{2,0},{3,1},{4,6},{5,7},{6,4},{7,5},{8,10},{9,11},{10,... | collective-permute-start | bytes 393224 | tf_op jit(solution)/shard_map/ppermute | solution.py:295
  28.7 11.3 %collective-permute-start.8 = (bf16[64,2176]{1,0:T(8,128)(2,1)S(1)}, bf16[64,2176]{1,0:T(8,128)(2,1)}, u32[]{:S(2)}, u32[]{:S(2)}) collective-permute-start(bf16[64,2176]{1,0:T(8,128)(2,1)S(1)} %fusion.42), channel_id=1, source_target_pairs={{0,4},{1,5},{2,0},{3,1},{4,8},{5,9},{6,2},{7,3},{8,12},{9,13},{10,... | collective-permute-start | bytes 835592 | tf_op jit(solution)/shard_map/ppermute | solution.py:295
  30.3 10.1 %collective-permute-start.5 = (bf16[64,2176]{1,0:T(8,128)(2,1)S(1)}, bf16[64,2176]{1,0:T(8,128)(2,1)}, u32[]{:S(2)}, u32[]{:S(2)}) collective-permute-start(bf16[64,2176]{1,0:T(8,128)(2,1)S(1)} %fusion.42), channel_id=1, source_target_pairs={{0,2},{1,3},{2,6},{3,7},{4,0},{5,1},{6,10},{7,11},{8,4},{9,5},{10,... | collective-permute-start | bytes 835592 | tf_op jit(solution)/shard_map/ppermute | solution.py:295
  34.7 11.3 %collective-permute-start.12 = (bf16[64,2176]{1,0:T(8,128)(2,1)}, bf16[64,2176]{1,0:T(8,128)(2,1)}, u32[]{:S(2)}, u32[]{:S(2)}) collective-permute-start(bf16[64,2176]{1,0:T(8,128)(2,1)} %fusion.41), channel_id=1, source_target_pairs={{0,2},{1,3},{2,6},{3,7},{4,0},{5,1},{6,10},{7,11},{8,4},{9,5},{10,... | collective-permute-start | bytes 835592 | tf_op jit(solution)/shard_map/ppermute | solution.py:295
  34.7 11.7 %collective-permute-start.18 = (bf16[64,2176]{1,0:T(8,128)(2,1)}, bf16[64,2176]{1,0:T(8,128)(2,1)}, u32[]{:S(2)}, u32[]{:S(2)}) collective-permute-start(bf16[64,2176]{1,0:T(8,128)(2,1)} %fusion.41), channel_id=1, source_target_pairs={{0,4},{1,5},{2,0},{3,1},{4,8},{5,9},{6,2},{7,3},{8,12},{9,13},{10,... | collective-permute-start | bytes 835592 | tf_op jit(solution)/shard_map/ppermute | solution.py:295
  40.0 11.9 %collective-permute-start.9 = (bf16[64,2176]{1,0:T(8,128)(2,1)}, bf16[64,2176]{1,0:T(8,128)(2,1)}, u32[]{:S(2)}, u32[]{:S(2)}) collective-permute-start(bf16[64,2176]{1,0:T(8,128)(2,1)} %collective-permute-done.8), channel_id=1, source_target_pairs={{0,4},{1,5},{2,0},{3,1},{4,8},{5,9},{6,2},{7,3},{8,12},{9,13},{10,... | collective-permute-start | bytes 835592 | tf_op jit(solution)/shard_map/ppermute | solution.py:295
  40.4 14.5 %collective-permute-start.6 = (bf16[64,2176]{1,0:T(8,128)(2,1)}, bf16[64,2176]{1,0:T(8,128)(2,1)S(1)}, u32[]{:S(2)}, u32[]{:S(2)}) collective-permute-start(bf16[64,2176]{1,0:T(8,128)(2,1)} %collective-permute-done.5), channel_id=1, source_target_pairs={{0,2},{1,3},{2,6},{3,7},{4,0},{5,1},{6,10},{7,11},{8,4},{9,5},{10,... | collective-permute-start | bytes 835592 | tf_op jit(solution)/shard_map/ppermute | solution.py:295
  46.0 11.8 %collective-permute-start.13 = (bf16[64,2176]{1,0:T(8,128)(2,1)}, bf16[64,2176]{1,0:T(8,128)(2,1)S(1)}, u32[]{:S(2)}, u32[]{:S(2)}) collective-permute-start(bf16[64,2176]{1,0:T(8,128)(2,1)} %collective-permute-done.12), channel_id=1, source_target_pairs={{0,2},{1,3},{2,6},{3,7},{4,0},{5,1},{6,10},{7,11},{8,4},{9,5},{10,... | collective-permute-start | bytes 835592 | tf_op jit(solution)/shard_map/ppermute | solution.py:295
  46.5 11.7 %collective-permute-start.19 = (bf16[64,2176]{1,0:T(8,128)(2,1)}, bf16[64,2176]{1,0:T(8,128)(2,1)S(1)}, u32[]{:S(2)}, u32[]{:S(2)}) collective-permute-start(bf16[64,2176]{1,0:T(8,128)(2,1)} %collective-permute-done.18), channel_id=1, source_target_pairs={{0,4},{1,5},{2,0},{3,1},{4,8},{5,9},{6,2},{7,3},{8,12},{9,13},{10,... | collective-permute-start | bytes 835592 | tf_op jit(solution)/shard_map/ppermute | solution.py:295
  52.0 11.8 %collective-permute-start.10 = (bf16[64,2176]{1,0:T(8,128)(2,1)}, bf16[64,2176]{1,0:T(8,128)(2,1)S(1)}, u32[]{:S(2)}, u32[]{:S(2)}) collective-permute-start(bf16[64,2176]{1,0:T(8,128)(2,1)} %collective-permute-done.9), channel_id=1, source_target_pairs={{0,4},{1,5},{2,0},{3,1},{4,8},{5,9},{6,2},{7,3},{8,12},{9,13},{10,... | collective-permute-start | bytes 835592 | tf_op jit(solution)/shard_map/ppermute | solution.py:295
  54.9 26.7 %collective-permute-start.7 = (bf16[64,2176]{1,0:T(8,128)(2,1)S(1)}, bf16[64,2176]{1,0:T(8,128)(2,1)S(1)}, u32[]{:S(2)}, u32[]{:S(2)}) collective-permute-start(bf16[64,2176]{1,0:T(8,128)(2,1)S(1)} %collective-permute-done.6), channel_id=1, source_target_pairs={{0,2},{1,3},{2,6},{3,7},{4,0},{5,1},{6,10},{7,11},{8,4},{9,5},{10,... | collective-permute-start | bytes 835592 | tf_op jit(solution)/shard_map/ppermute | solution.py:295
  57.8 15.0 %collective-permute-start.14 = (bf16[64,2176]{1,0:T(8,128)(2,1)S(1)}, bf16[64,2176]{1,0:T(8,128)(2,1)S(1)}, u32[]{:S(2)}, u32[]{:S(2)}) collective-permute-start(bf16[64,2176]{1,0:T(8,128)(2,1)S(1)} %collective-permute-done.13), channel_id=1, source_target_pairs={{0,2},{1,3},{2,6},{3,7},{4,0},{5,1},{6,10},{7,11},{8,4},{9,5},{10,... | collective-permute-start | bytes 835592 | tf_op jit(solution)/shard_map/ppermute | solution.py:295
  58.1 23.5 %collective-permute-start.20 = (bf16[64,2176]{1,0:T(8,128)(2,1)S(1)}, bf16[64,2176]{1,0:T(8,128)(2,1)S(1)}, u32[]{:S(2)}, u32[]{:S(2)}) collective-permute-start(bf16[64,2176]{1,0:T(8,128)(2,1)S(1)} %collective-permute-done.19), channel_id=1, source_target_pairs={{0,4},{1,5},{2,0},{3,1},{4,8},{5,9},{6,2},{7,3},{8,12},{9,13},{10,... | collective-permute-start | bytes 835592 | tf_op jit(solution)/shard_map/ppermute | solution.py:295
  63.8 10.6 %collective-permute-start.11 = (bf16[64,2176]{1,0:T(8,128)(2,1)S(1)}, bf16[64,2176]{1,0:T(8,128)(2,1)S(1)}, u32[]{:S(2)}, u32[]{:S(2)}) collective-permute-start(bf16[64,2176]{1,0:T(8,128)(2,1)S(1)} %collective-permute-done.10), channel_id=1, source_target_pairs={{0,4},{1,5},{2,0},{3,1},{4,8},{5,9},{6,2},{7,3},{8,12},{9,13},{10,... | collective-permute-start | bytes 835592 | tf_op jit(solution)/shard_map/ppermute | solution.py:295
  72.8 6.8 %collective-permute-start.15 = (bf16[64,2176]{1,0:T(8,128)(2,1)S(1)}, bf16[64,2176]{1,0:T(8,128)(2,1)S(1)}, u32[]{:S(2)}, u32[]{:S(2)}) collective-permute-start(bf16[64,2176]{1,0:T(8,128)(2,1)S(1)} %collective-permute-done.14), channel_id=1, source_target_pairs={{0,2},{1,3},{2,6},{3,7},{4,0},{5,1},{6,10},{7,11},{8,4},{9,5},{10,... | collective-permute-start | bytes 835592 | tf_op jit(solution)/shard_map/ppermute | solution.py:295
  83.9 6.4 %collective-permute-start.21 = (bf16[64,2048]{1,0:T(8,128)(2,1)S(1)}, bf16[64,2048]{1,0:T(8,128)(2,1)S(1)}, u32[]{:S(2)}, u32[]{:S(2)}) collective-permute-start(bf16[64,2048]{1,0:T(8,128)(2,1)S(1)} %get-tuple-element.89), channel_id=1, source_target_pairs={{0,4},{1,5},{2,0},{3,1},{4,8},{5,9},{6,2},{7,3},{8,12},{9,13},{10,... | collective-permute-start | bytes 786440 | tf_op jit(solution)/shard_map/ppermute | solution.py:295
  84.9 6.4 %collective-permute-start.31 = (bf16[64,2048]{1,0:T(8,128)(2,1)S(1)}, bf16[64,2048]{1,0:T(8,128)(2,1)S(1)}, u32[]{:S(2)}, u32[]{:S(2)}) collective-permute-start(bf16[64,2048]{1,0:T(8,128)(2,1)S(1)} %get-tuple-element.88), channel_id=1, source_target_pairs={{0,2},{1,3},{2,6},{3,7},{4,0},{5,1},{6,10},{7,11},{8,4},{9,5},{10,... | collective-permute-start | bytes 786440 | tf_op jit(solution)/shard_map/ppermute | solution.py:295
  87.2 7.4 %collective-permute-start.22 = (bf16[64,2048]{1,0:T(8,128)(2,1)S(1)}, bf16[64,2048]{1,0:T(8,128)(2,1)S(1)}, u32[]{:S(2)}, u32[]{:S(2)}) collective-permute-start(bf16[64,2048]{1,0:T(8,128)(2,1)S(1)} %get-tuple-element.87), channel_id=1, source_target_pairs={{0,4},{1,5},{2,0},{3,1},{4,8},{5,9},{6,2},{7,3},{8,12},{9,13},{10,... | collective-permute-start | bytes 786440 | tf_op jit(solution)/shard_map/ppermute | solution.py:295
  88.2 7.6 %collective-permute-start.25 = (bf16[64,2048]{1,0:T(8,128)(2,1)S(1)}, bf16[64,2048]{1,0:T(8,128)(2,1)S(1)}, u32[]{:S(2)}, u32[]{:S(2)}) collective-permute-start(bf16[64,2048]{1,0:T(8,128)(2,1)S(1)} %get-tuple-element.86), channel_id=1, source_target_pairs={{0,2},{1,3},{2,6},{3,7},{4,0},{5,1},{6,10},{7,11},{8,4},{9,5},{10,... | collective-permute-start | bytes 786440 | tf_op jit(solution)/shard_map/ppermute | solution.py:295
  102.0 18.5 %collective-permute-start.24 = (bf16[64,2048]{1,0:T(8,128)(2,1)S(1)}, bf16[64,2048]{1,0:T(8,128)(2,1)S(1)}, u32[]{:S(2)}, u32[]{:S(2)}) collective-permute-start(bf16[64,2048]{1,0:T(8,128)(2,1)S(1)} %get-tuple-element.77), channel_id=1, source_target_pairs={{0,4},{1,5},{2,0},{3,1},{4,8},{5,9},{6,2},{7,3},{8,12},{9,13},{10,... | collective-permute-start | bytes 786440 | tf_op jit(solution)/shard_map/ppermute | solution.py:295
  103.9 10.0 %collective-permute-start.23 = (bf16[64,2048]{1,0:T(8,128)(2,1)S(1)}, bf16[64,2048]{1,0:T(8,128)(2,1)S(1)}, u32[]{:S(2)}, u32[]{:S(2)}) collective-permute-start(bf16[64,2048]{1,0:T(8,128)(2,1)S(1)} %get-tuple-element.85), channel_id=1, source_target_pairs={{0,4},{1,5},{2,0},{3,1},{4,8},{5,9},{6,2},{7,3},{8,12},{9,13},{10,... | collective-permute-start | bytes 786440 | tf_op jit(solution)/shard_map/ppermute | solution.py:295
  105.9 14.7 %collective-permute-start.32 = (bf16[64,2048]{1,0:T(8,128)(2,1)S(1)}, bf16[64,2048]{1,0:T(8,128)(2,1)S(1)}, u32[]{:S(2)}, u32[]{:S(2)}) collective-permute-start(bf16[64,2048]{1,0:T(8,128)(2,1)S(1)} %get-tuple-element.76), channel_id=1, source_target_pairs={{0,2},{1,3},{2,6},{3,7},{4,0},{5,1},{6,10},{7,11},{8,4},{9,5},{10,... | collective-permute-start | bytes 786440 | tf_op jit(solution)/shard_map/ppermute | solution.py:295
  105.9 12.3 %collective-permute-start.27 = (bf16[64,2048]{1,0:T(8,128)(2,1)S(1)}, bf16[64,2048]{1,0:T(8,128)(2,1)S(1)}, u32[]{:S(2)}, u32[]{:S(2)}) collective-permute-start(bf16[64,2048]{1,0:T(8,128)(2,1)S(1)} %get-tuple-element.84), channel_id=1, source_target_pairs={{0,2},{1,3},{2,6},{3,7},{4,0},{5,1},{6,10},{7,11},{8,4},{9,5},{10,... | collective-permute-start | bytes 786440 | tf_op jit(solution)/shard_map/ppermute | solution.py:295
  118.3 14.2 %collective-permute-start.29 = (bf16[64,2048]{1,0:T(8,128)(2,1)S(1)}, bf16[64,2048]{1,0:T(8,128)(2,1)S(1)}, u32[]{:S(2)}, u32[]{:S(2)}) collective-permute-start(bf16[64,2048]{1,0:T(8,128)(2,1)S(1)} %get-tuple-element.79), channel_id=1, source_target_pairs={{0,4},{1,5},{2,0},{3,1},{4,8},{5,9},{6,2},{7,3},{8,12},{9,13},{10,... | collective-permute-start | bytes 786440 | tf_op jit(solution)/shard_map/ppermute | solution.py:295
  120.8 8.2 %collective-permute-start.26 = (bf16[64,2048]{1,0:T(8,128)(2,1)S(1)}, bf16[64,2048]{1,0:T(8,128)(2,1)S(1)}, u32[]{:S(2)}, u32[]{:S(2)}) collective-permute-start(bf16[64,2048]{1,0:T(8,128)(2,1)S(1)} %get-tuple-element.75), channel_id=1, source_target_pairs={{0,4},{1,5},{2,0},{3,1},{4,8},{5,9},{6,2},{7,3},{8,12},{9,13},{10,... | collective-permute-start | bytes 786440 | tf_op jit(solution)/shard_map/ppermute | solution.py:295
  123.0 6.4 %collective-permute-start.33 = (bf16[64,2048]{1,0:T(8,128)(2,1)S(1)}, bf16[64,2048]{1,0:T(8,128)(2,1)S(1)}, u32[]{:S(2)}, u32[]{:S(2)}) collective-permute-start(bf16[64,2048]{1,0:T(8,128)(2,1)S(1)} %get-tuple-element.74), channel_id=1, source_target_pairs={{0,2},{1,3},{2,6},{3,7},{4,0},{5,1},{6,10},{7,11},{8,4},{9,5},{10,... | collective-permute-start | bytes 786440 | tf_op jit(solution)/shard_map/ppermute | solution.py:295
  123.0 9.6 %collective-permute-start.30 = (bf16[64,2048]{1,0:T(8,128)(2,1)S(1)}, bf16[64,2048]{1,0:T(8,128)(2,1)S(1)}, u32[]{:S(2)}, u32[]{:S(2)}) collective-permute-start(bf16[64,2048]{1,0:T(8,128)(2,1)S(1)} %get-tuple-element.78), channel_id=1, source_target_pairs={{0,2},{1,3},{2,6},{3,7},{4,0},{5,1},{6,10},{7,11},{8,4},{9,5},{10,... | collective-permute-start | bytes 786440 | tf_op jit(solution)/shard_map/ppermute | solution.py:295
  129.5 6.4 %collective-permute-start.28 = (bf16[64,2048]{1,0:T(8,128)(2,1)S(1)}, bf16[64,2048]{1,0:T(8,128)(2,1)S(1)}, u32[]{:S(2)}, u32[]{:S(2)}) collective-permute-start(bf16[64,2048]{1,0:T(8,128)(2,1)S(1)} %get-tuple-element.73), channel_id=1, source_target_pairs={{0,4},{1,5},{2,0},{3,1},{4,8},{5,9},{6,2},{7,3},{8,12},{9,13},{10,... | collective-permute-start | bytes 786440 | tf_op jit(solution)/shard_map/ppermute | solution.py:295
  129.9 6.4 %collective-permute-start.34 = (bf16[64,2048]{1,0:T(8,128)(2,1)S(1)}, bf16[64,2048]{1,0:T(8,128)(2,1)S(1)}, u32[]{:S(2)}, u32[]{:S(2)}) collective-permute-start(bf16[64,2048]{1,0:T(8,128)(2,1)S(1)} %get-tuple-element.72), channel_id=1, source_target_pairs={{0,2},{1,3},{2,6},{3,7},{4,0},{5,1},{6,10},{7,11},{8,4},{9,5},{10,... | collective-permute-start | bytes 786440 | tf_op jit(solution)/shard_map/ppermute | solution.py:295

commit v11 on v9

--- a/solution.py
+++ b/solution.py
@@ -48,6 +48,7 @@
     state_ref,
     top_ref,
     bottom_ref,
+    next_ref,
     g_ref,
     ss_ref,
     step_ref,
@@ -61,10 +62,15 @@
     step_size, decay = step_ref[chunk, :], decay_ref[chunk, :]
     decay_col = decay.T
     carry_col = jnp.exp(decay_col)
+    end = decay[:, frames - 1 : frames]
+    tail = (jnp.exp(end - decay) * step_size).T
+    kept = jnp.exp(end)
+    b = b_ref[...]
+    upper = lax.broadcasted_iota(jnp.int32, (2 * head, b.shape[1]), 0) < head
     t = lax.broadcasted_iota(jnp.int32, (frames, frames), 0)
     s = lax.broadcasted_iota(jnp.int32, (frames, frames), 1)
     c = c_ref[...]
-    scores = lax.dot_general(c, b_ref[...], NT, preferred_element_type=jnp.float32)
+    scores = lax.dot_general(c, b, NT, preferred_element_type=jnp.float32)
     scores = jnp.where(s <= t, scores, 0.0)
     cc = jnp.concatenate([c, c], axis=1)
     left = lax.broadcasted_iota(jnp.int32, (frames, 2 * head), 1) < head
@@ -96,6 +102,11 @@
         z = z_ref[:, at].astype(jnp.float32)
         g = mixed * jax.nn.silu(z)
         g_ref[i, :, at] = g
+        factor = jnp.where(left, tail[:, 2 * pair : 2 * pair + 1], tail[:, 2 * pair + 1 : 2 * pair + 2])
+        scaled = (x.astype(jnp.float32) * factor).astype(jnp.bfloat16)
+        added = lax.dot_general(scaled, b, TN, preferred_element_type=jnp.float32)
+        keep = jnp.where(upper, kept[2 * pair : 2 * pair + 1, :], kept[2 * pair + 1 : 2 * pair + 2, :])
+        next_ref[at, :] = keep * state + added
         squares = g * g if squares is None else squares + g * g
 
     @pl.when(i == 0)
@@ -117,27 +128,6 @@
             normed = (g_ref[j] * scale * gain_ref[:, at]).astype(jnp.bfloat16)
             top_ref[:, at] = normed[: frames // 2]
             bottom_ref[:, at] = normed[frames // 2 :]
-
-
-def state_kernel(x_ref, b_ref, dt_ref, bias_ref, a_ref, state_ref, out_ref, step_ref, decay_ref):
-    i = pl.program_id(0)
-    frames, width = x_ref.shape
-    head = width // CHUNK
-    pl.when(i == 0)(lambda: decays(dt_ref, bias_ref, a_ref, step_ref, decay_ref))
-    chunk = pl.ds(pl.multiple_of(i * CHUNK, CHUNK), CHUNK)
-    step_size, decay = step_ref[chunk, :], decay_ref[chunk, :]
-    end = decay[:, frames - 1 : frames]
-    tail = (jnp.exp(end - decay) * step_size).T
-    kept = jnp.exp(end)
-    left = lax.broadcasted_iota(jnp.int32, (frames, 2 * head), 1) < head
-    upper = lax.broadcasted_iota(jnp.int32, (2 * head, b_ref.shape[1]), 0) < head
-    for pair in range(CHUNK // 2):
-        at = slice(2 * head * pair, 2 * head * (pair + 1))
-        factor = jnp.where(left, tail[:, 2 * pair : 2 * pair + 1], tail[:, 2 * pair + 1 : 2 * pair + 2])
-        scaled = (x_ref[:, at].astype(jnp.float32) * factor).astype(jnp.bfloat16)
-        added = lax.dot_general(scaled, b_ref[...], TN, preferred_element_type=jnp.float32)
-        keep = jnp.where(upper, kept[2 * pair : 2 * pair + 1, :], kept[2 * pair + 1 : 2 * pair + 2, :])
-        out_ref[at, :] = keep * state_ref[at, :] + added
 
 
 def ssm_mixer(
@@ -156,7 +146,7 @@
     rows = pl.BlockSpec((part, inner), lambda i: (i, 0))
     full_row = pl.BlockSpec((1, width), lambda i: (0, 0))
     tables = [pltpu.VMEM((heads, frames), jnp.float32)] * 2
-    normed = pl.pallas_call(
+    top, bottom, state = pl.pallas_call(
         mixer_kernel,
         grid=(steps,),
         in_specs=[
@@ -171,8 +161,9 @@
             full_row,
             rows,
         ],
-        out_specs=[pl.BlockSpec((frames // 2, width), lambda i: (0, 0))] * 2,
-        out_shape=[jax.ShapeDtypeStruct((frames // 2, width), jnp.bfloat16)] * 2,
+        out_specs=[pl.BlockSpec((frames // 2, width), lambda i: (0, 0))] * 2 + [rows],
+        out_shape=[jax.ShapeDtypeStruct((frames // 2, width), jnp.bfloat16)] * 2
+        + [jax.ShapeDtypeStruct((width, inner), jnp.float32)],
         scratch_shapes=[
             pltpu.VMEM((steps, frames, part), jnp.float32),
             pltpu.VMEM((frames, 2 * head), jnp.float32),
@@ -194,21 +185,7 @@
         state,
     )
 
-    def state_next(ssm_input):
-        out = pl.pallas_call(
-            state_kernel,
-            grid=(steps,),
-            in_specs=[column, whole, per_head, scalar, scalar, rows],
-            out_specs=rows,
-            out_shape=jax.ShapeDtypeStruct((width, inner), jnp.float32),
-            scratch_shapes=tables,
-            compiler_params=pltpu.CompilerParams(vmem_limit_bytes=16 << 20),
-            cost_estimate=pl.CostEstimate(flops=70_000_000, bytes_accessed=3_000_000, transcendentals=20_000),
-            name="state",
-        )(ssm_input, b_proj, dt, dt_bias[None, :], a_log[None, :], state)
-        return out.reshape(heads, head, inner)
-
-    return (normed, state_next)
+    return ((top, bottom), state.reshape(heads, head, inner))
 
 
 def slot_positions(route_ids, experts):
@@ -235,7 +212,7 @@
     route_ids,
     route_weights,
 ):
-    normed, state_next = ssm_mixer(
+    normed, state = ssm_mixer(
         ssm_input,
         gate_input,
         b_proj,
@@ -252,19 +229,13 @@
     experts = local_experts * lax.axis_size(("wide", "narrow"))
     wide, narrow = lax.axis_size("wide"), lax.axis_size("narrow")
     if experts <= 4 * topk_count and narrow == 4 and wide & (wide - 1) == 0 and local_experts == 1:
-        layer_out, state = dense_experts(
-            normed,
-            out_proj,
-            expert_in[0],
-            expert_out[0],
-            route_ids,
-            route_weights,
-            lambda tie: state_next(after(ssm_input, tie)),
+        layer_out = dense_experts(
+            normed, out_proj, expert_in[0], expert_out[0], route_ids, route_weights
         )
     else:
-        normed = jnp.concatenate(normed)
-        layer_out = routed_experts(normed, out_proj, expert_in, expert_out, route_ids, route_weights)
-        state = state_next(ssm_input)
+        layer_out = routed_experts(
+            jnp.concatenate(normed), out_proj, expert_in, expert_out, route_ids, route_weights
+        )
     return (layer_out, state[None])
 
 
@@ -282,7 +253,7 @@
     return lax.optimization_barrier((value, *others))[0]
 
 
-def dense_experts(normed, out_proj, expert_in, expert_out, route_ids, route_weights, state_next):
+def dense_experts(normed, out_proj, expert_in, expert_out, route_ids, route_weights):
     frames = route_ids.shape[0]
     wide = lax.axis_size("wide")
     ring = 2 * wide
@@ -326,25 +297,35 @@
             jnp.concatenate([out_other, out_proj], axis=1),
         )
     )
-    sent = [to_x(normed_top), to_x(after(normed_bottom, columns))]
+    columns, normed_bottom = lax.optimization_barrier((columns, normed_bottom))
+    sent = [to_x(normed_top), to_x(normed_bottom)]
 
     def project(rows):
         return jnp.dot(rows, columns, preferred_element_type=jnp.float32).astype(jnp.bfloat16)
-
-    own = [project(normed_top), project(normed_bottom)]
 
     def merge(gates, other, low):
         return jnp.where(
             low, jnp.concatenate([gates, other], axis=1), jnp.concatenate([other, gates], axis=1)
         )
 
-    rows, peer = [], None
+    own = [project(normed_top), project(normed_bottom)]
+    gates, own[0] = lax.optimization_barrier((gates, own[0]))
+    step = 1
+    while step < wide:
+        other = send(gates, lambda z, x, c: (z ^ step, x, c))
+        gates, step = merge(gates, other, z & step == 0), 2 * step
+    sent[1], gates = lax.optimization_barrier((sent[1], gates))
+    mine = (z * 2 + x) * 2 + core
+    pair = jnp.stack([mine, mine + 1 - 2 * core])
+    gates = jnp.sum(
+        jnp.where(pair[:, None] == jnp.arange(experts), gates[..., None, :], 0.0), axis=-1
+    )
+    gates = jnp.concatenate([gates[0], gates[1, ::-1]])
+    gates = lax.dynamic_slice_in_dim(jnp.concatenate([gates, gates]), place, ring, 0)
+
+    rows = []
     for h in halves:
-        arrived = sent[h]
-        if peer is not None:
-            arrived = after(arrived, peer)
-        peer = project(arrived)
-        back = to_x(peer)
+        back = to_x(project(sent[h]))
         rows.append(
             jnp.where(
                 x == 0,
@@ -353,27 +334,13 @@
             )
         )
 
+    rows[1], expert_in, expert_out = lax.optimization_barrier((rows[1], expert_in, expert_out))
+
     far = ring // 2
     fore_at, back_at = {0: rows}, {0: rows}
-    gates, step = after(gates, sent[1]), 1
     for k in range(1, far):
-        if step < wide:
-            other = send(gates, lambda z, x, c: (z ^ step, x, c))
         fore_at[k] = [along(fore_at[k - 1][h], 1) for h in halves]
         back_at[k] = [along(back_at[k - 1][h], -1) for h in halves]
-        if step < wide:
-            other, back_at[k][1] = lax.optimization_barrier((other, back_at[k][1]))
-            gates, step = merge(gates, other, z & step == 0), 2 * step
-    while step < wide:
-        other = send(gates, lambda z, x, c: (z ^ step, x, c))
-        gates, step = merge(gates, other, z & step == 0), 2 * step
-    mine = (z * 2 + x) * 2 + core
-    pair = jnp.stack([mine, mine + 1 - 2 * core])
-    gates = jnp.sum(
-        jnp.where(pair[:, None] == jnp.arange(experts), gates[..., None, :], 0.0), axis=-1
-    )
-    gates = jnp.concatenate([gates[0], gates[1, ::-1]])
-    gates = lax.dynamic_slice_in_dim(jnp.concatenate([gates, gates]), place, ring, 0)
     last = [along(fore_at[far - 1][0], 1), along(back_at[far - 1][1], -1)]
 
     joined_in = jnp.concatenate(
@@ -396,10 +363,10 @@
         return jnp.dot(hidden, joined_down, preferred_element_type=jnp.float32)
 
     def hop_experts(k, tie):
-        parts = rows if k == 0 else [*back_at[k], *fore_at[k]]
-        gate = gates[0] if k == 0 else jnp.concatenate([gates[k], gates[ring - k]])
-        parts = [after(part, tie) for part in parts]
-        total = run_experts(parts, gate)
+        parts = [after(part, tie) for part in (rows if k == 0 else [*back_at[k], *fore_at[k]])]
+        if k == 0:
+            return run_experts(parts, gates[0]), None
+        total = run_experts(parts, jnp.concatenate([gates[k], gates[ring - k]]))
         cut = [total[i * size : (i + 1) * size] for i in range(len(parts))]
         return cut[:2], cut[2:]
 
@@ -420,16 +387,10 @@
                 way[h] = along(load, step)
             if not before:
                 coming = hop_experts(k - 1, loads[0])
-                before = (*loads, *coming[0], *coming[1])
-                if k == 1:
-                    state = state_next(loads[0])
-                    before += (state,)
+                before = tuple(loads)
         ahead, behind = coming
-    out = []
-    for h in halves:
-        total = ahead[h] + fore[h].astype(jnp.float32) + back[h].astype(jnp.float32)
-        out.append((rows[h].astype(jnp.float32) + total).astype(jnp.bfloat16))
-    return jnp.concatenate(out), state
+    total = ahead + jnp.concatenate(fore).astype(jnp.float32) + jnp.concatenate(back).astype(jnp.float32)
+    return (jnp.concatenate(rows).astype(jnp.float32) + total).astype(jnp.bfloat16)
 
 
 def routed_experts(normed, out_proj, expert_in, expert_out, route_ids, route_weights):

time: 130 us -> 128 us (0.985)
  waiting for transfers between devices: 46.7 us -> 51 us
  matrix products: 19.1 us -> 16.6 us
  starting transfers between devices: 39.8 us -> 42 us
  Pallas kernels: 8.93 us -> 6.84 us
  local copies, waits for them, and re-layouts: 2.68 us -> 0.75 us
  other arithmetic: 11.2 us -> 9.53 us
    ppermute x38, waiting for transfers between devices: 46.7 us -> 51 us  [send(): return lax.ppermute(value, axes, routes(wide, move))]
    pallas_call x1 -> x0, Pallas kernels: 3.58 us -> none  [state_next(): pl.pallas_call(state_kernel, grid=(steps,), in_specs=[column, whole, per_...]
    dot_general x5, matrix products: 10.7 us -> 7.31 us  [run_experts(): jnp.dot(jnp.concatenate(parts), joined_in, preferred_element_type=jnp.flo...]
    ppermute x38, starting transfers between devices: 39.8 us -> 42 us  [send(): return lax.ppermute(value, axes, routes(wide, move))]
    slice x1, local copies, waits for them, and re-layouts: 2.2 us -> 0.32 us  [dense_experts(): in_other[:, :hidden_width]]
    select_n x1, other arithmetic: 3.54 us -> 5.1 us  [dense_experts(): jnp.where(core == 0, jnp.concatenate([out_proj, out_other], axis=1), jnp....]
    pallas_call x1, Pallas kernels: 5.36 us -> 6.84 us  [ssm_mixer(): pl.pallas_call(mixer_kernel, grid=(steps,), in_specs=[pl.BlockSpec(memory...]
  transfers between devices with their start and end apart: 38 -> 38, of which waited for: 19 -> 18; matrix products, arithmetic and copies ran while one was open for 21% -> 17% of each run, Pallas kernels for 7% -> 5%
where the time goes in v11:
time: 128 us
  waiting for transfers between devices  51 us (40%)
  starting transfers between devices  42 us (33%)
  matrix products  16.6 us (13%)
  other arithmetic  9.53 us (7%)
  Pallas kernels  6.84 us (5%)
    ppermute x38, waiting for transfers between devices, send(): return lax.ppermute(value, axes, routes(wide, move))  51 us
    ppermute x38, starting transfers between devices, send(): return lax.ppermute(value, axes, routes(wide, move))  42 us
    dot_general x5, matrix products, run_experts(): jnp.dot(jnp.concatenate(parts), joined_in, preferred_element_type=jnp.flo...  7.31 us
    pallas_call x1, Pallas kernels, ssm_mixer(): pl.pallas_call(mixer_kernel, grid=(steps,), in_specs=[pl.BlockSpec(memory...  6.84 us
    dot_general x5, matrix products, run_experts(): return jnp.dot(hidden, joined_down, preferred_element_type=jnp.float32)  5.9 us
    select_n x1, other arithmetic, dense_experts(): jnp.where(core == 0, jnp.concatenate([out_proj, out_other], axis=1), jnp....  5.1 us
    dot_general x4, matrix products, project(): jnp.dot(rows, columns, preferred_element_type=jnp.float32)  3.38 us
  transfers between devices with their start and end apart: 38, of which 18 were waited for; matrix products, arithmetic and copies ran while one was open for 17% of the time, Pallas kernels for 5%

profile of v11, /device:TPU:0, one launch (start us, length us, event | category | flops | bytes accessed | tf_op | source)
XLA Modules:
  0.0 127.7 jit_solution(12226879243802966620)
XLA Ops:
  1.9 2.6 %collective-permute-start = (f32[128,16]{0,1:T(8,128)S(1)}, f32[128,16]{0,1:T(8,128)S(1)}, u32[]{:S(2)}, u32[]{:S(2)}) collective-permute-start(f32[128,16]{0,1:T(8,128)S(1)} %select_reduce_fusion.1), channel_id=1, source_target_pairs={{0,2},{1,3},{2,0},{3,1},{4,6},{5,7},{6,4},{7,5},{8,10},{9,11},{10,... | collective-permute-start | bytes 24584 | tf_op jit(solution)/shard_map/ppermute | solution.py:266
  5.1 6.8 %mixer.1 = (bf16[64,2048]{1,0:T(8,128)(2,1)}, bf16[64,2048]{1,0:T(8,128)(2,1)}, f32[2048,128]{1,0:T(8,128)}) custom-call(f32[32]{0:T(128)} %skip_ref.1, bf16[128,2048]{1,0:T(8,128)(2,1)} %x_ref.1, bf16[128,2048]{1,0:T(8,128)(2,1)} %z_ref.1, bf16[128,128]{1,0:T(8,128)(2,1)} %b_ref.1, bf16[128,128]{1,0:T(8,128)(2,1)} %c_ref.1, f32[32,128]{1,0:T(8,128)} %bitcast.77, ...), custom_call_target="tpu_custom_call" | custom-call | flops 400000000 | bytes 6000000 | tf_op jit(solution)/shard_map/mixer/pallas_call | solution.py:149
  12.2 5.1 %maximum_select_fusion = bf16[2048,1024]{1,0:T(8,128)(2,1)S(1)} fusion(bf16[2048,512]{1,0:T(8,128)(2,1)} %collective-permute-done.1, bf16[2048,512]{1,0:T(8,128)(2,1)} %param.25, pred[]{:T(512)S(6)} %eq.47), kind=kLoop, calls=%fused_computation.1 | loop fusion | flops 18874368 | bytes 8388609 | tf_op jit(solution)/shard_map/jit(_where)/select_n | solution.py:294
  18.1 2.0 %collective-permute-start.5 = (f32[2,1,128,16]{2,3,1,0:T(8,128)S(1)}, f32[2,1,128,16]{2,3,1,0:T(8,128)S(1)}, u32[]{:S(2)}, u32[]{:S(2)}) collective-permute-start(f32[2,1,128,16]{2,3,1,0:T(8,128)S(1)} %maximum_select_fusion.5), channel_id=1, source_target_pairs={{0,4},{1,5},{2,6},{3,7},{4,0},{5,1},{6,2},{7,3},{8,12},{9,13},{10,... | collective-permute-start | bytes 49160 | tf_op jit(solution)/shard_map/ppermute | solution.py:266
  20.2 1.5 %collective-permute-start.4 = (bf16[64,2048]{1,0:T(8,128)(2,1)S(1)}, bf16[64,2048]{1,0:T(8,128)(2,1)S(1)}, u32[]{:S(2)}, u32[]{:S(2)}) collective-permute-start(bf16[64,2048]{1,0:T(8,128)(2,1)S(1)} %copy-done.2), channel_id=1, source_target_pairs={{0,2},{1,3},{2,0},{3,1},{4,6},{5,7},{6,4},{7,5},{8,10},{9,11},{10,... | collective-permute-start | bytes 786440 | tf_op jit(solution)/shard_map/ppermute | solution.py:266
  23.1 2.7 %collective-permute-start.6 = (f32[2,2,128,16]{2,3,1,0:T(8,128)S(1)}, f32[2,2,128,16]{2,3,1,0:T(8,128)S(1)}, u32[]{:S(2)}, u32[]{:S(2)}) collective-permute-start(f32[2,2,128,16]{2,3,1,0:T(8,128)S(1)} %maximum_select_fusion.4), channel_id=1, source_target_pairs={{0,8},{1,9},{2,10},{3,11},{4,12},{5,13},{6,14},{7,15},{8,0},{9,1},... | collective-permute-start | bytes 98312 | tf_op jit(solution)/shard_map/ppermute | solution.py:266
  26.7 1.7 %collective-permute-done.6 = f32[2,2,128,16]{2,3,1,0:T(8,128)S(1)} collective-permute-done((f32[2,2,128,16]{2,3,1,0:T(8,128)S(1)}, f32[2,2,128,16]{2,3,1,0:T(8,128)S(1)}, u32[]{:S(2)}, u32[]{:S(2)}) %collective-permute-start.6) | collective-permute-done | bytes 32800 | tf_op jit(solution)/shard_map/ppermute | solution.py:266
  28.4 2.5 %collective-permute-done.3 = bf16[64,1024]{1,0:T(8,128)(2,1)S(1)} collective-permute-done((bf16[64,1024]{1,0:T(8,128)(2,1)S(1)}, bf16[64,1024]{1,0:T(8,128)(2,1)S(1)}, u32[]{:S(2)}, u32[]{:S(2)}) %collective-permute-start.3) | collective-permute-done | bytes 131104 | tf_op jit(solution)/shard_map/ppermute | solution.py:266
  31.4 1.7 %collective-permute-start.8 = (bf16[64,2048]{1,0:T(8,128)(2,1)S(1)}, bf16[64,2048]{1,0:T(8,128)(2,1)S(1)}, u32[]{:S(2)}, u32[]{:S(2)}) collective-permute-start(bf16[64,2048]{1,0:T(8,128)(2,1)S(1)} %maximum_select_fusion.1), channel_id=1, source_target_pairs={{0,2},{1,3},{2,6},{3,7},{4,0},{5,1},{6,10},{7,11},{8,4},{9,5},{10,... | collective-permute-start | bytes 786440 | tf_op jit(solution)/shard_map/ppermute | solution.py:266
  33.9 1.6 %collective-permute-start.7 = (bf16[64,1024]{1,0:T(8,128)(2,1)S(1)}, bf16[64,1024]{1,0:T(8,128)(2,1)S(1)}, u32[]{:S(2)}, u32[]{:S(2)}) collective-permute-start(bf16[64,1024]{1,0:T(8,128)(2,1)S(1)} %convolution_convert_fusion.1), channel_id=1, source_target_pairs={{0,2},{1,3},{2,0},{3,1},{4,6},{5,7},{6,4},{7,5},{8,10},{9,11},{10,... | collective-permute-start | bytes 393224 | tf_op jit(solution)/shard_map/ppermute | solution.py:266
  35.7 5.1 %collective-permute-done.7 = bf16[64,1024]{1,0:T(8,128)(2,1)S(1)} collective-permute-done((bf16[64,1024]{1,0:T(8,128)(2,1)S(1)}, bf16[64,1024]{1,0:T(8,128)(2,1)S(1)}, u32[]{:S(2)}, u32[]{:S(2)}) %collective-permute-start.7) | collective-permute-done | bytes 131104 | tf_op jit(solution)/shard_map/ppermute | solution.py:266
  40.9 1.8 %collective-permute-start.15 = (bf16[64,2048]{1,0:T(8,128)(2,1)S(1)}, bf16[64,2048]{1,0:T(8,128)(2,1)S(1)}, u32[]{:S(2)}, u32[]{:S(2)}) collective-permute-start(bf16[64,2048]{1,0:T(8,128)(2,1)S(1)} %maximum_select_fusion.2), channel_id=1, source_target_pairs={{0,2},{1,3},{2,6},{3,7},{4,0},{5,1},{6,10},{7,11},{8,4},{9,5},{10,... | collective-permute-start | bytes 786440 | tf_op jit(solution)/shard_map/ppermute | solution.py:266
  43.3 2.0 %collective-permute-start.9 = (bf16[64,2048]{1,0:T(8,128)(2,1)S(1)}, bf16[64,2048]{1,0:T(8,128)(2,1)S(1)}, u32[]{:S(2)}, u32[]{:S(2)}) collective-permute-start(bf16[64,2048]{1,0:T(8,128)(2,1)S(1)} %collective-permute-done.8), channel_id=1, source_target_pairs={{0,2},{1,3},{2,6},{3,7},{4,0},{5,1},{6,10},{7,11},{8,4},{9,5},{10,... | collective-permute-start | bytes 786440 | tf_op jit(solution)/shard_map/ppermute | solution.py:266
  45.4 9.4 %collective-permute-done.12 = bf16[64,2048]{1,0:T(8,128)(2,1)S(1)} collective-permute-done((bf16[64,2048]{1,0:T(8,128)(2,1)S(1)}, bf16[64,2048]{1,0:T(8,128)(2,1)S(1)}, u32[]{:S(2)}, u32[]{:S(2)}) %collective-permute-start.12) | collective-permute-done | bytes 262176 | tf_op jit(solution)/shard_map/ppermute | solution.py:266
  55.0 1.7 %collective-permute-start.16 = (bf16[64,2048]{1,0:T(8,128)(2,1)S(1)}, bf16[64,2048]{1,0:T(8,128)(2,1)S(1)}, u32[]{:S(2)}, u32[]{:S(2)}) collective-permute-start(bf16[64,2048]{1,0:T(8,128)(2,1)S(1)} %collective-permute-done.15), channel_id=1, source_target_pairs={{0,2},{1,3},{2,6},{3,7},{4,0},{5,1},{6,10},{7,11},{8,4},{9,5},{10,... | collective-permute-start | bytes 786440 | tf_op jit(solution)/shard_map/ppermute | solution.py:266
  57.1 1.9 %pad_maximum_fusion.1 = bf16[768,2048]{1,0:T(8,128)(2,1)S(1)} fusion(bf16[384,2048]{1,0:T(8,128)(2,1)} %collective-permute-done.20, bf16[384,2048]{1,0:T(8,128)(2,1)S(1)} %bitcast.67), kind=kLoop, calls=%fused_computation.2 | loop fusion | flops 6291456 | bytes 6291456 | tf_op jit(solution)/shard_map/concatenate | solution.py:355
  59.0 1.8 %collective-permute-start.10 = (bf16[64,2048]{1,0:T(8,128)(2,1)S(1)}, bf16[64,2048]{1,0:T(8,128)(2,1)S(1)}, u32[]{:S(2)}, u32[]{:S(2)}) collective-permute-start(bf16[64,2048]{1,0:T(8,128)(2,1)S(1)} %collective-permute-done.9), channel_id=1, source_target_pairs={{0,2},{1,3},{2,6},{3,7},{4,0},{5,1},{6,10},{7,11},{8,4},{9,5},{10,... | collective-permute-start | bytes 786440 | tf_op jit(solution)/shard_map/ppermute | solution.py:266
  60.8 3.2 %collective-permute-done.13 = bf16[64,2048]{1,0:T(8,128)(2,1)S(1)} collective-permute-done((bf16[64,2048]{1,0:T(8,128)(2,1)S(1)}, bf16[64,2048]{1,0:T(8,128)(2,1)S(1)}, u32[]{:S(2)}, u32[]{:S(2)}) %collective-permute-start.13) | collective-permute-done | bytes 262176 | tf_op jit(solution)/shard_map/ppermute | solution.py:266
  64.3 1.7 %collective-permute-start.17 = (bf16[64,2048]{1,0:T(8,128)(2,1)S(1)}, bf16[64,2048]{1,0:T(8,128)(2,1)S(1)}, u32[]{:S(2)}, u32[]{:S(2)}) collective-permute-start(bf16[64,2048]{1,0:T(8,128)(2,1)S(1)} %collective-permute-done.16), channel_id=1, source_target_pairs={{0,2},{1,3},{2,6},{3,7},{4,0},{5,1},{6,10},{7,11},{8,4},{9,5},{10,... | collective-permute-start | bytes 786440 | tf_op jit(solution)/shard_map/ppermute | solution.py:266
  66.0 3.6 %collective-permute-done.22 = bf16[64,2048]{1,0:T(8,128)(2,1)S(1)} collective-permute-done((bf16[64,2048]{1,0:T(8,128)(2,1)S(1)}, bf16[64,2048]{1,0:T(8,128)(2,1)S(1)}, u32[]{:S(2)}, u32[]{:S(2)}) %collective-permute-start.22) | collective-permute-done | bytes 262176 | tf_op jit(solution)/shard_map/ppermute | solution.py:266
  70.2 2.5 %collective-permute-done.17 = bf16[64,2048]{1,0:T(8,128)(2,1)S(1)} collective-permute-done((bf16[64,2048]{1,0:T(8,128)(2,1)S(1)}, bf16[64,2048]{1,0:T(8,128)(2,1)S(1)}, u32[]{:S(2)}, u32[]{:S(2)}) %collective-permute-start.17) | collective-permute-done | bytes 262176 | tf_op jit(solution)/shard_map/ppermute | solution.py:266
  72.7 2.2 %collective-permute-start.18 = (bf16[64,2048]{1,0:T(8,128)(2,1)S(1)}, bf16[64,2048]{1,0:T(8,128)(2,1)S(1)}, u32[]{:S(2)}, u32[]{:S(2)}) collective-permute-start(bf16[64,2048]{1,0:T(8,128)(2,1)S(1)} %collective-permute-done.17), channel_id=1, source_target_pairs={{0,2},{1,3},{2,6},{3,7},{4,0},{5,1},{6,10},{7,11},{8,4},{9,5},{10,... | collective-permute-start | bytes 786440 | tf_op jit(solution)/shard_map/ppermute | solution.py:266
  75.7 3.4 %collective-permute-done.18 = bf16[64,2048]{1,0:T(8,128)(2,1)S(1)} collective-permute-done((bf16[64,2048]{1,0:T(8,128)(2,1)S(1)}, bf16[64,2048]{1,0:T(8,128)(2,1)S(1)}, u32[]{:S(2)}, u32[]{:S(2)}) %collective-permute-start.18) | collective-permute-done | bytes 262176 | tf_op jit(solution)/shard_map/ppermute | solution.py:266
  80.9 1.8 %fusion = f32[256,1536]{1,0:T(8,128)S(1)} fusion(bf16[2048,1536]{1,0:T(8,128)(2,1)S(1)} %pad_maximum_fusion, bf16[64,2048]{1,0:T(8,128)(2,1)S(1)} %collective-permute-done.23, bf16[64,2048]{1,0:T(8,128)(2,1)S(1)} %collective-permute-done.13, bf16[64,2048]{1,0:T(8,128)(2,1)S(1)} %collective-permute-done.17, bf16[64,2048]{1,0:T(8,128)(2,1)S(1)} %collective-permute-done.10), kind=kOutput, calls=%fused_computation.8 | convolution fusion | flops 1614807040 | bytes 8912896 | tf_op jit(solution)/shard_map/dot_general | solution.py:360
  82.7 1.2 fusion.104
  83.9 1.1 collective-permute-start.24
  85.0 1.5 %collective-permute-start.28 = (bf16[64,2048]{1,0:T(8,128)(2,1)S(1)}, bf16[64,2048]{1,0:T(8,128)(2,1)S(1)}, u32[]{:S(2)}, u32[]{:S(2)}) collective-permute-start(bf16[64,2048]{1,0:T(8,128)(2,1)S(1)} %get-tuple-element.90), channel_id=1, source_target_pairs={{0,2},{1,3},{2,6},{3,7},{4,0},{5,1},{6,10},{7,11},{8,4},{9,5},{10,... | collective-permute-start | bytes 786440 | tf_op jit(solution)/shard_map/ppermute | solution.py:266
  87.4 1.0 collective-permute-start.34
  88.5 1.8 %fusion.8 = f32[256,1536]{1,0:T(8,128)S(1)} fusion(bf16[2048,1536]{1,0:T(8,128)(2,1)S(1)} %pad_maximum_fusion, bf16[64,2048]{1,0:T(8,128)(2,1)S(1)} %collective-permute-done.22, bf16[64,2048]{1,0:T(8,128)(2,1)S(1)} %collective-permute-done.12, bf16[64,2048]{1,0:T(8,128)(2,1)S(1)} %collective-permute-done.16, bf16[64,2048]{1,0:T(8,128)(2,1)S(1)} %collective-permute-done.9), kind=kOutput, calls=%fused_computation.16 | convolution fusion | flops 1614807040 | bytes 8912896 | tf_op jit(solution)/shard_map/dot_general | solution.py:360
  90.3 1.1 fusion.50
  91.4 2.1 %collective-permute-done.24 = bf16[64,2048]{1,0:T(8,128)(2,1)S(1)} collective-permute-done((bf16[64,2048]{1,0:T(8,128)(2,1)S(1)}, bf16[64,2048]{1,0:T(8,128)(2,1)S(1)}, u32[]{:S(2)}, u32[]{:S(2)}) %collective-permute-start.24) | collective-permute-done | bytes 262176 | tf_op jit(solution)/shard_map/ppermute | solution.py:266
  94.7 2.1 %collective-permute-start.25 = (bf16[64,2048]{1,0:T(8,128)(2,1)S(1)}, bf16[64,2048]{1,0:T(8,128)(2,1)S(1)}, u32[]{:S(2)}, u32[]{:S(2)}) collective-permute-start(bf16[64,2048]{1,0:T(8,128)(2,1)S(1)} %get-tuple-element.89), channel_id=1, source_target_pairs={{0,4},{1,5},{2,0},{3,1},{4,8},{5,9},{6,2},{7,3},{8,12},{9,13},{10,... | collective-permute-start | bytes 786440 | tf_op jit(solution)/shard_map/ppermute | solution.py:266
  96.8 2.1 %collective-permute-done.26 = bf16[64,2048]{1,0:T(8,128)(2,1)S(1)} collective-permute-done((bf16[64,2048]{1,0:T(8,128)(2,1)S(1)}, bf16[64,2048]{1,0:T(8,128)(2,1)S(1)}, u32[]{:S(2)}, u32[]{:S(2)}) %collective-permute-start.26) | collective-permute-done | bytes 262176 | tf_op jit(solution)/shard_map/ppermute | solution.py:266
  98.9 1.3 %collective-permute-done.34 = bf16[64,2048]{1,0:T(8,128)(2,1)S(1)} collective-permute-done((bf16[64,2048]{1,0:T(8,128)(2,1)S(1)}, bf16[64,2048]{1,0:T(8,128)(2,1)S(1)}, u32[]{:S(2)}, u32[]{:S(2)}) %collective-permute-start.34) | collective-permute-done | bytes 262176 | tf_op jit(solution)/shard_map/ppermute | solution.py:266
  100.3 1.6 %collective-permute-start.27 = (bf16[64,2048]{1,0:T(8,128)(2,1)S(1)}, bf16[64,2048]{1,0:T(8,128)(2,1)S(1)}, u32[]{:S(2)}, u32[]{:S(2)}) collective-permute-start(bf16[64,2048]{1,0:T(8,128)(2,1)S(1)} %get-tuple-element.85), channel_id=1, source_target_pairs={{0,4},{1,5},{2,0},{3,1},{4,8},{5,9},{6,2},{7,3},{8,12},{9,13},{10,... | collective-permute-start | bytes 786440 | tf_op jit(solution)/shard_map/ppermute | solution.py:266
  102.3 1.8 %fusion.16 = f32[256,1536]{1,0:T(8,128)S(1)} fusion(bf16[2048,1536]{1,0:T(8,128)(2,1)S(1)} %pad_maximum_fusion, bf16[64,2048]{1,0:T(8,128)(2,1)S(1)} %collective-permute-done.21, bf16[64,2048]{1,0:T(8,128)(2,1)S(1)} %collective-permute-done.11, bf16[64,2048]{1,0:T(8,128)(2,1)S(1)} %collective-permute-done.15, bf16[64,2048]{1,0:T(8,128)(2,1)S(1)} %collective-permute-done.8), kind=kOutput, calls=%fused_computation.24 | convolution fusion | flops 1614807040 | bytes 8912896 | tf_op jit(solution)/shard_map/dot_general | solution.py:360
  104.1 1.2 fusion.52
  105.3 4.2 %collective-permute-done.27 = bf16[64,2048]{1,0:T(8,128)(2,1)S(1)} collective-permute-done((bf16[64,2048]{1,0:T(8,128)(2,1)S(1)}, bf16[64,2048]{1,0:T(8,128)(2,1)S(1)}, u32[]{:S(2)}, u32[]{:S(2)}) %collective-permute-start.27) | collective-permute-done | bytes 262176 | tf_op jit(solution)/shard_map/ppermute | solution.py:266
  109.5 1.6 %collective-permute-done.35 = bf16[64,2048]{1,0:T(8,128)(2,1)S(1)} collective-permute-done((bf16[64,2048]{1,0:T(8,128)(2,1)S(1)}, bf16[64,2048]{1,0:T(8,128)(2,1)S(1)}, u32[]{:S(2)}, u32[]{:S(2)}) %collective-permute-start.35) | collective-permute-done | bytes 262176 | tf_op jit(solution)/shard_map/ppermute | solution.py:266
  111.2 1.0 collective-permute-start.29
  112.2 1.1 collective-permute-start.36
  113.4 1.0 collective-permute-start.32
  114.4 1.1 collective-permute-start.33
  115.5 2.1 %collective-permute-done.29 = bf16[64,2048]{1,0:T(8,128)(2,1)S(1)} collective-permute-done((bf16[64,2048]{1,0:T(8,128)(2,1)S(1)}, bf16[64,2048]{1,0:T(8,128)(2,1)S(1)}, u32[]{:S(2)}, u32[]{:S(2)}) %collective-permute-start.29) | collective-permute-done | bytes 262176 | tf_op jit(solution)/shard_map/ppermute | solution.py:266
  119.6 1.2 collective-permute-start.37
  120.8 1.0 fusion.44
  121.8 3.3 %collective-permute-done.31 = bf16[64,2048]{1,0:T(8,128)(2,1)S(1)} collective-permute-done((bf16[64,2048]{1,0:T(8,128)(2,1)S(1)}, bf16[64,2048]{1,0:T(8,128)(2,1)S(1)}, u32[]{:S(2)}, u32[]{:S(2)}) %collective-permute-start.31) | collective-permute-done | bytes 262176 | tf_op jit(solution)/shard_map/ppermute | solution.py:266
  126.0 1.7 %add_convert_fusion = bf16[128,2048]{1,0:T(8,128)(2,1)} fusion(bf16[64,2048]{1,0:T(8,128)(2,1)S(1)} %maximum_select_fusion.2, bf16[64,2048]{1,0:T(8,128)(2,1)S(1)} %maximum_select_fusion.1, bf16[64,2048]{1,0:T(8,128)(2,1)S(1)} %collective-permute-done.32, bf16[64,2048]{1,0:T(8,128)(2,1)S(1)} %collective-permute-done.31, ...), kind=kOutput, calls=%fused_computation.32 | convolution fusion | flops 407633920 | bytes 6031104 | tf_op jit(solution)/shard_map/dot_general | solution.py:363
  (81 shorter events, 17.3 us)
Async XLA Ops:
  0.6 11.5 %collective-permute-start.1 = (bf16[2048,512]{1,0:T(8,128)(2,1)}, bf16[2048,512]{1,0:T(8,128)(2,1)}, u32[]{:S(2)}, u32[]{:S(2)}) collective-permute-start(bf16[2048,512]{1,0:T(8,128)(2,1)} %param.25), channel_id=1, source_target_pairs={{0,1},{1,0},{2,3},{3,2},{4,5},{5,4},{6,7},{7,6},{8,9},{9,8},{10,11... | collective-permute-start | bytes 6291464 | tf_op jit(solution)/shard_map/ppermute | solution.py:266
  1.9 10.1 %collective-permute-start = (f32[128,16]{0,1:T(8,128)S(1)}, f32[128,16]{0,1:T(8,128)S(1)}, u32[]{:S(2)}, u32[]{:S(2)}) collective-permute-start(f32[128,16]{0,1:T(8,128)S(1)} %select_reduce_fusion.1), channel_id=1, source_target_pairs={{0,2},{1,3},{2,0},{3,1},{4,6},{5,7},{6,4},{7,5},{8,10},{9,11},{10,... | collective-permute-start | bytes 24584 | tf_op jit(solution)/shard_map/ppermute | solution.py:266
  4.4 65.5 %collective-permute-start.19 = (bf16[2048,768]{1,0:T(8,128)(2,1)}, bf16[2048,768]{1,0:T(8,128)(2,1)S(1)}, u32[]{:S(2)}, u32[]{:S(2)}) collective-permute-start(bf16[2048,768]{1,0:T(8,128)(2,1)} %bitcast.64), channel_id=1, source_target_pairs={{0,1},{1,0},{2,3},{3,2},{4,5},{5,4},{6,7},{7,6},{8,9},{9,8},{10,11... | collective-permute-start | bytes 9437192 | tf_op jit(solution)/shard_map/ppermute | solution.py:266
  4.6 38.0 %collective-permute-start.20 = (bf16[384,2048]{1,0:T(8,128)(2,1)}, bf16[384,2048]{1,0:T(8,128)(2,1)}, u32[]{:S(2)}, u32[]{:S(2)}) collective-permute-start(bf16[384,2048]{1,0:T(8,128)(2,1)} %bitcast.66), channel_id=1, source_target_pairs={{0,1},{1,0},{2,3},{3,2},{4,5},{5,4},{6,7},{7,6},{8,9},{9,8},{10,11... | collective-permute-start | bytes 4718600 | tf_op jit(solution)/shard_map/ppermute | solution.py:266
  11.9 9.7 %collective-permute-start.2 = (bf16[64,2048]{1,0:T(8,128)(2,1)}, bf16[64,2048]{1,0:T(8,128)(2,1)S(1)}, u32[]{:S(2)}, u32[]{:S(2)}) collective-permute-start(bf16[64,2048]{1,0:T(8,128)(2,1)} %get-tuple-element.42), channel_id=1, source_target_pairs={{0,2},{1,3},{2,0},{3,1},{4,6},{5,7},{6,4},{7,5},{8,10},{9,11},{10,... | collective-permute-start | bytes 786440 | tf_op jit(solution)/shard_map/ppermute | solution.py:266
  12.2 5.1 %copy-start.3 = (bf16[64,2048]{1,0:T(8,128)(2,1)S(1)}, bf16[64,2048]{1,0:T(8,128)(2,1)}, u32[]{:S(2)}) copy-start(bf16[64,2048]{1,0:T(8,128)(2,1)} %get-tuple-element.42) | copy-start | bytes 786436
  17.3 2.9 %copy-start.2 = (bf16[64,2048]{1,0:T(8,128)(2,1)S(1)}, bf16[64,2048]{1,0:T(8,128)(2,1)}, u32[]{:S(2)}) copy-start(bf16[64,2048]{1,0:T(8,128)(2,1)} %get-tuple-element.46) | copy-start | bytes 786436
  18.1 5.0 %collective-permute-start.5 = (f32[2,1,128,16]{2,3,1,0:T(8,128)S(1)}, f32[2,1,128,16]{2,3,1,0:T(8,128)S(1)}, u32[]{:S(2)}, u32[]{:S(2)}) collective-permute-start(f32[2,1,128,16]{2,3,1,0:T(8,128)S(1)} %maximum_select_fusion.5), channel_id=1, source_target_pairs={{0,4},{1,5},{2,6},{3,7},{4,0},{5,1},{6,2},{7,3},{8,12},{9,13},{10,... | collective-permute-start | bytes 49160 | tf_op jit(solution)/shard_map/ppermute | solution.py:266
  20.2 12.8 %collective-permute-start.4 = (bf16[64,2048]{1,0:T(8,128)(2,1)S(1)}, bf16[64,2048]{1,0:T(8,128)(2,1)S(1)}, u32[]{:S(2)}, u32[]{:S(2)}) collective-permute-start(bf16[64,2048]{1,0:T(8,128)(2,1)S(1)} %copy-done.2), channel_id=1, source_target_pairs={{0,2},{1,3},{2,0},{3,1},{4,6},{5,7},{6,4},{7,5},{8,10},{9,11},{10,... | collective-permute-start | bytes 786440 | tf_op jit(solution)/shard_map/ppermute | solution.py:266
  22.5 8.3 %collective-permute-start.3 = (bf16[64,1024]{1,0:T(8,128)(2,1)S(1)}, bf16[64,1024]{1,0:T(8,128)(2,1)S(1)}, u32[]{:S(2)}, u32[]{:S(2)}) collective-permute-start(bf16[64,1024]{1,0:T(8,128)(2,1)S(1)} %convolution_convert_fusion.3), channel_id=1, source_target_pairs={{0,2},{1,3},{2,0},{3,1},{4,6},{5,7},{6,4},{7,5},{8,10},{9,11},{10,... | collective-permute-start | bytes 393224 | tf_op jit(solution)/shard_map/ppermute | solution.py:266
  23.1 5.2 %collective-permute-start.6 = (f32[2,2,128,16]{2,3,1,0:T(8,128)S(1)}, f32[2,2,128,16]{2,3,1,0:T(8,128)S(1)}, u32[]{:S(2)}, u32[]{:S(2)}) collective-permute-start(f32[2,2,128,16]{2,3,1,0:T(8,128)S(1)} %maximum_select_fusion.4), channel_id=1, source_target_pairs={{0,8},{1,9},{2,10},{3,11},{4,12},{5,13},{6,14},{7,15},{8,0},{9,1},... | collective-permute-start | bytes 98312 | tf_op jit(solution)/shard_map/ppermute | solution.py:266
  26.6 16.4 %copy-start = (bf16[1,2048,768]{2,1,0:T(8,128)(2,1)S(1)}, bf16[1,2048,768]{2,1,0:T(8,128)(2,1)}, u32[]{:S(2)}) copy-start(bf16[1,2048,768]{2,1,0:T(8,128)(2,1)} %param.26) | copy-start | bytes 9437188
  30.9 12.0 %collective-permute-start.11 = (bf16[64,2048]{1,0:T(8,128)(2,1)S(1)}, bf16[64,2048]{1,0:T(8,128)(2,1)S(1)}, u32[]{:S(2)}, u32[]{:S(2)}) collective-permute-start(bf16[64,2048]{1,0:T(8,128)(2,1)S(1)} %maximum_select_fusion.1), channel_id=1, source_target_pairs={{0,4},{1,5},{2,0},{3,1},{4,8},{5,9},{6,2},{7,3},{8,12},{9,13},{10,... | collective-permute-start | bytes 786440 | tf_op jit(solution)/shard_map/ppermute | solution.py:266
  31.4 12.0 %collective-permute-start.8 = (bf16[64,2048]{1,0:T(8,128)(2,1)S(1)}, bf16[64,2048]{1,0:T(8,128)(2,1)S(1)}, u32[]{:S(2)}, u32[]{:S(2)}) collective-permute-start(bf16[64,2048]{1,0:T(8,128)(2,1)S(1)} %maximum_select_fusion.1), channel_id=1, source_target_pairs={{0,2},{1,3},{2,6},{3,7},{4,0},{5,1},{6,10},{7,11},{8,4},{9,5},{10,... | collective-permute-start | bytes 786440 | tf_op jit(solution)/shard_map/ppermute | solution.py:266
  33.9 6.9 %collective-permute-start.7 = (bf16[64,1024]{1,0:T(8,128)(2,1)S(1)}, bf16[64,1024]{1,0:T(8,128)(2,1)S(1)}, u32[]{:S(2)}, u32[]{:S(2)}) collective-permute-start(bf16[64,1024]{1,0:T(8,128)(2,1)S(1)} %convolution_convert_fusion.1), channel_id=1, source_target_pairs={{0,2},{1,3},{2,0},{3,1},{4,6},{5,7},{6,4},{7,5},{8,10},{9,11},{10,... | collective-permute-start | bytes 393224 | tf_op jit(solution)/shard_map/ppermute | solution.py:266
  40.8 16.2 %copy-start.1 = (bf16[1,384,2048]{2,1,0:T(8,128)(2,1)S(1)}, bf16[1,384,2048]{2,1,0:T(8,128)(2,1)}, u32[]{:S(2)}) copy-start(bf16[1,384,2048]{2,1,0:T(8,128)(2,1)} %param.27) | copy-start | bytes 4718596
  40.9 14.2 %collective-permute-start.15 = (bf16[64,2048]{1,0:T(8,128)(2,1)S(1)}, bf16[64,2048]{1,0:T(8,128)(2,1)S(1)}, u32[]{:S(2)}, u32[]{:S(2)}) collective-permute-start(bf16[64,2048]{1,0:T(8,128)(2,1)S(1)} %maximum_select_fusion.2), channel_id=1, source_target_pairs={{0,2},{1,3},{2,6},{3,7},{4,0},{5,1},{6,10},{7,11},{8,4},{9,5},{10,... | collective-permute-start | bytes 786440 | tf_op jit(solution)/shard_map/ppermute | solution.py:266
  42.7 14.1 %collective-permute-start.21 = (bf16[64,2048]{1,0:T(8,128)(2,1)S(1)}, bf16[64,2048]{1,0:T(8,128)(2,1)S(1)}, u32[]{:S(2)}, u32[]{:S(2)}) collective-permute-start(bf16[64,2048]{1,0:T(8,128)(2,1)S(1)} %maximum_select_fusion.2), channel_id=1, source_target_pairs={{0,4},{1,5},{2,0},{3,1},{4,8},{5,9},{6,2},{7,3},{8,12},{9,13},{10,... | collective-permute-start | bytes 786440 | tf_op jit(solution)/shard_map/ppermute | solution.py:266
  42.9 11.8 %collective-permute-start.12 = (bf16[64,2048]{1,0:T(8,128)(2,1)S(1)}, bf16[64,2048]{1,0:T(8,128)(2,1)S(1)}, u32[]{:S(2)}, u32[]{:S(2)}) collective-permute-start(bf16[64,2048]{1,0:T(8,128)(2,1)S(1)} %collective-permute-done.11), channel_id=1, source_target_pairs={{0,4},{1,5},{2,0},{3,1},{4,8},{5,9},{6,2},{7,3},{8,12},{9,13},{10,... | collective-permute-start | bytes 786440 | tf_op jit(solution)/shard_map/ppermute | solution.py:266
  43.3 15.7 %collective-permute-start.9 = (bf16[64,2048]{1,0:T(8,128)(2,1)S(1)}, bf16[64,2048]{1,0:T(8,128)(2,1)S(1)}, u32[]{:S(2)}, u32[]{:S(2)}) collective-permute-start(bf16[64,2048]{1,0:T(8,128)(2,1)S(1)} %collective-permute-done.8), channel_id=1, source_target_pairs={{0,2},{1,3},{2,6},{3,7},{4,0},{5,1},{6,10},{7,11},{8,4},{9,5},{10,... | collective-permute-start | bytes 786440 | tf_op jit(solution)/shard_map/ppermute | solution.py:266
  54.8 9.2 %collective-permute-start.13 = (bf16[64,2048]{1,0:T(8,128)(2,1)S(1)}, bf16[64,2048]{1,0:T(8,128)(2,1)S(1)}, u32[]{:S(2)}, u32[]{:S(2)}) collective-permute-start(bf16[64,2048]{1,0:T(8,128)(2,1)S(1)} %collective-permute-done.12), channel_id=1, source_target_pairs={{0,4},{1,5},{2,0},{3,1},{4,8},{5,9},{6,2},{7,3},{8,12},{9,13},{10,... | collective-permute-start | bytes 786440 | tf_op jit(solution)/shard_map/ppermute | solution.py:266
  55.0 9.2 %collective-permute-start.16 = (bf16[64,2048]{1,0:T(8,128)(2,1)S(1)}, bf16[64,2048]{1,0:T(8,128)(2,1)S(1)}, u32[]{:S(2)}, u32[]{:S(2)}) collective-permute-start(bf16[64,2048]{1,0:T(8,128)(2,1)S(1)} %collective-permute-done.15), channel_id=1, source_target_pairs={{0,2},{1,3},{2,6},{3,7},{4,0},{5,1},{6,10},{7,11},{8,4},{9,5},{10,... | collective-permute-start | bytes 786440 | tf_op jit(solution)/shard_map/ppermute | solution.py:266
  56.8 12.8 %collective-permute-start.22 = (bf16[64,2048]{1,0:T(8,128)(2,1)S(1)}, bf16[64,2048]{1,0:T(8,128)(2,1)S(1)}, u32[]{:S(2)}, u32[]{:S(2)}) collective-permute-start(bf16[64,2048]{1,0:T(8,128)(2,1)S(1)} %collective-permute-done.21), channel_id=1, source_target_pairs={{0,4},{1,5},{2,0},{3,1},{4,8},{5,9},{6,2},{7,3},{8,12},{9,13},{10,... | collective-permute-start | bytes 786440 | tf_op jit(solution)/shard_map/ppermute | solution.py:266
  59.0 21.8 %collective-permute-start.10 = (bf16[64,2048]{1,0:T(8,128)(2,1)S(1)}, bf16[64,2048]{1,0:T(8,128)(2,1)S(1)}, u32[]{:S(2)}, u32[]{:S(2)}) collective-permute-start(bf16[64,2048]{1,0:T(8,128)(2,1)S(1)} %collective-permute-done.9), channel_id=1, source_target_pairs={{0,2},{1,3},{2,6},{3,7},{4,0},{5,1},{6,10},{7,11},{8,4},{9,5},{10,... | collective-permute-start | bytes 786440 | tf_op jit(solution)/shard_map/ppermute | solution.py:266
  64.0 11.7 %collective-permute-start.14 = (bf16[64,2048]{1,0:T(8,128)(2,1)S(1)}, bf16[64,2048]{1,0:T(8,128)(2,1)S(1)}, u32[]{:S(2)}, u32[]{:S(2)}) collective-permute-start(bf16[64,2048]{1,0:T(8,128)(2,1)S(1)} %collective-permute-done.13), channel_id=1, source_target_pairs={{0,4},{1,5},{2,0},{3,1},{4,8},{5,9},{6,2},{7,3},{8,12},{9,13},{10,... | collective-permute-start | bytes 786440 | tf_op jit(solution)/shard_map/ppermute | solution.py:266
  64.3 8.5 %collective-permute-start.17 = (bf16[64,2048]{1,0:T(8,128)(2,1)S(1)}, bf16[64,2048]{1,0:T(8,128)(2,1)S(1)}, u32[]{:S(2)}, u32[]{:S(2)}) collective-permute-start(bf16[64,2048]{1,0:T(8,128)(2,1)S(1)} %collective-permute-done.16), channel_id=1, source_target_pairs={{0,2},{1,3},{2,6},{3,7},{4,0},{5,1},{6,10},{7,11},{8,4},{9,5},{10,... | collective-permute-start | bytes 786440 | tf_op jit(solution)/shard_map/ppermute | solution.py:266
  69.6 11.3 %collective-permute-start.23 = (bf16[64,2048]{1,0:T(8,128)(2,1)S(1)}, bf16[64,2048]{1,0:T(8,128)(2,1)S(1)}, u32[]{:S(2)}, u32[]{:S(2)}) collective-permute-start(bf16[64,2048]{1,0:T(8,128)(2,1)S(1)} %collective-permute-done.22), channel_id=1, source_target_pairs={{0,4},{1,5},{2,0},{3,1},{4,8},{5,9},{6,2},{7,3},{8,12},{9,13},{10,... | collective-permute-start | bytes 786440 | tf_op jit(solution)/shard_map/ppermute | solution.py:266
  72.7 6.4 %collective-permute-start.18 = (bf16[64,2048]{1,0:T(8,128)(2,1)S(1)}, bf16[64,2048]{1,0:T(8,128)(2,1)S(1)}, u32[]{:S(2)}, u32[]{:S(2)}) collective-permute-start(bf16[64,2048]{1,0:T(8,128)(2,1)S(1)} %collective-permute-done.17), channel_id=1, source_target_pairs={{0,2},{1,3},{2,6},{3,7},{4,0},{5,1},{6,10},{7,11},{8,4},{9,5},{10,... | collective-permute-start | bytes 786440 | tf_op jit(solution)/shard_map/ppermute | solution.py:266
  83.9 9.6 %collective-permute-start.24 = (bf16[64,2048]{1,0:T(8,128)(2,1)S(1)}, bf16[64,2048]{1,0:T(8,128)(2,1)S(1)}, u32[]{:S(2)}, u32[]{:S(2)}) collective-permute-start(bf16[64,2048]{1,0:T(8,128)(2,1)S(1)} %get-tuple-element.91), channel_id=1, source_target_pairs={{0,4},{1,5},{2,0},{3,1},{4,8},{5,9},{6,2},{7,3},{8,12},{9,13},{10,... | collective-permute-start | bytes 786440 | tf_op jit(solution)/shard_map/ppermute | solution.py:266
  85.0 9.5 %collective-permute-start.28 = (bf16[64,2048]{1,0:T(8,128)(2,1)S(1)}, bf16[64,2048]{1,0:T(8,128)(2,1)S(1)}, u32[]{:S(2)}, u32[]{:S(2)}) collective-permute-start(bf16[64,2048]{1,0:T(8,128)(2,1)S(1)} %get-tuple-element.90), channel_id=1, source_target_pairs={{0,2},{1,3},{2,6},{3,7},{4,0},{5,1},{6,10},{7,11},{8,4},{9,5},{10,... | collective-permute-start | bytes 786440 | tf_op jit(solution)/shard_map/ppermute | solution.py:266
  86.5 12.4 %collective-permute-start.26 = (bf16[64,2048]{1,0:T(8,128)(2,1)S(1)}, bf16[64,2048]{1,0:T(8,128)(2,1)S(1)}, u32[]{:S(2)}, u32[]{:S(2)}) collective-permute-start(bf16[64,2048]{1,0:T(8,128)(2,1)S(1)} %get-tuple-element.93), channel_id=1, source_target_pairs={{0,4},{1,5},{2,0},{3,1},{4,8},{5,9},{6,2},{7,3},{8,12},{9,13},{10,... | collective-permute-start | bytes 786440 | tf_op jit(solution)/shard_map/ppermute | solution.py:266
  87.4 12.7 %collective-permute-start.34 = (bf16[64,2048]{1,0:T(8,128)(2,1)S(1)}, bf16[64,2048]{1,0:T(8,128)(2,1)S(1)}, u32[]{:S(2)}, u32[]{:S(2)}) collective-permute-start(bf16[64,2048]{1,0:T(8,128)(2,1)S(1)} %get-tuple-element.92), channel_id=1, source_target_pairs={{0,2},{1,3},{2,6},{3,7},{4,0},{5,1},{6,10},{7,11},{8,4},{9,5},{10,... | collective-permute-start | bytes 786440 | tf_op jit(solution)/shard_map/ppermute | solution.py:266
  94.7 18.6 %collective-permute-start.25 = (bf16[64,2048]{1,0:T(8,128)(2,1)S(1)}, bf16[64,2048]{1,0:T(8,128)(2,1)S(1)}, u32[]{:S(2)}, u32[]{:S(2)}) collective-permute-start(bf16[64,2048]{1,0:T(8,128)(2,1)S(1)} %get-tuple-element.89), channel_id=1, source_target_pairs={{0,4},{1,5},{2,0},{3,1},{4,8},{5,9},{6,2},{7,3},{8,12},{9,13},{10,... | collective-permute-start | bytes 786440 | tf_op jit(solution)/shard_map/ppermute | solution.py:266
  96.8 16.5 %collective-permute-start.30 = (bf16[64,2048]{1,0:T(8,128)(2,1)S(1)}, bf16[64,2048]{1,0:T(8,128)(2,1)S(1)}, u32[]{:S(2)}, u32[]{:S(2)}) collective-permute-start(bf16[64,2048]{1,0:T(8,128)(2,1)S(1)} %get-tuple-element.88), channel_id=1, source_target_pairs={{0,2},{1,3},{2,6},{3,7},{4,0},{5,1},{6,10},{7,11},{8,4},{9,5},{10,... | collective-permute-start | bytes 786440 | tf_op jit(solution)/shard_map/ppermute | solution.py:266
  100.3 9.2 %collective-permute-start.27 = (bf16[64,2048]{1,0:T(8,128)(2,1)S(1)}, bf16[64,2048]{1,0:T(8,128)(2,1)S(1)}, u32[]{:S(2)}, u32[]{:S(2)}) collective-permute-start(bf16[64,2048]{1,0:T(8,128)(2,1)S(1)} %get-tuple-element.85), channel_id=1, source_target_pairs={{0,4},{1,5},{2,0},{3,1},{4,8},{5,9},{6,2},{7,3},{8,12},{9,13},{10,... | collective-permute-start | bytes 786440 | tf_op jit(solution)/shard_map/ppermute | solution.py:266
  101.8 9.2 %collective-permute-start.35 = (bf16[64,2048]{1,0:T(8,128)(2,1)S(1)}, bf16[64,2048]{1,0:T(8,128)(2,1)S(1)}, u32[]{:S(2)}, u32[]{:S(2)}) collective-permute-start(bf16[64,2048]{1,0:T(8,128)(2,1)S(1)} %get-tuple-element.84), channel_id=1, source_target_pairs={{0,2},{1,3},{2,6},{3,7},{4,0},{5,1},{6,10},{7,11},{8,4},{9,5},{10,... | collective-permute-start | bytes 786440 | tf_op jit(solution)/shard_map/ppermute | solution.py:266
  111.2 6.4 %collective-permute-start.29 = (bf16[64,2048]{1,0:T(8,128)(2,1)S(1)}, bf16[64,2048]{1,0:T(8,128)(2,1)S(1)}, u32[]{:S(2)}, u32[]{:S(2)}) collective-permute-start(bf16[64,2048]{1,0:T(8,128)(2,1)S(1)} %get-tuple-element.83), channel_id=1, source_target_pairs={{0,4},{1,5},{2,0},{3,1},{4,8},{5,9},{6,2},{7,3},{8,12},{9,13},{10,... | collective-permute-start | bytes 786440 | tf_op jit(solution)/shard_map/ppermute | solution.py:266
  112.2 6.4 %collective-permute-start.36 = (bf16[64,2048]{1,0:T(8,128)(2,1)S(1)}, bf16[64,2048]{1,0:T(8,128)(2,1)S(1)}, u32[]{:S(2)}, u32[]{:S(2)}) collective-permute-start(bf16[64,2048]{1,0:T(8,128)(2,1)S(1)} %get-tuple-element.82), channel_id=1, source_target_pairs={{0,2},{1,3},{2,6},{3,7},{4,0},{5,1},{6,10},{7,11},{8,4},{9,5},{10,... | collective-permute-start | bytes 786440 | tf_op jit(solution)/shard_map/ppermute | solution.py:266
  113.4 8.4 %collective-permute-start.32 = (bf16[64,2048]{1,0:T(8,128)(2,1)S(1)}, bf16[64,2048]{1,0:T(8,128)(2,1)S(1)}, u32[]{:S(2)}, u32[]{:S(2)}) collective-permute-start(bf16[64,2048]{1,0:T(8,128)(2,1)S(1)} %get-tuple-element.87), channel_id=1, source_target_pairs={{0,4},{1,5},{2,0},{3,1},{4,8},{5,9},{6,2},{7,3},{8,12},{9,13},{10,... | collective-permute-start | bytes 786440 | tf_op jit(solution)/shard_map/ppermute | solution.py:266
  114.4 7.4 %collective-permute-start.33 = (bf16[64,2048]{1,0:T(8,128)(2,1)S(1)}, bf16[64,2048]{1,0:T(8,128)(2,1)S(1)}, u32[]{:S(2)}, u32[]{:S(2)}) collective-permute-start(bf16[64,2048]{1,0:T(8,128)(2,1)S(1)} %get-tuple-element.86), channel_id=1, source_target_pairs={{0,2},{1,3},{2,6},{3,7},{4,0},{5,1},{6,10},{7,11},{8,4},{9,5},{10,... | collective-permute-start | bytes 786440 | tf_op jit(solution)/shard_map/ppermute | solution.py:266
  118.7 6.4 %collective-permute-start.31 = (bf16[64,2048]{1,0:T(8,128)(2,1)S(1)}, bf16[64,2048]{1,0:T(8,128)(2,1)S(1)}, u32[]{:S(2)}, u32[]{:S(2)}) collective-permute-start(bf16[64,2048]{1,0:T(8,128)(2,1)S(1)} %get-tuple-element.81), channel_id=1, source_target_pairs={{0,4},{1,5},{2,0},{3,1},{4,8},{5,9},{6,2},{7,3},{8,12},{9,13},{10,... | collective-permute-start | bytes 786440 | tf_op jit(solution)/shard_map/ppermute | solution.py:266
  119.6 6.4 %collective-permute-start.37 = (bf16[64,2048]{1,0:T(8,128)(2,1)S(1)}, bf16[64,2048]{1,0:T(8,128)(2,1)S(1)}, u32[]{:S(2)}, u32[]{:S(2)}) collective-permute-start(bf16[64,2048]{1,0:T(8,128)(2,1)S(1)} %get-tuple-element.80), channel_id=1, source_target_pairs={{0,2},{1,3},{2,6},{3,7},{4,0},{5,1},{6,10},{7,11},{8,4},{9,5},{10,... | collective-permute-start | bytes 786440 | tf_op jit(solution)/shard_map/ppermute | solution.py:266

commit v12 on v11

--- a/solution.py
+++ b/solution.py
@@ -284,8 +284,9 @@
     gates = jnp.sum(
         jnp.where(route_ids[:, :, None] == jnp.arange(experts), route_weights[:, :, None], 0.0), axis=1
     )
-    normed_top, normed_bottom, other = lax.optimization_barrier((*normed, to_x(gates)))
-    gates = jnp.where(x == 0, jnp.stack([gates, other]), jnp.stack([other, gates]))[:, None]
+    gates = jnp.pad(gates, ((0, 0), (0, -experts % 128)))
+    gates = lax.all_gather(gates, axes, axis=0, tiled=False)
+    normed_top, normed_bottom = normed
 
     halves = range(2)
     size = frames // 2
@@ -303,26 +304,7 @@
     def project(rows):
         return jnp.dot(rows, columns, preferred_element_type=jnp.float32).astype(jnp.bfloat16)
 
-    def merge(gates, other, low):
-        return jnp.where(
-            low, jnp.concatenate([gates, other], axis=1), jnp.concatenate([other, gates], axis=1)
-        )
-
     own = [project(normed_top), project(normed_bottom)]
-    gates, own[0] = lax.optimization_barrier((gates, own[0]))
-    step = 1
-    while step < wide:
-        other = send(gates, lambda z, x, c: (z ^ step, x, c))
-        gates, step = merge(gates, other, z & step == 0), 2 * step
-    sent[1], gates = lax.optimization_barrier((sent[1], gates))
-    mine = (z * 2 + x) * 2 + core
-    pair = jnp.stack([mine, mine + 1 - 2 * core])
-    gates = jnp.sum(
-        jnp.where(pair[:, None] == jnp.arange(experts), gates[..., None, :], 0.0), axis=-1
-    )
-    gates = jnp.concatenate([gates[0], gates[1, ::-1]])
-    gates = lax.dynamic_slice_in_dim(jnp.concatenate([gates, gates]), place, ring, 0)
-
     rows = []
     for h in halves:
         back = to_x(project(sent[h]))
@@ -342,6 +324,17 @@
         fore_at[k] = [along(fore_at[k - 1][h], 1) for h in halves]
         back_at[k] = [along(back_at[k - 1][h], -1) for h in halves]
     last = [along(fore_at[far - 1][0], 1), along(back_at[far - 1][1], -1)]
+
+    back_at[far - 1][0], gates = lax.optimization_barrier((back_at[far - 1][0], gates))
+
+    mine = (z * 2 + x) * 2 + core
+    lanes = jnp.arange(gates.shape[-1])
+    gates = lax.dynamic_slice_in_dim(gates.reshape(wide, 2, 2, frames, -1), core, 1, 2)[:, :, 0]
+    gates = jnp.stack(
+        [jnp.sum(jnp.where(lanes == e, gates, 0.0), axis=-1) for e in (mine, mine + 1 - 2 * core)], axis=-1
+    )
+    gates = jnp.concatenate([gates[:, 0], gates[::-1, 1]])
+    gates = lax.dynamic_slice_in_dim(jnp.concatenate([gates, gates]), place, ring, 0)
 
     joined_in = jnp.concatenate(
         [

time: 128 us -> 176 us (1.38)
  waiting for transfers between devices: 51 us -> 72.2 us
  between operations: 1.01 us -> 14.5 us
  local copies, waits for them, and re-layouts: 0.75 us -> 10.6 us
  matrix products: 16.6 us -> 19.9 us
  starting transfers between devices: 42 us -> 40.1 us
    all_gather x0 -> x1, waiting for transfers between devices: none -> 31.2 us  [dense_experts(): gates = lax.all_gather(gates, axes, axis=0, tiled=False)]
    ppermute x38 -> x35, waiting for transfers between devices: 51 us -> 40.9 us  [send(): return lax.ppermute(value, axes, routes(wide, move))]
    unnamed x8 -> x30, local copies, waits for them, and re-layouts: 0.02 us -> 4.23 us
    dot_general x5, matrix products: 7.31 us -> 10.4 us  [run_experts(): jnp.dot(jnp.concatenate(parts), joined_in, preferred_element_type=jnp.flo...]
    concatenate x1, other arithmetic: 1.92 us -> 3.97 us  [dense_experts(): joined_down = jnp.concatenate([expert_out, down_other], axis=0)]
    ppermute x38 -> x35, starting transfers between devices: 42 us -> 40 us  [send(): return lax.ppermute(value, axes, routes(wide, move))]
    slice x1, local copies, waits for them, and re-layouts: 0.32 us -> 2.2 us  [dense_experts(): in_other[:, :hidden_width]]
    slice x1, local copies, waits for them, and re-layouts: 0.32 us -> 2.2 us  [dense_experts(): expert_in[:, :hidden_width]]
  transfers between devices with their start and end apart: 38 -> 36, of which waited for: 18 -> 19; matrix products, arithmetic and copies ran while one was open for 17% -> 20% of each run, Pallas kernels for 5% -> 4%
where the time goes in v12:
time: 176 us; the launch traced here: 175 us
  waiting for transfers between devices  72.2 us (41%)
  starting transfers between devices  40.1 us (23%)
  matrix products  19.9 us (11%)
  between operations  14.5 us (8%)
  other arithmetic  11.1 us (6%)
  local copies, waits for them, and re-layouts  10.6 us (6%)
  Pallas kernels  6.86 us (4%)
    ppermute x35, waiting for transfers between devices, send(): return lax.ppermute(value, axes, routes(wide, move))  40.9 us
    ppermute x35, starting transfers between devices, send(): return lax.ppermute(value, axes, routes(wide, move))  40 us
    all_gather x1, waiting for transfers between devices, dense_experts(): gates = lax.all_gather(gates, axes, axis=0, tiled=False)  31.2 us
    dot_general x5, matrix products, run_experts(): jnp.dot(jnp.concatenate(parts), joined_in, preferred_element_type=jnp.flo...  10.4 us
    pallas_call x1, Pallas kernels, ssm_mixer(): pl.pallas_call(mixer_kernel, grid=(steps,), in_specs=[pl.BlockSpec(memory...  6.86 us
    dot_general x5, matrix products, run_experts(): return jnp.dot(hidden, joined_down, preferred_element_type=jnp.float32)  6.05 us
    unnamed x30, local copies, waits for them, and re-layouts  4.23 us
    concatenate x1, other arithmetic, dense_experts(): joined_down = jnp.concatenate([expert_out, down_other], axis=0)  3.97 us
  transfers between devices with their start and end apart: 36, of which 19 were waited for; matrix products, arithmetic and copies ran while one was open for 20% of the time, Pallas kernels for 4%

profile of v12, /device:TPU:0, one launch (start us, length us, event | category | flops | bytes accessed | tf_op | source)
XLA Modules:
  0.0 175.2 jit_solution(6353151895885745620)
XLA Ops:
  9.2 6.9 %mixer.1 = (bf16[64,2048]{1,0:T(8,128)(2,1)}, bf16[64,2048]{1,0:T(8,128)(2,1)}, f32[2048,128]{1,0:T(8,128)}) custom-call(f32[32]{0:T(128)} %skip_ref.1, bf16[128,2048]{1,0:T(8,128)(2,1)} %x_ref.1, bf16[128,2048]{1,0:T(8,128)(2,1)} %z_ref.1, bf16[128,128]{1,0:T(8,128)(2,1)} %b_ref.1, bf16[128,128]{1,0:T(8,128)(2,1)} %c_ref.1, f32[32,128]{1,0:T(8,128)} %bitcast.93, ...), custom_call_target="tpu_custom_call" | custom-call | flops 400000000 | bytes 6000000 | tf_op jit(solution)/shard_map/mixer/pallas_call | solution.py:149
  16.0 2.6 %collective-permute-start.1 = (bf16[64,2048]{1,0:T(8,128)(2,1)}, bf16[64,2048]{1,0:T(8,128)(2,1)S(1)}, u32[]{:S(2)}, u32[]{:S(2)}) collective-permute-start(bf16[64,2048]{1,0:T(8,128)(2,1)} %get-tuple-element.34), channel_id=1, source_target_pairs={{0,2},{1,3},{2,0},{3,1},{4,6},{5,7},{6,4},{7,5},{8,10},{9,11},{10,... | collective-permute-start | bytes 786440 | tf_op jit(solution)/shard_map/ppermute | solution.py:266
  19.1 31.2 %all-gather.3.cloned.1.call-done = f32[2048,128]{0,1:T(8,128)} async-done(((f32[128,128]{0,1:T(8,128)}), f32[2048,128]{0,1:T(8,128)}) %all-gather.3.cloned.1.call-update) | async-done | bytes 1048592 | tf_op jit(solution)/shard_map/all_gather | solution.py:288
  50.4 1.4 copy.29
  51.8 3.5 %maximum_select_fusion = bf16[2048,1024]{1,0:T(8,128)(2,1)S(1)} fusion(bf16[2048,512]{1,0:T(8,128)(2,1)} %collective-permute-done, bf16[2048,512]{1,0:T(8,128)(2,1)S(1)} %copy-done.1, pred[]{:T(512)S(6)} %eq.36), kind=kLoop, calls=%fused_computation.1 | loop fusion | flops 18874368 | bytes 8388609 | tf_op jit(solution)/shard_map/jit(_where)/select_n | solution.py:295
  56.2 1.4 collective-permute-start.2
  59.2 3.4 %collective-permute-done.2 = bf16[64,1024]{1,0:T(8,128)(2,1)S(1)} collective-permute-done((bf16[64,1024]{1,0:T(8,128)(2,1)S(1)}, bf16[64,1024]{1,0:T(8,128)(2,1)S(1)}, u32[]{:S(2)}, u32[]{:S(2)}) %collective-permute-start.2) | collective-permute-done | bytes 131104 | tf_op jit(solution)/shard_map/ppermute | solution.py:266
  62.7 1.4 collective-permute-start.5
  64.1 3.5 %collective-permute-done.3 = bf16[64,2048]{1,0:T(8,128)(2,1)S(1)} collective-permute-done((bf16[64,2048]{1,0:T(8,128)(2,1)S(1)}, bf16[64,2048]{1,0:T(8,128)(2,1)S(1)}, u32[]{:S(2)}, u32[]{:S(2)}) %collective-permute-start.3) | collective-permute-done | bytes 262176 | tf_op jit(solution)/shard_map/ppermute | solution.py:266
  68.4 2.1 %collective-permute-start.4 = (bf16[64,1024]{1,0:T(8,128)(2,1)S(1)}, bf16[64,1024]{1,0:T(8,128)(2,1)S(1)}, u32[]{:S(2)}, u32[]{:S(2)}) collective-permute-start(bf16[64,1024]{1,0:T(8,128)(2,1)S(1)} %convolution_convert_fusion.1), channel_id=1, source_target_pairs={{0,2},{1,3},{2,0},{3,1},{4,6},{5,7},{6,4},{7,5},{8,10},{9,11},{10,... | collective-permute-start | bytes 393224 | tf_op jit(solution)/shard_map/ppermute | solution.py:266
  72.4 2.5 %collective-permute-done.4 = bf16[64,1024]{1,0:T(8,128)(2,1)S(1)} collective-permute-done((bf16[64,1024]{1,0:T(8,128)(2,1)S(1)}, bf16[64,1024]{1,0:T(8,128)(2,1)S(1)}, u32[]{:S(2)}, u32[]{:S(2)}) %collective-permute-start.4) | collective-permute-done | bytes 131104 | tf_op jit(solution)/shard_map/ppermute | solution.py:266
  75.0 2.5 %collective-permute-start.6 = (bf16[64,2048]{1,0:T(8,128)(2,1)S(1)}, bf16[64,2048]{1,0:T(8,128)(2,1)S(1)}, u32[]{:S(2)}, u32[]{:S(2)}) collective-permute-start(bf16[64,2048]{1,0:T(8,128)(2,1)S(1)} %collective-permute-done.5), channel_id=1, source_target_pairs={{0,2},{1,3},{2,6},{3,7},{4,0},{5,1},{6,10},{7,11},{8,4},{9,5},{10,... | collective-permute-start | bytes 786440 | tf_op jit(solution)/shard_map/ppermute | solution.py:266
  77.5 2.2 %fusion.102 = (bf16[2048,384]{1,0:T(8,128)(2,1)S(1)}, bf16[2048,384]{1,0:T(8,128)(2,1)S(1)}) fusion(bf16[2048,768]{1,0:T(8,128)(2,1)} %bitcast.5), kind=kLoop, calls=%fused_computation.149 | loop fusion | bytes 6291456 | tf_op jit(solution)/shard_map/slice | solution.py:341
  79.9 1.9 %collective-permute-start.18 = (bf16[64,2048]{1,0:T(8,128)(2,1)S(1)}, bf16[64,2048]{1,0:T(8,128)(2,1)}, u32[]{:S(2)}, u32[]{:S(2)}) collective-permute-start(bf16[64,2048]{1,0:T(8,128)(2,1)S(1)} %maximum_select_fusion.2), channel_id=1, source_target_pairs={{0,4},{1,5},{2,0},{3,1},{4,8},{5,9},{6,2},{7,3},{8,12},{9,13},{10,... | collective-permute-start | bytes 786440 | tf_op jit(solution)/shard_map/ppermute | solution.py:266
  81.9 2.4 %collective-permute-done.6 = bf16[64,2048]{1,0:T(8,128)(2,1)S(1)} collective-permute-done((bf16[64,2048]{1,0:T(8,128)(2,1)S(1)}, bf16[64,2048]{1,0:T(8,128)(2,1)S(1)}, u32[]{:S(2)}, u32[]{:S(2)}) %collective-permute-start.6) | collective-permute-done | bytes 262176 | tf_op jit(solution)/shard_map/ppermute | solution.py:266
  84.3 2.5 %collective-permute-start.7 = (bf16[64,2048]{1,0:T(8,128)(2,1)S(1)}, bf16[64,2048]{1,0:T(8,128)(2,1)S(1)}, u32[]{:S(2)}, u32[]{:S(2)}) collective-permute-start(bf16[64,2048]{1,0:T(8,128)(2,1)S(1)} %collective-permute-done.6), channel_id=1, source_target_pairs={{0,2},{1,3},{2,6},{3,7},{4,0},{5,1},{6,10},{7,11},{8,4},{9,5},{10,... | collective-permute-start | bytes 786440 | tf_op jit(solution)/shard_map/ppermute | solution.py:266
  86.8 4.0 %pad_maximum_fusion.1 = bf16[768,2048]{1,0:T(8,128)(2,1)} fusion(bf16[384,2048]{1,0:T(8,128)(2,1)} %collective-permute-done.17, bf16[384,2048]{1,0:T(8,128)(2,1)} %bitcast.6), kind=kLoop, calls=%fused_computation.2 | loop fusion | flops 6291456 | bytes 6291456 | tf_op jit(solution)/shard_map/concatenate | solution.py:348
  90.8 2.2 %collective-permute-done.9 = bf16[64,2048]{1,0:T(8,128)(2,1)} collective-permute-done((bf16[64,2048]{1,0:T(8,128)(2,1)S(1)}, bf16[64,2048]{1,0:T(8,128)(2,1)}, u32[]{:S(2)}, u32[]{:S(2)}) %collective-permute-start.9) | collective-permute-done | bytes 262176 | tf_op jit(solution)/shard_map/ppermute | solution.py:266
  93.0 1.6 collective-permute-start.10
  95.0 1.6 collective-permute-start.19
  97.4 1.2 constant_dynamic-slice_fusion
  98.6 1.9 %copy.24 = f32[4,2,1,128,128]{4,3,1,0,2:T(8,128)} copy(f32[4,2,1,128,128]{3,2,1,0,4:T(1,128)} %constant_dynamic-slice_fusion) | data formatting | bytes 1048576
  100.5 1.4 fusion.49
  102.6 1.6 collective-permute-start.11
  104.6 3.6 %collective-permute-done.19 = bf16[64,2048]{1,0:T(8,128)(2,1)} collective-permute-done((bf16[64,2048]{1,0:T(8,128)(2,1)}, bf16[64,2048]{1,0:T(8,128)(2,1)}, u32[]{:S(2)}, u32[]{:S(2)}) %collective-permute-start.19) | collective-permute-done | bytes 262176 | tf_op jit(solution)/shard_map/ppermute | solution.py:266
  108.2 1.6 collective-permute-start.20
  109.9 2.2 %fusion.103 = (bf16[2048,384]{1,0:T(8,128)(2,1)S(1)}, bf16[2048,384]{1,0:T(8,128)(2,1)S(1)}) fusion(bf16[2048,768]{1,0:T(8,128)(2,1)} %collective-permute-done.16), kind=kLoop, calls=%fused_computation.150 | loop fusion | bytes 6291456 | tf_op jit(solution)/shard_map/slice | solution.py:342
  113.7 5.6 %collective-permute-done.15 = bf16[64,2048]{1,0:T(8,128)(2,1)S(1)} collective-permute-done((bf16[64,2048]{1,0:T(8,128)(2,1)S(1)}, bf16[64,2048]{1,0:T(8,128)(2,1)S(1)}, u32[]{:S(2)}, u32[]{:S(2)}) %collective-permute-start.15) | collective-permute-done | bytes 262176 | tf_op jit(solution)/shard_map/ppermute | solution.py:266
  121.3 2.7 %fusion = f32[256,1536]{1,0:T(8,128)S(1)} fusion(bf16[2048,1536]{1,0:T(8,128)(2,1)S(1)} %pad_maximum_fusion, bf16[64,2048]{1,0:T(8,128)(2,1)S(1)} %collective-permute-done.20, bf16[64,2048]{1,0:T(8,128)(2,1)} %collective-permute-done.10, bf16[64,2048]{1,0:T(8,128)(2,1)S(1)} %collective-permute-done.14, bf16[64,2048]{1,0:T(8,128)(2,1)S(1)} %copy-done.13), kind=kOutput, calls=%fused_computation.8 | convolution fusion | flops 1614807040 | bytes 8912896 | tf_op jit(solution)/shard_map/dot_general | solution.py:353
  124.0 1.2 fusion.107
  125.3 2.0 %collective-permute-start.25 = (bf16[64,2048]{1,0:T(8,128)(2,1)S(1)}, bf16[64,2048]{1,0:T(8,128)(2,1)S(1)}, u32[]{:S(2)}, u32[]{:S(2)}) collective-permute-start(bf16[64,2048]{1,0:T(8,128)(2,1)S(1)} %get-tuple-element.82), channel_id=1, source_target_pairs={{0,2},{1,3},{2,6},{3,7},{4,0},{5,1},{6,10},{7,11},{8,4},{9,5},{10,... | collective-permute-start | bytes 786440 | tf_op jit(solution)/shard_map/ppermute | solution.py:266
  127.4 2.0 %collective-permute-start.31 = (bf16[64,2048]{1,0:T(8,128)(2,1)S(1)}, bf16[64,2048]{1,0:T(8,128)(2,1)S(1)}, u32[]{:S(2)}, u32[]{:S(2)}) collective-permute-start(bf16[64,2048]{1,0:T(8,128)(2,1)S(1)} %get-tuple-element.84), channel_id=1, source_target_pairs={{0,2},{1,3},{2,6},{3,7},{4,0},{5,1},{6,10},{7,11},{8,4},{9,5},{10,... | collective-permute-start | bytes 786440 | tf_op jit(solution)/shard_map/ppermute | solution.py:266
  129.4 2.9 %fusion.8 = f32[256,1536]{1,0:T(8,128)S(1)} fusion(bf16[2048,1536]{1,0:T(8,128)(2,1)S(1)} %pad_maximum_fusion, bf16[64,2048]{1,0:T(8,128)(2,1)} %collective-permute-done.19, bf16[64,2048]{1,0:T(8,128)(2,1)} %collective-permute-done.9, bf16[64,2048]{1,0:T(8,128)(2,1)} %collective-permute-done.13, bf16[64,2048]{1,0:T(8,128)(2,1)S(1)} %copy-done.11), kind=kOutput, calls=%fused_computation.16 | convolution fusion | flops 1614807040 | bytes 8912896 | tf_op jit(solution)/shard_map/dot_general | solution.py:353
  132.3 1.2 fusion.52
  134.1 2.3 %collective-permute-start.27 = (bf16[64,2048]{1,0:T(8,128)(2,1)S(1)}, bf16[64,2048]{1,0:T(8,128)(2,1)S(1)}, u32[]{:S(2)}, u32[]{:S(2)}) collective-permute-start(bf16[64,2048]{1,0:T(8,128)(2,1)S(1)} %get-tuple-element.80), channel_id=1, source_target_pairs={{0,2},{1,3},{2,6},{3,7},{4,0},{5,1},{6,10},{7,11},{8,4},{9,5},{10,... | collective-permute-start | bytes 786440 | tf_op jit(solution)/shard_map/ppermute | solution.py:266
  136.5 3.0 %collective-permute-done.23 = bf16[64,2048]{1,0:T(8,128)(2,1)S(1)} collective-permute-done((bf16[64,2048]{1,0:T(8,128)(2,1)S(1)}, bf16[64,2048]{1,0:T(8,128)(2,1)S(1)}, u32[]{:S(2)}, u32[]{:S(2)}) %collective-permute-start.23) | collective-permute-done | bytes 262176 | tf_op jit(solution)/shard_map/ppermute | solution.py:266
  139.7 2.3 %collective-permute-start.32 = (bf16[64,2048]{1,0:T(8,128)(2,1)S(1)}, bf16[64,2048]{1,0:T(8,128)(2,1)S(1)}, u32[]{:S(2)}, u32[]{:S(2)}) collective-permute-start(bf16[64,2048]{1,0:T(8,128)(2,1)S(1)} %get-tuple-element.76), channel_id=1, source_target_pairs={{0,2},{1,3},{2,6},{3,7},{4,0},{5,1},{6,10},{7,11},{8,4},{9,5},{10,... | collective-permute-start | bytes 786440 | tf_op jit(solution)/shard_map/ppermute | solution.py:266
  142.1 2.8 %fusion.16 = f32[256,1536]{1,0:T(8,128)S(1)} fusion(bf16[2048,1536]{1,0:T(8,128)(2,1)S(1)} %pad_maximum_fusion, bf16[64,2048]{1,0:T(8,128)(2,1)} %collective-permute-done.18, bf16[64,2048]{1,0:T(8,128)(2,1)S(1)} %copy-done.9, bf16[64,2048]{1,0:T(8,128)(2,1)} %collective-permute-done.12, bf16[64,2048]{1,0:T(8,128)(2,1)S(1)} %copy-done.7), kind=kOutput, calls=%fused_computation.24 | convolution fusion | flops 1614807040 | bytes 8912896 | tf_op jit(solution)/shard_map/dot_general | solution.py:353
  144.9 1.2 fusion.54
  146.1 3.0 %collective-permute-done.24 = bf16[64,2048]{1,0:T(8,128)(2,1)S(1)} collective-permute-done((bf16[64,2048]{1,0:T(8,128)(2,1)S(1)}, bf16[64,2048]{1,0:T(8,128)(2,1)S(1)}, u32[]{:S(2)}, u32[]{:S(2)}) %collective-permute-start.24) | collective-permute-done | bytes 262176 | tf_op jit(solution)/shard_map/ppermute | solution.py:266
  149.2 2.0 %collective-permute-start.26 = (bf16[64,2048]{1,0:T(8,128)(2,1)S(1)}, bf16[64,2048]{1,0:T(8,128)(2,1)S(1)}, u32[]{:S(2)}, u32[]{:S(2)}) collective-permute-start(bf16[64,2048]{1,0:T(8,128)(2,1)S(1)} %get-tuple-element.75), channel_id=1, source_target_pairs={{0,4},{1,5},{2,0},{3,1},{4,8},{5,9},{6,2},{7,3},{8,12},{9,13},{10,... | collective-permute-start | bytes 786440 | tf_op jit(solution)/shard_map/ppermute | solution.py:266
  151.6 1.7 collective-permute-start.29
  153.7 3.9 %collective-permute-done.26 = bf16[64,2048]{1,0:T(8,128)(2,1)S(1)} collective-permute-done((bf16[64,2048]{1,0:T(8,128)(2,1)S(1)}, bf16[64,2048]{1,0:T(8,128)(2,1)S(1)}, u32[]{:S(2)}, u32[]{:S(2)}) %collective-permute-start.26) | collective-permute-done | bytes 262176 | tf_op jit(solution)/shard_map/ppermute | solution.py:266
  158.7 1.5 collective-permute-start.28
  160.8 1.0 fusion.44
  161.8 3.3 %collective-permute-done.28 = bf16[64,2048]{1,0:T(8,128)(2,1)S(1)} collective-permute-done((bf16[64,2048]{1,0:T(8,128)(2,1)S(1)}, bf16[64,2048]{1,0:T(8,128)(2,1)S(1)}, u32[]{:S(2)}, u32[]{:S(2)}) %collective-permute-start.28) | collective-permute-done | bytes 262176 | tf_op jit(solution)/shard_map/ppermute | solution.py:266
  165.1 1.5 collective-permute-done.34
  166.6 1.8 %add_convert_fusion = bf16[128,2048]{1,0:T(8,128)(2,1)} fusion(bf16[64,2048]{1,0:T(8,128)(2,1)S(1)} %copy-done.3, bf16[64,2048]{1,0:T(8,128)(2,1)S(1)} %maximum_select_fusion.1, bf16[64,2048]{1,0:T(8,128)(2,1)S(1)} %collective-permute-done.29, bf16[64,2048]{1,0:T(8,128)(2,1)S(1)} %collective-permute-done.28, ...), kind=kOutput, calls=%fused_computation.32 | convolution fusion | flops 407633920 | bytes 6031104 | tf_op jit(solution)/shard_map/dot_general | solution.py:356
  (99 shorter events, 17.2 us)
Async XLA Ops:
  7.2 44.6 %copy-start.1 = (bf16[2048,512]{1,0:T(8,128)(2,1)S(1)}, bf16[2048,512]{1,0:T(8,128)(2,1)}, u32[]{:S(2)}) copy-start(bf16[2048,512]{1,0:T(8,128)(2,1)} %param.25) | copy-start | bytes 6291460
  7.2 43.2 %all-gather.3.cloned.1.call-start = ((), (), s32[]{:S(2)}) async-start(), calls=%async_computation | async-start | bytes 1114112 | tf_op jit(solution)/shard_map/all_gather | solution.py:288
  7.2 44.6 %collective-permute-start = (bf16[2048,512]{1,0:T(8,128)(2,1)}, bf16[2048,512]{1,0:T(8,128)(2,1)}, u32[]{:S(2)}, u32[]{:S(2)}) collective-permute-start(bf16[2048,512]{1,0:T(8,128)(2,1)} %param.25), channel_id=1, source_target_pairs={{0,1},{1,0},{2,3},{3,2},{4,5},{5,4},{6,7},{7,6},{8,9},{9,8},{10,11... | collective-permute-start | bytes 6291464 | tf_op jit(solution)/shard_map/ppermute | solution.py:266
  16.0 39.3 %collective-permute-start.1 = (bf16[64,2048]{1,0:T(8,128)(2,1)}, bf16[64,2048]{1,0:T(8,128)(2,1)S(1)}, u32[]{:S(2)}, u32[]{:S(2)}) collective-permute-start(bf16[64,2048]{1,0:T(8,128)(2,1)} %get-tuple-element.34), channel_id=1, source_target_pairs={{0,2},{1,3},{2,0},{3,1},{4,6},{5,7},{6,4},{7,5},{8,10},{9,11},{10,... | collective-permute-start | bytes 786440 | tf_op jit(solution)/shard_map/ppermute | solution.py:266
  18.6 91.3 %collective-permute-start.16 = (bf16[2048,768]{1,0:T(8,128)(2,1)}, bf16[2048,768]{1,0:T(8,128)(2,1)}, u32[]{:S(2)}, u32[]{:S(2)}) collective-permute-start(bf16[2048,768]{1,0:T(8,128)(2,1)} %bitcast.5), channel_id=1, source_target_pairs={{0,1},{1,0},{2,3},{3,2},{4,5},{5,4},{6,7},{7,6},{8,9},{9,8},{10,11... | collective-permute-start | bytes 9437192 | tf_op jit(solution)/shard_map/ppermute | solution.py:266
  18.7 61.2 %collective-permute-start.17 = (bf16[384,2048]{1,0:T(8,128)(2,1)}, bf16[384,2048]{1,0:T(8,128)(2,1)}, u32[]{:S(2)}, u32[]{:S(2)}) collective-permute-start(bf16[384,2048]{1,0:T(8,128)(2,1)} %bitcast.6), channel_id=1, source_target_pairs={{0,1},{1,0},{2,3},{3,2},{4,5},{5,4},{6,7},{7,6},{8,9},{9,8},{10,11... | collective-permute-start | bytes 4718600 | tf_op jit(solution)/shard_map/ppermute | solution.py:266
  55.3 2.3 %copy-start.4 = (bf16[64,2048]{1,0:T(8,128)(2,1)S(1)}, bf16[64,2048]{1,0:T(8,128)(2,1)}, u32[]{:S(2)}) copy-start(bf16[64,2048]{1,0:T(8,128)(2,1)} %get-tuple-element.37) | copy-start | bytes 786436
  55.4 3.0 %copy-start.5 = (bf16[64,2048]{1,0:T(8,128)(2,1)S(1)}, bf16[64,2048]{1,0:T(8,128)(2,1)}, u32[]{:S(2)}) copy-start(bf16[64,2048]{1,0:T(8,128)(2,1)} %get-tuple-element.34) | copy-start | bytes 786436
  56.2 6.4 %collective-permute-start.2 = (bf16[64,1024]{1,0:T(8,128)(2,1)S(1)}, bf16[64,1024]{1,0:T(8,128)(2,1)S(1)}, u32[]{:S(2)}, u32[]{:S(2)}) collective-permute-start(bf16[64,1024]{1,0:T(8,128)(2,1)S(1)} %convolution_convert_fusion.3), channel_id=1, source_target_pairs={{0,2},{1,3},{2,0},{3,1},{4,6},{5,7},{6,4},{7,5},{8,10},{9,11},{10,... | collective-permute-start | bytes 393224 | tf_op jit(solution)/shard_map/ppermute | solution.py:266
  57.7 9.9 %collective-permute-start.3 = (bf16[64,2048]{1,0:T(8,128)(2,1)S(1)}, bf16[64,2048]{1,0:T(8,128)(2,1)S(1)}, u32[]{:S(2)}, u32[]{:S(2)}) collective-permute-start(bf16[64,2048]{1,0:T(8,128)(2,1)S(1)} %copy-done.4), channel_id=1, source_target_pairs={{0,2},{1,3},{2,0},{3,1},{4,6},{5,7},{6,4},{7,5},{8,10},{9,11},{10,... | collective-permute-start | bytes 786440 | tf_op jit(solution)/shard_map/ppermute | solution.py:266
  62.7 12.3 %collective-permute-start.5 = (bf16[64,2048]{1,0:T(8,128)(2,1)S(1)}, bf16[64,2048]{1,0:T(8,128)(2,1)S(1)}, u32[]{:S(2)}, u32[]{:S(2)}) collective-permute-start(bf16[64,2048]{1,0:T(8,128)(2,1)S(1)} %maximum_select_fusion.1), channel_id=1, source_target_pairs={{0,2},{1,3},{2,6},{3,7},{4,0},{5,1},{6,10},{7,11},{8,4},{9,5},{10,... | collective-permute-start | bytes 786440 | tf_op jit(solution)/shard_map/ppermute | solution.py:266
  68.4 6.4 %collective-permute-start.4 = (bf16[64,1024]{1,0:T(8,128)(2,1)S(1)}, bf16[64,1024]{1,0:T(8,128)(2,1)S(1)}, u32[]{:S(2)}, u32[]{:S(2)}) collective-permute-start(bf16[64,1024]{1,0:T(8,128)(2,1)S(1)} %convolution_convert_fusion.1), channel_id=1, source_target_pairs={{0,2},{1,3},{2,0},{3,1},{4,6},{5,7},{6,4},{7,5},{8,10},{9,11},{10,... | collective-permute-start | bytes 393224 | tf_op jit(solution)/shard_map/ppermute | solution.py:266
  71.4 10.4 %collective-permute-start.8 = (bf16[64,2048]{1,0:T(8,128)(2,1)S(1)}, bf16[64,2048]{1,0:T(8,128)(2,1)S(1)}, u32[]{:S(2)}, u32[]{:S(2)}) collective-permute-start(bf16[64,2048]{1,0:T(8,128)(2,1)S(1)} %maximum_select_fusion.1), channel_id=1, source_target_pairs={{0,4},{1,5},{2,0},{3,1},{4,8},{5,9},{6,2},{7,3},{8,12},{9,13},{10,... | collective-permute-start | bytes 786440 | tf_op jit(solution)/shard_map/ppermute | solution.py:266
  75.0 15.8 %copy-start.2 = (bf16[64,2048]{1,0:T(8,128)(2,1)}, bf16[64,2048]{1,0:T(8,128)(2,1)S(1)}, u32[]{:S(2)}) copy-start(bf16[64,2048]{1,0:T(8,128)(2,1)S(1)} %maximum_select_fusion.2) | copy-start | bytes 786436
  75.0 6.8 %copy-start.6 = (bf16[64,2048]{1,0:T(8,128)(2,1)}, bf16[64,2048]{1,0:T(8,128)(2,1)S(1)}, u32[]{:S(2)}) copy-start(bf16[64,2048]{1,0:T(8,128)(2,1)S(1)} %collective-permute-done.5) | copy-start | bytes 786436
  75.0 9.3 %collective-permute-start.6 = (bf16[64,2048]{1,0:T(8,128)(2,1)S(1)}, bf16[64,2048]{1,0:T(8,128)(2,1)S(1)}, u32[]{:S(2)}, u32[]{:S(2)}) collective-permute-start(bf16[64,2048]{1,0:T(8,128)(2,1)S(1)} %collective-permute-done.5), channel_id=1, source_target_pairs={{0,2},{1,3},{2,6},{3,7},{4,0},{5,1},{6,10},{7,11},{8,4},{9,5},{10,... | collective-permute-start | bytes 786440 | tf_op jit(solution)/shard_map/ppermute | solution.py:266
  79.7 14.9 %collective-permute-start.12 = (bf16[64,2048]{1,0:T(8,128)(2,1)S(1)}, bf16[64,2048]{1,0:T(8,128)(2,1)}, u32[]{:S(2)}, u32[]{:S(2)}) collective-permute-start(bf16[64,2048]{1,0:T(8,128)(2,1)S(1)} %maximum_select_fusion.2), channel_id=1, source_target_pairs={{0,2},{1,3},{2,6},{3,7},{4,0},{5,1},{6,10},{7,11},{8,4},{9,5},{10,... | collective-permute-start | bytes 786440 | tf_op jit(solution)/shard_map/ppermute | solution.py:266
  79.9 15.1 %collective-permute-start.18 = (bf16[64,2048]{1,0:T(8,128)(2,1)S(1)}, bf16[64,2048]{1,0:T(8,128)(2,1)}, u32[]{:S(2)}, u32[]{:S(2)}) collective-permute-start(bf16[64,2048]{1,0:T(8,128)(2,1)S(1)} %maximum_select_fusion.2), channel_id=1, source_target_pairs={{0,4},{1,5},{2,0},{3,1},{4,8},{5,9},{6,2},{7,3},{8,12},{9,13},{10,... | collective-permute-start | bytes 786440 | tf_op jit(solution)/shard_map/ppermute | solution.py:266
  81.8 8.9 %copy-start.8 = (bf16[64,2048]{1,0:T(8,128)(2,1)}, bf16[64,2048]{1,0:T(8,128)(2,1)S(1)}, u32[]{:S(2)}) copy-start(bf16[64,2048]{1,0:T(8,128)(2,1)S(1)} %collective-permute-done.8) | copy-start | bytes 786436
  81.8 11.2 %collective-permute-start.9 = (bf16[64,2048]{1,0:T(8,128)(2,1)S(1)}, bf16[64,2048]{1,0:T(8,128)(2,1)}, u32[]{:S(2)}, u32[]{:S(2)}) collective-permute-start(bf16[64,2048]{1,0:T(8,128)(2,1)S(1)} %collective-permute-done.8), channel_id=1, source_target_pairs={{0,4},{1,5},{2,0},{3,1},{4,8},{5,9},{6,2},{7,3},{8,12},{9,13},{10,... | collective-permute-start | bytes 786440 | tf_op jit(solution)/shard_map/ppermute | solution.py:266
  84.3 6.5 %copy-start.10 = (bf16[64,2048]{1,0:T(8,128)(2,1)}, bf16[64,2048]{1,0:T(8,128)(2,1)S(1)}, u32[]{:S(2)}) copy-start(bf16[64,2048]{1,0:T(8,128)(2,1)S(1)} %collective-permute-done.6) | copy-start | bytes 786436
  84.3 12.4 %collective-permute-start.7 = (bf16[64,2048]{1,0:T(8,128)(2,1)S(1)}, bf16[64,2048]{1,0:T(8,128)(2,1)S(1)}, u32[]{:S(2)}, u32[]{:S(2)}) collective-permute-start(bf16[64,2048]{1,0:T(8,128)(2,1)S(1)} %collective-permute-done.6), channel_id=1, source_target_pairs={{0,2},{1,3},{2,6},{3,7},{4,0},{5,1},{6,10},{7,11},{8,4},{9,5},{10,... | collective-permute-start | bytes 786440 | tf_op jit(solution)/shard_map/ppermute | solution.py:266
  93.0 9.6 %collective-permute-start.10 = (bf16[64,2048]{1,0:T(8,128)(2,1)}, bf16[64,2048]{1,0:T(8,128)(2,1)}, u32[]{:S(2)}, u32[]{:S(2)}) collective-permute-start(bf16[64,2048]{1,0:T(8,128)(2,1)} %collective-permute-done.9), channel_id=1, source_target_pairs={{0,4},{1,5},{2,0},{3,1},{4,8},{5,9},{6,2},{7,3},{8,12},{9,13},{10,... | collective-permute-start | bytes 786440 | tf_op jit(solution)/shard_map/ppermute | solution.py:266
  94.6 9.6 %collective-permute-start.13 = (bf16[64,2048]{1,0:T(8,128)(2,1)}, bf16[64,2048]{1,0:T(8,128)(2,1)}, u32[]{:S(2)}, u32[]{:S(2)}) collective-permute-start(bf16[64,2048]{1,0:T(8,128)(2,1)} %collective-permute-done.12), channel_id=1, source_target_pairs={{0,2},{1,3},{2,6},{3,7},{4,0},{5,1},{6,10},{7,11},{8,4},{9,5},{10,... | collective-permute-start | bytes 786440 | tf_op jit(solution)/shard_map/ppermute | solution.py:266
  95.0 13.1 %collective-permute-start.19 = (bf16[64,2048]{1,0:T(8,128)(2,1)}, bf16[64,2048]{1,0:T(8,128)(2,1)}, u32[]{:S(2)}, u32[]{:S(2)}) collective-permute-start(bf16[64,2048]{1,0:T(8,128)(2,1)} %collective-permute-done.18), channel_id=1, source_target_pairs={{0,4},{1,5},{2,0},{3,1},{4,8},{5,9},{6,2},{7,3},{8,12},{9,13},{10,... | collective-permute-start | bytes 786440 | tf_op jit(solution)/shard_map/ppermute | solution.py:266
  102.6 11.1 %collective-permute-start.11 = (bf16[64,2048]{1,0:T(8,128)(2,1)}, bf16[64,2048]{1,0:T(8,128)(2,1)S(1)}, u32[]{:S(2)}, u32[]{:S(2)}) collective-permute-start(bf16[64,2048]{1,0:T(8,128)(2,1)} %collective-permute-done.10), channel_id=1, source_target_pairs={{0,4},{1,5},{2,0},{3,1},{4,8},{5,9},{6,2},{7,3},{8,12},{9,13},{10,... | collective-permute-start | bytes 786440 | tf_op jit(solution)/shard_map/ppermute | solution.py:266
  104.2 8.7 %collective-permute-start.14 = (bf16[64,2048]{1,0:T(8,128)(2,1)}, bf16[64,2048]{1,0:T(8,128)(2,1)S(1)}, u32[]{:S(2)}, u32[]{:S(2)}) collective-permute-start(bf16[64,2048]{1,0:T(8,128)(2,1)} %collective-permute-done.13), channel_id=1, source_target_pairs={{0,2},{1,3},{2,6},{3,7},{4,0},{5,1},{6,10},{7,11},{8,4},{9,5},{10,... | collective-permute-start | bytes 786440 | tf_op jit(solution)/shard_map/ppermute | solution.py:266
  108.2 12.9 %collective-permute-start.20 = (bf16[64,2048]{1,0:T(8,128)(2,1)}, bf16[64,2048]{1,0:T(8,128)(2,1)S(1)}, u32[]{:S(2)}, u32[]{:S(2)}) collective-permute-start(bf16[64,2048]{1,0:T(8,128)(2,1)} %collective-permute-done.19), channel_id=1, source_target_pairs={{0,4},{1,5},{2,0},{3,1},{4,8},{5,9},{6,2},{7,3},{8,12},{9,13},{10,... | collective-permute-start | bytes 786440 | tf_op jit(solution)/shard_map/ppermute | solution.py:266
  112.9 6.4 %collective-permute-start.15 = (bf16[64,2048]{1,0:T(8,128)(2,1)S(1)}, bf16[64,2048]{1,0:T(8,128)(2,1)S(1)}, u32[]{:S(2)}, u32[]{:S(2)}) collective-permute-start(bf16[64,2048]{1,0:T(8,128)(2,1)S(1)} %collective-permute-done.14), channel_id=1, source_target_pairs={{0,2},{1,3},{2,6},{3,7},{4,0},{5,1},{6,10},{7,11},{8,4},{9,5},{10,... | collective-permute-start | bytes 786440 | tf_op jit(solution)/shard_map/ppermute | solution.py:266
  113.7 6.7 %copy-start = (bf16[768,2048]{1,0:T(8,128)(2,1)S(1)}, bf16[768,2048]{1,0:T(8,128)(2,1)}, u32[]{:S(2)}) copy-start(bf16[768,2048]{1,0:T(8,128)(2,1)} %pad_maximum_fusion.1) | copy-start | bytes 9437188
  124.0 5.4 %copy-start.11 = (bf16[64,2048]{1,0:T(8,128)(2,1)S(1)}, bf16[64,2048]{1,0:T(8,128)(2,1)}, u32[]{:S(2)}) copy-start(bf16[64,2048]{1,0:T(8,128)(2,1)} %copy-done.10) | copy-start | bytes 786436
  125.3 8.6 %collective-permute-start.21 = (bf16[64,2048]{1,0:T(8,128)(2,1)S(1)}, bf16[64,2048]{1,0:T(8,128)(2,1)S(1)}, u32[]{:S(2)}, u32[]{:S(2)}) collective-permute-start(bf16[64,2048]{1,0:T(8,128)(2,1)S(1)} %get-tuple-element.83), channel_id=1, source_target_pairs={{0,4},{1,5},{2,0},{3,1},{4,8},{5,9},{6,2},{7,3},{8,12},{9,13},{10,... | collective-permute-start | bytes 786440 | tf_op jit(solution)/shard_map/ppermute | solution.py:266
  125.3 8.6 %collective-permute-start.25 = (bf16[64,2048]{1,0:T(8,128)(2,1)S(1)}, bf16[64,2048]{1,0:T(8,128)(2,1)S(1)}, u32[]{:S(2)}, u32[]{:S(2)}) collective-permute-start(bf16[64,2048]{1,0:T(8,128)(2,1)S(1)} %get-tuple-element.82), channel_id=1, source_target_pairs={{0,2},{1,3},{2,6},{3,7},{4,0},{5,1},{6,10},{7,11},{8,4},{9,5},{10,... | collective-permute-start | bytes 786440 | tf_op jit(solution)/shard_map/ppermute | solution.py:266
  127.3 12.2 %collective-permute-start.23 = (bf16[64,2048]{1,0:T(8,128)(2,1)S(1)}, bf16[64,2048]{1,0:T(8,128)(2,1)S(1)}, u32[]{:S(2)}, u32[]{:S(2)}) collective-permute-start(bf16[64,2048]{1,0:T(8,128)(2,1)S(1)} %get-tuple-element.85), channel_id=1, source_target_pairs={{0,4},{1,5},{2,0},{3,1},{4,8},{5,9},{6,2},{7,3},{8,12},{9,13},{10,... | collective-permute-start | bytes 786440 | tf_op jit(solution)/shard_map/ppermute | solution.py:266
  127.4 12.2 %collective-permute-start.31 = (bf16[64,2048]{1,0:T(8,128)(2,1)S(1)}, bf16[64,2048]{1,0:T(8,128)(2,1)S(1)}, u32[]{:S(2)}, u32[]{:S(2)}) collective-permute-start(bf16[64,2048]{1,0:T(8,128)(2,1)S(1)} %get-tuple-element.84), channel_id=1, source_target_pairs={{0,2},{1,3},{2,6},{3,7},{4,0},{5,1},{6,10},{7,11},{8,4},{9,5},{10,... | collective-permute-start | bytes 786440 | tf_op jit(solution)/shard_map/ppermute | solution.py:266
  133.5 8.6 %copy-start.7 = (bf16[64,2048]{1,0:T(8,128)(2,1)S(1)}, bf16[64,2048]{1,0:T(8,128)(2,1)}, u32[]{:S(2)}) copy-start(bf16[64,2048]{1,0:T(8,128)(2,1)} %copy-done.6) | copy-start | bytes 786436
  133.5 8.6 %copy-start.9 = (bf16[64,2048]{1,0:T(8,128)(2,1)S(1)}, bf16[64,2048]{1,0:T(8,128)(2,1)}, u32[]{:S(2)}) copy-start(bf16[64,2048]{1,0:T(8,128)(2,1)} %copy-done.8) | copy-start | bytes 786436
  134.0 17.4 %collective-permute-start.22 = (bf16[64,2048]{1,0:T(8,128)(2,1)S(1)}, bf16[64,2048]{1,0:T(8,128)(2,1)S(1)}, u32[]{:S(2)}, u32[]{:S(2)}) collective-permute-start(bf16[64,2048]{1,0:T(8,128)(2,1)S(1)} %get-tuple-element.81), channel_id=1, source_target_pairs={{0,4},{1,5},{2,0},{3,1},{4,8},{5,9},{6,2},{7,3},{8,12},{9,13},{10,... | collective-permute-start | bytes 786440 | tf_op jit(solution)/shard_map/ppermute | solution.py:266
  134.1 17.4 %collective-permute-start.27 = (bf16[64,2048]{1,0:T(8,128)(2,1)S(1)}, bf16[64,2048]{1,0:T(8,128)(2,1)S(1)}, u32[]{:S(2)}, u32[]{:S(2)}) collective-permute-start(bf16[64,2048]{1,0:T(8,128)(2,1)S(1)} %get-tuple-element.80), channel_id=1, source_target_pairs={{0,2},{1,3},{2,6},{3,7},{4,0},{5,1},{6,10},{7,11},{8,4},{9,5},{10,... | collective-permute-start | bytes 786440 | tf_op jit(solution)/shard_map/ppermute | solution.py:266
  139.7 9.4 %collective-permute-start.24 = (bf16[64,2048]{1,0:T(8,128)(2,1)S(1)}, bf16[64,2048]{1,0:T(8,128)(2,1)S(1)}, u32[]{:S(2)}, u32[]{:S(2)}) collective-permute-start(bf16[64,2048]{1,0:T(8,128)(2,1)S(1)} %get-tuple-element.77), channel_id=1, source_target_pairs={{0,4},{1,5},{2,0},{3,1},{4,8},{5,9},{6,2},{7,3},{8,12},{9,13},{10,... | collective-permute-start | bytes 786440 | tf_op jit(solution)/shard_map/ppermute | solution.py:266
  139.7 9.3 %collective-permute-start.32 = (bf16[64,2048]{1,0:T(8,128)(2,1)S(1)}, bf16[64,2048]{1,0:T(8,128)(2,1)S(1)}, u32[]{:S(2)}, u32[]{:S(2)}) collective-permute-start(bf16[64,2048]{1,0:T(8,128)(2,1)S(1)} %get-tuple-element.76), channel_id=1, source_target_pairs={{0,2},{1,3},{2,6},{3,7},{4,0},{5,1},{6,10},{7,11},{8,4},{9,5},{10,... | collective-permute-start | bytes 786440 | tf_op jit(solution)/shard_map/ppermute | solution.py:266
  146.1 14.7 %copy-start.3 = (bf16[64,2048]{1,0:T(8,128)(2,1)S(1)}, bf16[64,2048]{1,0:T(8,128)(2,1)}, u32[]{:S(2)}) copy-start(bf16[64,2048]{1,0:T(8,128)(2,1)} %copy-done.2) | copy-start | bytes 786436
  149.2 8.4 %collective-permute-start.26 = (bf16[64,2048]{1,0:T(8,128)(2,1)S(1)}, bf16[64,2048]{1,0:T(8,128)(2,1)S(1)}, u32[]{:S(2)}, u32[]{:S(2)}) collective-permute-start(bf16[64,2048]{1,0:T(8,128)(2,1)S(1)} %get-tuple-element.75), channel_id=1, source_target_pairs={{0,4},{1,5},{2,0},{3,1},{4,8},{5,9},{6,2},{7,3},{8,12},{9,13},{10,... | collective-permute-start | bytes 786440 | tf_op jit(solution)/shard_map/ppermute | solution.py:266
  151.1 7.4 %collective-permute-start.33 = (bf16[64,2048]{1,0:T(8,128)(2,1)S(1)}, bf16[64,2048]{1,0:T(8,128)(2,1)S(1)}, u32[]{:S(2)}, u32[]{:S(2)}) collective-permute-start(bf16[64,2048]{1,0:T(8,128)(2,1)S(1)} %get-tuple-element.74), channel_id=1, source_target_pairs={{0,2},{1,3},{2,6},{3,7},{4,0},{5,1},{6,10},{7,11},{8,4},{9,5},{10,... | collective-permute-start | bytes 786440 | tf_op jit(solution)/shard_map/ppermute | solution.py:266
  151.6 10.1 %collective-permute-start.29 = (bf16[64,2048]{1,0:T(8,128)(2,1)S(1)}, bf16[64,2048]{1,0:T(8,128)(2,1)S(1)}, u32[]{:S(2)}, u32[]{:S(2)}) collective-permute-start(bf16[64,2048]{1,0:T(8,128)(2,1)S(1)} %get-tuple-element.79), channel_id=1, source_target_pairs={{0,4},{1,5},{2,0},{3,1},{4,8},{5,9},{6,2},{7,3},{8,12},{9,13},{10,... | collective-permute-start | bytes 786440 | tf_op jit(solution)/shard_map/ppermute | solution.py:266
  153.4 8.4 %collective-permute-start.30 = (bf16[64,2048]{1,0:T(8,128)(2,1)S(1)}, bf16[64,2048]{1,0:T(8,128)(2,1)S(1)}, u32[]{:S(2)}, u32[]{:S(2)}) collective-permute-start(bf16[64,2048]{1,0:T(8,128)(2,1)S(1)} %get-tuple-element.78), channel_id=1, source_target_pairs={{0,2},{1,3},{2,6},{3,7},{4,0},{5,1},{6,10},{7,11},{8,4},{9,5},{10,... | collective-permute-start | bytes 786440 | tf_op jit(solution)/shard_map/ppermute | solution.py:266
  158.7 6.4 %collective-permute-start.28 = (bf16[64,2048]{1,0:T(8,128)(2,1)S(1)}, bf16[64,2048]{1,0:T(8,128)(2,1)S(1)}, u32[]{:S(2)}, u32[]{:S(2)}) collective-permute-start(bf16[64,2048]{1,0:T(8,128)(2,1)S(1)} %get-tuple-element.73), channel_id=1, source_target_pairs={{0,4},{1,5},{2,0},{3,1},{4,8},{5,9},{6,2},{7,3},{8,12},{9,13},{10,... | collective-permute-start | bytes 786440 | tf_op jit(solution)/shard_map/ppermute | solution.py:266
  160.2 6.4 %collective-permute-start.34 = (bf16[64,2048]{1,0:T(8,128)(2,1)S(1)}, bf16[64,2048]{1,0:T(8,128)(2,1)S(1)}, u32[]{:S(2)}, u32[]{:S(2)}) collective-permute-start(bf16[64,2048]{1,0:T(8,128)(2,1)S(1)} %get-tuple-element.72), channel_id=1, source_target_pairs={{0,2},{1,3},{2,6},{3,7},{4,0},{5,1},{6,10},{7,11},{8,4},{9,5},{10,... | collective-permute-start | bytes 786440 | tf_op jit(solution)/shard_map/ppermute | solution.py:266
  (2 other events, 1.7 us)
Sparse Core Ops, SparseCore 0:
  10.2 40.1 all-gather.2

commit v13 on v12

--- a/solution.py
+++ b/solution.py
@@ -280,12 +280,6 @@
 
     out_other, in_other, down_other = to_core(out_proj), to_core(expert_in), to_core(expert_out)
 
-    experts = wide * 4
-    gates = jnp.sum(
-        jnp.where(route_ids[:, :, None] == jnp.arange(experts), route_weights[:, :, None], 0.0), axis=1
-    )
-    gates = jnp.pad(gates, ((0, 0), (0, -experts % 128)))
-    gates = lax.all_gather(gates, axes, axis=0, tiled=False)
     normed_top, normed_bottom = normed
 
     halves = range(2)
@@ -298,11 +292,20 @@
             jnp.concatenate([out_other, out_proj], axis=1),
         )
     )
-    columns, normed_bottom = lax.optimization_barrier((columns, normed_bottom))
+    columns, normed_bottom, route_weights = lax.optimization_barrier(
+        (columns, normed_bottom, route_weights)
+    )
     sent = [to_x(normed_top), to_x(normed_bottom)]
 
     def project(rows):
         return jnp.dot(rows, columns, preferred_element_type=jnp.float32).astype(jnp.bfloat16)
+
+    experts = wide * 4
+    chosen = route_ids.T[None] == jnp.arange(experts)[:, None, None]
+    gates = jnp.sum(jnp.where(chosen, route_weights.T[None], 0.0), axis=1)
+    gates = jnp.pad(gates, ((0, -experts % 128), (0, 0)))
+    sent[0], gates = lax.optimization_barrier((sent[0], gates))
+    gates = lax.all_gather(gates, axes, axis=0, tiled=False)
 
     own = [project(normed_top), project(normed_bottom)]
     rows = []
@@ -325,16 +328,18 @@
         back_at[k] = [along(back_at[k - 1][h], -1) for h in halves]
     last = [along(fore_at[far - 1][0], 1), along(back_at[far - 1][1], -1)]
 
-    back_at[far - 1][0], gates = lax.optimization_barrier((back_at[far - 1][0], gates))
-
+    value = back_at[far - 1][0][0, 0]
+    late = (value != value).astype(jnp.int32)
     mine = (z * 2 + x) * 2 + core
-    lanes = jnp.arange(gates.shape[-1])
-    gates = lax.dynamic_slice_in_dim(gates.reshape(wide, 2, 2, frames, -1), core, 1, 2)[:, :, 0]
-    gates = jnp.stack(
-        [jnp.sum(jnp.where(lanes == e, gates, 0.0), axis=-1) for e in (mine, mine + 1 - 2 * core)], axis=-1
-    )
-    gates = jnp.concatenate([gates[:, 0], gates[::-1, 1]])
-    gates = lax.dynamic_slice_in_dim(jnp.concatenate([gates, gates]), place, ring, 0)
+    expert = jnp.arange(experts)[None, :, None]
+    at = (place + jnp.arange(ring)) % ring
+    clip = jnp.where(at < wide, at * 4, (ring - 1 - at) * 4 + 2) + core
+    clip = clip[:, None] == jnp.arange(4 * wide)
+    picked = []
+    for e in (mine + late, mine + 1 - 2 * core + late):
+        of_expert = jnp.sum(jnp.where(expert == e, gates[:, :experts], 0.0), axis=1)
+        picked.append(jnp.sum(jnp.where(clip[:, :, None], of_expert[None], 0.0), axis=1))
+    gates = jnp.stack(picked, axis=-1)
 
     joined_in = jnp.concatenate(
         [

time: 176 us -> 156 us (0.89)
  waiting for transfers between devices: 72.2 us -> 50.3 us
  matrix products: 19.9 us -> 24.9 us
  local copies, waits for them, and re-layouts: 10.6 us -> 7.3 us
    all_gather x1, waiting for transfers between devices: 31.2 us -> 0.01 us  [dense_experts(): gates = lax.all_gather(gates, axes, axis=0, tiled=False)]
    ppermute x35, waiting for transfers between devices: 40.9 us -> 50.3 us  [send(): return lax.ppermute(value, axes, routes(wide, move))]
    unnamed x30, local copies, waits for them, and re-layouts: 4.23 us -> 1.59 us
    dot_general x4, matrix products: 3.43 us -> 5.87 us  [project(): jnp.dot(rows, columns, preferred_element_type=jnp.float32)]
  transfers between devices with their start and end apart: 36 -> 36, of which waited for: 19 -> 18; matrix products, arithmetic and copies ran while one was open for 20% -> 23% of each run, Pallas kernels for 4% -> 4%
where the time goes in v13:
time: 156 us
  waiting for transfers between devices  50.3 us (32%)
  starting transfers between devices  39.2 us (25%)
  matrix products  24.9 us (16%)
  between operations  15.7 us (10%)
  other arithmetic  11.8 us (8%)
  local copies, waits for them, and re-layouts  7.3 us (5%)
  Pallas kernels  6.87 us (4%)
    ppermute x35, waiting for transfers between devices, send(): return lax.ppermute(value, axes, routes(wide, move))  50.3 us
    ppermute x35, starting transfers between devices, send(): return lax.ppermute(value, axes, routes(wide, move))  39.2 us
    dot_general x5, matrix products, run_experts(): jnp.dot(jnp.concatenate(parts), joined_in, preferred_element_type=jnp.flo...  11.8 us
    dot_general x5, matrix products, run_experts(): return jnp.dot(hidden, joined_down, preferred_element_type=jnp.float32)  7.2 us
    pallas_call x1, Pallas kernels, ssm_mixer(): pl.pallas_call(mixer_kernel, grid=(steps,), in_specs=[pl.BlockSpec(memory...  6.87 us
    dot_general x4, matrix products, project(): jnp.dot(rows, columns, preferred_element_type=jnp.float32)  5.87 us
    select_n x1, other arithmetic, dense_experts(): jnp.where(core == 0, jnp.concatenate([out_proj, out_other], axis=1), jnp....  5.08 us
    concatenate x1, other arithmetic, dense_experts(): joined_down = jnp.concatenate([expert_out, down_other], axis=0)  4.07 us
  transfers between devices with their start and end apart: 36, of which 18 were waited for; matrix products, arithmetic and copies ran while one was open for 23% of the time, Pallas kernels for 4%

profile of v13, /device:TPU:0, one launch (start us, length us, event | category | flops | bytes accessed | tf_op | source)
XLA Modules:
  0.0 156.1 jit_solution(11416268403046496688)
XLA Ops:
  7.7 6.9 %mixer.1 = (bf16[64,2048]{1,0:T(8,128)(2,1)}, bf16[64,2048]{1,0:T(8,128)(2,1)}, f32[2048,128]{1,0:T(8,128)}) custom-call(f32[32]{0:T(128)} %skip_ref.1, bf16[128,2048]{1,0:T(8,128)(2,1)} %x_ref.1, bf16[128,2048]{1,0:T(8,128)(2,1)} %z_ref.1, bf16[128,128]{1,0:T(8,128)(2,1)} %b_ref.1, bf16[128,128]{1,0:T(8,128)(2,1)} %c_ref.1, f32[32,128]{1,0:T(8,128)} %bitcast.80, ...), custom_call_target="tpu_custom_call" | custom-call | flops 400000000 | bytes 6000000 | tf_op jit(solution)/shard_map/mixer/pallas_call | solution.py:149
  14.6 2.6 %collective-permute-start.1 = (bf16[64,2048]{1,0:T(8,128)(2,1)}, bf16[64,2048]{1,0:T(8,128)(2,1)S(1)}, u32[]{:S(2)}, u32[]{:S(2)}) collective-permute-start(bf16[64,2048]{1,0:T(8,128)(2,1)} %get-tuple-element.35), channel_id=1, source_target_pairs={{0,2},{1,3},{2,0},{3,1},{4,6},{5,7},{6,4},{7,5},{8,10},{9,11},{10,... | collective-permute-start | bytes 786440 | tf_op jit(solution)/shard_map/ppermute | solution.py:266
  17.9 5.1 %maximum_select_fusion = bf16[2048,1024]{1,0:T(8,128)(2,1)} fusion(bf16[2048,512]{1,0:T(8,128)(2,1)} %collective-permute-done, bf16[2048,512]{1,0:T(8,128)(2,1)S(1)} %copy-done.4, pred[]{:T(512)S(6)} %eq.65), kind=kLoop, calls=%fused_computation.1 | loop fusion | flops 18874368 | bytes 8388609 | tf_op jit(solution)/shard_map/jit(_where)/select_n | solution.py:289
  24.3 3.3 %convolution_convert_fusion.3 = bf16[64,1024]{1,0:T(8,128)(2,1)S(1)} fusion(bf16[64,2048]{1,0:T(8,128)(2,1)S(1)} %collective-permute-done.1, bf16[2048,1024]{1,0:T(8,128)(2,1)} %maximum_select_fusion), kind=kOutput, calls=%fused_computation.6 | convolution fusion | flops 268500992 | bytes 4587520 | tf_op jit(solution)/shard_map/dot_general | solution.py:301
  27.6 1.5 collective-permute-start.2
  30.6 3.5 %collective-permute-done.2 = bf16[64,1024]{1,0:T(8,128)(2,1)S(1)} collective-permute-done((bf16[64,1024]{1,0:T(8,128)(2,1)S(1)}, bf16[64,1024]{1,0:T(8,128)(2,1)S(1)}, u32[]{:S(2)}, u32[]{:S(2)}) %collective-permute-start.2) | collective-permute-done | bytes 131104 | tf_op jit(solution)/shard_map/ppermute | solution.py:266
  34.2 1.5 collective-permute-start.5
  36.2 3.5 %collective-permute-done.3 = bf16[64,2048]{1,0:T(8,128)(2,1)S(1)} collective-permute-done((bf16[64,2048]{1,0:T(8,128)(2,1)S(1)}, bf16[64,2048]{1,0:T(8,128)(2,1)S(1)}, u32[]{:S(2)}, u32[]{:S(2)}) %collective-permute-start.3) | collective-permute-done | bytes 262176 | tf_op jit(solution)/shard_map/ppermute | solution.py:266
  40.6 1.5 collective-permute-start.4
  42.9 3.8 %collective-permute-done.4 = bf16[64,1024]{1,0:T(8,128)(2,1)S(1)} collective-permute-done((bf16[64,1024]{1,0:T(8,128)(2,1)S(1)}, bf16[64,1024]{1,0:T(8,128)(2,1)S(1)}, u32[]{:S(2)}, u32[]{:S(2)}) %collective-permute-start.4) | collective-permute-done | bytes 131104 | tf_op jit(solution)/shard_map/ppermute | solution.py:266
  46.9 1.4 collective-permute-start.12
  48.9 1.3 collective-permute-start.6
  51.0 2.2 %fusion.105 = (bf16[2048,384]{1,0:T(8,128)(2,1)S(1)}, bf16[2048,384]{1,0:T(8,128)(2,1)S(1)}) fusion(bf16[2048,768]{1,0:T(8,128)(2,1)} %bitcast.7), kind=kLoop, calls=%fused_computation.166 | loop fusion | bytes 6291456 | tf_op jit(solution)/shard_map/slice | solution.py:346
  53.2 7.8 %collective-permute-done.6 = bf16[64,2048]{1,0:T(8,128)(2,1)S(1)} collective-permute-done((bf16[64,2048]{1,0:T(8,128)(2,1)}, bf16[64,2048]{1,0:T(8,128)(2,1)S(1)}, u32[]{:S(2)}, u32[]{:S(2)}) %collective-permute-start.6) | collective-permute-done | bytes 262176 | tf_op jit(solution)/shard_map/ppermute | solution.py:266
  61.5 1.5 collective-permute-start.10
  63.6 1.5 collective-permute-start.19
  65.1 4.1 %pad_maximum_fusion.1 = bf16[768,2048]{1,0:T(8,128)(2,1)} fusion(bf16[384,2048]{1,0:T(8,128)(2,1)} %collective-permute-done.17, bf16[384,2048]{1,0:T(8,128)(2,1)} %bitcast.8), kind=kLoop, calls=%fused_computation.2 | loop fusion | flops 6291456 | bytes 6291456 | tf_op jit(solution)/shard_map/concatenate | solution.py:353
  72.6 1.3 collective-permute-start.11
  73.9 2.7 %collective-permute-done.13 = bf16[64,2048]{1,0:T(8,128)(2,1)} collective-permute-done((bf16[64,2048]{1,0:T(8,128)(2,1)}, bf16[64,2048]{1,0:T(8,128)(2,1)}, u32[]{:S(2)}, u32[]{:S(2)}) %collective-permute-start.13) | collective-permute-done | bytes 262176 | tf_op jit(solution)/shard_map/ppermute | solution.py:266
  77.7 1.7 %collective-permute-done.19 = bf16[64,2048]{1,0:T(8,128)(2,1)} collective-permute-done((bf16[64,2048]{1,0:T(8,128)(2,1)}, bf16[64,2048]{1,0:T(8,128)(2,1)}, u32[]{:S(2)}, u32[]{:S(2)}) %collective-permute-start.19) | collective-permute-done | bytes 262176 | tf_op jit(solution)/shard_map/ppermute | solution.py:266
  79.4 2.5 %collective-permute-start.20 = (bf16[64,2048]{1,0:T(8,128)(2,1)}, bf16[64,2048]{1,0:T(8,128)(2,1)}, u32[]{:S(2)}, u32[]{:S(2)}) collective-permute-start(bf16[64,2048]{1,0:T(8,128)(2,1)} %collective-permute-done.19), channel_id=1, source_target_pairs={{0,4},{1,5},{2,0},{3,1},{4,8},{5,9},{6,2},{7,3},{8,12},{9,13},{10,... | collective-permute-start | bytes 786440 | tf_op jit(solution)/shard_map/ppermute | solution.py:266
  81.9 2.2 %fusion.106 = (bf16[2048,384]{1,0:T(8,128)(2,1)S(1)}, bf16[2048,384]{1,0:T(8,128)(2,1)S(1)}) fusion(bf16[2048,768]{1,0:T(8,128)(2,1)} %collective-permute-done.16), kind=kLoop, calls=%fused_computation.167 | loop fusion | bytes 6291456 | tf_op jit(solution)/shard_map/slice | solution.py:347
  84.1 1.5 collective-permute-done.14
  87.4 4.5 %collective-permute-done.15 = bf16[64,2048]{1,0:T(8,128)(2,1)S(1)} collective-permute-done((bf16[64,2048]{1,0:T(8,128)(2,1)S(1)}, bf16[64,2048]{1,0:T(8,128)(2,1)S(1)}, u32[]{:S(2)}, u32[]{:S(2)}) %collective-permute-start.15) | collective-permute-done | bytes 262176 | tf_op jit(solution)/shard_map/ppermute | solution.py:266
  91.9 1.9 %fusion.40 = f32[128,1536]{1,0:T(8,128)} fusion(bf16[2048,1536]{1,0:T(8,128)(2,1)S(1)} %pad_maximum_fusion, bf16[64,2048]{1,0:T(8,128)(2,1)S(1)} %collective-permute-done.15, bf16[64,2048]{1,0:T(8,128)(2,1)S(1)} %collective-permute-done.11), kind=kOutput, calls=%fused_computation.62 | convolution fusion | flops 806354944 | bytes 7602176 | tf_op jit(solution)/shard_map/dot_general | solution.py:358
  95.0 2.0 %convolution_convert_fusion = bf16[128,2048]{1,0:T(8,128)(2,1)S(1)} fusion(bf16[768,2048]{1,0:T(8,128)(2,1)S(1)} %copy-done.3, f32[128,1536]{1,0:T(8,128)} %fusion.40, f32[128]{0:T(128)S(1)} %get-tuple-element.107, f32[128]{0:T(128)S(1)} %get-tuple-element.106, pred[768]{0:T(1024)(128)(4,1)S(1)} %iota_compare_fusion.2), kind=kOutput, calls=%fused_computation.3 | convolution fusion | flops 403701760 | bytes 4458240 | tf_op jit(solution)/shard_map/dot_general | solution.py:361
  97.9 3.0 %fusion = f32[256,1536]{1,0:T(8,128)S(1)} fusion(bf16[2048,1536]{1,0:T(8,128)(2,1)S(1)} %copy-done.2, bf16[64,2048]{1,0:T(8,128)(2,1)} %collective-permute-done.20, bf16[64,2048]{1,0:T(8,128)(2,1)} %collective-permute-done.10, bf16[64,2048]{1,0:T(8,128)(2,1)} %copy-done.14, bf16[64,2048]{1,0:T(8,128)(2,1)} %copy-done.13), kind=kOutput, calls=%fused_computation.8 | convolution fusion | flops 1614807040 | bytes 8912896 | tf_op jit(solution)/shard_map/dot_general | solution.py:358
  100.9 1.2 fusion.109
  102.1 1.6 %collective-permute-start.21 = (bf16[64,2048]{1,0:T(8,128)(2,1)S(1)}, bf16[64,2048]{1,0:T(8,128)(2,1)S(1)}, u32[]{:S(2)}, u32[]{:S(2)}) collective-permute-start(bf16[64,2048]{1,0:T(8,128)(2,1)S(1)} %get-tuple-element.87), channel_id=1, source_target_pairs={{0,4},{1,5},{2,0},{3,1},{4,8},{5,9},{6,2},{7,3},{8,12},{9,13},{10,... | collective-permute-start | bytes 786440 | tf_op jit(solution)/shard_map/ppermute | solution.py:266
  104.2 2.7 %collective-permute-start.23 = (bf16[64,2048]{1,0:T(8,128)(2,1)S(1)}, bf16[64,2048]{1,0:T(8,128)(2,1)S(1)}, u32[]{:S(2)}, u32[]{:S(2)}) collective-permute-start(bf16[64,2048]{1,0:T(8,128)(2,1)S(1)} %get-tuple-element.89), channel_id=1, source_target_pairs={{0,4},{1,5},{2,0},{3,1},{4,8},{5,9},{6,2},{7,3},{8,12},{9,13},{10,... | collective-permute-start | bytes 786440 | tf_op jit(solution)/shard_map/ppermute | solution.py:266
  106.9 2.9 %fusion.8 = f32[256,1536]{1,0:T(8,128)S(1)} fusion(bf16[2048,1536]{1,0:T(8,128)(2,1)S(1)} %copy-done.2, bf16[64,2048]{1,0:T(8,128)(2,1)} %collective-permute-done.19, bf16[64,2048]{1,0:T(8,128)(2,1)} %collective-permute-done.9, bf16[64,2048]{1,0:T(8,128)(2,1)} %collective-permute-done.13, bf16[64,2048]{1,0:T(8,128)(2,1)S(1)} %copy-done.12), kind=kOutput, calls=%fused_computation.16 | convolution fusion | flops 1614807040 | bytes 8912896 | tf_op jit(solution)/shard_map/dot_general | solution.py:358
  109.9 1.2 fusion.50
  111.1 2.6 %collective-permute-done.25 = bf16[64,2048]{1,0:T(8,128)(2,1)S(1)} collective-permute-done((bf16[64,2048]{1,0:T(8,128)(2,1)S(1)}, bf16[64,2048]{1,0:T(8,128)(2,1)S(1)}, u32[]{:S(2)}, u32[]{:S(2)}) %collective-permute-start.25) | collective-permute-done | bytes 262176 | tf_op jit(solution)/shard_map/ppermute | solution.py:266
  113.8 2.3 %collective-permute-start.22 = (bf16[64,2048]{1,0:T(8,128)(2,1)S(1)}, bf16[64,2048]{1,0:T(8,128)(2,1)S(1)}, u32[]{:S(2)}, u32[]{:S(2)}) collective-permute-start(bf16[64,2048]{1,0:T(8,128)(2,1)S(1)} %get-tuple-element.85), channel_id=1, source_target_pairs={{0,4},{1,5},{2,0},{3,1},{4,8},{5,9},{6,2},{7,3},{8,12},{9,13},{10,... | collective-permute-start | bytes 786440 | tf_op jit(solution)/shard_map/ppermute | solution.py:266
  116.1 3.2 %collective-permute-done.31 = bf16[64,2048]{1,0:T(8,128)(2,1)S(1)} collective-permute-done((bf16[64,2048]{1,0:T(8,128)(2,1)S(1)}, bf16[64,2048]{1,0:T(8,128)(2,1)S(1)}, u32[]{:S(2)}, u32[]{:S(2)}) %collective-permute-start.31) | collective-permute-done | bytes 262176 | tf_op jit(solution)/shard_map/ppermute | solution.py:266
  119.4 2.3 %collective-permute-start.24 = (bf16[64,2048]{1,0:T(8,128)(2,1)S(1)}, bf16[64,2048]{1,0:T(8,128)(2,1)S(1)}, u32[]{:S(2)}, u32[]{:S(2)}) collective-permute-start(bf16[64,2048]{1,0:T(8,128)(2,1)S(1)} %get-tuple-element.81), channel_id=1, source_target_pairs={{0,4},{1,5},{2,0},{3,1},{4,8},{5,9},{6,2},{7,3},{8,12},{9,13},{10,... | collective-permute-start | bytes 786440 | tf_op jit(solution)/shard_map/ppermute | solution.py:266
  121.7 3.0 %fusion.16 = f32[256,1536]{1,0:T(8,128)S(1)} fusion(bf16[2048,1536]{1,0:T(8,128)(2,1)S(1)} %copy-done.2, bf16[64,2048]{1,0:T(8,128)(2,1)} %collective-permute-done.18, bf16[64,2048]{1,0:T(8,128)(2,1)} %collective-permute-done.8, bf16[64,2048]{1,0:T(8,128)(2,1)} %collective-permute-done.12, bf16[64,2048]{1,0:T(8,128)(2,1)} %collective-permute-done.5), kind=kOutput, calls=%fused_computation.24 | convolution fusion | flops 1614807040 | bytes 8912896 | tf_op jit(solution)/shard_map/dot_general | solution.py:358
  124.7 1.2 fusion.52
  125.9 2.7 %collective-permute-done.24 = bf16[64,2048]{1,0:T(8,128)(2,1)S(1)} collective-permute-done((bf16[64,2048]{1,0:T(8,128)(2,1)S(1)}, bf16[64,2048]{1,0:T(8,128)(2,1)S(1)}, u32[]{:S(2)}, u32[]{:S(2)}) %collective-permute-start.24) | collective-permute-done | bytes 262176 | tf_op jit(solution)/shard_map/ppermute | solution.py:266
  128.6 2.3 %collective-permute-done.32 = bf16[64,2048]{1,0:T(8,128)(2,1)S(1)} collective-permute-done((bf16[64,2048]{1,0:T(8,128)(2,1)S(1)}, bf16[64,2048]{1,0:T(8,128)(2,1)S(1)}, u32[]{:S(2)}, u32[]{:S(2)}) %collective-permute-start.32) | collective-permute-done | bytes 262176 | tf_op jit(solution)/shard_map/ppermute | solution.py:266
  131.0 2.1 %collective-permute-start.26 = (bf16[64,2048]{1,0:T(8,128)(2,1)S(1)}, bf16[64,2048]{1,0:T(8,128)(2,1)S(1)}, u32[]{:S(2)}, u32[]{:S(2)}) collective-permute-start(bf16[64,2048]{1,0:T(8,128)(2,1)S(1)} %get-tuple-element.79), channel_id=1, source_target_pairs={{0,4},{1,5},{2,0},{3,1},{4,8},{5,9},{6,2},{7,3},{8,12},{9,13},{10,... | collective-permute-start | bytes 786440 | tf_op jit(solution)/shard_map/ppermute | solution.py:266
  133.3 2.1 %collective-permute-start.29 = (bf16[64,2048]{1,0:T(8,128)(2,1)S(1)}, bf16[64,2048]{1,0:T(8,128)(2,1)S(1)}, u32[]{:S(2)}, u32[]{:S(2)}) collective-permute-start(bf16[64,2048]{1,0:T(8,128)(2,1)S(1)} %get-tuple-element.83), channel_id=1, source_target_pairs={{0,4},{1,5},{2,0},{3,1},{4,8},{5,9},{6,2},{7,3},{8,12},{9,13},{10,... | collective-permute-start | bytes 786440 | tf_op jit(solution)/shard_map/ppermute | solution.py:266
  135.4 2.1 %collective-permute-done.26 = bf16[64,2048]{1,0:T(8,128)(2,1)S(1)} collective-permute-done((bf16[64,2048]{1,0:T(8,128)(2,1)S(1)}, bf16[64,2048]{1,0:T(8,128)(2,1)S(1)}, u32[]{:S(2)}, u32[]{:S(2)}) %collective-permute-start.26) | collective-permute-done | bytes 262176 | tf_op jit(solution)/shard_map/ppermute | solution.py:266
  137.5 2.0 %collective-permute-done.33 = bf16[64,2048]{1,0:T(8,128)(2,1)S(1)} collective-permute-done((bf16[64,2048]{1,0:T(8,128)(2,1)S(1)}, bf16[64,2048]{1,0:T(8,128)(2,1)S(1)}, u32[]{:S(2)}, u32[]{:S(2)}) %collective-permute-start.33) | collective-permute-done | bytes 262176 | tf_op jit(solution)/shard_map/ppermute | solution.py:266
  139.6 1.5 collective-permute-start.28
  142.8 3.3 %collective-permute-done.28 = bf16[64,2048]{1,0:T(8,128)(2,1)S(1)} collective-permute-done((bf16[64,2048]{1,0:T(8,128)(2,1)S(1)}, bf16[64,2048]{1,0:T(8,128)(2,1)S(1)}, u32[]{:S(2)}, u32[]{:S(2)}) %collective-permute-start.28) | collective-permute-done | bytes 262176 | tf_op jit(solution)/shard_map/ppermute | solution.py:266
  146.1 1.5 collective-permute-done.34
  147.5 1.7 %add_convert_fusion = bf16[128,2048]{1,0:T(8,128)(2,1)} fusion(bf16[64,2048]{1,0:T(8,128)(2,1)S(1)} %copy-done.6, bf16[64,2048]{1,0:T(8,128)(2,1)S(1)} %maximum_select_fusion.1, bf16[64,2048]{1,0:T(8,128)(2,1)S(1)} %collective-permute-done.29, bf16[64,2048]{1,0:T(8,128)(2,1)S(1)} %collective-permute-done.28, ...), kind=kOutput, calls=%fused_computation.32 | convolution fusion | flops 407633920 | bytes 6031104 | tf_op jit(solution)/shard_map/dot_general | solution.py:361
  (99 shorter events, 18.6 us)
Async XLA Ops:
  7.2 10.7 %copy-start.4 = (bf16[2048,512]{1,0:T(8,128)(2,1)S(1)}, bf16[2048,512]{1,0:T(8,128)(2,1)}, u32[]{:S(2)}) copy-start(bf16[2048,512]{1,0:T(8,128)(2,1)} %param.25) | copy-start | bytes 6291460
  7.2 86.7 %all-gather.3.cloned.1.call-start = ((), (), s32[]{:S(2)}) async-start(), calls=%async_computation | async-start | bytes 1114112 | tf_op jit(solution)/shard_map/all_gather | solution.py:308
  7.2 10.6 %collective-permute-start = (bf16[2048,512]{1,0:T(8,128)(2,1)}, bf16[2048,512]{1,0:T(8,128)(2,1)}, u32[]{:S(2)}, u32[]{:S(2)}) collective-permute-start(bf16[2048,512]{1,0:T(8,128)(2,1)} %param.25), channel_id=1, source_target_pairs={{0,1},{1,0},{2,3},{3,2},{4,5},{5,4},{6,7},{7,6},{8,9},{9,8},{10,11... | collective-permute-start | bytes 6291464 | tf_op jit(solution)/shard_map/ppermute | solution.py:266
  14.6 9.7 %collective-permute-start.1 = (bf16[64,2048]{1,0:T(8,128)(2,1)}, bf16[64,2048]{1,0:T(8,128)(2,1)S(1)}, u32[]{:S(2)}, u32[]{:S(2)}) collective-permute-start(bf16[64,2048]{1,0:T(8,128)(2,1)} %get-tuple-element.35), channel_id=1, source_target_pairs={{0,2},{1,3},{2,0},{3,1},{4,6},{5,7},{6,4},{7,5},{8,10},{9,11},{10,... | collective-permute-start | bytes 786440 | tf_op jit(solution)/shard_map/ppermute | solution.py:266
  17.2 64.7 %collective-permute-start.16 = (bf16[2048,768]{1,0:T(8,128)(2,1)}, bf16[2048,768]{1,0:T(8,128)(2,1)}, u32[]{:S(2)}, u32[]{:S(2)}) collective-permute-start(bf16[2048,768]{1,0:T(8,128)(2,1)} %bitcast.7), channel_id=1, source_target_pairs={{0,1},{1,0},{2,3},{3,2},{4,5},{5,4},{6,7},{7,6},{8,9},{9,8},{10,11... | collective-permute-start | bytes 9437192 | tf_op jit(solution)/shard_map/ppermute | solution.py:266
  17.3 30.9 %collective-permute-start.17 = (bf16[384,2048]{1,0:T(8,128)(2,1)}, bf16[384,2048]{1,0:T(8,128)(2,1)}, u32[]{:S(2)}, u32[]{:S(2)}) collective-permute-start(bf16[384,2048]{1,0:T(8,128)(2,1)} %bitcast.8), channel_id=1, source_target_pairs={{0,1},{1,0},{2,3},{3,2},{4,5},{5,4},{6,7},{7,6},{8,9},{9,8},{10,11... | collective-permute-start | bytes 4718600 | tf_op jit(solution)/shard_map/ppermute | solution.py:266
  17.8 5.1 %copy-start.9 = (f32[128,8]{0,1:T(8,128)S(1)}, f32[128,8]{0,1:T(8,128)}, u32[]{:S(2)}) copy-start(f32[128,8]{0,1:T(8,128)} %param.29) | copy-start | bytes 12292
  17.8 5.1 %copy-start.10 = (s32[128,8]{0,1:T(8,128)S(1)}, s32[128,8]{0,1:T(8,128)}, u32[]{:S(2)}) copy-start(s32[128,8]{0,1:T(8,128)} %param.28) | copy-start | bytes 12292
  17.9 11.8 %copy-start.8 = (bf16[64,2048]{1,0:T(8,128)(2,1)S(1)}, bf16[64,2048]{1,0:T(8,128)(2,1)}, u32[]{:S(2)}) copy-start(bf16[64,2048]{1,0:T(8,128)(2,1)} %get-tuple-element.35) | copy-start | bytes 786436
  23.0 6.2 %copy-start.7 = (bf16[64,2048]{1,0:T(8,128)(2,1)S(1)}, bf16[64,2048]{1,0:T(8,128)(2,1)}, u32[]{:S(2)}) copy-start(bf16[64,2048]{1,0:T(8,128)(2,1)} %get-tuple-element.40) | copy-start | bytes 786436
  23.6 6.1 %copy-start = (bf16[2048,1024]{1,0:T(8,128)(2,1)S(1)}, bf16[2048,1024]{1,0:T(8,128)(2,1)}, u32[]{:S(2)}) copy-start(bf16[2048,1024]{1,0:T(8,128)(2,1)} %maximum_select_fusion) | copy-start | bytes 12582916
  27.6 6.5 %collective-permute-start.2 = (bf16[64,1024]{1,0:T(8,128)(2,1)S(1)}, bf16[64,1024]{1,0:T(8,128)(2,1)S(1)}, u32[]{:S(2)}, u32[]{:S(2)}) collective-permute-start(bf16[64,1024]{1,0:T(8,128)(2,1)S(1)} %convolution_convert_fusion.3), channel_id=1, source_target_pairs={{0,2},{1,3},{2,0},{3,1},{4,6},{5,7},{6,4},{7,5},{8,10},{9,11},{10,... | collective-permute-start | bytes 393224 | tf_op jit(solution)/shard_map/ppermute | solution.py:266
  29.1 10.6 %collective-permute-start.3 = (bf16[64,2048]{1,0:T(8,128)(2,1)S(1)}, bf16[64,2048]{1,0:T(8,128)(2,1)S(1)}, u32[]{:S(2)}, u32[]{:S(2)}) collective-permute-start(bf16[64,2048]{1,0:T(8,128)(2,1)S(1)} %copy-done.7), channel_id=1, source_target_pairs={{0,2},{1,3},{2,0},{3,1},{4,6},{5,7},{6,4},{7,5},{8,10},{9,11},{10,... | collective-permute-start | bytes 786440 | tf_op jit(solution)/shard_map/ppermute | solution.py:266
  34.2 14.8 %collective-permute-start.5 = (bf16[64,2048]{1,0:T(8,128)(2,1)S(1)}, bf16[64,2048]{1,0:T(8,128)(2,1)}, u32[]{:S(2)}, u32[]{:S(2)}) collective-permute-start(bf16[64,2048]{1,0:T(8,128)(2,1)S(1)} %maximum_select_fusion.1), channel_id=1, source_target_pairs={{0,2},{1,3},{2,6},{3,7},{4,0},{5,1},{6,10},{7,11},{8,4},{9,5},{10,... | collective-permute-start | bytes 786440 | tf_op jit(solution)/shard_map/ppermute | solution.py:266
  35.7 14.6 %collective-permute-start.8 = (bf16[64,2048]{1,0:T(8,128)(2,1)S(1)}, bf16[64,2048]{1,0:T(8,128)(2,1)}, u32[]{:S(2)}, u32[]{:S(2)}) collective-permute-start(bf16[64,2048]{1,0:T(8,128)(2,1)S(1)} %maximum_select_fusion.1), channel_id=1, source_target_pairs={{0,4},{1,5},{2,0},{3,1},{4,8},{5,9},{6,2},{7,3},{8,12},{9,13},{10,... | collective-permute-start | bytes 786440 | tf_op jit(solution)/shard_map/ppermute | solution.py:266
  40.6 6.2 %collective-permute-start.4 = (bf16[64,1024]{1,0:T(8,128)(2,1)S(1)}, bf16[64,1024]{1,0:T(8,128)(2,1)S(1)}, u32[]{:S(2)}, u32[]{:S(2)}) collective-permute-start(bf16[64,1024]{1,0:T(8,128)(2,1)S(1)} %convolution_convert_fusion.1), channel_id=1, source_target_pairs={{0,2},{1,3},{2,0},{3,1},{4,6},{5,7},{6,4},{7,5},{8,10},{9,11},{10,... | collective-permute-start | bytes 393224 | tf_op jit(solution)/shard_map/ppermute | solution.py:266
  46.8 3.4 %copy-start.5 = (bf16[64,2048]{1,0:T(8,128)(2,1)}, bf16[64,2048]{1,0:T(8,128)(2,1)S(1)}, u32[]{:S(2)}) copy-start(bf16[64,2048]{1,0:T(8,128)(2,1)S(1)} %maximum_select_fusion.2) | copy-start | bytes 786436
  46.9 16.2 %collective-permute-start.12 = (bf16[64,2048]{1,0:T(8,128)(2,1)S(1)}, bf16[64,2048]{1,0:T(8,128)(2,1)}, u32[]{:S(2)}, u32[]{:S(2)}) collective-permute-start(bf16[64,2048]{1,0:T(8,128)(2,1)S(1)} %maximum_select_fusion.2), channel_id=1, source_target_pairs={{0,2},{1,3},{2,6},{3,7},{4,0},{5,1},{6,10},{7,11},{8,4},{9,5},{10,... | collective-permute-start | bytes 786440 | tf_op jit(solution)/shard_map/ppermute | solution.py:266
  48.2 15.3 %collective-permute-start.18 = (bf16[64,2048]{1,0:T(8,128)(2,1)S(1)}, bf16[64,2048]{1,0:T(8,128)(2,1)}, u32[]{:S(2)}, u32[]{:S(2)}) collective-permute-start(bf16[64,2048]{1,0:T(8,128)(2,1)S(1)} %maximum_select_fusion.2), channel_id=1, source_target_pairs={{0,4},{1,5},{2,0},{3,1},{4,8},{5,9},{6,2},{7,3},{8,12},{9,13},{10,... | collective-permute-start | bytes 786440 | tf_op jit(solution)/shard_map/ppermute | solution.py:266
  48.9 12.1 %collective-permute-start.6 = (bf16[64,2048]{1,0:T(8,128)(2,1)}, bf16[64,2048]{1,0:T(8,128)(2,1)S(1)}, u32[]{:S(2)}, u32[]{:S(2)}) collective-permute-start(bf16[64,2048]{1,0:T(8,128)(2,1)} %collective-permute-done.5), channel_id=1, source_target_pairs={{0,2},{1,3},{2,6},{3,7},{4,0},{5,1},{6,10},{7,11},{8,4},{9,5},{10,... | collective-permute-start | bytes 786440 | tf_op jit(solution)/shard_map/ppermute | solution.py:266
  50.3 11.2 %collective-permute-start.9 = (bf16[64,2048]{1,0:T(8,128)(2,1)}, bf16[64,2048]{1,0:T(8,128)(2,1)}, u32[]{:S(2)}, u32[]{:S(2)}) collective-permute-start(bf16[64,2048]{1,0:T(8,128)(2,1)} %collective-permute-done.8), channel_id=1, source_target_pairs={{0,4},{1,5},{2,0},{3,1},{4,8},{5,9},{6,2},{7,3},{8,12},{9,13},{10,... | collective-permute-start | bytes 786440 | tf_op jit(solution)/shard_map/ppermute | solution.py:266
  61.0 8.1 %copy-start.11 = (bf16[64,2048]{1,0:T(8,128)(2,1)}, bf16[64,2048]{1,0:T(8,128)(2,1)S(1)}, u32[]{:S(2)}) copy-start(bf16[64,2048]{1,0:T(8,128)(2,1)S(1)} %collective-permute-done.6) | copy-start | bytes 786436
  61.0 9.0 %collective-permute-start.7 = (bf16[64,2048]{1,0:T(8,128)(2,1)S(1)}, bf16[64,2048]{1,0:T(8,128)(2,1)S(1)}, u32[]{:S(2)}, u32[]{:S(2)}) collective-permute-start(bf16[64,2048]{1,0:T(8,128)(2,1)S(1)} %collective-permute-done.6), channel_id=1, source_target_pairs={{0,2},{1,3},{2,6},{3,7},{4,0},{5,1},{6,10},{7,11},{8,4},{9,5},{10,... | collective-permute-start | bytes 786440 | tf_op jit(solution)/shard_map/ppermute | solution.py:266
  61.5 11.1 %collective-permute-start.10 = (bf16[64,2048]{1,0:T(8,128)(2,1)}, bf16[64,2048]{1,0:T(8,128)(2,1)}, u32[]{:S(2)}, u32[]{:S(2)}) collective-permute-start(bf16[64,2048]{1,0:T(8,128)(2,1)} %collective-permute-done.9), channel_id=1, source_target_pairs={{0,4},{1,5},{2,0},{3,1},{4,8},{5,9},{6,2},{7,3},{8,12},{9,13},{10,... | collective-permute-start | bytes 786440 | tf_op jit(solution)/shard_map/ppermute | solution.py:266
  63.0 13.5 %collective-permute-start.13 = (bf16[64,2048]{1,0:T(8,128)(2,1)}, bf16[64,2048]{1,0:T(8,128)(2,1)}, u32[]{:S(2)}, u32[]{:S(2)}) collective-permute-start(bf16[64,2048]{1,0:T(8,128)(2,1)} %collective-permute-done.12), channel_id=1, source_target_pairs={{0,2},{1,3},{2,6},{3,7},{4,0},{5,1},{6,10},{7,11},{8,4},{9,5},{10,... | collective-permute-start | bytes 786440 | tf_op jit(solution)/shard_map/ppermute | solution.py:266
  63.6 15.9 %collective-permute-start.19 = (bf16[64,2048]{1,0:T(8,128)(2,1)}, bf16[64,2048]{1,0:T(8,128)(2,1)}, u32[]{:S(2)}, u32[]{:S(2)}) collective-permute-start(bf16[64,2048]{1,0:T(8,128)(2,1)} %collective-permute-done.18), channel_id=1, source_target_pairs={{0,4},{1,5},{2,0},{3,1},{4,8},{5,9},{6,2},{7,3},{8,12},{9,13},{10,... | collective-permute-start | bytes 786440 | tf_op jit(solution)/shard_map/ppermute | solution.py:266
  72.6 14.9 %collective-permute-start.11 = (bf16[64,2048]{1,0:T(8,128)(2,1)}, bf16[64,2048]{1,0:T(8,128)(2,1)S(1)}, u32[]{:S(2)}, u32[]{:S(2)}) collective-permute-start(bf16[64,2048]{1,0:T(8,128)(2,1)} %collective-permute-done.10), channel_id=1, source_target_pairs={{0,4},{1,5},{2,0},{3,1},{4,8},{5,9},{6,2},{7,3},{8,12},{9,13},{10,... | collective-permute-start | bytes 786440 | tf_op jit(solution)/shard_map/ppermute | solution.py:266
  76.6 9.0 %collective-permute-start.14 = (bf16[64,2048]{1,0:T(8,128)(2,1)}, bf16[64,2048]{1,0:T(8,128)(2,1)S(1)}, u32[]{:S(2)}, u32[]{:S(2)}) collective-permute-start(bf16[64,2048]{1,0:T(8,128)(2,1)} %collective-permute-done.13), channel_id=1, source_target_pairs={{0,2},{1,3},{2,6},{3,7},{4,0},{5,1},{6,10},{7,11},{8,4},{9,5},{10,... | collective-permute-start | bytes 786440 | tf_op jit(solution)/shard_map/ppermute | solution.py:266
  79.4 17.6 %collective-permute-start.20 = (bf16[64,2048]{1,0:T(8,128)(2,1)}, bf16[64,2048]{1,0:T(8,128)(2,1)}, u32[]{:S(2)}, u32[]{:S(2)}) collective-permute-start(bf16[64,2048]{1,0:T(8,128)(2,1)} %collective-permute-done.19), channel_id=1, source_target_pairs={{0,4},{1,5},{2,0},{3,1},{4,8},{5,9},{6,2},{7,3},{8,12},{9,13},{10,... | collective-permute-start | bytes 786440 | tf_op jit(solution)/shard_map/ppermute | solution.py:266
  85.6 6.4 %collective-permute-start.15 = (bf16[64,2048]{1,0:T(8,128)(2,1)S(1)}, bf16[64,2048]{1,0:T(8,128)(2,1)S(1)}, u32[]{:S(2)}, u32[]{:S(2)}) collective-permute-start(bf16[64,2048]{1,0:T(8,128)(2,1)S(1)} %collective-permute-done.14), channel_id=1, source_target_pairs={{0,2},{1,3},{2,6},{3,7},{4,0},{5,1},{6,10},{7,11},{8,4},{9,5},{10,... | collective-permute-start | bytes 786440 | tf_op jit(solution)/shard_map/ppermute | solution.py:266
  87.4 4.5 %copy-start.1 = (bf16[2048,1536]{1,0:T(8,128)(2,1)}, bf16[2048,1536]{1,0:T(8,128)(2,1)S(1)}, u32[]{:S(2)}) copy-start(bf16[2048,1536]{1,0:T(8,128)(2,1)S(1)} %pad_maximum_fusion) | copy-start | bytes 18874372
  87.4 7.6 %copy-start.3 = (bf16[768,2048]{1,0:T(8,128)(2,1)S(1)}, bf16[768,2048]{1,0:T(8,128)(2,1)}, u32[]{:S(2)}) copy-start(bf16[768,2048]{1,0:T(8,128)(2,1)} %pad_maximum_fusion.1) | copy-start | bytes 9437188
  100.9 6.0 %copy-start.12 = (bf16[64,2048]{1,0:T(8,128)(2,1)S(1)}, bf16[64,2048]{1,0:T(8,128)(2,1)}, u32[]{:S(2)}) copy-start(bf16[64,2048]{1,0:T(8,128)(2,1)} %copy-done.11) | copy-start | bytes 786436
  102.1 8.9 %collective-permute-start.21 = (bf16[64,2048]{1,0:T(8,128)(2,1)S(1)}, bf16[64,2048]{1,0:T(8,128)(2,1)S(1)}, u32[]{:S(2)}, u32[]{:S(2)}) collective-permute-start(bf16[64,2048]{1,0:T(8,128)(2,1)S(1)} %get-tuple-element.87), channel_id=1, source_target_pairs={{0,4},{1,5},{2,0},{3,1},{4,8},{5,9},{6,2},{7,3},{8,12},{9,13},{10,... | collective-permute-start | bytes 786440 | tf_op jit(solution)/shard_map/ppermute | solution.py:266
  103.8 9.9 %collective-permute-start.25 = (bf16[64,2048]{1,0:T(8,128)(2,1)S(1)}, bf16[64,2048]{1,0:T(8,128)(2,1)S(1)}, u32[]{:S(2)}, u32[]{:S(2)}) collective-permute-start(bf16[64,2048]{1,0:T(8,128)(2,1)S(1)} %get-tuple-element.86), channel_id=1, source_target_pairs={{0,2},{1,3},{2,6},{3,7},{4,0},{5,1},{6,10},{7,11},{8,4},{9,5},{10,... | collective-permute-start | bytes 786440 | tf_op jit(solution)/shard_map/ppermute | solution.py:266
  104.2 11.9 %collective-permute-start.23 = (bf16[64,2048]{1,0:T(8,128)(2,1)S(1)}, bf16[64,2048]{1,0:T(8,128)(2,1)S(1)}, u32[]{:S(2)}, u32[]{:S(2)}) collective-permute-start(bf16[64,2048]{1,0:T(8,128)(2,1)S(1)} %get-tuple-element.89), channel_id=1, source_target_pairs={{0,4},{1,5},{2,0},{3,1},{4,8},{5,9},{6,2},{7,3},{8,12},{9,13},{10,... | collective-permute-start | bytes 786440 | tf_op jit(solution)/shard_map/ppermute | solution.py:266
  106.9 12.4 %collective-permute-start.31 = (bf16[64,2048]{1,0:T(8,128)(2,1)S(1)}, bf16[64,2048]{1,0:T(8,128)(2,1)S(1)}, u32[]{:S(2)}, u32[]{:S(2)}) collective-permute-start(bf16[64,2048]{1,0:T(8,128)(2,1)S(1)} %get-tuple-element.88), channel_id=1, source_target_pairs={{0,2},{1,3},{2,6},{3,7},{4,0},{5,1},{6,10},{7,11},{8,4},{9,5},{10,... | collective-permute-start | bytes 786440 | tf_op jit(solution)/shard_map/ppermute | solution.py:266
  113.8 19.4 %collective-permute-start.22 = (bf16[64,2048]{1,0:T(8,128)(2,1)S(1)}, bf16[64,2048]{1,0:T(8,128)(2,1)S(1)}, u32[]{:S(2)}, u32[]{:S(2)}) collective-permute-start(bf16[64,2048]{1,0:T(8,128)(2,1)S(1)} %get-tuple-element.85), channel_id=1, source_target_pairs={{0,4},{1,5},{2,0},{3,1},{4,8},{5,9},{6,2},{7,3},{8,12},{9,13},{10,... | collective-permute-start | bytes 786440 | tf_op jit(solution)/shard_map/ppermute | solution.py:266
  116.1 17.1 %collective-permute-start.27 = (bf16[64,2048]{1,0:T(8,128)(2,1)S(1)}, bf16[64,2048]{1,0:T(8,128)(2,1)S(1)}, u32[]{:S(2)}, u32[]{:S(2)}) collective-permute-start(bf16[64,2048]{1,0:T(8,128)(2,1)S(1)} %get-tuple-element.84), channel_id=1, source_target_pairs={{0,2},{1,3},{2,6},{3,7},{4,0},{5,1},{6,10},{7,11},{8,4},{9,5},{10,... | collective-permute-start | bytes 786440 | tf_op jit(solution)/shard_map/ppermute | solution.py:266
  119.4 9.2 %collective-permute-start.24 = (bf16[64,2048]{1,0:T(8,128)(2,1)S(1)}, bf16[64,2048]{1,0:T(8,128)(2,1)S(1)}, u32[]{:S(2)}, u32[]{:S(2)}) collective-permute-start(bf16[64,2048]{1,0:T(8,128)(2,1)S(1)} %get-tuple-element.81), channel_id=1, source_target_pairs={{0,4},{1,5},{2,0},{3,1},{4,8},{5,9},{6,2},{7,3},{8,12},{9,13},{10,... | collective-permute-start | bytes 786440 | tf_op jit(solution)/shard_map/ppermute | solution.py:266
  121.7 9.2 %collective-permute-start.32 = (bf16[64,2048]{1,0:T(8,128)(2,1)S(1)}, bf16[64,2048]{1,0:T(8,128)(2,1)S(1)}, u32[]{:S(2)}, u32[]{:S(2)}) collective-permute-start(bf16[64,2048]{1,0:T(8,128)(2,1)S(1)} %get-tuple-element.80), channel_id=1, source_target_pairs={{0,2},{1,3},{2,6},{3,7},{4,0},{5,1},{6,10},{7,11},{8,4},{9,5},{10,... | collective-permute-start | bytes 786440 | tf_op jit(solution)/shard_map/ppermute | solution.py:266
  125.9 15.8 %copy-start.6 = (bf16[64,2048]{1,0:T(8,128)(2,1)S(1)}, bf16[64,2048]{1,0:T(8,128)(2,1)}, u32[]{:S(2)}) copy-start(bf16[64,2048]{1,0:T(8,128)(2,1)} %copy-done.5) | copy-start | bytes 786436
  131.0 6.5 %collective-permute-start.26 = (bf16[64,2048]{1,0:T(8,128)(2,1)S(1)}, bf16[64,2048]{1,0:T(8,128)(2,1)S(1)}, u32[]{:S(2)}, u32[]{:S(2)}) collective-permute-start(bf16[64,2048]{1,0:T(8,128)(2,1)S(1)} %get-tuple-element.79), channel_id=1, source_target_pairs={{0,4},{1,5},{2,0},{3,1},{4,8},{5,9},{6,2},{7,3},{8,12},{9,13},{10,... | collective-permute-start | bytes 786440 | tf_op jit(solution)/shard_map/ppermute | solution.py:266
  133.2 6.4 %collective-permute-start.33 = (bf16[64,2048]{1,0:T(8,128)(2,1)S(1)}, bf16[64,2048]{1,0:T(8,128)(2,1)S(1)}, u32[]{:S(2)}, u32[]{:S(2)}) collective-permute-start(bf16[64,2048]{1,0:T(8,128)(2,1)S(1)} %get-tuple-element.78), channel_id=1, source_target_pairs={{0,2},{1,3},{2,6},{3,7},{4,0},{5,1},{6,10},{7,11},{8,4},{9,5},{10,... | collective-permute-start | bytes 786440 | tf_op jit(solution)/shard_map/ppermute | solution.py:266
  133.3 9.5 %collective-permute-start.29 = (bf16[64,2048]{1,0:T(8,128)(2,1)S(1)}, bf16[64,2048]{1,0:T(8,128)(2,1)S(1)}, u32[]{:S(2)}, u32[]{:S(2)}) collective-permute-start(bf16[64,2048]{1,0:T(8,128)(2,1)S(1)} %get-tuple-element.83), channel_id=1, source_target_pairs={{0,4},{1,5},{2,0},{3,1},{4,8},{5,9},{6,2},{7,3},{8,12},{9,13},{10,... | collective-permute-start | bytes 786440 | tf_op jit(solution)/shard_map/ppermute | solution.py:266
  135.4 7.4 %collective-permute-start.30 = (bf16[64,2048]{1,0:T(8,128)(2,1)S(1)}, bf16[64,2048]{1,0:T(8,128)(2,1)S(1)}, u32[]{:S(2)}, u32[]{:S(2)}) collective-permute-start(bf16[64,2048]{1,0:T(8,128)(2,1)S(1)} %get-tuple-element.82), channel_id=1, source_target_pairs={{0,2},{1,3},{2,6},{3,7},{4,0},{5,1},{6,10},{7,11},{8,4},{9,5},{10,... | collective-permute-start | bytes 786440 | tf_op jit(solution)/shard_map/ppermute | solution.py:266
  139.6 6.4 %collective-permute-start.28 = (bf16[64,2048]{1,0:T(8,128)(2,1)S(1)}, bf16[64,2048]{1,0:T(8,128)(2,1)S(1)}, u32[]{:S(2)}, u32[]{:S(2)}) collective-permute-start(bf16[64,2048]{1,0:T(8,128)(2,1)S(1)} %get-tuple-element.77), channel_id=1, source_target_pairs={{0,4},{1,5},{2,0},{3,1},{4,8},{5,9},{6,2},{7,3},{8,12},{9,13},{10,... | collective-permute-start | bytes 786440 | tf_op jit(solution)/shard_map/ppermute | solution.py:266
  141.2 6.4 %collective-permute-start.34 = (bf16[64,2048]{1,0:T(8,128)(2,1)S(1)}, bf16[64,2048]{1,0:T(8,128)(2,1)S(1)}, u32[]{:S(2)}, u32[]{:S(2)}) collective-permute-start(bf16[64,2048]{1,0:T(8,128)(2,1)S(1)} %get-tuple-element.76), channel_id=1, source_target_pairs={{0,2},{1,3},{2,6},{3,7},{4,0},{5,1},{6,10},{7,11},{8,4},{9,5},{10,... | collective-permute-start | bytes 786440 | tf_op jit(solution)/shard_map/ppermute | solution.py:266
  (3 other events, 5.6 us)
Sparse Core Ops, SparseCore 0:
  43.1 41.2 all-gather.2

commit v14 on v12

--- a/solution.py
+++ b/solution.py
@@ -284,9 +284,8 @@
     gates = jnp.sum(
         jnp.where(route_ids[:, :, None] == jnp.arange(experts), route_weights[:, :, None], 0.0), axis=1
     )
-    gates = jnp.pad(gates, ((0, 0), (0, -experts % 128)))
-    gates = lax.all_gather(gates, axes, axis=0, tiled=False)
-    normed_top, normed_bottom = normed
+    normed_top, normed_bottom, other = lax.optimization_barrier((*normed, to_x(gates)))
+    gates = jnp.where(x == 0, jnp.stack([gates, other]), jnp.stack([other, gates]))[:, None]
 
     halves = range(2)
     size = frames // 2
@@ -323,17 +322,24 @@
     for k in range(1, far):
         fore_at[k] = [along(fore_at[k - 1][h], 1) for h in halves]
         back_at[k] = [along(back_at[k - 1][h], -1) for h in halves]
+        if k == far // 2:
+            fore_at[k][0], gates = lax.optimization_barrier((fore_at[k][0], gates))
     last = [along(fore_at[far - 1][0], 1), along(back_at[far - 1][1], -1)]
 
-    back_at[far - 1][0], gates = lax.optimization_barrier((back_at[far - 1][0], gates))
+    spread = [gates]
+    for away in range(1, wide):
+        spread.append(send(gates, lambda z, x, c: (z ^ away, x, c)))
+    gates, bit = jnp.concatenate(spread, axis=1), 1
+    while bit < wide:
+        turned = jnp.concatenate([gates[:, (i ^ bit) : (i ^ bit) + 1] for i in range(wide)], axis=1)
+        gates, bit = jnp.where(z & bit == 0, gates, turned), 2 * bit
 
     mine = (z * 2 + x) * 2 + core
-    lanes = jnp.arange(gates.shape[-1])
-    gates = lax.dynamic_slice_in_dim(gates.reshape(wide, 2, 2, frames, -1), core, 1, 2)[:, :, 0]
-    gates = jnp.stack(
-        [jnp.sum(jnp.where(lanes == e, gates, 0.0), axis=-1) for e in (mine, mine + 1 - 2 * core)], axis=-1
-    )
-    gates = jnp.concatenate([gates[:, 0], gates[::-1, 1]])
+    pair = jnp.stack([mine, mine + 1 - 2 * core])
+    gates = jnp.sum(
+        jnp.where(pair[:, None] == jnp.arange(experts), gates[..., None, :], 0.0), axis=-1
+    )
+    gates = jnp.concatenate([gates[0], gates[1, ::-1]])
     gates = lax.dynamic_slice_in_dim(jnp.concatenate([gates, gates]), place, ring, 0)
 
     joined_in = jnp.concatenate(

time: 176 us -> 131 us (0.74)
  waiting for transfers between devices: 72.2 us -> 53.6 us
  between operations: 14.5 us -> 1.02 us
  local copies, waits for them, and re-layouts: 10.6 us -> 0.77 us
  matrix products: 19.9 us -> 16.6 us
  starting transfers between devices: 40.1 us -> 42.2 us
    all_gather x1 -> x0, waiting for transfers between devices: 31.2 us -> none  [dense_experts(): gates = lax.all_gather(gates, axes, axis=0, tiled=False)]
    ppermute x35 -> x39, waiting for transfers between devices: 40.9 us -> 53.6 us  [send(): return lax.ppermute(value, axes, routes(wide, move))]
    unnamed x30 -> x8, local copies, waits for them, and re-layouts: 4.23 us -> 0.02 us
    dot_general x5, matrix products: 10.4 us -> 7.31 us  [run_experts(): jnp.dot(jnp.concatenate(parts), joined_in, preferred_element_type=jnp.flo...]
    ppermute x35 -> x39, starting transfers between devices: 40 us -> 42.2 us  [send(): return lax.ppermute(value, axes, routes(wide, move))]
    concatenate x1, other arithmetic: 3.97 us -> 1.92 us  [dense_experts(): joined_down = jnp.concatenate([expert_out, down_other], axis=0)]
    slice x1, local copies, waits for them, and re-layouts: 2.2 us -> 0.32 us  [dense_experts(): in_other[:, :hidden_width]]
    slice x1, local copies, waits for them, and re-layouts: 2.2 us -> 0.32 us  [dense_experts(): expert_in[:, :hidden_width]]
  transfers between devices with their start and end apart: 36 -> 39, of which waited for: 19 -> 21; matrix products, arithmetic and copies ran while one was open for 20% -> 17% of each run, Pallas kernels for 4% -> 5%
where the time goes in v14:
time: 131 us
  waiting for transfers between devices  53.6 us (41%)
  starting transfers between devices  42.2 us (32%)
  matrix products  16.6 us (13%)
  other arithmetic  9.59 us (7%)
  Pallas kernels  6.84 us (5%)
    ppermute x39, waiting for transfers between devices, send(): return lax.ppermute(value, axes, routes(wide, move))  53.6 us
    ppermute x39, starting transfers between devices, send(): return lax.ppermute(value, axes, routes(wide, move))  42.2 us
    dot_general x5, matrix products, run_experts(): jnp.dot(jnp.concatenate(parts), joined_in, preferred_element_type=jnp.flo...  7.31 us
    pallas_call x1, Pallas kernels, ssm_mixer(): pl.pallas_call(mixer_kernel, grid=(steps,), in_specs=[pl.BlockSpec(memory...  6.84 us
    dot_general x5, matrix products, run_experts(): return jnp.dot(hidden, joined_down, preferred_element_type=jnp.float32)  5.89 us
    select_n x1, other arithmetic, dense_experts(): jnp.where(core == 0, jnp.concatenate([out_proj, out_other], axis=1), jnp....  5.15 us
    dot_general x4, matrix products, project(): jnp.dot(rows, columns, preferred_element_type=jnp.float32)  3.39 us
  transfers between devices with their start and end apart: 39, of which 21 were waited for; matrix products, arithmetic and copies ran while one was open for 17% of the time, Pallas kernels for 5%

profile of v14, /device:TPU:0, one launch (start us, length us, event | category | flops | bytes accessed | tf_op | source)
XLA Modules:
  0.0 130.6 jit_solution(12556755172128586164)
XLA Ops:
  1.9 2.6 %collective-permute-start = (f32[128,16]{0,1:T(8,128)S(1)}, f32[128,16]{0,1:T(8,128)S(1)}, u32[]{:S(2)}, u32[]{:S(2)}) collective-permute-start(f32[128,16]{0,1:T(8,128)S(1)} %select_reduce_fusion.1), channel_id=1, source_target_pairs={{0,2},{1,3},{2,0},{3,1},{4,6},{5,7},{6,4},{7,5},{8,10},{9,11},{10,... | collective-permute-start | bytes 24584 | tf_op jit(solution)/shard_map/ppermute | solution.py:266
  5.1 6.8 %mixer.1 = (bf16[64,2048]{1,0:T(8,128)(2,1)}, bf16[64,2048]{1,0:T(8,128)(2,1)}, f32[2048,128]{1,0:T(8,128)}) custom-call(f32[32]{0:T(128)} %skip_ref.1, bf16[128,2048]{1,0:T(8,128)(2,1)} %x_ref.1, bf16[128,2048]{1,0:T(8,128)(2,1)} %z_ref.1, bf16[128,128]{1,0:T(8,128)(2,1)} %b_ref.1, bf16[128,128]{1,0:T(8,128)(2,1)} %c_ref.1, f32[32,128]{1,0:T(8,128)} %bitcast.77, ...), custom_call_target="tpu_custom_call" | custom-call | flops 400000000 | bytes 6000000 | tf_op jit(solution)/shard_map/mixer/pallas_call | solution.py:149
  12.2 5.1 %maximum_select_fusion = bf16[2048,1024]{1,0:T(8,128)(2,1)S(1)} fusion(bf16[2048,512]{1,0:T(8,128)(2,1)} %collective-permute-done.1, bf16[2048,512]{1,0:T(8,128)(2,1)} %param.25, pred[]{:T(512)S(6)} %eq.47), kind=kLoop, calls=%fused_computation.1 | loop fusion | flops 18874368 | bytes 8388609 | tf_op jit(solution)/shard_map/jit(_where)/select_n | solution.py:294
  17.3 3.3 %collective-permute-done.2 = bf16[64,2048]{1,0:T(8,128)(2,1)S(1)} collective-permute-done((bf16[64,2048]{1,0:T(8,128)(2,1)}, bf16[64,2048]{1,0:T(8,128)(2,1)S(1)}, u32[]{:S(2)}, u32[]{:S(2)}) %collective-permute-start.2) | collective-permute-done | bytes 262176 | tf_op jit(solution)/shard_map/ppermute | solution.py:266
  21.9 1.7 %collective-permute-start.4 = (bf16[64,2048]{1,0:T(8,128)(2,1)S(1)}, bf16[64,2048]{1,0:T(8,128)(2,1)S(1)}, u32[]{:S(2)}, u32[]{:S(2)}) collective-permute-start(bf16[64,2048]{1,0:T(8,128)(2,1)S(1)} %copy-done.2), channel_id=1, source_target_pairs={{0,2},{1,3},{2,0},{3,1},{4,6},{5,7},{6,4},{7,5},{8,10},{9,11},{10,... | collective-permute-start | bytes 786440 | tf_op jit(solution)/shard_map/ppermute | solution.py:266
  23.6 0.9 convolution_convert_fusion.4
  24.5 3.5 %collective-permute-done.3 = bf16[64,1024]{1,0:T(8,128)(2,1)S(1)} collective-permute-done((bf16[64,1024]{1,0:T(8,128)(2,1)S(1)}, bf16[64,1024]{1,0:T(8,128)(2,1)S(1)}, u32[]{:S(2)}, u32[]{:S(2)}) %collective-permute-start.3) | collective-permute-done | bytes 131104 | tf_op jit(solution)/shard_map/ppermute | solution.py:266
  28.1 1.6 %collective-permute-start.9 = (bf16[64,2048]{1,0:T(8,128)(2,1)S(1)}, bf16[64,2048]{1,0:T(8,128)(2,1)S(1)}, u32[]{:S(2)}, u32[]{:S(2)}) collective-permute-start(bf16[64,2048]{1,0:T(8,128)(2,1)S(1)} %maximum_select_fusion.1), channel_id=1, source_target_pairs={{0,4},{1,5},{2,0},{3,1},{4,8},{5,9},{6,2},{7,3},{8,12},{9,13},{10,... | collective-permute-start | bytes 786440 | tf_op jit(solution)/shard_map/ppermute | solution.py:266
  30.2 3.5 %collective-permute-done.4 = bf16[64,2048]{1,0:T(8,128)(2,1)S(1)} collective-permute-done((bf16[64,2048]{1,0:T(8,128)(2,1)S(1)}, bf16[64,2048]{1,0:T(8,128)(2,1)S(1)}, u32[]{:S(2)}, u32[]{:S(2)}) %collective-permute-start.4) | collective-permute-done | bytes 262176 | tf_op jit(solution)/shard_map/ppermute | solution.py:266
  35.7 4.6 %collective-permute-done.5 = bf16[64,1024]{1,0:T(8,128)(2,1)S(1)} collective-permute-done((bf16[64,1024]{1,0:T(8,128)(2,1)S(1)}, bf16[64,1024]{1,0:T(8,128)(2,1)S(1)}, u32[]{:S(2)}, u32[]{:S(2)}) %collective-permute-start.5) | collective-permute-done | bytes 131104 | tf_op jit(solution)/shard_map/ppermute | solution.py:266
  41.2 1.4 %collective-permute-start.10 = (bf16[64,2048]{1,0:T(8,128)(2,1)S(1)}, bf16[64,2048]{1,0:T(8,128)(2,1)S(1)}, u32[]{:S(2)}, u32[]{:S(2)}) collective-permute-start(bf16[64,2048]{1,0:T(8,128)(2,1)S(1)} %collective-permute-done.9), channel_id=1, source_target_pairs={{0,4},{1,5},{2,0},{3,1},{4,8},{5,9},{6,2},{7,3},{8,12},{9,13},{10,... | collective-permute-start | bytes 786440 | tf_op jit(solution)/shard_map/ppermute | solution.py:266
  43.5 4.3 %collective-permute-done.10 = bf16[64,2048]{1,0:T(8,128)(2,1)S(1)} collective-permute-done((bf16[64,2048]{1,0:T(8,128)(2,1)S(1)}, bf16[64,2048]{1,0:T(8,128)(2,1)S(1)}, u32[]{:S(2)}, u32[]{:S(2)}) %collective-permute-start.10) | collective-permute-done | bytes 262176 | tf_op jit(solution)/shard_map/ppermute | solution.py:266
  47.9 1.2 collective-permute-start.22
  49.8 3.4 %collective-permute-start.20 = (f32[2,1,128,16]{2,3,1,0:T(8,128)S(1)}, f32[2,1,128,16]{2,3,1,0:T(8,128)S(1)}, u32[]{:S(2)}, u32[]{:S(2)}) collective-permute-start(f32[2,1,128,16]{2,3,1,0:T(8,128)S(1)} %maximum_select_fusion.5), channel_id=1, source_target_pairs={{0,8},{1,9},{2,10},{3,11},{4,12},{5,13},{6,14},{7,15},{8,0},{9,1},... | collective-permute-start | bytes 49160 | tf_op jit(solution)/shard_map/ppermute | solution.py:266
  53.2 3.3 %collective-permute-start.21 = (f32[2,1,128,16]{2,3,1,0:T(8,128)S(1)}, f32[2,1,128,16]{2,3,1,0:T(8,128)S(1)}, u32[]{:S(2)}, u32[]{:S(2)}) collective-permute-start(f32[2,1,128,16]{2,3,1,0:T(8,128)S(1)} %maximum_select_fusion.5), channel_id=1, source_target_pairs={{0,12},{1,13},{2,14},{3,15},{4,8},{5,9},{6,10},{7,11},{8,4},{9,5},... | collective-permute-start | bytes 49160 | tf_op jit(solution)/shard_map/ppermute | solution.py:266
  56.5 1.9 %pad_maximum_fusion.1 = bf16[768,2048]{1,0:T(8,128)(2,1)S(1)} fusion(bf16[384,2048]{1,0:T(8,128)(2,1)} %collective-permute-done.18, bf16[384,2048]{1,0:T(8,128)(2,1)S(1)} %bitcast.67), kind=kLoop, calls=%fused_computation.2 | loop fusion | flops 6291456 | bytes 6291456 | tf_op jit(solution)/shard_map/concatenate | solution.py:354
  58.5 2.0 %collective-permute-start.14 = (bf16[64,2048]{1,0:T(8,128)(2,1)S(1)}, bf16[64,2048]{1,0:T(8,128)(2,1)S(1)}, u32[]{:S(2)}, u32[]{:S(2)}) collective-permute-start(bf16[64,2048]{1,0:T(8,128)(2,1)S(1)} %collective-permute-done.13), channel_id=1, source_target_pairs={{0,2},{1,3},{2,6},{3,7},{4,0},{5,1},{6,10},{7,11},{8,4},{9,5},{10,... | collective-permute-start | bytes 786440 | tf_op jit(solution)/shard_map/ppermute | solution.py:266
  60.5 0.9 collective-permute-start.8
  61.4 1.2 collective-permute-start.23
  62.8 4.9 %collective-permute-done.11 = bf16[64,2048]{1,0:T(8,128)(2,1)S(1)} collective-permute-done((bf16[64,2048]{1,0:T(8,128)(2,1)S(1)}, bf16[64,2048]{1,0:T(8,128)(2,1)S(1)}, u32[]{:S(2)}, u32[]{:S(2)}) %collective-permute-start.11) | collective-permute-done | bytes 262176 | tf_op jit(solution)/shard_map/ppermute | solution.py:266
  67.8 2.0 %collective-permute-start.15 = (bf16[64,2048]{1,0:T(8,128)(2,1)S(1)}, bf16[64,2048]{1,0:T(8,128)(2,1)S(1)}, u32[]{:S(2)}, u32[]{:S(2)}) collective-permute-start(bf16[64,2048]{1,0:T(8,128)(2,1)S(1)} %collective-permute-done.14), channel_id=1, source_target_pairs={{0,2},{1,3},{2,6},{3,7},{4,0},{5,1},{6,10},{7,11},{8,4},{9,5},{10,... | collective-permute-start | bytes 786440 | tf_op jit(solution)/shard_map/ppermute | solution.py:266
  69.7 3.6 %collective-permute-done.23 = bf16[64,2048]{1,0:T(8,128)(2,1)S(1)} collective-permute-done((bf16[64,2048]{1,0:T(8,128)(2,1)S(1)}, bf16[64,2048]{1,0:T(8,128)(2,1)S(1)}, u32[]{:S(2)}, u32[]{:S(2)}) %collective-permute-start.23) | collective-permute-done | bytes 262176 | tf_op jit(solution)/shard_map/ppermute | solution.py:266
  73.6 2.6 %collective-permute-done.15 = bf16[64,2048]{1,0:T(8,128)(2,1)S(1)} collective-permute-done((bf16[64,2048]{1,0:T(8,128)(2,1)S(1)}, bf16[64,2048]{1,0:T(8,128)(2,1)S(1)}, u32[]{:S(2)}, u32[]{:S(2)}) %collective-permute-start.15) | collective-permute-done | bytes 262176 | tf_op jit(solution)/shard_map/ppermute | solution.py:266
  76.2 2.0 %collective-permute-start.16 = (bf16[64,2048]{1,0:T(8,128)(2,1)S(1)}, bf16[64,2048]{1,0:T(8,128)(2,1)S(1)}, u32[]{:S(2)}, u32[]{:S(2)}) collective-permute-start(bf16[64,2048]{1,0:T(8,128)(2,1)S(1)} %collective-permute-done.15), channel_id=1, source_target_pairs={{0,2},{1,3},{2,6},{3,7},{4,0},{5,1},{6,10},{7,11},{8,4},{9,5},{10,... | collective-permute-start | bytes 786440 | tf_op jit(solution)/shard_map/ppermute | solution.py:266
  78.9 3.7 %collective-permute-done.16 = bf16[64,2048]{1,0:T(8,128)(2,1)S(1)} collective-permute-done((bf16[64,2048]{1,0:T(8,128)(2,1)S(1)}, bf16[64,2048]{1,0:T(8,128)(2,1)S(1)}, u32[]{:S(2)}, u32[]{:S(2)}) %collective-permute-start.16) | collective-permute-done | bytes 262176 | tf_op jit(solution)/shard_map/ppermute | solution.py:266
  82.6 1.0 fusion.40
  84.3 1.8 %fusion = f32[256,1536]{1,0:T(8,128)S(1)} fusion(bf16[2048,1536]{1,0:T(8,128)(2,1)S(1)} %pad_maximum_fusion, bf16[64,2048]{1,0:T(8,128)(2,1)S(1)} %collective-permute-done.24, bf16[64,2048]{1,0:T(8,128)(2,1)S(1)} %collective-permute-done.11, bf16[64,2048]{1,0:T(8,128)(2,1)S(1)} %collective-permute-done.15, bf16[64,2048]{1,0:T(8,128)(2,1)S(1)} %collective-permute-done.8), kind=kOutput, calls=%fused_computation.8 | convolution fusion | flops 1614807040 | bytes 8912896 | tf_op jit(solution)/shard_map/dot_general | solution.py:359
  86.1 1.2 fusion.105
  87.6 2.1 %collective-permute-start.29 = (bf16[64,2048]{1,0:T(8,128)(2,1)S(1)}, bf16[64,2048]{1,0:T(8,128)(2,1)S(1)}, u32[]{:S(2)}, u32[]{:S(2)}) collective-permute-start(bf16[64,2048]{1,0:T(8,128)(2,1)S(1)} %get-tuple-element.86), channel_id=1, source_target_pairs={{0,2},{1,3},{2,6},{3,7},{4,0},{5,1},{6,10},{7,11},{8,4},{9,5},{10,... | collective-permute-start | bytes 786440 | tf_op jit(solution)/shard_map/ppermute | solution.py:266
  89.7 2.0 %collective-permute-start.35 = (bf16[64,2048]{1,0:T(8,128)(2,1)S(1)}, bf16[64,2048]{1,0:T(8,128)(2,1)S(1)}, u32[]{:S(2)}, u32[]{:S(2)}) collective-permute-start(bf16[64,2048]{1,0:T(8,128)(2,1)S(1)} %get-tuple-element.88), channel_id=1, source_target_pairs={{0,2},{1,3},{2,6},{3,7},{4,0},{5,1},{6,10},{7,11},{8,4},{9,5},{10,... | collective-permute-start | bytes 786440 | tf_op jit(solution)/shard_map/ppermute | solution.py:266
  91.7 1.8 %fusion.8 = f32[256,1536]{1,0:T(8,128)S(1)} fusion(bf16[2048,1536]{1,0:T(8,128)(2,1)S(1)} %pad_maximum_fusion, bf16[64,2048]{1,0:T(8,128)(2,1)S(1)} %collective-permute-done.23, bf16[64,2048]{1,0:T(8,128)(2,1)S(1)} %collective-permute-done.10, bf16[64,2048]{1,0:T(8,128)(2,1)S(1)} %collective-permute-done.14, bf16[64,2048]{1,0:T(8,128)(2,1)S(1)} %collective-permute-done.7), kind=kOutput, calls=%fused_computation.16 | convolution fusion | flops 1614807040 | bytes 8912896 | tf_op jit(solution)/shard_map/dot_general | solution.py:359
  93.5 1.2 fusion.50
  94.7 1.9 %collective-permute-done.25 = bf16[64,2048]{1,0:T(8,128)(2,1)S(1)} collective-permute-done((bf16[64,2048]{1,0:T(8,128)(2,1)S(1)}, bf16[64,2048]{1,0:T(8,128)(2,1)S(1)}, u32[]{:S(2)}, u32[]{:S(2)}) %collective-permute-start.25) | collective-permute-done | bytes 262176 | tf_op jit(solution)/shard_map/ppermute | solution.py:266
  96.9 1.8 %collective-permute-start.26 = (bf16[64,2048]{1,0:T(8,128)(2,1)S(1)}, bf16[64,2048]{1,0:T(8,128)(2,1)S(1)}, u32[]{:S(2)}, u32[]{:S(2)}) collective-permute-start(bf16[64,2048]{1,0:T(8,128)(2,1)S(1)} %get-tuple-element.85), channel_id=1, source_target_pairs={{0,4},{1,5},{2,0},{3,1},{4,8},{5,9},{6,2},{7,3},{8,12},{9,13},{10,... | collective-permute-start | bytes 786440 | tf_op jit(solution)/shard_map/ppermute | solution.py:266
  99.0 3.3 %collective-permute-done.27 = bf16[64,2048]{1,0:T(8,128)(2,1)S(1)} collective-permute-done((bf16[64,2048]{1,0:T(8,128)(2,1)S(1)}, bf16[64,2048]{1,0:T(8,128)(2,1)S(1)}, u32[]{:S(2)}, u32[]{:S(2)}) %collective-permute-start.27) | collective-permute-done | bytes 262176 | tf_op jit(solution)/shard_map/ppermute | solution.py:266
  102.5 1.8 %collective-permute-start.28 = (bf16[64,2048]{1,0:T(8,128)(2,1)S(1)}, bf16[64,2048]{1,0:T(8,128)(2,1)S(1)}, u32[]{:S(2)}, u32[]{:S(2)}) collective-permute-start(bf16[64,2048]{1,0:T(8,128)(2,1)S(1)} %get-tuple-element.81), channel_id=1, source_target_pairs={{0,4},{1,5},{2,0},{3,1},{4,8},{5,9},{6,2},{7,3},{8,12},{9,13},{10,... | collective-permute-start | bytes 786440 | tf_op jit(solution)/shard_map/ppermute | solution.py:266
  104.6 1.8 %fusion.16 = f32[256,1536]{1,0:T(8,128)S(1)} fusion(bf16[2048,1536]{1,0:T(8,128)(2,1)S(1)} %pad_maximum_fusion, bf16[64,2048]{1,0:T(8,128)(2,1)S(1)} %collective-permute-done.22, bf16[64,2048]{1,0:T(8,128)(2,1)S(1)} %collective-permute-done.9, bf16[64,2048]{1,0:T(8,128)(2,1)S(1)} %collective-permute-done.13, bf16[64,2048]{1,0:T(8,128)(2,1)S(1)} %collective-permute-done.6), kind=kOutput, calls=%fused_computation.24 | convolution fusion | flops 1614807040 | bytes 8912896 | tf_op jit(solution)/shard_map/dot_general | solution.py:359
  106.4 1.2 fusion.52
  107.6 4.1 %collective-permute-done.28 = bf16[64,2048]{1,0:T(8,128)(2,1)S(1)} collective-permute-done((bf16[64,2048]{1,0:T(8,128)(2,1)S(1)}, bf16[64,2048]{1,0:T(8,128)(2,1)S(1)}, u32[]{:S(2)}, u32[]{:S(2)}) %collective-permute-start.28) | collective-permute-done | bytes 262176 | tf_op jit(solution)/shard_map/ppermute | solution.py:266
  111.6 1.8 %collective-permute-done.36 = bf16[64,2048]{1,0:T(8,128)(2,1)S(1)} collective-permute-done((bf16[64,2048]{1,0:T(8,128)(2,1)S(1)}, bf16[64,2048]{1,0:T(8,128)(2,1)S(1)}, u32[]{:S(2)}, u32[]{:S(2)}) %collective-permute-start.36) | collective-permute-done | bytes 262176 | tf_op jit(solution)/shard_map/ppermute | solution.py:266
  113.9 1.8 %collective-permute-start.37 = (bf16[64,2048]{1,0:T(8,128)(2,1)S(1)}, bf16[64,2048]{1,0:T(8,128)(2,1)S(1)}, u32[]{:S(2)}, u32[]{:S(2)}) collective-permute-start(bf16[64,2048]{1,0:T(8,128)(2,1)S(1)} %get-tuple-element.78), channel_id=1, source_target_pairs={{0,2},{1,3},{2,6},{3,7},{4,0},{5,1},{6,10},{7,11},{8,4},{9,5},{10,... | collective-permute-start | bytes 786440 | tf_op jit(solution)/shard_map/ppermute | solution.py:266
  116.1 1.8 %collective-permute-start.34 = (bf16[64,2048]{1,0:T(8,128)(2,1)S(1)}, bf16[64,2048]{1,0:T(8,128)(2,1)S(1)}, u32[]{:S(2)}, u32[]{:S(2)}) collective-permute-start(bf16[64,2048]{1,0:T(8,128)(2,1)S(1)} %get-tuple-element.82), channel_id=1, source_target_pairs={{0,2},{1,3},{2,6},{3,7},{4,0},{5,1},{6,10},{7,11},{8,4},{9,5},{10,... | collective-permute-start | bytes 786440 | tf_op jit(solution)/shard_map/ppermute | solution.py:266
  117.9 2.4 %collective-permute-done.30 = bf16[64,2048]{1,0:T(8,128)(2,1)S(1)} collective-permute-done((bf16[64,2048]{1,0:T(8,128)(2,1)S(1)}, bf16[64,2048]{1,0:T(8,128)(2,1)S(1)}, u32[]{:S(2)}, u32[]{:S(2)}) %collective-permute-start.30) | collective-permute-done | bytes 262176 | tf_op jit(solution)/shard_map/ppermute | solution.py:266
  121.0 1.6 %collective-permute-start.32 = (bf16[64,2048]{1,0:T(8,128)(2,1)S(1)}, bf16[64,2048]{1,0:T(8,128)(2,1)S(1)}, u32[]{:S(2)}, u32[]{:S(2)}) collective-permute-start(bf16[64,2048]{1,0:T(8,128)(2,1)S(1)} %get-tuple-element.77), channel_id=1, source_target_pairs={{0,4},{1,5},{2,0},{3,1},{4,8},{5,9},{6,2},{7,3},{8,12},{9,13},{10,... | collective-permute-start | bytes 786440 | tf_op jit(solution)/shard_map/ppermute | solution.py:266
  123.0 1.0 fusion.44
  124.1 3.3 %collective-permute-done.32 = bf16[64,2048]{1,0:T(8,128)(2,1)S(1)} collective-permute-done((bf16[64,2048]{1,0:T(8,128)(2,1)S(1)}, bf16[64,2048]{1,0:T(8,128)(2,1)S(1)}, u32[]{:S(2)}, u32[]{:S(2)}) %collective-permute-start.32) | collective-permute-done | bytes 262176 | tf_op jit(solution)/shard_map/ppermute | solution.py:266
  127.4 1.5 %collective-permute-done.38 = bf16[64,2048]{1,0:T(8,128)(2,1)S(1)} collective-permute-done((bf16[64,2048]{1,0:T(8,128)(2,1)S(1)}, bf16[64,2048]{1,0:T(8,128)(2,1)S(1)}, u32[]{:S(2)}, u32[]{:S(2)}) %collective-permute-start.38) | collective-permute-done | bytes 262176 | tf_op jit(solution)/shard_map/ppermute | solution.py:266
  128.9 1.7 %add_convert_fusion = bf16[128,2048]{1,0:T(8,128)(2,1)} fusion(bf16[64,2048]{1,0:T(8,128)(2,1)S(1)} %maximum_select_fusion.2, bf16[64,2048]{1,0:T(8,128)(2,1)S(1)} %maximum_select_fusion.1, bf16[64,2048]{1,0:T(8,128)(2,1)S(1)} %collective-permute-done.33, bf16[64,2048]{1,0:T(8,128)(2,1)S(1)} %collective-permute-done.32, ...), kind=kOutput, calls=%fused_computation.32 | convolution fusion | flops 407633920 | bytes 6031104 | tf_op jit(solution)/shard_map/dot_general | solution.py:362
  (84 shorter events, 14.2 us)
Async XLA Ops:
  0.6 11.5 %collective-permute-start.1 = (bf16[2048,512]{1,0:T(8,128)(2,1)}, bf16[2048,512]{1,0:T(8,128)(2,1)}, u32[]{:S(2)}, u32[]{:S(2)}) collective-permute-start(bf16[2048,512]{1,0:T(8,128)(2,1)} %param.25), channel_id=1, source_target_pairs={{0,1},{1,0},{2,3},{3,2},{4,5},{5,4},{6,7},{7,6},{8,9},{9,8},{10,11... | collective-permute-start | bytes 6291464 | tf_op jit(solution)/shard_map/ppermute | solution.py:266
  1.9 10.1 %collective-permute-start = (f32[128,16]{0,1:T(8,128)S(1)}, f32[128,16]{0,1:T(8,128)S(1)}, u32[]{:S(2)}, u32[]{:S(2)}) collective-permute-start(f32[128,16]{0,1:T(8,128)S(1)} %select_reduce_fusion.1), channel_id=1, source_target_pairs={{0,2},{1,3},{2,0},{3,1},{4,6},{5,7},{6,4},{7,5},{8,10},{9,11},{10,... | collective-permute-start | bytes 24584 | tf_op jit(solution)/shard_map/ppermute | solution.py:266
  4.4 68.9 %collective-permute-start.17 = (bf16[2048,768]{1,0:T(8,128)(2,1)}, bf16[2048,768]{1,0:T(8,128)(2,1)S(1)}, u32[]{:S(2)}, u32[]{:S(2)}) collective-permute-start(bf16[2048,768]{1,0:T(8,128)(2,1)} %bitcast.64), channel_id=1, source_target_pairs={{0,1},{1,0},{2,3},{3,2},{4,5},{5,4},{6,7},{7,6},{8,9},{9,8},{10,11... | collective-permute-start | bytes 9437192 | tf_op jit(solution)/shard_map/ppermute | solution.py:266
  4.6 44.4 %collective-permute-start.18 = (bf16[384,2048]{1,0:T(8,128)(2,1)}, bf16[384,2048]{1,0:T(8,128)(2,1)}, u32[]{:S(2)}, u32[]{:S(2)}) collective-permute-start(bf16[384,2048]{1,0:T(8,128)(2,1)} %bitcast.66), channel_id=1, source_target_pairs={{0,1},{1,0},{2,3},{3,2},{4,5},{5,4},{6,7},{7,6},{8,9},{9,8},{10,11... | collective-permute-start | bytes 4718600 | tf_op jit(solution)/shard_map/ppermute | solution.py:266
  11.9 8.7 %collective-permute-start.2 = (bf16[64,2048]{1,0:T(8,128)(2,1)}, bf16[64,2048]{1,0:T(8,128)(2,1)S(1)}, u32[]{:S(2)}, u32[]{:S(2)}) collective-permute-start(bf16[64,2048]{1,0:T(8,128)(2,1)} %get-tuple-element.39), channel_id=1, source_target_pairs={{0,2},{1,3},{2,0},{3,1},{4,6},{5,7},{6,4},{7,5},{8,10},{9,11},{10,... | collective-permute-start | bytes 786440 | tf_op jit(solution)/shard_map/ppermute | solution.py:266
  17.3 4.6 %copy-start.2 = (bf16[64,2048]{1,0:T(8,128)(2,1)S(1)}, bf16[64,2048]{1,0:T(8,128)(2,1)}, u32[]{:S(2)}) copy-start(bf16[64,2048]{1,0:T(8,128)(2,1)} %get-tuple-element.42) | copy-start | bytes 786436
  17.3 6.3 %copy-start.3 = (bf16[64,2048]{1,0:T(8,128)(2,1)S(1)}, bf16[64,2048]{1,0:T(8,128)(2,1)}, u32[]{:S(2)}) copy-start(bf16[64,2048]{1,0:T(8,128)(2,1)} %get-tuple-element.39) | copy-start | bytes 786436
  21.5 6.5 %collective-permute-start.3 = (bf16[64,1024]{1,0:T(8,128)(2,1)S(1)}, bf16[64,1024]{1,0:T(8,128)(2,1)S(1)}, u32[]{:S(2)}, u32[]{:S(2)}) collective-permute-start(bf16[64,1024]{1,0:T(8,128)(2,1)S(1)} %convolution_convert_fusion.3), channel_id=1, source_target_pairs={{0,2},{1,3},{2,0},{3,1},{4,6},{5,7},{6,4},{7,5},{8,10},{9,11},{10,... | collective-permute-start | bytes 393224 | tf_op jit(solution)/shard_map/ppermute | solution.py:266
  21.9 11.7 %collective-permute-start.4 = (bf16[64,2048]{1,0:T(8,128)(2,1)S(1)}, bf16[64,2048]{1,0:T(8,128)(2,1)S(1)}, u32[]{:S(2)}, u32[]{:S(2)}) collective-permute-start(bf16[64,2048]{1,0:T(8,128)(2,1)S(1)} %copy-done.2), channel_id=1, source_target_pairs={{0,2},{1,3},{2,0},{3,1},{4,6},{5,7},{6,4},{7,5},{8,10},{9,11},{10,... | collective-permute-start | bytes 786440 | tf_op jit(solution)/shard_map/ppermute | solution.py:266
  28.1 13.1 %collective-permute-start.9 = (bf16[64,2048]{1,0:T(8,128)(2,1)S(1)}, bf16[64,2048]{1,0:T(8,128)(2,1)S(1)}, u32[]{:S(2)}, u32[]{:S(2)}) collective-permute-start(bf16[64,2048]{1,0:T(8,128)(2,1)S(1)} %maximum_select_fusion.1), channel_id=1, source_target_pairs={{0,4},{1,5},{2,0},{3,1},{4,8},{5,9},{6,2},{7,3},{8,12},{9,13},{10,... | collective-permute-start | bytes 786440 | tf_op jit(solution)/shard_map/ppermute | solution.py:266
  29.7 12.9 %collective-permute-start.6 = (bf16[64,2048]{1,0:T(8,128)(2,1)S(1)}, bf16[64,2048]{1,0:T(8,128)(2,1)S(1)}, u32[]{:S(2)}, u32[]{:S(2)}) collective-permute-start(bf16[64,2048]{1,0:T(8,128)(2,1)S(1)} %maximum_select_fusion.1), channel_id=1, source_target_pairs={{0,2},{1,3},{2,6},{3,7},{4,0},{5,1},{6,10},{7,11},{8,4},{9,5},{10,... | collective-permute-start | bytes 786440 | tf_op jit(solution)/shard_map/ppermute | solution.py:266
  34.5 8.7 %copy-start = (bf16[1,2048,768]{2,1,0:T(8,128)(2,1)S(1)}, bf16[1,2048,768]{2,1,0:T(8,128)(2,1)}, u32[]{:S(2)}) copy-start(bf16[1,2048,768]{2,1,0:T(8,128)(2,1)} %param.26) | copy-start | bytes 9437188
  34.5 5.9 %collective-permute-start.5 = (bf16[64,1024]{1,0:T(8,128)(2,1)S(1)}, bf16[64,1024]{1,0:T(8,128)(2,1)S(1)}, u32[]{:S(2)}, u32[]{:S(2)}) collective-permute-start(bf16[64,1024]{1,0:T(8,128)(2,1)S(1)} %convolution_convert_fusion.1), channel_id=1, source_target_pairs={{0,2},{1,3},{2,0},{3,1},{4,6},{5,7},{6,4},{7,5},{8,10},{9,11},{10,... | collective-permute-start | bytes 393224 | tf_op jit(solution)/shard_map/ppermute | solution.py:266
  40.5 16.0 %copy-start.1 = (bf16[1,384,2048]{2,1,0:T(8,128)(2,1)S(1)}, bf16[1,384,2048]{2,1,0:T(8,128)(2,1)}, u32[]{:S(2)}) copy-start(bf16[1,384,2048]{2,1,0:T(8,128)(2,1)} %param.27) | copy-start | bytes 4718596
  40.5 9.3 %collective-permute-start.13 = (bf16[64,2048]{1,0:T(8,128)(2,1)S(1)}, bf16[64,2048]{1,0:T(8,128)(2,1)S(1)}, u32[]{:S(2)}, u32[]{:S(2)}) collective-permute-start(bf16[64,2048]{1,0:T(8,128)(2,1)S(1)} %maximum_select_fusion.2), channel_id=1, source_target_pairs={{0,2},{1,3},{2,6},{3,7},{4,0},{5,1},{6,10},{7,11},{8,4},{9,5},{10,... | collective-permute-start | bytes 786440 | tf_op jit(solution)/shard_map/ppermute | solution.py:266
  41.2 6.7 %collective-permute-start.10 = (bf16[64,2048]{1,0:T(8,128)(2,1)S(1)}, bf16[64,2048]{1,0:T(8,128)(2,1)S(1)}, u32[]{:S(2)}, u32[]{:S(2)}) collective-permute-start(bf16[64,2048]{1,0:T(8,128)(2,1)S(1)} %collective-permute-done.9), channel_id=1, source_target_pairs={{0,4},{1,5},{2,0},{3,1},{4,8},{5,9},{6,2},{7,3},{8,12},{9,13},{10,... | collective-permute-start | bytes 786440 | tf_op jit(solution)/shard_map/ppermute | solution.py:266
  42.6 10.6 %collective-permute-start.7 = (bf16[64,2048]{1,0:T(8,128)(2,1)S(1)}, bf16[64,2048]{1,0:T(8,128)(2,1)S(1)}, u32[]{:S(2)}, u32[]{:S(2)}) collective-permute-start(bf16[64,2048]{1,0:T(8,128)(2,1)S(1)} %collective-permute-done.6), channel_id=1, source_target_pairs={{0,2},{1,3},{2,6},{3,7},{4,0},{5,1},{6,10},{7,11},{8,4},{9,5},{10,... | collective-permute-start | bytes 786440 | tf_op jit(solution)/shard_map/ppermute | solution.py:266
  47.9 10.5 %collective-permute-start.22 = (bf16[64,2048]{1,0:T(8,128)(2,1)S(1)}, bf16[64,2048]{1,0:T(8,128)(2,1)S(1)}, u32[]{:S(2)}, u32[]{:S(2)}) collective-permute-start(bf16[64,2048]{1,0:T(8,128)(2,1)S(1)} %maximum_select_fusion.2), channel_id=1, source_target_pairs={{0,4},{1,5},{2,0},{3,1},{4,8},{5,9},{6,2},{7,3},{8,12},{9,13},{10,... | collective-permute-start | bytes 786440 | tf_op jit(solution)/shard_map/ppermute | solution.py:266
  49.0 9.5 %collective-permute-start.19 = (f32[2,1,128,16]{2,3,1,0:T(8,128)S(1)}, f32[2,1,128,16]{2,3,1,0:T(8,128)S(1)}, u32[]{:S(2)}, u32[]{:S(2)}) collective-permute-start(f32[2,1,128,16]{2,3,1,0:T(8,128)S(1)} %maximum_select_fusion.5), channel_id=1, source_target_pairs={{0,4},{1,5},{2,6},{3,7},{4,0},{5,1},{6,2},{7,3},{8,12},{9,13},{10,... | collective-permute-start | bytes 49160 | tf_op jit(solution)/shard_map/ppermute | solution.py:266
  49.8 10.7 %collective-permute-start.20 = (f32[2,1,128,16]{2,3,1,0:T(8,128)S(1)}, f32[2,1,128,16]{2,3,1,0:T(8,128)S(1)}, u32[]{:S(2)}, u32[]{:S(2)}) collective-permute-start(f32[2,1,128,16]{2,3,1,0:T(8,128)S(1)} %maximum_select_fusion.5), channel_id=1, source_target_pairs={{0,8},{1,9},{2,10},{3,11},{4,12},{5,13},{6,14},{7,15},{8,0},{9,1},... | collective-permute-start | bytes 49160 | tf_op jit(solution)/shard_map/ppermute | solution.py:266
  53.2 8.2 %collective-permute-start.21 = (f32[2,1,128,16]{2,3,1,0:T(8,128)S(1)}, f32[2,1,128,16]{2,3,1,0:T(8,128)S(1)}, u32[]{:S(2)}, u32[]{:S(2)}) collective-permute-start(f32[2,1,128,16]{2,3,1,0:T(8,128)S(1)} %maximum_select_fusion.5), channel_id=1, source_target_pairs={{0,12},{1,13},{2,14},{3,15},{4,8},{5,9},{6,10},{7,11},{8,4},{9,5},... | collective-permute-start | bytes 49160 | tf_op jit(solution)/shard_map/ppermute | solution.py:266
  58.4 9.3 %collective-permute-start.11 = (bf16[64,2048]{1,0:T(8,128)(2,1)S(1)}, bf16[64,2048]{1,0:T(8,128)(2,1)S(1)}, u32[]{:S(2)}, u32[]{:S(2)}) collective-permute-start(bf16[64,2048]{1,0:T(8,128)(2,1)S(1)} %collective-permute-done.10), channel_id=1, source_target_pairs={{0,4},{1,5},{2,0},{3,1},{4,8},{5,9},{6,2},{7,3},{8,12},{9,13},{10,... | collective-permute-start | bytes 786440 | tf_op jit(solution)/shard_map/ppermute | solution.py:266
  58.5 9.3 %collective-permute-start.14 = (bf16[64,2048]{1,0:T(8,128)(2,1)S(1)}, bf16[64,2048]{1,0:T(8,128)(2,1)S(1)}, u32[]{:S(2)}, u32[]{:S(2)}) collective-permute-start(bf16[64,2048]{1,0:T(8,128)(2,1)S(1)} %collective-permute-done.13), channel_id=1, source_target_pairs={{0,2},{1,3},{2,6},{3,7},{4,0},{5,1},{6,10},{7,11},{8,4},{9,5},{10,... | collective-permute-start | bytes 786440 | tf_op jit(solution)/shard_map/ppermute | solution.py:266
  60.5 23.8 %collective-permute-start.8 = (bf16[64,2048]{1,0:T(8,128)(2,1)S(1)}, bf16[64,2048]{1,0:T(8,128)(2,1)S(1)}, u32[]{:S(2)}, u32[]{:S(2)}) collective-permute-start(bf16[64,2048]{1,0:T(8,128)(2,1)S(1)} %collective-permute-done.7), channel_id=1, source_target_pairs={{0,2},{1,3},{2,6},{3,7},{4,0},{5,1},{6,10},{7,11},{8,4},{9,5},{10,... | collective-permute-start | bytes 786440 | tf_op jit(solution)/shard_map/ppermute | solution.py:266
  61.4 11.9 %collective-permute-start.23 = (bf16[64,2048]{1,0:T(8,128)(2,1)S(1)}, bf16[64,2048]{1,0:T(8,128)(2,1)S(1)}, u32[]{:S(2)}, u32[]{:S(2)}) collective-permute-start(bf16[64,2048]{1,0:T(8,128)(2,1)S(1)} %collective-permute-done.22), channel_id=1, source_target_pairs={{0,4},{1,5},{2,0},{3,1},{4,8},{5,9},{6,2},{7,3},{8,12},{9,13},{10,... | collective-permute-start | bytes 786440 | tf_op jit(solution)/shard_map/ppermute | solution.py:266
  67.7 11.2 %collective-permute-start.12 = (bf16[64,2048]{1,0:T(8,128)(2,1)S(1)}, bf16[64,2048]{1,0:T(8,128)(2,1)S(1)}, u32[]{:S(2)}, u32[]{:S(2)}) collective-permute-start(bf16[64,2048]{1,0:T(8,128)(2,1)S(1)} %collective-permute-done.11), channel_id=1, source_target_pairs={{0,4},{1,5},{2,0},{3,1},{4,8},{5,9},{6,2},{7,3},{8,12},{9,13},{10,... | collective-permute-start | bytes 786440 | tf_op jit(solution)/shard_map/ppermute | solution.py:266
  67.8 8.5 %collective-permute-start.15 = (bf16[64,2048]{1,0:T(8,128)(2,1)S(1)}, bf16[64,2048]{1,0:T(8,128)(2,1)S(1)}, u32[]{:S(2)}, u32[]{:S(2)}) collective-permute-start(bf16[64,2048]{1,0:T(8,128)(2,1)S(1)} %collective-permute-done.14), channel_id=1, source_target_pairs={{0,2},{1,3},{2,6},{3,7},{4,0},{5,1},{6,10},{7,11},{8,4},{9,5},{10,... | collective-permute-start | bytes 786440 | tf_op jit(solution)/shard_map/ppermute | solution.py:266
  73.3 11.0 %collective-permute-start.24 = (bf16[64,2048]{1,0:T(8,128)(2,1)S(1)}, bf16[64,2048]{1,0:T(8,128)(2,1)S(1)}, u32[]{:S(2)}, u32[]{:S(2)}) collective-permute-start(bf16[64,2048]{1,0:T(8,128)(2,1)S(1)} %collective-permute-done.23), channel_id=1, source_target_pairs={{0,4},{1,5},{2,0},{3,1},{4,8},{5,9},{6,2},{7,3},{8,12},{9,13},{10,... | collective-permute-start | bytes 786440 | tf_op jit(solution)/shard_map/ppermute | solution.py:266
  76.2 6.4 %collective-permute-start.16 = (bf16[64,2048]{1,0:T(8,128)(2,1)S(1)}, bf16[64,2048]{1,0:T(8,128)(2,1)S(1)}, u32[]{:S(2)}, u32[]{:S(2)}) collective-permute-start(bf16[64,2048]{1,0:T(8,128)(2,1)S(1)} %collective-permute-done.15), channel_id=1, source_target_pairs={{0,2},{1,3},{2,6},{3,7},{4,0},{5,1},{6,10},{7,11},{8,4},{9,5},{10,... | collective-permute-start | bytes 786440 | tf_op jit(solution)/shard_map/ppermute | solution.py:266
  87.4 9.3 %collective-permute-start.25 = (bf16[64,2048]{1,0:T(8,128)(2,1)S(1)}, bf16[64,2048]{1,0:T(8,128)(2,1)S(1)}, u32[]{:S(2)}, u32[]{:S(2)}) collective-permute-start(bf16[64,2048]{1,0:T(8,128)(2,1)S(1)} %get-tuple-element.87), channel_id=1, source_target_pairs={{0,4},{1,5},{2,0},{3,1},{4,8},{5,9},{6,2},{7,3},{8,12},{9,13},{10,... | collective-permute-start | bytes 786440 | tf_op jit(solution)/shard_map/ppermute | solution.py:266
  87.6 9.1 %collective-permute-start.29 = (bf16[64,2048]{1,0:T(8,128)(2,1)S(1)}, bf16[64,2048]{1,0:T(8,128)(2,1)S(1)}, u32[]{:S(2)}, u32[]{:S(2)}) collective-permute-start(bf16[64,2048]{1,0:T(8,128)(2,1)S(1)} %get-tuple-element.86), channel_id=1, source_target_pairs={{0,2},{1,3},{2,6},{3,7},{4,0},{5,1},{6,10},{7,11},{8,4},{9,5},{10,... | collective-permute-start | bytes 786440 | tf_op jit(solution)/shard_map/ppermute | solution.py:266
  89.7 12.5 %collective-permute-start.27 = (bf16[64,2048]{1,0:T(8,128)(2,1)S(1)}, bf16[64,2048]{1,0:T(8,128)(2,1)S(1)}, u32[]{:S(2)}, u32[]{:S(2)}) collective-permute-start(bf16[64,2048]{1,0:T(8,128)(2,1)S(1)} %get-tuple-element.89), channel_id=1, source_target_pairs={{0,4},{1,5},{2,0},{3,1},{4,8},{5,9},{6,2},{7,3},{8,12},{9,13},{10,... | collective-permute-start | bytes 786440 | tf_op jit(solution)/shard_map/ppermute | solution.py:266
  89.7 12.7 %collective-permute-start.35 = (bf16[64,2048]{1,0:T(8,128)(2,1)S(1)}, bf16[64,2048]{1,0:T(8,128)(2,1)S(1)}, u32[]{:S(2)}, u32[]{:S(2)}) collective-permute-start(bf16[64,2048]{1,0:T(8,128)(2,1)S(1)} %get-tuple-element.88), channel_id=1, source_target_pairs={{0,2},{1,3},{2,6},{3,7},{4,0},{5,1},{6,10},{7,11},{8,4},{9,5},{10,... | collective-permute-start | bytes 786440 | tf_op jit(solution)/shard_map/ppermute | solution.py:266
  96.9 18.8 %collective-permute-start.26 = (bf16[64,2048]{1,0:T(8,128)(2,1)S(1)}, bf16[64,2048]{1,0:T(8,128)(2,1)S(1)}, u32[]{:S(2)}, u32[]{:S(2)}) collective-permute-start(bf16[64,2048]{1,0:T(8,128)(2,1)S(1)} %get-tuple-element.85), channel_id=1, source_target_pairs={{0,4},{1,5},{2,0},{3,1},{4,8},{5,9},{6,2},{7,3},{8,12},{9,13},{10,... | collective-permute-start | bytes 786440 | tf_op jit(solution)/shard_map/ppermute | solution.py:266
  98.7 17.0 %collective-permute-start.31 = (bf16[64,2048]{1,0:T(8,128)(2,1)S(1)}, bf16[64,2048]{1,0:T(8,128)(2,1)S(1)}, u32[]{:S(2)}, u32[]{:S(2)}) collective-permute-start(bf16[64,2048]{1,0:T(8,128)(2,1)S(1)} %get-tuple-element.84), channel_id=1, source_target_pairs={{0,2},{1,3},{2,6},{3,7},{4,0},{5,1},{6,10},{7,11},{8,4},{9,5},{10,... | collective-permute-start | bytes 786440 | tf_op jit(solution)/shard_map/ppermute | solution.py:266
  102.5 9.1 %collective-permute-start.28 = (bf16[64,2048]{1,0:T(8,128)(2,1)S(1)}, bf16[64,2048]{1,0:T(8,128)(2,1)S(1)}, u32[]{:S(2)}, u32[]{:S(2)}) collective-permute-start(bf16[64,2048]{1,0:T(8,128)(2,1)S(1)} %get-tuple-element.81), channel_id=1, source_target_pairs={{0,4},{1,5},{2,0},{3,1},{4,8},{5,9},{6,2},{7,3},{8,12},{9,13},{10,... | collective-permute-start | bytes 786440 | tf_op jit(solution)/shard_map/ppermute | solution.py:266
  104.3 9.2 %collective-permute-start.36 = (bf16[64,2048]{1,0:T(8,128)(2,1)S(1)}, bf16[64,2048]{1,0:T(8,128)(2,1)S(1)}, u32[]{:S(2)}, u32[]{:S(2)}) collective-permute-start(bf16[64,2048]{1,0:T(8,128)(2,1)S(1)} %get-tuple-element.80), channel_id=1, source_target_pairs={{0,2},{1,3},{2,6},{3,7},{4,0},{5,1},{6,10},{7,11},{8,4},{9,5},{10,... | collective-permute-start | bytes 786440 | tf_op jit(solution)/shard_map/ppermute | solution.py:266
  113.6 6.7 %collective-permute-start.30 = (bf16[64,2048]{1,0:T(8,128)(2,1)S(1)}, bf16[64,2048]{1,0:T(8,128)(2,1)S(1)}, u32[]{:S(2)}, u32[]{:S(2)}) collective-permute-start(bf16[64,2048]{1,0:T(8,128)(2,1)S(1)} %get-tuple-element.79), channel_id=1, source_target_pairs={{0,4},{1,5},{2,0},{3,1},{4,8},{5,9},{6,2},{7,3},{8,12},{9,13},{10,... | collective-permute-start | bytes 786440 | tf_op jit(solution)/shard_map/ppermute | solution.py:266
  113.9 6.9 %collective-permute-start.37 = (bf16[64,2048]{1,0:T(8,128)(2,1)S(1)}, bf16[64,2048]{1,0:T(8,128)(2,1)S(1)}, u32[]{:S(2)}, u32[]{:S(2)}) collective-permute-start(bf16[64,2048]{1,0:T(8,128)(2,1)S(1)} %get-tuple-element.78), channel_id=1, source_target_pairs={{0,2},{1,3},{2,6},{3,7},{4,0},{5,1},{6,10},{7,11},{8,4},{9,5},{10,... | collective-permute-start | bytes 786440 | tf_op jit(solution)/shard_map/ppermute | solution.py:266
  115.8 8.2 %collective-permute-start.33 = (bf16[64,2048]{1,0:T(8,128)(2,1)S(1)}, bf16[64,2048]{1,0:T(8,128)(2,1)S(1)}, u32[]{:S(2)}, u32[]{:S(2)}) collective-permute-start(bf16[64,2048]{1,0:T(8,128)(2,1)S(1)} %get-tuple-element.83), channel_id=1, source_target_pairs={{0,4},{1,5},{2,0},{3,1},{4,8},{5,9},{6,2},{7,3},{8,12},{9,13},{10,... | collective-permute-start | bytes 786440 | tf_op jit(solution)/shard_map/ppermute | solution.py:266
  116.1 8.0 %collective-permute-start.34 = (bf16[64,2048]{1,0:T(8,128)(2,1)S(1)}, bf16[64,2048]{1,0:T(8,128)(2,1)S(1)}, u32[]{:S(2)}, u32[]{:S(2)}) collective-permute-start(bf16[64,2048]{1,0:T(8,128)(2,1)S(1)} %get-tuple-element.82), channel_id=1, source_target_pairs={{0,2},{1,3},{2,6},{3,7},{4,0},{5,1},{6,10},{7,11},{8,4},{9,5},{10,... | collective-permute-start | bytes 786440 | tf_op jit(solution)/shard_map/ppermute | solution.py:266
  121.0 6.4 %collective-permute-start.32 = (bf16[64,2048]{1,0:T(8,128)(2,1)S(1)}, bf16[64,2048]{1,0:T(8,128)(2,1)S(1)}, u32[]{:S(2)}, u32[]{:S(2)}) collective-permute-start(bf16[64,2048]{1,0:T(8,128)(2,1)S(1)} %get-tuple-element.77), channel_id=1, source_target_pairs={{0,4},{1,5},{2,0},{3,1},{4,8},{5,9},{6,2},{7,3},{8,12},{9,13},{10,... | collective-permute-start | bytes 786440 | tf_op jit(solution)/shard_map/ppermute | solution.py:266
  122.6 6.4 %collective-permute-start.38 = (bf16[64,2048]{1,0:T(8,128)(2,1)S(1)}, bf16[64,2048]{1,0:T(8,128)(2,1)S(1)}, u32[]{:S(2)}, u32[]{:S(2)}) collective-permute-start(bf16[64,2048]{1,0:T(8,128)(2,1)S(1)} %get-tuple-element.76), channel_id=1, source_target_pairs={{0,2},{1,3},{2,6},{3,7},{4,0},{5,1},{6,10},{7,11},{8,4},{9,5},{10,... | collective-permute-start | bytes 786440 | tf_op jit(solution)/shard_map/ppermute | solution.py:266

commit v15 on v8

--- a/solution.py
+++ b/solution.py
@@ -319,9 +319,7 @@
     halves = range(2)
     size = frames // 2
     hidden_width = expert_out.shape[0]
-    expert_in = after(expert_in, normed_top)
-    gate_in, up_in = lax.optimization_barrier((expert_in[:, :hidden_width], expert_in[:, hidden_width:]))
-    sent = [to_x(normed_top), to_x(after(normed_bottom, gate_in))]
+    sent = [to_x(normed_top), to_x(normed_bottom)]
 
     step = 1
     while step < wide:
@@ -367,6 +365,9 @@
                 jnp.concatenate([back, own[h]], axis=1),
             )
         )
+
+    rows[1], expert_in, expert_out = lax.optimization_barrier((rows[1], expert_in, expert_out))
+    gate_in, up_in = expert_in[:, :hidden_width], expert_in[:, hidden_width:]
 
     far = ring // 2
     fore_at, back_at = {0: rows}, {0: rows}

time: 128 us -> 124 us (0.969)
  waiting for transfers between devices: 42.3 us -> 46.6 us
  local copies, waits for them, and re-layouts: 4.53 us -> 0.79 us
  starting transfers between devices: 42.1 us -> 40 us
  matrix products: 17.6 us -> 15.9 us
    ppermute x38, waiting for transfers between devices: 42.3 us -> 46.6 us  [send(): return lax.ppermute(value, axes, routes(wide, move))]
    ppermute x38, starting transfers between devices: 42.1 us -> 40 us  [send(): return lax.ppermute(value, axes, routes(wide, move))]
    dot_general x4, matrix products: 5.31 us -> 3.41 us  [project(): jnp.dot(rows, columns, preferred_element_type=jnp.float32)]
    slice x1, local copies, waits for them, and re-layouts: 2.2 us -> 0.32 us  [dense_experts(): in_other[:, :hidden_width]]
    slice x1, local copies, waits for them, and re-layouts: 2.2 us -> 0.32 us  [dense_experts(): gate_in, up_in = (expert_in[:, :hidden_width], expert_in[:, hidden_width:])]
  transfers between devices with their start and end apart: 38 -> 38, of which waited for: 18 -> 21; matrix products, arithmetic and copies ran while one was open for 25% -> 21% of each run, Pallas kernels for 7% -> 7%
where the time goes in v15:
time: 124 us
  waiting for transfers between devices  46.6 us (38%)
  starting transfers between devices  40 us (32%)
  matrix products  15.9 us (13%)
  other arithmetic  10.7 us (9%)
  Pallas kernels  8.93 us (7%)
    ppermute x38, waiting for transfers between devices, send(): return lax.ppermute(value, axes, routes(wide, move))  46.6 us
    ppermute x38, starting transfers between devices, send(): return lax.ppermute(value, axes, routes(wide, move))  40 us
    dot_general x5, matrix products, run_experts(): jnp.dot(jnp.concatenate(parts), joined_in, preferred_element_type=jnp.flo...  7.47 us
    pallas_call x1, Pallas kernels, ssm_mixer(): pl.pallas_call(mixer_kernel, grid=(steps,), in_specs=[pl.BlockSpec(memory...  5.36 us
    select_n x1, other arithmetic, dense_experts(): jnp.where(core == 0, jnp.concatenate([out_proj, out_other], axis=1), jnp....  5.16 us
    dot_general x5, matrix products, run_experts(): return jnp.dot(hidden, joined_down, preferred_element_type=jnp.float32)  5.03 us
    pallas_call x1, Pallas kernels, state_next(): pl.pallas_call(state_kernel, grid=(steps,), in_specs=[column, whole, per_...  3.57 us
    dot_general x4, matrix products, project(): jnp.dot(rows, columns, preferred_element_type=jnp.float32)  3.41 us
  transfers between devices with their start and end apart: 38, of which 21 were waited for; matrix products, arithmetic and copies ran while one was open for 21% of the time, Pallas kernels for 7%

profile of v15, /device:TPU:0, one launch (start us, length us, event | category | flops | bytes accessed | tf_op | source)
XLA Modules:
  0.0 124.0 jit_solution(15255858915144052722)
XLA Ops:
  1.9 3.0 %collective-permute-start = (f32[128,16]{0,1:T(8,128)S(1)}, f32[128,16]{0,1:T(8,128)S(1)}, u32[]{:S(2)}, u32[]{:S(2)}) collective-permute-start(f32[128,16]{0,1:T(8,128)S(1)} %select_reduce_fusion.1), channel_id=1, source_target_pairs={{0,2},{1,3},{2,0},{3,1},{4,6},{5,7},{6,4},{7,5},{8,10},{9,11},{10,... | collective-permute-start | bytes 24584 | tf_op jit(solution)/shard_map/ppermute | solution.py:295
  5.0 5.4 %mixer.1 = (bf16[64,2048]{1,0:T(8,128)(2,1)}, bf16[64,2048]{1,0:T(8,128)(2,1)}) custom-call(f32[32]{0:T(128)} %skip_ref.1, bf16[128,2048]{1,0:T(8,128)(2,1)} %x_ref.2, bf16[128,2048]{1,0:T(8,128)(2,1)} %z_ref.1, bf16[128,128]{1,0:T(8,128)(2,1)} %b_ref.3, bf16[128,128]{1,0:T(8,128)(2,1)} %c_ref.1, f32[32,128]{1,0:T(8,128)} %bitcast.66, f32[1,32]{1,0:T(1,128)} %bitcast.68, ...), custom_call_target="tpu_custom_call" | custom-call | flops 400000000 | bytes 6000000 | tf_op jit(solution)/shard_map/mixer/pallas_call | solution.py:159
  10.4 1.6 %collective-permute-start.12 = (f32[2,1,128,16]{2,3,1,0:T(8,128)S(1)}, f32[2,1,128,16]{2,3,1,0:T(8,128)S(1)}, u32[]{:S(2)}, u32[]{:S(2)}) collective-permute-start(f32[2,1,128,16]{2,3,1,0:T(8,128)S(1)} %maximum_select_fusion.5), channel_id=1, source_target_pairs={{0,4},{1,5},{2,6},{3,7},{4,0},{5,1},{6,2},{7,3},{8,12},{9,13},{10,... | collective-permute-start | bytes 49160 | tf_op jit(solution)/shard_map/ppermute | solution.py:295
  12.6 1.6 %collective-permute-done.12 = f32[2,1,128,16]{2,3,1,0:T(8,128)S(1)} collective-permute-done((f32[2,1,128,16]{2,3,1,0:T(8,128)S(1)}, f32[2,1,128,16]{2,3,1,0:T(8,128)S(1)}, u32[]{:S(2)}, u32[]{:S(2)}) %collective-permute-start.12) | collective-permute-done | bytes 16416 | tf_op jit(solution)/shard_map/ppermute | solution.py:295
  14.2 2.6 %collective-permute-start.13 = (f32[2,2,128,16]{2,3,1,0:T(8,128)S(1)}, f32[2,2,128,16]{2,3,1,0:T(8,128)S(1)}, u32[]{:S(2)}, u32[]{:S(2)}) collective-permute-start(f32[2,2,128,16]{2,3,1,0:T(8,128)S(1)} %maximum_select_fusion.4), channel_id=1, source_target_pairs={{0,8},{1,9},{2,10},{3,11},{4,12},{5,13},{6,14},{7,15},{8,0},{9,1},... | collective-permute-start | bytes 98312 | tf_op jit(solution)/shard_map/ppermute | solution.py:295
  16.8 2.2 %collective-permute-done.13 = f32[2,2,128,16]{2,3,1,0:T(8,128)S(1)} collective-permute-done((f32[2,2,128,16]{2,3,1,0:T(8,128)S(1)}, f32[2,2,128,16]{2,3,1,0:T(8,128)S(1)}, u32[]{:S(2)}, u32[]{:S(2)}) %collective-permute-start.13) | collective-permute-done | bytes 32800 | tf_op jit(solution)/shard_map/ppermute | solution.py:295
  19.3 2.1 %collective-permute-done.11 = bf16[64,2048]{1,0:T(8,128)(2,1)S(1)} collective-permute-done((bf16[64,2048]{1,0:T(8,128)(2,1)}, bf16[64,2048]{1,0:T(8,128)(2,1)S(1)}, u32[]{:S(2)}, u32[]{:S(2)}) %collective-permute-start.11) | collective-permute-done | bytes 262176 | tf_op jit(solution)/shard_map/ppermute | solution.py:295
  21.7 5.2 %maximum_select_fusion = bf16[2048,1024]{1,0:T(8,128)(2,1)S(1)} fusion(bf16[2048,512]{1,0:T(8,128)(2,1)} %collective-permute-done.1, bf16[2048,512]{1,0:T(8,128)(2,1)} %param.25, pred[]{:T(512)S(6)} %eq.47), kind=kLoop, calls=%fused_computation.1 | loop fusion | flops 18874368 | bytes 8388609 | tf_op jit(solution)/shard_map/jit(_where)/select_n | solution.py:343
  29.1 1.7 %collective-permute-start.14 = (bf16[64,1024]{1,0:T(8,128)(2,1)S(1)}, bf16[64,1024]{1,0:T(8,128)(2,1)S(1)}, u32[]{:S(2)}, u32[]{:S(2)}) collective-permute-start(bf16[64,1024]{1,0:T(8,128)(2,1)S(1)} %convolution_convert_fusion.1), channel_id=1, source_target_pairs={{0,2},{1,3},{2,0},{3,1},{4,6},{5,7},{6,4},{7,5},{8,10},{9,11},{10,... | collective-permute-start | bytes 393224 | tf_op jit(solution)/shard_map/ppermute | solution.py:295
  31.7 0.9 convolution_convert_fusion.4
  32.5 2.2 %collective-permute-done.14 = bf16[64,1024]{1,0:T(8,128)(2,1)S(1)} collective-permute-done((bf16[64,1024]{1,0:T(8,128)(2,1)S(1)}, bf16[64,1024]{1,0:T(8,128)(2,1)S(1)}, u32[]{:S(2)}, u32[]{:S(2)}) %collective-permute-start.14) | collective-permute-done | bytes 131104 | tf_op jit(solution)/shard_map/ppermute | solution.py:295
  34.8 1.3 %collective-permute-start.15 = (bf16[64,2048]{1,0:T(8,128)(2,1)S(1)}, bf16[64,2048]{1,0:T(8,128)(2,1)S(1)}, u32[]{:S(2)}, u32[]{:S(2)}) collective-permute-start(bf16[64,2048]{1,0:T(8,128)(2,1)S(1)} %maximum_select_fusion.2), channel_id=1, source_target_pairs={{0,2},{1,3},{2,6},{3,7},{4,0},{5,1},{6,10},{7,11},{8,4},{9,5},{10,... | collective-permute-start | bytes 786440 | tf_op jit(solution)/shard_map/ppermute | solution.py:295
  37.0 1.2 collective-permute-start.21
  38.3 0.9 collective-permute-start.4
  39.1 4.9 %collective-permute-done.15 = bf16[64,2048]{1,0:T(8,128)(2,1)S(1)} collective-permute-done((bf16[64,2048]{1,0:T(8,128)(2,1)S(1)}, bf16[64,2048]{1,0:T(8,128)(2,1)S(1)}, u32[]{:S(2)}, u32[]{:S(2)}) %collective-permute-start.15) | collective-permute-done | bytes 262176 | tf_op jit(solution)/shard_map/ppermute | solution.py:295
  44.0 1.3 %collective-permute-start.16 = (bf16[64,2048]{1,0:T(8,128)(2,1)S(1)}, bf16[64,2048]{1,0:T(8,128)(2,1)S(1)}, u32[]{:S(2)}, u32[]{:S(2)}) collective-permute-start(bf16[64,2048]{1,0:T(8,128)(2,1)S(1)} %collective-permute-done.15), channel_id=1, source_target_pairs={{0,2},{1,3},{2,6},{3,7},{4,0},{5,1},{6,10},{7,11},{8,4},{9,5},{10,... | collective-permute-start | bytes 786440 | tf_op jit(solution)/shard_map/ppermute | solution.py:295
  46.6 4.5 %collective-permute-done.21 = bf16[64,2048]{1,0:T(8,128)(2,1)S(1)} collective-permute-done((bf16[64,2048]{1,0:T(8,128)(2,1)S(1)}, bf16[64,2048]{1,0:T(8,128)(2,1)S(1)}, u32[]{:S(2)}, u32[]{:S(2)}) %collective-permute-start.21) | collective-permute-done | bytes 262176 | tf_op jit(solution)/shard_map/ppermute | solution.py:295
  51.9 1.3 %collective-permute-start.5 = (bf16[64,2048]{1,0:T(8,128)(2,1)S(1)}, bf16[64,2048]{1,0:T(8,128)(2,1)S(1)}, u32[]{:S(2)}, u32[]{:S(2)}) collective-permute-start(bf16[64,2048]{1,0:T(8,128)(2,1)S(1)} %collective-permute-done.4), channel_id=1, source_target_pairs={{0,2},{1,3},{2,6},{3,7},{4,0},{5,1},{6,10},{7,11},{8,4},{9,5},{10,... | collective-permute-start | bytes 786440 | tf_op jit(solution)/shard_map/ppermute | solution.py:295
  53.2 2.1 %collective-permute-done.16 = bf16[64,2048]{1,0:T(8,128)(2,1)S(1)} collective-permute-done((bf16[64,2048]{1,0:T(8,128)(2,1)S(1)}, bf16[64,2048]{1,0:T(8,128)(2,1)S(1)}, u32[]{:S(2)}, u32[]{:S(2)}) %collective-permute-start.16) | collective-permute-done | bytes 262176 | tf_op jit(solution)/shard_map/ppermute | solution.py:295
  55.3 1.3 %collective-permute-start.17 = (bf16[64,2048]{1,0:T(8,128)(2,1)S(1)}, bf16[64,2048]{1,0:T(8,128)(2,1)S(1)}, u32[]{:S(2)}, u32[]{:S(2)}) collective-permute-start(bf16[64,2048]{1,0:T(8,128)(2,1)S(1)} %collective-permute-done.16), channel_id=1, source_target_pairs={{0,2},{1,3},{2,6},{3,7},{4,0},{5,1},{6,10},{7,11},{8,4},{9,5},{10,... | collective-permute-start | bytes 786440 | tf_op jit(solution)/shard_map/ppermute | solution.py:295
  57.5 1.9 %pad_maximum_fusion.1 = bf16[768,2048]{1,0:T(8,128)(2,1)S(1)} fusion(bf16[384,2048]{1,0:T(8,128)(2,1)} %collective-permute-done.20, bf16[384,2048]{1,0:T(8,128)(2,1)S(1)} %bitcast.75), kind=kLoop, calls=%fused_computation.2 | loop fusion | flops 6291456 | bytes 6291456 | tf_op jit(solution)/shard_map/concatenate | solution.py:382
  59.4 2.9 %collective-permute-done.22 = bf16[64,2048]{1,0:T(8,128)(2,1)S(1)} collective-permute-done((bf16[64,2048]{1,0:T(8,128)(2,1)S(1)}, bf16[64,2048]{1,0:T(8,128)(2,1)S(1)}, u32[]{:S(2)}, u32[]{:S(2)}) %collective-permute-start.22) | collective-permute-done | bytes 262176 | tf_op jit(solution)/shard_map/ppermute | solution.py:295
  63.1 1.3 %collective-permute-start.6 = (bf16[64,2048]{1,0:T(8,128)(2,1)S(1)}, bf16[64,2048]{1,0:T(8,128)(2,1)S(1)}, u32[]{:S(2)}, u32[]{:S(2)}) collective-permute-start(bf16[64,2048]{1,0:T(8,128)(2,1)S(1)} %collective-permute-done.5), channel_id=1, source_target_pairs={{0,2},{1,3},{2,6},{3,7},{4,0},{5,1},{6,10},{7,11},{8,4},{9,5},{10,... | collective-permute-start | bytes 786440 | tf_op jit(solution)/shard_map/ppermute | solution.py:295
  64.4 2.3 %collective-permute-done.17 = bf16[64,2048]{1,0:T(8,128)(2,1)S(1)} collective-permute-done((bf16[64,2048]{1,0:T(8,128)(2,1)S(1)}, bf16[64,2048]{1,0:T(8,128)(2,1)S(1)}, u32[]{:S(2)}, u32[]{:S(2)}) %collective-permute-start.17) | collective-permute-done | bytes 262176 | tf_op jit(solution)/shard_map/ppermute | solution.py:295
  66.7 1.3 %collective-permute-start.18 = (bf16[64,2048]{1,0:T(8,128)(2,1)S(1)}, bf16[64,2048]{1,0:T(8,128)(2,1)S(1)}, u32[]{:S(2)}, u32[]{:S(2)}) collective-permute-start(bf16[64,2048]{1,0:T(8,128)(2,1)S(1)} %collective-permute-done.17), channel_id=1, source_target_pairs={{0,2},{1,3},{2,6},{3,7},{4,0},{5,1},{6,10},{7,11},{8,4},{9,5},{10,... | collective-permute-start | bytes 786440 | tf_op jit(solution)/shard_map/ppermute | solution.py:295
  69.8 4.8 %collective-permute-done.18 = bf16[64,2048]{1,0:T(8,128)(2,1)S(1)} collective-permute-done((bf16[64,2048]{1,0:T(8,128)(2,1)S(1)}, bf16[64,2048]{1,0:T(8,128)(2,1)S(1)}, u32[]{:S(2)}, u32[]{:S(2)}) %collective-permute-start.18) | collective-permute-done | bytes 262176 | tf_op jit(solution)/shard_map/ppermute | solution.py:295
  74.6 2.0 %collective-permute-done.10 = bf16[64,2048]{1,0:T(8,128)(2,1)S(1)} collective-permute-done((bf16[64,2048]{1,0:T(8,128)(2,1)S(1)}, bf16[64,2048]{1,0:T(8,128)(2,1)S(1)}, u32[]{:S(2)}, u32[]{:S(2)}) %collective-permute-start.10) | collective-permute-done | bytes 262176 | tf_op jit(solution)/shard_map/ppermute | solution.py:295
  76.6 1.0 fusion.46
  78.5 1.5 %collective-permute-start.34 = (bf16[64,2048]{1,0:T(8,128)(2,1)S(1)}, bf16[64,2048]{1,0:T(8,128)(2,1)S(1)}, u32[]{:S(2)}, u32[]{:S(2)}) collective-permute-start(bf16[64,2048]{1,0:T(8,128)(2,1)S(1)} %get-tuple-element.88), channel_id=1, source_target_pairs={{0,2},{1,3},{2,6},{3,7},{4,0},{5,1},{6,10},{7,11},{8,4},{9,5},{10,... | collective-permute-start | bytes 786440 | tf_op jit(solution)/shard_map/ppermute | solution.py:295
  79.9 1.8 %fusion = f32[256,1536]{1,0:T(8,128)S(1)} fusion(bf16[2048,1536]{1,0:T(8,128)(2,1)S(1)} %pad_maximum_fusion, bf16[64,2048]{1,0:T(8,128)(2,1)S(1)} %collective-permute-done.23, bf16[64,2048]{1,0:T(8,128)(2,1)S(1)} %collective-permute-done.9, bf16[64,2048]{1,0:T(8,128)(2,1)S(1)} %collective-permute-done.17, bf16[64,2048]{1,0:T(8,128)(2,1)S(1)} %collective-permute-done.6), kind=kOutput, calls=%fused_computation.8 | convolution fusion | flops 1614807040 | bytes 8912896 | tf_op jit(solution)/shard_map/dot_general | solution.py:387
  81.8 1.2 fusion.108
  83.6 1.4 %collective-permute-start.27 = (bf16[64,2048]{1,0:T(8,128)(2,1)S(1)}, bf16[64,2048]{1,0:T(8,128)(2,1)S(1)}, u32[]{:S(2)}, u32[]{:S(2)}) collective-permute-start(bf16[64,2048]{1,0:T(8,128)(2,1)S(1)} %get-tuple-element.86), channel_id=1, source_target_pairs={{0,2},{1,3},{2,6},{3,7},{4,0},{5,1},{6,10},{7,11},{8,4},{9,5},{10,... | collective-permute-start | bytes 786440 | tf_op jit(solution)/shard_map/ppermute | solution.py:295
  85.7 1.8 %fusion.16 = f32[256,1536]{1,0:T(8,128)S(1)} fusion(bf16[2048,1536]{1,0:T(8,128)(2,1)S(1)} %pad_maximum_fusion, bf16[64,2048]{1,0:T(8,128)(2,1)S(1)} %collective-permute-done.22, bf16[64,2048]{1,0:T(8,128)(2,1)S(1)} %collective-permute-done.8, bf16[64,2048]{1,0:T(8,128)(2,1)S(1)} %collective-permute-done.16, bf16[64,2048]{1,0:T(8,128)(2,1)S(1)} %collective-permute-done.5), kind=kOutput, calls=%fused_computation.24 | convolution fusion | flops 1614807040 | bytes 8912896 | tf_op jit(solution)/shard_map/dot_general | solution.py:387
  87.5 1.2 fusion.58
  88.7 3.6 %collective-permute-done.24 = bf16[64,2048]{1,0:T(8,128)(2,1)S(1)} collective-permute-done((bf16[64,2048]{1,0:T(8,128)(2,1)S(1)}, bf16[64,2048]{1,0:T(8,128)(2,1)S(1)}, u32[]{:S(2)}, u32[]{:S(2)}) %collective-permute-start.24) | collective-permute-done | bytes 262176 | tf_op jit(solution)/shard_map/ppermute | solution.py:295
  93.0 1.4 %collective-permute-start.35 = (bf16[64,2048]{1,0:T(8,128)(2,1)S(1)}, bf16[64,2048]{1,0:T(8,128)(2,1)S(1)}, u32[]{:S(2)}, u32[]{:S(2)}) collective-permute-start(bf16[64,2048]{1,0:T(8,128)(2,1)S(1)} %get-tuple-element.78), channel_id=1, source_target_pairs={{0,2},{1,3},{2,6},{3,7},{4,0},{5,1},{6,10},{7,11},{8,4},{9,5},{10,... | collective-permute-start | bytes 786440 | tf_op jit(solution)/shard_map/ppermute | solution.py:295
  94.5 1.8 %fusion.8 = f32[256,1536]{1,0:T(8,128)S(1)} fusion(bf16[2048,1536]{1,0:T(8,128)(2,1)S(1)} %pad_maximum_fusion, bf16[64,2048]{1,0:T(8,128)(2,1)S(1)} %collective-permute-done.21, bf16[64,2048]{1,0:T(8,128)(2,1)S(1)} %collective-permute-done.7, bf16[64,2048]{1,0:T(8,128)(2,1)S(1)} %collective-permute-done.15, bf16[64,2048]{1,0:T(8,128)(2,1)S(1)} %collective-permute-done.4), kind=kOutput, calls=%fused_computation.16 | convolution fusion | flops 1614807040 | bytes 8912896 | tf_op jit(solution)/shard_map/dot_general | solution.py:387
  96.3 1.2 fusion.56
  97.5 2.5 %collective-permute-done.26 = bf16[64,2048]{1,0:T(8,128)(2,1)S(1)} collective-permute-done((bf16[64,2048]{1,0:T(8,128)(2,1)S(1)}, bf16[64,2048]{1,0:T(8,128)(2,1)S(1)}, u32[]{:S(2)}, u32[]{:S(2)}) %collective-permute-start.26) | collective-permute-done | bytes 262176 | tf_op jit(solution)/shard_map/ppermute | solution.py:295
  100.1 2.2 %collective-permute-start.30 = (bf16[64,2048]{1,0:T(8,128)(2,1)S(1)}, bf16[64,2048]{1,0:T(8,128)(2,1)S(1)}, u32[]{:S(2)}, u32[]{:S(2)}) collective-permute-start(bf16[64,2048]{1,0:T(8,128)(2,1)S(1)} %get-tuple-element.82), channel_id=1, source_target_pairs={{0,2},{1,3},{2,6},{3,7},{4,0},{5,1},{6,10},{7,11},{8,4},{9,5},{10,... | collective-permute-start | bytes 786440 | tf_op jit(solution)/shard_map/ppermute | solution.py:295
  102.6 2.0 %collective-permute-start.36 = (bf16[64,2048]{1,0:T(8,128)(2,1)S(1)}, bf16[64,2048]{1,0:T(8,128)(2,1)S(1)}, u32[]{:S(2)}, u32[]{:S(2)}) collective-permute-start(bf16[64,2048]{1,0:T(8,128)(2,1)S(1)} %get-tuple-element.76), channel_id=1, source_target_pairs={{0,2},{1,3},{2,6},{3,7},{4,0},{5,1},{6,10},{7,11},{8,4},{9,5},{10,... | collective-permute-start | bytes 786440 | tf_op jit(solution)/shard_map/ppermute | solution.py:295
  104.7 3.1 %collective-permute-done.30 = bf16[64,2048]{1,0:T(8,128)(2,1)S(1)} collective-permute-done((bf16[64,2048]{1,0:T(8,128)(2,1)S(1)}, bf16[64,2048]{1,0:T(8,128)(2,1)S(1)}, u32[]{:S(2)}, u32[]{:S(2)}) %collective-permute-start.30) | collective-permute-done | bytes 262176 | tf_op jit(solution)/shard_map/ppermute | solution.py:295
  107.8 1.0 collective-permute-done.29
  108.9 3.1 %collective-permute-done.36 = bf16[64,2048]{1,0:T(8,128)(2,1)S(1)} collective-permute-done((bf16[64,2048]{1,0:T(8,128)(2,1)S(1)}, bf16[64,2048]{1,0:T(8,128)(2,1)S(1)}, u32[]{:S(2)}, u32[]{:S(2)}) %collective-permute-start.36) | collective-permute-done | bytes 262176 | tf_op jit(solution)/shard_map/ppermute | solution.py:295
  112.3 1.2 collective-permute-start.32
  114.4 1.8 %collective-permute-start.33 = (bf16[64,2048]{1,0:T(8,128)(2,1)S(1)}, bf16[64,2048]{1,0:T(8,128)(2,1)S(1)}, u32[]{:S(2)}, u32[]{:S(2)}) collective-permute-start(bf16[64,2048]{1,0:T(8,128)(2,1)S(1)} %get-tuple-element.75), channel_id=1, source_target_pairs={{0,4},{1,5},{2,0},{3,1},{4,8},{5,9},{6,2},{7,3},{8,12},{9,13},{10,... | collective-permute-start | bytes 786440 | tf_op jit(solution)/shard_map/ppermute | solution.py:295
  116.4 3.6 %state.1 = f32[2048,128]{1,0:T(8,128)} custom-call(bf16[128,2048]{1,0:T(8,128)(2,1)S(1)} %copy-done.1, bf16[128,128]{1,0:T(8,128)(2,1)S(1)} %copy-done.2, f32[32,128]{1,0:T(8,128)S(1)} %bitcast.67, f32[1,32]{1,0:T(1,128)S(1)} %bitcast.69, f32[1,32]{1,0:T(1,128)S(1)} %bitcast.71, f32[2048,128]{1,0:T(8,128)S(1)} %bitcast.65), custom_call_target="tpu_custom_call" | custom-call | flops 70000000 | bytes 3000000 | tf_op jit(solution)/shard_map/state/pallas_call | solution.py:198
  120.0 1.0 fusion.50
  (96 shorter events, 19.4 us)
Async XLA Ops:
  0.6 21.1 %collective-permute-start.1 = (bf16[2048,512]{1,0:T(8,128)(2,1)}, bf16[2048,512]{1,0:T(8,128)(2,1)}, u32[]{:S(2)}, u32[]{:S(2)}) collective-permute-start(bf16[2048,512]{1,0:T(8,128)(2,1)} %param.25), channel_id=1, source_target_pairs={{0,1},{1,0},{2,3},{3,2},{4,5},{5,4},{6,7},{7,6},{8,9},{9,8},{10,11... | collective-permute-start | bytes 6291464 | tf_op jit(solution)/shard_map/ppermute | solution.py:295
  1.1 67.6 %collective-permute-start.19 = (bf16[2048,768]{1,0:T(8,128)(2,1)}, bf16[2048,768]{1,0:T(8,128)(2,1)S(1)}, u32[]{:S(2)}, u32[]{:S(2)}) collective-permute-start(bf16[2048,768]{1,0:T(8,128)(2,1)} %bitcast.72), channel_id=1, source_target_pairs={{0,1},{1,0},{2,3},{3,2},{4,5},{5,4},{6,7},{7,6},{8,9},{9,8},{10,11... | collective-permute-start | bytes 9437192 | tf_op jit(solution)/shard_map/ppermute | solution.py:295
  1.9 8.4 %collective-permute-start = (f32[128,16]{0,1:T(8,128)S(1)}, f32[128,16]{0,1:T(8,128)S(1)}, u32[]{:S(2)}, u32[]{:S(2)}) collective-permute-start(f32[128,16]{0,1:T(8,128)S(1)} %select_reduce_fusion.1), channel_id=1, source_target_pairs={{0,2},{1,3},{2,0},{3,1},{4,6},{5,7},{6,4},{7,5},{8,10},{9,11},{10,... | collective-permute-start | bytes 24584 | tf_op jit(solution)/shard_map/ppermute | solution.py:295
  4.9 33.3 %collective-permute-start.20 = (bf16[384,2048]{1,0:T(8,128)(2,1)}, bf16[384,2048]{1,0:T(8,128)(2,1)}, u32[]{:S(2)}, u32[]{:S(2)}) collective-permute-start(bf16[384,2048]{1,0:T(8,128)(2,1)} %bitcast.74), channel_id=1, source_target_pairs={{0,1},{1,0},{2,3},{3,2},{4,5},{5,4},{6,7},{7,6},{8,9},{9,8},{10,11... | collective-permute-start | bytes 4718600 | tf_op jit(solution)/shard_map/ppermute | solution.py:295
  10.4 3.8 %collective-permute-start.12 = (f32[2,1,128,16]{2,3,1,0:T(8,128)S(1)}, f32[2,1,128,16]{2,3,1,0:T(8,128)S(1)}, u32[]{:S(2)}, u32[]{:S(2)}) collective-permute-start(f32[2,1,128,16]{2,3,1,0:T(8,128)S(1)} %maximum_select_fusion.5), channel_id=1, source_target_pairs={{0,4},{1,5},{2,6},{3,7},{4,0},{5,1},{6,2},{7,3},{8,12},{9,13},{10,... | collective-permute-start | bytes 49160 | tf_op jit(solution)/shard_map/ppermute | solution.py:295
  12.1 9.3 %collective-permute-start.11 = (bf16[64,2048]{1,0:T(8,128)(2,1)}, bf16[64,2048]{1,0:T(8,128)(2,1)S(1)}, u32[]{:S(2)}, u32[]{:S(2)}) collective-permute-start(bf16[64,2048]{1,0:T(8,128)(2,1)} %get-tuple-element.39), channel_id=1, source_target_pairs={{0,2},{1,3},{2,0},{3,1},{4,6},{5,7},{6,4},{7,5},{8,10},{9,11},{10,... | collective-permute-start | bytes 786440 | tf_op jit(solution)/shard_map/ppermute | solution.py:295
  14.2 4.8 %collective-permute-start.13 = (f32[2,2,128,16]{2,3,1,0:T(8,128)S(1)}, f32[2,2,128,16]{2,3,1,0:T(8,128)S(1)}, u32[]{:S(2)}, u32[]{:S(2)}) collective-permute-start(f32[2,2,128,16]{2,3,1,0:T(8,128)S(1)} %maximum_select_fusion.4), channel_id=1, source_target_pairs={{0,8},{1,9},{2,10},{3,11},{4,12},{5,13},{6,14},{7,15},{8,0},{9,1},... | collective-permute-start | bytes 98312 | tf_op jit(solution)/shard_map/ppermute | solution.py:295
  19.0 7.9 %collective-permute-start.2 = (bf16[64,2048]{1,0:T(8,128)(2,1)}, bf16[64,2048]{1,0:T(8,128)(2,1)S(1)}, u32[]{:S(2)}, u32[]{:S(2)}) collective-permute-start(bf16[64,2048]{1,0:T(8,128)(2,1)} %get-tuple-element.38), channel_id=1, source_target_pairs={{0,2},{1,3},{2,0},{3,1},{4,6},{5,7},{6,4},{7,5},{8,10},{9,11},{10,... | collective-permute-start | bytes 786440 | tf_op jit(solution)/shard_map/ppermute | solution.py:295
  27.7 3.0 %copy-start.9 = (bf16[64,2048]{1,0:T(8,128)(2,1)S(1)}, bf16[64,2048]{1,0:T(8,128)(2,1)}, u32[]{:S(2)}) copy-start(bf16[64,2048]{1,0:T(8,128)(2,1)} %get-tuple-element.39) | copy-start | bytes 786436
  27.7 8.4 %collective-permute-start.3 = (bf16[64,1024]{1,0:T(8,128)(2,1)S(1)}, bf16[64,1024]{1,0:T(8,128)(2,1)S(1)}, u32[]{:S(2)}, u32[]{:S(2)}) collective-permute-start(bf16[64,1024]{1,0:T(8,128)(2,1)S(1)} %convolution_convert_fusion.3), channel_id=1, source_target_pairs={{0,2},{1,3},{2,0},{3,1},{4,6},{5,7},{6,4},{7,5},{8,10},{9,11},{10,... | collective-permute-start | bytes 393224 | tf_op jit(solution)/shard_map/ppermute | solution.py:295
  29.1 2.5 %copy-start.8 = (bf16[64,2048]{1,0:T(8,128)(2,1)S(1)}, bf16[64,2048]{1,0:T(8,128)(2,1)}, u32[]{:S(2)}) copy-start(bf16[64,2048]{1,0:T(8,128)(2,1)} %get-tuple-element.38) | copy-start | bytes 786436
  29.1 5.6 %collective-permute-start.14 = (bf16[64,1024]{1,0:T(8,128)(2,1)S(1)}, bf16[64,1024]{1,0:T(8,128)(2,1)S(1)}, u32[]{:S(2)}, u32[]{:S(2)}) collective-permute-start(bf16[64,1024]{1,0:T(8,128)(2,1)S(1)} %convolution_convert_fusion.1), channel_id=1, source_target_pairs={{0,2},{1,3},{2,0},{3,1},{4,6},{5,7},{6,4},{7,5},{8,10},{9,11},{10,... | collective-permute-start | bytes 393224 | tf_op jit(solution)/shard_map/ppermute | solution.py:295
  31.6 14.6 %copy-start.6 = (bf16[1,2048,768]{2,1,0:T(8,128)(2,1)S(1)}, bf16[1,2048,768]{2,1,0:T(8,128)(2,1)}, u32[]{:S(2)}) copy-start(bf16[1,2048,768]{2,1,0:T(8,128)(2,1)} %param.26) | copy-start | bytes 9437188
  34.8 9.2 %collective-permute-start.15 = (bf16[64,2048]{1,0:T(8,128)(2,1)S(1)}, bf16[64,2048]{1,0:T(8,128)(2,1)S(1)}, u32[]{:S(2)}, u32[]{:S(2)}) collective-permute-start(bf16[64,2048]{1,0:T(8,128)(2,1)S(1)} %maximum_select_fusion.2), channel_id=1, source_target_pairs={{0,2},{1,3},{2,6},{3,7},{4,0},{5,1},{6,10},{7,11},{8,4},{9,5},{10,... | collective-permute-start | bytes 786440 | tf_op jit(solution)/shard_map/ppermute | solution.py:295
  36.2 9.3 %collective-permute-start.7 = (bf16[64,2048]{1,0:T(8,128)(2,1)S(1)}, bf16[64,2048]{1,0:T(8,128)(2,1)S(1)}, u32[]{:S(2)}, u32[]{:S(2)}) collective-permute-start(bf16[64,2048]{1,0:T(8,128)(2,1)S(1)} %maximum_select_fusion.1), channel_id=1, source_target_pairs={{0,4},{1,5},{2,0},{3,1},{4,8},{5,9},{6,2},{7,3},{8,12},{9,13},{10,... | collective-permute-start | bytes 786440 | tf_op jit(solution)/shard_map/ppermute | solution.py:295
  37.0 20.5 %copy-start.7 = (bf16[1,384,2048]{2,1,0:T(8,128)(2,1)S(1)}, bf16[1,384,2048]{2,1,0:T(8,128)(2,1)}, u32[]{:S(2)}) copy-start(bf16[1,384,2048]{2,1,0:T(8,128)(2,1)} %param.27) | copy-start | bytes 4718596
  37.0 14.1 %collective-permute-start.21 = (bf16[64,2048]{1,0:T(8,128)(2,1)S(1)}, bf16[64,2048]{1,0:T(8,128)(2,1)S(1)}, u32[]{:S(2)}, u32[]{:S(2)}) collective-permute-start(bf16[64,2048]{1,0:T(8,128)(2,1)S(1)} %maximum_select_fusion.2), channel_id=1, source_target_pairs={{0,4},{1,5},{2,0},{3,1},{4,8},{5,9},{6,2},{7,3},{8,12},{9,13},{10,... | collective-permute-start | bytes 786440 | tf_op jit(solution)/shard_map/ppermute | solution.py:295
  38.3 13.6 %collective-permute-start.4 = (bf16[64,2048]{1,0:T(8,128)(2,1)S(1)}, bf16[64,2048]{1,0:T(8,128)(2,1)S(1)}, u32[]{:S(2)}, u32[]{:S(2)}) collective-permute-start(bf16[64,2048]{1,0:T(8,128)(2,1)S(1)} %maximum_select_fusion.1), channel_id=1, source_target_pairs={{0,2},{1,3},{2,6},{3,7},{4,0},{5,1},{6,10},{7,11},{8,4},{9,5},{10,... | collective-permute-start | bytes 786440 | tf_op jit(solution)/shard_map/ppermute | solution.py:295
  44.0 11.2 %collective-permute-start.16 = (bf16[64,2048]{1,0:T(8,128)(2,1)S(1)}, bf16[64,2048]{1,0:T(8,128)(2,1)S(1)}, u32[]{:S(2)}, u32[]{:S(2)}) collective-permute-start(bf16[64,2048]{1,0:T(8,128)(2,1)S(1)} %collective-permute-done.15), channel_id=1, source_target_pairs={{0,2},{1,3},{2,6},{3,7},{4,0},{5,1},{6,10},{7,11},{8,4},{9,5},{10,... | collective-permute-start | bytes 786440 | tf_op jit(solution)/shard_map/ppermute | solution.py:295
  45.5 11.2 %collective-permute-start.8 = (bf16[64,2048]{1,0:T(8,128)(2,1)S(1)}, bf16[64,2048]{1,0:T(8,128)(2,1)S(1)}, u32[]{:S(2)}, u32[]{:S(2)}) collective-permute-start(bf16[64,2048]{1,0:T(8,128)(2,1)S(1)} %collective-permute-done.7), channel_id=1, source_target_pairs={{0,4},{1,5},{2,0},{3,1},{4,8},{5,9},{6,2},{7,3},{8,12},{9,13},{10,... | collective-permute-start | bytes 786440 | tf_op jit(solution)/shard_map/ppermute | solution.py:295
  51.1 11.2 %collective-permute-start.22 = (bf16[64,2048]{1,0:T(8,128)(2,1)S(1)}, bf16[64,2048]{1,0:T(8,128)(2,1)S(1)}, u32[]{:S(2)}, u32[]{:S(2)}) collective-permute-start(bf16[64,2048]{1,0:T(8,128)(2,1)S(1)} %collective-permute-done.21), channel_id=1, source_target_pairs={{0,4},{1,5},{2,0},{3,1},{4,8},{5,9},{6,2},{7,3},{8,12},{9,13},{10,... | collective-permute-start | bytes 786440 | tf_op jit(solution)/shard_map/ppermute | solution.py:295
  51.9 11.2 %collective-permute-start.5 = (bf16[64,2048]{1,0:T(8,128)(2,1)S(1)}, bf16[64,2048]{1,0:T(8,128)(2,1)S(1)}, u32[]{:S(2)}, u32[]{:S(2)}) collective-permute-start(bf16[64,2048]{1,0:T(8,128)(2,1)S(1)} %collective-permute-done.4), channel_id=1, source_target_pairs={{0,2},{1,3},{2,6},{3,7},{4,0},{5,1},{6,10},{7,11},{8,4},{9,5},{10,... | collective-permute-start | bytes 786440 | tf_op jit(solution)/shard_map/ppermute | solution.py:295
  55.3 11.5 %collective-permute-start.17 = (bf16[64,2048]{1,0:T(8,128)(2,1)S(1)}, bf16[64,2048]{1,0:T(8,128)(2,1)S(1)}, u32[]{:S(2)}, u32[]{:S(2)}) collective-permute-start(bf16[64,2048]{1,0:T(8,128)(2,1)S(1)} %collective-permute-done.16), channel_id=1, source_target_pairs={{0,2},{1,3},{2,6},{3,7},{4,0},{5,1},{6,10},{7,11},{8,4},{9,5},{10,... | collective-permute-start | bytes 786440 | tf_op jit(solution)/shard_map/ppermute | solution.py:295
  56.8 11.3 %collective-permute-start.9 = (bf16[64,2048]{1,0:T(8,128)(2,1)S(1)}, bf16[64,2048]{1,0:T(8,128)(2,1)S(1)}, u32[]{:S(2)}, u32[]{:S(2)}) collective-permute-start(bf16[64,2048]{1,0:T(8,128)(2,1)S(1)} %collective-permute-done.8), channel_id=1, source_target_pairs={{0,4},{1,5},{2,0},{3,1},{4,8},{5,9},{6,2},{7,3},{8,12},{9,13},{10,... | collective-permute-start | bytes 786440 | tf_op jit(solution)/shard_map/ppermute | solution.py:295
  62.4 16.0 %collective-permute-start.23 = (bf16[64,2048]{1,0:T(8,128)(2,1)S(1)}, bf16[64,2048]{1,0:T(8,128)(2,1)S(1)}, u32[]{:S(2)}, u32[]{:S(2)}) collective-permute-start(bf16[64,2048]{1,0:T(8,128)(2,1)S(1)} %collective-permute-done.22), channel_id=1, source_target_pairs={{0,4},{1,5},{2,0},{3,1},{4,8},{5,9},{6,2},{7,3},{8,12},{9,13},{10,... | collective-permute-start | bytes 786440 | tf_op jit(solution)/shard_map/ppermute | solution.py:295
  63.1 15.3 %collective-permute-start.6 = (bf16[64,2048]{1,0:T(8,128)(2,1)S(1)}, bf16[64,2048]{1,0:T(8,128)(2,1)S(1)}, u32[]{:S(2)}, u32[]{:S(2)}) collective-permute-start(bf16[64,2048]{1,0:T(8,128)(2,1)S(1)} %collective-permute-done.5), channel_id=1, source_target_pairs={{0,2},{1,3},{2,6},{3,7},{4,0},{5,1},{6,10},{7,11},{8,4},{9,5},{10,... | collective-permute-start | bytes 786440 | tf_op jit(solution)/shard_map/ppermute | solution.py:295
  66.7 7.8 %collective-permute-start.18 = (bf16[64,2048]{1,0:T(8,128)(2,1)S(1)}, bf16[64,2048]{1,0:T(8,128)(2,1)S(1)}, u32[]{:S(2)}, u32[]{:S(2)}) collective-permute-start(bf16[64,2048]{1,0:T(8,128)(2,1)S(1)} %collective-permute-done.17), channel_id=1, source_target_pairs={{0,2},{1,3},{2,6},{3,7},{4,0},{5,1},{6,10},{7,11},{8,4},{9,5},{10,... | collective-permute-start | bytes 786440 | tf_op jit(solution)/shard_map/ppermute | solution.py:295
  68.0 8.6 %collective-permute-start.10 = (bf16[64,2048]{1,0:T(8,128)(2,1)S(1)}, bf16[64,2048]{1,0:T(8,128)(2,1)S(1)}, u32[]{:S(2)}, u32[]{:S(2)}) collective-permute-start(bf16[64,2048]{1,0:T(8,128)(2,1)S(1)} %collective-permute-done.9), channel_id=1, source_target_pairs={{0,4},{1,5},{2,0},{3,1},{4,8},{5,9},{6,2},{7,3},{8,12},{9,13},{10,... | collective-permute-start | bytes 786440 | tf_op jit(solution)/shard_map/ppermute | solution.py:295
  78.5 10.2 %collective-permute-start.34 = (bf16[64,2048]{1,0:T(8,128)(2,1)S(1)}, bf16[64,2048]{1,0:T(8,128)(2,1)S(1)}, u32[]{:S(2)}, u32[]{:S(2)}) collective-permute-start(bf16[64,2048]{1,0:T(8,128)(2,1)S(1)} %get-tuple-element.88), channel_id=1, source_target_pairs={{0,2},{1,3},{2,6},{3,7},{4,0},{5,1},{6,10},{7,11},{8,4},{9,5},{10,... | collective-permute-start | bytes 786440 | tf_op jit(solution)/shard_map/ppermute | solution.py:295
  83.0 9.3 %collective-permute-start.24 = (bf16[64,2048]{1,0:T(8,128)(2,1)S(1)}, bf16[64,2048]{1,0:T(8,128)(2,1)S(1)}, u32[]{:S(2)}, u32[]{:S(2)}) collective-permute-start(bf16[64,2048]{1,0:T(8,128)(2,1)S(1)} %get-tuple-element.89), channel_id=1, source_target_pairs={{0,4},{1,5},{2,0},{3,1},{4,8},{5,9},{6,2},{7,3},{8,12},{9,13},{10,... | collective-permute-start | bytes 786440 | tf_op jit(solution)/shard_map/ppermute | solution.py:295
  83.6 12.6 %collective-permute-start.27 = (bf16[64,2048]{1,0:T(8,128)(2,1)S(1)}, bf16[64,2048]{1,0:T(8,128)(2,1)S(1)}, u32[]{:S(2)}, u32[]{:S(2)}) collective-permute-start(bf16[64,2048]{1,0:T(8,128)(2,1)S(1)} %get-tuple-element.86), channel_id=1, source_target_pairs={{0,2},{1,3},{2,6},{3,7},{4,0},{5,1},{6,10},{7,11},{8,4},{9,5},{10,... | collective-permute-start | bytes 786440 | tf_op jit(solution)/shard_map/ppermute | solution.py:295
  85.1 17.4 %collective-permute-start.25 = (bf16[64,2048]{1,0:T(8,128)(2,1)S(1)}, bf16[64,2048]{1,0:T(8,128)(2,1)S(1)}, u32[]{:S(2)}, u32[]{:S(2)}) collective-permute-start(bf16[64,2048]{1,0:T(8,128)(2,1)S(1)} %get-tuple-element.87), channel_id=1, source_target_pairs={{0,4},{1,5},{2,0},{3,1},{4,8},{5,9},{6,2},{7,3},{8,12},{9,13},{10,... | collective-permute-start | bytes 786440 | tf_op jit(solution)/shard_map/ppermute | solution.py:295
  92.4 7.6 %collective-permute-start.26 = (bf16[64,2048]{1,0:T(8,128)(2,1)S(1)}, bf16[64,2048]{1,0:T(8,128)(2,1)S(1)}, u32[]{:S(2)}, u32[]{:S(2)}) collective-permute-start(bf16[64,2048]{1,0:T(8,128)(2,1)S(1)} %get-tuple-element.79), channel_id=1, source_target_pairs={{0,4},{1,5},{2,0},{3,1},{4,8},{5,9},{6,2},{7,3},{8,12},{9,13},{10,... | collective-permute-start | bytes 786440 | tf_op jit(solution)/shard_map/ppermute | solution.py:295
  93.0 9.4 %collective-permute-start.35 = (bf16[64,2048]{1,0:T(8,128)(2,1)S(1)}, bf16[64,2048]{1,0:T(8,128)(2,1)S(1)}, u32[]{:S(2)}, u32[]{:S(2)}) collective-permute-start(bf16[64,2048]{1,0:T(8,128)(2,1)S(1)} %get-tuple-element.78), channel_id=1, source_target_pairs={{0,2},{1,3},{2,6},{3,7},{4,0},{5,1},{6,10},{7,11},{8,4},{9,5},{10,... | collective-permute-start | bytes 786440 | tf_op jit(solution)/shard_map/ppermute | solution.py:295
  100.1 7.7 %collective-permute-start.30 = (bf16[64,2048]{1,0:T(8,128)(2,1)S(1)}, bf16[64,2048]{1,0:T(8,128)(2,1)S(1)}, u32[]{:S(2)}, u32[]{:S(2)}) collective-permute-start(bf16[64,2048]{1,0:T(8,128)(2,1)S(1)} %get-tuple-element.82), channel_id=1, source_target_pairs={{0,2},{1,3},{2,6},{3,7},{4,0},{5,1},{6,10},{7,11},{8,4},{9,5},{10,... | collective-permute-start | bytes 786440 | tf_op jit(solution)/shard_map/ppermute | solution.py:295
  102.4 14.0 %copy-start = (f32[1,32,64,128]{3,2,1,0:T(8,128)S(1)}, f32[1,32,64,128]{3,2,1,0:T(8,128)}, u32[]{:S(2)}) copy-start(f32[1,32,64,128]{3,2,1,0:T(8,128)} %param.24) | copy-start | bytes 3145732
  102.4 14.0 %copy-start.1 = (bf16[128,2048]{1,0:T(8,128)(2,1)S(1)}, bf16[128,2048]{1,0:T(8,128)(2,1)}, u32[]{:S(2)}) copy-start(bf16[128,2048]{1,0:T(8,128)(2,1)} %x_ref.2) | copy-start | bytes 1572868
  102.4 14.0 %copy-start.2 = (bf16[128,128]{1,0:T(8,128)(2,1)S(1)}, bf16[128,128]{1,0:T(8,128)(2,1)}, u32[]{:S(2)}) copy-start(bf16[128,128]{1,0:T(8,128)(2,1)} %b_ref.3) | copy-start | bytes 98308
  102.4 14.0 %copy-start.3 = (f32[128,32]{0,1:T(8,128)S(1)}, f32[128,32]{0,1:T(8,128)}, u32[]{:S(2)}) copy-start(f32[128,32]{0,1:T(8,128)} %param.19) | copy-start | bytes 49156
  102.4 14.0 %copy-start.4 = (f32[32]{0:T(128)S(1)}, f32[32]{0:T(128)}, u32[]{:S(2)}) copy-start(f32[32]{0:T(128)} %param.21) | copy-start | bytes 388
  102.4 14.0 %copy-start.5 = (f32[32]{0:T(128)S(1)}, f32[32]{0:T(128)}, u32[]{:S(2)}) copy-start(f32[32]{0:T(128)} %param.20) | copy-start | bytes 388
  102.4 6.4 %collective-permute-start.29 = (bf16[64,2048]{1,0:T(8,128)(2,1)S(1)}, bf16[64,2048]{1,0:T(8,128)(2,1)S(1)}, u32[]{:S(2)}, u32[]{:S(2)}) collective-permute-start(bf16[64,2048]{1,0:T(8,128)(2,1)S(1)} %get-tuple-element.83), channel_id=1, source_target_pairs={{0,4},{1,5},{2,0},{3,1},{4,8},{5,9},{6,2},{7,3},{8,12},{9,13},{10,... | collective-permute-start | bytes 786440 | tf_op jit(solution)/shard_map/ppermute | solution.py:295
  102.6 9.4 %collective-permute-start.36 = (bf16[64,2048]{1,0:T(8,128)(2,1)S(1)}, bf16[64,2048]{1,0:T(8,128)(2,1)S(1)}, u32[]{:S(2)}, u32[]{:S(2)}) collective-permute-start(bf16[64,2048]{1,0:T(8,128)(2,1)S(1)} %get-tuple-element.76), channel_id=1, source_target_pairs={{0,2},{1,3},{2,6},{3,7},{4,0},{5,1},{6,10},{7,11},{8,4},{9,5},{10,... | collective-permute-start | bytes 786440 | tf_op jit(solution)/shard_map/ppermute | solution.py:295
  104.7 7.5 %collective-permute-start.28 = (bf16[64,2048]{1,0:T(8,128)(2,1)S(1)}, bf16[64,2048]{1,0:T(8,128)(2,1)S(1)}, u32[]{:S(2)}, u32[]{:S(2)}) collective-permute-start(bf16[64,2048]{1,0:T(8,128)(2,1)S(1)} %get-tuple-element.77), channel_id=1, source_target_pairs={{0,4},{1,5},{2,0},{3,1},{4,8},{5,9},{6,2},{7,3},{8,12},{9,13},{10,... | collective-permute-start | bytes 786440 | tf_op jit(solution)/shard_map/ppermute | solution.py:295
  112.3 9.5 %collective-permute-start.32 = (bf16[64,2048]{1,0:T(8,128)(2,1)S(1)}, bf16[64,2048]{1,0:T(8,128)(2,1)S(1)}, u32[]{:S(2)}, u32[]{:S(2)}) collective-permute-start(bf16[64,2048]{1,0:T(8,128)(2,1)S(1)} %get-tuple-element.80), channel_id=1, source_target_pairs={{0,2},{1,3},{2,6},{3,7},{4,0},{5,1},{6,10},{7,11},{8,4},{9,5},{10,... | collective-permute-start | bytes 786440 | tf_op jit(solution)/shard_map/ppermute | solution.py:295
  113.5 8.3 %collective-permute-start.31 = (bf16[64,2048]{1,0:T(8,128)(2,1)S(1)}, bf16[64,2048]{1,0:T(8,128)(2,1)S(1)}, u32[]{:S(2)}, u32[]{:S(2)}) collective-permute-start(bf16[64,2048]{1,0:T(8,128)(2,1)S(1)} %get-tuple-element.81), channel_id=1, source_target_pairs={{0,4},{1,5},{2,0},{3,1},{4,8},{5,9},{6,2},{7,3},{8,12},{9,13},{10,... | collective-permute-start | bytes 786440 | tf_op jit(solution)/shard_map/ppermute | solution.py:295
  114.4 8.5 %collective-permute-start.33 = (bf16[64,2048]{1,0:T(8,128)(2,1)S(1)}, bf16[64,2048]{1,0:T(8,128)(2,1)S(1)}, u32[]{:S(2)}, u32[]{:S(2)}) collective-permute-start(bf16[64,2048]{1,0:T(8,128)(2,1)S(1)} %get-tuple-element.75), channel_id=1, source_target_pairs={{0,4},{1,5},{2,0},{3,1},{4,8},{5,9},{6,2},{7,3},{8,12},{9,13},{10,... | collective-permute-start | bytes 786440 | tf_op jit(solution)/shard_map/ppermute | solution.py:295
  116.1 6.4 %collective-permute-start.37 = (bf16[64,2048]{1,0:T(8,128)(2,1)S(1)}, bf16[64,2048]{1,0:T(8,128)(2,1)S(1)}, u32[]{:S(2)}, u32[]{:S(2)}) collective-permute-start(bf16[64,2048]{1,0:T(8,128)(2,1)S(1)} %get-tuple-element.74), channel_id=1, source_target_pairs={{0,2},{1,3},{2,6},{3,7},{4,0},{5,1},{6,10},{7,11},{8,4},{9,5},{10,... | collective-permute-start | bytes 786440 | tf_op jit(solution)/shard_map/ppermute | solution.py:295
